TPU v7x, 32 devices: a whole 2x2x4 slice. The times are simulated.
32 devices in a mesh: group: 4 (over z), span: 8 (over y, x, core).
Axes of the slice: x: 2, y: 2, z: 4, core: 2. Of those that a mesh axis runs over, the one named last changes fastest.
Arguments:
- tokens: bfloat16 [16384, 1024], P(('group', 'span')), may hold values from -16 to 16
- params: bfloat16 [12623872], P(('group', 'span')), may hold values from -14 to 4
- cotangent: bfloat16 [16384, 1024], P(('group', 'span')), may hold values from -6 to 6
- offsets: int32 [4, 4], P('group'), may hold values from 0 to 4096, as said below
Outputs:
- output: bfloat16 [16384, 1024], P(('group', 'span'))
- grad_tokens: float32 [16384, 1024], P(('group', 'span'))
- grad_params: float32 [12623872], P(('group', 'span'))
- stats: float32 [4], replicated
Inputs may be any that keep to these rules, and one draw needn't show every extreme that they name: `offsets`: each row lists, for one group, 0, the starts of its second and third sequences, and 4096. The first sequence ends on the group's first device and the third starts on its last device.
All inputs are finite; a program needn't handle non-finite values.
Results may differ from a plain program's by a relative error of at most 0.014.
Values may be sent and summed in bfloat16 or wider, within the bound.
No kernel may reach another device: no remote copies, remote signals or barrier semaphores. Data moves between devices by JAX's collectives and lax.ppermute only.
A program may use at most 320 MiB of HBM per device.

v0:
```python
import math

import jax
import jax.numpy as jnp
from jax import lax
from jax.sharding import PartitionSpec as P

D = 1024
HEADS_Q = 8
HEADS_KV = 2
HEAD_DIM = 64
SSM_HEADS = 24
SSM_DIM = 64
STATE = 128
CONV = 4
FF = 2048


epsilon = 1e-05
rope_base = 100000000000.0
masked_score = -1e30
highest = lax.Precision.HIGHEST
small_names = (
    "norm_attn",
    "conv_weight",
    "conv_bias",
    "step_bias",
    "decay_log",
    "skip_gain",
    "norm_ssm",
    "norm_ffn",
)


def passed_along(value, axis, steps):
    count = lax.axis_size(axis)
    first, last = (max(0, -steps), min(count, count - steps))
    return lax.ppermute(value, axis, [(source, source + steps) for source in range(first, last)])


def prefix(value, axis, combine, identity):
    peers, place = (lax.axis_size(axis), lax.axis_index(axis))
    everything = jax.tree.map(
        lambda part, kind: lax.all_gather(part.astype(kind), axis),
        value,
        (jnp.bfloat16, jnp.bfloat16),
    )
    start = jax.tree.map(
        lambda part, zero: jnp.broadcast_to(jnp.asarray(zero, part.dtype), part.shape),
        value,
        identity,
    )

    def prefix_turn(k, before):
        reached = k < place
        new = combine(
            before, jax.tree.map(lambda part, own: part[k].astype(own.dtype), everything, value)
        )
        return jax.tree.map(lambda a, b: jnp.where(reached, a, b), new, before)

    return lax.fori_loop(0, peers, prefix_turn, start)


def carried_in(value, axis, combine, identity):
    peers, place = (lax.axis_size(axis), lax.axis_index(axis))
    everything = jax.tree.map(
        lambda part, kind: lax.all_gather(part.astype(kind), axis),
        value,
        jax.tree.map(lambda a: jnp.bfloat16 if a.dtype == jnp.float32 else a.dtype, value),
    )
    start = jax.tree.map(
        lambda part, zero: jnp.broadcast_to(jnp.asarray(zero, part.dtype), part.shape),
        value,
        identity,
    )

    def carried_turn(k, before):
        at = peers - 1 - k
        reached = at > place
        new = combine(
            before, jax.tree.map(lambda part, own: part[at].astype(own.dtype), everything, value)
        )
        return jax.tree.map(lambda a, b: jnp.where(reached, a, b), new, before)

    return lax.fori_loop(0, peers, carried_turn, start)


def layout():
    ssm_inner = SSM_HEADS * SSM_DIM
    channels = ssm_inner + 2 * STATE
    return [
        ("norm_attn", (D,)),
        ("w_query", (D, HEADS_Q * HEAD_DIM)),
        ("w_key", (D, HEADS_KV * HEAD_DIM)),
        ("w_value", (D, HEADS_KV * HEAD_DIM)),
        ("w_attn_out", (HEADS_Q * HEAD_DIM, D)),
        ("w_gate_ssm", (D, ssm_inner)),
        ("w_x_ssm", (D, ssm_inner)),
        ("w_b_c", (D, 2 * STATE)),
        ("w_step", (D, SSM_HEADS)),
        ("conv_weight", (CONV, channels)),
        ("conv_bias", (channels,)),
        ("step_bias", (SSM_HEADS,)),
        ("decay_log", (SSM_HEADS,)),
        ("skip_gain", (SSM_HEADS,)),
        ("norm_ssm", (ssm_inner,)),
        ("w_ssm_out", (ssm_inner, D)),
        ("norm_ffn", (D,)),
        ("w_gate", (D, FF)),
        ("w_up_proj", (D, FF)),
        ("w_down", (FF, D)),
    ]


def unpack(flat_vector):
    unpacked = {}
    offset = 0
    for name_key, extent in layout():
        amount = math.prod(extent)
        unpacked[name_key] = flat_vector[offset : offset + amount].reshape(extent)
        offset += amount
    return unpacked


def matmul(left, right):
    return jnp.dot(left, right, preferred_element_type=jnp.float32)


def matmul_left_t(left, right):
    return lax.dot_general(
        left, right, (((0,), (0,)), ((), ())), preferred_element_type=jnp.float32
    )


def matmul_right_t(left, right):
    return lax.dot_general(
        left, right, (((1,), (1,)), ((), ())), preferred_element_type=jnp.float32
    )


def rms_norm(values, gain):
    return values * lax.rsqrt(jnp.mean(values * values, axis=-1, keepdims=True) + epsilon) * gain


def gated_norm(ssm_y, gate_ssm, gain):
    return rms_norm(ssm_y * jax.nn.silu(gate_ssm), gain)


def swiglu(gate_ffn, upper):
    return jax.nn.silu(gate_ffn) * upper


def sequence_info(row_index, bounds):
    starts = bounds[:-1]
    inside = row_index[:, None] >= starts[None, :]
    seq_id = jnp.sum(inside.astype(jnp.int32), axis=1) - 1
    seq_start = jnp.max(jnp.where(inside, starts[None, :], 0), axis=1)
    return (seq_id, row_index - seq_start)


def rotary_tables(positions):
    half_dim = HEAD_DIM // 2
    freqs = jnp.exp(
        -jnp.arange(half_dim, dtype=jnp.float32) * (2.0 * math.log(rope_base) / HEAD_DIM)
    )
    angles = positions.astype(jnp.float32)[:, None] * freqs[None, :]
    return (jnp.cos(angles), jnp.sin(angles))


def rotate(values, cosine, sine, heads):
    row_count = values.shape[0]
    half_dim = HEAD_DIM // 2
    split_heads = values.reshape(row_count, heads, HEAD_DIM)
    first_half = split_heads[..., :half_dim]
    second_half = split_heads[..., half_dim:]
    cos_b = cosine[:, None, :]
    sin_b = sine[:, None, :]
    turned = jnp.concatenate(
        [first_half * cos_b - second_half * sin_b, second_half * cos_b + first_half * sin_b],
        axis=-1,
    )
    return turned.reshape(row_count, heads * HEAD_DIM)


def conv_apply(extended, conv_weight, conv_bias, positions):
    row_count = positions.shape[0]
    conv_total = conv_bias[None, :]
    for tap_index in range(CONV):
        window = extended[tap_index : tap_index + row_count]
        valid_rows = (positions >= CONV - 1 - tap_index)[:, None]
        conv_total = (
            conv_total + jnp.where(valid_rows, window, 0.0) * conv_weight[tap_index][None, :]
        )
    return jax.nn.silu(conv_total)


def split_conv(conv_values):
    ssm_inner = SSM_HEADS * SSM_DIM
    x_ssm = conv_values[:, :ssm_inner].reshape(conv_values.shape[0], SSM_HEADS, SSM_DIM)
    return (
        x_ssm,
        conv_values[:, ssm_inner : ssm_inner + STATE],
        conv_values[:, ssm_inner + STATE :],
    )


def ssd_entry(cumul, seq_id, positions):
    carried = (seq_id == seq_id[0]) & (positions[0] > 0)
    return jnp.where(carried[:, None], jnp.exp(cumul), 0.0)


def ssd_output(x_ssm, b_in, c_in, step_size, decay, skip_gain, seq_id, positions, state_in):
    row_count = seq_id.shape[0]
    cumul = jnp.cumsum(step_size * decay[None, :], axis=0)
    order_rows = jnp.arange(row_count)
    visible = (seq_id[:, None] == seq_id[None, :]) & (order_rows[:, None] >= order_rows[None, :])
    log_gaps = cumul.T[:, :, None] - cumul.T[:, None, :]
    kernel = jnp.exp(jnp.where(visible[None], log_gaps, masked_score))
    inner_products = jnp.dot(c_in, b_in.T, precision=highest)
    scaled_x = x_ssm * step_size[:, :, None]
    intra_part = jnp.einsum(
        "hts,shp->thp", kernel * inner_products[None], scaled_x, precision=highest
    )
    entry_decay = ssd_entry(cumul, seq_id, positions)
    from_state = (
        jnp.einsum("hpn,tn->thp", state_in, c_in, precision=highest) * entry_decay[:, :, None]
    )
    return intra_part + from_state + skip_gain[None, :, None] * x_ssm


def ssd_summary(x_ssm, b_in, step_size, decay, seq_id, positions):
    cumul = jnp.cumsum(step_size * decay[None, :], axis=0)
    carried_last = (seq_id[-1] == seq_id[0]) & (positions[0] > 0)
    carry_all = jnp.where(carried_last, jnp.exp(cumul[-1]), 0.0)
    tail_decay = jnp.exp(
        jnp.where((seq_id == seq_id[-1])[:, None], cumul[-1:] - cumul, masked_score)
    )
    local_state = jnp.einsum(
        "sh,shp,sn->hpn", tail_decay, x_ssm * step_size[:, :, None], b_in, precision=highest
    )
    return (carry_all, local_state)


def chain_states(earlier, later):
    return (earlier[0] * later[0], earlier[1] * later[0][:, None, None] + later[1])


def add_rows(target, addend, first_row):
    current = lax.dynamic_slice_in_dim(target, first_row, addend.shape[0], 0)
    return lax.dynamic_update_slice_in_dim(target, current + addend, first_row, 0)


def body(tokens, params, cotangent, offsets):
    rows_dev = tokens.shape[0]
    group_rows = rows_dev * lax.axis_size("span")
    all_rows = group_rows * lax.axis_size("group")
    group_ratio = HEADS_Q // HEADS_KV
    ssm_inner = SSM_HEADS * SSM_DIM
    score_scale = HEAD_DIM ** (-0.5)
    bounds = offsets[0]
    my_start = lax.axis_index("span") * rows_dev
    row_index = my_start + jnp.arange(rows_dev, dtype=jnp.int32)
    seq_id, positions = sequence_info(row_index, bounds)
    first_start = row_index[0] - positions[0]
    last_row = my_start + rows_dev - 1
    cosine, sine = rotary_tables(positions)
    full_params = lax.all_gather(params, ("group", "span"), axis=0, tiled=True)
    weights = unpack(full_params)
    small_f32 = {name_key: weights[name_key].astype(jnp.float32) for name_key in small_names}
    x_rows = tokens.astype(jnp.float32)
    normed_one, norm_one_back = jax.vjp(rms_norm, x_rows, small_f32["norm_attn"])
    hidden = normed_one.astype(jnp.bfloat16)
    query = matmul(hidden, weights["w_query"])
    key_raw = matmul(hidden, weights["w_key"])
    value_low = matmul(hidden, weights["w_value"]).astype(jnp.bfloat16)
    q_rot = rotate(query, cosine, sine, HEADS_Q).astype(jnp.bfloat16)
    k_rot = rotate(key_raw, cosine, sine, HEADS_KV).astype(jnp.bfloat16)
    q_heads = q_rot.reshape(rows_dev, HEADS_KV, group_ratio, HEAD_DIM)

    def block_scores(key_block, key_rows):
        scores = (
            jnp.einsum(
                "tgjd,kgd->gjtk",
                q_heads,
                key_block.reshape(-1, HEADS_KV, HEAD_DIM),
                preferred_element_type=jnp.float32,
            )
            * score_scale
        )
        key_seq, _ = sequence_info(key_rows, bounds)
        visible = (seq_id[:, None] == key_seq[None, :]) & (key_rows[None, :] <= row_index[:, None])
        return (scores, visible[None, None])

    def over_blocks(carry_now, piece_pair, step_fn):
        keys_piece, values_piece = piece_pair
        piece_rows = keys_piece.shape[0]
        block_rows = math.gcd(piece_rows, 512)
        block_count = piece_rows // block_rows

        def one_block(state_now, inputs):
            index_block, key_block, value_block = inputs
            key_start = index_block * block_rows
            needed = (key_start <= last_row) & (key_start + block_rows > first_start)

            def compute(state_in_block):
                key_rows = key_start + jnp.arange(block_rows, dtype=jnp.int32)
                return step_fn(state_in_block, key_block, value_block, key_rows, key_start)

            def unchanged(state_in_block):
                return state_in_block

            return (lax.cond(needed, compute, unchanged, state_now), None)

        carry_now, _ = lax.scan(
            one_block,
            carry_now,
            (
                jnp.arange(block_count, dtype=jnp.int32),
                keys_piece.reshape(block_count, block_rows, -1),
                values_piece.reshape(block_count, block_rows, -1),
            ),
        )
        return carry_now

    def forward_step(state_now, key_block, value_block, key_rows, key_start):
        running_max, running_sum, accum = state_now
        scores, visible = block_scores(key_block, key_rows)
        new_max = jnp.maximum(
            running_max, jnp.max(jnp.where(visible, scores, masked_score), axis=-1)
        )
        weights_p = jnp.where(visible, jnp.exp(scores - new_max[..., None]), 0.0)
        factor = jnp.exp(running_max - new_max)
        mixed_values = jnp.einsum(
            "gjtk,kgd->gjtd",
            weights_p.astype(jnp.bfloat16),
            value_block.reshape(-1, HEADS_KV, HEAD_DIM),
            preferred_element_type=jnp.float32,
        )
        return (
            new_max,
            running_sum * factor + jnp.sum(weights_p, axis=-1),
            accum * factor[..., None] + mixed_values,
        )

    head_shape = (HEADS_KV, group_ratio, rows_dev)
    initial = (
        jnp.full(head_shape, masked_score, jnp.float32),
        jnp.zeros(head_shape, jnp.float32),
        jnp.zeros(head_shape + (HEAD_DIM,), jnp.float32),
    )
    running_max, running_sum, accum = over_blocks(
        initial,
        (
            lax.all_gather(k_rot, "span", axis=0, tiled=True),
            lax.all_gather(value_low, "span", axis=0, tiled=True),
        ),
        forward_step,
    )
    attn_f32 = accum / running_sum[..., None]
    log_total = running_max + jnp.log(running_sum)
    attended = (
        attn_f32.transpose(2, 0, 1, 3).reshape(rows_dev, HEADS_Q * HEAD_DIM).astype(jnp.bfloat16)
    )
    attn_out = matmul(attended, weights["w_attn_out"])
    gate_ssm = matmul(hidden, weights["w_gate_ssm"])
    xbc = jnp.concatenate(
        [matmul(hidden, weights["w_x_ssm"]), matmul(hidden, weights["w_b_c"])], axis=1
    )
    step_raw = matmul(hidden, weights["w_step"])
    rim_rows = passed_along(xbc[rows_dev - (CONV - 1) :], "span", 1)
    extended = jnp.concatenate([rim_rows, xbc], axis=0)

    def conv_local(extended_in, conv_weight, conv_bias):
        return conv_apply(extended_in, conv_weight, conv_bias, positions)

    conv_values, conv_back = jax.vjp(
        conv_local, extended, small_f32["conv_weight"], small_f32["conv_bias"]
    )

    def ssd_full(conv_in, step_in, step_bias, decay_log, skip_gain, state_in):
        x_ssm, b_in, c_in = split_conv(conv_in)
        step_size = jax.nn.softplus(step_in + step_bias[None, :])
        decay = -jnp.exp(decay_log)
        output = ssd_output(
            x_ssm, b_in, c_in, step_size, decay, skip_gain, seq_id, positions, state_in
        )
        carry_all, local_state = ssd_summary(x_ssm, b_in, step_size, decay, seq_id, positions)
        return (
            output.reshape(rows_dev, ssm_inner),
            carry_all[:, None, None] * state_in + local_state,
        )

    x_ssm, b_in, c_in = split_conv(conv_values)
    step_size = jax.nn.softplus(step_raw + small_f32["step_bias"][None, :])
    decay = -jnp.exp(small_f32["decay_log"])
    carry_all, local_state = ssd_summary(x_ssm, b_in, step_size, decay, seq_id, positions)
    state_ident = (jnp.ones_like(carry_all), jnp.zeros_like(local_state))
    _, state_in = prefix((carry_all, local_state), "span", chain_states, state_ident)
    (ssm_y, _), ssd_back = jax.vjp(
        ssd_full,
        conv_values,
        step_raw,
        small_f32["step_bias"],
        small_f32["decay_log"],
        small_f32["skip_gain"],
        state_in,
    )
    normed_ssm, gnorm_back = jax.vjp(gated_norm, ssm_y, gate_ssm, small_f32["norm_ssm"])
    ssm_low = normed_ssm.astype(jnp.bfloat16)
    ssm_out = matmul(ssm_low, weights["w_ssm_out"])
    middle = x_rows + attn_out + ssm_out
    normed_two, norm_two_back = jax.vjp(rms_norm, middle, small_f32["norm_ffn"])
    hidden_two = normed_two.astype(jnp.bfloat16)
    gate_ffn = matmul(hidden_two, weights["w_gate"])
    upper = matmul(hidden_two, weights["w_up_proj"])
    activation_f32, swiglu_back = jax.vjp(swiglu, gate_ffn, upper)
    activation = activation_f32.astype(jnp.bfloat16)
    ffn_out = matmul(activation, weights["w_down"])
    result = middle + ffn_out
    squares = jnp.stack(
        [
            jnp.sum(result * result),
            jnp.sum(attn_out * attn_out),
            jnp.sum(ssm_out * ssm_out),
            jnp.sum(ffn_out * ffn_out),
        ]
    )
    totals = lax.psum(squares, ("group", "span"))
    stats = jnp.sqrt(totals / (all_rows * D))
    back_weights = unpack(lax.all_gather(params, ("group", "span"), axis=0, tiled=True))
    grad_out = cotangent.astype(jnp.float32)
    grad_w_down = matmul_left_t(activation, cotangent)
    grad_activation = matmul_right_t(cotangent, back_weights["w_down"])
    grad_gate_f32, grad_upper_f32 = swiglu_back(grad_activation)
    grad_gate = grad_gate_f32.astype(jnp.bfloat16)
    grad_upper = grad_upper_f32.astype(jnp.bfloat16)
    grad_w_gate = matmul_left_t(hidden_two, grad_gate)
    grad_w_up = matmul_left_t(hidden_two, grad_upper)
    grad_hidden_two = matmul_right_t(grad_gate, back_weights["w_gate"]) + matmul_right_t(
        grad_upper, back_weights["w_up_proj"]
    )
    grad_middle_norm, grad_norm_ffn = norm_two_back(grad_hidden_two)
    grad_middle = grad_out + grad_middle_norm
    grad_branch = grad_middle.astype(jnp.bfloat16)
    grad_w_attn_out = matmul_left_t(attended, grad_branch)
    grad_w_ssm_out = matmul_left_t(ssm_low, grad_branch)
    grad_attended = matmul_right_t(grad_branch, back_weights["w_attn_out"]).astype(jnp.bfloat16)
    grad_ssm_low = matmul_right_t(grad_branch, back_weights["w_ssm_out"])
    grad_ssm_y, grad_gate_ssm_f32, grad_norm_ssm = gnorm_back(grad_ssm_low)
    cumul = jnp.cumsum(step_size * decay[None, :], axis=0)
    entry_decay = ssd_entry(cumul, seq_id, positions)
    grad_y_heads = grad_ssm_y.reshape(rows_dev, SSM_HEADS, SSM_DIM)
    grad_state_local = jnp.einsum(
        "thp,tn,th->hpn", grad_y_heads, c_in, entry_decay, precision=highest
    )
    _, grad_state_out = carried_in((carry_all, grad_state_local), "span", chain_states, state_ident)
    grad_conv_values, grad_step_raw_f32, grad_step_bias, grad_decay_log, grad_skip_gain, _ = (
        ssd_back((grad_ssm_y, grad_state_out))
    )
    grad_extended, grad_conv_weight, grad_conv_bias = conv_back(grad_conv_values)
    rim_back = passed_along(grad_extended[: CONV - 1], "span", -1)
    grad_xbc_f32 = grad_extended[CONV - 1 :]
    grad_xbc_f32 = grad_xbc_f32.at[rows_dev - (CONV - 1) :].add(rim_back)
    grad_xbc = grad_xbc_f32.astype(jnp.bfloat16)
    grad_gate_ssm = grad_gate_ssm_f32.astype(jnp.bfloat16)
    grad_step_raw = grad_step_raw_f32.astype(jnp.bfloat16)
    grad_w_gate_ssm = matmul_left_t(hidden, grad_gate_ssm)
    grad_w_x_ssm = matmul_left_t(hidden, grad_xbc[:, :ssm_inner])
    grad_w_b_c = matmul_left_t(hidden, grad_xbc[:, ssm_inner:])
    grad_w_step = matmul_left_t(hidden, grad_step_raw)
    grad_hidden_ssm = (
        matmul_right_t(grad_gate_ssm, back_weights["w_gate_ssm"])
        + matmul_right_t(grad_xbc[:, :ssm_inner], back_weights["w_x_ssm"])
        + matmul_right_t(grad_xbc[:, ssm_inner:], back_weights["w_b_c"])
        + matmul_right_t(grad_step_raw, back_weights["w_step"])
    )
    grad_heads = grad_attended.reshape(rows_dev, HEADS_KV, group_ratio, HEAD_DIM).transpose(
        1, 2, 0, 3
    )
    delta = jnp.sum(grad_heads.astype(jnp.float32) * attn_f32, axis=-1)

    def backward_step(state_now, key_block, value_block, key_rows, key_start):
        grad_query, grad_keys, grad_values = state_now
        scores, visible = block_scores(key_block, key_rows)
        probs = jnp.where(visible, jnp.exp(scores - log_total[..., None]), 0.0)
        key_heads = key_block.reshape(-1, HEADS_KV, HEAD_DIM)
        value_heads = value_block.reshape(-1, HEADS_KV, HEAD_DIM)
        grad_probs = jnp.einsum(
            "gjtd,kgd->gjtk", grad_heads, value_heads, preferred_element_type=jnp.float32
        )
        grad_scores = (probs * (grad_probs - delta[..., None])).astype(jnp.bfloat16)
        grad_query = (
            grad_query
            + jnp.einsum(
                "gjtk,kgd->gjtd", grad_scores, key_heads, preferred_element_type=jnp.float32
            )
            * score_scale
        )
        key_part = (
            jnp.einsum("gjtk,tgjd->kgd", grad_scores, q_heads, preferred_element_type=jnp.float32)
            * score_scale
        )
        value_part = jnp.einsum(
            "gjtk,gjtd->kgd",
            probs.astype(jnp.bfloat16),
            grad_heads,
            preferred_element_type=jnp.float32,
        )
        block_rows = key_block.shape[0]
        grad_keys = add_rows(grad_keys, key_part.reshape(block_rows, -1), key_start)
        grad_values = add_rows(grad_values, value_part.reshape(block_rows, -1), key_start)
        return (grad_query, grad_keys, grad_values)

    initial_back = (
        jnp.zeros(head_shape + (HEAD_DIM,), jnp.float32),
        jnp.zeros((group_rows, HEADS_KV * HEAD_DIM), jnp.float32),
        jnp.zeros((group_rows, HEADS_KV * HEAD_DIM), jnp.float32),
    )
    grad_query_all, grad_keys_all, grad_values_all = over_blocks(
        initial_back,
        (
            lax.all_gather(k_rot, "span", axis=0, tiled=True),
            lax.all_gather(value_low, "span", axis=0, tiled=True),
        ),
        backward_step,
    )
    grad_keys_mine, grad_values_mine = (
        lax.psum_scatter(
            grad_keys_all.astype(jnp.bfloat16), "span", scatter_dimension=0, tiled=True
        ).astype(jnp.float32),
        lax.psum_scatter(
            grad_values_all.astype(jnp.bfloat16), "span", scatter_dimension=0, tiled=True
        ).astype(jnp.float32),
    )
    grad_q_rot = grad_query_all.transpose(2, 0, 1, 3).reshape(rows_dev, HEADS_Q * HEAD_DIM)
    grad_query_low = rotate(grad_q_rot, cosine, -sine, HEADS_Q).astype(jnp.bfloat16)
    grad_key_low = rotate(grad_keys_mine, cosine, -sine, HEADS_KV).astype(jnp.bfloat16)
    grad_value_low = grad_values_mine.astype(jnp.bfloat16)
    grad_w_query = matmul_left_t(hidden, grad_query_low)
    grad_w_key = matmul_left_t(hidden, grad_key_low)
    grad_w_value = matmul_left_t(hidden, grad_value_low)
    grad_hidden = (
        grad_hidden_ssm
        + matmul_right_t(grad_query_low, back_weights["w_query"])
        + matmul_right_t(grad_key_low, back_weights["w_key"])
        + matmul_right_t(grad_value_low, back_weights["w_value"])
    )
    grad_x_norm, grad_norm_attn = norm_one_back(grad_hidden)
    grad_tokens = grad_middle + grad_x_norm
    grad_dict = {
        "norm_attn": grad_norm_attn,
        "w_query": grad_w_query,
        "w_key": grad_w_key,
        "w_value": grad_w_value,
        "w_attn_out": grad_w_attn_out,
        "w_gate_ssm": grad_w_gate_ssm,
        "w_x_ssm": grad_w_x_ssm,
        "w_b_c": grad_w_b_c,
        "w_step": grad_w_step,
        "conv_weight": grad_conv_weight,
        "conv_bias": grad_conv_bias,
        "step_bias": grad_step_bias,
        "decay_log": grad_decay_log,
        "skip_gain": grad_skip_gain,
        "norm_ssm": grad_norm_ssm,
        "w_ssm_out": grad_w_ssm_out,
        "norm_ffn": grad_norm_ffn,
        "w_gate": grad_w_gate,
        "w_up_proj": grad_w_up,
        "w_down": grad_w_down,
    }
    flat_parts = [grad_dict[name_key].reshape(-1) for name_key, extent in layout()]
    used_entries = 0
    for part_array in flat_parts:
        used_entries += part_array.shape[0]
    flat_parts.append(jnp.zeros((full_params.shape[0] - used_entries,), jnp.float32))
    grad_shard = lax.psum_scatter(
        jnp.concatenate(flat_parts), ("group", "span"), scatter_dimension=0, tiled=True
    )
    return (result.astype(jnp.bfloat16), grad_tokens, grad_shard, stats)


def solution(mesh):
    return jax.shard_map(
        body,
        mesh=mesh,
        in_specs=(
            P(("group", "span"), None),
            P(("group", "span")),
            P(("group", "span"), None),
            P("group", None),
        ),
        out_specs=(
            P(("group", "span"), None),
            P(("group", "span"), None),
            P(("group", "span")),
            P(),
        ),
        check_vma=False,
    )
```

profile of v0, /device:TPU:0, one launch (start us, length us, event | category | flops | bytes accessed | tf_op | source)
XLA Modules:
  0.0 2409.2 jit_solution(11479411547991848744)
XLA Ops:
  7.2 9.2 reshape.817
  26.1 269.5 %all-gather.18.cloned.1.call-done = bf16[32,1,394496]{2,1,0:T(2,128)(2,1)} async-done(((bf16[1,1,394496]{2,1,0:T(2,128)(2,1)}), bf16[32,1,394496]{2,1,0:T(2,128)(2,1)}) %all-gather.18.cloned.1.call-update) | async-done | bytes 25247760 | tf_op jit(solution)/shard_map/all_gather | solution.py:267
  295.6 151.6 %reduce.5 = bf16[32,394496]{1,0:T(8,128)(2,1)} reduce(bf16[32,1,394496]{2,1,0:T(2,128)(2,1)} %all-gather.18.cloned.1.call-done, bf16[]{:T(256)} %constant.295), dimensions={1}, to_apply=%all-gather.2.reduce_sub_computation | reduce | bytes 50495488 | tf_op jit(solution)/shard_map/all_gather | solution.py:267
  447.3 59.2 %reshape.818 = bf16[12623872]{0:T(1024)(128)(2,1)} reshape(bf16[32,394496]{1,0:T(8,128)(2,1)} %reduce.5) | data formatting | bytes 50495488
  508.2 7.0 fusion.213
  516.6 12.0 fusion.211
  531.7 7.0 reshape.771
  556.5 15.9 fusion.54
  579.8 5.3 fusion.101
  593.5 5.8 reshape.778
  599.5 8.7 all-gather.3
  608.2 6.8 reshape.777
  615.0 7.3 reshape.779
  622.3 7.3 reshape.780
  629.7 7.4 reshape.781
  647.6 18.0 while.61
  648.8 7.6 conditional.6
  670.4 10.0 while.63
  684.5 29.3 %fusion.60 = f32[512,24,64]{0,2,1:T(8,128)} fusion(f32[512,24,64]{0,2,1:T(8,128)S(1)} %bitcast.421, f32[512,24,64]{0,2,1:T(8,128)S(1)} %fusion.124, f32[512,512]{1,0:T(8,128)S(1)} %copy-done.62, f32[24,512]{1,0:T(8,128)S(1)} %get-tuple-element.1008, pred[512,512]{1,0:T(8,128)(4,1)S(1)} %copy-done.77, f32[24]{0:T(128)S(1)} %copy-done.139, ...), kind=kOutput, calls=%fused_computation.121 | convolution fusion | flops 4854644736 | bytes 10895456 | tf_op jit(solution)/shard_map/jvp(hts,shp->thp)/dot_general | solution.py:221
  717.8 6.9 multiply_reduce_fusion.11
  736.8 7.9 multiply_convert_fusion
  744.7 4.9 fusion.220
  768.1 29.9 %while.62 = (s32[]{:T(128)}, f32[2,4,512,64]{2,3,1,0:T(8,128)S(1)}, f32[4096,128]{0,1:T(8,128)}, f32[4096,128]{0,1:T(8,128)}, s32[8]{0:T(128)S(1)}, /*index=5*/s...) while((s32[]{:T(128)}, f32[2,4,512,64]{2,3,1,0:T(8,128)S(1)}, ...), condition=%wide.region_37.38_spmd.clone, body=%wide.region_33.37_spmd.clone.sunk | while | flops 1364661760 | bytes 63644168 | solution.py:314
  769.6 19.1 conditional.7
  801.2 8.4 multiply_reduce_fusion.7
  812.1 33.3 %fusion.36 = (f32[24,512]{1,0:T(8,128)}, f32[24,512]{1,0:T(8,128)}, f32[512,512]{1,0:T(8,128)}) fusion(f32[512,512]{1,0:T(8,128)} %fusion.134, f32[24,512]{1,0:T(8,128)S(1)} %copy-done.101, pred[512,512]{1,0:T(8,128)(4,1)S(1)} %copy-done.77, f32[24,64,512]{2,1,0:T(8,128)S(1)} %bitcast.411, f32[512,24,64]{0,2,1:T(8,128)} %bitcast.419, ...), kind=kOutput, calls=%fused_computation.61 | convolution fusion | flops 4888961024 | bytes 8847360 | tf_op jit(solution)/shard_map/transpose(jvp(hts,shp->thp))/dot_general | solution.py:221
  849.6 5.4 reduce-window.26
  869.5 6.9 reshape.796
  891.9 5.3 copy.138
  899.6 5.3 copy.139
  907.6 5.4 copy.140
  913.7 6.3 fusion.110
  927.4 22.4 fusion.31
  949.8 71.5 %reduce-scatter.3.cloned.1.call-done = bf16[512,128]{0,1:T(8,128)(2,1)} async-done(((bf16[4096,128]{0,1:T(8,128)(2,1)}), bf16[512,128]{0,1:T(8,128)(2,1)}) %reduce-scatter.3.cloned.1.call-update) | async-done | bytes 131088 | tf_op jit(solution)/shard_map/reduce_scatter | solution.py:528
  1025.5 50.6 %reduce-scatter.5.cloned.1.call-done = bf16[512,128]{0,1:T(8,128)(2,1)} async-done(((bf16[4096,128]{0,1:T(8,128)(2,1)}), bf16[512,128]{0,1:T(8,128)(2,1)}) %reduce-scatter.5.cloned.1.call-update) | async-done | bytes 131088 | tf_op jit(solution)/shard_map/reduce_scatter | solution.py:531
  1084.3 26.0 %all-gather.16.cloned.1.call-done = bf16[192,64,128]{2,1,0:T(8,128)(2,1)} async-done(((bf16[24,64,128]{2,1,0:T(8,128)(2,1)}), bf16[192,64,128]{2,1,0:T(8,128)(2,1)}) %all-gather.16.cloned.1.call-update) | async-done | bytes 3145744 | tf_op jit(solution)/shard_map/all_gather | solution.py:67
  1110.3 23.6 while.64
  1136.4 7.8 fusion.107
  1144.2 7.5 multiply_reduce_fusion.5
  1158.6 10.7 multiply_reduce_fusion.3
  1178.0 5.0 reduce-window.24
  1198.4 5.7 fusion.99
  1210.3 7.0 reshape.797
  1219.1 6.9 fusion.78
  1226.0 409.6 %concatenate.33 = f32[12623872]{0:T(1024)} concatenate(f32[1024]{0:T(1024)S(1)} %get-tuple-element.860, f32[524288]{0:T(1024)S(1)} %bitcast.432, f32[131072]{0:T(1024)} %convolution_bitcast_fusion.2, f32[131072]{0:T(1024)} %convolution_bitcast_fusion.1, f32[524288]{0:T(1024)} %bitcast.433, f32[1572864]{0:T(1024)} %reshape.796, f32[1572864]{0:T(1024)} %reshape.797, ...), dimensions={0} | concatenate | bytes 100990976 | tf_op jit(solution)/shard_map/concatenate | solution.py:578
  1638.3 76.9 %psum.7 = f32[4]{0:T(128)S(1)} all-reduce(f32[4]{0:T(128)S(1)} %pad_maximum_fusion.5), channel_id=1, replica_groups=mesh['group'=4,'span'=8] {'group','span'}, use_global_device_ids=true, to_apply=%region_59.60 | all-reduce | flops 4 | bytes 32 | tf_op jit(solution)/shard_map/psum | solution.py:428
  1715.8 4.9 fusion.80
  1720.8 678.2 %all-reduce.16.cloned.1.call-done = f32[12623872]{0:T(1024)} async-done(((f32[12623872]{0:T(1024)}), f32[12623872]{0:T(1024)}) %all-reduce.16.cloned.1.call-update) | async-done | bytes 50495504
  (590 shorter events, 281.7 us)
Async XLA Ops:
  7.2 14.3 copy-start.17
  7.2 288.5 %all-gather.18.cloned.1.call-start = ((), (), s32[]{:S(2)}) async-start(), calls=%async_computation.8 | async-start | bytes 52073472 | tf_op jit(solution)/shard_map/all_gather | solution.py:267
  16.4 625.5 %all-gather.10.cloned.1.call-start = ((), (), s32[]{:S(2)}) async-start(), calls=%async_computation.2 | async-start | bytes 1179648 | tf_op jit(solution)/shard_map/all_gather | solution.py:354
  21.8 425.5 %copy-start.120 = (f32[512]{0:T(512)}, f32[512]{0:T(512)S(1)}, u32[]{:S(2)}) copy-start(f32[512]{0:T(512)S(1)} %fusion.81) | copy-start | bytes 6148
  24.3 504.5 %copy-start.107 = (f32[512]{0:T(512)}, f32[512]{0:T(512)S(1)}, u32[]{:S(2)}) copy-start(f32[512]{0:T(512)S(1)} %fusion.173) | copy-start | bytes 6148
  25.2 612.7 %copy-start.54 = (f32[512,32]{0,1:T(8,128)}, f32[512,32]{0,1:T(8,128)S(1)}, u32[]{:S(2)}) copy-start(f32[512,32]{0,1:T(8,128)S(1)} %get-tuple-element.1016) | copy-start | bytes 196612
  508.2 209.5 %copy-start.95 = (f32[1024]{0:T(1024)}, f32[1024]{0:T(1024)S(1)}, u32[]{:S(2)}) copy-start(f32[1024]{0:T(1024)S(1)} %get-tuple-element.976) | copy-start | bytes 12292
  508.2 248.4 %copy-start.93 = (f32[1024]{0:T(1024)}, f32[1024]{0:T(1024)S(1)}, u32[]{:S(2)}) copy-start(f32[1024]{0:T(1024)S(1)} %get-tuple-element.975) | copy-start | bytes 12292
  530.3 113.9 %all-gather.12.cloned.1.call-start = ((), (), s32[]{:S(2)}) async-start(), calls=%async_computation.3 | async-start | bytes 1179648 | tf_op jit(solution)/shard_map/all_gather | solution.py:355
  531.7 24.4 %copy-start.33 = (f32[512,256]{1,0:T(8,128)}, f32[512,256]{1,0:T(8,128)S(1)}, u32[]{:S(2)}) copy-start(f32[512,256]{1,0:T(8,128)S(1)} %fusion.196) | copy-start | bytes 1572868
  544.3 9.4 collective-permute-start
  548.1 263.9 %copy-start.70 = (f32[512,24]{0,1:T(8,128)}, f32[512,24]{0,1:T(8,128)S(1)}, u32[]{:S(2)}) copy-start(f32[512,24]{0,1:T(8,128)S(1)} %get-tuple-element.1025) | copy-start | bytes 147460
  549.7 49.6 %copy-start.83 = (f32[512,24]{0,1:T(8,128)}, f32[512,24]{0,1:T(8,128)S(1)}, u32[]{:S(2)}) copy-start(f32[512,24]{0,1:T(8,128)S(1)} %get-tuple-element.1009) | copy-start | bytes 147460
  549.7 134.7 %copy-start.100 = (f32[24,512]{1,0:T(8,128)}, f32[24,512]{1,0:T(8,128)S(1)}, u32[]{:S(2)}) copy-start(f32[24,512]{1,0:T(8,128)S(1)} %get-tuple-element.1008) | copy-start | bytes 147460
  552.8 117.6 %all-gather.14.cloned.1.call-start = ((), (), s32[]{:S(2)}) async-start(), calls=%async_computation.6 | async-start | bytes 3538944 | tf_op jit(solution)/shard_map/all_gather | solution.py:44
  553.0 26.9 %copy-start.52 = (f32[512,24]{0,1:T(8,128)}, f32[512,24]{0,1:T(8,128)S(1)}, u32[]{:S(2)}) copy-start(f32[512,24]{0,1:T(8,128)S(1)} %get-tuple-element.1007) | copy-start | bytes 147460
  553.0 131.5 %copy-start.72 = (f32[512,24]{0,1:T(8,128)}, f32[512,24]{0,1:T(8,128)S(1)}, u32[]{:S(2)}) copy-start(f32[512,24]{0,1:T(8,128)S(1)} %get-tuple-element.1006) | copy-start | bytes 147460
  556.1 16.3 copy-start.1
  585.1 436.1 %reduce-scatter.3.cloned.1.call-start = ((), (), s32[]{:S(2)}) async-start(), calls=%async_computation.4 | async-start | bytes 1179648 | tf_op jit(solution)/shard_map/reduce_scatter | solution.py:528
  638.9 162.3 %copy-start.105 = (f32[1536]{0:T(1024)}, f32[1536]{0:T(1024)S(1)}, u32[]{:S(2)}) copy-start(f32[1536]{0:T(1024)S(1)} %slice_convert_fusion.1) | copy-start | bytes 18436
  670.4 14.0 copy-start.77
  680.5 33.4 %copy-start.7 = (f32[24,64,128]{2,1,0:T(8,128)}, f32[24,64,128]{2,1,0:T(8,128)S(1)}, u32[]{:S(2)}) copy-start(f32[24,64,128]{2,1,0:T(8,128)S(1)} %get-tuple-element.612) | copy-start | bytes 2359300
  680.5 33.3 %copy-start.141 = (bf16[8,24]{1,0:T(8,128)(2,1)}, bf16[8,24]{1,0:T(8,128)(2,1)S(1)}, u32[]{:S(2)}) copy-start(bf16[8,24]{1,0:T(8,128)(2,1)S(1)} %get-tuple-element.1503) | copy-start | bytes 1156
  684.4 29.4 %copy-start.21 = (f32[512,24,64]{0,2,1:T(8,128)}, f32[512,24,64]{0,2,1:T(8,128)S(1)}, u32[]{:S(2)}) copy-start(f32[512,24,64]{0,2,1:T(8,128)S(1)} %fusion.124) | copy-start | bytes 9437188
  724.6 34.4 %copy-start.44 = (f32[512,1536]{1,0:T(8,128)}, f32[512,1536]{1,0:T(8,128)S(1)}, u32[]{:S(2)}) copy-start(f32[512,1536]{1,0:T(8,128)S(1)} %get-tuple-element.961) | copy-start | bytes 9437188
  724.6 76.6 %copy-start.132 = (f32[512]{0:T(512)}, f32[512]{0:T(512)S(1)}, u32[]{:S(2)}) copy-start(f32[512]{0:T(512)S(1)} %fusion.174) | copy-start | bytes 6148
  727.6 29.1 %copy-start.15 = (f32[512,1024]{1,0:T(8,128)}, f32[512,1024]{1,0:T(8,128)S(1)}, u32[]{:S(2)}) copy-start(f32[512,1024]{1,0:T(8,128)S(1)} %get-tuple-element.957) | copy-start | bytes 6291460
  727.6 29.1 %copy-start.115 = (f32[512]{0:T(512)}, f32[512]{0:T(512)S(1)}, u32[]{:S(2)}) copy-start(f32[512]{0:T(512)S(1)} %fusion.175) | copy-start | bytes 6148
  798.0 11.6 copy-start.6
  801.1 274.9 %reduce-scatter.5.cloned.1.call-start = ((), (), s32[]{:S(2)}) async-start(), calls=%async_computation.5 | async-start | bytes 1179648 | tf_op jit(solution)/shard_map/reduce_scatter | solution.py:531
  812.1 33.4 %copy-start.20 = (f32[4096,128]{0,1:T(8,128)S(1)}, f32[4096,128]{0,1:T(8,128)}, u32[]{:S(2)}) copy-start(f32[4096,128]{0,1:T(8,128)} %get-tuple-element.617) | copy-start | bytes 6291460
  855.8 254.5 %all-gather.16.cloned.1.call-start = ((), (), s32[]{:S(2)}) async-start(), calls=%async_computation.7 | async-start | bytes 3538944 | tf_op jit(solution)/shard_map/all_gather | solution.py:67
  880.8 1518.1 %all-reduce.16.cloned.1.call-start = ((), (), s32[]{:S(2)}) async-start(), calls=%async_computation.9 | async-start | bytes 100990976
  1110.3 26.1 %copy-start.53 = (f32[512,24]{0,1:T(8,128)S(1)}, f32[512,24]{0,1:T(8,128)}, u32[]{:S(2)}) copy-start(f32[512,24]{0,1:T(8,128)} %copy-done.52) | copy-start | bytes 147460
  1110.3 26.1 %copy-start.71 = (f32[512,24]{0,1:T(8,128)S(1)}, f32[512,24]{0,1:T(8,128)}, u32[]{:S(2)}) copy-start(f32[512,24]{0,1:T(8,128)} %copy-done.70) | copy-start | bytes 147460
  1158.6 10.7 copy-start.86
  1158.6 10.7 copy-start.88
  1158.6 10.7 copy-start.90
  1158.6 10.7 copy-start.92
  1176.8 10.5 copy-start.19
  1176.8 10.5 copy-start.97
  1176.8 10.5 copy-start.111
  1188.7 8.0 collective-permute-start.1
  1635.6 80.2 %copy-start.121 = (f32[512]{0:T(512)S(1)}, f32[512]{0:T(512)}, u32[]{:S(2)}) copy-start(f32[512]{0:T(512)} %copy-done.120) | copy-start | bytes 6148
  1635.6 80.2 %copy-start.16 = (f32[512,1024]{1,0:T(8,128)S(1)}, f32[512,1024]{1,0:T(8,128)}, u32[]{:S(2)}) copy-start(f32[512,1024]{1,0:T(8,128)} %copy-done.15) | copy-start | bytes 6291460
  1635.6 80.2 %copy-start.94 = (f32[1024]{0:T(1024)S(1)}, f32[1024]{0:T(1024)}, u32[]{:S(2)}) copy-start(f32[1024]{0:T(1024)} %copy-done.93) | copy-start | bytes 12292
  1635.6 80.2 %copy-start.116 = (f32[512]{0:T(512)S(1)}, f32[512]{0:T(512)}, u32[]{:S(2)}) copy-start(f32[512]{0:T(512)} %copy-done.115) | copy-start | bytes 6148
  1635.6 80.2 %copy-start.119 = (f32[512]{0:T(512)S(1)}, f32[512]{0:T(512)}, u32[]{:S(2)}) copy-start(f32[512]{0:T(512)} %copy-done.118) | copy-start | bytes 6148
  (115 other events, 583.3 us)
Sparse Core Ops, SparseCore 0:
  16.5 279.0 all-gather.17
  530.4 21.9 all-gather.9
  554.2 23.2 all-gather.11
  585.2 31.4 all-gather.13
  801.3 219.9 reduce-scatter.2
  1024.3 51.7 reduce-scatter.4
  1078.0 32.2 all-gather.15
  1635.8 763.1 all-reduce.15
where the time goes:
time: 2450 us; the launch traced here: 2410 us
  waiting for transfers between devices  1100 us (45%)
  local copies, waits for them, and re-layouts  657 us (27%)
  other arithmetic  280 us (11%)
  matrix products  256 us (10%)
  blocking collectives  85.6 us (3%)
    unnamed x9, waiting for transfers between devices  678 us
    concatenate x1, local copies, waits for them, and re-layouts, body(): jnp.concatenate(flat_parts)  410 us
    all_gather x1, waiting for transfers between devices, body(): full_params = lax.all_gather(params, ('group', 'span'), axis=0, tiled=True)  270 us
    all_gather x1, other arithmetic, body(): full_params = lax.all_gather(params, ('group', 'span'), axis=0, tiled=True)  152 us
    unnamed x309, local copies, waits for them, and re-layouts  115 us
    dot_general x3, matrix products, ssd_output(): jnp.einsum('hts,shp->thp', kernel * inner_products[None], scaled_x, preci...  85.1 us
    psum x1, blocking collectives, body(): totals = lax.psum(squares, ('group', 'span'))  76.9 us
    reduce_scatter x1, waiting for transfers between devices, body(): lax.psum_scatter(grad_keys_all.astype(jnp.bfloat16), 'span', scatter_dime...  71.5 us
  transfers between devices with their start and end apart: 10, of which 5 were waited for; matrix products, arithmetic and copies ran while one was open for 12% of the time, Pallas kernels for 0%

commit v1 on v0

--- a/solution.py
+++ b/solution.py
@@ -2,8 +2,11 @@
 
 import jax
 import jax.numpy as jnp
+import numpy as np
 from jax import lax
-from jax.sharding import PartitionSpec as P
+from jax.experimental import pallas as pl
+from jax.experimental.pallas import tpu as pltpu
+from jax.sharding import Mesh, PartitionSpec as P
 
 D = 1024
 HEADS_Q = 8
@@ -14,6 +17,28 @@
 STATE = 128
 CONV = 4
 FF = 2048
+(
+    NORM_ATTN,
+    W_QUERY,
+    W_KEY,
+    W_VALUE,
+    W_ATTN_OUT,
+    W_GATE_SSM,
+    W_X_SSM,
+    W_B_C,
+    W_STEP,
+    CONV_WEIGHT,
+    CONV_BIAS,
+    STEP_BIAS,
+    DECAY_LOG,
+    SKIP_GAIN,
+    NORM_SSM,
+    W_SSM_OUT,
+    NORM_FFN,
+    W_GATE,
+    W_UP_PROJ,
+    W_DOWN,
+) = range(20)
 
 
 epsilon = 1e-05
@@ -21,14 +46,14 @@
 masked_score = -1e30
 highest = lax.Precision.HIGHEST
 small_names = (
-    "norm_attn",
-    "conv_weight",
-    "conv_bias",
-    "step_bias",
-    "decay_log",
-    "skip_gain",
-    "norm_ssm",
-    "norm_ffn",
+    NORM_ATTN,
+    CONV_WEIGHT,
+    CONV_BIAS,
+    STEP_BIAS,
+    DECAY_LOG,
+    SKIP_GAIN,
+    NORM_SSM,
+    NORM_FFN,
 )
 
 
@@ -89,26 +114,26 @@
     ssm_inner = SSM_HEADS * SSM_DIM
     channels = ssm_inner + 2 * STATE
     return [
-        ("norm_attn", (D,)),
-        ("w_query", (D, HEADS_Q * HEAD_DIM)),
-        ("w_key", (D, HEADS_KV * HEAD_DIM)),
-        ("w_value", (D, HEADS_KV * HEAD_DIM)),
-        ("w_attn_out", (HEADS_Q * HEAD_DIM, D)),
-        ("w_gate_ssm", (D, ssm_inner)),
-        ("w_x_ssm", (D, ssm_inner)),
-        ("w_b_c", (D, 2 * STATE)),
-        ("w_step", (D, SSM_HEADS)),
-        ("conv_weight", (CONV, channels)),
-        ("conv_bias", (channels,)),
-        ("step_bias", (SSM_HEADS,)),
-        ("decay_log", (SSM_HEADS,)),
-        ("skip_gain", (SSM_HEADS,)),
-        ("norm_ssm", (ssm_inner,)),
-        ("w_ssm_out", (ssm_inner, D)),
-        ("norm_ffn", (D,)),
-        ("w_gate", (D, FF)),
-        ("w_up_proj", (D, FF)),
-        ("w_down", (FF, D)),
+        (NORM_ATTN, (D,)),
+        (W_QUERY, (D, HEADS_Q * HEAD_DIM)),
+        (W_KEY, (D, HEADS_KV * HEAD_DIM)),
+        (W_VALUE, (D, HEADS_KV * HEAD_DIM)),
+        (W_ATTN_OUT, (HEADS_Q * HEAD_DIM, D)),
+        (W_GATE_SSM, (D, ssm_inner)),
+        (W_X_SSM, (D, ssm_inner)),
+        (W_B_C, (D, 2 * STATE)),
+        (W_STEP, (D, SSM_HEADS)),
+        (CONV_WEIGHT, (CONV, channels)),
+        (CONV_BIAS, (channels,)),
+        (STEP_BIAS, (SSM_HEADS,)),
+        (DECAY_LOG, (SSM_HEADS,)),
+        (SKIP_GAIN, (SSM_HEADS,)),
+        (NORM_SSM, (ssm_inner,)),
+        (W_SSM_OUT, (ssm_inner, D)),
+        (NORM_FFN, (D,)),
+        (W_GATE, (D, FF)),
+        (W_UP_PROJ, (D, FF)),
+        (W_DOWN, (FF, D)),
     ]
 
 
@@ -250,29 +275,534 @@
     return lax.dynamic_update_slice_in_dim(target, current + addend, first_row, 0)
 
 
-def body(tokens, params, cotangent, offsets):
+FAST = (4, 8)
+LINE = 128
+SHARD = 3082
+SPAD = 3088
+WIN = 3104
+PLANE = 8 * SHARD
+DEPTH = 4
+TALL = {1: 1024, 2: 1024, 4: 512, 8: 256, 12: 128, 16: 128}
+GRID = ("z", "y", "x", "c")
+ZC = ("z", "c")
+SWAP = [(0, 1), (1, 0)]
+
+
+def zc_pairs(*pairs):
+    return [(2 * a + c, 2 * b + c) for a, b, c in pairs]
+
+
+def gather_lines(params):
+    z, y, x, c = (lax.axis_index(name) for name in GRID)
+    lines = jnp.pad(params.reshape(SHARD, LINE), ((0, SPAD - SHARD), (0, 0)))
+    sibling = lax.ppermute(lines, ZC, [(2 * k + 1 - k % 2, 2 * k + k % 2) for k in range(4)])
+    batches = []
+    for batch in range(2):
+        buffers = []
+        for part in range(2):
+            here = jnp.where(c == part, lines, sibling)
+            if batch == 0:
+                one = lax.ppermute(here, ZC, zc_pairs((0, 1, 0), (1, 2, 1)))
+                side = lax.ppermute(here, ZC, zc_pairs((1, 0, 1)))
+                two = lax.ppermute(one, ZC, zc_pairs((1, 2, 0), (2, 3, 1)))
+                three = lax.ppermute(two, ZC, zc_pairs((2, 3, 0)))
+            else:
+                one = lax.ppermute(here, ZC, zc_pairs((2, 1, 0), (3, 2, 1)))
+                side = lax.ppermute(here, ZC, zc_pairs((2, 3, 0)))
+                two = lax.ppermute(one, ZC, zc_pairs((1, 0, 0), (2, 1, 1)))
+                three = lax.ppermute(two, ZC, zc_pairs((1, 0, 1)))
+            mine = z == 2 * batch + c
+            column = jnp.where(mine, here, one + side + two + three)
+            over_x = lax.ppermute(column, "x", SWAP)
+            over_y = lax.ppermute(column, "y", SWAP)
+            if part == 0:
+                corner = lax.ppermute(over_x, "y", SWAP)
+            else:
+                corner = lax.ppermute(over_y, "x", SWAP)
+            local = [column, over_x, over_y, corner]
+            buffers += local + [lax.ppermute(piece, "c", SWAP) for piece in local]
+        batches.append(buffers)
+    shard = np.arange(32)
+    sz, sy, sx, sc = shard // 8, shard // 4 % 2, shard // 2 % 2, shard % 2
+    away = jnp.where(sz % 2 == c, 0, 4)
+    where = sc * 8 + away + 2 * (sy ^ y) + (sx ^ x) + 16 * (sz // 2)
+    return batches, where.astype(jnp.int32)
+
+
+def unpack_lines(buffers, first, where, segments):
+    jobs, starts = [], []
+    reach = 0
+    for offset, rows, columns in segments:
+        per_row = columns // LINE
+        lane, base = offset % LINE, offset // LINE
+        if per_row == 1 and rows < 1024:
+            lane, tall = 0, rows
+        else:
+            tall = TALL[per_row]
+        starts.append(len(jobs))
+        for k in range(rows // tall):
+            jobs.append((base + k * tall * per_row, tall * per_row, 1 if lane else 0))
+    window = max(job[1] for job in jobs) + 32
+    table = np.zeros((len(jobs), 5), np.int32)
+    for k, (line, count, extra) in enumerate(jobs):
+        owner = line // SHARD
+        inside = line - owner * SHARD
+        begin = min(inside // 16 * 16, SPAD - window)
+        crosses = int(line + count + extra > (owner + 1) * SHARD)
+        table[k] = (owner, begin, begin - inside, crosses, (owner + 1) * SHARD - line)
+    base_row = (int(-table[:, 2].min()) + 7) // 8 * 8
+    table[:, 2] += base_row
+    table[:, 4] += base_row
+    room = int(max((table[:, 2] + window).max(), ((table[:, 4] + window) * table[:, 3]).max()))
+    room = (room + 15) // 8 * 8
+    total = len(jobs)
+    count_buffers = len(buffers)
+    shapes = []
+    for offset, rows, columns in segments:
+        per_row = columns // LINE
+        tall = rows if per_row == 1 and rows < 1024 else TALL[per_row]
+        shapes.append((rows, columns, tall, per_row, offset % LINE if tall != rows or per_row != 1 else 0))
+    sizes = sorted({(tall, columns) for _, columns, tall, _, _ in shapes})
+
+    def kernel(table_ref, where_ref, *refs):
+        sources = refs[:count_buffers]
+        outs = refs[count_buffers : count_buffers + len(segments)]
+        rest = refs[count_buffers + len(segments) :]
+        stages = dict(zip(sizes, rest))
+        raw, flat, in_sem, out_sem = rest[len(sizes) :]
+        step = pl.program_id(0)
+
+        def fetch(job, slot):
+            owner = table_ref[job, 0]
+            begin = pl.multiple_of(table_ref[job, 1], 16)
+            for b in range(count_buffers):
+
+                @pl.when(where_ref[owner] == first + b)
+                def _():
+                    pltpu.make_async_copy(
+                        sources[b].at[pl.ds(begin, window), :], raw.at[slot, 0], in_sem.at[slot, 0]
+                    ).start()
+
+            @pl.when(table_ref[job, 3] == 1)
+            def _():
+                for b in range(count_buffers):
+
+                    @pl.when(where_ref[owner + 1] == first + b)
+                    def _():
+                        pltpu.make_async_copy(
+                            sources[b].at[pl.ds(0, window), :], raw.at[slot, 1], in_sem.at[slot, 1]
+                        ).start()
+
+        def fetched(slot, half):
+            return pltpu.make_async_copy(
+                sources[0].at[pl.ds(0, window), :], raw.at[slot, half], in_sem.at[slot, half]
+            )
+
+        @pl.when(step == 0)
+        def _():
+            for k in range(min(DEPTH - 1, total)):
+                fetch(k, k)
+
+        @pl.when(step + DEPTH - 1 < total)
+        def _():
+            fetch(step + DEPTH - 1, lax.rem(step + DEPTH - 1, DEPTH))
+
+        slot = lax.rem(step, DEPTH)
+        fetched(slot, 0).wait()
+        flat[pl.ds(table_ref[step, 2], window), :] = raw[slot, 0].astype(jnp.float32)
+
+        @pl.when(table_ref[step, 3] == 1)
+        def _():
+            fetched(slot, 1).wait()
+            flat[pl.ds(table_ref[step, 4], window), :] = raw[slot, 1].astype(jnp.float32)
+
+        for index, (rows, columns, tall, per_row, lane) in enumerate(shapes):
+            begin = starts[index]
+            blocks = rows // tall
+            stage = stages[(tall, columns)]
+
+            @pl.when((step >= begin) & (step < begin + blocks))
+            def _():
+                block = step - begin
+                side = lax.rem(block, 2)
+
+                def written(k, s):
+                    return pltpu.make_async_copy(
+                        stage.at[s],
+                        outs[index].at[pl.ds(pl.multiple_of(k * tall, 16), tall), :],
+                        out_sem.at[s],
+                    )
+
+                @pl.when(block >= 2)
+                def _():
+                    written(block - 2, side).wait()
+
+                def tile(j):
+                    picked = flat[pl.ds(base_row + j, tall, stride=per_row), :]
+                    return pltpu.roll(picked, LINE - lane, 1) if lane else picked
+
+                if lane:
+                    lanes = lax.broadcasted_iota(jnp.int32, (tall, LINE), 1)
+                    now = tile(0)
+                    for j in range(per_row):
+                        later = tile(j + 1)
+                        stage[side, :, j * LINE : (j + 1) * LINE] = jnp.where(
+                            lanes < LINE - lane, now, later
+                        ).astype(jnp.bfloat16)
+                        now = later
+                else:
+                    for j in range(per_row):
+                        stage[side, :, j * LINE : (j + 1) * LINE] = tile(j).astype(jnp.bfloat16)
+                written(block, side).start()
+
+                @pl.when(block == blocks - 1)
+                def _():
+                    if blocks > 1:
+                        written(block - 1, 1 - side).wait()
+                    written(block, side).wait()
+
+    return pl.pallas_call(
+        kernel,
+        grid_spec=pltpu.PrefetchScalarGridSpec(
+            num_scalar_prefetch=2,
+            grid=(total,),
+            in_specs=[pl.BlockSpec(memory_space=pl.ANY)] * count_buffers,
+            out_specs=[pl.BlockSpec(memory_space=pl.ANY)] * len(segments),
+            scratch_shapes=[pltpu.VMEM((2,) + size, jnp.bfloat16) for size in sizes]
+            + [
+                pltpu.VMEM((DEPTH, 2, window, LINE), jnp.bfloat16),
+                pltpu.VMEM((room, LINE), jnp.float32),
+                pltpu.SemaphoreType.DMA((DEPTH, 2)),
+                pltpu.SemaphoreType.DMA((2,)),
+            ],
+        ),
+        out_shape=[jax.ShapeDtypeStruct((rows, columns), jnp.bfloat16) for _, rows, columns in segments],
+        compiler_params=pltpu.CompilerParams(vmem_limit_bytes=48 * 2**20),
+        cost_estimate=pl.CostEstimate(flops=0, bytes_accessed=total * window * LINE * 4, transcendentals=0),
+        name="unpack",
+    )(jnp.asarray(table), where, *buffers)
+
+
+def pack_lines(target, target_rows, first_row, segments, lane, phase, extras, carry, tail_rows):
+    tall = 256
+    lefts, rights, plan = [], [], []
+    left_of, right_of = {}, {}
+    row = first_row
+    begin = 0
+    for left, right in segments:
+        for value, seen, kept in ((left, left_of, lefts), (right, right_of, rights)):
+            if id(value) not in seen:
+                seen[id(value)] = len(kept)
+                kept.append(value)
+        blocks = left.shape[1] // tall
+        plan.append((left_of[id(left)], right_of[id(right)], right.shape[1] // LINE, begin, blocks, row))
+        begin += blocks
+        row += left.shape[1] * right.shape[1] // LINE
+    end_row = row
+    total = begin
+    biggest = max(entry[2] for entry in plan) * tall
+    tokens = lefts[0].shape[0]
+    count_left, count_right, count_extra = len(lefts), len(rights), len(extras)
+    rolled = [jnp.roll(right, lane, axis=1) if lane else right for right in rights]
+    carry_in = [carry] if lane else []
+    targets = [] if target is None else [target]
+
+    def left_spec(index):
+        mine = [entry for entry in plan if entry[0] == index]
+
+        def place(step):
+            block = 0
+            for _, _, _, start, blocks, _ in mine:
+                block = jnp.where(step >= start, jnp.minimum(step - start, blocks - 1), block)
+            return (0, block)
+
+        return pl.BlockSpec((tokens, tall), place)
+
+    def kernel(*refs):
+        left_refs = refs[:count_left]
+        right_refs = refs[count_left : count_left + count_right]
+        at = count_left + count_right
+        extra_refs = refs[at : at + count_extra]
+        at += count_extra
+        carry_refs = refs[at : at + len(carry_in)]
+        at += len(carry_in) + len(targets)
+        out = refs[at]
+        flat, stage, shift, last, sems, extra_sems = refs[at + 1 :]
+        step = pl.program_id(0)
+        side = lax.rem(step, 2)
+
+        def extra_copy(k):
+            rows = extras[k][0].shape[0]
+            return pltpu.make_async_copy(
+                extra_refs[k], out.at[pl.ds(extras[k][1], rows), :], extra_sems.at[k]
+            )
+
+        @pl.when(step == 0)
+        def _():
+            for k in range(count_extra):
+                extra_copy(k).start()
+            if lane:
+                shift[0:8, :] = carry_refs[0][...]
+            if phase:
+                flat[0:8, :] = jnp.zeros((8, LINE), jnp.float32)
+
+        for left_at, right_at, per_row, start, blocks, row in plan:
+            lines = per_row * tall
+
+            def written(block, s, row=row, lines=lines):
+                return pltpu.make_async_copy(
+                    stage.at[s, pl.ds(0, lines), :],
+                    out.at[pl.ds(pl.multiple_of(row + block * lines, 16), lines), :],
+                    sems.at[s],
+                )
+
+            @pl.when((step >= start) & (step < start + blocks))
+            def _():
+                block = step - start
+                if phase:
+
+                    @pl.when(step > 0)
+                    def _():
+                        flat[0:8, :] = flat[lines : lines + 8, :]
+
+                turned = left_refs[left_at][...].T
+                lanes = lax.broadcasted_iota(jnp.int32, (tall, LINE), 1)
+                for j0 in range(0, per_row, 2):
+                    wide = min(2, per_row - j0)
+                    tile = jnp.dot(
+                        turned,
+                        right_refs[right_at][:, j0 * LINE : (j0 + wide) * LINE],
+                        preferred_element_type=jnp.float32,
+                    )
+                    for j in range(wide):
+                        piece = tile[:, j * LINE : (j + 1) * LINE]
+                        if lane and j0 + j == 0:
+                            shift[8 : 8 + tall, :] = piece
+                            piece = jnp.where(lanes < lane, shift[7 : 7 + tall, :], piece)
+                            shift[0:8, :] = shift[tall : tall + 8, :]
+                        if per_row == 1:
+                            flat[phase : phase + tall, :] = piece
+                        else:
+                            flat[pl.ds(phase + j0 + j, tall, stride=per_row), :] = piece
+
+                stage[side, 0:lines, :] = flat[0:lines, :].astype(jnp.bfloat16)
+                written(block, side).start()
+
+            @pl.when((step > start) & (step <= start + blocks))
+            def _():
+                written(step - start - 1, 1 - side).wait()
+
+            if start + blocks == total:
+
+                @pl.when(step == total - 1)
+                def _():
+                    written(blocks - 1, side).wait()
+
+        @pl.when(step == total - 1)
+        def _():
+            if tail_rows:
+                lanes = lax.broadcasted_iota(jnp.int32, (tail_rows, LINE), 1)
+                rows_at = lax.broadcasted_iota(jnp.int32, (tail_rows, LINE), 0)
+                final = jnp.broadcast_to(shift[7:8, :], (tail_rows, LINE))
+                last[...] = jnp.where((rows_at == 0) & (lanes < lane), final, 0.0).astype(jnp.bfloat16)
+                closing = pltpu.make_async_copy(
+                    last, out.at[pl.ds(end_row, tail_rows), :], extra_sems.at[count_extra]
+                )
+                closing.start()
+                closing.wait()
+            for k in range(count_extra):
+                extra_copy(k).wait()
+
+    whole = [pl.BlockSpec(array.shape, lambda step: (0, 0)) for array in rolled]
+    flops = sum(2 * tokens * entry[4] * tall * entry[2] * LINE for entry in plan)
+    return pl.pallas_call(
+        kernel,
+        grid=(total,),
+        in_specs=[left_spec(k) for k in range(count_left)]
+        + whole
+        + [pl.BlockSpec(array.shape, lambda step: (0, 0)) for array, _ in extras]
+        + [pl.BlockSpec(array.shape, lambda step: (0, 0)) for array in carry_in]
+        + [pl.BlockSpec(memory_space=pl.ANY)] * len(targets),
+        out_specs=pl.BlockSpec(memory_space=pl.ANY),
+        out_shape=jax.ShapeDtypeStruct((target_rows, LINE), jnp.bfloat16),
+        scratch_shapes=[
+            pltpu.VMEM((biggest + 16, LINE), jnp.float32),
+            pltpu.VMEM((2, biggest, LINE), jnp.bfloat16),
+            pltpu.VMEM((tall + 8, LINE), jnp.float32),
+            pltpu.VMEM((max(tail_rows, 16), LINE), jnp.bfloat16),
+            pltpu.SemaphoreType.DMA((2,)),
+            pltpu.SemaphoreType.DMA((count_extra + 1,)),
+        ],
+        input_output_aliases={count_left + count_right + count_extra + len(carry_in): 0} if targets else {},
+        compiler_params=pltpu.CompilerParams(vmem_limit_bytes=48 * 2**20),
+        cost_estimate=pl.CostEstimate(flops=flops, bytes_accessed=total * biggest * LINE * 2, transcendentals=0),
+        name="pack",
+    )(*lefts, *rolled, *[array for array, _ in extras], *carry_in, *targets)
+
+
+def added(*parts):
+    total = parts[0].astype(jnp.float32)
+    for part in parts[1:]:
+        total = total + part.astype(jnp.float32)
+    return total.astype(jnp.bfloat16)
+
+
+def reduce_lines(flat, batch, shift):
+    z, y, x, c = (lax.axis_index(name) for name in GRID)
+    length = PLANE + 32
+    keep = lax.dynamic_slice(flat, (c * PLANE, 0), (length, LINE))
+    send = lax.dynamic_slice(flat, ((1 - c) * PLANE, 0), (length, LINE))
+    chip = added(keep, lax.ppermute(send, "c", SWAP))
+
+    def window(sy, sx, part):
+        shard = sy * 4 + sx * 2 + part
+        start = (shift + SHARD * shard) // 16 * 16
+        return lax.dynamic_slice(chip, (start, 0), (WIN, LINE))
+
+    ends = []
+    for part in range(2):
+        if part == 0:
+            away = jnp.stack([window(1 - y, 0, part), window(1 - y, 1, part)])
+            home = jnp.stack([window(y, 0, part), window(y, 1, part)])
+            first_axis, second_axis, place = "y", "x", x
+        else:
+            away = jnp.stack([window(0, 1 - x, part), window(1, 1 - x, part)])
+            home = jnp.stack([window(0, x, part), window(1, x, part)])
+            first_axis, second_axis, place = "x", "y", y
+        half = added(home, lax.ppermute(away, first_axis, SWAP))
+        other = lax.dynamic_index_in_dim(half, 1 - place, 0, keepdims=False)
+        mine = lax.dynamic_index_in_dim(half, place, 0, keepdims=False)
+        column = added(mine, lax.ppermute(other, second_axis, SWAP))
+        if batch == 0:
+            one = added(column, lax.ppermute(column, ZC, zc_pairs((3, 2, 0), (3, 2, 1))))
+            side = lax.ppermute(column, ZC, zc_pairs((0, 1, 1)))
+            two = added(one, lax.ppermute(one, ZC, zc_pairs((2, 1, 0), (2, 1, 1))), side)
+            end = added(two, lax.ppermute(two, ZC, zc_pairs((1, 0, 0))))
+        else:
+            one = added(column, lax.ppermute(column, ZC, zc_pairs((0, 1, 0), (0, 1, 1))))
+            side = lax.ppermute(column, ZC, zc_pairs((3, 2, 0)))
+            two = added(one, lax.ppermute(one, ZC, zc_pairs((1, 2, 0), (1, 2, 1))), side)
+            end = added(two, lax.ppermute(two, ZC, zc_pairs((2, 3, 1))))
+        ends.append(end)
+    mine = jnp.where(c == 0, ends[0], ends[1])
+    other = jnp.where(c == 0, ends[1], ends[0])
+    holders = [(2 * k + k % 2, 2 * k + 1 - k % 2) for k in range(4)]
+    handed = lax.ppermute(other, ZC, holders)
+    return jnp.where(c == z % 2, mine, handed)
+
+
+def offsets_of():
+    places, at = {}, 0
+    for name_key, extent in layout():
+        places[name_key] = (at, extent)
+        at += math.prod(extent)
+    return places
+
+
+def fast_weights(params):
+    places = offsets_of()
+    (early, late), where = gather_lines(params)
+    early_names = (W_QUERY, W_KEY, W_VALUE, W_ATTN_OUT, W_GATE_SSM, W_X_SSM, W_B_C)
+    late_names = (W_SSM_OUT, W_GATE, W_UP_PROJ, W_DOWN)
+
+    def segment(name_key):
+        at, extent = places[name_key]
+        return (at, extent[0], extent[1])
+
+    misc_at = places[W_STEP][0]
+    first = unpack_lines(
+        early, 0, where,
+        [segment(name_key) for name_key in early_names] + [(0, 16, LINE), (misc_at, 288, LINE)],
+    )
+    second = unpack_lines(
+        early + late, 0, where,
+        [segment(name_key) for name_key in late_names] + [(places[NORM_FFN][0], 16, LINE)],
+    )
+    weights = dict(zip(early_names, first))
+    weights.update(zip(late_names, second))
+    weights[NORM_ATTN] = first[-2].reshape(-1)[:D]
+    misc = first[-1].reshape(-1)
+    for name_key in (W_STEP,) + small_names[1:-1]:
+        at, extent = places[name_key]
+        weights[name_key] = misc[at - misc_at : at - misc_at + math.prod(extent)].reshape(extent)
+    lane = places[NORM_FFN][0] % LINE
+    weights[NORM_FFN] = second[-1].reshape(-1)[lane : lane + D]
+    return weights
+
+
+def fast_gradients(small, pairs):
+    places = offsets_of()
+    z, y, x, c = (lax.axis_index(name) for name in GRID)
+    ssm_low, grad_branch = pairs[W_SSM_OUT]
+    out_at = places[W_SSM_OUT][0]
+    lane = places[W_GATE][0] % LINE
+    boundary = 2 * PLANE * LINE
+    tail_from = (boundary - out_at) // D
+    tail = matmul_left_t(ssm_low[:, tail_from:], grad_branch).reshape(-1)
+    tail = tail[boundary - out_at - tail_from * D :]
+    head = jnp.concatenate([jnp.zeros((14 * LINE,), jnp.float32), tail, small[NORM_FFN]])
+    head_rows = head.shape[0] // LINE
+    carry = jnp.zeros((8, LINE), jnp.float32).at[7, :lane].set(head[head_rows * LINE :])
+    head = head[: head_rows * LINE].reshape(head_rows, LINE).astype(jnp.bfloat16)
+    length = 2 * PLANE + 32
+    late = pack_lines(
+        None, length, head_rows,
+        [pairs[W_GATE], pairs[W_UP_PROJ], pairs[W_DOWN]],
+        lane, 0, [(head, 0)], carry, 48,
+    )
+    late_sum = reduce_lines(late, 1, 14)
+    first_row = (8 + out_at // LINE) // 16 * 16
+    early_rows = first_row + SSM_HEADS * SSM_DIM * D // LINE
+    early = pack_lines(
+        None, early_rows, first_row, [pairs[W_SSM_OUT]],
+        lane, (8 + out_at // LINE) % 8, [], jnp.zeros((8, LINE), jnp.float32), 0,
+    )
+    names = (W_STEP,) + small_names[1:-1]
+    misc = [small[name_key].reshape(-1) for name_key in names]
+    count = sum(part.shape[0] for part in misc)
+    misc_rows = (count // LINE + 16) // 16 * 16
+    opening = matmul_left_t(ssm_low[:, :16], grad_branch).reshape(-1)
+    misc = jnp.concatenate(misc + [opening[: misc_rows * LINE - count]])
+    misc = misc.reshape(misc_rows, LINE).astype(jnp.bfloat16)
+    first = jnp.concatenate([jnp.zeros((8 * LINE,), jnp.float32), small[NORM_ATTN]])
+    first = first.reshape(16, LINE).astype(jnp.bfloat16)
+    early = pack_lines(
+        early, early_rows, 16,
+        [pairs[k] for k in (W_QUERY, W_KEY, W_VALUE, W_ATTN_OUT, W_GATE_SSM, W_X_SSM, W_B_C)],
+        0, 0, [(first, 0), (misc, 8 + places[W_STEP][0] // LINE)], None, 0,
+    )
+    early_sum = reduce_lines(early, 0, 8)
+    shard = SHARD * (4 * y + 2 * x + c)
+    start = jnp.where(z < 2, (8 + shard) % 16, (14 + shard) % 16)
+    lines = jnp.where(z < 2, early_sum, late_sum)
+    return lax.dynamic_slice(lines, (start, 0), (SHARD, LINE)).astype(jnp.float32).reshape(-1)
+
+
+def body(span, group, fast, tokens, params, cotangent, offsets):
     rows_dev = tokens.shape[0]
-    group_rows = rows_dev * lax.axis_size("span")
-    all_rows = group_rows * lax.axis_size("group")
+    group_rows = rows_dev * lax.axis_size(span)
+    all_rows = group_rows * lax.axis_size(group)
     group_ratio = HEADS_Q // HEADS_KV
     ssm_inner = SSM_HEADS * SSM_DIM
     score_scale = HEAD_DIM ** (-0.5)
     bounds = offsets[0]
-    my_start = lax.axis_index("span") * rows_dev
+    my_start = lax.axis_index(span) * rows_dev
     row_index = my_start + jnp.arange(rows_dev, dtype=jnp.int32)
     seq_id, positions = sequence_info(row_index, bounds)
     first_start = row_index[0] - positions[0]
     last_row = my_start + rows_dev - 1
     cosine, sine = rotary_tables(positions)
-    full_params = lax.all_gather(params, ("group", "span"), axis=0, tiled=True)
-    weights = unpack(full_params)
+    if fast:
+        weights = fast_weights(params)
+    else:
+        weights = unpack(lax.all_gather(params, group + span, axis=0, tiled=True))
     small_f32 = {name_key: weights[name_key].astype(jnp.float32) for name_key in small_names}
     x_rows = tokens.astype(jnp.float32)
-    normed_one, norm_one_back = jax.vjp(rms_norm, x_rows, small_f32["norm_attn"])
+    normed_one, norm_one_back = jax.vjp(rms_norm, x_rows, small_f32[NORM_ATTN])
     hidden = normed_one.astype(jnp.bfloat16)
-    query = matmul(hidden, weights["w_query"])
-    key_raw = matmul(hidden, weights["w_key"])
-    value_low = matmul(hidden, weights["w_value"]).astype(jnp.bfloat16)
+    query = matmul(hidden, weights[W_QUERY])
+    key_raw = matmul(hidden, weights[W_KEY])
+    value_low = matmul(hidden, weights[W_VALUE]).astype(jnp.bfloat16)
     q_rot = rotate(query, cosine, sine, HEADS_Q).astype(jnp.bfloat16)
     k_rot = rotate(key_raw, cosine, sine, HEADS_KV).astype(jnp.bfloat16)
     q_heads = q_rot.reshape(rows_dev, HEADS_KV, group_ratio, HEAD_DIM)
@@ -351,8 +881,8 @@
     running_max, running_sum, accum = over_blocks(
         initial,
         (
-            lax.all_gather(k_rot, "span", axis=0, tiled=True),
-            lax.all_gather(value_low, "span", axis=0, tiled=True),
+            lax.all_gather(k_rot, span, axis=0, tiled=True),
+            lax.all_gather(value_low, span, axis=0, tiled=True),
         ),
         forward_step,
     )
@@ -361,20 +891,20 @@
     attended = (
         attn_f32.transpose(2, 0, 1, 3).reshape(rows_dev, HEADS_Q * HEAD_DIM).astype(jnp.bfloat16)
     )
-    attn_out = matmul(attended, weights["w_attn_out"])
-    gate_ssm = matmul(hidden, weights["w_gate_ssm"])
+    attn_out = matmul(attended, weights[W_ATTN_OUT])
+    gate_ssm = matmul(hidden, weights[W_GATE_SSM])
     xbc = jnp.concatenate(
-        [matmul(hidden, weights["w_x_ssm"]), matmul(hidden, weights["w_b_c"])], axis=1
-    )
-    step_raw = matmul(hidden, weights["w_step"])
-    rim_rows = passed_along(xbc[rows_dev - (CONV - 1) :], "span", 1)
+        [matmul(hidden, weights[W_X_SSM]), matmul(hidden, weights[W_B_C])], axis=1
+    )
+    step_raw = matmul(hidden, weights[W_STEP])
+    rim_rows = passed_along(xbc[rows_dev - (CONV - 1) :], span, 1)
     extended = jnp.concatenate([rim_rows, xbc], axis=0)
 
     def conv_local(extended_in, conv_weight, conv_bias):
         return conv_apply(extended_in, conv_weight, conv_bias, positions)
 
     conv_values, conv_back = jax.vjp(
-        conv_local, extended, small_f32["conv_weight"], small_f32["conv_bias"]
+        conv_local, extended, small_f32[CONV_WEIGHT], small_f32[CONV_BIAS]
     )
 
     def ssd_full(conv_in, step_in, step_bias, decay_log, skip_gain, state_in):
@@ -391,31 +921,31 @@
         )
 
     x_ssm, b_in, c_in = split_conv(conv_values)
-    step_size = jax.nn.softplus(step_raw + small_f32["step_bias"][None, :])
-    decay = -jnp.exp(small_f32["decay_log"])
+    step_size = jax.nn.softplus(step_raw + small_f32[STEP_BIAS][None, :])
+    decay = -jnp.exp(small_f32[DECAY_LOG])
     carry_all, local_state = ssd_summary(x_ssm, b_in, step_size, decay, seq_id, positions)
     state_ident = (jnp.ones_like(carry_all), jnp.zeros_like(local_state))
-    _, state_in = prefix((carry_all, local_state), "span", chain_states, state_ident)
+    _, state_in = prefix((carry_all, local_state), span, chain_states, state_ident)
     (ssm_y, _), ssd_back = jax.vjp(
         ssd_full,
         conv_values,
         step_raw,
-        small_f32["step_bias"],
-        small_f32["decay_log"],
-        small_f32["skip_gain"],
+        small_f32[STEP_BIAS],
+        small_f32[DECAY_LOG],
+        small_f32[SKIP_GAIN],
         state_in,
     )
-    normed_ssm, gnorm_back = jax.vjp(gated_norm, ssm_y, gate_ssm, small_f32["norm_ssm"])
+    normed_ssm, gnorm_back = jax.vjp(gated_norm, ssm_y, gate_ssm, small_f32[NORM_SSM])
     ssm_low = normed_ssm.astype(jnp.bfloat16)
-    ssm_out = matmul(ssm_low, weights["w_ssm_out"])
+    ssm_out = matmul(ssm_low, weights[W_SSM_OUT])
     middle = x_rows + attn_out + ssm_out
-    normed_two, norm_two_back = jax.vjp(rms_norm, middle, small_f32["norm_ffn"])
+    normed_two, norm_two_back = jax.vjp(rms_norm, middle, small_f32[NORM_FFN])
     hidden_two = normed_two.astype(jnp.bfloat16)
-    gate_ffn = matmul(hidden_two, weights["w_gate"])
-    upper = matmul(hidden_two, weights["w_up_proj"])
+    gate_ffn = matmul(hidden_two, weights[W_GATE])
+    upper = matmul(hidden_two, weights[W_UP_PROJ])
     activation_f32, swiglu_back = jax.vjp(swiglu, gate_ffn, upper)
     activation = activation_f32.astype(jnp.bfloat16)
-    ffn_out = matmul(activation, weights["w_down"])
+    ffn_out = matmul(activation, weights[W_DOWN])
     result = middle + ffn_out
     squares = jnp.stack(
         [
@@ -425,27 +955,22 @@
             jnp.sum(ffn_out * ffn_out),
         ]
     )
-    totals = lax.psum(squares, ("group", "span"))
+    totals = lax.psum(squares, group + span)
     stats = jnp.sqrt(totals / (all_rows * D))
-    back_weights = unpack(lax.all_gather(params, ("group", "span"), axis=0, tiled=True))
+    back_weights = weights
     grad_out = cotangent.astype(jnp.float32)
-    grad_w_down = matmul_left_t(activation, cotangent)
-    grad_activation = matmul_right_t(cotangent, back_weights["w_down"])
+    grad_activation = matmul_right_t(cotangent, back_weights[W_DOWN])
     grad_gate_f32, grad_upper_f32 = swiglu_back(grad_activation)
     grad_gate = grad_gate_f32.astype(jnp.bfloat16)
     grad_upper = grad_upper_f32.astype(jnp.bfloat16)
-    grad_w_gate = matmul_left_t(hidden_two, grad_gate)
-    grad_w_up = matmul_left_t(hidden_two, grad_upper)
-    grad_hidden_two = matmul_right_t(grad_gate, back_weights["w_gate"]) + matmul_right_t(
-        grad_upper, back_weights["w_up_proj"]
+    grad_hidden_two = matmul_right_t(grad_gate, back_weights[W_GATE]) + matmul_right_t(
+        grad_upper, back_weights[W_UP_PROJ]
     )
     grad_middle_norm, grad_norm_ffn = norm_two_back(grad_hidden_two)
     grad_middle = grad_out + grad_middle_norm
     grad_branch = grad_middle.astype(jnp.bfloat16)
-    grad_w_attn_out = matmul_left_t(attended, grad_branch)
-    grad_w_ssm_out = matmul_left_t(ssm_low, grad_branch)
-    grad_attended = matmul_right_t(grad_branch, back_weights["w_attn_out"]).astype(jnp.bfloat16)
-    grad_ssm_low = matmul_right_t(grad_branch, back_weights["w_ssm_out"])
+    grad_attended = matmul_right_t(grad_branch, back_weights[W_ATTN_OUT]).astype(jnp.bfloat16)
+    grad_ssm_low = matmul_right_t(grad_branch, back_weights[W_SSM_OUT])
     grad_ssm_y, grad_gate_ssm_f32, grad_norm_ssm = gnorm_back(grad_ssm_low)
     cumul = jnp.cumsum(step_size * decay[None, :], axis=0)
     entry_decay = ssd_entry(cumul, seq_id, positions)
@@ -453,26 +978,23 @@
     grad_state_local = jnp.einsum(
         "thp,tn,th->hpn", grad_y_heads, c_in, entry_decay, precision=highest
     )
-    _, grad_state_out = carried_in((carry_all, grad_state_local), "span", chain_states, state_ident)
+    _, grad_state_out = carried_in((carry_all, grad_state_local), span, chain_states, state_ident)
     grad_conv_values, grad_step_raw_f32, grad_step_bias, grad_decay_log, grad_skip_gain, _ = (
         ssd_back((grad_ssm_y, grad_state_out))
     )
     grad_extended, grad_conv_weight, grad_conv_bias = conv_back(grad_conv_values)
-    rim_back = passed_along(grad_extended[: CONV - 1], "span", -1)
+    rim_back = passed_along(grad_extended[: CONV - 1], span, -1)
     grad_xbc_f32 = grad_extended[CONV - 1 :]
     grad_xbc_f32 = grad_xbc_f32.at[rows_dev - (CONV - 1) :].add(rim_back)
     grad_xbc = grad_xbc_f32.astype(jnp.bfloat16)
     grad_gate_ssm = grad_gate_ssm_f32.astype(jnp.bfloat16)
     grad_step_raw = grad_step_raw_f32.astype(jnp.bfloat16)
-    grad_w_gate_ssm = matmul_left_t(hidden, grad_gate_ssm)
-    grad_w_x_ssm = matmul_left_t(hidden, grad_xbc[:, :ssm_inner])
-    grad_w_b_c = matmul_left_t(hidden, grad_xbc[:, ssm_inner:])
     grad_w_step = matmul_left_t(hidden, grad_step_raw)
     grad_hidden_ssm = (
-        matmul_right_t(grad_gate_ssm, back_weights["w_gate_ssm"])
-        + matmul_right_t(grad_xbc[:, :ssm_inner], back_weights["w_x_ssm"])
-        + matmul_right_t(grad_xbc[:, ssm_inner:], back_weights["w_b_c"])
-        + matmul_right_t(grad_step_raw, back_weights["w_step"])
+        matmul_right_t(grad_gate_ssm, back_weights[W_GATE_SSM])
+        + matmul_right_t(grad_xbc[:, :ssm_inner], back_weights[W_X_SSM])
+        + matmul_right_t(grad_xbc[:, ssm_inner:], back_weights[W_B_C])
+        + matmul_right_t(grad_step_raw, back_weights[W_STEP])
     )
     grad_heads = grad_attended.reshape(rows_dev, HEADS_KV, group_ratio, HEAD_DIM).transpose(
         1, 2, 0, 3
@@ -519,82 +1041,86 @@
     grad_query_all, grad_keys_all, grad_values_all = over_blocks(
         initial_back,
         (
-            lax.all_gather(k_rot, "span", axis=0, tiled=True),
-            lax.all_gather(value_low, "span", axis=0, tiled=True),
+            lax.all_gather(k_rot, span, axis=0, tiled=True),
+            lax.all_gather(value_low, span, axis=0, tiled=True),
         ),
         backward_step,
     )
     grad_keys_mine, grad_values_mine = (
         lax.psum_scatter(
-            grad_keys_all.astype(jnp.bfloat16), "span", scatter_dimension=0, tiled=True
+            grad_keys_all.astype(jnp.bfloat16), span, scatter_dimension=0, tiled=True
         ).astype(jnp.float32),
         lax.psum_scatter(
-            grad_values_all.astype(jnp.bfloat16), "span", scatter_dimension=0, tiled=True
+            grad_values_all.astype(jnp.bfloat16), span, scatter_dimension=0, tiled=True
         ).astype(jnp.float32),
     )
     grad_q_rot = grad_query_all.transpose(2, 0, 1, 3).reshape(rows_dev, HEADS_Q * HEAD_DIM)
     grad_query_low = rotate(grad_q_rot, cosine, -sine, HEADS_Q).astype(jnp.bfloat16)
     grad_key_low = rotate(grad_keys_mine, cosine, -sine, HEADS_KV).astype(jnp.bfloat16)
     grad_value_low = grad_values_mine.astype(jnp.bfloat16)
-    grad_w_query = matmul_left_t(hidden, grad_query_low)
-    grad_w_key = matmul_left_t(hidden, grad_key_low)
-    grad_w_value = matmul_left_t(hidden, grad_value_low)
     grad_hidden = (
         grad_hidden_ssm
-        + matmul_right_t(grad_query_low, back_weights["w_query"])
-        + matmul_right_t(grad_key_low, back_weights["w_key"])
-        + matmul_right_t(grad_value_low, back_weights["w_value"])
+        + matmul_right_t(grad_query_low, back_weights[W_QUERY])
+        + matmul_right_t(grad_key_low, back_weights[W_KEY])
+        + matmul_right_t(grad_value_low, back_weights[W_VALUE])
     )
     grad_x_norm, grad_norm_attn = norm_one_back(grad_hidden)
     grad_tokens = grad_middle + grad_x_norm
-    grad_dict = {
-        "norm_attn": grad_norm_attn,
-        "w_query": grad_w_query,
-        "w_key": grad_w_key,
-        "w_value": grad_w_value,
-        "w_attn_out": grad_w_attn_out,
-        "w_gate_ssm": grad_w_gate_ssm,
-        "w_x_ssm": grad_w_x_ssm,
-        "w_b_c": grad_w_b_c,
-        "w_step": grad_w_step,
-        "conv_weight": grad_conv_weight,
-        "conv_bias": grad_conv_bias,
-        "step_bias": grad_step_bias,
-        "decay_log": grad_decay_log,
-        "skip_gain": grad_skip_gain,
-        "norm_ssm": grad_norm_ssm,
-        "w_ssm_out": grad_w_ssm_out,
-        "norm_ffn": grad_norm_ffn,
-        "w_gate": grad_w_gate,
-        "w_up_proj": grad_w_up,
-        "w_down": grad_w_down,
+    small = {
+        NORM_ATTN: grad_norm_attn,
+        W_STEP: grad_w_step,
+        CONV_WEIGHT: grad_conv_weight,
+        CONV_BIAS: grad_conv_bias,
+        STEP_BIAS: grad_step_bias,
+        DECAY_LOG: grad_decay_log,
+        SKIP_GAIN: grad_skip_gain,
+        NORM_SSM: grad_norm_ssm,
+        NORM_FFN: grad_norm_ffn,
     }
+    pairs = {
+        W_QUERY: (hidden, grad_query_low),
+        W_KEY: (hidden, grad_key_low),
+        W_VALUE: (hidden, grad_value_low),
+        W_ATTN_OUT: (attended, grad_branch),
+        W_GATE_SSM: (hidden, grad_gate_ssm),
+        W_X_SSM: (hidden, grad_xbc[:, :ssm_inner]),
+        W_B_C: (hidden, grad_xbc[:, ssm_inner:]),
+        W_SSM_OUT: (ssm_low, grad_branch),
+        W_GATE: (hidden_two, grad_gate),
+        W_UP_PROJ: (hidden_two, grad_upper),
+        W_DOWN: (activation, cotangent),
+    }
+    if fast:
+        return (result.astype(jnp.bfloat16), grad_tokens, fast_gradients(small, pairs), stats)
+    grad_dict = dict(small)
+    for name_key, (left, right) in pairs.items():
+        grad_dict[name_key] = matmul_left_t(left, right)
     flat_parts = [grad_dict[name_key].reshape(-1) for name_key, extent in layout()]
     used_entries = 0
     for part_array in flat_parts:
         used_entries += part_array.shape[0]
-    flat_parts.append(jnp.zeros((full_params.shape[0] - used_entries,), jnp.float32))
+    flat_parts.append(jnp.zeros((params.shape[0] * lax.axis_size(group + span) - used_entries,), jnp.float32))
     grad_shard = lax.psum_scatter(
-        jnp.concatenate(flat_parts), ("group", "span"), scatter_dimension=0, tiled=True
+        jnp.concatenate(flat_parts), group + span, scatter_dimension=0, tiled=True
     )
     return (result.astype(jnp.bfloat16), grad_tokens, grad_shard, stats)
 
 
 def solution(mesh):
+    fast = (mesh.shape["group"], mesh.shape["span"]) == FAST
+    if fast:
+        mesh = Mesh(mesh.devices.reshape(4, 2, 2, 2), GRID)
+        group, span = (GRID[:1], GRID[1:])
+    else:
+        group, span = (("group",), ("span",))
+
+    def program(tokens, params, cotangent, offsets):
+        return body(span, group, fast, tokens, params, cotangent, offsets)
+
     return jax.shard_map(
-        body,
+        program,
         mesh=mesh,
-        in_specs=(
-            P(("group", "span"), None),
-            P(("group", "span")),
-            P(("group", "span"), None),
-            P("group", None),
-        ),
-        out_specs=(
-            P(("group", "span"), None),
-            P(("group", "span"), None),
-            P(("group", "span")),
-            P(),
-        ),
+        in_specs=(P(group + span, None), P(group + span), P(group + span, None), P(group, None)),
+        out_specs=(P(group + span, None), P(group + span, None), P(group + span), P()),
         check_vma=False,
     )

time: 2450 us -> 1310 us (0.53); the launches traced: 2410 us -> 1300 us
  waiting for transfers between devices: 1100 us -> 335 us
  local copies, waits for them, and re-layouts: 657 us -> 103 us
  starting transfers between devices: 3.96 us -> 277 us
  other arithmetic: 280 us -> 149 us
  Pallas kernels: 0 us -> 87.4 us
  matrix products: 256 us -> 222 us
    unnamed x9 -> x6, waiting for transfers between devices: 678 us -> 0.1 us
    concatenate x1 -> x2, local copies, waits for them, and re-layouts: 410 us -> 2.61 us  [the longest x1 1.33 us: fast_gradients(): jnp.concatenate([jnp.zeros((14 * LINE,), jnp.float32), tail, small[NORM_F...]
    all_gather x3 -> x2, waiting for transfers between devices: 270 us -> 0.01 us  [the longest x1 0.01 us: body(): lax.all_gather(value_low, span, axis=0, tiled=True)]
    ppermute x0 -> x73, waiting for transfers between devices: none -> 231 us  [the longest x4 65.1 us: reduce_lines(): half = added(home, lax.ppermute(away, first_axis, SWAP))]
    ppermute x0 -> x73, starting transfers between devices: none -> 227 us  [the longest x2 71.4 us: reduce_lines(): handed = lax.ppermute(other, ZC, holders)]
    all_gather x1 -> x0, other arithmetic: 152 us -> none  [body(): full_params = lax.all_gather(params, ('group', 'span'), axis=0, tiled=True)]
    unnamed x309 -> x359, local copies, waits for them, and re-layouts: 115 us -> 23.6 us
    pallas_call x0 -> x5, Pallas kernels: none -> 87.4 us  [the longest x3 46.3 us: pack_lines(): pl.pallas_call(kernel, grid=(total,), in_specs=[left_spec(k) for k in ran...]
  transfers between devices with their start and end apart: 10 -> 81, of which waited for: 5 -> 20; matrix products, arithmetic and copies ran while one was open for 12% -> 19% of each run, Pallas kernels for 0% -> 6%
where the time goes in v1:
time: 1310 us; the launch traced here: 1300 us
  waiting for transfers between devices  335 us (26%)
  starting transfers between devices  277 us (21%)
  matrix products  222 us (17%)
  other arithmetic  149 us (11%)
  local copies, waits for them, and re-layouts  103 us (8%)
  blocking collectives  92.4 us (7%)
  Pallas kernels  87.4 us (7%)
  between operations  20.3 us (2%)
  loops' own time  13.3 us (1%)
    dot_general x3, matrix products, ssd_output(): jnp.einsum('hts,shp->thp', kernel * inner_products[None], scaled_x, preci...  84.7 us
    psum x1, blocking collectives, body(): totals = lax.psum(squares, group + span)  84.1 us
    reduce_scatter x1, waiting for transfers between devices, body(): lax.psum_scatter(grad_keys_all.astype(jnp.bfloat16), span, scatter_dimens...  72.9 us
    ppermute x2, starting transfers between devices, reduce_lines(): handed = lax.ppermute(other, ZC, holders)  71.4 us
    ppermute x4, waiting for transfers between devices, reduce_lines(): half = added(home, lax.ppermute(away, first_axis, SWAP))  65.1 us
    ppermute x2, starting transfers between devices, passed_along(): lax.ppermute(value, axis, [(source, source + steps) for source in range(f...  49.4 us
    pallas_call x3, Pallas kernels, pack_lines(): pl.pallas_call(kernel, grid=(total,), in_specs=[left_spec(k) for k in ran...  46.3 us
    ppermute x16, starting transfers between devices, gather_lines(): buffers += local + [lax.ppermute(piece, 'c', SWAP) for piece in local]  42 us
  transfers between devices with their start and end apart: 81, of which 20 were waited for; matrix products, arithmetic and copies ran while one was open for 19% of the time, Pallas kernels for 6%

profile of v1, /device:TPU:0, one launch (start us, length us, event | category | flops | bytes accessed | tf_op | source)
XLA Modules:
  0.0 1298.3 jit_solution(5008584756894861747)
XLA Ops:
  8.4 7.7 collective-permute-start
  28.3 6.8 collective-permute-start.24
  56.8 12.2 collective-permute-done.26
  82.5 13.6 %collective-permute-start.19 = (bf16[3088,128]{1,0:T(8,128)(2,1)}, bf16[3088,128]{1,0:T(8,128)(2,1)S(1)}, u32[]{:S(2)}, u32[]{:S(2)}) collective-permute-start(bf16[3088,128]{1,0:T(8,128)(2,1)} %get-tuple-element.1054.refs_8_), channel_id=1, source_target_pairs={{0,1},{1,0},{2,3},{3,2},{4,5},{5,4},{6,7},{7,6},{8,9},{9,8},{10,11... | collective-permute-start | bytes 2371592 | tf_op jit(solution)/shard_map/ppermute | solution.py:323
  104.9 20.8 %collective-permute-start.21 = (bf16[3088,128]{1,0:T(8,128)(2,1)}, bf16[3088,128]{1,0:T(8,128)(2,1)S(1)}, u32[]{:S(2)}, u32[]{:S(2)}) collective-permute-start(bf16[3088,128]{1,0:T(8,128)(2,1)} %collective-permute-done.17.refs_10_), channel_id=1, source_target_pairs={{0,1},{1,0},{2,3},{3,2},{4,5},{5,4},{6,7},{7,6},{8,9},{9,8},{10,11... | collective-permute-start | bytes 2371592 | tf_op jit(solution)/shard_map/ppermute | solution.py:323
  134.4 10.9 collective-permute-done.7.refs_3_
  151.3 14.5 %unpack.2 = (bf16[1024,512]{1,0:T(8,128)(2,1)}, bf16[1024,128]{1,0:T(8,128)(2,1)S(1)}, bf16[1024,128]{1,0:T(8,128)(2,1)S(1)}, bf16[512,1024]{1,0:T(8,128)(2,1)},...) custom-call(s32[25,5]{1,0:T(8,128)S(1)} %copy-done.29, ...), custom_call_target="tpu_custom_call" | custom-call | bytes 26624000 | tf_op jit(solution)/shard_map/unpack/pallas_call | solution.py:464
  189.4 9.4 collective-permute-start.23
  230.0 19.5 %collective-permute-done.40.refs_26_ = bf16[3088,128]{1,0:T(8,128)(2,1)S(1)} collective-permute-done((bf16[3088,128]{1,0:T(8,128)(2,1)}, bf16[3088,128]{1,0:T(8,128)(2,1)S(1)}, u32[]{:S(2)}, u32[]{:S(2)}) %collective-permute-start.40) | collective-permute-done | bytes 790560 | tf_op jit(solution)/shard_map/ppermute | solution.py:317
  252.4 22.3 %collective-permute-done.39.refs_25_ = bf16[3088,128]{1,0:T(8,128)(2,1)} collective-permute-done((bf16[3088,128]{1,0:T(8,128)(2,1)}, bf16[3088,128]{1,0:T(8,128)(2,1)}, u32[]{:S(2)}, u32[]{:S(2)}) %collective-permute-start.39) | collective-permute-done | bytes 790560 | tf_op jit(solution)/shard_map/ppermute | solution.py:316
  275.4 20.9 %collective-permute-done.41.refs_27_ = bf16[3088,128]{1,0:T(8,128)(2,1)} collective-permute-done((bf16[3088,128]{1,0:T(8,128)(2,1)S(1)}, bf16[3088,128]{1,0:T(8,128)(2,1)}, u32[]{:S(2)}, u32[]{:S(2)}) %collective-permute-start.41) | collective-permute-done | bytes 790560 | tf_op jit(solution)/shard_map/ppermute | solution.py:321
  307.5 8.3 all-gather.2
  320.4 26.7 %unpack.3 = (bf16[1536,1024]{1,0:T(8,128)(2,1)}, bf16[1024,2048]{1,0:T(8,128)(2,1)}, bf16[1024,2048]{1,0:T(8,128)(2,1)}, bf16[2048,1024]{1,0:T(8,128)(2,1)}, bf16[16,128]{1,0:T(8,128)(2,1)S(1)}) custom-call(s32[31,5]{1,0:T(8,128)S(1)} %copy-done.28, s32[32]{0:T(128)S(1)} %fusion.179.where_ref, bf16[3088,128]{1,0:T(8,128)(2,1)S(1)} %get-tuple-element.1056.refs_0_, ...), custom_call_target="tpu_custom_call" | custom-call | bytes 33013760 | tf_op jit(solution)/shard_map/unpack/pallas_call | solution.py:464
  362.4 17.6 %while.62 = (s32[]{:T(128)}, f32[2,4,512]{2,1,0:T(4,128)S(1)}, f32[2,4,512]{2,1,0:T(4,128)S(1)}, f32[2,4,512,64]{2,3,1,0:T(8,128)S(1)}, s32[8]{0:T(128)S(1)}, /*...) while((s32[]{:T(128)}, f32[2,4,512]{2,1,0:T(4,128)S(1)}, ...), condition=%wide.region_9.10_spmd.clone, body=%wide.region_3.9_spmd.clone.sunk | while | flops 561264128 | bytes 29909380 | solution.py:844
  364.2 6.6 conditional.6
  386.4 9.8 while.64
  400.3 29.6 %fusion.61 = f32[512,24,64]{0,2,1:T(8,128)} fusion(f32[512,24,64]{0,2,1:T(8,128)S(1)} %bitcast.487, f32[512,24,64]{0,2,1:T(8,128)S(1)} %fusion.126, f32[512,512]{1,0:T(8,128)S(1)} %copy-done.88, f32[24,512]{1,0:T(8,128)S(1)} %copy-done.127, pred[512,512]{1,0:T(8,128)(4,1)S(1)} %copy-done.109, f32[24]{0:T(128)S(1)} %copy-done.157, ...), kind=kOutput, calls=%fused_computation.124 | convolution fusion | flops 4854644736 | bytes 10895456 | tf_op jit(solution)/shard_map/jvp(hts,shp->thp)/dot_general | solution.py:246
  433.6 6.8 multiply_reduce_fusion.11
  451.5 7.0 fusion.49
  479.1 84.1 %psum.7 = f32[4]{0:T(128)} all-reduce(f32[4]{0:T(128)S(1)} %pad_maximum_fusion.13), channel_id=1, replica_groups=mesh['z'=4,'y'=2,'x'=2,'c'=2] {'z','y','x','c'}, use_global_device_ids=true, to_apply=%region_58.59 | all-reduce | flops 4 | bytes 32 | tf_op jit(solution)/shard_map/psum | solution.py:958
  563.2 8.8 multiply_reduce_fusion.7
  580.3 33.2 %fusion.36 = (f32[24,512]{1,0:T(8,128)}, f32[24,512]{1,0:T(8,128)}, f32[512,512]{1,0:T(8,128)}) fusion(f32[512,512]{1,0:T(8,128)S(1)} %copy-done.89, f32[24,512]{1,0:T(8,128)S(1)} %copy-done.127, pred[512,512]{1,0:T(8,128)(4,1)} %fusion.116, f32[24,64,512]{2,1,0:T(8,128)S(1)} %bitcast.480, f32[512,24,64]{0,2,1:T(8,128)S(1)} %bitcast.488, ...), kind=kOutput, calls=%fused_computation.59 | convolution fusion | flops 4888961024 | bytes 8847360 | tf_op jit(solution)/shard_map/transpose(jvp(hts,shp->thp))/dot_general | solution.py:246
  617.7 34.0 %while.63 = (s32[]{:T(128)}, f32[2,4,512,64]{2,3,1,0:T(8,128)}, f32[4096,128]{0,1:T(8,128)}, f32[4096,128]{0,1:T(8,128)}, s32[8]{0:T(128)S(1)}, /*index=5*/s32[]...) while((s32[]{:T(128)}, f32[2,4,512,64]{2,3,1,0:T(8,128)}, ...), condition=%wide.region_37.38_spmd.clone, body=%wide.region_33.37_spmd.clone.sunk | while | flops 1364661760 | bytes 63644160 | solution.py:844
  619.4 23.2 %conditional.7 = ((f32[2,4,512,64]{2,3,1,0:T(8,128)}, f32[4096,128]{0,1:T(8,128)}, f32[4096,128]{0,1:T(8,128)})) conditional(s32[]{:T(128)} %convert_element_type.746, (f32[2,4,512,64]{2,3,1,0:T(8,128)}, f32[4096,128]{0,1:T(8,128)}, f32[4096,128]{0,1:T(8,128)}) %tuple.254, (s32[512]{0:T(512)S(1)}, s32[]{:T(128)}, s32[4]{0:T(128)S(1)}, s32[]{:T(128)}, ...), branch_computations={%region_34.34_spmd, %region_35.36_spmd} | conditional | flops 1364661760 | bytes 63641732 | solution.py:842
  681.7 6.5 pad_maximum_fusion.1
  688.2 20.6 %pack.5 = bf16[49344,128]{1,0:T(8,128)(2,1)} custom-call(bf16[512,1024]{1,0:T(8,128)(2,1)S(1)} %copy-done.21, bf16[512,2048]{1,0:T(8,128)(2,1)S(1)} %copy-done.31, bf16[512,2048]{1,0:T(8,128)(2,1)} %get-tuple-element.1092.refs_2_, bf16[512,2048]{1,0:T(8,128)(2,1)} %get-tuple-element.1093.refs_3_, bf16[512,1024]{1,0:T(8,128)(2,1)S(1)} %copy-done.19, ...), custom_call_target="tpu_custom_call" | custom-call | flops 6442450944 | bytes 16777216 | tf_op jit(solution)/shard_map/pack/pallas_call | solution.py:618
  708.8 6.0 constant_dynamic-slice_fusion.4
  714.8 22.5 %collective-permute-start.61 = (bf16[24688,128]{1,0:T(8,128)(2,1)}, bf16[24688,128]{1,0:T(8,128)(2,1)}, u32[]{:S(2)}, u32[]{:S(2)}) collective-permute-start(bf16[24688,128]{1,0:T(8,128)(2,1)} %constant_dynamic-slice_fusion.4), channel_id=1, source_target_pairs={{0,1},{1,0},{2,3},{3,2},{4,5},{5,4},{6,7},{7,6},{8,9},{9,8},{10,11... | collective-permute-start | bytes 18960392 | tf_op jit(solution)/shard_map/ppermute | solution.py:655
  756.5 22.0 %fusion.31 = f32[24,64,512]{2,1,0:T(8,128)} fusion(f32[24,64,512]{2,1,0:T(8,128)S(1)} %bitcast.482, f32[512,512]{1,0:T(8,128)S(1)} %copy-done.90, f32[24,512]{1,0:T(8,128)S(1)} %copy-done.128, pred[512,512]{1,0:T(8,128)(4,1)S(1)} %copy-done.110), kind=kOutput, calls=%fused_computation.56 | convolution fusion | flops 4850712576 | bytes 7651328 | tf_op jit(solution)/shard_map/transpose(jvp(hts,shp->thp))/dot_general | solution.py:246
  778.5 72.9 %reduce-scatter.3.cloned.1.call-done = bf16[512,128]{0,1:T(8,128)(2,1)} async-done(((bf16[4096,128]{0,1:T(8,128)(2,1)}), bf16[512,128]{0,1:T(8,128)(2,1)}) %reduce-scatter.3.cloned.1.call-update) | async-done | bytes 131088 | tf_op jit(solution)/shard_map/reduce_scatter | solution.py:1050
  854.3 31.1 %all-gather.14.cloned.1.call-done = bf16[192,64,128]{2,1,0:T(8,128)(2,1)} async-done(((bf16[24,64,128]{2,1,0:T(8,128)(2,1)}), bf16[192,64,128]{2,1,0:T(8,128)(2,1)}) %all-gather.14.cloned.1.call-update) | async-done | bytes 3145744 | tf_op jit(solution)/shard_map/all_gather | solution.py:92
  885.4 15.4 %while.65 = (s32[]{:T(128)}, f32[24,64,128]{2,1,0:T(8,128)S(1)}, s32[]{:T(128)}, bf16[8,24]{1,0:T(8,128)(2,1)}, bf16[8,24,64,128]{3,2,1,0:T(8,128)(2,1)}, /*index=5*/s32[]{:T(128)}, s32[]{:T(128)}, s32[]{:T(128)}, s32[]{:T(128)}) while((s32[]{:T(128)}, f32[24,64,128]{2,1,0:T(8,128)S(1)}, s32[]{:T(128)}, ...), condition=%wide.region_20.21_spmd.clone, body=%wide.region_19.20_spmd.clone.sunk | while | flops 983072 | bytes 1966487 | solution.py:110
  901.1 7.1 fusion.108
  908.3 7.3 multiply_reduce_fusion.5
  928.8 10.2 multiply_reduce_fusion.3
  940.7 40.0 %collective-permute-start.46 = (f32[3,1792]{1,0:T(4,128)S(1)}, f32[3,1792]{1,0:T(4,128)S(1)}, u32[]{:S(2)}, u32[]{:S(2)}) collective-permute-start(f32[3,1792]{1,0:T(4,128)S(1)} %pad_add_fusion.1), channel_id=1, source_target_pairs={{1,0},{2,1},{3,2},{4,3},{5,4},{6,5},{7,6},{9,8},{10,9},{11,10},{12... | collective-permute-start | bytes 64520 | tf_op jit(solution)/shard_map/ppermute | solution.py:63
  1001.6 6.4 fusion.79
  1008.0 21.0 %pack.4 = bf16[49440,128]{1,0:T(8,128)(2,1)} custom-call(bf16[512,1024]{1,0:T(8,128)(2,1)S(1)} %copy-done.1, bf16[512,512]{1,0:T(8,128)(2,1)S(1)} %copy.137.refs_1_, bf16[512,512]{1,0:T(8,128)(2,1)S(1)} %copy-done.14, bf16[512,128]{1,0:T(8,128)(2,1)S(1)} %copy.139.refs_3_, bf16[512,128]{1,0:T(8,128)(2,1)S(1)} %copy-done.25, ...), custom_call_target="tpu_custom_call", output_to_operand_aliasing={{}: (11, {})} | custom-call | flops 4831838208 | bytes 20447232 | tf_op jit(solution)/shard_map/pack/pallas_call | solution.py:618
  1029.1 7.3 add_convert_fusion
  1041.9 32.9 %collective-permute-done.68 = bf16[2,3104,128]{2,1,0:T(8,128)(2,1)S(1)} collective-permute-done((bf16[2,3104,128]{2,1,0:T(8,128)(2,1)S(1)}, bf16[2,3104,128]{2,1,0:T(8,128)(2,1)S(1)}, u32[]{:S(2)}, u32[]{:S(2)}) %collective-permute-start.68) | collective-permute-done | bytes 1589280 | tf_op jit(solution)/shard_map/ppermute | solution.py:672
  1078.9 15.6 %collective-permute-done.69 = bf16[3104,128]{1,0:T(8,128)(2,1)S(1)} collective-permute-done((bf16[3104,128]{1,0:T(8,128)(2,1)S(1)}, bf16[3104,128]{1,0:T(8,128)(2,1)S(1)}, u32[]{:S(2)}, u32[]{:S(2)}) %collective-permute-start.69) | collective-permute-done | bytes 794656 | tf_op jit(solution)/shard_map/ppermute | solution.py:675
  1101.8 15.1 %collective-permute-done.70 = bf16[3104,128]{1,0:T(8,128)(2,1)S(1)} collective-permute-done((bf16[3104,128]{1,0:T(8,128)(2,1)S(1)}, bf16[3104,128]{1,0:T(8,128)(2,1)S(1)}, u32[]{:S(2)}, u32[]{:S(2)}) %collective-permute-start.70) | collective-permute-done | bytes 794656 | tf_op jit(solution)/shard_map/ppermute | solution.py:682
  1117.8 14.0 %collective-permute-done.64 = bf16[3104,128]{1,0:T(8,128)(2,1)S(1)} collective-permute-done((bf16[3104,128]{1,0:T(8,128)(2,1)S(1)}, bf16[3104,128]{1,0:T(8,128)(2,1)S(1)}, u32[]{:S(2)}, u32[]{:S(2)}) %collective-permute-start.64) | collective-permute-done | bytes 794656 | tf_op jit(solution)/shard_map/ppermute | solution.py:682
  1139.4 30.6 %collective-permute-done.54 = bf16[2,3104,128]{2,1,0:T(8,128)(2,1)S(1)} collective-permute-done((bf16[2,3104,128]{2,1,0:T(8,128)(2,1)S(1)}, bf16[2,3104,128]{2,1,0:T(8,128)(2,1)S(1)}, u32[]{:S(2)}, u32[]{:S(2)}) %collective-permute-start.54) | collective-permute-done | bytes 1589280 | tf_op jit(solution)/shard_map/ppermute | solution.py:672
  1176.0 12.3 collective-permute-done.55
  1194.6 7.1 collective-permute-start.50
  1208.2 67.5 %collective-permute-start.74 = (bf16[3104,128]{1,0:T(8,128)(2,1)S(1)}, bf16[3104,128]{1,0:T(8,128)(2,1)S(1)}, u32[]{:S(2)}, u32[]{:S(2)}) collective-permute-start(bf16[3104,128]{1,0:T(8,128)(2,1)S(1)} %get-tuple-element.999), channel_id=1, source_target_pairs={{0,1},{9,8},{16,17},{25,24},{2,3},{11,10},{18,19},{27,26},{4,5},{1... | collective-permute-start | bytes 2383880 | tf_op jit(solution)/shard_map/ppermute | solution.py:690
  1275.7 5.9 collective-permute-done.53
  (815 shorter events, 420.2 us)
Async XLA Ops:
  7.2 349.9 %all-gather.10.cloned.1.call-start = ((), (), s32[]{:S(2)}) async-start(), calls=%async_computation.3 | async-start | bytes 1179648 | tf_op jit(solution)/shard_map/all_gather | solution.py:885
  43.4 25.6 %collective-permute-start.26 = (bf16[3088,128]{1,0:T(8,128)(2,1)S(1)}, bf16[3088,128]{1,0:T(8,128)(2,1)}, u32[]{:S(2)}, u32[]{:S(2)}) collective-permute-start(bf16[3088,128]{1,0:T(8,128)(2,1)S(1)} %collective-permute-done.24), channel_id=1, source_target_pairs={{8,0},{17,9},{10,2},{19,11},{12,4},{21,13},{14,6},{23,15}} | collective-permute-start | bytes 2371592 | tf_op jit(solution)/shard_map/ppermute | solution.py:312
  48.4 21.3 %collective-permute-start.3 = (bf16[3088,128]{1,0:T(8,128)(2,1)S(1)}, bf16[3088,128]{1,0:T(8,128)(2,1)}, u32[]{:S(2)}, u32[]{:S(2)}) collective-permute-start(bf16[3088,128]{1,0:T(8,128)(2,1)S(1)} %collective-permute-done.1), channel_id=1, source_target_pairs={{8,16},{17,25},{10,18},{19,27},{12,20},{21,29},{14,22},{23,31}} | collective-permute-start | bytes 2371592 | tf_op jit(solution)/shard_map/ppermute | solution.py:307
  49.9 20.5 %collective-permute-start.15 = (bf16[3088,128]{1,0:T(8,128)(2,1)}, bf16[3088,128]{1,0:T(8,128)(2,1)}, u32[]{:S(2)}, u32[]{:S(2)}) collective-permute-start(bf16[3088,128]{1,0:T(8,128)(2,1)} %collective-permute-done.14), channel_id=1, source_target_pairs={{16,24},{18,26},{20,28},{22,30}} | collective-permute-start | bytes 2371592 | tf_op jit(solution)/shard_map/ppermute | solution.py:308
  56.1 21.0 %collective-permute-start.2 = (bf16[3088,128]{1,0:T(8,128)(2,1)S(1)}, bf16[3088,128]{1,0:T(8,128)(2,1)S(1)}, u32[]{:S(2)}, u32[]{:S(2)}) collective-permute-start(bf16[3088,128]{1,0:T(8,128)(2,1)S(1)} %get-tuple-element.1048), channel_id=1, source_target_pairs={{9,1},{11,3},{13,5},{15,7}} | collective-permute-start | bytes 2371592 | tf_op jit(solution)/shard_map/ppermute | solution.py:306
  75.5 20.6 %collective-permute-start.17 = (bf16[3088,128]{1,0:T(8,128)(2,1)}, bf16[3088,128]{1,0:T(8,128)(2,1)}, u32[]{:S(2)}, u32[]{:S(2)}) collective-permute-start(bf16[3088,128]{1,0:T(8,128)(2,1)} %get-tuple-element.1054.refs_8_), channel_id=1, source_target_pairs={{0,4},{4,0},{1,5},{5,1},{2,6},{6,2},{3,7},{7,3},{8,12},{12,8},{9,1... | collective-permute-start | bytes 2371592 | tf_op jit(solution)/shard_map/ppermute | solution.py:317
  81.3 23.6 %collective-permute-start.16 = (bf16[3088,128]{1,0:T(8,128)(2,1)}, bf16[3088,128]{1,0:T(8,128)(2,1)}, u32[]{:S(2)}, u32[]{:S(2)}) collective-permute-start(bf16[3088,128]{1,0:T(8,128)(2,1)} %get-tuple-element.1054.refs_8_), channel_id=1, source_target_pairs={{0,2},{2,0},{1,3},{3,1},{4,6},{6,4},{5,7},{7,5},{8,10},{10,8},{9,1... | collective-permute-start | bytes 2371592 | tf_op jit(solution)/shard_map/ppermute | solution.py:316
  81.9 43.8 %collective-permute-start.6 = (bf16[3088,128]{1,0:T(8,128)(2,1)S(1)}, bf16[3088,128]{1,0:T(8,128)(2,1)S(1)}, u32[]{:S(2)}, u32[]{:S(2)}) collective-permute-start(bf16[3088,128]{1,0:T(8,128)(2,1)S(1)} %get-tuple-element.1056.refs_0_), channel_id=1, source_target_pairs={{0,4},{4,0},{1,5},{5,1},{2,6},{6,2},{3,7},{7,3},{8,12},{12,8},{9,1... | collective-permute-start | bytes 2371592 | tf_op jit(solution)/shard_map/ppermute | solution.py:317
  82.5 47.4 %collective-permute-start.19 = (bf16[3088,128]{1,0:T(8,128)(2,1)}, bf16[3088,128]{1,0:T(8,128)(2,1)S(1)}, u32[]{:S(2)}, u32[]{:S(2)}) collective-permute-start(bf16[3088,128]{1,0:T(8,128)(2,1)} %get-tuple-element.1054.refs_8_), channel_id=1, source_target_pairs={{0,1},{1,0},{2,3},{3,2},{4,5},{5,4},{6,7},{7,6},{8,9},{9,8},{10,11... | collective-permute-start | bytes 2371592 | tf_op jit(solution)/shard_map/ppermute | solution.py:323
  96.1 33.9 %collective-permute-start.8 = (bf16[3088,128]{1,0:T(8,128)(2,1)S(1)}, bf16[3088,128]{1,0:T(8,128)(2,1)S(1)}, u32[]{:S(2)}, u32[]{:S(2)}) collective-permute-start(bf16[3088,128]{1,0:T(8,128)(2,1)S(1)} %get-tuple-element.1056.refs_0_), channel_id=1, source_target_pairs={{0,1},{1,0},{2,3},{3,2},{4,5},{5,4},{6,7},{7,6},{8,9},{9,8},{10,11... | collective-permute-start | bytes 2371592 | tf_op jit(solution)/shard_map/ppermute | solution.py:323
  97.6 32.9 %collective-permute-start.18 = (bf16[3088,128]{1,0:T(8,128)(2,1)}, bf16[3088,128]{1,0:T(8,128)(2,1)S(1)}, u32[]{:S(2)}, u32[]{:S(2)}) collective-permute-start(bf16[3088,128]{1,0:T(8,128)(2,1)} %collective-permute-done.17.refs_10_), channel_id=1, source_target_pairs={{0,2},{2,0},{1,3},{3,1},{4,6},{6,4},{5,7},{7,5},{8,10},{10,8},{9,1... | collective-permute-start | bytes 2371592 | tf_op jit(solution)/shard_map/ppermute | solution.py:321
  104.9 40.3 %collective-permute-start.21 = (bf16[3088,128]{1,0:T(8,128)(2,1)}, bf16[3088,128]{1,0:T(8,128)(2,1)S(1)}, u32[]{:S(2)}, u32[]{:S(2)}) collective-permute-start(bf16[3088,128]{1,0:T(8,128)(2,1)} %collective-permute-done.17.refs_10_), channel_id=1, source_target_pairs={{0,1},{1,0},{2,3},{3,2},{4,5},{5,4},{6,7},{7,6},{8,9},{9,8},{10,11... | collective-permute-start | bytes 2371592 | tf_op jit(solution)/shard_map/ppermute | solution.py:323
  125.7 19.5 %collective-permute-start.7 = (bf16[3088,128]{1,0:T(8,128)(2,1)S(1)}, bf16[3088,128]{1,0:T(8,128)(2,1)S(1)}, u32[]{:S(2)}, u32[]{:S(2)}) collective-permute-start(bf16[3088,128]{1,0:T(8,128)(2,1)S(1)} %collective-permute-done.5.refs_1_), channel_id=1, source_target_pairs={{0,4},{4,0},{1,5},{5,1},{2,6},{6,2},{3,7},{7,3},{8,12},{12,8},{9,1... | collective-permute-start | bytes 2371592 | tf_op jit(solution)/shard_map/ppermute | solution.py:319
  185.6 173.7 %all-gather.8.cloned.1.call-start = ((), (), s32[]{:S(2)}) async-start(), calls=%async_computation.2 | async-start | bytes 1179648 | tf_op jit(solution)/shard_map/all_gather | solution.py:884
  202.9 183.5 %all-gather.12.cloned.1.call-start = ((), (), s32[]{:S(2)}) async-start(), calls=%async_computation.6 | async-start | bytes 3538944 | tf_op jit(solution)/shard_map/all_gather | solution.py:69
  225.8 625.5 %reduce-scatter.3.cloned.1.call-start = ((), (), s32[]{:S(2)}) async-start(), calls=%async_computation.4 | async-start | bytes 1179648 | tf_op jit(solution)/shard_map/reduce_scatter | solution.py:1050
  225.9 23.6 %collective-permute-start.40 = (bf16[3088,128]{1,0:T(8,128)(2,1)}, bf16[3088,128]{1,0:T(8,128)(2,1)S(1)}, u32[]{:S(2)}, u32[]{:S(2)}) collective-permute-start(bf16[3088,128]{1,0:T(8,128)(2,1)} %get-tuple-element.1053.refs_24_), channel_id=1, source_target_pairs={{0,4},{4,0},{1,5},{5,1},{2,6},{6,2},{3,7},{7,3},{8,12},{12,8},{9,1... | collective-permute-start | bytes 2371592 | tf_op jit(solution)/shard_map/ppermute | solution.py:317
  227.3 23.6 %collective-permute-start.28 = (bf16[3088,128]{1,0:T(8,128)(2,1)}, bf16[3088,128]{1,0:T(8,128)(2,1)}, u32[]{:S(2)}, u32[]{:S(2)}) collective-permute-start(bf16[3088,128]{1,0:T(8,128)(2,1)} %get-tuple-element.1055.refs_16_), channel_id=1, source_target_pairs={{0,2},{2,0},{1,3},{3,1},{4,6},{6,4},{5,7},{7,5},{8,10},{10,8},{9,1... | collective-permute-start | bytes 2371592 | tf_op jit(solution)/shard_map/ppermute | solution.py:316
  228.7 46.0 %collective-permute-start.39 = (bf16[3088,128]{1,0:T(8,128)(2,1)}, bf16[3088,128]{1,0:T(8,128)(2,1)}, u32[]{:S(2)}, u32[]{:S(2)}) collective-permute-start(bf16[3088,128]{1,0:T(8,128)(2,1)} %get-tuple-element.1053.refs_24_), channel_id=1, source_target_pairs={{0,2},{2,0},{1,3},{3,1},{4,6},{6,4},{5,7},{7,5},{8,10},{10,8},{9,1... | collective-permute-start | bytes 2371592 | tf_op jit(solution)/shard_map/ppermute | solution.py:316
  229.3 45.5 %collective-permute-start.29 = (bf16[3088,128]{1,0:T(8,128)(2,1)}, bf16[3088,128]{1,0:T(8,128)(2,1)}, u32[]{:S(2)}, u32[]{:S(2)}) collective-permute-start(bf16[3088,128]{1,0:T(8,128)(2,1)} %get-tuple-element.1055.refs_16_), channel_id=1, source_target_pairs={{0,4},{4,0},{1,5},{5,1},{2,6},{6,2},{3,7},{7,3},{8,12},{12,8},{9,1... | collective-permute-start | bytes 2371592 | tf_op jit(solution)/shard_map/ppermute | solution.py:317
  230.0 44.9 %collective-permute-start.42 = (bf16[3088,128]{1,0:T(8,128)(2,1)}, bf16[3088,128]{1,0:T(8,128)(2,1)S(1)}, u32[]{:S(2)}, u32[]{:S(2)}) collective-permute-start(bf16[3088,128]{1,0:T(8,128)(2,1)} %get-tuple-element.1053.refs_24_), channel_id=1, source_target_pairs={{0,1},{1,0},{2,3},{3,2},{4,5},{5,4},{6,7},{7,6},{8,9},{9,8},{10,11... | collective-permute-start | bytes 2371592 | tf_op jit(solution)/shard_map/ppermute | solution.py:323
  249.5 25.9 %collective-permute-start.31 = (bf16[3088,128]{1,0:T(8,128)(2,1)}, bf16[3088,128]{1,0:T(8,128)(2,1)S(1)}, u32[]{:S(2)}, u32[]{:S(2)}) collective-permute-start(bf16[3088,128]{1,0:T(8,128)(2,1)} %get-tuple-element.1055.refs_16_), channel_id=1, source_target_pairs={{0,1},{1,0},{2,3},{3,2},{4,5},{5,4},{6,7},{7,6},{8,9},{9,8},{10,11... | collective-permute-start | bytes 2371592 | tf_op jit(solution)/shard_map/ppermute | solution.py:323
  250.9 45.4 %collective-permute-start.41 = (bf16[3088,128]{1,0:T(8,128)(2,1)S(1)}, bf16[3088,128]{1,0:T(8,128)(2,1)}, u32[]{:S(2)}, u32[]{:S(2)}) collective-permute-start(bf16[3088,128]{1,0:T(8,128)(2,1)S(1)} %collective-permute-done.40.refs_26_), channel_id=1, source_target_pairs={{0,2},{2,0},{1,3},{3,1},{4,6},{6,4},{5,7},{7,5},{8,10},{10,8},{9,1... | collective-permute-start | bytes 2371592 | tf_op jit(solution)/shard_map/ppermute | solution.py:321
  274.8 21.6 %collective-permute-start.30 = (bf16[3088,128]{1,0:T(8,128)(2,1)}, bf16[3088,128]{1,0:T(8,128)(2,1)}, u32[]{:S(2)}, u32[]{:S(2)}) collective-permute-start(bf16[3088,128]{1,0:T(8,128)(2,1)} %collective-permute-done.28.refs_17_), channel_id=1, source_target_pairs={{0,4},{4,0},{1,5},{5,1},{2,6},{6,2},{3,7},{7,3},{8,12},{12,8},{9,1... | collective-permute-start | bytes 2371592 | tf_op jit(solution)/shard_map/ppermute | solution.py:319
  274.8 22.1 %collective-permute-start.44 = (bf16[3088,128]{1,0:T(8,128)(2,1)S(1)}, bf16[3088,128]{1,0:T(8,128)(2,1)S(1)}, u32[]{:S(2)}, u32[]{:S(2)}) collective-permute-start(bf16[3088,128]{1,0:T(8,128)(2,1)S(1)} %collective-permute-done.40.refs_26_), channel_id=1, source_target_pairs={{0,1},{1,0},{2,3},{3,2},{4,5},{5,4},{6,7},{7,6},{8,9},{9,8},{10,11... | collective-permute-start | bytes 2371592 | tf_op jit(solution)/shard_map/ppermute | solution.py:323
  274.9 41.0 %collective-permute-start.32 = (bf16[3088,128]{1,0:T(8,128)(2,1)}, bf16[3088,128]{1,0:T(8,128)(2,1)}, u32[]{:S(2)}, u32[]{:S(2)}) collective-permute-start(bf16[3088,128]{1,0:T(8,128)(2,1)} %collective-permute-done.28.refs_17_), channel_id=1, source_target_pairs={{0,1},{1,0},{2,3},{3,2},{4,5},{5,4},{6,7},{7,6},{8,9},{9,8},{10,11... | collective-permute-start | bytes 2371592 | tf_op jit(solution)/shard_map/ppermute | solution.py:323
  275.4 40.5 %collective-permute-start.43 = (bf16[3088,128]{1,0:T(8,128)(2,1)}, bf16[3088,128]{1,0:T(8,128)(2,1)}, u32[]{:S(2)}, u32[]{:S(2)}) collective-permute-start(bf16[3088,128]{1,0:T(8,128)(2,1)} %collective-permute-done.39.refs_25_), channel_id=1, source_target_pairs={{0,1},{1,0},{2,3},{3,2},{4,5},{5,4},{6,7},{7,6},{8,9},{9,8},{10,11... | collective-permute-start | bytes 2371592 | tf_op jit(solution)/shard_map/ppermute | solution.py:323
  296.3 19.5 %collective-permute-start.45 = (bf16[3088,128]{1,0:T(8,128)(2,1)}, bf16[3088,128]{1,0:T(8,128)(2,1)}, u32[]{:S(2)}, u32[]{:S(2)}) collective-permute-start(bf16[3088,128]{1,0:T(8,128)(2,1)} %collective-permute-done.41.refs_27_), channel_id=1, source_target_pairs={{0,1},{1,0},{2,3},{3,2},{4,5},{5,4},{6,7},{7,6},{8,9},{9,8},{10,11... | collective-permute-start | bytes 2371592 | tf_op jit(solution)/shard_map/ppermute | solution.py:323
  654.6 230.8 %all-gather.14.cloned.1.call-start = ((), (), s32[]{:S(2)}) async-start(), calls=%async_computation.7 | async-start | bytes 3538944 | tf_op jit(solution)/shard_map/all_gather | solution.py:92
  680.8 320.8 %reduce-scatter.5.cloned.1.call-start = ((), (), s32[]{:S(2)}) async-start(), calls=%async_computation.5 | async-start | bytes 1179648 | tf_op jit(solution)/shard_map/reduce_scatter | solution.py:1053
  714.8 314.3 %collective-permute-start.61 = (bf16[24688,128]{1,0:T(8,128)(2,1)}, bf16[24688,128]{1,0:T(8,128)(2,1)}, u32[]{:S(2)}, u32[]{:S(2)}) collective-permute-start(bf16[24688,128]{1,0:T(8,128)(2,1)} %constant_dynamic-slice_fusion.4), channel_id=1, source_target_pairs={{0,1},{1,0},{2,3},{3,2},{4,5},{5,4},{6,7},{7,6},{8,9},{9,8},{10,11... | collective-permute-start | bytes 18960392 | tf_op jit(solution)/shard_map/ppermute | solution.py:655
  940.7 50.7 %collective-permute-start.46 = (f32[3,1792]{1,0:T(4,128)S(1)}, f32[3,1792]{1,0:T(4,128)S(1)}, u32[]{:S(2)}, u32[]{:S(2)}) collective-permute-start(f32[3,1792]{1,0:T(4,128)S(1)} %pad_add_fusion.1), channel_id=1, source_target_pairs={{1,0},{2,1},{3,2},{4,3},{5,4},{6,5},{7,6},{9,8},{10,9},{11,10},{12... | collective-permute-start | bytes 64520 | tf_op jit(solution)/shard_map/ppermute | solution.py:63
  1037.0 37.7 %collective-permute-start.68 = (bf16[2,3104,128]{2,1,0:T(8,128)(2,1)S(1)}, bf16[2,3104,128]{2,1,0:T(8,128)(2,1)S(1)}, u32[]{:S(2)}, u32[]{:S(2)}) collective-permute-start(bf16[2,3104,128]{2,1,0:T(8,128)(2,1)S(1)} %pad_maximum_fusion.6), channel_id=1, source_target_pairs={{0,2},{2,0},{1,3},{3,1},{4,6},{6,4},{5,7},{7,5},{8,10},{10,8},{9,1... | collective-permute-start | bytes 4767752 | tf_op jit(solution)/shard_map/ppermute | solution.py:672
  1039.8 37.2 %collective-permute-start.62 = (bf16[2,3104,128]{2,1,0:T(8,128)(2,1)S(1)}, bf16[2,3104,128]{2,1,0:T(8,128)(2,1)S(1)}, u32[]{:S(2)}, u32[]{:S(2)}) collective-permute-start(bf16[2,3104,128]{2,1,0:T(8,128)(2,1)S(1)} %pad_maximum_fusion.5), channel_id=1, source_target_pairs={{0,4},{4,0},{1,5},{5,1},{2,6},{6,2},{3,7},{7,3},{8,12},{12,8},{9,1... | collective-permute-start | bytes 4767752 | tf_op jit(solution)/shard_map/ppermute | solution.py:672
  1041.8 91.0 %collective-permute-start.47 = (bf16[24688,128]{1,0:T(8,128)(2,1)S(1)}, bf16[24688,128]{1,0:T(8,128)(2,1)S(1)}, u32[]{:S(2)}, u32[]{:S(2)}) collective-permute-start(bf16[24688,128]{1,0:T(8,128)(2,1)S(1)} %constant_dynamic-slice_fusion.5), channel_id=1, source_target_pairs={{0,1},{1,0},{2,3},{3,2},{4,5},{5,4},{6,7},{7,6},{8,9},{9,8},{10,11... | collective-permute-start | bytes 18960392 | tf_op jit(solution)/shard_map/ppermute | solution.py:655
  1077.5 22.0 %collective-permute-start.63 = (bf16[3104,128]{1,0:T(8,128)(2,1)S(1)}, bf16[3104,128]{1,0:T(8,128)(2,1)S(1)}, u32[]{:S(2)}, u32[]{:S(2)}) collective-permute-start(bf16[3104,128]{1,0:T(8,128)(2,1)S(1)} %dynamic-slice_bitcast_fusion.5), channel_id=1, source_target_pairs={{0,2},{2,0},{1,3},{3,1},{4,6},{6,4},{5,7},{7,5},{8,10},{10,8},{9,1... | collective-permute-start | bytes 2383880 | tf_op jit(solution)/shard_map/ppermute | solution.py:675
  1094.8 22.1 %collective-permute-start.70 = (bf16[3104,128]{1,0:T(8,128)(2,1)S(1)}, bf16[3104,128]{1,0:T(8,128)(2,1)S(1)}, u32[]{:S(2)}, u32[]{:S(2)}) collective-permute-start(bf16[3104,128]{1,0:T(8,128)(2,1)S(1)} %fusion.89), channel_id=1, source_target_pairs={{0,8},{1,9},{2,10},{3,11},{4,12},{5,13},{6,14},{7,15}} | collective-permute-start | bytes 2383880 | tf_op jit(solution)/shard_map/ppermute | solution.py:682
  1098.8 36.9 %collective-permute-start.72 = (bf16[3104,128]{1,0:T(8,128)(2,1)S(1)}, bf16[3104,128]{1,0:T(8,128)(2,1)S(1)}, u32[]{:S(2)}, u32[]{:S(2)}) collective-permute-start(bf16[3104,128]{1,0:T(8,128)(2,1)S(1)} %fusion.89), channel_id=1, source_target_pairs={{24,16},{26,18},{28,20},{30,22}} | collective-permute-start | bytes 2383880 | tf_op jit(solution)/shard_map/ppermute | solution.py:683
  1099.7 32.1 %collective-permute-start.64 = (bf16[3104,128]{1,0:T(8,128)(2,1)S(1)}, bf16[3104,128]{1,0:T(8,128)(2,1)S(1)}, u32[]{:S(2)}, u32[]{:S(2)}) collective-permute-start(bf16[3104,128]{1,0:T(8,128)(2,1)S(1)} %fusion.90), channel_id=1, source_target_pairs={{0,8},{1,9},{2,10},{3,11},{4,12},{5,13},{6,14},{7,15}} | collective-permute-start | bytes 2383880 | tf_op jit(solution)/shard_map/ppermute | solution.py:682
  1101.1 37.3 %collective-permute-start.66 = (bf16[3104,128]{1,0:T(8,128)(2,1)S(1)}, bf16[3104,128]{1,0:T(8,128)(2,1)S(1)}, u32[]{:S(2)}, u32[]{:S(2)}) collective-permute-start(bf16[3104,128]{1,0:T(8,128)(2,1)S(1)} %fusion.90), channel_id=1, source_target_pairs={{24,16},{26,18},{28,20},{30,22}} | collective-permute-start | bytes 2383880 | tf_op jit(solution)/shard_map/ppermute | solution.py:683
  1135.2 34.8 %collective-permute-start.54 = (bf16[2,3104,128]{2,1,0:T(8,128)(2,1)S(1)}, bf16[2,3104,128]{2,1,0:T(8,128)(2,1)S(1)}, u32[]{:S(2)}, u32[]{:S(2)}) collective-permute-start(bf16[2,3104,128]{2,1,0:T(8,128)(2,1)S(1)} %pad_maximum_fusion.4), channel_id=1, source_target_pairs={{0,2},{2,0},{1,3},{3,1},{4,6},{6,4},{5,7},{7,5},{8,10},{10,8},{9,1... | collective-permute-start | bytes 4767752 | tf_op jit(solution)/shard_map/ppermute | solution.py:672
  1135.9 71.6 %collective-permute-start.73 = (bf16[3104,128]{1,0:T(8,128)(2,1)S(1)}, bf16[3104,128]{1,0:T(8,128)(2,1)S(1)}, u32[]{:S(2)}, u32[]{:S(2)}) collective-permute-start(bf16[3104,128]{1,0:T(8,128)(2,1)S(1)} %add_convert_fusion.7), channel_id=1, source_target_pairs={{17,25},{19,27},{21,29},{23,31}} | collective-permute-start | bytes 2383880 | tf_op jit(solution)/shard_map/ppermute | solution.py:685
  1136.8 35.4 %collective-permute-start.48 = (bf16[2,3104,128]{2,1,0:T(8,128)(2,1)S(1)}, bf16[2,3104,128]{2,1,0:T(8,128)(2,1)S(1)}, u32[]{:S(2)}, u32[]{:S(2)}) collective-permute-start(bf16[2,3104,128]{2,1,0:T(8,128)(2,1)S(1)} %pad_maximum_fusion.3), channel_id=1, source_target_pairs={{0,4},{4,0},{1,5},{5,1},{2,6},{6,2},{3,7},{7,3},{8,12},{12,8},{9,1... | collective-permute-start | bytes 4767752 | tf_op jit(solution)/shard_map/ppermute | solution.py:672
  1138.7 68.9 %collective-permute-start.67 = (bf16[3104,128]{1,0:T(8,128)(2,1)S(1)}, bf16[3104,128]{1,0:T(8,128)(2,1)S(1)}, u32[]{:S(2)}, u32[]{:S(2)}) collective-permute-start(bf16[3104,128]{1,0:T(8,128)(2,1)S(1)} %add_convert_fusion.10), channel_id=1, source_target_pairs={{17,25},{19,27},{21,29},{23,31}} | collective-permute-start | bytes 2383880 | tf_op jit(solution)/shard_map/ppermute | solution.py:685
  1172.7 21.6 %collective-permute-start.49 = (bf16[3104,128]{1,0:T(8,128)(2,1)S(1)}, bf16[3104,128]{1,0:T(8,128)(2,1)S(1)}, u32[]{:S(2)}, u32[]{:S(2)}) collective-permute-start(bf16[3104,128]{1,0:T(8,128)(2,1)S(1)} %dynamic-slice_bitcast_fusion.15), channel_id=1, source_target_pairs={{0,2},{2,0},{1,3},{3,1},{4,6},{6,4},{5,7},{7,5},{8,10},{10,8},{9,1... | collective-permute-start | bytes 2383880 | tf_op jit(solution)/shard_map/ppermute | solution.py:675
  1204.6 71.1 %collective-permute-start.59 = (bf16[3104,128]{1,0:T(8,128)(2,1)S(1)}, bf16[3104,128]{1,0:T(8,128)(2,1)S(1)}, u32[]{:S(2)}, u32[]{:S(2)}) collective-permute-start(bf16[3104,128]{1,0:T(8,128)(2,1)S(1)} %add_convert_fusion.13), channel_id=1, source_target_pairs={{8,0},{10,2},{12,4},{14,6}} | collective-permute-start | bytes 2383880 | tf_op jit(solution)/shard_map/ppermute | solution.py:680
  1206.2 75.3 %collective-permute-start.53 = (bf16[3104,128]{1,0:T(8,128)(2,1)S(1)}, bf16[3104,128]{1,0:T(8,128)(2,1)S(1)}, u32[]{:S(2)}, u32[]{:S(2)}) collective-permute-start(bf16[3104,128]{1,0:T(8,128)(2,1)S(1)} %add_convert_fusion.16), channel_id=1, source_target_pairs={{8,0},{10,2},{12,4},{14,6}} | collective-permute-start | bytes 2383880 | tf_op jit(solution)/shard_map/ppermute | solution.py:680
  1208.2 80.8 %collective-permute-start.74 = (bf16[3104,128]{1,0:T(8,128)(2,1)S(1)}, bf16[3104,128]{1,0:T(8,128)(2,1)S(1)}, u32[]{:S(2)}, u32[]{:S(2)}) collective-permute-start(bf16[3104,128]{1,0:T(8,128)(2,1)S(1)} %get-tuple-element.999), channel_id=1, source_target_pairs={{0,1},{9,8},{16,17},{25,24},{2,3},{11,10},{18,19},{27,26},{4,5},{1... | collective-permute-start | bytes 2383880 | tf_op jit(solution)/shard_map/ppermute | solution.py:690
  (211 other events, 3997.7 us)
Sparse Core Ops, SparseCore 0:
  185.7 26.6 all-gather.9
  214.3 26.4 all-gather.7
  242.8 45.0 all-gather.11
  654.7 196.5 reduce-scatter.2
  853.1 32.2 all-gather.13
  888.4 64.9 reduce-scatter.4

commit v2 on v1

--- a/solution.py
+++ b/solution.py
@@ -691,6 +691,218 @@
     return jnp.where(c == z % 2, mine, handed)
 
 
+KEYS = 512
+PAIR = 2 * HEAD_DIM
+NT = (((1,), (1,)), ((), ()))
+
+
+def attention_forward(q_wide, kv, meta, starts):
+    rows = q_wide.shape[1]
+    blocks = kv.shape[0]
+    tall = min(256, rows)
+
+    def kernel(meta_ref, q_ref, kv_ref, start_ref, o_ref, log_ref, top, total, mixed):
+        top[...] = jnp.full(top.shape, masked_score, jnp.float32)
+        total[...] = jnp.zeros(total.shape, jnp.float32)
+        mixed[...] = jnp.zeros(mixed.shape, jnp.float32)
+
+        def block(b, partial):
+            pair = kv_ref[b, 0]
+            for r in range(0, rows, tall):
+                here = slice(r, r + tall)
+                scores = lax.dot_general(q_ref[0, here, :], pair, NT, preferred_element_type=jnp.float32)
+                if partial:
+                    keys = b * KEYS + lax.broadcasted_iota(jnp.int32, scores.shape, 1)
+                    mine = meta_ref[2] + r + lax.broadcasted_iota(jnp.int32, scores.shape, 0)
+                    visible = (keys >= start_ref[here, :]) & (keys <= mine)
+                    scores = jnp.where(visible, scores, masked_score)
+                before = top[here, :]
+                peak = jnp.maximum(before, jnp.max(scores, axis=1, keepdims=True))
+                part = jnp.exp(scores - peak[:, :1])
+                if partial:
+                    part = jnp.where(visible, part, 0.0)
+                fade = jnp.exp(before - peak)
+                top[here, :] = peak
+                total[here, :] = total[here, :] * fade + jnp.sum(part, axis=1, keepdims=True)
+                mixed[here, :] = mixed[here, :] * fade + jnp.dot(
+                    part.astype(jnp.bfloat16), pair, preferred_element_type=jnp.float32
+                )
+
+        def turn(b, nothing):
+            partial = ((b + 1) * KEYS > meta_ref[2]) | (b * KEYS < meta_ref[3])
+
+            @pl.when(partial)
+            def _():
+                block(b, True)
+
+            @pl.when(jnp.logical_not(partial))
+            def _():
+                block(b, False)
+
+            return nothing
+
+        lax.fori_loop(meta_ref[0], meta_ref[1], turn, 0)
+        o_ref[0] = mixed[...] / total[...]
+        log_ref[0] = (top[...] + jnp.log(total[...])).T[:8, :]
+
+    ratio = HEADS_Q // HEADS_KV
+    return pl.pallas_call(
+        kernel,
+        grid_spec=pltpu.PrefetchScalarGridSpec(
+            num_scalar_prefetch=1,
+            grid=(HEADS_Q,),
+            in_specs=[
+                pl.BlockSpec((1, rows, PAIR), lambda h, m: (h, 0, 0)),
+                pl.BlockSpec((blocks, 1, KEYS, PAIR), lambda h, m: (0, h // ratio, 0, 0)),
+                pl.BlockSpec((rows, 1), lambda h, m: (0, 0)),
+            ],
+            out_specs=[
+                pl.BlockSpec((1, rows, PAIR), lambda h, m: (h, 0, 0)),
+                pl.BlockSpec((1, 8, rows), lambda h, m: (h, 0, 0)),
+            ],
+            scratch_shapes=[pltpu.VMEM((rows, PAIR), jnp.float32)] * 3,
+        ),
+        out_shape=[
+            jax.ShapeDtypeStruct((HEADS_Q, rows, PAIR), jnp.float32),
+            jax.ShapeDtypeStruct((HEADS_Q, 8, rows), jnp.float32),
+        ],
+        compiler_params=pltpu.CompilerParams(vmem_limit_bytes=48 * 2**20),
+        cost_estimate=pl.CostEstimate(flops=2 * 10**9, bytes_accessed=2**23, transcendentals=2**23),
+        name="attend",
+    )(meta, q_wide, kv, starts)
+
+
+def attention_backward(q_wide, g_wide, kv, logs, mixed, meta, starts):
+    rows = q_wide.shape[1]
+    blocks = kv.shape[0]
+    ratio = HEADS_Q // HEADS_KV
+    wide = min(256, rows)
+
+    def kernel(meta_ref, q_ref, g_ref, kv_ref, log_ref, o_ref, start_ref, dkv_ref, dq_ref, delta, sums):
+        b = pl.program_id(1)
+
+        @pl.when(b == 0)
+        def _():
+            dq_ref[...] = jnp.zeros(dq_ref.shape, jnp.float32)
+            for h in range(ratio):
+                both = g_ref[h].astype(jnp.float32) * o_ref[h]
+                delta[h] = jnp.broadcast_to(jnp.sum(both.T, axis=0, keepdims=True), (8, rows))
+
+        def block(partial):
+            pair = kv_ref[0, 0]
+            turned = pair.T[:HEAD_DIM, :]
+            for h in range(ratio):
+                for r in range(0, rows, wide):
+                    here = slice(r, r + wide)
+                    q_now = q_ref[h, here, :]
+                    g_now = g_ref[h, here, :]
+                    scores = lax.dot_general(pair, q_now, NT, preferred_element_type=jnp.float32)
+                    probs = jnp.exp(scores - log_ref[h, 0:1, here])
+                    if partial:
+                        keys = b * KEYS + lax.broadcasted_iota(jnp.int32, scores.shape, 0)
+                        mine = meta_ref[2] + r + lax.broadcasted_iota(jnp.int32, scores.shape, 1)
+                        visible = (keys >= start_ref[0:1, here]) & (keys <= mine)
+                        probs = jnp.where(visible, probs, 0.0)
+                    grads = lax.dot_general(pair, g_now, NT, preferred_element_type=jnp.float32)
+                    low_grads = (probs * (grads - delta[h, 0:1, here])).astype(jnp.bfloat16)
+                    change = jnp.dot(
+                        probs.astype(jnp.bfloat16), g_now, preferred_element_type=jnp.float32
+                    ) + jnp.dot(low_grads, q_now, preferred_element_type=jnp.float32)
+                    if h == 0 and r == 0:
+                        sums[...] = change
+                    else:
+                        sums[...] += change
+                    dq_ref[h, :, here] += jnp.dot(turned, low_grads, preferred_element_type=jnp.float32)
+            dkv_ref[0, 0] = sums[...].astype(jnp.bfloat16)
+
+        needed = (b >= meta_ref[0]) & (b < meta_ref[1])
+        partial = ((b + 1) * KEYS > meta_ref[2]) | (b * KEYS < meta_ref[3])
+
+        @pl.when(needed & partial)
+        def _():
+            block(True)
+
+        @pl.when(needed & jnp.logical_not(partial))
+        def _():
+            block(False)
+
+        @pl.when(jnp.logical_not(needed))
+        def _():
+            dkv_ref[0, 0] = jnp.zeros((KEYS, PAIR), jnp.bfloat16)
+
+    heads = lambda g, b, m: (g, 0, 0)
+    return pl.pallas_call(
+        kernel,
+        grid_spec=pltpu.PrefetchScalarGridSpec(
+            num_scalar_prefetch=1,
+            grid=(HEADS_KV, blocks),
+            in_specs=[
+                pl.BlockSpec((ratio, rows, PAIR), heads),
+                pl.BlockSpec((ratio, rows, PAIR), heads),
+                pl.BlockSpec((1, 1, KEYS, PAIR), lambda g, b, m: (b, g, 0, 0)),
+                pl.BlockSpec((ratio, 8, rows), heads),
+                pl.BlockSpec((ratio, rows, PAIR), heads),
+                pl.BlockSpec((8, rows), lambda g, b, m: (0, 0)),
+            ],
+            out_specs=[
+                pl.BlockSpec((1, 1, KEYS, PAIR), lambda g, b, m: (b, g, 0, 0)),
+                pl.BlockSpec((ratio, HEAD_DIM, rows), heads),
+            ],
+            scratch_shapes=[
+                pltpu.VMEM((ratio, 8, rows), jnp.float32),
+                pltpu.VMEM((KEYS, PAIR), jnp.float32),
+            ],
+        ),
+        out_shape=[
+            jax.ShapeDtypeStruct((blocks, HEADS_KV, KEYS, PAIR), jnp.bfloat16),
+            jax.ShapeDtypeStruct((HEADS_Q, HEAD_DIM, rows), jnp.float32),
+        ],
+        compiler_params=pltpu.CompilerParams(vmem_limit_bytes=48 * 2**20),
+        cost_estimate=pl.CostEstimate(flops=5 * 10**9, bytes_accessed=2**23, transcendentals=2**23),
+        name="attend_back",
+    )(meta, q_wide, g_wide, kv, logs, mixed, starts)
+
+
+def ordered(place, own, other, axis):
+    first = jnp.where(place == 0, own, other)
+    second = jnp.where(place == 0, other, own)
+    return jnp.stack([first, second], axis=axis)
+
+
+def gather_span(value, span, fast):
+    if not fast:
+        return lax.all_gather(value, span)
+    _, y, x, c = (lax.axis_index(name) for name in GRID)
+    two = ordered(x, value, lax.ppermute(value, "x", SWAP), 0)
+    four = ordered(y, two, lax.ppermute(two, "y", SWAP), 0)
+    eight = ordered(c, four, lax.ppermute(four, "c", SWAP), 2)
+    return eight.reshape((8,) + value.shape)
+
+
+def scatter_span(value, span, fast):
+    if not fast:
+        return lax.psum_scatter(value, span, scatter_dimension=0).astype(jnp.float32)
+    _, y, x, c = (lax.axis_index(name) for name in GRID)
+    value = value.reshape((2, 2, 2) + value.shape[1:])
+    for name, place, axis in (("c", c, 2), ("y", y, 0), ("x", x, 0)):
+        keep = lax.dynamic_index_in_dim(value, place, axis, keepdims=False)
+        send = lax.dynamic_index_in_dim(value, 1 - place, axis, keepdims=False)
+        value = keep.astype(jnp.float32) + lax.ppermute(send, name, SWAP).astype(jnp.float32)
+        if name != "x":
+            value = value.astype(jnp.bfloat16)
+    return value
+
+
+def sum_all(value, axes, fast):
+    if not fast:
+        return lax.psum(value, axes)
+    for name in GRID[1:]:
+        value = value + lax.ppermute(value, name, SWAP)
+    for pairs in ([(0, 1), (1, 0), (2, 3), (3, 2)], [(0, 2), (2, 0), (1, 3), (3, 1)]):
+        value = value + lax.ppermute(value, "z", pairs)
+    return value
+
+
 def offsets_of():
     places, at = {}, 0
     for name_key, extent in layout():
@@ -782,7 +994,6 @@
     rows_dev = tokens.shape[0]
     group_rows = rows_dev * lax.axis_size(span)
     all_rows = group_rows * lax.axis_size(group)
-    group_ratio = HEADS_Q // HEADS_KV
     ssm_inner = SSM_HEADS * SSM_DIM
     score_scale = HEAD_DIM ** (-0.5)
     bounds = offsets[0]
@@ -805,91 +1016,21 @@
     value_low = matmul(hidden, weights[W_VALUE]).astype(jnp.bfloat16)
     q_rot = rotate(query, cosine, sine, HEADS_Q).astype(jnp.bfloat16)
     k_rot = rotate(key_raw, cosine, sine, HEADS_KV).astype(jnp.bfloat16)
-    q_heads = q_rot.reshape(rows_dev, HEADS_KV, group_ratio, HEAD_DIM)
-
-    def block_scores(key_block, key_rows):
-        scores = (
-            jnp.einsum(
-                "tgjd,kgd->gjtk",
-                q_heads,
-                key_block.reshape(-1, HEADS_KV, HEAD_DIM),
-                preferred_element_type=jnp.float32,
-            )
-            * score_scale
-        )
-        key_seq, _ = sequence_info(key_rows, bounds)
-        visible = (seq_id[:, None] == key_seq[None, :]) & (key_rows[None, :] <= row_index[:, None])
-        return (scores, visible[None, None])
-
-    def over_blocks(carry_now, piece_pair, step_fn):
-        keys_piece, values_piece = piece_pair
-        piece_rows = keys_piece.shape[0]
-        block_rows = math.gcd(piece_rows, 512)
-        block_count = piece_rows // block_rows
-
-        def one_block(state_now, inputs):
-            index_block, key_block, value_block = inputs
-            key_start = index_block * block_rows
-            needed = (key_start <= last_row) & (key_start + block_rows > first_start)
-
-            def compute(state_in_block):
-                key_rows = key_start + jnp.arange(block_rows, dtype=jnp.int32)
-                return step_fn(state_in_block, key_block, value_block, key_rows, key_start)
-
-            def unchanged(state_in_block):
-                return state_in_block
-
-            return (lax.cond(needed, compute, unchanged, state_now), None)
-
-        carry_now, _ = lax.scan(
-            one_block,
-            carry_now,
-            (
-                jnp.arange(block_count, dtype=jnp.int32),
-                keys_piece.reshape(block_count, block_rows, -1),
-                values_piece.reshape(block_count, block_rows, -1),
-            ),
-        )
-        return carry_now
-
-    def forward_step(state_now, key_block, value_block, key_rows, key_start):
-        running_max, running_sum, accum = state_now
-        scores, visible = block_scores(key_block, key_rows)
-        new_max = jnp.maximum(
-            running_max, jnp.max(jnp.where(visible, scores, masked_score), axis=-1)
-        )
-        weights_p = jnp.where(visible, jnp.exp(scores - new_max[..., None]), 0.0)
-        factor = jnp.exp(running_max - new_max)
-        mixed_values = jnp.einsum(
-            "gjtk,kgd->gjtd",
-            weights_p.astype(jnp.bfloat16),
-            value_block.reshape(-1, HEADS_KV, HEAD_DIM),
-            preferred_element_type=jnp.float32,
-        )
-        return (
-            new_max,
-            running_sum * factor + jnp.sum(weights_p, axis=-1),
-            accum * factor[..., None] + mixed_values,
-        )
-
-    head_shape = (HEADS_KV, group_ratio, rows_dev)
-    initial = (
-        jnp.full(head_shape, masked_score, jnp.float32),
-        jnp.zeros(head_shape, jnp.float32),
-        jnp.zeros(head_shape + (HEAD_DIM,), jnp.float32),
-    )
-    running_max, running_sum, accum = over_blocks(
-        initial,
-        (
-            lax.all_gather(k_rot, span, axis=0, tiled=True),
-            lax.all_gather(value_low, span, axis=0, tiled=True),
-        ),
-        forward_step,
-    )
-    attn_f32 = accum / running_sum[..., None]
-    log_total = running_max + jnp.log(running_sum)
+    k_heads = k_rot.reshape(rows_dev, HEADS_KV, HEAD_DIM)
+    v_heads = value_low.reshape(rows_dev, HEADS_KV, HEAD_DIM)
+    kv_mine = jnp.concatenate([k_heads, v_heads], axis=2).transpose(1, 0, 2)
+    key_blocks = gather_span(kv_mine.reshape(HEADS_KV, rows_dev, PAIR), span, fast)
+    if rows_dev != KEYS:
+        key_blocks = key_blocks.transpose(1, 0, 2, 3).reshape(HEADS_KV, -1, KEYS, PAIR).transpose(1, 0, 2, 3)
+    row_starts = row_index - positions
+    meta = jnp.stack(
+        [first_start // KEYS, last_row // KEYS + 1, my_start, row_starts[rows_dev - 1]]
+    ).astype(jnp.int32)
+    q_low = (q_rot * jnp.bfloat16(score_scale)).reshape(rows_dev, HEADS_Q, HEAD_DIM).transpose(1, 0, 2)
+    q_wide = jnp.pad(q_low, ((0, 0), (0, 0), (0, HEAD_DIM)))
+    mixed, logs = attention_forward(q_wide, key_blocks, meta, row_starts[:, None])
     attended = (
-        attn_f32.transpose(2, 0, 1, 3).reshape(rows_dev, HEADS_Q * HEAD_DIM).astype(jnp.bfloat16)
+        mixed[:, :, HEAD_DIM:].transpose(1, 0, 2).reshape(rows_dev, HEADS_Q * HEAD_DIM).astype(jnp.bfloat16)
     )
     attn_out = matmul(attended, weights[W_ATTN_OUT])
     gate_ssm = matmul(hidden, weights[W_GATE_SSM])
@@ -955,7 +1096,7 @@
             jnp.sum(ffn_out * ffn_out),
         ]
     )
-    totals = lax.psum(squares, group + span)
+    totals = sum_all(squares, group + span, fast)
     stats = jnp.sqrt(totals / (all_rows * D))
     back_weights = weights
     grad_out = cotangent.astype(jnp.float32)
@@ -996,65 +1137,17 @@
         + matmul_right_t(grad_xbc[:, ssm_inner:], back_weights[W_B_C])
         + matmul_right_t(grad_step_raw, back_weights[W_STEP])
     )
-    grad_heads = grad_attended.reshape(rows_dev, HEADS_KV, group_ratio, HEAD_DIM).transpose(
-        1, 2, 0, 3
-    )
-    delta = jnp.sum(grad_heads.astype(jnp.float32) * attn_f32, axis=-1)
-
-    def backward_step(state_now, key_block, value_block, key_rows, key_start):
-        grad_query, grad_keys, grad_values = state_now
-        scores, visible = block_scores(key_block, key_rows)
-        probs = jnp.where(visible, jnp.exp(scores - log_total[..., None]), 0.0)
-        key_heads = key_block.reshape(-1, HEADS_KV, HEAD_DIM)
-        value_heads = value_block.reshape(-1, HEADS_KV, HEAD_DIM)
-        grad_probs = jnp.einsum(
-            "gjtd,kgd->gjtk", grad_heads, value_heads, preferred_element_type=jnp.float32
-        )
-        grad_scores = (probs * (grad_probs - delta[..., None])).astype(jnp.bfloat16)
-        grad_query = (
-            grad_query
-            + jnp.einsum(
-                "gjtk,kgd->gjtd", grad_scores, key_heads, preferred_element_type=jnp.float32
-            )
-            * score_scale
-        )
-        key_part = (
-            jnp.einsum("gjtk,tgjd->kgd", grad_scores, q_heads, preferred_element_type=jnp.float32)
-            * score_scale
-        )
-        value_part = jnp.einsum(
-            "gjtk,gjtd->kgd",
-            probs.astype(jnp.bfloat16),
-            grad_heads,
-            preferred_element_type=jnp.float32,
-        )
-        block_rows = key_block.shape[0]
-        grad_keys = add_rows(grad_keys, key_part.reshape(block_rows, -1), key_start)
-        grad_values = add_rows(grad_values, value_part.reshape(block_rows, -1), key_start)
-        return (grad_query, grad_keys, grad_values)
-
-    initial_back = (
-        jnp.zeros(head_shape + (HEAD_DIM,), jnp.float32),
-        jnp.zeros((group_rows, HEADS_KV * HEAD_DIM), jnp.float32),
-        jnp.zeros((group_rows, HEADS_KV * HEAD_DIM), jnp.float32),
-    )
-    grad_query_all, grad_keys_all, grad_values_all = over_blocks(
-        initial_back,
-        (
-            lax.all_gather(k_rot, span, axis=0, tiled=True),
-            lax.all_gather(value_low, span, axis=0, tiled=True),
-        ),
-        backward_step,
-    )
-    grad_keys_mine, grad_values_mine = (
-        lax.psum_scatter(
-            grad_keys_all.astype(jnp.bfloat16), span, scatter_dimension=0, tiled=True
-        ).astype(jnp.float32),
-        lax.psum_scatter(
-            grad_values_all.astype(jnp.bfloat16), span, scatter_dimension=0, tiled=True
-        ).astype(jnp.float32),
-    )
-    grad_q_rot = grad_query_all.transpose(2, 0, 1, 3).reshape(rows_dev, HEADS_Q * HEAD_DIM)
+    g_low = grad_attended.reshape(rows_dev, HEADS_Q, HEAD_DIM).transpose(1, 0, 2)
+    g_wide = jnp.pad(g_low, ((0, 0), (0, 0), (HEAD_DIM, 0)))
+    grad_kv, grad_q_turned = attention_backward(
+        q_wide, g_wide, key_blocks, logs, mixed, meta, jnp.broadcast_to(row_starts[None, :], (8, rows_dev))
+    )
+    if rows_dev != KEYS:
+        grad_kv = grad_kv.transpose(1, 0, 2, 3).reshape(HEADS_KV, -1, rows_dev, PAIR).transpose(1, 0, 2, 3)
+    grad_kv_mine = scatter_span(grad_kv, span, fast)
+    grad_keys_mine = grad_kv_mine[:, :, :HEAD_DIM].transpose(1, 0, 2).reshape(rows_dev, -1)
+    grad_values_mine = grad_kv_mine[:, :, HEAD_DIM:].transpose(1, 0, 2).reshape(rows_dev, -1)
+    grad_q_rot = grad_q_turned.transpose(2, 0, 1).reshape(rows_dev, HEADS_Q * HEAD_DIM) * score_scale
     grad_query_low = rotate(grad_q_rot, cosine, -sine, HEADS_Q).astype(jnp.bfloat16)
     grad_key_low = rotate(grad_keys_mine, cosine, -sine, HEADS_KV).astype(jnp.bfloat16)
     grad_value_low = grad_values_mine.astype(jnp.bfloat16)

time: 1310 us -> 1160 us (0.89)
  waiting for transfers between devices: 335 us -> 209 us
  blocking collectives: 92.4 us -> 12.1 us
  starting transfers between devices: 277 us -> 318 us
  Pallas kernels: 87.4 us -> 117 us
  matrix products: 222 us -> 202 us
    ppermute x0 -> x11, starting transfers between devices: none -> 132 us  [the longest x3 82.5 us: scatter_span(): lax.ppermute(send, name, SWAP).astype(jnp.float32)]
    psum x1 -> x0, blocking collectives: 84.1 us -> none  [body(): totals = lax.psum(squares, group + span)]
    reduce_scatter x2 -> x0, waiting for transfers between devices: 72.9 us -> none  [the longest x1 72.9 us: body(): lax.psum_scatter(grad_keys_all.astype(jnp.bfloat16), span, scatter_dimens...]
    ppermute x2, starting transfers between devices: 49.4 us -> 13.5 us  [passed_along(): lax.ppermute(value, axis, [(source, source + steps) for source in range(f...]
    all_gather x1, waiting for transfers between devices: 31.1 us -> 0.01 us  [carried_in(): lax.all_gather(part.astype(kind), axis)]
    pallas_call x0 -> x2, Pallas kernels: none -> 29.3 us  [the longest x1 17.4 us: attention_backward(): pl.pallas_call(kernel, grid_spec=pltpu.PrefetchScalarGridSpec(num_scalar_...]
    ppermute x16, starting transfers between devices: 42 us -> 18.7 us  [gather_lines(): buffers += local + [lax.ppermute(piece, 'c', SWAP) for piece in local]]
    ppermute x2, starting transfers between devices: 22.6 us -> 0.07 us  [reduce_lines(): chip = added(keep, lax.ppermute(send, 'c', SWAP))]
  transfers between devices with their start and end apart: 81 -> 88, of which waited for: 20 -> 23; matrix products, arithmetic and copies ran while one was open for 19% -> 28% of each run, Pallas kernels for 6% -> 10%
where the time goes in v2:
time: 1160 us; the launch traced here: 1140 us
  starting transfers between devices  318 us (27%)
  waiting for transfers between devices  209 us (18%)
  matrix products  202 us (17%)
  other arithmetic  155 us (13%)
  Pallas kernels  117 us (10%)
  local copies, waits for them, and re-layouts  108 us (9%)
  between operations  20.7 us (2%)
  blocking collectives  12.1 us (1%)
    dot_general x3, matrix products, ssd_output(): jnp.einsum('hts,shp->thp', kernel * inner_products[None], scaled_x, preci...  85.9 us
    ppermute x3, starting transfers between devices, scatter_span(): lax.ppermute(send, name, SWAP).astype(jnp.float32)  82.5 us
    ppermute x2, starting transfers between devices, reduce_lines(): handed = lax.ppermute(other, ZC, holders)  74.8 us
    ppermute x4, waiting for transfers between devices, reduce_lines(): half = added(home, lax.ppermute(away, first_axis, SWAP))  64.9 us
    pallas_call x3, Pallas kernels, pack_lines(): pl.pallas_call(kernel, grid=(total,), in_specs=[left_spec(k) for k in ran...  46.7 us
    pallas_call x2, Pallas kernels, unpack_lines(): pl.pallas_call(kernel, grid_spec=pltpu.PrefetchScalarGridSpec(num_scalar_...  41.1 us
    dot_general x12, matrix products, matmul(): return jnp.dot(left, right, preferred_element_type=jnp.float32)  38.1 us
    ppermute x3, starting transfers between devices, sum_all(): value = value + lax.ppermute(value, name, SWAP)  36.2 us
  transfers between devices with their start and end apart: 88, of which 23 were waited for; matrix products, arithmetic and copies ran while one was open for 28% of the time, Pallas kernels for 10%

profile of v2, /device:TPU:0, one launch (start us, length us, event | category | flops | bytes accessed | tf_op | source)
XLA Modules:
  0.0 1143.5 jit_solution(14957283907032265496)
XLA Ops:
  8.4 7.7 collective-permute-start
  51.8 15.6 %collective-permute-done.29 = bf16[3088,128]{1,0:T(8,128)(2,1)} collective-permute-done((bf16[3088,128]{1,0:T(8,128)(2,1)S(1)}, bf16[3088,128]{1,0:T(8,128)(2,1)}, u32[]{:S(2)}, u32[]{:S(2)}) %collective-permute-start.29) | collective-permute-done | bytes 790560 | tf_op jit(solution)/shard_map/ppermute | solution.py:312
  81.5 12.0 %collective-permute-start.19 = (bf16[3088,128]{1,0:T(8,128)(2,1)}, bf16[3088,128]{1,0:T(8,128)(2,1)}, u32[]{:S(2)}, u32[]{:S(2)}) collective-permute-start(bf16[3088,128]{1,0:T(8,128)(2,1)} %get-tuple-element.436.refs_8_), channel_id=1, source_target_pairs={{0,1},{1,0},{2,3},{3,2},{4,5},{5,4},{6,7},{7,6},{8,9},{9,8},{10,11... | collective-permute-start | bytes 2371592 | tf_op jit(solution)/shard_map/ppermute | solution.py:323
  94.5 15.7 %collective-permute-done.5.refs_1_ = bf16[3088,128]{1,0:T(8,128)(2,1)S(1)} collective-permute-done((bf16[3088,128]{1,0:T(8,128)(2,1)S(1)}, bf16[3088,128]{1,0:T(8,128)(2,1)S(1)}, u32[]{:S(2)}, u32[]{:S(2)}) %collective-permute-start.5) | collective-permute-done | bytes 790560 | tf_op jit(solution)/shard_map/ppermute | solution.py:316
  123.3 6.0 collective-permute-done.18.refs_11_
  141.1 14.8 %unpack.2 = (bf16[1024,512]{1,0:T(8,128)(2,1)}, bf16[1024,128]{1,0:T(8,128)(2,1)S(1)}, bf16[1024,128]{1,0:T(8,128)(2,1)S(1)}, bf16[512,1024]{1,0:T(8,128)(2,1)},...) custom-call(s32[25,5]{1,0:T(8,128)S(1)} %copy-done.35, ...), custom_call_target="tpu_custom_call" | custom-call | bytes 26624000 | tf_op jit(solution)/shard_map/unpack/pallas_call | solution.py:464
  174.9 7.0 collective-permute-start.26
  195.4 5.3 fusion.75
  212.9 6.2 collective-permute-start.44
  240.1 8.0 collective-permute-done.44.refs_27_
  259.9 12.1 %all-gather.2 = bf16[8,1,24]{2,1,0:T(2,128)(2,1)S(1)} all-gather(bf16[1,1,24]{2,1,0:T(2,128)(2,1)S(1)} %bitcast.461), channel_id=1, replica_groups=mesh['z'=4,'y'=2,'x'=2,'c'=2] {'y','x','c'}, dimensions={0}, use_global_device_ids=true | all-gather | bytes 432 | tf_op jit(solution)/shard_map/all_gather | solution.py:69
  275.9 26.3 %unpack.3 = (bf16[1536,1024]{1,0:T(8,128)(2,1)}, bf16[1024,2048]{1,0:T(8,128)(2,1)}, bf16[1024,2048]{1,0:T(8,128)(2,1)}, bf16[2048,1024]{1,0:T(8,128)(2,1)}, bf16[16,128]{1,0:T(8,128)(2,1)S(1)}) custom-call(s32[31,5]{1,0:T(8,128)S(1)} %copy-done.34, s32[32]{0:T(128)S(1)} %fusion.154.where_ref, bf16[3088,128]{1,0:T(8,128)(2,1)S(1)} %get-tuple-element.438.refs_0_, ...), custom_call_target="tpu_custom_call" | custom-call | bytes 33013760 | tf_op jit(solution)/shard_map/unpack/pallas_call | solution.py:464
  303.5 6.5 fusion.180
  314.2 11.9 %attend.1 = (f32[8,512,128]{2,1,0:T(8,128)S(1)}, f32[8,8,512]{2,1,0:T(8,128)S(1)}) custom-call(s32[4]{0:T(128)S(1)} %pad_add_fusion.2.meta_ref, bf16[8,512,128]{2,1,0:T(8,128)(2,1)S(1)} %pad.60.q_ref, bf16[8,2,512,128]{3,2,1,0:T(8,128)(2,1)S(1)} %bitcast.412, s32[512,1]{1,0:T(8,128)S(1)} %copy-done.32), custom_call_target="tpu_custom_call" | custom-call | flops 2000000000 | bytes 8388608 | tf_op jit(solution)/shard_map/attend/pallas_call | solution.py:749
  334.5 15.3 %while.32 = (s32[]{:T(128)}, f32[24,64,128]{2,1,0:T(8,128)S(1)}, s32[]{:T(128)}, bf16[8,24]{1,0:T(8,128)(2,1)}, bf16[8,24,64,128]{3,2,1,0:T(8,128)(2,1)}, /*index=5*/s32[]{:T(128)}, s32[]{:T(128)}) while((s32[]{:T(128)}, f32[24,64,128]{2,1,0:T(8,128)S(1)}, s32[]{:T(128)}, bf16[8,24]{1,0:T(8,128)(2,1)}, ...), condition=%wide.region_6.7_spmd.clone, body=%wide.region_5.6_spmd.clone.sunk | while | flops 983068 | bytes 1966425 | solution.py:86
  353.8 30.3 %fusion.33 = f32[512,24,64]{0,2,1:T(8,128)} fusion(f32[512,24,64]{0,2,1:T(8,128)S(1)} %bitcast.432, f32[512,24,64]{0,2,1:T(8,128)S(1)} %fusion.101, f32[512,512]{1,0:T(8,128)S(1)} %copy-done.103, f32[24,512]{1,0:T(8,128)} %get-tuple-element.451, pred[512,512]{1,0:T(8,128)(4,1)} %fusion.92, f32[24]{0:T(128)S(1)} %copy-done.175, ...), kind=kOutput, calls=%fused_computation.78 | convolution fusion | flops 4854644736 | bytes 10895456 | tf_op jit(solution)/shard_map/jvp(hts,shp->thp)/dot_general | solution.py:246
  388.1 5.3 multiply_reduce_fusion.11
  402.8 6.7 fusion.21
  454.1 36.1 %collective-permute-start.81 = (f32[4]{0:T(128)}, f32[4]{0:T(128)}, u32[]{:S(2)}, u32[]{:S(2)}) collective-permute-start(f32[4]{0:T(128)} %pad_maximum_fusion.14), channel_id=1, source_target_pairs={{0,4},{4,0},{1,5},{5,1},{2,6},{6,2},{3,7},{7,3},{8,12},{12,8},{9,1... | collective-permute-start | bytes 56 | tf_op jit(solution)/shard_map/ppermute | solution.py:900
  490.3 33.0 %fusion.8 = (f32[24,512]{1,0:T(8,128)S(1)}, f32[24,512]{1,0:T(8,128)S(1)}, f32[512,512]{1,0:T(8,128)}) fusion(f32[512,512]{1,0:T(8,128)S(1)} %copy-done.104, f32[24,512]{1,0:T(8,128)S(1)} %copy-done.147, pred[512,512]{1,0:T(8,128)(4,1)} %fusion.92, f32[24,64,512]{2,1,0:T(8,128)S(1)} %bitcast.424, f32[512,24,64]{0,2,1:T(8,128)} %bitcast.429, ...), kind=kOutput, calls=%fused_computation.13 | convolution fusion | flops 4888961024 | bytes 8847360 | tf_op jit(solution)/shard_map/transpose(jvp(hts,shp->thp))/dot_general | solution.py:246
  523.4 5.6 reduce-window.26
  534.3 17.4 %attend_back.1 = (bf16[8,2,512,128]{3,2,1,0:T(8,128)(2,1)S(1)}, f32[8,64,512]{2,1,0:T(8,128)S(1)}) custom-call(s32[4]{0:T(128)S(1)} %pad_add_fusion.2.meta_ref, bf16[8,512,128]{2,1,0:T(8,128)(2,1)S(1)} %copy-done.22, bf16[8,512,128]{2,1,0:T(8,128)(2,1)S(1)} %pad.70.g_ref, bf16[8,2,512,128]{3,2,1,0:T(8,128)(2,1)} %bitcast.413, f32[8,8,512]{2,1,0:T(8,128)S(1)} %copy-done.39, ...), custom_call_target="tpu_custom_call" | custom-call | flops 5000000000 | bytes 8388608 | tf_op jit(solution)/shard_map/attend_back/pallas_call | solution.py:834
  570.8 20.9 %pack.5 = bf16[49344,128]{1,0:T(8,128)(2,1)} custom-call(bf16[512,1024]{1,0:T(8,128)(2,1)S(1)} %copy-done.25, bf16[512,2048]{1,0:T(8,128)(2,1)S(1)} %copy-done.37, bf16[512,2048]{1,0:T(8,128)(2,1)} %pad_maximum_fusion.2.refs_2_, bf16[512,2048]{1,0:T(8,128)(2,1)} %pad_maximum_fusion.3.refs_3_, bf16[512,1024]{1,0:T(8,128)(2,1)S(1)} %copy-done.23, ...), custom_call_target="tpu_custom_call" | custom-call | flops 6442450944 | bytes 16777216 | tf_op jit(solution)/shard_map/pack/pallas_call | solution.py:618
  591.7 6.1 constant_dynamic-slice_fusion
  601.7 15.2 %collective-permute-start.50 = (bf16[2,2,2,512,128]{3,4,2,1,0:T(8,128)(2,1)}, bf16[2,2,2,512,128]{3,4,2,1,0:T(8,128)(2,1)}, u32[]{:S(2)}, u32[]{:S(2)}) collective-permute-start(bf16[2,2,2,512,128]{3,4,2,1,0:T(8,128)(2,1)} %bitcast.452), channel_id=1, source_target_pairs={{0,1},{1,0},{2,3},{3,2},{4,5},{5,4},{6,7},{7,6},{8,9},{9,8},{10,11... | collective-permute-start | bytes 3145736 | tf_op jit(solution)/shard_map/ppermute | solution.py:890
  624.9 5.0 fusion.84
  635.0 22.6 %fusion.3 = f32[24,64,512]{2,1,0:T(8,128)} fusion(f32[24,64,512]{2,1,0:T(8,128)S(1)} %bitcast.426, f32[512,512]{1,0:T(8,128)S(1)} %copy-done.105, f32[24,512]{1,0:T(8,128)S(1)} %copy-done.148, pred[512,512]{1,0:T(8,128)(4,1)S(1)} %copy-done.130), kind=kOutput, calls=%fused_computation.10 | convolution fusion | flops 4850712576 | bytes 7651328 | tf_op jit(solution)/shard_map/transpose(jvp(hts,shp->thp))/dot_general | solution.py:246
  660.9 25.8 %collective-permute-start.51 = (bf16[2,2,512,128]{2,3,1,0:T(8,128)(2,1)}, bf16[2,2,512,128]{2,3,1,0:T(8,128)(2,1)}, u32[]{:S(2)}, u32[]{:S(2)}) collective-permute-start(bf16[2,2,512,128]{2,3,1,0:T(8,128)(2,1)} %dynamic-slice_bitcast_fusion.20), channel_id=1, source_target_pairs={{0,4},{4,0},{1,5},{5,1},{2,6},{6,2},{3,7},{7,3},{8,12},{12,8},{9,1... | collective-permute-start | bytes 1572872 | tf_op jit(solution)/shard_map/ppermute | solution.py:890
  689.7 5.1 fusion.182
  694.8 4.9 collective-permute-done.51
  700.9 41.4 %collective-permute-start.52 = (bf16[2,512,128]{1,2,0:T(8,128)(2,1)S(1)}, bf16[2,512,128]{1,2,0:T(8,128)(2,1)S(1)}, u32[]{:S(2)}, u32[]{:S(2)}) collective-permute-start(bf16[2,512,128]{1,2,0:T(8,128)(2,1)S(1)} %dynamic-slice_bitcast_fusion.21), channel_id=1, source_target_pairs={{0,2},{2,0},{1,3},{3,1},{4,6},{6,4},{5,7},{7,5},{8,10},{10,8},{9,1... | collective-permute-start | bytes 786440 | tf_op jit(solution)/shard_map/ppermute | solution.py:890
  753.7 5.2 collective-permute-start.84
  770.3 15.2 %while.33 = (s32[]{:T(128)}, f32[24,64,128]{2,1,0:T(8,128)S(1)}, s32[]{:T(128)}, bf16[8,24]{1,0:T(8,128)(2,1)}, bf16[8,24,64,128]{3,2,1,0:T(8,128)(2,1)}, /*index=5*/s32[]{:T(128)}, s32[]{:T(128)}, s32[]{:T(128)}, s32[]{:T(128)}) while((s32[]{:T(128)}, f32[24,64,128]{2,1,0:T(8,128)S(1)}, s32[]{:T(128)}, ...), condition=%wide.region_13.14_spmd.clone, body=%wide.region_12.13_spmd.clone.sunk | while | flops 983072 | bytes 1966487 | solution.py:110
  785.9 7.1 fusion.81
  793.0 7.5 multiply_reduce_fusion.5
  801.6 5.0 reduce-window.24
  813.5 10.3 multiply_reduce_fusion.3
  825.5 6.5 collective-permute-start.49
  854.4 21.1 %pack.4 = bf16[49440,128]{1,0:T(8,128)(2,1)} custom-call(bf16[512,1024]{1,0:T(8,128)(2,1)S(1)} %copy-done.1, bf16[512,512]{1,0:T(8,128)(2,1)S(1)} %copy.188.refs_1_, bf16[512,512]{1,0:T(8,128)(2,1)S(1)} %copy-done.10, bf16[512,128]{1,0:T(8,128)(2,1)S(1)} %copy.190.refs_3_, bf16[512,128]{1,0:T(8,128)(2,1)S(1)} %copy-done.29, ...), custom_call_target="tpu_custom_call", output_to_operand_aliasing={{}: (11, {})} | custom-call | flops 4831838208 | bytes 20447232 | tf_op jit(solution)/shard_map/pack/pallas_call | solution.py:618
  875.5 7.3 add_convert_fusion
  888.2 32.9 %collective-permute-done.74 = bf16[2,3104,128]{2,1,0:T(8,128)(2,1)S(1)} collective-permute-done((bf16[2,3104,128]{2,1,0:T(8,128)(2,1)S(1)}, bf16[2,3104,128]{2,1,0:T(8,128)(2,1)S(1)}, u32[]{:S(2)}, u32[]{:S(2)}) %collective-permute-start.74) | collective-permute-done | bytes 1589280 | tf_op jit(solution)/shard_map/ppermute | solution.py:672
  925.3 15.6 %collective-permute-done.75 = bf16[3104,128]{1,0:T(8,128)(2,1)S(1)} collective-permute-done((bf16[3104,128]{1,0:T(8,128)(2,1)S(1)}, bf16[3104,128]{1,0:T(8,128)(2,1)S(1)}, u32[]{:S(2)}, u32[]{:S(2)}) %collective-permute-start.75) | collective-permute-done | bytes 794656 | tf_op jit(solution)/shard_map/ppermute | solution.py:675
  948.1 14.9 %collective-permute-done.76 = bf16[3104,128]{1,0:T(8,128)(2,1)S(1)} collective-permute-done((bf16[3104,128]{1,0:T(8,128)(2,1)S(1)}, bf16[3104,128]{1,0:T(8,128)(2,1)S(1)}, u32[]{:S(2)}, u32[]{:S(2)}) %collective-permute-start.76) | collective-permute-done | bytes 794656 | tf_op jit(solution)/shard_map/ppermute | solution.py:682
  964.8 13.2 %collective-permute-done.70 = bf16[3104,128]{1,0:T(8,128)(2,1)S(1)} collective-permute-done((bf16[3104,128]{1,0:T(8,128)(2,1)S(1)}, bf16[3104,128]{1,0:T(8,128)(2,1)S(1)}, u32[]{:S(2)}, u32[]{:S(2)}) %collective-permute-start.70) | collective-permute-done | bytes 794656 | tf_op jit(solution)/shard_map/ppermute | solution.py:682
  991.0 27.6 %collective-permute-done.60 = bf16[2,3104,128]{2,1,0:T(8,128)(2,1)S(1)} collective-permute-done((bf16[2,3104,128]{2,1,0:T(8,128)(2,1)S(1)}, bf16[2,3104,128]{2,1,0:T(8,128)(2,1)S(1)}, u32[]{:S(2)}, u32[]{:S(2)}) %collective-permute-start.60) | collective-permute-done | bytes 1589280 | tf_op jit(solution)/shard_map/ppermute | solution.py:672
  1026.8 11.5 %collective-permute-done.61 = bf16[3104,128]{1,0:T(8,128)(2,1)S(1)} collective-permute-done((bf16[3104,128]{1,0:T(8,128)(2,1)S(1)}, bf16[3104,128]{1,0:T(8,128)(2,1)S(1)}, u32[]{:S(2)}, u32[]{:S(2)}) %collective-permute-start.61) | collective-permute-done | bytes 794656 | tf_op jit(solution)/shard_map/ppermute | solution.py:675
  1047.4 73.2 %collective-permute-start.80 = (bf16[3104,128]{1,0:T(8,128)(2,1)S(1)}, bf16[3104,128]{1,0:T(8,128)(2,1)S(1)}, u32[]{:S(2)}, u32[]{:S(2)}) collective-permute-start(bf16[3104,128]{1,0:T(8,128)(2,1)S(1)} %get-tuple-element.381), channel_id=1, source_target_pairs={{0,1},{9,8},{16,17},{25,24},{2,3},{11,10},{18,19},{27,26},{4,5},{1... | collective-permute-start | bytes 2383880 | tf_op jit(solution)/shard_map/ppermute | solution.py:690
  1120.6 7.8 collective-permute-done.59
  (807 shorter events, 419.1 us)
Async XLA Ops:
  7.2 327.3 %all-gather.6.cloned.1.call-start = ((), (), s32[]{:S(2)}) async-start(), calls=%async_computation | async-start | bytes 3538944 | tf_op jit(solution)/shard_map/all_gather | solution.py:69
  37.9 29.5 %collective-permute-start.29 = (bf16[3088,128]{1,0:T(8,128)(2,1)S(1)}, bf16[3088,128]{1,0:T(8,128)(2,1)}, u32[]{:S(2)}, u32[]{:S(2)}) collective-permute-start(bf16[3088,128]{1,0:T(8,128)(2,1)S(1)} %collective-permute-done.27), channel_id=1, source_target_pairs={{8,0},{17,9},{10,2},{19,11},{12,4},{21,13},{14,6},{23,15}} | collective-permute-start | bytes 2371592 | tf_op jit(solution)/shard_map/ppermute | solution.py:312
  41.9 26.2 %collective-permute-start.3 = (bf16[3088,128]{1,0:T(8,128)(2,1)S(1)}, bf16[3088,128]{1,0:T(8,128)(2,1)}, u32[]{:S(2)}, u32[]{:S(2)}) collective-permute-start(bf16[3088,128]{1,0:T(8,128)(2,1)S(1)} %collective-permute-done.1), channel_id=1, source_target_pairs={{8,16},{17,25},{10,18},{19,27},{12,20},{21,29},{14,22},{23,31}} | collective-permute-start | bytes 2371592 | tf_op jit(solution)/shard_map/ppermute | solution.py:307
  43.5 25.4 %collective-permute-start.15 = (bf16[3088,128]{1,0:T(8,128)(2,1)}, bf16[3088,128]{1,0:T(8,128)(2,1)}, u32[]{:S(2)}, u32[]{:S(2)}) collective-permute-start(bf16[3088,128]{1,0:T(8,128)(2,1)} %collective-permute-done.14), channel_id=1, source_target_pairs={{16,24},{18,26},{20,28},{22,30}} | collective-permute-start | bytes 2371592 | tf_op jit(solution)/shard_map/ppermute | solution.py:308
  51.1 24.3 %collective-permute-start.2 = (bf16[3088,128]{1,0:T(8,128)(2,1)S(1)}, bf16[3088,128]{1,0:T(8,128)(2,1)S(1)}, u32[]{:S(2)}, u32[]{:S(2)}) collective-permute-start(bf16[3088,128]{1,0:T(8,128)(2,1)S(1)} %get-tuple-element.430), channel_id=1, source_target_pairs={{9,1},{11,3},{13,5},{15,7}} | collective-permute-start | bytes 2371592 | tf_op jit(solution)/shard_map/ppermute | solution.py:306
  73.8 20.7 %collective-permute-start.17 = (bf16[3088,128]{1,0:T(8,128)(2,1)}, bf16[3088,128]{1,0:T(8,128)(2,1)}, u32[]{:S(2)}, u32[]{:S(2)}) collective-permute-start(bf16[3088,128]{1,0:T(8,128)(2,1)} %get-tuple-element.436.refs_8_), channel_id=1, source_target_pairs={{0,4},{4,0},{1,5},{5,1},{2,6},{6,2},{3,7},{7,3},{8,12},{12,8},{9,1... | collective-permute-start | bytes 2371592 | tf_op jit(solution)/shard_map/ppermute | solution.py:317
  75.4 36.3 %collective-permute-start.16 = (bf16[3088,128]{1,0:T(8,128)(2,1)}, bf16[3088,128]{1,0:T(8,128)(2,1)S(1)}, u32[]{:S(2)}, u32[]{:S(2)}) collective-permute-start(bf16[3088,128]{1,0:T(8,128)(2,1)} %get-tuple-element.436.refs_8_), channel_id=1, source_target_pairs={{0,2},{2,0},{1,3},{3,1},{4,6},{6,4},{5,7},{7,5},{8,10},{10,8},{9,1... | collective-permute-start | bytes 2371592 | tf_op jit(solution)/shard_map/ppermute | solution.py:316
  79.7 30.5 %collective-permute-start.5 = (bf16[3088,128]{1,0:T(8,128)(2,1)S(1)}, bf16[3088,128]{1,0:T(8,128)(2,1)S(1)}, u32[]{:S(2)}, u32[]{:S(2)}) collective-permute-start(bf16[3088,128]{1,0:T(8,128)(2,1)S(1)} %get-tuple-element.438.refs_0_), channel_id=1, source_target_pairs={{0,2},{2,0},{1,3},{3,1},{4,6},{6,4},{5,7},{7,5},{8,10},{10,8},{9,1... | collective-permute-start | bytes 2371592 | tf_op jit(solution)/shard_map/ppermute | solution.py:316
  80.3 33.7 %collective-permute-start.6 = (bf16[3088,128]{1,0:T(8,128)(2,1)S(1)}, bf16[3088,128]{1,0:T(8,128)(2,1)S(1)}, u32[]{:S(2)}, u32[]{:S(2)}) collective-permute-start(bf16[3088,128]{1,0:T(8,128)(2,1)S(1)} %get-tuple-element.438.refs_0_), channel_id=1, source_target_pairs={{0,4},{4,0},{1,5},{5,1},{2,6},{6,2},{3,7},{7,3},{8,12},{12,8},{9,1... | collective-permute-start | bytes 2371592 | tf_op jit(solution)/shard_map/ppermute | solution.py:317
  81.5 41.3 %collective-permute-start.19 = (bf16[3088,128]{1,0:T(8,128)(2,1)}, bf16[3088,128]{1,0:T(8,128)(2,1)}, u32[]{:S(2)}, u32[]{:S(2)}) collective-permute-start(bf16[3088,128]{1,0:T(8,128)(2,1)} %get-tuple-element.436.refs_8_), channel_id=1, source_target_pairs={{0,1},{1,0},{2,3},{3,2},{4,5},{5,4},{6,7},{7,6},{8,9},{9,8},{10,11... | collective-permute-start | bytes 2371592 | tf_op jit(solution)/shard_map/ppermute | solution.py:323
  94.5 28.3 %collective-permute-start.8 = (bf16[3088,128]{1,0:T(8,128)(2,1)S(1)}, bf16[3088,128]{1,0:T(8,128)(2,1)S(1)}, u32[]{:S(2)}, u32[]{:S(2)}) collective-permute-start(bf16[3088,128]{1,0:T(8,128)(2,1)S(1)} %get-tuple-element.438.refs_0_), channel_id=1, source_target_pairs={{0,1},{1,0},{2,3},{3,2},{4,5},{5,4},{6,7},{7,6},{8,9},{9,8},{10,11... | collective-permute-start | bytes 2371592 | tf_op jit(solution)/shard_map/ppermute | solution.py:323
  111.6 22.1 %collective-permute-start.21 = (bf16[3088,128]{1,0:T(8,128)(2,1)}, bf16[3088,128]{1,0:T(8,128)(2,1)}, u32[]{:S(2)}, u32[]{:S(2)}) collective-permute-start(bf16[3088,128]{1,0:T(8,128)(2,1)} %collective-permute-done.17.refs_10_), channel_id=1, source_target_pairs={{0,1},{1,0},{2,3},{3,2},{4,5},{5,4},{6,7},{7,6},{8,9},{9,8},{10,11... | collective-permute-start | bytes 2371592 | tf_op jit(solution)/shard_map/ppermute | solution.py:323
  136.1 76.1 %collective-permute-start.43 = (bf16[3088,128]{1,0:T(8,128)(2,1)}, bf16[3088,128]{1,0:T(8,128)(2,1)}, u32[]{:S(2)}, u32[]{:S(2)}) collective-permute-start(bf16[3088,128]{1,0:T(8,128)(2,1)} %get-tuple-element.435.refs_24_), channel_id=1, source_target_pairs={{0,4},{4,0},{1,5},{5,1},{2,6},{6,2},{3,7},{7,3},{8,12},{12,8},{9,1... | collective-permute-start | bytes 2371592 | tf_op jit(solution)/shard_map/ppermute | solution.py:317
  136.8 82.3 %collective-permute-start.42 = (bf16[3088,128]{1,0:T(8,128)(2,1)}, bf16[3088,128]{1,0:T(8,128)(2,1)}, u32[]{:S(2)}, u32[]{:S(2)}) collective-permute-start(bf16[3088,128]{1,0:T(8,128)(2,1)} %get-tuple-element.435.refs_24_), channel_id=1, source_target_pairs={{0,2},{2,0},{1,3},{3,1},{4,6},{6,4},{5,7},{7,5},{8,10},{10,8},{9,1... | collective-permute-start | bytes 2371592 | tf_op jit(solution)/shard_map/ppermute | solution.py:316
  137.3 75.5 %collective-permute-start.31 = (bf16[3088,128]{1,0:T(8,128)(2,1)}, bf16[3088,128]{1,0:T(8,128)(2,1)}, u32[]{:S(2)}, u32[]{:S(2)}) collective-permute-start(bf16[3088,128]{1,0:T(8,128)(2,1)} %get-tuple-element.437.refs_16_), channel_id=1, source_target_pairs={{0,2},{2,0},{1,3},{3,1},{4,6},{6,4},{5,7},{7,5},{8,10},{10,8},{9,1... | collective-permute-start | bytes 2371592 | tf_op jit(solution)/shard_map/ppermute | solution.py:316
  138.8 80.6 %collective-permute-start.32 = (bf16[3088,128]{1,0:T(8,128)(2,1)}, bf16[3088,128]{1,0:T(8,128)(2,1)}, u32[]{:S(2)}, u32[]{:S(2)}) collective-permute-start(bf16[3088,128]{1,0:T(8,128)(2,1)} %get-tuple-element.437.refs_16_), channel_id=1, source_target_pairs={{0,4},{4,0},{1,5},{5,1},{2,6},{6,2},{3,7},{7,3},{8,12},{12,8},{9,1... | collective-permute-start | bytes 2371592 | tf_op jit(solution)/shard_map/ppermute | solution.py:317
  200.7 569.6 %all-gather.8.cloned.1.call-start = ((), (), s32[]{:S(2)}) async-start(), calls=%async_computation.1 | async-start | bytes 3538944 | tf_op jit(solution)/shard_map/all_gather | solution.py:92
  212.9 35.2 %collective-permute-start.44 = (bf16[3088,128]{1,0:T(8,128)(2,1)}, bf16[3088,128]{1,0:T(8,128)(2,1)}, u32[]{:S(2)}, u32[]{:S(2)}) collective-permute-start(bf16[3088,128]{1,0:T(8,128)(2,1)} %collective-permute-done.43.refs_26_), channel_id=1, source_target_pairs={{0,2},{2,0},{1,3},{3,1},{4,6},{6,4},{5,7},{7,5},{8,10},{10,8},{9,1... | collective-permute-start | bytes 2371592 | tf_op jit(solution)/shard_map/ppermute | solution.py:321
  219.1 29.6 %collective-permute-start.47 = (bf16[3088,128]{1,0:T(8,128)(2,1)}, bf16[3088,128]{1,0:T(8,128)(2,1)}, u32[]{:S(2)}, u32[]{:S(2)}) collective-permute-start(bf16[3088,128]{1,0:T(8,128)(2,1)} %collective-permute-done.43.refs_26_), channel_id=1, source_target_pairs={{0,1},{1,0},{2,3},{3,2},{4,5},{5,4},{6,7},{7,6},{8,9},{9,8},{10,11... | collective-permute-start | bytes 2371592 | tf_op jit(solution)/shard_map/ppermute | solution.py:323
  219.4 28.7 %collective-permute-start.33 = (bf16[3088,128]{1,0:T(8,128)(2,1)}, bf16[3088,128]{1,0:T(8,128)(2,1)}, u32[]{:S(2)}, u32[]{:S(2)}) collective-permute-start(bf16[3088,128]{1,0:T(8,128)(2,1)} %collective-permute-done.31.refs_17_), channel_id=1, source_target_pairs={{0,4},{4,0},{1,5},{5,1},{2,6},{6,2},{3,7},{7,3},{8,12},{12,8},{9,1... | collective-permute-start | bytes 2371592 | tf_op jit(solution)/shard_map/ppermute | solution.py:319
  222.3 32.5 %collective-permute-start.35 = (bf16[3088,128]{1,0:T(8,128)(2,1)}, bf16[3088,128]{1,0:T(8,128)(2,1)}, u32[]{:S(2)}, u32[]{:S(2)}) collective-permute-start(bf16[3088,128]{1,0:T(8,128)(2,1)} %collective-permute-done.31.refs_17_), channel_id=1, source_target_pairs={{0,1},{1,0},{2,3},{3,2},{4,5},{5,4},{6,7},{7,6},{8,9},{9,8},{10,11... | collective-permute-start | bytes 2371592 | tf_op jit(solution)/shard_map/ppermute | solution.py:323
  230.4 22.9 %collective-permute-start.23 = (bf16[2,512,128]{2,1,0:T(8,128)(2,1)}, bf16[2,512,128]{2,1,0:T(8,128)(2,1)}, u32[]{:S(2)}, u32[]{:S(2)}) collective-permute-start(bf16[2,512,128]{2,1,0:T(8,128)(2,1)} %maximum_bitcast_fusion), channel_id=1, source_target_pairs={{0,2},{2,0},{1,3},{3,1},{4,6},{6,4},{5,7},{7,5},{8,10},{10,8},{9,1... | collective-permute-start | bytes 786440 | tf_op jit(solution)/shard_map/ppermute | solution.py:876
  248.1 25.4 %collective-permute-start.46 = (bf16[3088,128]{1,0:T(8,128)(2,1)}, bf16[3088,128]{1,0:T(8,128)(2,1)S(1)}, u32[]{:S(2)}, u32[]{:S(2)}) collective-permute-start(bf16[3088,128]{1,0:T(8,128)(2,1)} %collective-permute-done.42.refs_25_), channel_id=1, source_target_pairs={{0,1},{1,0},{2,3},{3,2},{4,5},{5,4},{6,7},{7,6},{8,9},{9,8},{10,11... | collective-permute-start | bytes 2371592 | tf_op jit(solution)/shard_map/ppermute | solution.py:323
  248.1 25.4 %collective-permute-start.36 = (bf16[3088,128]{1,0:T(8,128)(2,1)}, bf16[3088,128]{1,0:T(8,128)(2,1)S(1)}, u32[]{:S(2)}, u32[]{:S(2)}) collective-permute-start(bf16[3088,128]{1,0:T(8,128)(2,1)} %collective-permute-done.32.refs_18_), channel_id=1, source_target_pairs={{0,1},{1,0},{2,3},{3,2},{4,5},{5,4},{6,7},{7,6},{8,9},{9,8},{10,11... | collective-permute-start | bytes 2371592 | tf_op jit(solution)/shard_map/ppermute | solution.py:323
  248.6 24.9 %collective-permute-start.48 = (bf16[3088,128]{1,0:T(8,128)(2,1)}, bf16[3088,128]{1,0:T(8,128)(2,1)S(1)}, u32[]{:S(2)}, u32[]{:S(2)}) collective-permute-start(bf16[3088,128]{1,0:T(8,128)(2,1)} %collective-permute-done.44.refs_27_), channel_id=1, source_target_pairs={{0,1},{1,0},{2,3},{3,2},{4,5},{5,4},{6,7},{7,6},{8,9},{9,8},{10,11... | collective-permute-start | bytes 2371592 | tf_op jit(solution)/shard_map/ppermute | solution.py:323
  253.2 20.3 %collective-permute-start.37 = (bf16[3088,128]{1,0:T(8,128)(2,1)}, bf16[3088,128]{1,0:T(8,128)(2,1)S(1)}, u32[]{:S(2)}, u32[]{:S(2)}) collective-permute-start(bf16[3088,128]{1,0:T(8,128)(2,1)} %collective-permute-done.33.refs_19_), channel_id=1, source_target_pairs={{0,1},{1,0},{2,3},{3,2},{4,5},{5,4},{6,7},{7,6},{8,9},{9,8},{10,11... | collective-permute-start | bytes 2371592 | tf_op jit(solution)/shard_map/ppermute | solution.py:323
  254.8 48.1 %collective-permute-start.24 = (bf16[2,2,512,128]{3,2,1,0:T(8,128)(2,1)S(1)}, bf16[2,2,512,128]{3,2,1,0:T(8,128)(2,1)S(1)}, u32[]{:S(2)}, u32[]{:S(2)}) collective-permute-start(bf16[2,2,512,128]{3,2,1,0:T(8,128)(2,1)S(1)} %pad_maximum_fusion.12), channel_id=1, source_target_pairs={{0,4},{4,0},{1,5},{5,1},{2,6},{6,2},{3,7},{7,3},{8,12},{12,8},{9,1... | collective-permute-start | bytes 1572872 | tf_op jit(solution)/shard_map/ppermute | solution.py:877
  454.1 288.2 %collective-permute-start.81 = (f32[4]{0:T(128)}, f32[4]{0:T(128)}, u32[]{:S(2)}, u32[]{:S(2)}) collective-permute-start(f32[4]{0:T(128)} %pad_maximum_fusion.14), channel_id=1, source_target_pairs={{0,4},{4,0},{1,5},{5,1},{2,6},{6,2},{3,7},{7,3},{8,12},{12,8},{9,1... | collective-permute-start | bytes 56 | tf_op jit(solution)/shard_map/ppermute | solution.py:900
  601.7 55.8 %collective-permute-start.50 = (bf16[2,2,2,512,128]{3,4,2,1,0:T(8,128)(2,1)}, bf16[2,2,2,512,128]{3,4,2,1,0:T(8,128)(2,1)}, u32[]{:S(2)}, u32[]{:S(2)}) collective-permute-start(bf16[2,2,2,512,128]{3,4,2,1,0:T(8,128)(2,1)} %bitcast.452), channel_id=1, source_target_pairs={{0,1},{1,0},{2,3},{3,2},{4,5},{5,4},{6,7},{7,6},{8,9},{9,8},{10,11... | collective-permute-start | bytes 3145736 | tf_op jit(solution)/shard_map/ppermute | solution.py:890
  619.2 256.3 %collective-permute-start.67 = (bf16[24688,128]{1,0:T(8,128)(2,1)}, bf16[24688,128]{1,0:T(8,128)(2,1)}, u32[]{:S(2)}, u32[]{:S(2)}) collective-permute-start(bf16[24688,128]{1,0:T(8,128)(2,1)} %constant_dynamic-slice_fusion), channel_id=1, source_target_pairs={{0,1},{1,0},{2,3},{3,2},{4,5},{5,4},{6,7},{7,6},{8,9},{9,8},{10,11... | collective-permute-start | bytes 18960392 | tf_op jit(solution)/shard_map/ppermute | solution.py:655
  660.9 38.8 %collective-permute-start.51 = (bf16[2,2,512,128]{2,3,1,0:T(8,128)(2,1)}, bf16[2,2,512,128]{2,3,1,0:T(8,128)(2,1)}, u32[]{:S(2)}, u32[]{:S(2)}) collective-permute-start(bf16[2,2,512,128]{2,3,1,0:T(8,128)(2,1)} %dynamic-slice_bitcast_fusion.20), channel_id=1, source_target_pairs={{0,4},{4,0},{1,5},{5,1},{2,6},{6,2},{3,7},{7,3},{8,12},{12,8},{9,1... | collective-permute-start | bytes 1572872 | tf_op jit(solution)/shard_map/ppermute | solution.py:890
  700.9 66.5 %collective-permute-start.52 = (bf16[2,512,128]{1,2,0:T(8,128)(2,1)S(1)}, bf16[2,512,128]{1,2,0:T(8,128)(2,1)S(1)}, u32[]{:S(2)}, u32[]{:S(2)}) collective-permute-start(bf16[2,512,128]{1,2,0:T(8,128)(2,1)S(1)} %dynamic-slice_bitcast_fusion.21), channel_id=1, source_target_pairs={{0,2},{2,0},{1,3},{3,1},{4,6},{6,4},{5,7},{7,5},{8,10},{10,8},{9,1... | collective-permute-start | bytes 786440 | tf_op jit(solution)/shard_map/ppermute | solution.py:890
  762.8 367.6 %collective-permute-start.85 = (f32[4]{0:T(128)}, f32[4]{0:T(128)}, u32[]{:S(2)}, u32[]{:S(2)}) collective-permute-start(f32[4]{0:T(128)} %add.823), channel_id=1, source_target_pairs={{0,16},{16,0},{8,24},{24,8},{1,17},{17,1},{9,25},{25,9},{2,18},{18... | collective-permute-start | bytes 56 | tf_op jit(solution)/shard_map/ppermute | solution.py:902
  883.4 37.8 %collective-permute-start.74 = (bf16[2,3104,128]{2,1,0:T(8,128)(2,1)S(1)}, bf16[2,3104,128]{2,1,0:T(8,128)(2,1)S(1)}, u32[]{:S(2)}, u32[]{:S(2)}) collective-permute-start(bf16[2,3104,128]{2,1,0:T(8,128)(2,1)S(1)} %pad_maximum_fusion.7), channel_id=1, source_target_pairs={{0,2},{2,0},{1,3},{3,1},{4,6},{6,4},{5,7},{7,5},{8,10},{10,8},{9,1... | collective-permute-start | bytes 4767752 | tf_op jit(solution)/shard_map/ppermute | solution.py:672
  886.2 37.2 %collective-permute-start.68 = (bf16[2,3104,128]{2,1,0:T(8,128)(2,1)S(1)}, bf16[2,3104,128]{2,1,0:T(8,128)(2,1)S(1)}, u32[]{:S(2)}, u32[]{:S(2)}) collective-permute-start(bf16[2,3104,128]{2,1,0:T(8,128)(2,1)S(1)} %pad_maximum_fusion.6), channel_id=1, source_target_pairs={{0,4},{4,0},{1,5},{5,1},{2,6},{6,2},{3,7},{7,3},{8,12},{12,8},{9,1... | collective-permute-start | bytes 4767752 | tf_op jit(solution)/shard_map/ppermute | solution.py:672
  888.2 91.7 %collective-permute-start.53 = (bf16[24688,128]{1,0:T(8,128)(2,1)S(1)}, bf16[24688,128]{1,0:T(8,128)(2,1)S(1)}, u32[]{:S(2)}, u32[]{:S(2)}) collective-permute-start(bf16[24688,128]{1,0:T(8,128)(2,1)S(1)} %constant_dynamic-slice_fusion.1), channel_id=1, source_target_pairs={{0,1},{1,0},{2,3},{3,2},{4,5},{5,4},{6,7},{7,6},{8,9},{9,8},{10,11... | collective-permute-start | bytes 18960392 | tf_op jit(solution)/shard_map/ppermute | solution.py:655
  923.9 22.7 %collective-permute-start.69 = (bf16[3104,128]{1,0:T(8,128)(2,1)S(1)}, bf16[3104,128]{1,0:T(8,128)(2,1)S(1)}, u32[]{:S(2)}, u32[]{:S(2)}) collective-permute-start(bf16[3104,128]{1,0:T(8,128)(2,1)S(1)} %dynamic-slice_bitcast_fusion.5), channel_id=1, source_target_pairs={{0,2},{2,0},{1,3},{3,1},{4,6},{6,4},{5,7},{7,5},{8,10},{10,8},{9,1... | collective-permute-start | bytes 2383880 | tf_op jit(solution)/shard_map/ppermute | solution.py:675
  941.1 21.9 %collective-permute-start.76 = (bf16[3104,128]{1,0:T(8,128)(2,1)S(1)}, bf16[3104,128]{1,0:T(8,128)(2,1)S(1)}, u32[]{:S(2)}, u32[]{:S(2)}) collective-permute-start(bf16[3104,128]{1,0:T(8,128)(2,1)S(1)} %fusion.62), channel_id=1, source_target_pairs={{0,8},{1,9},{2,10},{3,11},{4,12},{5,13},{6,14},{7,15}} | collective-permute-start | bytes 2383880 | tf_op jit(solution)/shard_map/ppermute | solution.py:682
  945.0 38.8 %collective-permute-start.78 = (bf16[3104,128]{1,0:T(8,128)(2,1)S(1)}, bf16[3104,128]{1,0:T(8,128)(2,1)}, u32[]{:S(2)}, u32[]{:S(2)}) collective-permute-start(bf16[3104,128]{1,0:T(8,128)(2,1)S(1)} %fusion.62), channel_id=1, source_target_pairs={{24,16},{26,18},{28,20},{30,22}} | collective-permute-start | bytes 2383880 | tf_op jit(solution)/shard_map/ppermute | solution.py:683
  946.8 31.3 %collective-permute-start.70 = (bf16[3104,128]{1,0:T(8,128)(2,1)S(1)}, bf16[3104,128]{1,0:T(8,128)(2,1)S(1)}, u32[]{:S(2)}, u32[]{:S(2)}) collective-permute-start(bf16[3104,128]{1,0:T(8,128)(2,1)S(1)} %fusion.63), channel_id=1, source_target_pairs={{0,8},{1,9},{2,10},{3,11},{4,12},{5,13},{6,14},{7,15}} | collective-permute-start | bytes 2383880 | tf_op jit(solution)/shard_map/ppermute | solution.py:682
  963.1 23.7 %collective-permute-start.72 = (bf16[3104,128]{1,0:T(8,128)(2,1)S(1)}, bf16[3104,128]{1,0:T(8,128)(2,1)}, u32[]{:S(2)}, u32[]{:S(2)}) collective-permute-start(bf16[3104,128]{1,0:T(8,128)(2,1)S(1)} %fusion.63), channel_id=1, source_target_pairs={{24,16},{26,18},{28,20},{30,22}} | collective-permute-start | bytes 2383880 | tf_op jit(solution)/shard_map/ppermute | solution.py:683
  983.8 34.8 %collective-permute-start.60 = (bf16[2,3104,128]{2,1,0:T(8,128)(2,1)S(1)}, bf16[2,3104,128]{2,1,0:T(8,128)(2,1)S(1)}, u32[]{:S(2)}, u32[]{:S(2)}) collective-permute-start(bf16[2,3104,128]{2,1,0:T(8,128)(2,1)S(1)} %pad_maximum_fusion.5), channel_id=1, source_target_pairs={{0,2},{2,0},{1,3},{3,1},{4,6},{6,4},{5,7},{7,5},{8,10},{10,8},{9,1... | collective-permute-start | bytes 4767752 | tf_op jit(solution)/shard_map/ppermute | solution.py:672
  985.9 60.9 %collective-permute-start.79 = (bf16[3104,128]{1,0:T(8,128)(2,1)S(1)}, bf16[3104,128]{1,0:T(8,128)(2,1)S(1)}, u32[]{:S(2)}, u32[]{:S(2)}) collective-permute-start(bf16[3104,128]{1,0:T(8,128)(2,1)S(1)} %add_convert_fusion.9), channel_id=1, source_target_pairs={{17,25},{19,27},{21,29},{23,31}} | collective-permute-start | bytes 2383880 | tf_op jit(solution)/shard_map/ppermute | solution.py:685
  986.8 36.8 %collective-permute-start.54 = (bf16[2,3104,128]{2,1,0:T(8,128)(2,1)S(1)}, bf16[2,3104,128]{2,1,0:T(8,128)(2,1)S(1)}, u32[]{:S(2)}, u32[]{:S(2)}) collective-permute-start(bf16[2,3104,128]{2,1,0:T(8,128)(2,1)S(1)} %pad_maximum_fusion.4), channel_id=1, source_target_pairs={{0,4},{4,0},{1,5},{5,1},{2,6},{6,2},{3,7},{7,3},{8,12},{12,8},{9,1... | collective-permute-start | bytes 4767752 | tf_op jit(solution)/shard_map/ppermute | solution.py:672
  990.1 56.7 %collective-permute-start.73 = (bf16[3104,128]{1,0:T(8,128)(2,1)S(1)}, bf16[3104,128]{1,0:T(8,128)(2,1)S(1)}, u32[]{:S(2)}, u32[]{:S(2)}) collective-permute-start(bf16[3104,128]{1,0:T(8,128)(2,1)S(1)} %add_convert_fusion.12), channel_id=1, source_target_pairs={{17,25},{19,27},{21,29},{23,31}} | collective-permute-start | bytes 2383880 | tf_op jit(solution)/shard_map/ppermute | solution.py:685
  1043.8 76.7 %collective-permute-start.65 = (bf16[3104,128]{1,0:T(8,128)(2,1)S(1)}, bf16[3104,128]{1,0:T(8,128)(2,1)S(1)}, u32[]{:S(2)}, u32[]{:S(2)}) collective-permute-start(bf16[3104,128]{1,0:T(8,128)(2,1)S(1)} %add_convert_fusion.15), channel_id=1, source_target_pairs={{8,0},{10,2},{12,4},{14,6}} | collective-permute-start | bytes 2383880 | tf_op jit(solution)/shard_map/ppermute | solution.py:680
  1045.5 82.8 %collective-permute-start.59 = (bf16[3104,128]{1,0:T(8,128)(2,1)S(1)}, bf16[3104,128]{1,0:T(8,128)(2,1)S(1)}, u32[]{:S(2)}, u32[]{:S(2)}) collective-permute-start(bf16[3104,128]{1,0:T(8,128)(2,1)S(1)} %add_convert_fusion.18), channel_id=1, source_target_pairs={{8,0},{10,2},{12,4},{14,6}} | collective-permute-start | bytes 2383880 | tf_op jit(solution)/shard_map/ppermute | solution.py:680
  1047.4 86.8 %collective-permute-start.80 = (bf16[3104,128]{1,0:T(8,128)(2,1)S(1)}, bf16[3104,128]{1,0:T(8,128)(2,1)S(1)}, u32[]{:S(2)}, u32[]{:S(2)}) collective-permute-start(bf16[3104,128]{1,0:T(8,128)(2,1)S(1)} %get-tuple-element.381), channel_id=1, source_target_pairs={{0,1},{9,8},{16,17},{25,24},{2,3},{11,10},{18,19},{27,26},{4,5},{1... | collective-permute-start | bytes 2383880 | tf_op jit(solution)/shard_map/ppermute | solution.py:690
  (234 other events, 3563.1 us)
Sparse Core Ops, SparseCore 0:
  200.9 42.6 all-gather.5
  529.2 66.8 all-gather.7

commit v3 on v2

--- a/solution.py
+++ b/solution.py
@@ -217,57 +217,6 @@
             conv_total + jnp.where(valid_rows, window, 0.0) * conv_weight[tap_index][None, :]
         )
     return jax.nn.silu(conv_total)
-
-
-def split_conv(conv_values):
-    ssm_inner = SSM_HEADS * SSM_DIM
-    x_ssm = conv_values[:, :ssm_inner].reshape(conv_values.shape[0], SSM_HEADS, SSM_DIM)
-    return (
-        x_ssm,
-        conv_values[:, ssm_inner : ssm_inner + STATE],
-        conv_values[:, ssm_inner + STATE :],
-    )
-
-
-def ssd_entry(cumul, seq_id, positions):
-    carried = (seq_id == seq_id[0]) & (positions[0] > 0)
-    return jnp.where(carried[:, None], jnp.exp(cumul), 0.0)
-
-
-def ssd_output(x_ssm, b_in, c_in, step_size, decay, skip_gain, seq_id, positions, state_in):
-    row_count = seq_id.shape[0]
-    cumul = jnp.cumsum(step_size * decay[None, :], axis=0)
-    order_rows = jnp.arange(row_count)
-    visible = (seq_id[:, None] == seq_id[None, :]) & (order_rows[:, None] >= order_rows[None, :])
-    log_gaps = cumul.T[:, :, None] - cumul.T[:, None, :]
-    kernel = jnp.exp(jnp.where(visible[None], log_gaps, masked_score))
-    inner_products = jnp.dot(c_in, b_in.T, precision=highest)
-    scaled_x = x_ssm * step_size[:, :, None]
-    intra_part = jnp.einsum(
-        "hts,shp->thp", kernel * inner_products[None], scaled_x, precision=highest
-    )
-    entry_decay = ssd_entry(cumul, seq_id, positions)
-    from_state = (
-        jnp.einsum("hpn,tn->thp", state_in, c_in, precision=highest) * entry_decay[:, :, None]
-    )
-    return intra_part + from_state + skip_gain[None, :, None] * x_ssm
-
-
-def ssd_summary(x_ssm, b_in, step_size, decay, seq_id, positions):
-    cumul = jnp.cumsum(step_size * decay[None, :], axis=0)
-    carried_last = (seq_id[-1] == seq_id[0]) & (positions[0] > 0)
-    carry_all = jnp.where(carried_last, jnp.exp(cumul[-1]), 0.0)
-    tail_decay = jnp.exp(
-        jnp.where((seq_id == seq_id[-1])[:, None], cumul[-1:] - cumul, masked_score)
-    )
-    local_state = jnp.einsum(
-        "sh,shp,sn->hpn", tail_decay, x_ssm * step_size[:, :, None], b_in, precision=highest
-    )
-    return (carry_all, local_state)
-
-
-def chain_states(earlier, later):
-    return (earlier[0] * later[0], earlier[1] * later[0][:, None, None] + later[1])
 
 
 def add_rows(target, addend, first_row):
@@ -691,15 +640,314 @@
     return jnp.where(c == z % 2, mine, handed)
 
 
+CHUNK = 128
+NT = (((1,), (1,)), ((), ()))
+TN = (((0,), (0,)), ((), ()))
+INNER = SSM_HEADS * SSM_DIM
+PAIRS = SSM_HEADS // 2
+
+
+def spread(rows_a, rows_b):
+    length = rows_a.shape[1]
+    tall = jnp.concatenate(
+        [jnp.broadcast_to(rows_a, (SSM_DIM, length)), jnp.broadcast_to(rows_b, (SSM_DIM, length))], axis=0
+    )
+    return tall.T
+
+
+def weighted_state(left, values, weight_rows):
+    rows = left.shape[0]
+
+    def kernel(left_ref, value_ref, weight_ref, out_ref):
+        wide = spread(weight_ref[0, 0:1, :], weight_ref[0, 1:2, :])
+        scaled = (value_ref[...] * wide).astype(jnp.bfloat16)
+        out_ref[...] = lax.dot_general(
+            left_ref[...].astype(jnp.bfloat16), scaled, TN, preferred_element_type=jnp.float32
+        )
+
+    return pl.pallas_call(
+        kernel,
+        grid=(PAIRS,),
+        in_specs=[
+            pl.BlockSpec((rows, STATE), lambda i: (0, 0)),
+            pl.BlockSpec((rows, 2 * SSM_DIM), lambda i: (0, i)),
+            pl.BlockSpec((1, 2, rows), lambda i: (i, 0, 0)),
+        ],
+        out_specs=pl.BlockSpec((STATE, 2 * SSM_DIM), lambda i: (0, i)),
+        out_shape=jax.ShapeDtypeStruct((STATE, INNER), jnp.float32),
+        cost_estimate=pl.CostEstimate(flops=2 * rows * STATE * INNER, bytes_accessed=rows * INNER * 4, transcendentals=0),
+        name="state",
+    )(left, values, weight_rows.reshape(PAIRS, 2, rows))
+
+
+def chunk_rows(k, meta_ref, cum_ref, start_ref):
+    here = slice(k * CHUNK, (k + 1) * CHUNK)
+    first = meta_ref[0] + k * CHUNK
+    index = first + lax.broadcasted_iota(jnp.int32, (1, CHUNK), 1)
+    entering = start_ref[0:1, here] < first
+    ending = index >= meta_ref[1 + k]
+    cums, entries, tails = [], [], []
+    for e in range(2):
+        cum = cum_ref[0, e : e + 1, here]
+        cums.append(cum)
+        entries.append(jnp.where(entering, jnp.exp(cum), 0.0))
+        gap = jnp.where(ending, cum[:, CHUNK - 1 :] - cum, masked_score)
+        tails.append(jnp.exp(gap))
+    return cums, entries, tails
+
+
+def ssm_forward(x, b_in, c_in, cum, step, state_in, skip, meta, start_column, start_row):
+    rows = x.shape[0]
+    chunks = rows // CHUNK
+
+    def kernel(meta_ref, x_ref, b_ref, c_ref, cum_ref, step_ref, state_ref, skip_ref, col_ref, row_ref,
+               y_ref, inner, hide, state):
+        @pl.when(pl.program_id(0) == 0)
+        def _():
+            for k in range(chunks):
+                here = slice(k * CHUNK, (k + 1) * CHUNK)
+                inner[k] = lax.dot_general(
+                    c_ref[here, :], b_ref[here, :], NT, precision=highest, preferred_element_type=jnp.float32
+                )
+                t = lax.broadcasted_iota(jnp.int32, (CHUNK, CHUNK), 0)
+                s = lax.broadcasted_iota(jnp.int32, (CHUNK, CHUNK), 1)
+                shown = (s <= t) & (meta_ref[0] + k * CHUNK + s >= col_ref[here, :])
+                hide[k] = jnp.where(shown, 0.0, masked_score)
+
+        low_lane = lax.broadcasted_iota(jnp.int32, (CHUNK, 2 * SSM_DIM), 1) < SSM_DIM
+        state[...] = state_ref[...]
+        for k in range(chunks):
+            here = slice(k * CHUNK, (k + 1) * CHUNK)
+            cums, entries, tails = chunk_rows(k, meta_ref, cum_ref, row_ref)
+            x_now = x_ref[here, :]
+            x_low = x_now.astype(jnp.bfloat16)
+            entry = spread(*entries)
+            weight = spread(*[tails[e] * step_ref[0, e : e + 1, here] for e in range(2)])
+            parts = []
+            for e in range(2):
+                across = jnp.broadcast_to(cums[e], (CHUNK, CHUNK))
+                decays = jnp.exp(across.T - across + hide[k])
+                mix = (inner[k] * decays * step_ref[0, e : e + 1, here]).astype(jnp.bfloat16)
+                parts.append(jnp.dot(mix, x_low, preferred_element_type=jnp.float32))
+            carried = jnp.dot(
+                c_ref[here, :].astype(jnp.bfloat16), state[...].astype(jnp.bfloat16),
+                preferred_element_type=jnp.float32,
+            )
+            y_ref[here, :] = jnp.where(low_lane, parts[0], parts[1]) + entry * carried + skip_ref[...] * x_now
+            fresh = lax.dot_general(
+                b_ref[here, :].astype(jnp.bfloat16), (x_now * weight).astype(jnp.bfloat16), TN,
+                preferred_element_type=jnp.float32,
+            )
+            state[...] = entry[CHUNK - 1 :, :] * state[...] + fresh
+
+    whole = lambda i, m: (0, 0)
+    lanes = lambda i, m: (0, i)
+    return pl.pallas_call(
+        kernel,
+        grid_spec=pltpu.PrefetchScalarGridSpec(
+            num_scalar_prefetch=1,
+            grid=(PAIRS,),
+            in_specs=[
+                pl.BlockSpec((rows, 2 * SSM_DIM), lanes),
+                pl.BlockSpec((rows, STATE), whole),
+                pl.BlockSpec((rows, STATE), whole),
+                pl.BlockSpec((1, 2, rows), lambda i, m: (i, 0, 0)),
+                pl.BlockSpec((1, 2, rows), lambda i, m: (i, 0, 0)),
+                pl.BlockSpec((STATE, 2 * SSM_DIM), lanes),
+                pl.BlockSpec((1, 2 * SSM_DIM), lanes),
+                pl.BlockSpec((rows, 1), whole),
+                pl.BlockSpec((8, rows), whole),
+            ],
+            out_specs=pl.BlockSpec((rows, 2 * SSM_DIM), lanes),
+            scratch_shapes=[
+                pltpu.VMEM((chunks, CHUNK, CHUNK), jnp.float32),
+                pltpu.VMEM((chunks, CHUNK, CHUNK), jnp.float32),
+                pltpu.VMEM((STATE, 2 * SSM_DIM), jnp.float32),
+            ],
+        ),
+        out_shape=jax.ShapeDtypeStruct((rows, INNER), jnp.float32),
+        compiler_params=pltpu.CompilerParams(vmem_limit_bytes=40 * 2**20),
+        cost_estimate=pl.CostEstimate(flops=10**9, bytes_accessed=rows * INNER * 8, transcendentals=2**21),
+        name="ssm",
+    )(meta, x, b_in, c_in, cum.reshape(PAIRS, 2, rows), step.reshape(PAIRS, 2, rows), state_in, skip,
+      start_column, start_row)
+
+
+def ssm_backward(x, dy, b_in, c_in, cum, step, state_in, state_grad, skip, meta, start_row):
+    rows = x.shape[0]
+    chunks = rows // CHUNK
+
+    def kernel(meta_ref, x_ref, dy_ref, b_ref, c_ref, cum_ref, step_ref, state_ref, grad_ref, skip_ref, row_ref,
+               dx_ref, db_ref, dc_ref, small_ref, inner, hide, inner_grad, states, flow):
+        low = lambda v: v.astype(jnp.bfloat16)
+        dot = lambda p, q, dims=(((1,), (0,)), ((), ())): lax.dot_general(
+            p, q, dims, preferred_element_type=jnp.float32
+        )
+        exact = lambda p, q, dims=(((1,), (0,)), ((), ())): lax.dot_general(
+            p, q, dims, precision=highest, preferred_element_type=jnp.float32
+        )
+        s = lax.broadcasted_iota(jnp.int32, (CHUNK, CHUNK), 0)
+        t = lax.broadcasted_iota(jnp.int32, (CHUNK, CHUNK), 1)
+
+        @pl.when(pl.program_id(0) == 0)
+        def _():
+            db_ref[...] = jnp.zeros(db_ref.shape, jnp.float32)
+            dc_ref[...] = jnp.zeros(dc_ref.shape, jnp.float32)
+            inner_grad[...] = jnp.zeros(inner_grad.shape, jnp.float32)
+            for k in range(chunks):
+                here = slice(k * CHUNK, (k + 1) * CHUNK)
+                inner[k] = exact(b_ref[here, :], c_ref[here, :], NT)
+                shown = (s <= t) & (meta_ref[0] + k * CHUNK + s >= row_ref[0:1, here])
+                hide[k] = jnp.where(shown, 0.0, masked_score)
+
+        before = (s < t).astype(jnp.float32)
+        until = low((s >= t).astype(jnp.float32))
+        low_lane = t < SSM_DIM
+        pick_row = lax.broadcasted_iota(jnp.int32, (8, 2 * SSM_DIM), 0)
+        pick_lane = lax.broadcasted_iota(jnp.int32, (8, 2 * SSM_DIM), 1) // SSM_DIM
+        pick = low((pick_row == pick_lane).astype(jnp.float32))
+        spreads = []
+        states[0] = state_ref[...]
+        for k in range(chunks):
+            here = slice(k * CHUNK, (k + 1) * CHUNK)
+            cums, entries, tails = chunk_rows(k, meta_ref, cum_ref, row_ref)
+            entry, tail = spread(*entries), spread(*tails)
+            steps = spread(step_ref[0, 0:1, here], step_ref[0, 1:2, here])
+            spreads.append((cums, entry, tail, steps))
+            if k < chunks - 1:
+                fresh = dot(low(b_ref[here, :]), low(x_ref[here, :] * steps * tail), TN)
+                states[k + 1] = entry[CHUNK - 1 :, :] * states[k] + fresh
+        flow[...] = grad_ref[...]
+        skip_sum = jnp.zeros((1, 2 * SSM_DIM), jnp.float32)
+        for k in reversed(range(chunks)):
+            here = slice(k * CHUNK, (k + 1) * CHUNK)
+            cums, entry, tail, steps = spreads[k]
+            x_now, dy_now = x_ref[here, :], dy_ref[here, :]
+            b_low, c_low = low(b_ref[here, :]), low(c_ref[here, :])
+            scaled = x_now * steps
+            dy_low = low(dy_now)
+            flow_low, state_low = low(flow[...]), low(states[k])
+            mixed, within = [], []
+            for e in range(2):
+                across = jnp.broadcast_to(cums[e], (CHUNK, CHUNK))
+                decays = jnp.exp(across - across.T + hide[k])
+                own = low(jnp.where(low_lane == (e == 0), scaled, 0.0))
+                reach = decays * dot(own, dy_low, NT)
+                inner_grad[k] += reach
+                sums = dot(low(inner[k] * reach), until)
+                within.append(jnp.sum(sums * before, axis=0, keepdims=True))
+                mixed.append(dot(low(inner[k] * decays), dy_low))
+            back = tail * dot(b_low, flow_low)
+            dxs = jnp.where(low_lane, mixed[0], mixed[1]) + back
+            db_ref[here, :] += dot(low(scaled * tail), flow_low, NT)
+            entered = low(dy_now * entry)
+            dc_ref[here, :] += dot(entered, state_low, NT)
+            brought = dy_now * entry * dot(c_low, state_low)
+            ends = dot(pick, low(brought), NT)
+            begins = dot(pick, low(scaled * back), NT)
+            direct = dot(pick, low(x_now * dxs), NT)
+            through = jnp.sum(flow[...] * states[k], axis=0, keepdims=True) * entry[CHUNK - 1 :, :]
+            log_grad = exact(ends, until.astype(jnp.float32)) + exact(begins, before)
+            for e in range(2):
+                lanes = slice(e * SSM_DIM, (e + 1) * SSM_DIM)
+                kept = jnp.sum(through[:, lanes], axis=1, keepdims=True)
+                small_ref[0, e : e + 1, here] = direct[e : e + 1, :]
+                small_ref[0, 2 + e : 3 + e, here] = log_grad[e : e + 1, :] + within[e] + kept
+            dx_ref[here, :] = dxs * steps + skip_ref[...] * dy_now
+            skip_sum += jnp.sum(x_now * dy_now, axis=0, keepdims=True)
+            flow[...] = entry[CHUNK - 1 :, :] * flow[...] + dot(c_low, entered, TN)
+        small_ref[0, 4:8, :] = jnp.zeros((4, rows), jnp.float32)
+        small_ref[0, 4:5, 0 : 2 * SSM_DIM] = skip_sum
+
+        @pl.when(pl.program_id(0) == PAIRS - 1)
+        def _():
+            for k in range(chunks):
+                here = slice(k * CHUNK, (k + 1) * CHUNK)
+                grads = low(inner_grad[k])
+                db_ref[here, :] += dot(grads, low(c_ref[here, :]))
+                dc_ref[here, :] += dot(grads, low(b_ref[here, :]), TN)
+
+    whole = lambda i, m: (0, 0)
+    lanes = lambda i, m: (0, i)
+    pair = lambda i, m: (i, 0, 0)
+    return pl.pallas_call(
+        kernel,
+        grid_spec=pltpu.PrefetchScalarGridSpec(
+            num_scalar_prefetch=1,
+            grid=(PAIRS,),
+            in_specs=[
+                pl.BlockSpec((rows, 2 * SSM_DIM), lanes),
+                pl.BlockSpec((rows, 2 * SSM_DIM), lanes),
+                pl.BlockSpec((rows, STATE), whole),
+                pl.BlockSpec((rows, STATE), whole),
+                pl.BlockSpec((1, 2, rows), pair),
+                pl.BlockSpec((1, 2, rows), pair),
+                pl.BlockSpec((STATE, 2 * SSM_DIM), lanes),
+                pl.BlockSpec((STATE, 2 * SSM_DIM), lanes),
+                pl.BlockSpec((1, 2 * SSM_DIM), lanes),
+                pl.BlockSpec((8, rows), whole),
+            ],
+            out_specs=[
+                pl.BlockSpec((rows, 2 * SSM_DIM), lanes),
+                pl.BlockSpec((rows, STATE), whole),
+                pl.BlockSpec((rows, STATE), whole),
+                pl.BlockSpec((1, 8, rows), pair),
+            ],
+            scratch_shapes=[
+                pltpu.VMEM((chunks, CHUNK, CHUNK), jnp.float32),
+                pltpu.VMEM((chunks, CHUNK, CHUNK), jnp.float32),
+                pltpu.VMEM((chunks, CHUNK, CHUNK), jnp.float32),
+                pltpu.VMEM((chunks, STATE, 2 * SSM_DIM), jnp.float32),
+                pltpu.VMEM((STATE, 2 * SSM_DIM), jnp.float32),
+            ],
+        ),
+        out_shape=[
+            jax.ShapeDtypeStruct((rows, INNER), jnp.float32),
+            jax.ShapeDtypeStruct((rows, STATE), jnp.float32),
+            jax.ShapeDtypeStruct((rows, STATE), jnp.float32),
+            jax.ShapeDtypeStruct((PAIRS, 8, rows), jnp.float32),
+        ],
+        compiler_params=pltpu.CompilerParams(vmem_limit_bytes=40 * 2**20),
+        cost_estimate=pl.CostEstimate(flops=3 * 10**9, bytes_accessed=rows * INNER * 12, transcendentals=2**21),
+        name="ssm_back",
+    )(meta, x, dy, b_in, c_in, cum.reshape(PAIRS, 2, rows), step.reshape(PAIRS, 2, rows), state_in, state_grad,
+      skip, start_row)
+
+
+def chain_states(earlier, later):
+    return (earlier[0] * later[0], earlier[1] * later[0] + later[1])
+
+
+def scan_states(carry, state, span, fast, backward):
+    wide = jnp.repeat(carry, SSM_DIM)[None, :]
+    if not fast:
+        ident = (jnp.ones_like(wide), jnp.zeros_like(state))
+        return (carried_in if backward else prefix)((wide, state), span, chain_states, ident)[1]
+    total = (wide, state)
+    start = None
+    for name in ("c", "x", "y"):
+        place = lax.axis_index(name)
+        packed = jnp.concatenate([total[1], jnp.broadcast_to(total[0], (16, INNER))], axis=0)
+        packed = lax.ppermute(packed.astype(jnp.bfloat16), name, SWAP).astype(jnp.float32)
+        other = (packed[STATE : STATE + 1], packed[:STATE])
+        leads = place == (0 if backward else 1)
+        seen = (jnp.where(leads, other[0], 1.0), jnp.where(leads, other[1], 0.0))
+        start = seen if start is None else chain_states(seen, start)
+        if name != "y":
+            forward = chain_states(other, total)
+            reverse = chain_states(total, other)
+            total = jax.tree.map(lambda p, q: jnp.where(leads, p, q), forward, reverse)
+    return start[1]
+
+
 KEYS = 512
 PAIR = 2 * HEAD_DIM
-NT = (((1,), (1,)), ((), ()))
 
 
 def attention_forward(q_wide, kv, meta, starts):
     rows = q_wide.shape[1]
     blocks = kv.shape[0]
-    tall = min(256, rows)
+    wide = min(256, rows)
 
     def kernel(meta_ref, q_ref, kv_ref, start_ref, o_ref, log_ref, top, total, mixed):
         top[...] = jnp.full(top.shape, masked_score, jnp.float32)
@@ -708,24 +956,25 @@
 
         def block(b, partial):
             pair = kv_ref[b, 0]
-            for r in range(0, rows, tall):
-                here = slice(r, r + tall)
-                scores = lax.dot_general(q_ref[0, here, :], pair, NT, preferred_element_type=jnp.float32)
+            turned = pair.T[HEAD_DIM:, :]
+            for r in range(0, rows, wide):
+                here = slice(r, r + wide)
+                scores = lax.dot_general(pair, q_ref[0, here, :], NT, preferred_element_type=jnp.float32)
                 if partial:
-                    keys = b * KEYS + lax.broadcasted_iota(jnp.int32, scores.shape, 1)
-                    mine = meta_ref[2] + r + lax.broadcasted_iota(jnp.int32, scores.shape, 0)
-                    visible = (keys >= start_ref[here, :]) & (keys <= mine)
+                    keys = b * KEYS + lax.broadcasted_iota(jnp.int32, scores.shape, 0)
+                    mine = meta_ref[2] + r + lax.broadcasted_iota(jnp.int32, scores.shape, 1)
+                    visible = (keys >= start_ref[0:1, here]) & (keys <= mine)
                     scores = jnp.where(visible, scores, masked_score)
-                before = top[here, :]
-                peak = jnp.maximum(before, jnp.max(scores, axis=1, keepdims=True))
-                part = jnp.exp(scores - peak[:, :1])
+                before = top[0:1, here]
+                peak = jnp.maximum(before, jnp.max(scores, axis=0, keepdims=True))
+                part = jnp.exp(scores - peak)
                 if partial:
                     part = jnp.where(visible, part, 0.0)
                 fade = jnp.exp(before - peak)
-                top[here, :] = peak
-                total[here, :] = total[here, :] * fade + jnp.sum(part, axis=1, keepdims=True)
-                mixed[here, :] = mixed[here, :] * fade + jnp.dot(
-                    part.astype(jnp.bfloat16), pair, preferred_element_type=jnp.float32
+                top[0:1, here] = peak
+                total[0:1, here] = total[0:1, here] * fade + jnp.sum(part, axis=0, keepdims=True)
+                mixed[:, here] = mixed[:, here] * fade + jnp.dot(
+                    turned, part.astype(jnp.bfloat16), preferred_element_type=jnp.float32
                 )
 
         def turn(b, nothing):
@@ -742,8 +991,8 @@
             return nothing
 
         lax.fori_loop(meta_ref[0], meta_ref[1], turn, 0)
-        o_ref[0] = mixed[...] / total[...]
-        log_ref[0] = (top[...] + jnp.log(total[...])).T[:8, :]
+        o_ref[0] = mixed[...] / total[0:1, :]
+        log_ref[0] = jnp.broadcast_to(top[0:1, :] + jnp.log(total[0:1, :]), (8, rows))
 
     ratio = HEADS_Q // HEADS_KV
     return pl.pallas_call(
@@ -754,20 +1003,24 @@
             in_specs=[
                 pl.BlockSpec((1, rows, PAIR), lambda h, m: (h, 0, 0)),
                 pl.BlockSpec((blocks, 1, KEYS, PAIR), lambda h, m: (0, h // ratio, 0, 0)),
-                pl.BlockSpec((rows, 1), lambda h, m: (0, 0)),
+                pl.BlockSpec((8, rows), lambda h, m: (0, 0)),
             ],
             out_specs=[
-                pl.BlockSpec((1, rows, PAIR), lambda h, m: (h, 0, 0)),
+                pl.BlockSpec((1, HEAD_DIM, rows), lambda h, m: (h, 0, 0)),
                 pl.BlockSpec((1, 8, rows), lambda h, m: (h, 0, 0)),
             ],
-            scratch_shapes=[pltpu.VMEM((rows, PAIR), jnp.float32)] * 3,
+            scratch_shapes=[
+                pltpu.VMEM((8, rows), jnp.float32),
+                pltpu.VMEM((8, rows), jnp.float32),
+                pltpu.VMEM((HEAD_DIM, rows), jnp.float32),
+            ],
         ),
         out_shape=[
-            jax.ShapeDtypeStruct((HEADS_Q, rows, PAIR), jnp.float32),
+            jax.ShapeDtypeStruct((HEADS_Q, HEAD_DIM, rows), jnp.float32),
             jax.ShapeDtypeStruct((HEADS_Q, 8, rows), jnp.float32),
         ],
         compiler_params=pltpu.CompilerParams(vmem_limit_bytes=48 * 2**20),
-        cost_estimate=pl.CostEstimate(flops=2 * 10**9, bytes_accessed=2**23, transcendentals=2**23),
+        cost_estimate=pl.CostEstimate(flops=4 * 10**9, bytes_accessed=2**23, transcendentals=2**23),
         name="attend",
     )(meta, q_wide, kv, starts)
 
@@ -785,8 +1038,8 @@
         def _():
             dq_ref[...] = jnp.zeros(dq_ref.shape, jnp.float32)
             for h in range(ratio):
-                both = g_ref[h].astype(jnp.float32) * o_ref[h]
-                delta[h] = jnp.broadcast_to(jnp.sum(both.T, axis=0, keepdims=True), (8, rows))
+                both = g_ref[h].astype(jnp.float32).T[HEAD_DIM:, :] * o_ref[h]
+                delta[h] = jnp.broadcast_to(jnp.sum(both, axis=0, keepdims=True), (8, rows))
 
         def block(partial):
             pair = kv_ref[0, 0]
@@ -841,7 +1094,7 @@
                 pl.BlockSpec((ratio, rows, PAIR), heads),
                 pl.BlockSpec((1, 1, KEYS, PAIR), lambda g, b, m: (b, g, 0, 0)),
                 pl.BlockSpec((ratio, 8, rows), heads),
-                pl.BlockSpec((ratio, rows, PAIR), heads),
+                pl.BlockSpec((ratio, HEAD_DIM, rows), heads),
                 pl.BlockSpec((8, rows), lambda g, b, m: (0, 0)),
             ],
             out_specs=[
@@ -1028,10 +1281,9 @@
     ).astype(jnp.int32)
     q_low = (q_rot * jnp.bfloat16(score_scale)).reshape(rows_dev, HEADS_Q, HEAD_DIM).transpose(1, 0, 2)
     q_wide = jnp.pad(q_low, ((0, 0), (0, 0), (0, HEAD_DIM)))
-    mixed, logs = attention_forward(q_wide, key_blocks, meta, row_starts[:, None])
-    attended = (
-        mixed[:, :, HEAD_DIM:].transpose(1, 0, 2).reshape(rows_dev, HEADS_Q * HEAD_DIM).astype(jnp.bfloat16)
-    )
+    start_row = jnp.broadcast_to(row_starts[None, :], (8, rows_dev))
+    mixed, logs = attention_forward(q_wide, key_blocks, meta, start_row)
+    attended = mixed.astype(jnp.bfloat16).reshape(HEADS_Q * HEAD_DIM, rows_dev).T
     attn_out = matmul(attended, weights[W_ATTN_OUT])
     gate_ssm = matmul(hidden, weights[W_GATE_SSM])
     xbc = jnp.concatenate(
@@ -1048,33 +1300,30 @@
         conv_local, extended, small_f32[CONV_WEIGHT], small_f32[CONV_BIAS]
     )
 
-    def ssd_full(conv_in, step_in, step_bias, decay_log, skip_gain, state_in):
-        x_ssm, b_in, c_in = split_conv(conv_in)
-        step_size = jax.nn.softplus(step_in + step_bias[None, :])
-        decay = -jnp.exp(decay_log)
-        output = ssd_output(
-            x_ssm, b_in, c_in, step_size, decay, skip_gain, seq_id, positions, state_in
-        )
-        carry_all, local_state = ssd_summary(x_ssm, b_in, step_size, decay, seq_id, positions)
-        return (
-            output.reshape(rows_dev, ssm_inner),
-            carry_all[:, None, None] * state_in + local_state,
-        )
-
-    x_ssm, b_in, c_in = split_conv(conv_values)
-    step_size = jax.nn.softplus(step_raw + small_f32[STEP_BIAS][None, :])
+    x_ssm = conv_values[:, :ssm_inner]
+    b_in = conv_values[:, ssm_inner : ssm_inner + STATE]
+    c_in = conv_values[:, ssm_inner + STATE :]
+    step_in = step_raw.T + small_f32[STEP_BIAS][:, None]
+    step_rows = jax.nn.softplus(step_in)
     decay = -jnp.exp(small_f32[DECAY_LOG])
-    carry_all, local_state = ssd_summary(x_ssm, b_in, step_size, decay, seq_id, positions)
-    state_ident = (jnp.ones_like(carry_all), jnp.zeros_like(local_state))
-    _, state_in = prefix((carry_all, local_state), span, chain_states, state_ident)
-    (ssm_y, _), ssd_back = jax.vjp(
-        ssd_full,
-        conv_values,
-        step_raw,
-        small_f32[STEP_BIAS],
-        small_f32[DECAY_LOG],
-        small_f32[SKIP_GAIN],
-        state_in,
+    logs_step = step_rows * decay[:, None]
+    order = jnp.arange(rows_dev)
+    upto = (order[:, None] <= order[None, :]).astype(jnp.float32)
+    cumul = jnp.dot(logs_step, upto, precision=highest)
+    chunk_cum = jnp.dot(
+        logs_step.reshape(-1, CHUNK), upto[:CHUNK, :CHUNK], precision=highest
+    ).reshape(SSM_HEADS, rows_dev)
+    went_on = row_starts < my_start
+    entry_rows = jnp.where(went_on[None, :], jnp.exp(cumul), 0.0)
+    in_last = row_index >= row_starts[rows_dev - 1]
+    tail_rows = jnp.exp(jnp.where(in_last[None, :], cumul[:, -1:] - cumul, masked_score))
+    carry_all = entry_rows[:, -1]
+    local_state = weighted_state(b_in, x_ssm, tail_rows * step_rows)
+    state_in = scan_states(carry_all, local_state, span, fast, False)
+    skip_wide = jnp.repeat(small_f32[SKIP_GAIN], SSM_DIM)[None, :]
+    ssm_meta = jnp.concatenate([my_start[None], row_starts[CHUNK - 1 :: CHUNK]]).astype(jnp.int32)
+    ssm_y = ssm_forward(
+        x_ssm, b_in, c_in, chunk_cum, step_rows, state_in, skip_wide, ssm_meta, row_starts[:, None], start_row
     )
     normed_ssm, gnorm_back = jax.vjp(gated_norm, ssm_y, gate_ssm, small_f32[NORM_SSM])
     ssm_low = normed_ssm.astype(jnp.bfloat16)
@@ -1113,16 +1362,19 @@
     grad_attended = matmul_right_t(grad_branch, back_weights[W_ATTN_OUT]).astype(jnp.bfloat16)
     grad_ssm_low = matmul_right_t(grad_branch, back_weights[W_SSM_OUT])
     grad_ssm_y, grad_gate_ssm_f32, grad_norm_ssm = gnorm_back(grad_ssm_low)
-    cumul = jnp.cumsum(step_size * decay[None, :], axis=0)
-    entry_decay = ssd_entry(cumul, seq_id, positions)
-    grad_y_heads = grad_ssm_y.reshape(rows_dev, SSM_HEADS, SSM_DIM)
-    grad_state_local = jnp.einsum(
-        "thp,tn,th->hpn", grad_y_heads, c_in, entry_decay, precision=highest
-    )
-    _, grad_state_out = carried_in((carry_all, grad_state_local), span, chain_states, state_ident)
-    grad_conv_values, grad_step_raw_f32, grad_step_bias, grad_decay_log, grad_skip_gain, _ = (
-        ssd_back((grad_ssm_y, grad_state_out))
-    )
+    grad_state_local = weighted_state(c_in, grad_ssm_y, entry_rows)
+    grad_state_out = scan_states(carry_all, grad_state_local, span, fast, True)
+    grad_x, grad_b, grad_c, grad_small = ssm_backward(
+        x_ssm, grad_ssm_y, b_in, c_in, chunk_cum, step_rows, state_in, grad_state_out, skip_wide, ssm_meta, start_row
+    )
+    grad_conv_values = jnp.concatenate([grad_x, grad_b, grad_c], axis=1)
+    grad_direct = grad_small[:, 0:2].reshape(SSM_HEADS, rows_dev)
+    grad_logs = grad_small[:, 2:4].reshape(SSM_HEADS, rows_dev)
+    grad_decay_log = decay * jnp.sum(step_rows * grad_logs, axis=1)
+    grad_step_rows = (grad_direct + decay[:, None] * grad_logs) * jax.nn.sigmoid(step_in)
+    grad_step_bias = jnp.sum(grad_step_rows, axis=1)
+    grad_step_raw_f32 = grad_step_rows.T
+    grad_skip_gain = jnp.sum(grad_small[:, 4, : 2 * SSM_DIM].reshape(SSM_HEADS, SSM_DIM), axis=1)
     grad_extended, grad_conv_weight, grad_conv_bias = conv_back(grad_conv_values)
     rim_back = passed_along(grad_extended[: CONV - 1], span, -1)
     grad_xbc_f32 = grad_extended[CONV - 1 :]
@@ -1140,14 +1392,14 @@
     g_low = grad_attended.reshape(rows_dev, HEADS_Q, HEAD_DIM).transpose(1, 0, 2)
     g_wide = jnp.pad(g_low, ((0, 0), (0, 0), (HEAD_DIM, 0)))
     grad_kv, grad_q_turned = attention_backward(
-        q_wide, g_wide, key_blocks, logs, mixed, meta, jnp.broadcast_to(row_starts[None, :], (8, rows_dev))
+        q_wide, g_wide, key_blocks, logs, mixed, meta, start_row
     )
     if rows_dev != KEYS:
         grad_kv = grad_kv.transpose(1, 0, 2, 3).reshape(HEADS_KV, -1, rows_dev, PAIR).transpose(1, 0, 2, 3)
     grad_kv_mine = scatter_span(grad_kv, span, fast)
     grad_keys_mine = grad_kv_mine[:, :, :HEAD_DIM].transpose(1, 0, 2).reshape(rows_dev, -1)
     grad_values_mine = grad_kv_mine[:, :, HEAD_DIM:].transpose(1, 0, 2).reshape(rows_dev, -1)
-    grad_q_rot = grad_q_turned.transpose(2, 0, 1).reshape(rows_dev, HEADS_Q * HEAD_DIM) * score_scale
+    grad_q_rot = grad_q_turned.reshape(HEADS_Q * HEAD_DIM, rows_dev).T * score_scale
     grad_query_low = rotate(grad_q_rot, cosine, -sine, HEADS_Q).astype(jnp.bfloat16)
     grad_key_low = rotate(grad_keys_mine, cosine, -sine, HEADS_KV).astype(jnp.bfloat16)
     grad_value_low = grad_values_mine.astype(jnp.bfloat16)

time: 1160 us -> 985 us (0.85)
  matrix products: 202 us -> 79.6 us
  Pallas kernels: 117 us -> 185 us
  starting transfers between devices: 318 us -> 265 us
  other arithmetic: 155 us -> 114 us
  waiting for transfers between devices: 209 us -> 229 us
  between operations: 20.7 us -> 5.57 us
  blocking collectives: 12.1 us -> 0 us
    dot_general x12 -> x2, matrix products: 128 us -> 2.4 us  [the longest x1 1.49 us: body(): jnp.dot(logs_step.reshape(-1, CHUNK), upto[:CHUNK, :CHUNK], precision=hig...]
    ppermute x0 -> x6, starting transfers between devices: none -> 105 us  [scan_states(): lax.ppermute(packed.astype(jnp.bfloat16), name, SWAP).astype(jnp.float32)]
    ppermute x3, starting transfers between devices: 82.5 us -> 9.67 us  [scatter_span(): lax.ppermute(send, name, SWAP).astype(jnp.float32)]
    pallas_call x0 -> x4, Pallas kernels: none -> 69.3 us  [the longest x1 39.9 us: ssm_backward(): pl.pallas_call(kernel, grid_spec=pltpu.PrefetchScalarGridSpec(num_scalar_...]
    ppermute x4, waiting for transfers between devices: 64.9 us -> 0.01 us  [reduce_lines(): half = added(home, lax.ppermute(away, first_axis, SWAP))]
    ppermute x2, waiting for transfers between devices: 7.76 us -> 55.7 us  [reduce_lines(): end = added(two, lax.ppermute(two, ZC, zc_pairs((1, 0, 0))))]
    ppermute x2, starting transfers between devices: 74.8 us -> 34.2 us  [reduce_lines(): handed = lax.ppermute(other, ZC, holders)]
    ppermute x3, starting transfers between devices: 36.2 us -> 1.64 us  [sum_all(): value = value + lax.ppermute(value, name, SWAP)]
  transfers between devices with their start and end apart: 88 -> 92, of which waited for: 23 -> 27; matrix products, arithmetic and copies ran while one was open for 28% -> 23% of each run, Pallas kernels for 10% -> 17%
where the time goes in v3:
time: 985 us; the launch traced here: 979 us
  starting transfers between devices  265 us (27%)
  waiting for transfers between devices  229 us (23%)
  Pallas kernels  185 us (19%)
  other arithmetic  114 us (12%)
  local copies, waits for them, and re-layouts  101 us (10%)
  matrix products  79.6 us (8%)
    ppermute x6, starting transfers between devices, scan_states(): lax.ppermute(packed.astype(jnp.bfloat16), name, SWAP).astype(jnp.float32)  105 us
    ppermute x2, waiting for transfers between devices, reduce_lines(): end = added(two, lax.ppermute(two, ZC, zc_pairs((1, 0, 0))))  55.7 us
    pallas_call x3, Pallas kernels, pack_lines(): pl.pallas_call(kernel, grid=(total,), in_specs=[left_spec(k) for k in ran...  46.2 us
    pallas_call x2, Pallas kernels, unpack_lines(): pl.pallas_call(kernel, grid_spec=pltpu.PrefetchScalarGridSpec(num_scalar_...  41.2 us
    dot_general x12, matrix products, matmul_right_t(): lax.dot_general(left, right, (((1,), (1,)), ((), ())), preferred_element_...  40.6 us
    pallas_call x1, Pallas kernels, ssm_backward(): pl.pallas_call(kernel, grid_spec=pltpu.PrefetchScalarGridSpec(num_scalar_...  39.9 us
    dot_general x12, matrix products, matmul(): return jnp.dot(left, right, preferred_element_type=jnp.float32)  34.5 us
    ppermute x2, starting transfers between devices, reduce_lines(): handed = lax.ppermute(other, ZC, holders)  34.2 us
  transfers between devices with their start and end apart: 92, of which 27 were waited for; matrix products, arithmetic and copies ran while one was open for 23% of the time, Pallas kernels for 17%

profile of v3, /device:TPU:0, one launch (start us, length us, event | category | flops | bytes accessed | tf_op | source)
XLA Modules:
  0.0 979.1 jit_solution(14723504925173705312)
XLA Ops:
  1.9 7.7 collective-permute-start
  21.0 4.9 collective-permute-done.12
  44.2 15.7 %collective-permute-done.32 = bf16[3088,128]{1,0:T(8,128)(2,1)} collective-permute-done((bf16[3088,128]{1,0:T(8,128)(2,1)S(1)}, bf16[3088,128]{1,0:T(8,128)(2,1)}, u32[]{:S(2)}, u32[]{:S(2)}) %collective-permute-start.32) | collective-permute-done | bytes 790560 | tf_op jit(solution)/shard_map/ppermute | solution.py:261
  74.3 11.8 %collective-permute-start.19 = (bf16[3088,128]{1,0:T(8,128)(2,1)}, bf16[3088,128]{1,0:T(8,128)(2,1)}, u32[]{:S(2)}, u32[]{:S(2)}) collective-permute-start(bf16[3088,128]{1,0:T(8,128)(2,1)} %get-tuple-element.162.refs_8_), channel_id=1, source_target_pairs={{0,1},{1,0},{2,3},{3,2},{4,5},{5,4},{6,7},{7,6},{8,9},{9,8},{10,11... | collective-permute-start | bytes 2371592 | tf_op jit(solution)/shard_map/ppermute | solution.py:272
  86.9 15.9 %collective-permute-done.5.refs_1_ = bf16[3088,128]{1,0:T(8,128)(2,1)S(1)} collective-permute-done((bf16[3088,128]{1,0:T(8,128)(2,1)S(1)}, bf16[3088,128]{1,0:T(8,128)(2,1)S(1)}, u32[]{:S(2)}, u32[]{:S(2)}) %collective-permute-start.5) | collective-permute-done | bytes 790560 | tf_op jit(solution)/shard_map/ppermute | solution.py:265
  134.1 14.8 %unpack.2 = (bf16[1024,512]{1,0:T(8,128)(2,1)}, bf16[1024,128]{1,0:T(8,128)(2,1)S(1)}, bf16[1024,128]{1,0:T(8,128)(2,1)S(1)}, bf16[512,1024]{1,0:T(8,128)(2,1)},...) custom-call(s32[25,5]{1,0:T(8,128)S(1)} %copy-done.39, ...), custom_call_target="tpu_custom_call" | custom-call | bytes 26624000 | tf_op jit(solution)/shard_map/unpack/pallas_call | solution.py:413
  167.7 5.5 fusion.85
  179.6 13.9 %collective-permute-done.47.refs_27_ = bf16[3088,128]{1,0:T(8,128)(2,1)} collective-permute-done((bf16[3088,128]{1,0:T(8,128)(2,1)}, bf16[3088,128]{1,0:T(8,128)(2,1)}, u32[]{:S(2)}, u32[]{:S(2)}) %collective-permute-start.47) | collective-permute-done | bytes 790560 | tf_op jit(solution)/shard_map/ppermute | solution.py:270
  196.5 6.9 collective-permute-start.26
  206.8 26.3 %unpack.3 = (bf16[1536,1024]{1,0:T(8,128)(2,1)}, bf16[1024,2048]{1,0:T(8,128)(2,1)}, bf16[1024,2048]{1,0:T(8,128)(2,1)}, bf16[2048,1024]{1,0:T(8,128)(2,1)}, bf16[16,128]{1,0:T(8,128)(2,1)S(1)}) custom-call(s32[31,5]{1,0:T(8,128)S(1)} %copy-done.38, s32[32]{0:T(128)S(1)} %fusion.64.where_ref, bf16[3088,128]{1,0:T(8,128)(2,1)S(1)} %get-tuple-element.164.refs_0_, ...), custom_call_target="tpu_custom_call" | custom-call | bytes 33013760 | tf_op jit(solution)/shard_map/unpack/pallas_call | solution.py:413
  233.2 6.6 fusion.88
  245.8 4.8 fusion.8
  253.4 9.6 state.2
  278.1 8.1 collective-permute-done.28
  293.8 7.2 collective-permute-done.29
  302.2 10.3 %ssm.1 = f32[512,1536]{1,0:T(8,128)S(1)} custom-call(s32[5]{0:T(128)S(1)} %pad_add_fusion.3.meta_ref, f32[512,1536]{1,0:T(8,128)S(1)} %copy-done, f32[512,128]{1,0:T(8,128)S(1)} %copy-done.15, f32[512,128]{1,0:T(8,128)S(1)} %get-tuple-element.145.c_ref.left_ref, f32[12,2,512]{2,1,0:T(2,128)S(1)} %reshape_reshape.4.cum_ref, ...), custom_call_target="tpu_custom_call" | custom-call | flops 1000000000 | bytes 6291456 | tf_op jit(solution)/shard_map/ssm/pallas_call | solution.py:745
  317.2 10.4 %attend.1 = (f32[8,64,512]{2,1,0:T(8,128)S(1)}, f32[8,8,512]{2,1,0:T(8,128)S(1)}) custom-call(s32[4]{0:T(128)S(1)} %pad_add_fusion.2.meta_ref, bf16[8,512,128]{2,1,0:T(8,128)(2,1)S(1)} %pad.45.q_ref, bf16[8,2,512,128]{3,2,1,0:T(8,128)(2,1)S(1)} %bitcast.220, s32[8,512]{1,0:T(8,128)S(1)} %broadcast_in_dim.191.start_ref.row_ref), custom_call_target="tpu_custom_call" | custom-call | flops 4000000000 | bytes 8388608 | tf_op jit(solution)/shard_map/attend/pallas_call | solution.py:998
  338.3 6.7 fusion.2
  352.9 4.6 multiply_reduce_fusion.10
  372.3 9.5 state.3
  383.8 8.3 collective-permute-start.52
  396.4 17.8 %attend_back.1 = (bf16[8,2,512,128]{3,2,1,0:T(8,128)(2,1)}, f32[8,64,512]{2,1,0:T(8,128)S(1)}) custom-call(s32[4]{0:T(128)S(1)} %pad_add_fusion.2.meta_ref, bf16[8,512,128]{2,1,0:T(8,128)(2,1)S(1)} %copy-done.24, bf16[8,512,128]{2,1,0:T(8,128)(2,1)S(1)} %pad.50.g_ref, bf16[8,2,512,128]{3,2,1,0:T(8,128)(2,1)} %bitcast.221, ...), custom_call_target="tpu_custom_call" | custom-call | flops 5000000000 | bytes 8388608 | tf_op jit(solution)/shard_map/attend_back/pallas_call | solution.py:1087
  433.5 6.5 collective-permute-start.56
  440.7 6.5 pad_maximum_fusion.2
  447.3 20.4 %pack.5 = bf16[49344,128]{1,0:T(8,128)(2,1)} custom-call(bf16[512,1024]{1,0:T(8,128)(2,1)S(1)} %copy-done.30, bf16[512,2048]{1,0:T(8,128)(2,1)S(1)} %copy-done.41, bf16[512,2048]{1,0:T(8,128)(2,1)} %get-tuple-element.194.refs_2_, bf16[512,2048]{1,0:T(8,128)(2,1)} %get-tuple-element.195.refs_3_, bf16[512,1024]{1,0:T(8,128)(2,1)S(1)} %copy-done.28, ...), custom_call_target="tpu_custom_call" | custom-call | flops 6442450944 | bytes 16777216 | tf_op jit(solution)/shard_map/pack/pallas_call | solution.py:567
  467.7 6.0 constant_dynamic-slice_fusion
  478.7 28.6 %collective-permute-start.53 = (bf16[144,1536]{1,0:T(8,128)(2,1)S(1)}, bf16[144,1536]{1,0:T(8,128)(2,1)S(1)}, u32[]{:S(2)}, u32[]{:S(2)}) collective-permute-start(bf16[144,1536]{1,0:T(8,128)(2,1)S(1)} %pad_maximum_fusion.17), channel_id=1, source_target_pairs={{0,2},{2,0},{1,3},{3,1},{4,6},{6,4},{5,7},{7,5},{8,10},{10,8},{9,1... | collective-permute-start | bytes 1327112 | tf_op jit(solution)/shard_map/ppermute | solution.py:931
  510.4 7.2 collective-permute-done.53
  519.0 65.1 %collective-permute-start.54 = (bf16[144,1536]{1,0:T(8,128)(2,1)}, bf16[144,1536]{1,0:T(8,128)(2,1)}, u32[]{:S(2)}, u32[]{:S(2)}) collective-permute-start(bf16[144,1536]{1,0:T(8,128)(2,1)} %pad_maximum_fusion.18), channel_id=1, source_target_pairs={{0,4},{4,0},{1,5},{5,1},{2,6},{6,2},{3,7},{7,3},{8,12},{12,8},{9,1... | collective-permute-start | bytes 1327112 | tf_op jit(solution)/shard_map/ppermute | solution.py:931
  584.1 4.7 pack.3.refs_11_
  600.5 39.9 %ssm_back.1 = (f32[512,1536]{1,0:T(8,128)S(1)}, f32[512,128]{1,0:T(8,128)S(1)}, f32[512,128]{1,0:T(8,128)S(1)}, f32[12,8,512]{2,1,0:T(8,128)S(1)}) custom-call(s32[5]{0:T(128)S(1)} %pad_add_fusion.3.meta_ref, f32[512,1536]{1,0:T(8,128)S(1)} %copy-done.1, f32[512,1536]{1,0:T(8,128)S(1)} %copy-done.2, f32[512,128]{1,0:T(8,128)S(1)} %copy-done.15, ...), custom_call_target="tpu_custom_call" | custom-call | flops 3000000000 | bytes 9437184 | tf_op jit(solution)/shard_map/ssm_back/pallas_call | solution.py:873
  660.6 6.1 collective-permute-start.55
  678.1 5.2 fusion.69
  689.0 4.9 collective-permute-done.58
  696.3 7.3 fusion.16
  703.7 21.1 %pack.4 = bf16[49440,128]{1,0:T(8,128)(2,1)} custom-call(bf16[512,1024]{1,0:T(8,128)(2,1)S(1)} %fusion.15.refs_0_, bf16[512,512]{1,0:T(8,128)(2,1)S(1)} %bitcast.219, bf16[512,512]{1,0:T(8,128)(2,1)S(1)} %copy-done.16, bf16[512,128]{1,0:T(8,128)(2,1)S(1)} %copy.95.refs_3_, bf16[512,128]{1,0:T(8,128)(2,1)S(1)} %copy-done.34, ...), custom_call_target="tpu_custom_call", output_to_operand_aliasing={{}: (11, {})} | custom-call | flops 4831838208 | bytes 20447232 | tf_op jit(solution)/shard_map/pack/pallas_call | solution.py:567
  724.8 6.3 constant_dynamic-slice_fusion.1
  752.3 23.5 %collective-permute-done.88 = f32[4]{0:T(128)S(1)} collective-permute-done((f32[4]{0:T(128)S(1)}, f32[4]{0:T(128)S(1)}, u32[]{:S(2)}, u32[]{:S(2)}) %collective-permute-start.88) | collective-permute-done | bytes 48 | tf_op jit(solution)/shard_map/ppermute | solution.py:1153
  779.4 5.5 collective-permute-start.90
  798.6 5.8 add_convert_fusion.1
  806.1 9.2 collective-permute-done.81
  820.2 14.7 %collective-permute-done.82 = bf16[3104,128]{1,0:T(8,128)(2,1)S(1)} collective-permute-done((bf16[3104,128]{1,0:T(8,128)(2,1)S(1)}, bf16[3104,128]{1,0:T(8,128)(2,1)S(1)}, u32[]{:S(2)}, u32[]{:S(2)}) %collective-permute-start.82) | collective-permute-done | bytes 794656 | tf_op jit(solution)/shard_map/ppermute | solution.py:631
  834.9 4.7 collective-permute-start.76
  839.8 14.2 %collective-permute-done.76 = bf16[3104,128]{1,0:T(8,128)(2,1)S(1)} collective-permute-done((bf16[3104,128]{1,0:T(8,128)(2,1)S(1)}, bf16[3104,128]{1,0:T(8,128)(2,1)S(1)}, u32[]{:S(2)}, u32[]{:S(2)}) %collective-permute-start.76) | collective-permute-done | bytes 794656 | tf_op jit(solution)/shard_map/ppermute | solution.py:631
  862.5 11.3 %collective-permute-done.67 = bf16[3104,128]{1,0:T(8,128)(2,1)S(1)} collective-permute-done((bf16[3104,128]{1,0:T(8,128)(2,1)S(1)}, bf16[3104,128]{1,0:T(8,128)(2,1)S(1)}, u32[]{:S(2)}, u32[]{:S(2)}) %collective-permute-start.67) | collective-permute-done | bytes 794656 | tf_op jit(solution)/shard_map/ppermute | solution.py:624
  883.2 32.8 %collective-permute-start.86 = (bf16[3104,128]{1,0:T(8,128)(2,1)S(1)}, bf16[3104,128]{1,0:T(8,128)(2,1)S(1)}, u32[]{:S(2)}, u32[]{:S(2)}) collective-permute-start(bf16[3104,128]{1,0:T(8,128)(2,1)S(1)} %get-tuple-element.103), channel_id=1, source_target_pairs={{0,1},{9,8},{16,17},{25,24},{2,3},{11,10},{18,19},{27,26},{4,5},{1... | collective-permute-start | bytes 2383880 | tf_op jit(solution)/shard_map/ppermute | solution.py:639
  916.0 41.2 %collective-permute-done.71 = bf16[3104,128]{1,0:T(8,128)(2,1)S(1)} collective-permute-done((bf16[3104,128]{1,0:T(8,128)(2,1)S(1)}, bf16[3104,128]{1,0:T(8,128)(2,1)S(1)}, u32[]{:S(2)}, u32[]{:S(2)}) %collective-permute-start.71) | collective-permute-done | bytes 794656 | tf_op jit(solution)/shard_map/ppermute | solution.py:629
  957.2 14.5 %collective-permute-done.65 = bf16[3104,128]{1,0:T(8,128)(2,1)S(1)} collective-permute-done((bf16[3104,128]{1,0:T(8,128)(2,1)S(1)}, bf16[3104,128]{1,0:T(8,128)(2,1)S(1)}, u32[]{:S(2)}, u32[]{:S(2)}) %collective-permute-start.65) | collective-permute-done | bytes 794656 | tf_op jit(solution)/shard_map/ppermute | solution.py:629
  (788 shorter events, 333.0 us)
Async XLA Ops:
  30.3 29.6 %collective-permute-start.32 = (bf16[3088,128]{1,0:T(8,128)(2,1)S(1)}, bf16[3088,128]{1,0:T(8,128)(2,1)}, u32[]{:S(2)}, u32[]{:S(2)}) collective-permute-start(bf16[3088,128]{1,0:T(8,128)(2,1)S(1)} %collective-permute-done.30), channel_id=1, source_target_pairs={{8,0},{17,9},{10,2},{19,11},{12,4},{21,13},{14,6},{23,15}} | collective-permute-start | bytes 2371592 | tf_op jit(solution)/shard_map/ppermute | solution.py:261
  34.3 26.3 %collective-permute-start.3 = (bf16[3088,128]{1,0:T(8,128)(2,1)S(1)}, bf16[3088,128]{1,0:T(8,128)(2,1)}, u32[]{:S(2)}, u32[]{:S(2)}) collective-permute-start(bf16[3088,128]{1,0:T(8,128)(2,1)S(1)} %collective-permute-done.1), channel_id=1, source_target_pairs={{8,16},{17,25},{10,18},{19,27},{12,20},{21,29},{14,22},{23,31}} | collective-permute-start | bytes 2371592 | tf_op jit(solution)/shard_map/ppermute | solution.py:256
  35.9 25.4 %collective-permute-start.15 = (bf16[3088,128]{1,0:T(8,128)(2,1)}, bf16[3088,128]{1,0:T(8,128)(2,1)}, u32[]{:S(2)}, u32[]{:S(2)}) collective-permute-start(bf16[3088,128]{1,0:T(8,128)(2,1)} %collective-permute-done.14), channel_id=1, source_target_pairs={{16,24},{18,26},{20,28},{22,30}} | collective-permute-start | bytes 2371592 | tf_op jit(solution)/shard_map/ppermute | solution.py:257
  41.9 20.3 %collective-permute-start.44 = (bf16[3088,128]{1,0:T(8,128)(2,1)}, bf16[3088,128]{1,0:T(8,128)(2,1)}, u32[]{:S(2)}, u32[]{:S(2)}) collective-permute-start(bf16[3088,128]{1,0:T(8,128)(2,1)} %collective-permute-done.43), channel_id=1, source_target_pairs={{9,1},{11,3},{13,5},{15,7}} | collective-permute-start | bytes 2371592 | tf_op jit(solution)/shard_map/ppermute | solution.py:262
  43.5 24.4 %collective-permute-start.2 = (bf16[3088,128]{1,0:T(8,128)(2,1)S(1)}, bf16[3088,128]{1,0:T(8,128)(2,1)S(1)}, u32[]{:S(2)}, u32[]{:S(2)}) collective-permute-start(bf16[3088,128]{1,0:T(8,128)(2,1)S(1)} %get-tuple-element.154), channel_id=1, source_target_pairs={{9,1},{11,3},{13,5},{15,7}} | collective-permute-start | bytes 2371592 | tf_op jit(solution)/shard_map/ppermute | solution.py:255
  66.4 20.5 %collective-permute-start.17 = (bf16[3088,128]{1,0:T(8,128)(2,1)}, bf16[3088,128]{1,0:T(8,128)(2,1)}, u32[]{:S(2)}, u32[]{:S(2)}) collective-permute-start(bf16[3088,128]{1,0:T(8,128)(2,1)} %get-tuple-element.162.refs_8_), channel_id=1, source_target_pairs={{0,4},{4,0},{1,5},{5,1},{2,6},{6,2},{3,7},{7,3},{8,12},{12,8},{9,1... | collective-permute-start | bytes 2371592 | tf_op jit(solution)/shard_map/ppermute | solution.py:266
  67.9 36.4 %collective-permute-start.16 = (bf16[3088,128]{1,0:T(8,128)(2,1)}, bf16[3088,128]{1,0:T(8,128)(2,1)S(1)}, u32[]{:S(2)}, u32[]{:S(2)}) collective-permute-start(bf16[3088,128]{1,0:T(8,128)(2,1)} %get-tuple-element.162.refs_8_), channel_id=1, source_target_pairs={{0,2},{2,0},{1,3},{3,1},{4,6},{6,4},{5,7},{7,5},{8,10},{10,8},{9,1... | collective-permute-start | bytes 2371592 | tf_op jit(solution)/shard_map/ppermute | solution.py:265
  72.1 30.8 %collective-permute-start.5 = (bf16[3088,128]{1,0:T(8,128)(2,1)S(1)}, bf16[3088,128]{1,0:T(8,128)(2,1)S(1)}, u32[]{:S(2)}, u32[]{:S(2)}) collective-permute-start(bf16[3088,128]{1,0:T(8,128)(2,1)S(1)} %get-tuple-element.164.refs_0_), channel_id=1, source_target_pairs={{0,2},{2,0},{1,3},{3,1},{4,6},{6,4},{5,7},{7,5},{8,10},{10,8},{9,1... | collective-permute-start | bytes 2371592 | tf_op jit(solution)/shard_map/ppermute | solution.py:265
  72.7 33.8 %collective-permute-start.6 = (bf16[3088,128]{1,0:T(8,128)(2,1)S(1)}, bf16[3088,128]{1,0:T(8,128)(2,1)S(1)}, u32[]{:S(2)}, u32[]{:S(2)}) collective-permute-start(bf16[3088,128]{1,0:T(8,128)(2,1)S(1)} %get-tuple-element.164.refs_0_), channel_id=1, source_target_pairs={{0,4},{4,0},{1,5},{5,1},{2,6},{6,2},{3,7},{7,3},{8,12},{12,8},{9,1... | collective-permute-start | bytes 2371592 | tf_op jit(solution)/shard_map/ppermute | solution.py:266
  74.3 46.3 %collective-permute-start.19 = (bf16[3088,128]{1,0:T(8,128)(2,1)}, bf16[3088,128]{1,0:T(8,128)(2,1)}, u32[]{:S(2)}, u32[]{:S(2)}) collective-permute-start(bf16[3088,128]{1,0:T(8,128)(2,1)} %get-tuple-element.162.refs_8_), channel_id=1, source_target_pairs={{0,1},{1,0},{2,3},{3,2},{4,5},{5,4},{6,7},{7,6},{8,9},{9,8},{10,11... | collective-permute-start | bytes 2371592 | tf_op jit(solution)/shard_map/ppermute | solution.py:272
  86.9 34.4 %collective-permute-start.8 = (bf16[3088,128]{1,0:T(8,128)(2,1)S(1)}, bf16[3088,128]{1,0:T(8,128)(2,1)S(1)}, u32[]{:S(2)}, u32[]{:S(2)}) collective-permute-start(bf16[3088,128]{1,0:T(8,128)(2,1)S(1)} %get-tuple-element.164.refs_0_), channel_id=1, source_target_pairs={{0,1},{1,0},{2,3},{3,2},{4,5},{5,4},{6,7},{7,6},{8,9},{9,8},{10,11... | collective-permute-start | bytes 2371592 | tf_op jit(solution)/shard_map/ppermute | solution.py:272
  102.9 19.2 %collective-permute-start.18 = (bf16[3088,128]{1,0:T(8,128)(2,1)}, bf16[3088,128]{1,0:T(8,128)(2,1)}, u32[]{:S(2)}, u32[]{:S(2)}) collective-permute-start(bf16[3088,128]{1,0:T(8,128)(2,1)} %collective-permute-done.17.refs_10_), channel_id=1, source_target_pairs={{0,2},{2,0},{1,3},{3,1},{4,6},{6,4},{5,7},{7,5},{8,10},{10,8},{9,1... | collective-permute-start | bytes 2371592 | tf_op jit(solution)/shard_map/ppermute | solution.py:270
  104.3 22.8 %collective-permute-start.21 = (bf16[3088,128]{1,0:T(8,128)(2,1)}, bf16[3088,128]{1,0:T(8,128)(2,1)}, u32[]{:S(2)}, u32[]{:S(2)}) collective-permute-start(bf16[3088,128]{1,0:T(8,128)(2,1)} %collective-permute-done.17.refs_10_), channel_id=1, source_target_pairs={{0,1},{1,0},{2,3},{3,2},{4,5},{5,4},{6,7},{7,6},{8,9},{9,8},{10,11... | collective-permute-start | bytes 2371592 | tf_op jit(solution)/shard_map/ppermute | solution.py:272
  106.5 20.5 %collective-permute-start.7 = (bf16[3088,128]{1,0:T(8,128)(2,1)S(1)}, bf16[3088,128]{1,0:T(8,128)(2,1)}, u32[]{:S(2)}, u32[]{:S(2)}) collective-permute-start(bf16[3088,128]{1,0:T(8,128)(2,1)S(1)} %collective-permute-done.5.refs_1_), channel_id=1, source_target_pairs={{0,4},{4,0},{1,5},{5,1},{2,6},{6,2},{3,7},{7,3},{8,12},{12,8},{9,1... | collective-permute-start | bytes 2371592 | tf_op jit(solution)/shard_map/ppermute | solution.py:268
  129.0 44.2 %collective-permute-start.46 = (bf16[3088,128]{1,0:T(8,128)(2,1)}, bf16[3088,128]{1,0:T(8,128)(2,1)}, u32[]{:S(2)}, u32[]{:S(2)}) collective-permute-start(bf16[3088,128]{1,0:T(8,128)(2,1)} %get-tuple-element.161.refs_24_), channel_id=1, source_target_pairs={{0,4},{4,0},{1,5},{5,1},{2,6},{6,2},{3,7},{7,3},{8,12},{12,8},{9,1... | collective-permute-start | bytes 2371592 | tf_op jit(solution)/shard_map/ppermute | solution.py:266
  129.7 44.0 %collective-permute-start.45 = (bf16[3088,128]{1,0:T(8,128)(2,1)}, bf16[3088,128]{1,0:T(8,128)(2,1)}, u32[]{:S(2)}, u32[]{:S(2)}) collective-permute-start(bf16[3088,128]{1,0:T(8,128)(2,1)} %get-tuple-element.161.refs_24_), channel_id=1, source_target_pairs={{0,2},{2,0},{1,3},{3,1},{4,6},{6,4},{5,7},{7,5},{8,10},{10,8},{9,1... | collective-permute-start | bytes 2371592 | tf_op jit(solution)/shard_map/ppermute | solution.py:265
  130.3 42.9 %collective-permute-start.34 = (bf16[3088,128]{1,0:T(8,128)(2,1)}, bf16[3088,128]{1,0:T(8,128)(2,1)}, u32[]{:S(2)}, u32[]{:S(2)}) collective-permute-start(bf16[3088,128]{1,0:T(8,128)(2,1)} %get-tuple-element.163.refs_16_), channel_id=1, source_target_pairs={{0,2},{2,0},{1,3},{3,1},{4,6},{6,4},{5,7},{7,5},{8,10},{10,8},{9,1... | collective-permute-start | bytes 2371592 | tf_op jit(solution)/shard_map/ppermute | solution.py:265
  131.8 42.1 %collective-permute-start.35 = (bf16[3088,128]{1,0:T(8,128)(2,1)}, bf16[3088,128]{1,0:T(8,128)(2,1)}, u32[]{:S(2)}, u32[]{:S(2)}) collective-permute-start(bf16[3088,128]{1,0:T(8,128)(2,1)} %get-tuple-element.163.refs_16_), channel_id=1, source_target_pairs={{0,4},{4,0},{1,5},{5,1},{2,6},{6,2},{3,7},{7,3},{8,12},{12,8},{9,1... | collective-permute-start | bytes 2371592 | tf_op jit(solution)/shard_map/ppermute | solution.py:266
  133.2 45.9 %collective-permute-start.48 = (bf16[3088,128]{1,0:T(8,128)(2,1)}, bf16[3088,128]{1,0:T(8,128)(2,1)}, u32[]{:S(2)}, u32[]{:S(2)}) collective-permute-start(bf16[3088,128]{1,0:T(8,128)(2,1)} %get-tuple-element.161.refs_24_), channel_id=1, source_target_pairs={{0,1},{1,0},{2,3},{3,2},{4,5},{5,4},{6,7},{7,6},{8,9},{9,8},{10,11... | collective-permute-start | bytes 2371592 | tf_op jit(solution)/shard_map/ppermute | solution.py:272
  173.2 20.4 %collective-permute-start.47 = (bf16[3088,128]{1,0:T(8,128)(2,1)}, bf16[3088,128]{1,0:T(8,128)(2,1)}, u32[]{:S(2)}, u32[]{:S(2)}) collective-permute-start(bf16[3088,128]{1,0:T(8,128)(2,1)} %collective-permute-done.46.refs_26_), channel_id=1, source_target_pairs={{0,2},{2,0},{1,3},{3,1},{4,6},{6,4},{5,7},{7,5},{8,10},{10,8},{9,1... | collective-permute-start | bytes 2371592 | tf_op jit(solution)/shard_map/ppermute | solution.py:270
  173.7 20.4 %collective-permute-start.50 = (bf16[3088,128]{1,0:T(8,128)(2,1)}, bf16[3088,128]{1,0:T(8,128)(2,1)}, u32[]{:S(2)}, u32[]{:S(2)}) collective-permute-start(bf16[3088,128]{1,0:T(8,128)(2,1)} %collective-permute-done.46.refs_26_), channel_id=1, source_target_pairs={{0,1},{1,0},{2,3},{3,2},{4,5},{5,4},{6,7},{7,6},{8,9},{9,8},{10,11... | collective-permute-start | bytes 2371592 | tf_op jit(solution)/shard_map/ppermute | solution.py:272
  173.9 20.2 %collective-permute-start.36 = (bf16[3088,128]{1,0:T(8,128)(2,1)}, bf16[3088,128]{1,0:T(8,128)(2,1)}, u32[]{:S(2)}, u32[]{:S(2)}) collective-permute-start(bf16[3088,128]{1,0:T(8,128)(2,1)} %collective-permute-done.34.refs_17_), channel_id=1, source_target_pairs={{0,4},{4,0},{1,5},{5,1},{2,6},{6,2},{3,7},{7,3},{8,12},{12,8},{9,1... | collective-permute-start | bytes 2371592 | tf_op jit(solution)/shard_map/ppermute | solution.py:268
  179.2 24.2 %collective-permute-start.49 = (bf16[3088,128]{1,0:T(8,128)(2,1)}, bf16[3088,128]{1,0:T(8,128)(2,1)S(1)}, u32[]{:S(2)}, u32[]{:S(2)}) collective-permute-start(bf16[3088,128]{1,0:T(8,128)(2,1)} %collective-permute-done.45.refs_25_), channel_id=1, source_target_pairs={{0,1},{1,0},{2,3},{3,2},{4,5},{5,4},{6,7},{7,6},{8,9},{9,8},{10,11... | collective-permute-start | bytes 2371592 | tf_op jit(solution)/shard_map/ppermute | solution.py:272
  196.5 46.5 %collective-permute-start.26 = (f32[3,1792]{1,0:T(4,128)}, f32[3,1792]{1,0:T(4,128)}, u32[]{:S(2)}, u32[]{:S(2)}) collective-permute-start(f32[3,1792]{1,0:T(4,128)} %fusion.43), channel_id=1, source_target_pairs={{0,1},{1,2},{2,3},{3,4},{4,5},{5,6},{6,7},{8,9},{9,10},{10,11},{11... | collective-permute-start | bytes 64520 | tf_op jit(solution)/shard_map/ppermute | solution.py:63
  203.4 71.5 %collective-permute-start.23 = (bf16[2,512,128]{2,1,0:T(8,128)(2,1)}, bf16[2,512,128]{2,1,0:T(8,128)(2,1)}, u32[]{:S(2)}, u32[]{:S(2)}) collective-permute-start(bf16[2,512,128]{2,1,0:T(8,128)(2,1)} %maximum_bitcast_fusion), channel_id=1, source_target_pairs={{0,2},{2,0},{1,3},{3,1},{4,6},{6,4},{5,7},{7,5},{8,10},{10,8},{9,1... | collective-permute-start | bytes 786440 | tf_op jit(solution)/shard_map/ppermute | solution.py:1129
  293.7 23.1 %collective-permute-start.25 = (bf16[2,2,2,512,128]{4,3,2,1,0:T(8,128)(2,1)S(1)}, bf16[2,2,2,512,128]{4,3,2,1,0:T(8,128)(2,1)S(1)}, u32[]{:S(2)}, u32[]{:S(2)}) collective-permute-start(bf16[2,2,2,512,128]{4,3,2,1,0:T(8,128)(2,1)S(1)} %pad_maximum_fusion.8), channel_id=1, source_target_pairs={{0,1},{1,0},{2,3},{3,2},{4,5},{5,4},{6,7},{7,6},{8,9},{9,8},{10,11... | collective-permute-start | bytes 3145736 | tf_op jit(solution)/shard_map/ppermute | solution.py:1131
  383.8 93.3 %collective-permute-start.52 = (bf16[144,1536]{1,0:T(8,128)(2,1)}, bf16[144,1536]{1,0:T(8,128)(2,1)}, u32[]{:S(2)}, u32[]{:S(2)}) collective-permute-start(bf16[144,1536]{1,0:T(8,128)(2,1)} %pad_maximum_fusion.12), channel_id=1, source_target_pairs={{0,1},{1,0},{2,3},{3,2},{4,5},{5,4},{6,7},{7,6},{8,9},{9,8},{10,11... | collective-permute-start | bytes 1327112 | tf_op jit(solution)/shard_map/ppermute | solution.py:931
  433.5 161.7 %collective-permute-start.56 = (bf16[2,2,2,512,128]{3,4,2,1,0:T(8,128)(2,1)}, bf16[2,2,2,512,128]{3,4,2,1,0:T(8,128)(2,1)}, u32[]{:S(2)}, u32[]{:S(2)}) collective-permute-start(bf16[2,2,2,512,128]{3,4,2,1,0:T(8,128)(2,1)} %bitcast.245), channel_id=1, source_target_pairs={{0,1},{1,0},{2,3},{3,2},{4,5},{5,4},{6,7},{7,6},{8,9},{9,8},{10,11... | collective-permute-start | bytes 3145736 | tf_op jit(solution)/shard_map/ppermute | solution.py:1143
  473.7 257.4 %collective-permute-start.73 = (bf16[24688,128]{1,0:T(8,128)(2,1)}, bf16[24688,128]{1,0:T(8,128)(2,1)}, u32[]{:S(2)}, u32[]{:S(2)}) collective-permute-start(bf16[24688,128]{1,0:T(8,128)(2,1)} %constant_dynamic-slice_fusion), channel_id=1, source_target_pairs={{0,1},{1,0},{2,3},{3,2},{4,5},{5,4},{6,7},{7,6},{8,9},{9,8},{10,11... | collective-permute-start | bytes 18960392 | tf_op jit(solution)/shard_map/ppermute | solution.py:604
  478.7 39.0 %collective-permute-start.53 = (bf16[144,1536]{1,0:T(8,128)(2,1)S(1)}, bf16[144,1536]{1,0:T(8,128)(2,1)S(1)}, u32[]{:S(2)}, u32[]{:S(2)}) collective-permute-start(bf16[144,1536]{1,0:T(8,128)(2,1)S(1)} %pad_maximum_fusion.17), channel_id=1, source_target_pairs={{0,2},{2,0},{1,3},{3,1},{4,6},{6,4},{5,7},{7,5},{8,10},{10,8},{9,1... | collective-permute-start | bytes 1327112 | tf_op jit(solution)/shard_map/ppermute | solution.py:931
  519.0 79.7 %collective-permute-start.54 = (bf16[144,1536]{1,0:T(8,128)(2,1)}, bf16[144,1536]{1,0:T(8,128)(2,1)}, u32[]{:S(2)}, u32[]{:S(2)}) collective-permute-start(bf16[144,1536]{1,0:T(8,128)(2,1)} %pad_maximum_fusion.18), channel_id=1, source_target_pairs={{0,4},{4,0},{1,5},{5,1},{2,6},{6,2},{3,7},{7,3},{8,12},{12,8},{9,1... | collective-permute-start | bytes 1327112 | tf_op jit(solution)/shard_map/ppermute | solution.py:931
  598.1 85.2 %collective-permute-start.57 = (bf16[2,2,512,128]{2,3,1,0:T(8,128)(2,1)}, bf16[2,2,512,128]{2,3,1,0:T(8,128)(2,1)}, u32[]{:S(2)}, u32[]{:S(2)}) collective-permute-start(bf16[2,2,512,128]{2,3,1,0:T(8,128)(2,1)} %dynamic-slice_bitcast_fusion.20), channel_id=1, source_target_pairs={{0,4},{4,0},{1,5},{5,1},{2,6},{6,2},{3,7},{7,3},{8,12},{12,8},{9,1... | collective-permute-start | bytes 1572872 | tf_op jit(solution)/shard_map/ppermute | solution.py:1143
  731.1 67.5 %collective-permute-start.59 = (bf16[24688,128]{1,0:T(8,128)(2,1)}, bf16[24688,128]{1,0:T(8,128)(2,1)}, u32[]{:S(2)}, u32[]{:S(2)}) collective-permute-start(bf16[24688,128]{1,0:T(8,128)(2,1)} %constant_dynamic-slice_fusion.1), channel_id=1, source_target_pairs={{0,1},{1,0},{2,3},{3,2},{4,5},{5,4},{6,7},{7,6},{8,9},{9,8},{10,11... | collective-permute-start | bytes 18960392 | tf_op jit(solution)/shard_map/ppermute | solution.py:604
  738.2 54.5 %collective-permute-start.80 = (bf16[2,3104,128]{2,1,0:T(8,128)(2,1)}, bf16[2,3104,128]{2,1,0:T(8,128)(2,1)}, u32[]{:S(2)}, u32[]{:S(2)}) collective-permute-start(bf16[2,3104,128]{2,1,0:T(8,128)(2,1)} %pad_maximum_fusion.7), channel_id=1, source_target_pairs={{0,2},{2,0},{1,3},{3,1},{4,6},{6,4},{5,7},{7,5},{8,10},{10,8},{9,1... | collective-permute-start | bytes 4767752 | tf_op jit(solution)/shard_map/ppermute | solution.py:621
  748.7 27.1 %collective-permute-start.88 = (f32[4]{0:T(128)S(1)}, f32[4]{0:T(128)S(1)}, u32[]{:S(2)}, u32[]{:S(2)}) collective-permute-start(f32[4]{0:T(128)S(1)} %fusion.145), channel_id=1, source_target_pairs={{0,2},{2,0},{1,3},{3,1},{4,6},{6,4},{5,7},{7,5},{8,10},{10,8},{9,1... | collective-permute-start | bytes 56 | tf_op jit(solution)/shard_map/ppermute | solution.py:1153
  750.4 46.1 %collective-permute-start.74 = (bf16[2,3104,128]{2,1,0:T(8,128)(2,1)S(1)}, bf16[2,3104,128]{2,1,0:T(8,128)(2,1)S(1)}, u32[]{:S(2)}, u32[]{:S(2)}) collective-permute-start(bf16[2,3104,128]{2,1,0:T(8,128)(2,1)S(1)} %pad_maximum_fusion.6), channel_id=1, source_target_pairs={{0,4},{4,0},{1,5},{5,1},{2,6},{6,2},{3,7},{7,3},{8,12},{12,8},{9,1... | collective-permute-start | bytes 4767752 | tf_op jit(solution)/shard_map/ppermute | solution.py:621
  788.3 185.2 %collective-permute-start.91 = (f32[4]{0:T(128)S(1)}, f32[4]{0:T(128)S(1)}, u32[]{:S(2)}, u32[]{:S(2)}) collective-permute-start(f32[4]{0:T(128)S(1)} %add.761), channel_id=1, source_target_pairs={{0,16},{16,0},{8,24},{24,8},{1,17},{17,1},{9,25},{25,9},{2,18},{18... | collective-permute-start | bytes 56 | tf_op jit(solution)/shard_map/ppermute | solution.py:1155
  794.6 20.6 %collective-permute-start.81 = (bf16[3104,128]{1,0:T(8,128)(2,1)S(1)}, bf16[3104,128]{1,0:T(8,128)(2,1)S(1)}, u32[]{:S(2)}, u32[]{:S(2)}) collective-permute-start(bf16[3104,128]{1,0:T(8,128)(2,1)S(1)} %dynamic-slice_bitcast_fusion), channel_id=1, source_target_pairs={{0,4},{4,0},{1,5},{5,1},{2,6},{6,2},{3,7},{7,3},{8,12},{12,8},{9,1... | collective-permute-start | bytes 2383880 | tf_op jit(solution)/shard_map/ppermute | solution.py:624
  797.0 22.3 %collective-permute-start.75 = (bf16[3104,128]{1,0:T(8,128)(2,1)S(1)}, bf16[3104,128]{1,0:T(8,128)(2,1)S(1)}, u32[]{:S(2)}, u32[]{:S(2)}) collective-permute-start(bf16[3104,128]{1,0:T(8,128)(2,1)S(1)} %dynamic-slice_bitcast_fusion.5), channel_id=1, source_target_pairs={{0,2},{2,0},{1,3},{3,1},{4,6},{6,4},{5,7},{7,5},{8,10},{10,8},{9,1... | collective-permute-start | bytes 2383880 | tf_op jit(solution)/shard_map/ppermute | solution.py:624
  805.1 49.9 %collective-permute-start.66 = (bf16[2,3104,128]{2,1,0:T(8,128)(2,1)S(1)}, bf16[2,3104,128]{2,1,0:T(8,128)(2,1)S(1)}, u32[]{:S(2)}, u32[]{:S(2)}) collective-permute-start(bf16[2,3104,128]{2,1,0:T(8,128)(2,1)S(1)} %pad_maximum_fusion.5), channel_id=1, source_target_pairs={{0,2},{2,0},{1,3},{3,1},{4,6},{6,4},{5,7},{7,5},{8,10},{10,8},{9,1... | collective-permute-start | bytes 4767752 | tf_op jit(solution)/shard_map/ppermute | solution.py:621
  805.7 50.3 %collective-permute-start.60 = (bf16[2,3104,128]{2,1,0:T(8,128)(2,1)S(1)}, bf16[2,3104,128]{2,1,0:T(8,128)(2,1)S(1)}, u32[]{:S(2)}, u32[]{:S(2)}) collective-permute-start(bf16[2,3104,128]{2,1,0:T(8,128)(2,1)S(1)} %pad_maximum_fusion.4), channel_id=1, source_target_pairs={{0,4},{4,0},{1,5},{5,1},{2,6},{6,2},{3,7},{7,3},{8,12},{12,8},{9,1... | collective-permute-start | bytes 4767752 | tf_op jit(solution)/shard_map/ppermute | solution.py:621
  815.4 19.5 %collective-permute-start.82 = (bf16[3104,128]{1,0:T(8,128)(2,1)S(1)}, bf16[3104,128]{1,0:T(8,128)(2,1)S(1)}, u32[]{:S(2)}, u32[]{:S(2)}) collective-permute-start(bf16[3104,128]{1,0:T(8,128)(2,1)S(1)} %fusion.23), channel_id=1, source_target_pairs={{0,8},{1,9},{2,10},{3,11},{4,12},{5,13},{6,14},{7,15}} | collective-permute-start | bytes 2383880 | tf_op jit(solution)/shard_map/ppermute | solution.py:631
  819.3 38.1 %collective-permute-start.84 = (bf16[3104,128]{1,0:T(8,128)(2,1)S(1)}, bf16[3104,128]{1,0:T(8,128)(2,1)S(1)}, u32[]{:S(2)}, u32[]{:S(2)}) collective-permute-start(bf16[3104,128]{1,0:T(8,128)(2,1)S(1)} %fusion.23), channel_id=1, source_target_pairs={{24,16},{26,18},{28,20},{30,22}} | collective-permute-start | bytes 2383880 | tf_op jit(solution)/shard_map/ppermute | solution.py:632
  860.7 21.8 %collective-permute-start.85 = (bf16[3104,128]{1,0:T(8,128)(2,1)S(1)}, bf16[3104,128]{1,0:T(8,128)(2,1)S(1)}, u32[]{:S(2)}, u32[]{:S(2)}) collective-permute-start(bf16[3104,128]{1,0:T(8,128)(2,1)S(1)} %add_convert_fusion.9), channel_id=1, source_target_pairs={{17,25},{19,27},{21,29},{23,31}} | collective-permute-start | bytes 2383880 | tf_op jit(solution)/shard_map/ppermute | solution.py:634
  861.8 20.7 %collective-permute-start.79 = (bf16[3104,128]{1,0:T(8,128)(2,1)S(1)}, bf16[3104,128]{1,0:T(8,128)(2,1)S(1)}, u32[]{:S(2)}, u32[]{:S(2)}) collective-permute-start(bf16[3104,128]{1,0:T(8,128)(2,1)S(1)} %add_convert_fusion.12), channel_id=1, source_target_pairs={{17,25},{19,27},{21,29},{23,31}} | collective-permute-start | bytes 2383880 | tf_op jit(solution)/shard_map/ppermute | solution.py:634
  879.6 77.7 %collective-permute-start.71 = (bf16[3104,128]{1,0:T(8,128)(2,1)S(1)}, bf16[3104,128]{1,0:T(8,128)(2,1)S(1)}, u32[]{:S(2)}, u32[]{:S(2)}) collective-permute-start(bf16[3104,128]{1,0:T(8,128)(2,1)S(1)} %add_convert_fusion.15), channel_id=1, source_target_pairs={{8,0},{10,2},{12,4},{14,6}} | collective-permute-start | bytes 2383880 | tf_op jit(solution)/shard_map/ppermute | solution.py:629
  881.2 90.5 %collective-permute-start.65 = (bf16[3104,128]{1,0:T(8,128)(2,1)S(1)}, bf16[3104,128]{1,0:T(8,128)(2,1)S(1)}, u32[]{:S(2)}, u32[]{:S(2)}) collective-permute-start(bf16[3104,128]{1,0:T(8,128)(2,1)S(1)} %add_convert_fusion.18), channel_id=1, source_target_pairs={{8,0},{10,2},{12,4},{14,6}} | collective-permute-start | bytes 2383880 | tf_op jit(solution)/shard_map/ppermute | solution.py:629
  883.2 93.4 %collective-permute-start.86 = (bf16[3104,128]{1,0:T(8,128)(2,1)S(1)}, bf16[3104,128]{1,0:T(8,128)(2,1)S(1)}, u32[]{:S(2)}, u32[]{:S(2)}) collective-permute-start(bf16[3104,128]{1,0:T(8,128)(2,1)S(1)} %get-tuple-element.103), channel_id=1, source_target_pairs={{0,1},{9,8},{16,17},{25,24},{2,3},{11,10},{18,19},{27,26},{4,5},{1... | collective-permute-start | bytes 2383880 | tf_op jit(solution)/shard_map/ppermute | solution.py:639
  (235 other events, 3642.6 us)

commit v4 on v3

--- a/solution.py
+++ b/solution.py
@@ -239,6 +239,14 @@
 
 def zc_pairs(*pairs):
     return [(2 * a + c, 2 * b + c) for a, b, c in pairs]
+
+
+def pinned(kernel, count, after):
+    return lambda *refs: kernel(*refs[:count], *refs[count + len(after) :])
+
+
+def pins(after):
+    return [pl.BlockSpec(memory_space=pltpu.HBM)] * len(after)
 
 
 def gather_lines(params):
@@ -278,7 +286,7 @@
     return batches, where.astype(jnp.int32)
 
 
-def unpack_lines(buffers, first, where, segments):
+def unpack_lines(buffers, first, where, segments, after=()):
     jobs, starts = [], []
     reach = 0
     for offset, rows, columns in segments:
@@ -411,11 +419,11 @@
                     written(block, side).wait()
 
     return pl.pallas_call(
-        kernel,
+        pinned(kernel, 2 + count_buffers, after),
         grid_spec=pltpu.PrefetchScalarGridSpec(
             num_scalar_prefetch=2,
             grid=(total,),
-            in_specs=[pl.BlockSpec(memory_space=pl.ANY)] * count_buffers,
+            in_specs=[pl.BlockSpec(memory_space=pl.ANY)] * count_buffers + pins(after),
             out_specs=[pl.BlockSpec(memory_space=pl.ANY)] * len(segments),
             scratch_shapes=[pltpu.VMEM((2,) + size, jnp.bfloat16) for size in sizes]
             + [
@@ -429,10 +437,10 @@
         compiler_params=pltpu.CompilerParams(vmem_limit_bytes=48 * 2**20),
         cost_estimate=pl.CostEstimate(flops=0, bytes_accessed=total * window * LINE * 4, transcendentals=0),
         name="unpack",
-    )(jnp.asarray(table), where, *buffers)
-
-
-def pack_lines(target, target_rows, first_row, segments, lane, phase, extras, carry, tail_rows):
+    )(jnp.asarray(table), where, *buffers, *after)
+
+
+def pack_lines(target, target_rows, first_row, segments, lane, phase, extras, carry, tail_rows, after=()):
     tall = 256
     lefts, rights, plan = [], [], []
     left_of, right_of = {}, {}
@@ -564,14 +572,16 @@
 
     whole = [pl.BlockSpec(array.shape, lambda step: (0, 0)) for array in rolled]
     flops = sum(2 * tokens * entry[4] * tall * entry[2] * LINE for entry in plan)
+    inputs = count_left + count_right + count_extra + len(carry_in) + len(targets)
     return pl.pallas_call(
-        kernel,
+        pinned(kernel, inputs, after),
         grid=(total,),
         in_specs=[left_spec(k) for k in range(count_left)]
         + whole
         + [pl.BlockSpec(array.shape, lambda step: (0, 0)) for array, _ in extras]
         + [pl.BlockSpec(array.shape, lambda step: (0, 0)) for array in carry_in]
-        + [pl.BlockSpec(memory_space=pl.ANY)] * len(targets),
+        + [pl.BlockSpec(memory_space=pl.ANY)] * len(targets)
+        + pins(after),
         out_specs=pl.BlockSpec(memory_space=pl.ANY),
         out_shape=jax.ShapeDtypeStruct((target_rows, LINE), jnp.bfloat16),
         scratch_shapes=[
@@ -586,7 +596,7 @@
         compiler_params=pltpu.CompilerParams(vmem_limit_bytes=48 * 2**20),
         cost_estimate=pl.CostEstimate(flops=flops, bytes_accessed=total * biggest * LINE * 2, transcendentals=0),
         name="pack",
-    )(*lefts, *rolled, *[array for array, _ in extras], *carry_in, *targets)
+    )(*lefts, *rolled, *[array for array, _ in extras], *carry_in, *targets, *after)
 
 
 def added(*parts):
@@ -596,48 +606,78 @@
     return total.astype(jnp.bfloat16)
 
 
-def reduce_lines(flat, batch, shift):
+class Flow:
+    def __init__(self, stages):
+        self.stages = stages
+        self.sends = next(stages)
+        self.result = None
+
+    def values(self):
+        return [value for value, _, _ in self.sends]
+
+    def go(self):
+        arrived = [lax.ppermute(value, axis, pairs) for value, axis, pairs in self.sends]
+        try:
+            self.sends = self.stages.send(arrived)
+        except StopIteration as stop:
+            self.sends, self.result = [], stop.value
+        return self
+
+
+def reduce_stages(flat, batch, shift):
     z, y, x, c = (lax.axis_index(name) for name in GRID)
     length = PLANE + 32
-    keep = lax.dynamic_slice(flat, (c * PLANE, 0), (length, LINE))
     send = lax.dynamic_slice(flat, ((1 - c) * PLANE, 0), (length, LINE))
-    chip = added(keep, lax.ppermute(send, "c", SWAP))
+    (arrived,) = yield [(send, "c", SWAP)]
+    chip = added(lax.dynamic_slice(flat, (c * PLANE, 0), (length, LINE)), arrived)
 
     def window(sy, sx, part):
         shard = sy * 4 + sx * 2 + part
         start = (shift + SHARD * shard) // 16 * 16
         return lax.dynamic_slice(chip, (start, 0), (WIN, LINE))
 
-    ends = []
-    for part in range(2):
-        if part == 0:
-            away = jnp.stack([window(1 - y, 0, part), window(1 - y, 1, part)])
-            home = jnp.stack([window(y, 0, part), window(y, 1, part)])
-            first_axis, second_axis, place = "y", "x", x
-        else:
-            away = jnp.stack([window(0, 1 - x, part), window(1, 1 - x, part)])
-            home = jnp.stack([window(0, x, part), window(1, x, part)])
-            first_axis, second_axis, place = "x", "y", y
-        half = added(home, lax.ppermute(away, first_axis, SWAP))
-        other = lax.dynamic_index_in_dim(half, 1 - place, 0, keepdims=False)
-        mine = lax.dynamic_index_in_dim(half, place, 0, keepdims=False)
-        column = added(mine, lax.ppermute(other, second_axis, SWAP))
-        if batch == 0:
-            one = added(column, lax.ppermute(column, ZC, zc_pairs((3, 2, 0), (3, 2, 1))))
-            side = lax.ppermute(column, ZC, zc_pairs((0, 1, 1)))
-            two = added(one, lax.ppermute(one, ZC, zc_pairs((2, 1, 0), (2, 1, 1))), side)
-            end = added(two, lax.ppermute(two, ZC, zc_pairs((1, 0, 0))))
-        else:
-            one = added(column, lax.ppermute(column, ZC, zc_pairs((0, 1, 0), (0, 1, 1))))
-            side = lax.ppermute(column, ZC, zc_pairs((3, 2, 0)))
-            two = added(one, lax.ppermute(one, ZC, zc_pairs((1, 2, 0), (1, 2, 1))), side)
-            end = added(two, lax.ppermute(two, ZC, zc_pairs((2, 3, 1))))
-        ends.append(end)
+    away_0 = jnp.stack([window(1 - y, 0, 0), window(1 - y, 1, 0)])
+    away_1 = jnp.stack([window(0, 1 - x, 1), window(1, 1 - x, 1)])
+    home_0 = jnp.stack([window(y, 0, 0), window(y, 1, 0)])
+    home_1 = jnp.stack([window(0, x, 1), window(1, x, 1)])
+    got_0, got_1 = yield [(away_0, "y", SWAP), (away_1, "x", SWAP)]
+    half_0, half_1 = added(home_0, got_0), added(home_1, got_1)
+    pick = lambda value, at: lax.dynamic_index_in_dim(value, at, 0, keepdims=False)
+    got_0, got_1 = yield [(pick(half_0, 1 - x), "x", SWAP), (pick(half_1, 1 - y), "y", SWAP)]
+    columns = [added(pick(half_0, x), got_0), added(pick(half_1, y), got_1)]
+    if batch == 0:
+        hops = [((1, 0, 0), (2, 1, 1)), ((2, 0, 0), (3, 1, 1)), ((3, 0, 0), (0, 1, 1))]
+    else:
+        hops = [((1, 2, 0), (2, 3, 1)), ((0, 2, 0), (1, 3, 1)), ((3, 2, 0), (0, 3, 1))]
+    got = yield [(column, ZC, zc_pairs(*hop)) for column in columns for hop in hops]
+    ends = [added(columns[0], *got[:3]), added(columns[1], *got[3:])]
     mine = jnp.where(c == 0, ends[0], ends[1])
     other = jnp.where(c == 0, ends[1], ends[0])
-    holders = [(2 * k + k % 2, 2 * k + 1 - k % 2) for k in range(4)]
-    handed = lax.ppermute(other, ZC, holders)
+    (handed,) = yield [(other, ZC, [(2 * k + k % 2, 2 * k + 1 - k % 2) for k in range(4)])]
     return jnp.where(c == z % 2, mine, handed)
+
+
+PIECE = 400
+
+
+def corner_stages(flat):
+    z, y, x, c = (lax.axis_index(name) for name in GRID)
+    length = 8 * PIECE
+    second = (8 + SHARD) // 16 * 16
+    take = lambda at: lax.dynamic_slice(flat, (at * second, 0), (length, LINE))
+    (arrived,) = yield [(take(1 - c), "c", SWAP)]
+    chip = added(take(c), arrived).reshape(2, 2, 2, PIECE, LINE)
+    pick = lambda value, at: lax.dynamic_index_in_dim(value, at, 0, keepdims=False)
+    got = yield [(pick(chip[0], 1 - x), "x", SWAP), (pick(chip[1], 1 - y), "y", SWAP)]
+    halves = [added(pick(chip[0], x), got[0]), added(pick(chip[1], y), got[1])]
+    got = yield [(pick(halves[0], 1 - y), "y", SWAP), (pick(halves[1], 1 - x), "x", SWAP)]
+    pieces = jnp.stack([added(pick(halves[0], y), got[0]), added(pick(halves[1], x), got[1])])
+    got = yield [(pieces, "z", [(k, 0)]) for k in (1, 2, 3)]
+    pieces = added(pieces, *got)
+    got = yield [(pieces[0], "y", [(1, 0)]), (pieces[1], "x", [(1, 0)])]
+    halves = [jnp.stack([pieces[0], got[0]]), jnp.stack([pieces[1], got[1]])]
+    got = yield [(halves[0], "x", [(1, 0)]), (halves[1], "y", [(1, 0)])]
+    return jnp.stack([halves[0], got[0], halves[1], got[1]]).reshape(length, LINE)
 
 
 CHUNK = 128
@@ -655,29 +695,32 @@
     return tall.T
 
 
-def weighted_state(left, values, weight_rows):
+def weighted_state(left, values, weight_rows, after=()):
     rows = left.shape[0]
 
-    def kernel(left_ref, value_ref, weight_ref, out_ref):
+    def kernel(left_ref, value_ref, weight_ref, out_ref, turned):
+        @pl.when(pl.program_id(0) == 0)
+        def _():
+            turned[...] = left_ref[...].T.astype(jnp.bfloat16)
+
         wide = spread(weight_ref[0, 0:1, :], weight_ref[0, 1:2, :])
         scaled = (value_ref[...] * wide).astype(jnp.bfloat16)
-        out_ref[...] = lax.dot_general(
-            left_ref[...].astype(jnp.bfloat16), scaled, TN, preferred_element_type=jnp.float32
-        )
+        out_ref[...] = jnp.dot(turned[...], scaled, preferred_element_type=jnp.float32)
 
     return pl.pallas_call(
-        kernel,
+        pinned(kernel, 3, after),
         grid=(PAIRS,),
         in_specs=[
             pl.BlockSpec((rows, STATE), lambda i: (0, 0)),
             pl.BlockSpec((rows, 2 * SSM_DIM), lambda i: (0, i)),
             pl.BlockSpec((1, 2, rows), lambda i: (i, 0, 0)),
-        ],
+        ] + pins(after),
         out_specs=pl.BlockSpec((STATE, 2 * SSM_DIM), lambda i: (0, i)),
         out_shape=jax.ShapeDtypeStruct((STATE, INNER), jnp.float32),
+        scratch_shapes=[pltpu.VMEM((STATE, rows), jnp.bfloat16)],
         cost_estimate=pl.CostEstimate(flops=2 * rows * STATE * INNER, bytes_accessed=rows * INNER * 4, transcendentals=0),
         name="state",
-    )(left, values, weight_rows.reshape(PAIRS, 2, rows))
+    )(left, values, weight_rows.reshape(PAIRS, 2, rows), *after)
 
 
 def chunk_rows(k, meta_ref, cum_ref, start_ref):
@@ -701,11 +744,12 @@
     chunks = rows // CHUNK
 
     def kernel(meta_ref, x_ref, b_ref, c_ref, cum_ref, step_ref, state_ref, skip_ref, col_ref, row_ref,
-               y_ref, inner, hide, state):
+               y_ref, inner, hide, state, b_turned):
         @pl.when(pl.program_id(0) == 0)
         def _():
             for k in range(chunks):
                 here = slice(k * CHUNK, (k + 1) * CHUNK)
+                b_turned[:, here] = b_ref[here, :].T.astype(jnp.bfloat16)
                 inner[k] = lax.dot_general(
                     c_ref[here, :], b_ref[here, :], NT, precision=highest, preferred_element_type=jnp.float32
                 )
@@ -734,9 +778,8 @@
                 preferred_element_type=jnp.float32,
             )
             y_ref[here, :] = jnp.where(low_lane, parts[0], parts[1]) + entry * carried + skip_ref[...] * x_now
-            fresh = lax.dot_general(
-                b_ref[here, :].astype(jnp.bfloat16), (x_now * weight).astype(jnp.bfloat16), TN,
-                preferred_element_type=jnp.float32,
+            fresh = jnp.dot(
+                b_turned[:, here], (x_now * weight).astype(jnp.bfloat16), preferred_element_type=jnp.float32
             )
             state[...] = entry[CHUNK - 1 :, :] * state[...] + fresh
 
@@ -763,6 +806,7 @@
                 pltpu.VMEM((chunks, CHUNK, CHUNK), jnp.float32),
                 pltpu.VMEM((chunks, CHUNK, CHUNK), jnp.float32),
                 pltpu.VMEM((STATE, 2 * SSM_DIM), jnp.float32),
+                pltpu.VMEM((STATE, rows), jnp.bfloat16),
             ],
         ),
         out_shape=jax.ShapeDtypeStruct((rows, INNER), jnp.float32),
@@ -773,12 +817,13 @@
       start_column, start_row)
 
 
-def ssm_backward(x, dy, b_in, c_in, cum, step, state_in, state_grad, skip, meta, start_row):
+def ssm_backward(x, dy, b_in, c_in, cum, step, state_in, state_grad, skip, meta, start_row, after=()):
     rows = x.shape[0]
     chunks = rows // CHUNK
 
     def kernel(meta_ref, x_ref, dy_ref, b_ref, c_ref, cum_ref, step_ref, state_ref, grad_ref, skip_ref, row_ref,
-               dx_ref, db_ref, dc_ref, small_ref, inner, hide, inner_grad, states, flow):
+               dx_ref, db_ref, dc_ref, small_ref, inner, hide, inner_grad, states, flow,
+               b_turned, c_turned):
         low = lambda v: v.astype(jnp.bfloat16)
         dot = lambda p, q, dims=(((1,), (0,)), ((), ())): lax.dot_general(
             p, q, dims, preferred_element_type=jnp.float32
@@ -796,6 +841,8 @@
             inner_grad[...] = jnp.zeros(inner_grad.shape, jnp.float32)
             for k in range(chunks):
                 here = slice(k * CHUNK, (k + 1) * CHUNK)
+                b_turned[:, here] = low(b_ref[here, :].T)
+                c_turned[:, here] = low(c_ref[here, :].T)
                 inner[k] = exact(b_ref[here, :], c_ref[here, :], NT)
                 shown = (s <= t) & (meta_ref[0] + k * CHUNK + s >= row_ref[0:1, here])
                 hide[k] = jnp.where(shown, 0.0, masked_score)
@@ -815,7 +862,7 @@
             steps = spread(step_ref[0, 0:1, here], step_ref[0, 1:2, here])
             spreads.append((cums, entry, tail, steps))
             if k < chunks - 1:
-                fresh = dot(low(b_ref[here, :]), low(x_ref[here, :] * steps * tail), TN)
+                fresh = dot(b_turned[:, here], low(x_ref[here, :] * steps * tail))
                 states[k + 1] = entry[CHUNK - 1 :, :] * states[k] + fresh
         flow[...] = grad_ref[...]
         skip_sum = jnp.zeros((1, 2 * SSM_DIM), jnp.float32)
@@ -855,7 +902,7 @@
                 small_ref[0, 2 + e : 3 + e, here] = log_grad[e : e + 1, :] + within[e] + kept
             dx_ref[here, :] = dxs * steps + skip_ref[...] * dy_now
             skip_sum += jnp.sum(x_now * dy_now, axis=0, keepdims=True)
-            flow[...] = entry[CHUNK - 1 :, :] * flow[...] + dot(c_low, entered, TN)
+            flow[...] = entry[CHUNK - 1 :, :] * flow[...] + dot(c_turned[:, here], entered)
         small_ref[0, 4:8, :] = jnp.zeros((4, rows), jnp.float32)
         small_ref[0, 4:5, 0 : 2 * SSM_DIM] = skip_sum
 
@@ -871,7 +918,7 @@
     lanes = lambda i, m: (0, i)
     pair = lambda i, m: (i, 0, 0)
     return pl.pallas_call(
-        kernel,
+        pinned(kernel, 11, after),
         grid_spec=pltpu.PrefetchScalarGridSpec(
             num_scalar_prefetch=1,
             grid=(PAIRS,),
@@ -886,7 +933,7 @@
                 pl.BlockSpec((STATE, 2 * SSM_DIM), lanes),
                 pl.BlockSpec((1, 2 * SSM_DIM), lanes),
                 pl.BlockSpec((8, rows), whole),
-            ],
+            ] + pins(after),
             out_specs=[
                 pl.BlockSpec((rows, 2 * SSM_DIM), lanes),
                 pl.BlockSpec((rows, STATE), whole),
@@ -899,6 +946,8 @@
                 pltpu.VMEM((chunks, CHUNK, CHUNK), jnp.float32),
                 pltpu.VMEM((chunks, STATE, 2 * SSM_DIM), jnp.float32),
                 pltpu.VMEM((STATE, 2 * SSM_DIM), jnp.float32),
+                pltpu.VMEM((STATE, rows), jnp.bfloat16),
+                pltpu.VMEM((STATE, rows), jnp.bfloat16),
             ],
         ),
         out_shape=[
@@ -911,7 +960,7 @@
         cost_estimate=pl.CostEstimate(flops=3 * 10**9, bytes_accessed=rows * INNER * 12, transcendentals=2**21),
         name="ssm_back",
     )(meta, x, dy, b_in, c_in, cum.reshape(PAIRS, 2, rows), step.reshape(PAIRS, 2, rows), state_in, state_grad,
-      skip, start_row)
+      skip, start_row, *after)
 
 
 def chain_states(earlier, later):
@@ -944,75 +993,81 @@
 PAIR = 2 * HEAD_DIM
 
 
-def attention_forward(q_wide, kv, meta, starts):
+def attention_forward(q_wide, kv, meta, starts, after=()):
     rows = q_wide.shape[1]
     blocks = kv.shape[0]
+    ratio = HEADS_Q // HEADS_KV
     wide = min(256, rows)
 
-    def kernel(meta_ref, q_ref, kv_ref, start_ref, o_ref, log_ref, top, total, mixed):
-        top[...] = jnp.full(top.shape, masked_score, jnp.float32)
-        total[...] = jnp.zeros(total.shape, jnp.float32)
-        mixed[...] = jnp.zeros(mixed.shape, jnp.float32)
-
-        def block(b, partial):
-            pair = kv_ref[b, 0]
+    def kernel(meta_ref, q_ref, kv_ref, start_ref, o_ref, log_ref, top, total):
+        b = pl.program_id(1)
+
+        @pl.when(b == 0)
+        def _():
+            top[...] = jnp.full(top.shape, masked_score, jnp.float32)
+            total[...] = jnp.zeros(total.shape, jnp.float32)
+            o_ref[...] = jnp.zeros(o_ref.shape, jnp.float32)
+
+        def block(partial):
+            pair = kv_ref[0, 0]
             turned = pair.T[HEAD_DIM:, :]
-            for r in range(0, rows, wide):
-                here = slice(r, r + wide)
-                scores = lax.dot_general(pair, q_ref[0, here, :], NT, preferred_element_type=jnp.float32)
-                if partial:
-                    keys = b * KEYS + lax.broadcasted_iota(jnp.int32, scores.shape, 0)
-                    mine = meta_ref[2] + r + lax.broadcasted_iota(jnp.int32, scores.shape, 1)
-                    visible = (keys >= start_ref[0:1, here]) & (keys <= mine)
-                    scores = jnp.where(visible, scores, masked_score)
-                before = top[0:1, here]
-                peak = jnp.maximum(before, jnp.max(scores, axis=0, keepdims=True))
-                part = jnp.exp(scores - peak)
-                if partial:
-                    part = jnp.where(visible, part, 0.0)
-                fade = jnp.exp(before - peak)
-                top[0:1, here] = peak
-                total[0:1, here] = total[0:1, here] * fade + jnp.sum(part, axis=0, keepdims=True)
-                mixed[:, here] = mixed[:, here] * fade + jnp.dot(
-                    turned, part.astype(jnp.bfloat16), preferred_element_type=jnp.float32
-                )
-
-        def turn(b, nothing):
-            partial = ((b + 1) * KEYS > meta_ref[2]) | (b * KEYS < meta_ref[3])
-
-            @pl.when(partial)
-            def _():
-                block(b, True)
-
-            @pl.when(jnp.logical_not(partial))
-            def _():
-                block(b, False)
-
-            return nothing
-
-        lax.fori_loop(meta_ref[0], meta_ref[1], turn, 0)
-        o_ref[0] = mixed[...] / total[0:1, :]
-        log_ref[0] = jnp.broadcast_to(top[0:1, :] + jnp.log(total[0:1, :]), (8, rows))
-
-    ratio = HEADS_Q // HEADS_KV
+            for h in range(ratio):
+                for r in range(0, rows, wide):
+                    here = slice(r, r + wide)
+                    scores = lax.dot_general(pair, q_ref[h, here, :], NT, preferred_element_type=jnp.float32)
+                    if partial:
+                        keys = b * KEYS + lax.broadcasted_iota(jnp.int32, scores.shape, 0)
+                        mine = meta_ref[2] + r + lax.broadcasted_iota(jnp.int32, scores.shape, 1)
+                        visible = (keys >= start_ref[0:1, here]) & (keys <= mine)
+                        scores = jnp.where(visible, scores, masked_score)
+                    before = top[h, 0:1, here]
+                    peak = jnp.maximum(before, jnp.max(scores, axis=0, keepdims=True))
+                    part = jnp.exp(scores - peak)
+                    if partial:
+                        part = jnp.where(visible, part, 0.0)
+                    fade = jnp.exp(before - peak)
+                    top[h, 0:1, here] = peak
+                    total[h, 0:1, here] = total[h, 0:1, here] * fade + jnp.sum(part, axis=0, keepdims=True)
+                    o_ref[h, :, here] = o_ref[h, :, here] * fade + jnp.dot(
+                        turned, part.astype(jnp.bfloat16), preferred_element_type=jnp.float32
+                    )
+
+        needed = (b >= meta_ref[0]) & (b < meta_ref[1])
+        partial = ((b + 1) * KEYS > meta_ref[2]) | (b * KEYS < meta_ref[3])
+
+        @pl.when(needed & partial)
+        def _():
+            block(True)
+
+        @pl.when(needed & jnp.logical_not(partial))
+        def _():
+            block(False)
+
+        @pl.when(b == blocks - 1)
+        def _():
+            for h in range(ratio):
+                sums = total[h, 0:1, :]
+                o_ref[h] = o_ref[h] / sums
+                log_ref[h] = jnp.broadcast_to(top[h, 0:1, :] + jnp.log(sums), (8, rows))
+
+    heads = lambda g, b, m: (g, 0, 0)
     return pl.pallas_call(
-        kernel,
+        pinned(kernel, 4, after),
         grid_spec=pltpu.PrefetchScalarGridSpec(
             num_scalar_prefetch=1,
-            grid=(HEADS_Q,),
+            grid=(HEADS_KV, blocks),
             in_specs=[
-                pl.BlockSpec((1, rows, PAIR), lambda h, m: (h, 0, 0)),
-                pl.BlockSpec((blocks, 1, KEYS, PAIR), lambda h, m: (0, h // ratio, 0, 0)),
-                pl.BlockSpec((8, rows), lambda h, m: (0, 0)),
-            ],
+                pl.BlockSpec((ratio, rows, PAIR), heads),
+                pl.BlockSpec((1, 1, KEYS, PAIR), lambda g, b, m: (b, g, 0, 0)),
+                pl.BlockSpec((8, rows), lambda g, b, m: (0, 0)),
+            ] + pins(after),
             out_specs=[
-                pl.BlockSpec((1, HEAD_DIM, rows), lambda h, m: (h, 0, 0)),
-                pl.BlockSpec((1, 8, rows), lambda h, m: (h, 0, 0)),
+                pl.BlockSpec((ratio, HEAD_DIM, rows), heads),
+                pl.BlockSpec((ratio, 8, rows), heads),
             ],
             scratch_shapes=[
-                pltpu.VMEM((8, rows), jnp.float32),
-                pltpu.VMEM((8, rows), jnp.float32),
-                pltpu.VMEM((HEAD_DIM, rows), jnp.float32),
+                pltpu.VMEM((ratio, 8, rows), jnp.float32),
+                pltpu.VMEM((ratio, 8, rows), jnp.float32),
             ],
         ),
         out_shape=[
@@ -1020,19 +1075,19 @@
             jax.ShapeDtypeStruct((HEADS_Q, 8, rows), jnp.float32),
         ],
         compiler_params=pltpu.CompilerParams(vmem_limit_bytes=48 * 2**20),
-        cost_estimate=pl.CostEstimate(flops=4 * 10**9, bytes_accessed=2**23, transcendentals=2**23),
+        cost_estimate=pl.CostEstimate(flops=2 * 10**10, bytes_accessed=2**23, transcendentals=2**23),
         name="attend",
-    )(meta, q_wide, kv, starts)
-
-
-def attention_backward(q_wide, g_wide, kv, logs, mixed, meta, starts):
+    )(meta, q_wide, kv, starts, *after)
+
+
+def attention_backward(q_wide, g_wide, kv, logs, mixed, meta, starts, group, after=()):
     rows = q_wide.shape[1]
     blocks = kv.shape[0]
     ratio = HEADS_Q // HEADS_KV
     wide = min(256, rows)
 
     def kernel(meta_ref, q_ref, g_ref, kv_ref, log_ref, o_ref, start_ref, dkv_ref, dq_ref, delta, sums):
-        b = pl.program_id(1)
+        b = pl.program_id(0)
 
         @pl.when(b == 0)
         def _():
@@ -1083,23 +1138,23 @@
         def _():
             dkv_ref[0, 0] = jnp.zeros((KEYS, PAIR), jnp.bfloat16)
 
-    heads = lambda g, b, m: (g, 0, 0)
+    heads = lambda b, m: (group, 0, 0)
     return pl.pallas_call(
-        kernel,
+        pinned(kernel, 7, after),
         grid_spec=pltpu.PrefetchScalarGridSpec(
             num_scalar_prefetch=1,
-            grid=(HEADS_KV, blocks),
+            grid=(blocks,),
             in_specs=[
                 pl.BlockSpec((ratio, rows, PAIR), heads),
                 pl.BlockSpec((ratio, rows, PAIR), heads),
-                pl.BlockSpec((1, 1, KEYS, PAIR), lambda g, b, m: (b, g, 0, 0)),
+                pl.BlockSpec((1, 1, KEYS, PAIR), lambda b, m: (b, group, 0, 0)),
                 pl.BlockSpec((ratio, 8, rows), heads),
                 pl.BlockSpec((ratio, HEAD_DIM, rows), heads),
-                pl.BlockSpec((8, rows), lambda g, b, m: (0, 0)),
-            ],
+                pl.BlockSpec((8, rows), lambda b, m: (0, 0)),
+            ] + pins(after),
             out_specs=[
-                pl.BlockSpec((1, 1, KEYS, PAIR), lambda g, b, m: (b, g, 0, 0)),
-                pl.BlockSpec((ratio, HEAD_DIM, rows), heads),
+                pl.BlockSpec((1, 1, KEYS, PAIR), lambda b, m: (b, 0, 0, 0)),
+                pl.BlockSpec((ratio, HEAD_DIM, rows), lambda b, m: (0, 0, 0)),
             ],
             scratch_shapes=[
                 pltpu.VMEM((ratio, 8, rows), jnp.float32),
@@ -1107,13 +1162,13 @@
             ],
         ),
         out_shape=[
-            jax.ShapeDtypeStruct((blocks, HEADS_KV, KEYS, PAIR), jnp.bfloat16),
-            jax.ShapeDtypeStruct((HEADS_Q, HEAD_DIM, rows), jnp.float32),
+            jax.ShapeDtypeStruct((blocks, 1, KEYS, PAIR), jnp.bfloat16),
+            jax.ShapeDtypeStruct((ratio, HEAD_DIM, rows), jnp.float32),
         ],
         compiler_params=pltpu.CompilerParams(vmem_limit_bytes=48 * 2**20),
-        cost_estimate=pl.CostEstimate(flops=5 * 10**9, bytes_accessed=2**23, transcendentals=2**23),
+        cost_estimate=pl.CostEstimate(flops=2 * 10**10, bytes_accessed=2**23, transcendentals=2**23),
         name="attend_back",
-    )(meta, q_wide, g_wide, kv, logs, mixed, starts)
+    )(meta, q_wide, g_wide, kv, logs, mixed, starts, *after)
 
 
 def ordered(place, own, other, axis):
@@ -1164,83 +1219,102 @@
     return places
 
 
-def fast_weights(params):
+def early_weights(params):
     places = offsets_of()
     (early, late), where = gather_lines(params)
-    early_names = (W_QUERY, W_KEY, W_VALUE, W_ATTN_OUT, W_GATE_SSM, W_X_SSM, W_B_C)
-    late_names = (W_SSM_OUT, W_GATE, W_UP_PROJ, W_DOWN)
-
-    def segment(name_key):
-        at, extent = places[name_key]
-        return (at, extent[0], extent[1])
-
+    names = (W_QUERY, W_KEY, W_VALUE, W_ATTN_OUT, W_GATE_SSM, W_X_SSM, W_B_C)
     misc_at = places[W_STEP][0]
     first = unpack_lines(
-        early, 0, where,
-        [segment(name_key) for name_key in early_names] + [(0, 16, LINE), (misc_at, 288, LINE)],
-    )
-    second = unpack_lines(
-        early + late, 0, where,
-        [segment(name_key) for name_key in late_names] + [(places[NORM_FFN][0], 16, LINE)],
-    )
-    weights = dict(zip(early_names, first))
-    weights.update(zip(late_names, second))
+        early, 0, where, [flat_segment(name_key) for name_key in names] + [(0, 16, LINE), (misc_at, 288, LINE)]
+    )
+    weights = dict(zip(names, first))
     weights[NORM_ATTN] = first[-2].reshape(-1)[:D]
     misc = first[-1].reshape(-1)
     for name_key in (W_STEP,) + small_names[1:-1]:
         at, extent = places[name_key]
         weights[name_key] = misc[at - misc_at : at - misc_at + math.prod(extent)].reshape(extent)
-    lane = places[NORM_FFN][0] % LINE
-    weights[NORM_FFN] = second[-1].reshape(-1)[lane : lane + D]
+    return weights, (early + late, where)
+
+
+def flat_segment(name_key):
+    at, extent = offsets_of()[name_key]
+    return (at, extent[0], extent[1])
+
+
+def late_weights(held, after):
+    buffers, where = held
+    names = (W_SSM_OUT, W_GATE, W_UP_PROJ, W_DOWN)
+    norm_at = offsets_of()[NORM_FFN][0]
+    second = unpack_lines(
+        buffers, 0, where, [flat_segment(name_key) for name_key in names] + [(norm_at, 16, LINE)], after
+    )
+    weights = dict(zip(names, second))
+    weights[NORM_FFN] = second[-1].reshape(-1)[norm_at % LINE : norm_at % LINE + D]
     return weights
 
 
-def fast_gradients(small, pairs):
+def pack_late(gate, up, down, ssm_low, grad_branch, grad_norm_ffn, after):
     places = offsets_of()
-    z, y, x, c = (lax.axis_index(name) for name in GRID)
-    ssm_low, grad_branch = pairs[W_SSM_OUT]
     out_at = places[W_SSM_OUT][0]
     lane = places[W_GATE][0] % LINE
     boundary = 2 * PLANE * LINE
     tail_from = (boundary - out_at) // D
     tail = matmul_left_t(ssm_low[:, tail_from:], grad_branch).reshape(-1)
     tail = tail[boundary - out_at - tail_from * D :]
-    head = jnp.concatenate([jnp.zeros((14 * LINE,), jnp.float32), tail, small[NORM_FFN]])
+    head = jnp.concatenate([jnp.zeros((14 * LINE,), jnp.float32), tail, grad_norm_ffn])
     head_rows = head.shape[0] // LINE
     carry = jnp.zeros((8, LINE), jnp.float32).at[7, :lane].set(head[head_rows * LINE :])
     head = head[: head_rows * LINE].reshape(head_rows, LINE).astype(jnp.bfloat16)
-    length = 2 * PLANE + 32
-    late = pack_lines(
-        None, length, head_rows,
-        [pairs[W_GATE], pairs[W_UP_PROJ], pairs[W_DOWN]],
-        lane, 0, [(head, 0)], carry, 48,
-    )
-    late_sum = reduce_lines(late, 1, 14)
+    return pack_lines(
+        None, 2 * PLANE + 32, head_rows, [gate, up, down], lane, 0, [(head, 0)], carry, 48, after
+    )
+
+
+def pack_out(ssm_low, grad_branch, after):
+    out_at = offsets_of()[W_SSM_OUT][0]
     first_row = (8 + out_at // LINE) // 16 * 16
-    early_rows = first_row + SSM_HEADS * SSM_DIM * D // LINE
-    early = pack_lines(
-        None, early_rows, first_row, [pairs[W_SSM_OUT]],
-        lane, (8 + out_at // LINE) % 8, [], jnp.zeros((8, LINE), jnp.float32), 0,
-    )
-    names = (W_STEP,) + small_names[1:-1]
-    misc = [small[name_key].reshape(-1) for name_key in names]
+    rows = first_row + SSM_HEADS * SSM_DIM * D // LINE
+    return pack_lines(
+        None, rows, first_row, [(ssm_low, grad_branch)], out_at % LINE, (8 + out_at // LINE) % 8, [],
+        jnp.zeros((8, LINE), jnp.float32), 0, after,
+    )
+
+
+def pack_ssm(target, segments, small, ssm_low, grad_branch, after):
+    places = offsets_of()
+    misc = [small[name_key].reshape(-1) for name_key in (W_STEP,) + small_names[1:-1]]
     count = sum(part.shape[0] for part in misc)
     misc_rows = (count // LINE + 16) // 16 * 16
     opening = matmul_left_t(ssm_low[:, :16], grad_branch).reshape(-1)
     misc = jnp.concatenate(misc + [opening[: misc_rows * LINE - count]])
     misc = misc.reshape(misc_rows, LINE).astype(jnp.bfloat16)
-    first = jnp.concatenate([jnp.zeros((8 * LINE,), jnp.float32), small[NORM_ATTN]])
-    first = first.reshape(16, LINE).astype(jnp.bfloat16)
-    early = pack_lines(
-        early, early_rows, 16,
-        [pairs[k] for k in (W_QUERY, W_KEY, W_VALUE, W_ATTN_OUT, W_GATE_SSM, W_X_SSM, W_B_C)],
-        0, 0, [(first, 0), (misc, 8 + places[W_STEP][0] // LINE)], None, 0,
-    )
-    early_sum = reduce_lines(early, 0, 8)
-    shard = SHARD * (4 * y + 2 * x + c)
+    first_row = 8 + places[W_ATTN_OUT][0] // LINE
+    return pack_lines(
+        target, target.shape[0], first_row, segments, 0, 0, [(misc, 8 + places[W_STEP][0] // LINE)], None, 0, after
+    )
+
+
+def pack_qkv(segments, attended, grad_branch, after):
+    places = offsets_of()
+    out_row = 8 + places[W_ATTN_OUT][0] // LINE
+    rows = (8 + SHARD) // 16 * 16 + 8 * PIECE
+    closing = matmul_left_t(attended[:, :16], grad_branch).reshape(-1, LINE)
+    closing = closing[: rows - out_row].astype(jnp.bfloat16)
+    return pack_lines(
+        None, rows, 16, segments, 0, 0, [(jnp.zeros((16, LINE), jnp.bfloat16), 0), (closing, out_row)], None, 0, after
+    )
+
+
+def own_lines(early, late, corner, grad_norm_attn):
+    z, y, x, c = (lax.axis_index(name) for name in GRID)
+    place = 4 * y + 2 * x + c
+    shard = SHARD * place
     start = jnp.where(z < 2, (8 + shard) % 16, (14 + shard) % 16)
-    lines = jnp.where(z < 2, early_sum, late_sum)
-    return lax.dynamic_slice(lines, (start, 0), (SHARD, LINE)).astype(jnp.float32).reshape(-1)
+    lines = jnp.where(z < 2, early, late)
+    lines = jnp.where((z == 0) & (place < 2), corner[:WIN], lines)
+    lines = lax.dynamic_slice(lines, (start, 0), (SHARD, LINE)).astype(jnp.float32)
+    norms = jnp.where((z == 0) & (place == 0), grad_norm_attn.reshape(-1, LINE), lines[: D // LINE])
+    return jnp.concatenate([norms, lines[D // LINE :]]).reshape(-1)
 
 
 def body(span, group, fast, tokens, params, cotangent, offsets):
@@ -1257,10 +1331,10 @@
     last_row = my_start + rows_dev - 1
     cosine, sine = rotary_tables(positions)
     if fast:
-        weights = fast_weights(params)
+        weights, held = early_weights(params)
     else:
         weights = unpack(lax.all_gather(params, group + span, axis=0, tiled=True))
-    small_f32 = {name_key: weights[name_key].astype(jnp.float32) for name_key in small_names}
+    small_f32 = {name_key: weights[name_key].astype(jnp.float32) for name_key in small_names[:-1]}
     x_rows = tokens.astype(jnp.float32)
     normed_one, norm_one_back = jax.vjp(rms_norm, x_rows, small_f32[NORM_ATTN])
     hidden = normed_one.astype(jnp.bfloat16)
@@ -1327,6 +1401,9 @@
     )
     normed_ssm, gnorm_back = jax.vjp(gated_norm, ssm_y, gate_ssm, small_f32[NORM_SSM])
     ssm_low = normed_ssm.astype(jnp.bfloat16)
+    if fast:
+        weights.update(late_weights(held, [mixed]))
+    small_f32[NORM_FFN] = weights[NORM_FFN].astype(jnp.float32)
     ssm_out = matmul(ssm_low, weights[W_SSM_OUT])
     middle = x_rows + attn_out + ssm_out
     normed_two, norm_two_back = jax.vjp(rms_norm, middle, small_f32[NORM_FFN])
@@ -1347,25 +1424,34 @@
     )
     totals = sum_all(squares, group + span, fast)
     stats = jnp.sqrt(totals / (all_rows * D))
-    back_weights = weights
     grad_out = cotangent.astype(jnp.float32)
-    grad_activation = matmul_right_t(cotangent, back_weights[W_DOWN])
+    grad_activation = matmul_right_t(cotangent, weights[W_DOWN])
     grad_gate_f32, grad_upper_f32 = swiglu_back(grad_activation)
     grad_gate = grad_gate_f32.astype(jnp.bfloat16)
     grad_upper = grad_upper_f32.astype(jnp.bfloat16)
-    grad_hidden_two = matmul_right_t(grad_gate, back_weights[W_GATE]) + matmul_right_t(
-        grad_upper, back_weights[W_UP_PROJ]
+    grad_hidden_two = matmul_right_t(grad_gate, weights[W_GATE]) + matmul_right_t(
+        grad_upper, weights[W_UP_PROJ]
     )
     grad_middle_norm, grad_norm_ffn = norm_two_back(grad_hidden_two)
     grad_middle = grad_out + grad_middle_norm
     grad_branch = grad_middle.astype(jnp.bfloat16)
-    grad_attended = matmul_right_t(grad_branch, back_weights[W_ATTN_OUT]).astype(jnp.bfloat16)
-    grad_ssm_low = matmul_right_t(grad_branch, back_weights[W_SSM_OUT])
+    grad_attended = matmul_right_t(grad_branch, weights[W_ATTN_OUT]).astype(jnp.bfloat16)
+    grad_ssm_low = matmul_right_t(grad_branch, weights[W_SSM_OUT])
     grad_ssm_y, grad_gate_ssm_f32, grad_norm_ssm = gnorm_back(grad_ssm_low)
     grad_state_local = weighted_state(c_in, grad_ssm_y, entry_rows)
+    pinned_by = ()
+    if fast:
+        late = pack_late(
+            (hidden_two, grad_gate), (hidden_two, grad_upper), (activation, cotangent),
+            ssm_low, grad_branch, grad_norm_ffn, [grad_state_local],
+        )
+        late_flow = Flow(reduce_stages(late, 1, 14))
+        early = pack_out(ssm_low, grad_branch, late_flow.values())
+        late_flow.go()
+        pinned_by = late_flow.values()
     grad_state_out = scan_states(carry_all, grad_state_local, span, fast, True)
     grad_x, grad_b, grad_c, grad_small = ssm_backward(
-        x_ssm, grad_ssm_y, b_in, c_in, chunk_cum, step_rows, state_in, grad_state_out, skip_wide, ssm_meta, start_row
+        x_ssm, grad_ssm_y, b_in, c_in, chunk_cum, step_rows, state_in, grad_state_out, skip_wide, ssm_meta, start_row, pinned_by
     )
     grad_conv_values = jnp.concatenate([grad_x, grad_b, grad_c], axis=1)
     grad_direct = grad_small[:, 0:2].reshape(SSM_HEADS, rows_dev)
@@ -1384,16 +1470,46 @@
     grad_step_raw = grad_step_raw_f32.astype(jnp.bfloat16)
     grad_w_step = matmul_left_t(hidden, grad_step_raw)
     grad_hidden_ssm = (
-        matmul_right_t(grad_gate_ssm, back_weights[W_GATE_SSM])
-        + matmul_right_t(grad_xbc[:, :ssm_inner], back_weights[W_X_SSM])
-        + matmul_right_t(grad_xbc[:, ssm_inner:], back_weights[W_B_C])
-        + matmul_right_t(grad_step_raw, back_weights[W_STEP])
-    )
+        matmul_right_t(grad_gate_ssm, weights[W_GATE_SSM])
+        + matmul_right_t(grad_xbc[:, :ssm_inner], weights[W_X_SSM])
+        + matmul_right_t(grad_xbc[:, ssm_inner:], weights[W_B_C])
+        + matmul_right_t(grad_step_raw, weights[W_STEP])
+    )
+    small = {
+        W_STEP: grad_w_step,
+        CONV_WEIGHT: grad_conv_weight,
+        CONV_BIAS: grad_conv_bias,
+        STEP_BIAS: grad_step_bias,
+        DECAY_LOG: grad_decay_log,
+        SKIP_GAIN: grad_skip_gain,
+        NORM_SSM: grad_norm_ssm,
+        NORM_FFN: grad_norm_ffn,
+    }
     g_low = grad_attended.reshape(rows_dev, HEADS_Q, HEAD_DIM).transpose(1, 0, 2)
     g_wide = jnp.pad(g_low, ((0, 0), (0, 0), (HEAD_DIM, 0)))
-    grad_kv, grad_q_turned = attention_backward(
-        q_wide, g_wide, key_blocks, logs, mixed, meta, start_row
-    )
+    if fast:
+        late_flow.go()
+        early = pack_ssm(
+            early,
+            [
+                (attended, grad_branch), (hidden, grad_gate_ssm),
+                (hidden, grad_xbc[:, :ssm_inner]), (hidden, grad_xbc[:, ssm_inner:]),
+            ],
+            small, ssm_low, grad_branch, late_flow.values(),
+        )
+        late_flow.go()
+        early_flow = Flow(reduce_stages(early, 0, 8))
+        pinned_by = late_flow.values() + early_flow.values()
+    parts = []
+    for group_at in range(HEADS_KV):
+        parts.append(
+            attention_backward(q_wide, g_wide, key_blocks, logs, mixed, meta, start_row, group_at, pinned_by)
+        )
+        if fast:
+            early_flow.go()
+            pinned_by = early_flow.values() + [parts[-1][1]]
+    grad_kv = jnp.concatenate([part[0] for part in parts], axis=1)
+    grad_q_turned = jnp.concatenate([part[1] for part in parts], axis=0)
     if rows_dev != KEYS:
         grad_kv = grad_kv.transpose(1, 0, 2, 3).reshape(HEADS_KV, -1, rows_dev, PAIR).transpose(1, 0, 2, 3)
     grad_kv_mine = scatter_span(grad_kv, span, fast)
@@ -1403,25 +1519,30 @@
     grad_query_low = rotate(grad_q_rot, cosine, -sine, HEADS_Q).astype(jnp.bfloat16)
     grad_key_low = rotate(grad_keys_mine, cosine, -sine, HEADS_KV).astype(jnp.bfloat16)
     grad_value_low = grad_values_mine.astype(jnp.bfloat16)
+    if fast:
+        corner = pack_qkv(
+            [(hidden, grad_query_low), (hidden, grad_key_low), (hidden, grad_value_low)],
+            attended, grad_branch, early_flow.values(),
+        )
+        early_flow.go()
+        late_flow.go()
+        corner_flow = Flow(corner_stages(corner))
+        for flow in (early_flow, late_flow, corner_flow):
+            while flow.sends:
+                flow.go()
     grad_hidden = (
         grad_hidden_ssm
-        + matmul_right_t(grad_query_low, back_weights[W_QUERY])
-        + matmul_right_t(grad_key_low, back_weights[W_KEY])
-        + matmul_right_t(grad_value_low, back_weights[W_VALUE])
+        + matmul_right_t(grad_query_low, weights[W_QUERY])
+        + matmul_right_t(grad_key_low, weights[W_KEY])
+        + matmul_right_t(grad_value_low, weights[W_VALUE])
     )
     grad_x_norm, grad_norm_attn = norm_one_back(grad_hidden)
     grad_tokens = grad_middle + grad_x_norm
-    small = {
-        NORM_ATTN: grad_norm_attn,
-        W_STEP: grad_w_step,
-        CONV_WEIGHT: grad_conv_weight,
-        CONV_BIAS: grad_conv_bias,
-        STEP_BIAS: grad_step_bias,
-        DECAY_LOG: grad_decay_log,
-        SKIP_GAIN: grad_skip_gain,
-        NORM_SSM: grad_norm_ssm,
-        NORM_FFN: grad_norm_ffn,
-    }
+    if fast:
+        norms = sum_all(grad_norm_attn, group + span, fast)
+        grad_shard = own_lines(early_flow.result, late_flow.result, corner_flow.result, norms)
+        return (result.astype(jnp.bfloat16), grad_tokens, grad_shard, stats)
+    small[NORM_ATTN] = grad_norm_attn
     pairs = {
         W_QUERY: (hidden, grad_query_low),
         W_KEY: (hidden, grad_key_low),
@@ -1435,8 +1556,6 @@
         W_UP_PROJ: (hidden_two, grad_upper),
         W_DOWN: (activation, cotangent),
     }
-    if fast:
-        return (result.astype(jnp.bfloat16), grad_tokens, fast_gradients(small, pairs), stats)
     grad_dict = dict(small)
     for name_key, (left, right) in pairs.items():
         grad_dict[name_key] = matmul_left_t(left, right)

time: 985 us -> 1050 us (1.066)
  waiting for transfers between devices: 229 us -> 267 us
  other arithmetic: 114 us -> 126 us
    ppermute x6, starting transfers between devices: 105 us -> 54.4 us  [scan_states(): lax.ppermute(packed.astype(jnp.bfloat16), name, SWAP).astype(jnp.float32)]
    ppermute x28 -> x36, starting transfers between devices: 64.7 us -> 106 us  [go(): lax.ppermute(value, axis, pairs)]
    ppermute x28 -> x36, waiting for transfers between devices: 105 us -> 131 us  [go(): lax.ppermute(value, axis, pairs)]
    ppermute x3 -> x6, waiting for transfers between devices: 26.7 us -> 1.98 us  [sum_all(): value = value + lax.ppermute(value, name, SWAP)]
    ppermute x3, waiting for transfers between devices: 4.92 us -> 27.7 us  [scatter_span(): lax.ppermute(send, name, SWAP).astype(jnp.float32)]
    ppermute x6, waiting for transfers between devices: 22.5 us -> 34.4 us  [scan_states(): lax.ppermute(packed.astype(jnp.bfloat16), name, SWAP).astype(jnp.float32)]
    unnamed x391 -> x415, local copies, waits for them, and re-layouts: 31.2 us -> 36.9 us
    convert_element_type x18 -> x14, other arithmetic: 16.1 us -> 21.1 us  [added(): return total.astype(jnp.bfloat16)]
  transfers between devices with their start and end apart: 92 -> 105, of which waited for: 27 -> 32; matrix products, arithmetic and copies ran while one was open for 23% -> 20% of each run, Pallas kernels for 17% -> 11%
where the time goes in v4:
time: 1050 us; the launch traced here: 1040 us
  starting transfers between devices  272 us (26%)
  waiting for transfers between devices  267 us (25%)
  Pallas kernels  181 us (17%)
  other arithmetic  126 us (12%)
  local copies, waits for them, and re-layouts  107 us (10%)
  matrix products  81.6 us (8%)
    ppermute x36, waiting for transfers between devices, go(): lax.ppermute(value, axis, pairs)  131 us
    ppermute x36, starting transfers between devices, go(): lax.ppermute(value, axis, pairs)  106 us
    ppermute x6, starting transfers between devices, scan_states(): lax.ppermute(packed.astype(jnp.bfloat16), name, SWAP).astype(jnp.float32)  54.4 us
    pallas_call x4, Pallas kernels, pack_lines(): pl.pallas_call(pinned(kernel, inputs, after), grid=(total,), in_specs=[le...  44.9 us
    dot_general x12, matrix products, matmul_right_t(): lax.dot_general(left, right, (((1,), (1,)), ((), ())), preferred_element_...  43 us
    pallas_call x2, Pallas kernels, unpack_lines(): pl.pallas_call(pinned(kernel, 2 + count_buffers, after), grid_spec=pltpu....  41.6 us
    pallas_call x1, Pallas kernels, ssm_backward(): pl.pallas_call(pinned(kernel, 11, after), grid_spec=pltpu.PrefetchScalarG...  40.4 us
    unnamed x415, local copies, waits for them, and re-layouts  36.9 us
  transfers between devices with their start and end apart: 105, of which 32 were waited for; matrix products, arithmetic and copies ran while one was open for 20% of the time, Pallas kernels for 11%

profile of v4, /device:TPU:0, one launch (start us, length us, event | category | flops | bytes accessed | tf_op | source)
XLA Modules:
  0.0 1040.3 jit_solution(5913080021998095987)
XLA Ops:
  1.9 7.7 collective-permute-start
  44.2 15.6 %collective-permute-done.32 = bf16[3088,128]{1,0:T(8,128)(2,1)} collective-permute-done((bf16[3088,128]{1,0:T(8,128)(2,1)S(1)}, bf16[3088,128]{1,0:T(8,128)(2,1)}, u32[]{:S(2)}, u32[]{:S(2)}) %collective-permute-start.32) | collective-permute-done | bytes 790560 | tf_op jit(solution)/shard_map/ppermute | solution.py:269
  74.9 11.9 %collective-permute-start.19 = (bf16[3088,128]{1,0:T(8,128)(2,1)}, bf16[3088,128]{1,0:T(8,128)(2,1)}, u32[]{:S(2)}, u32[]{:S(2)}) collective-permute-start(bf16[3088,128]{1,0:T(8,128)(2,1)} %get-tuple-element.168.refs_10_), channel_id=1, source_target_pairs={{0,1},{1,0},{2,3},{3,2},{4,5},{5,4},{6,7},{7,6},{8,9},{9,8},{10,11... | collective-permute-start | bytes 2371592 | tf_op jit(solution)/shard_map/ppermute | solution.py:280
  86.9 15.7 %collective-permute-done.5.refs_3_ = bf16[3088,128]{1,0:T(8,128)(2,1)S(1)} collective-permute-done((bf16[3088,128]{1,0:T(8,128)(2,1)S(1)}, bf16[3088,128]{1,0:T(8,128)(2,1)S(1)}, u32[]{:S(2)}, u32[]{:S(2)}) %collective-permute-start.5) | collective-permute-done | bytes 790560 | tf_op jit(solution)/shard_map/ppermute | solution.py:273
  132.7 5.9 collective-permute-start.45
  142.3 14.8 %unpack.2 = (bf16[1024,512]{1,0:T(8,128)(2,1)}, bf16[1024,128]{1,0:T(8,128)(2,1)S(1)}, bf16[1024,128]{1,0:T(8,128)(2,1)S(1)}, bf16[512,1024]{1,0:T(8,128)(2,1)},...) custom-call(s32[25,5]{1,0:T(8,128)S(1)} %copy-done.51, ...), custom_call_target="tpu_custom_call" | custom-call | bytes 26624000 | tf_op jit(solution)/shard_map/unpack/pallas_call | solution.py:421
  175.3 7.8 collective-permute-start.26
  198.8 9.3 state.2
  226.8 7.5 collective-permute-done.28
  251.3 8.6 ssm.1
  268.9 15.9 %collective-permute-done.47.refs_29_ = bf16[3088,128]{1,0:T(8,128)(2,1)} collective-permute-done((bf16[3088,128]{1,0:T(8,128)(2,1)}, bf16[3088,128]{1,0:T(8,128)(2,1)}, u32[]{:S(2)}, u32[]{:S(2)}) %collective-permute-start.47) | collective-permute-done | bytes 790560 | tf_op jit(solution)/shard_map/ppermute | solution.py:278
  292.1 9.4 attend.1
  307.1 26.8 %unpack.3 = (bf16[1536,1024]{1,0:T(8,128)(2,1)}, bf16[1024,2048]{1,0:T(8,128)(2,1)}, bf16[1024,2048]{1,0:T(8,128)(2,1)}, bf16[2048,1024]{1,0:T(8,128)(2,1)}, bf16[16,128]{1,0:T(8,128)(2,1)S(1)}) custom-call(s32[31,5]{1,0:T(8,128)S(1)} %copy-done.50, s32[32]{0:T(128)S(1)} %fusion.71.refs_1_, bf16[3088,128]{1,0:T(8,128)(2,1)S(1)} %get-tuple-element.170.refs_2_, ...), custom_call_target="tpu_custom_call" | custom-call | bytes 33013760 | tf_op jit(solution)/shard_map/unpack/pallas_call | solution.py:421
  348.4 6.7 fusion.2
  355.2 6.9 fusion.100
  376.4 7.2 fusion.27
  383.6 9.5 state.3.refs_7_
  393.1 6.5 pad_maximum_fusion.2
  399.6 20.6 %pack.4 = bf16[49344,128]{1,0:T(8,128)(2,1)} custom-call(bf16[512,1024]{1,0:T(8,128)(2,1)S(1)} %copy-done.40, bf16[512,2048]{1,0:T(8,128)(2,1)S(1)} %copy-done.53, bf16[512,2048]{1,0:T(8,128)(2,1)} %get-tuple-element.208.refs_2_, bf16[512,2048]{1,0:T(8,128)(2,1)} %get-tuple-element.209.refs_3_, bf16[512,1024]{1,0:T(8,128)(2,1)S(1)} %copy-done.38, ...), custom_call_target="tpu_custom_call" | custom-call | flops 6442450944 | bytes 16777216 | tf_op jit(solution)/shard_map/pack/pallas_call | solution.py:576
  420.2 5.9 constant_dynamic-slice_fusion.4.refs_3_
  426.2 8.4 collective-permute-start.55
  434.7 8.4 collective-permute-done.52
  445.1 15.5 %collective-permute-start.53 = (bf16[144,1536]{1,0:T(8,128)(2,1)}, bf16[144,1536]{1,0:T(8,128)(2,1)}, u32[]{:S(2)}, u32[]{:S(2)}) collective-permute-start(bf16[144,1536]{1,0:T(8,128)(2,1)} %pad_maximum_fusion.19), channel_id=1, source_target_pairs={{0,2},{2,0},{1,3},{3,1},{4,6},{6,4},{5,7},{7,5},{8,10},{10,8},{9,1... | collective-permute-start | bytes 1327112 | tf_op jit(solution)/shard_map/ppermute | solution.py:980
  462.8 8.6 collective-permute-done.53
  475.8 36.0 %collective-permute-start.54 = (bf16[144,1536]{1,0:T(8,128)(2,1)S(1)}, bf16[144,1536]{1,0:T(8,128)(2,1)S(1)}, u32[]{:S(2)}, u32[]{:S(2)}) collective-permute-start(bf16[144,1536]{1,0:T(8,128)(2,1)S(1)} %pad_maximum_fusion.20), channel_id=1, source_target_pairs={{0,4},{4,0},{1,5},{5,1},{2,6},{6,2},{3,7},{7,3},{8,12},{12,8},{9,1... | collective-permute-start | bytes 1327112 | tf_op jit(solution)/shard_map/ppermute | solution.py:980
  522.0 5.8 add_convert_fusion.1
  535.5 40.4 %ssm_back.1 = (f32[512,1536]{1,0:T(8,128)S(1)}, f32[512,128]{1,0:T(8,128)S(1)}, f32[512,128]{1,0:T(8,128)S(1)}, f32[12,8,512]{2,1,0:T(8,128)S(1)}) custom-call(s32[5]{0:T(128)S(1)} %pad_add_fusion.3.meta_ref.refs_0_, f32[512,1536]{1,0:T(8,128)S(1)} %copy-done.1, f32[512,1536]{1,0:T(8,128)} %get-tuple-element.119.refs_1_.refs_2_, f32[512,128]{1,0:T(8,128)S(1)} %copy-done.13, ...), custom_call_target="tpu_custom_call" | custom-call | flops 3000000000 | bytes 9437184 | tf_op jit(solution)/shard_map/ssm_back/pallas_call | solution.py:920
  581.7 7.0 multiply_reduce_fusion.2
  615.5 14.2 %pack.6 = bf16[49440,128]{1,0:T(8,128)(2,1)} custom-call(bf16[512,512]{1,0:T(8,128)(2,1)S(1)} %bitcast.256, bf16[512,1024]{1,0:T(8,128)(2,1)S(1)} %fusion.15.refs_1_.refs_0_, bf16[512,1024]{1,0:T(8,128)(2,1)S(1)} %fusion.80.refs_2_, bf16[512,1536]{1,0:T(8,128)(2,1)S(1)} %copy-done.8, ...), custom_call_target="tpu_custom_call", output_to_operand_aliasing={{}: (7, {})} | custom-call | flops 4026531840 | bytes 11010048 | tf_op jit(solution)/shard_map/pack/pallas_call | solution.py:576
  629.7 5.9 constant_dynamic-slice_fusion.3.refs_13_
  650.2 5.5 fusion.101
  662.5 7.1 collective-permute-done.60
  669.8 11.5 %collective-permute-done.58 = bf16[3104,128]{1,0:T(8,128)(2,1)S(1)} collective-permute-done((bf16[3104,128]{1,0:T(8,128)(2,1)S(1)}, bf16[3104,128]{1,0:T(8,128)(2,1)S(1)}, u32[]{:S(2)}, u32[]{:S(2)}) %collective-permute-start.58) | collective-permute-done | bytes 794656 | tf_op jit(solution)/shard_map/ppermute | solution.py:619
  681.5 8.7 attend_back.2
  690.3 6.0 add_convert_fusion
  701.1 8.5 attend_back.3
  714.2 5.9 collective-permute-start.62
  728.0 13.3 %collective-permute-start.71 = (bf16[2,3104,128]{2,1,0:T(8,128)(2,1)}, bf16[2,3104,128]{2,1,0:T(8,128)(2,1)}, u32[]{:S(2)}, u32[]{:S(2)}) collective-permute-start(bf16[2,3104,128]{2,1,0:T(8,128)(2,1)} %pad_maximum_fusion.8.refs_8_), channel_id=1, source_target_pairs={{0,2},{2,0},{1,3},{3,1},{4,6},{6,4},{5,7},{7,5},{8,10},{10,8},{9,1... | collective-permute-start | bytes 4767752 | tf_op jit(solution)/shard_map/ppermute | solution.py:619
  741.4 27.9 %collective-permute-start.70 = (bf16[2,3104,128]{2,1,0:T(8,128)(2,1)}, bf16[2,3104,128]{2,1,0:T(8,128)(2,1)}, u32[]{:S(2)}, u32[]{:S(2)}) collective-permute-start(bf16[2,3104,128]{2,1,0:T(8,128)(2,1)} %pad_maximum_fusion.7.refs_7_), channel_id=1, source_target_pairs={{0,4},{4,0},{1,5},{5,1},{2,6},{6,2},{3,7},{7,3},{8,12},{12,8},{9,1... | collective-permute-start | bytes 4767752 | tf_op jit(solution)/shard_map/ppermute | solution.py:619
  789.8 25.8 %collective-permute-done.63 = bf16[2,2,512,128]{2,3,1,0:T(8,128)(2,1)} collective-permute-done((bf16[2,2,512,128]{2,3,1,0:T(8,128)(2,1)}, bf16[2,2,512,128]{2,3,1,0:T(8,128)(2,1)}, u32[]{:S(2)}, u32[]{:S(2)}) %collective-permute-start.63) | collective-permute-done | bytes 524320 | tf_op jit(solution)/shard_map/ppermute | solution.py:1198
  862.6 18.7 %collective-permute-done.75 = bf16[2,400,128]{2,1,0:T(8,128)(2,1)S(1)} collective-permute-done((bf16[2,400,128]{2,1,0:T(8,128)(2,1)S(1)}, bf16[2,400,128]{2,1,0:T(8,128)(2,1)S(1)}, u32[]{:S(2)}, u32[]{:S(2)}) %collective-permute-start.75) | collective-permute-done | bytes 204832 | tf_op jit(solution)/shard_map/ppermute | solution.py:619
  900.8 11.2 %collective-permute-done.94 = bf16[3104,128]{1,0:T(8,128)(2,1)S(1)} collective-permute-done((bf16[3104,128]{1,0:T(8,128)(2,1)S(1)}, bf16[3104,128]{1,0:T(8,128)(2,1)S(1)}, u32[]{:S(2)}, u32[]{:S(2)}) %collective-permute-start.94) | collective-permute-done | bytes 794656 | tf_op jit(solution)/shard_map/ppermute | solution.py:619
  917.4 32.5 %collective-permute-done.77 = bf16[2,400,128]{2,1,0:T(8,128)(2,1)S(1)} collective-permute-done((bf16[2,400,128]{2,1,0:T(8,128)(2,1)S(1)}, bf16[2,400,128]{2,1,0:T(8,128)(2,1)S(1)}, u32[]{:S(2)}, u32[]{:S(2)}) %collective-permute-start.77) | collective-permute-done | bytes 204832 | tf_op jit(solution)/shard_map/ppermute | solution.py:619
  951.3 19.5 %collective-permute-done.78 = bf16[2,400,128]{2,1,0:T(8,128)(2,1)S(1)} collective-permute-done((bf16[2,400,128]{2,1,0:T(8,128)(2,1)S(1)}, bf16[2,400,128]{2,1,0:T(8,128)(2,1)S(1)}, u32[]{:S(2)}, u32[]{:S(2)}) %collective-permute-start.78) | collective-permute-done | bytes 204832 | tf_op jit(solution)/shard_map/ppermute | solution.py:619
  976.1 18.1 %collective-permute-done.90 = bf16[3104,128]{1,0:T(8,128)(2,1)S(1)} collective-permute-done((bf16[3104,128]{1,0:T(8,128)(2,1)S(1)}, bf16[3104,128]{1,0:T(8,128)(2,1)S(1)}, u32[]{:S(2)}, u32[]{:S(2)}) %collective-permute-start.90) | collective-permute-done | bytes 794656 | tf_op jit(solution)/shard_map/ppermute | solution.py:619
  997.6 10.0 collective-permute-done.85
  1013.5 7.8 collective-permute-start.92
  1021.4 6.1 collective-permute-start.81
  (859 shorter events, 419.7 us)
Async XLA Ops:
  30.3 29.6 %collective-permute-start.32 = (bf16[3088,128]{1,0:T(8,128)(2,1)S(1)}, bf16[3088,128]{1,0:T(8,128)(2,1)}, u32[]{:S(2)}, u32[]{:S(2)}) collective-permute-start(bf16[3088,128]{1,0:T(8,128)(2,1)S(1)} %collective-permute-done.30), channel_id=1, source_target_pairs={{8,0},{17,9},{10,2},{19,11},{12,4},{21,13},{14,6},{23,15}} | collective-permute-start | bytes 2371592 | tf_op jit(solution)/shard_map/ppermute | solution.py:269
  34.3 26.2 %collective-permute-start.3 = (bf16[3088,128]{1,0:T(8,128)(2,1)S(1)}, bf16[3088,128]{1,0:T(8,128)(2,1)}, u32[]{:S(2)}, u32[]{:S(2)}) collective-permute-start(bf16[3088,128]{1,0:T(8,128)(2,1)S(1)} %collective-permute-done.1), channel_id=1, source_target_pairs={{8,16},{17,25},{10,18},{19,27},{12,20},{21,29},{14,22},{23,31}} | collective-permute-start | bytes 2371592 | tf_op jit(solution)/shard_map/ppermute | solution.py:264
  35.9 25.4 %collective-permute-start.15 = (bf16[3088,128]{1,0:T(8,128)(2,1)}, bf16[3088,128]{1,0:T(8,128)(2,1)}, u32[]{:S(2)}, u32[]{:S(2)}) collective-permute-start(bf16[3088,128]{1,0:T(8,128)(2,1)} %collective-permute-done.14), channel_id=1, source_target_pairs={{16,24},{18,26},{20,28},{22,30}} | collective-permute-start | bytes 2371592 | tf_op jit(solution)/shard_map/ppermute | solution.py:265
  43.5 24.2 %collective-permute-start.2 = (bf16[3088,128]{1,0:T(8,128)(2,1)S(1)}, bf16[3088,128]{1,0:T(8,128)(2,1)S(1)}, u32[]{:S(2)}, u32[]{:S(2)}) collective-permute-start(bf16[3088,128]{1,0:T(8,128)(2,1)S(1)} %get-tuple-element.158), channel_id=1, source_target_pairs={{9,1},{11,3},{13,5},{15,7}} | collective-permute-start | bytes 2371592 | tf_op jit(solution)/shard_map/ppermute | solution.py:263
  66.3 20.6 %collective-permute-start.17 = (bf16[3088,128]{1,0:T(8,128)(2,1)}, bf16[3088,128]{1,0:T(8,128)(2,1)}, u32[]{:S(2)}, u32[]{:S(2)}) collective-permute-start(bf16[3088,128]{1,0:T(8,128)(2,1)} %get-tuple-element.168.refs_10_), channel_id=1, source_target_pairs={{0,4},{4,0},{1,5},{5,1},{2,6},{6,2},{3,7},{7,3},{8,12},{12,8},{9,1... | collective-permute-start | bytes 2371592 | tf_op jit(solution)/shard_map/ppermute | solution.py:274
  67.7 36.3 %collective-permute-start.16 = (bf16[3088,128]{1,0:T(8,128)(2,1)}, bf16[3088,128]{1,0:T(8,128)(2,1)S(1)}, u32[]{:S(2)}, u32[]{:S(2)}) collective-permute-start(bf16[3088,128]{1,0:T(8,128)(2,1)} %get-tuple-element.168.refs_10_), channel_id=1, source_target_pairs={{0,2},{2,0},{1,3},{3,1},{4,6},{6,4},{5,7},{7,5},{8,10},{10,8},{9,1... | collective-permute-start | bytes 2371592 | tf_op jit(solution)/shard_map/ppermute | solution.py:273
  72.0 30.5 %collective-permute-start.5 = (bf16[3088,128]{1,0:T(8,128)(2,1)S(1)}, bf16[3088,128]{1,0:T(8,128)(2,1)S(1)}, u32[]{:S(2)}, u32[]{:S(2)}) collective-permute-start(bf16[3088,128]{1,0:T(8,128)(2,1)S(1)} %get-tuple-element.170.refs_2_), channel_id=1, source_target_pairs={{0,2},{2,0},{1,3},{3,1},{4,6},{6,4},{5,7},{7,5},{8,10},{10,8},{9,1... | collective-permute-start | bytes 2371592 | tf_op jit(solution)/shard_map/ppermute | solution.py:273
  72.6 33.8 %collective-permute-start.6 = (bf16[3088,128]{1,0:T(8,128)(2,1)S(1)}, bf16[3088,128]{1,0:T(8,128)(2,1)S(1)}, u32[]{:S(2)}, u32[]{:S(2)}) collective-permute-start(bf16[3088,128]{1,0:T(8,128)(2,1)S(1)} %get-tuple-element.170.refs_2_), channel_id=1, source_target_pairs={{0,4},{4,0},{1,5},{5,1},{2,6},{6,2},{3,7},{7,3},{8,12},{12,8},{9,1... | collective-permute-start | bytes 2371592 | tf_op jit(solution)/shard_map/ppermute | solution.py:274
  74.9 44.8 %collective-permute-start.19 = (bf16[3088,128]{1,0:T(8,128)(2,1)}, bf16[3088,128]{1,0:T(8,128)(2,1)}, u32[]{:S(2)}, u32[]{:S(2)}) collective-permute-start(bf16[3088,128]{1,0:T(8,128)(2,1)} %get-tuple-element.168.refs_10_), channel_id=1, source_target_pairs={{0,1},{1,0},{2,3},{3,2},{4,5},{5,4},{6,7},{7,6},{8,9},{9,8},{10,11... | collective-permute-start | bytes 2371592 | tf_op jit(solution)/shard_map/ppermute | solution.py:280
  86.9 33.3 %collective-permute-start.8 = (bf16[3088,128]{1,0:T(8,128)(2,1)S(1)}, bf16[3088,128]{1,0:T(8,128)(2,1)S(1)}, u32[]{:S(2)}, u32[]{:S(2)}) collective-permute-start(bf16[3088,128]{1,0:T(8,128)(2,1)S(1)} %get-tuple-element.170.refs_2_), channel_id=1, source_target_pairs={{0,1},{1,0},{2,3},{3,2},{4,5},{5,4},{6,7},{7,6},{8,9},{9,8},{10,11... | collective-permute-start | bytes 2371592 | tf_op jit(solution)/shard_map/ppermute | solution.py:280
  104.0 22.9 %collective-permute-start.21 = (bf16[3088,128]{1,0:T(8,128)(2,1)}, bf16[3088,128]{1,0:T(8,128)(2,1)}, u32[]{:S(2)}, u32[]{:S(2)}) collective-permute-start(bf16[3088,128]{1,0:T(8,128)(2,1)} %collective-permute-done.17.refs_12_), channel_id=1, source_target_pairs={{0,1},{1,0},{2,3},{3,2},{4,5},{5,4},{6,7},{7,6},{8,9},{9,8},{10,11... | collective-permute-start | bytes 2371592 | tf_op jit(solution)/shard_map/ppermute | solution.py:280
  128.9 134.9 %collective-permute-start.46 = (bf16[3088,128]{1,0:T(8,128)(2,1)}, bf16[3088,128]{1,0:T(8,128)(2,1)}, u32[]{:S(2)}, u32[]{:S(2)}) collective-permute-start(bf16[3088,128]{1,0:T(8,128)(2,1)} %get-tuple-element.167.refs_26_), channel_id=1, source_target_pairs={{0,4},{4,0},{1,5},{5,1},{2,6},{6,2},{3,7},{7,3},{8,12},{12,8},{9,1... | collective-permute-start | bytes 2371592 | tf_op jit(solution)/shard_map/ppermute | solution.py:274
  132.7 131.8 %collective-permute-start.45 = (bf16[3088,128]{1,0:T(8,128)(2,1)}, bf16[3088,128]{1,0:T(8,128)(2,1)}, u32[]{:S(2)}, u32[]{:S(2)}) collective-permute-start(bf16[3088,128]{1,0:T(8,128)(2,1)} %get-tuple-element.167.refs_26_), channel_id=1, source_target_pairs={{0,2},{2,0},{1,3},{3,1},{4,6},{6,4},{5,7},{7,5},{8,10},{10,8},{9,1... | collective-permute-start | bytes 2371592 | tf_op jit(solution)/shard_map/ppermute | solution.py:273
  138.6 125.8 %collective-permute-start.34 = (bf16[3088,128]{1,0:T(8,128)(2,1)}, bf16[3088,128]{1,0:T(8,128)(2,1)}, u32[]{:S(2)}, u32[]{:S(2)}) collective-permute-start(bf16[3088,128]{1,0:T(8,128)(2,1)} %get-tuple-element.169.refs_18_), channel_id=1, source_target_pairs={{0,2},{2,0},{1,3},{3,1},{4,6},{6,4},{5,7},{7,5},{8,10},{10,8},{9,1... | collective-permute-start | bytes 2371592 | tf_op jit(solution)/shard_map/ppermute | solution.py:273
  164.7 58.6 %collective-permute-start.23 = (bf16[2,512,128]{2,1,0:T(8,128)(2,1)}, bf16[2,512,128]{2,1,0:T(8,128)(2,1)}, u32[]{:S(2)}, u32[]{:S(2)}) collective-permute-start(bf16[2,512,128]{2,1,0:T(8,128)(2,1)} %maximum_bitcast_fusion.1), channel_id=1, source_target_pairs={{0,2},{2,0},{1,3},{3,1},{4,6},{6,4},{5,7},{7,5},{8,10},{10,8},{9,1... | collective-permute-start | bytes 786440 | tf_op jit(solution)/shard_map/ppermute | solution.py:1184
  242.4 23.7 %collective-permute-start.35 = (bf16[3088,128]{1,0:T(8,128)(2,1)}, bf16[3088,128]{1,0:T(8,128)(2,1)}, u32[]{:S(2)}, u32[]{:S(2)}) collective-permute-start(bf16[3088,128]{1,0:T(8,128)(2,1)} %get-tuple-element.169.refs_18_), channel_id=1, source_target_pairs={{0,4},{4,0},{1,5},{5,1},{2,6},{6,2},{3,7},{7,3},{8,12},{12,8},{9,1... | collective-permute-start | bytes 2371592 | tf_op jit(solution)/shard_map/ppermute | solution.py:274
  266.1 25.0 %collective-permute-start.50 = (bf16[3088,128]{1,0:T(8,128)(2,1)}, bf16[3088,128]{1,0:T(8,128)(2,1)S(1)}, u32[]{:S(2)}, u32[]{:S(2)}) collective-permute-start(bf16[3088,128]{1,0:T(8,128)(2,1)} %collective-permute-done.46.refs_28_), channel_id=1, source_target_pairs={{0,1},{1,0},{2,3},{3,2},{4,5},{5,4},{6,7},{7,6},{8,9},{9,8},{10,11... | collective-permute-start | bytes 2371592 | tf_op jit(solution)/shard_map/ppermute | solution.py:280
  268.3 37.6 %collective-permute-start.38 = (bf16[3088,128]{1,0:T(8,128)(2,1)}, bf16[3088,128]{1,0:T(8,128)(2,1)S(1)}, u32[]{:S(2)}, u32[]{:S(2)}) collective-permute-start(bf16[3088,128]{1,0:T(8,128)(2,1)} %collective-permute-done.34.refs_19_), channel_id=1, source_target_pairs={{0,1},{1,0},{2,3},{3,2},{4,5},{5,4},{6,7},{7,6},{8,9},{9,8},{10,11... | collective-permute-start | bytes 2371592 | tf_op jit(solution)/shard_map/ppermute | solution.py:280
  268.6 37.3 %collective-permute-start.49 = (bf16[3088,128]{1,0:T(8,128)(2,1)}, bf16[3088,128]{1,0:T(8,128)(2,1)S(1)}, u32[]{:S(2)}, u32[]{:S(2)}) collective-permute-start(bf16[3088,128]{1,0:T(8,128)(2,1)} %collective-permute-done.45.refs_27_), channel_id=1, source_target_pairs={{0,1},{1,0},{2,3},{3,2},{4,5},{5,4},{6,7},{7,6},{8,9},{9,8},{10,11... | collective-permute-start | bytes 2371592 | tf_op jit(solution)/shard_map/ppermute | solution.py:280
  284.8 21.2 %collective-permute-start.39 = (bf16[3088,128]{1,0:T(8,128)(2,1)}, bf16[3088,128]{1,0:T(8,128)(2,1)}, u32[]{:S(2)}, u32[]{:S(2)}) collective-permute-start(bf16[3088,128]{1,0:T(8,128)(2,1)} %collective-permute-done.35.refs_20_), channel_id=1, source_target_pairs={{0,1},{1,0},{2,3},{3,2},{4,5},{5,4},{6,7},{7,6},{8,9},{9,8},{10,11... | collective-permute-start | bytes 2371592 | tf_op jit(solution)/shard_map/ppermute | solution.py:280
  426.2 95.8 %collective-permute-start.55 = (bf16[24688,128]{1,0:T(8,128)(2,1)}, bf16[24688,128]{1,0:T(8,128)(2,1)}, u32[]{:S(2)}, u32[]{:S(2)}) collective-permute-start(bf16[24688,128]{1,0:T(8,128)(2,1)} %constant_dynamic-slice_fusion.4.refs_3_), channel_id=1, source_target_pairs={{0,1},{1,0},{2,3},{3,2},{4,5},{5,4},{6,7},{7,6},{8,9},{9,8},{10,11... | collective-permute-start | bytes 18960392 | tf_op jit(solution)/shard_map/ppermute | solution.py:619
  445.1 26.3 %collective-permute-start.53 = (bf16[144,1536]{1,0:T(8,128)(2,1)}, bf16[144,1536]{1,0:T(8,128)(2,1)}, u32[]{:S(2)}, u32[]{:S(2)}) collective-permute-start(bf16[144,1536]{1,0:T(8,128)(2,1)} %pad_maximum_fusion.19), channel_id=1, source_target_pairs={{0,2},{2,0},{1,3},{3,1},{4,6},{6,4},{5,7},{7,5},{8,10},{10,8},{9,1... | collective-permute-start | bytes 1327112 | tf_op jit(solution)/shard_map/ppermute | solution.py:980
  475.8 45.9 %collective-permute-start.54 = (bf16[144,1536]{1,0:T(8,128)(2,1)S(1)}, bf16[144,1536]{1,0:T(8,128)(2,1)S(1)}, u32[]{:S(2)}, u32[]{:S(2)}) collective-permute-start(bf16[144,1536]{1,0:T(8,128)(2,1)S(1)} %pad_maximum_fusion.20), channel_id=1, source_target_pairs={{0,4},{4,0},{1,5},{5,1},{2,6},{6,2},{3,7},{7,3},{8,12},{12,8},{9,1... | collective-permute-start | bytes 1327112 | tf_op jit(solution)/shard_map/ppermute | solution.py:980
  531.1 79.8 %collective-permute-start.59 = (bf16[2,3104,128]{2,1,0:T(8,128)(2,1)}, bf16[2,3104,128]{2,1,0:T(8,128)(2,1)}, u32[]{:S(2)}, u32[]{:S(2)}) collective-permute-start(bf16[2,3104,128]{2,1,0:T(8,128)(2,1)} %pad_maximum_fusion.6.refs_12_), channel_id=1, source_target_pairs={{0,2},{2,0},{1,3},{3,1},{4,6},{6,4},{5,7},{7,5},{8,10},{10,8},{9,1... | collective-permute-start | bytes 4767752 | tf_op jit(solution)/shard_map/ppermute | solution.py:619
  533.8 79.2 %collective-permute-start.57 = (bf16[2,3104,128]{2,1,0:T(8,128)(2,1)}, bf16[2,3104,128]{2,1,0:T(8,128)(2,1)}, u32[]{:S(2)}, u32[]{:S(2)}) collective-permute-start(bf16[2,3104,128]{2,1,0:T(8,128)(2,1)} %pad_maximum_fusion.5.refs_11_), channel_id=1, source_target_pairs={{0,4},{4,0},{1,5},{5,1},{2,6},{6,2},{3,7},{7,3},{8,12},{12,8},{9,1... | collective-permute-start | bytes 4767752 | tf_op jit(solution)/shard_map/ppermute | solution.py:619
  635.7 54.6 %collective-permute-start.61 = (bf16[24688,128]{1,0:T(8,128)(2,1)}, bf16[24688,128]{1,0:T(8,128)(2,1)}, u32[]{:S(2)}, u32[]{:S(2)}) collective-permute-start(bf16[24688,128]{1,0:T(8,128)(2,1)} %constant_dynamic-slice_fusion.3.refs_13_), channel_id=1, source_target_pairs={{0,1},{1,0},{2,3},{3,2},{4,5},{5,4},{6,7},{7,6},{8,9},{9,8},{10,11... | collective-permute-start | bytes 18960392 | tf_op jit(solution)/shard_map/ppermute | solution.py:619
  658.5 188.3 %collective-permute-start.101 = (f32[4]{0:T(128)S(1)}, f32[4]{0:T(128)S(1)}, u32[]{:S(2)}, u32[]{:S(2)}) collective-permute-start(f32[4]{0:T(128)S(1)} %fusion.157), channel_id=1, source_target_pairs={{0,2},{2,0},{1,3},{3,1},{4,6},{6,4},{5,7},{7,5},{8,10},{10,8},{9,1... | collective-permute-start | bytes 56 | tf_op jit(solution)/shard_map/ppermute | solution.py:1208
  714.2 63.5 %collective-permute-start.62 = (bf16[2,2,2,512,128]{3,4,2,1,0:T(8,128)(2,1)}, bf16[2,2,2,512,128]{3,4,2,1,0:T(8,128)(2,1)}, u32[]{:S(2)}, u32[]{:S(2)}) collective-permute-start(bf16[2,2,2,512,128]{3,4,2,1,0:T(8,128)(2,1)} %bitcast.287), channel_id=1, source_target_pairs={{0,1},{1,0},{2,3},{3,2},{4,5},{5,4},{6,7},{7,6},{8,9},{9,8},{10,11... | collective-permute-start | bytes 3145736 | tf_op jit(solution)/shard_map/ppermute | solution.py:1198
  728.0 89.1 %collective-permute-start.71 = (bf16[2,3104,128]{2,1,0:T(8,128)(2,1)}, bf16[2,3104,128]{2,1,0:T(8,128)(2,1)}, u32[]{:S(2)}, u32[]{:S(2)}) collective-permute-start(bf16[2,3104,128]{2,1,0:T(8,128)(2,1)} %pad_maximum_fusion.8.refs_8_), channel_id=1, source_target_pairs={{0,2},{2,0},{1,3},{3,1},{4,6},{6,4},{5,7},{7,5},{8,10},{10,8},{9,1... | collective-permute-start | bytes 4767752 | tf_op jit(solution)/shard_map/ppermute | solution.py:619
  741.4 78.7 %collective-permute-start.70 = (bf16[2,3104,128]{2,1,0:T(8,128)(2,1)}, bf16[2,3104,128]{2,1,0:T(8,128)(2,1)}, u32[]{:S(2)}, u32[]{:S(2)}) collective-permute-start(bf16[2,3104,128]{2,1,0:T(8,128)(2,1)} %pad_maximum_fusion.7.refs_7_), channel_id=1, source_target_pairs={{0,4},{4,0},{1,5},{5,1},{2,6},{6,2},{3,7},{7,3},{8,12},{12,8},{9,1... | collective-permute-start | bytes 4767752 | tf_op jit(solution)/shard_map/ppermute | solution.py:619
  781.6 34.0 %collective-permute-start.63 = (bf16[2,2,512,128]{2,3,1,0:T(8,128)(2,1)}, bf16[2,2,512,128]{2,3,1,0:T(8,128)(2,1)}, u32[]{:S(2)}, u32[]{:S(2)}) collective-permute-start(bf16[2,2,512,128]{2,3,1,0:T(8,128)(2,1)} %dynamic-slice_bitcast_fusion.20), channel_id=1, source_target_pairs={{0,4},{4,0},{1,5},{5,1},{2,6},{6,2},{3,7},{7,3},{8,12},{12,8},{9,1... | collective-permute-start | bytes 1572872 | tf_op jit(solution)/shard_map/ppermute | solution.py:1198
  854.1 29.3 %collective-permute-start.104 = (f32[4]{0:T(128)S(1)}, f32[4]{0:T(128)S(1)}, u32[]{:S(2)}, u32[]{:S(2)}) collective-permute-start(f32[4]{0:T(128)S(1)} %add.813), channel_id=1, source_target_pairs={{0,16},{16,0},{8,24},{24,8},{1,17},{17,1},{9,25},{25,9},{2,18},{18... | collective-permute-start | bytes 56 | tf_op jit(solution)/shard_map/ppermute | solution.py:1210
  856.5 30.9 %collective-permute-start.96 = (bf16[3104,128]{1,0:T(8,128)(2,1)S(1)}, bf16[3104,128]{1,0:T(8,128)(2,1)S(1)}, u32[]{:S(2)}, u32[]{:S(2)}) collective-permute-start(bf16[3104,128]{1,0:T(8,128)(2,1)S(1)} %fusion.25.refs_10_.refs_11_.refs_12_), channel_id=1, source_target_pairs={{8,16},{17,25},{10,18},{19,27},{12,20},{21,29},{14,22},{23,31}} | collective-permute-start | bytes 2383880 | tf_op jit(solution)/shard_map/ppermute | solution.py:619
  857.2 31.0 %collective-permute-start.97 = (bf16[3104,128]{1,0:T(8,128)(2,1)S(1)}, bf16[3104,128]{1,0:T(8,128)(2,1)S(1)}, u32[]{:S(2)}, u32[]{:S(2)}) collective-permute-start(bf16[3104,128]{1,0:T(8,128)(2,1)S(1)} %fusion.25.refs_10_.refs_11_.refs_12_), channel_id=1, source_target_pairs={{0,16},{9,25},{2,18},{11,27},{4,20},{13,29},{6,22},{15,31}} | collective-permute-start | bytes 2383880 | tf_op jit(solution)/shard_map/ppermute | solution.py:619
  860.3 28.6 %collective-permute-start.88 = (bf16[3104,128]{1,0:T(8,128)(2,1)S(1)}, bf16[3104,128]{1,0:T(8,128)(2,1)S(1)}, u32[]{:S(2)}, u32[]{:S(2)}) collective-permute-start(bf16[3104,128]{1,0:T(8,128)(2,1)S(1)} %copy-done.14), channel_id=1, source_target_pairs={{0,4},{4,0},{1,5},{5,1},{2,6},{6,2},{3,7},{7,3},{8,12},{12,8},{9,1... | collective-permute-start | bytes 2383880 | tf_op jit(solution)/shard_map/ppermute | solution.py:619
  888.9 23.1 %collective-permute-start.94 = (bf16[3104,128]{1,0:T(8,128)(2,1)S(1)}, bf16[3104,128]{1,0:T(8,128)(2,1)S(1)}, u32[]{:S(2)}, u32[]{:S(2)}) collective-permute-start(bf16[3104,128]{1,0:T(8,128)(2,1)S(1)} %fusion.26.refs_7_.refs_8_.refs_9_), channel_id=1, source_target_pairs={{0,16},{9,25},{2,18},{11,27},{4,20},{13,29},{6,22},{15,31}} | collective-permute-start | bytes 2383880 | tf_op jit(solution)/shard_map/ppermute | solution.py:619
  899.5 73.9 %collective-permute-start.89 = (bf16[3104,128]{1,0:T(8,128)(2,1)S(1)}, bf16[3104,128]{1,0:T(8,128)(2,1)S(1)}, u32[]{:S(2)}, u32[]{:S(2)}) collective-permute-start(bf16[3104,128]{1,0:T(8,128)(2,1)S(1)} %fusion.23), channel_id=1, source_target_pairs={{8,0},{17,9},{10,2},{19,11},{12,4},{21,13},{14,6},{23,15}} | collective-permute-start | bytes 2383880 | tf_op jit(solution)/shard_map/ppermute | solution.py:619
  912.0 38.0 %collective-permute-start.77 = (bf16[2,400,128]{2,1,0:T(8,128)(2,1)S(1)}, bf16[2,400,128]{2,1,0:T(8,128)(2,1)S(1)}, u32[]{:S(2)}, u32[]{:S(2)}) collective-permute-start(bf16[2,400,128]{2,1,0:T(8,128)(2,1)S(1)} %pad_maximum_fusion.21), channel_id=1, source_target_pairs={{8,0},{9,1},{10,2},{11,3},{12,4},{13,5},{14,6},{15,7}} | collective-permute-start | bytes 614408 | tf_op jit(solution)/shard_map/ppermute | solution.py:619
  913.3 57.5 %collective-permute-start.78 = (bf16[2,400,128]{2,1,0:T(8,128)(2,1)S(1)}, bf16[2,400,128]{2,1,0:T(8,128)(2,1)S(1)}, u32[]{:S(2)}, u32[]{:S(2)}) collective-permute-start(bf16[2,400,128]{2,1,0:T(8,128)(2,1)S(1)} %pad_maximum_fusion.21), channel_id=1, source_target_pairs={{16,0},{17,1},{18,2},{19,3},{20,4},{21,5},{22,6},{23,7}} | collective-permute-start | bytes 614408 | tf_op jit(solution)/shard_map/ppermute | solution.py:619
  914.6 57.5 %collective-permute-start.79 = (bf16[2,400,128]{2,1,0:T(8,128)(2,1)S(1)}, bf16[2,400,128]{2,1,0:T(8,128)(2,1)S(1)}, u32[]{:S(2)}, u32[]{:S(2)}) collective-permute-start(bf16[2,400,128]{2,1,0:T(8,128)(2,1)S(1)} %pad_maximum_fusion.21), channel_id=1, source_target_pairs={{24,0},{25,1},{26,2},{27,3},{28,4},{29,5},{30,6},{31,7}} | collective-permute-start | bytes 614408 | tf_op jit(solution)/shard_map/ppermute | solution.py:619
  916.1 78.1 %collective-permute-start.90 = (bf16[3104,128]{1,0:T(8,128)(2,1)S(1)}, bf16[3104,128]{1,0:T(8,128)(2,1)S(1)}, u32[]{:S(2)}, u32[]{:S(2)}) collective-permute-start(bf16[3104,128]{1,0:T(8,128)(2,1)S(1)} %fusion.23), channel_id=1, source_target_pairs={{16,0},{25,9},{18,2},{27,11},{20,4},{29,13},{22,6},{31,15}} | collective-permute-start | bytes 2383880 | tf_op jit(solution)/shard_map/ppermute | solution.py:619
  950.0 46.4 %collective-permute-start.91 = (bf16[3104,128]{1,0:T(8,128)(2,1)S(1)}, bf16[3104,128]{1,0:T(8,128)(2,1)S(1)}, u32[]{:S(2)}, u32[]{:S(2)}) collective-permute-start(bf16[3104,128]{1,0:T(8,128)(2,1)S(1)} %fusion.23), channel_id=1, source_target_pairs={{24,0},{1,9},{26,2},{3,11},{28,4},{5,13},{30,6},{7,15}} | collective-permute-start | bytes 2383880 | tf_op jit(solution)/shard_map/ppermute | solution.py:619
  970.7 36.8 %collective-permute-start.85 = (bf16[3104,128]{1,0:T(8,128)(2,1)S(1)}, bf16[3104,128]{1,0:T(8,128)(2,1)S(1)}, u32[]{:S(2)}, u32[]{:S(2)}) collective-permute-start(bf16[3104,128]{1,0:T(8,128)(2,1)S(1)} %fusion.24), channel_id=1, source_target_pairs={{8,0},{17,9},{10,2},{19,11},{12,4},{21,13},{14,6},{23,15}} | collective-permute-start | bytes 2383880 | tf_op jit(solution)/shard_map/ppermute | solution.py:619
  972.0 36.8 %collective-permute-start.86 = (bf16[3104,128]{1,0:T(8,128)(2,1)S(1)}, bf16[3104,128]{1,0:T(8,128)(2,1)S(1)}, u32[]{:S(2)}, u32[]{:S(2)}) collective-permute-start(bf16[3104,128]{1,0:T(8,128)(2,1)S(1)} %fusion.24), channel_id=1, source_target_pairs={{16,0},{25,9},{18,2},{27,11},{20,4},{29,13},{22,6},{31,15}} | collective-permute-start | bytes 2383880 | tf_op jit(solution)/shard_map/ppermute | solution.py:619
  973.4 39.2 %collective-permute-start.87 = (bf16[3104,128]{1,0:T(8,128)(2,1)S(1)}, bf16[3104,128]{1,0:T(8,128)(2,1)S(1)}, u32[]{:S(2)}, u32[]{:S(2)}) collective-permute-start(bf16[3104,128]{1,0:T(8,128)(2,1)S(1)} %fusion.24), channel_id=1, source_target_pairs={{24,0},{1,9},{26,2},{3,11},{28,4},{5,13},{30,6},{7,15}} | collective-permute-start | bytes 2383880 | tf_op jit(solution)/shard_map/ppermute | solution.py:619
  994.2 42.7 %collective-permute-start.99 = (bf16[3104,128]{1,0:T(8,128)(2,1)S(1)}, bf16[3104,128]{1,0:T(8,128)(2,1)S(1)}, u32[]{:S(2)}, u32[]{:S(2)}) collective-permute-start(bf16[3104,128]{1,0:T(8,128)(2,1)S(1)} %get-tuple-element.104), channel_id=1, source_target_pairs={{0,1},{9,8},{16,17},{25,24},{2,3},{11,10},{18,19},{27,26},{4,5},{1... | collective-permute-start | bytes 2383880 | tf_op jit(solution)/shard_map/ppermute | solution.py:619
  996.4 34.9 %collective-permute-start.68 = (f32[1024]{0:T(1024)S(1)}, f32[1024]{0:T(1024)S(1)}, u32[]{:S(2)}, u32[]{:S(2)}) collective-permute-start(f32[1024]{0:T(1024)S(1)} %add.767), channel_id=1, source_target_pairs={{0,8},{8,0},{16,24},{24,16},{1,9},{9,1},{17,25},{25,17},{2,10},{10... | collective-permute-start | bytes 12296 | tf_op jit(solution)/shard_map/ppermute | solution.py:1210
  1013.5 23.5 %collective-permute-start.92 = (bf16[3104,128]{1,0:T(8,128)(2,1)S(1)}, bf16[3104,128]{1,0:T(8,128)(2,1)S(1)}, u32[]{:S(2)}, u32[]{:S(2)}) collective-permute-start(bf16[3104,128]{1,0:T(8,128)(2,1)S(1)} %get-tuple-element.101), channel_id=1, source_target_pairs={{0,1},{9,8},{16,17},{25,24},{2,3},{11,10},{18,19},{27,26},{4,5},{1... | collective-permute-start | bytes 2383880 | tf_op jit(solution)/shard_map/ppermute | solution.py:619
  (260 other events, 3127.8 us)

commit v5 on v4

--- a/solution.py
+++ b/solution.py
@@ -205,18 +205,6 @@
         axis=-1,
     )
     return turned.reshape(row_count, heads * HEAD_DIM)
-
-
-def conv_apply(extended, conv_weight, conv_bias, positions):
-    row_count = positions.shape[0]
-    conv_total = conv_bias[None, :]
-    for tap_index in range(CONV):
-        window = extended[tap_index : tap_index + row_count]
-        valid_rows = (positions >= CONV - 1 - tap_index)[:, None]
-        conv_total = (
-            conv_total + jnp.where(valid_rows, window, 0.0) * conv_weight[tap_index][None, :]
-        )
-    return jax.nn.silu(conv_total)
 
 
 def add_rows(target, addend, first_row):
@@ -695,7 +683,122 @@
     return tall.T
 
 
-def weighted_state(left, values, weight_rows, after=()):
+CHANNELS = INNER + 2 * STATE
+LANES = 2 * SSM_DIM
+COLUMNS = CHANNELS // LANES
+
+
+def conv_parts(ext, weight_ref, bias_ref, start_ref, first, rows):
+    place = first + lax.broadcasted_iota(jnp.int32, (rows, 1), 0) - start_ref[...]
+    windows = []
+    total = bias_ref[...]
+    for tap in range(CONV):
+        reach = CONV - 1 - tap
+        window = jnp.where(place >= reach, ext[8 - reach : 8 - reach + rows, :], 0.0)
+        windows.append(window)
+        total = total + window * weight_ref[tap : tap + 1, :]
+    return place, windows, total
+
+
+def conv_forward(xbc, rim, weight, bias, meta, start_column):
+    rows = xbc.shape[0]
+
+    def kernel(meta_ref, x_ref, rim_ref, weight_ref, bias_ref, start_ref, out_ref, ext):
+        ext[0:8, :] = rim_ref[...]
+        ext[8:, :] = x_ref[...]
+        _, _, total = conv_parts(ext, weight_ref, bias_ref, start_ref, meta_ref[0], rows)
+        out_ref[...] = total * jax.nn.sigmoid(total)
+
+    lanes = lambda i, m: (0, i)
+    return pl.pallas_call(
+        kernel,
+        grid_spec=pltpu.PrefetchScalarGridSpec(
+            num_scalar_prefetch=1,
+            grid=(COLUMNS,),
+            in_specs=[
+                pl.BlockSpec((rows, LANES), lanes),
+                pl.BlockSpec((8, LANES), lanes),
+                pl.BlockSpec((CONV, LANES), lanes),
+                pl.BlockSpec((1, LANES), lanes),
+                pl.BlockSpec((rows, 1), lambda i, m: (0, 0)),
+            ],
+            out_specs=pl.BlockSpec((rows, LANES), lanes),
+            scratch_shapes=[pltpu.VMEM((rows + 8, LANES), jnp.float32)],
+        ),
+        out_shape=jax.ShapeDtypeStruct((rows, CHANNELS), jnp.float32),
+        cost_estimate=pl.CostEstimate(flops=10**9, bytes_accessed=rows * CHANNELS * 8, transcendentals=0),
+        name="conv",
+    )(meta, xbc, rim, weight, bias, start_column)
+
+
+def conv_backward(dx, db, dc, xbc, rim, weight, bias, meta, start_column, after=()):
+    rows = xbc.shape[0]
+
+    def kernel(meta_ref, dx_ref, db_ref, dc_ref, x_ref, rim_ref, weight_ref, bias_ref, start_ref,
+               low_ref, tail_ref, edge_ref, small_ref, ext, upper):
+        ext[0:8, :] = rim_ref[...]
+        ext[8:, :] = x_ref[...]
+        at = pl.program_id(0)
+        arrived = jnp.where(at < PAIRS, dx_ref[...], jnp.where(at == PAIRS, db_ref[...], dc_ref[...]))
+        place, windows, total = conv_parts(ext, weight_ref, bias_ref, start_ref, meta_ref[0], rows)
+        gate = jax.nn.sigmoid(total)
+        change = arrived * gate * (1.0 + total * (1.0 - gate))
+        upper[0:8, :] = jnp.zeros((8, LANES), jnp.float32)
+        upper[8 + rows :, :] = jnp.zeros((8, LANES), jnp.float32)
+        main = jnp.zeros((rows, LANES), jnp.float32)
+        edge = jnp.zeros((8, LANES), jnp.float32)
+        small_ref[...] = jnp.zeros((8, LANES), jnp.float32)
+        small_ref[CONV : CONV + 1, :] = jnp.sum(change, axis=0, keepdims=True)
+        for tap in range(CONV):
+            reach = CONV - 1 - tap
+            small_ref[tap : tap + 1, :] = jnp.sum(change * windows[tap], axis=0, keepdims=True)
+            upper[8 : 8 + rows, :] = jnp.where(place >= reach, change, 0.0) * weight_ref[tap : tap + 1, :]
+            main = main + upper[8 + reach : 8 + reach + rows, :]
+            edge = edge + upper[reach : reach + 8, :]
+        low_ref[...] = main.astype(jnp.bfloat16)
+        tail_ref[...] = main[rows - 16 :, :]
+        edge_ref[...] = edge
+
+    lanes = lambda i, m: (0, i)
+    whole = lambda i, m: (0, 0)
+    return pl.pallas_call(
+        pinned(kernel, 9, after),
+        grid_spec=pltpu.PrefetchScalarGridSpec(
+            num_scalar_prefetch=1,
+            grid=(COLUMNS,),
+            in_specs=[
+                pl.BlockSpec((rows, LANES), lambda i, m: (0, jnp.minimum(i, PAIRS - 1))),
+                pl.BlockSpec((rows, STATE), whole),
+                pl.BlockSpec((rows, STATE), whole),
+                pl.BlockSpec((rows, LANES), lanes),
+                pl.BlockSpec((8, LANES), lanes),
+                pl.BlockSpec((CONV, LANES), lanes),
+                pl.BlockSpec((1, LANES), lanes),
+                pl.BlockSpec((rows, 1), whole),
+            ] + pins(after),
+            out_specs=[
+                pl.BlockSpec((rows, LANES), lanes),
+                pl.BlockSpec((16, LANES), lanes),
+                pl.BlockSpec((8, LANES), lanes),
+                pl.BlockSpec((8, LANES), lanes),
+            ],
+            scratch_shapes=[
+                pltpu.VMEM((rows + 8, LANES), jnp.float32),
+                pltpu.VMEM((rows + 16, LANES), jnp.float32),
+            ],
+        ),
+        out_shape=[
+            jax.ShapeDtypeStruct((rows, CHANNELS), jnp.bfloat16),
+            jax.ShapeDtypeStruct((16, CHANNELS), jnp.float32),
+            jax.ShapeDtypeStruct((8, CHANNELS), jnp.float32),
+            jax.ShapeDtypeStruct((8, CHANNELS), jnp.float32),
+        ],
+        cost_estimate=pl.CostEstimate(flops=2 * 10**9, bytes_accessed=rows * CHANNELS * 10, transcendentals=0),
+        name="conv_back",
+    )(meta, dx, db, dc, xbc, rim, weight, bias, start_column, *after)
+
+
+def weighted_state(left, left_block, values, weight_rows, after=()):
     rows = left.shape[0]
 
     def kernel(left_ref, value_ref, weight_ref, out_ref, turned):
@@ -711,7 +814,7 @@
         pinned(kernel, 3, after),
         grid=(PAIRS,),
         in_specs=[
-            pl.BlockSpec((rows, STATE), lambda i: (0, 0)),
+            pl.BlockSpec((rows, STATE), lambda i: (0, left_block)),
             pl.BlockSpec((rows, 2 * SSM_DIM), lambda i: (0, i)),
             pl.BlockSpec((1, 2, rows), lambda i: (i, 0, 0)),
         ] + pins(after),
@@ -739,8 +842,8 @@
     return cums, entries, tails
 
 
-def ssm_forward(x, b_in, c_in, cum, step, state_in, skip, meta, start_column, start_row):
-    rows = x.shape[0]
+def ssm_forward(conv, cum, step, state_in, skip, meta, start_column, start_row):
+    rows = conv.shape[0]
     chunks = rows // CHUNK
 
     def kernel(meta_ref, x_ref, b_ref, c_ref, cum_ref, step_ref, state_ref, skip_ref, col_ref, row_ref,
@@ -792,8 +895,8 @@
             grid=(PAIRS,),
             in_specs=[
                 pl.BlockSpec((rows, 2 * SSM_DIM), lanes),
-                pl.BlockSpec((rows, STATE), whole),
-                pl.BlockSpec((rows, STATE), whole),
+                pl.BlockSpec((rows, STATE), lambda i, m: (0, PAIRS)),
+                pl.BlockSpec((rows, STATE), lambda i, m: (0, PAIRS + 1)),
                 pl.BlockSpec((1, 2, rows), lambda i, m: (i, 0, 0)),
                 pl.BlockSpec((1, 2, rows), lambda i, m: (i, 0, 0)),
                 pl.BlockSpec((STATE, 2 * SSM_DIM), lanes),
@@ -813,12 +916,12 @@
         compiler_params=pltpu.CompilerParams(vmem_limit_bytes=40 * 2**20),
         cost_estimate=pl.CostEstimate(flops=10**9, bytes_accessed=rows * INNER * 8, transcendentals=2**21),
         name="ssm",
-    )(meta, x, b_in, c_in, cum.reshape(PAIRS, 2, rows), step.reshape(PAIRS, 2, rows), state_in, skip,
+    )(meta, conv, conv, conv, cum.reshape(PAIRS, 2, rows), step.reshape(PAIRS, 2, rows), state_in, skip,
       start_column, start_row)
 
 
-def ssm_backward(x, dy, b_in, c_in, cum, step, state_in, state_grad, skip, meta, start_row, after=()):
-    rows = x.shape[0]
+def ssm_backward(conv, dy, cum, step, state_in, state_grad, skip, meta, start_row, after=()):
+    rows = conv.shape[0]
     chunks = rows // CHUNK
 
     def kernel(meta_ref, x_ref, dy_ref, b_ref, c_ref, cum_ref, step_ref, state_ref, grad_ref, skip_ref, row_ref,
@@ -925,8 +1028,8 @@
             in_specs=[
                 pl.BlockSpec((rows, 2 * SSM_DIM), lanes),
                 pl.BlockSpec((rows, 2 * SSM_DIM), lanes),
-                pl.BlockSpec((rows, STATE), whole),
-                pl.BlockSpec((rows, STATE), whole),
+                pl.BlockSpec((rows, STATE), lambda i, m: (0, PAIRS)),
+                pl.BlockSpec((rows, STATE), lambda i, m: (0, PAIRS + 1)),
                 pl.BlockSpec((1, 2, rows), pair),
                 pl.BlockSpec((1, 2, rows), pair),
                 pl.BlockSpec((STATE, 2 * SSM_DIM), lanes),
@@ -959,7 +1062,7 @@
         compiler_params=pltpu.CompilerParams(vmem_limit_bytes=40 * 2**20),
         cost_estimate=pl.CostEstimate(flops=3 * 10**9, bytes_accessed=rows * INNER * 12, transcendentals=2**21),
         name="ssm_back",
-    )(meta, x, dy, b_in, c_in, cum.reshape(PAIRS, 2, rows), step.reshape(PAIRS, 2, rows), state_in, state_grad,
+    )(meta, conv, dy, conv, conv, cum.reshape(PAIRS, 2, rows), step.reshape(PAIRS, 2, rows), state_in, state_grad,
       skip, start_row, *after)
 
 
@@ -997,7 +1100,7 @@
     rows = q_wide.shape[1]
     blocks = kv.shape[0]
     ratio = HEADS_Q // HEADS_KV
-    wide = min(256, rows)
+    wide = min(512, rows)
 
     def kernel(meta_ref, q_ref, kv_ref, start_ref, o_ref, log_ref, top, total):
         b = pl.program_id(1)
@@ -1084,7 +1187,7 @@
     rows = q_wide.shape[1]
     blocks = kv.shape[0]
     ratio = HEADS_Q // HEADS_KV
-    wide = min(256, rows)
+    wide = min(512, rows)
 
     def kernel(meta_ref, q_ref, g_ref, kv_ref, log_ref, o_ref, start_ref, dkv_ref, dq_ref, delta, sums):
         b = pl.program_id(0)
@@ -1364,19 +1467,10 @@
         [matmul(hidden, weights[W_X_SSM]), matmul(hidden, weights[W_B_C])], axis=1
     )
     step_raw = matmul(hidden, weights[W_STEP])
-    rim_rows = passed_along(xbc[rows_dev - (CONV - 1) :], span, 1)
-    extended = jnp.concatenate([rim_rows, xbc], axis=0)
-
-    def conv_local(extended_in, conv_weight, conv_bias):
-        return conv_apply(extended_in, conv_weight, conv_bias, positions)
-
-    conv_values, conv_back = jax.vjp(
-        conv_local, extended, small_f32[CONV_WEIGHT], small_f32[CONV_BIAS]
-    )
-
-    x_ssm = conv_values[:, :ssm_inner]
-    b_in = conv_values[:, ssm_inner : ssm_inner + STATE]
-    c_in = conv_values[:, ssm_inner + STATE :]
+    rim_rows = passed_along(xbc[rows_dev - 8 :], span, 1)
+    ssm_meta = jnp.concatenate([my_start[None], row_starts[CHUNK - 1 :: CHUNK]]).astype(jnp.int32)
+    conv_bias = small_f32[CONV_BIAS][None, :]
+    conv_values = conv_forward(xbc, rim_rows, small_f32[CONV_WEIGHT], conv_bias, ssm_meta, row_starts[:, None])
     step_in = step_raw.T + small_f32[STEP_BIAS][:, None]
     step_rows = jax.nn.softplus(step_in)
     decay = -jnp.exp(small_f32[DECAY_LOG])
@@ -1392,12 +1486,11 @@
     in_last = row_index >= row_starts[rows_dev - 1]
     tail_rows = jnp.exp(jnp.where(in_last[None, :], cumul[:, -1:] - cumul, masked_score))
     carry_all = entry_rows[:, -1]
-    local_state = weighted_state(b_in, x_ssm, tail_rows * step_rows)
+    local_state = weighted_state(conv_values, PAIRS, conv_values, tail_rows * step_rows)
     state_in = scan_states(carry_all, local_state, span, fast, False)
     skip_wide = jnp.repeat(small_f32[SKIP_GAIN], SSM_DIM)[None, :]
-    ssm_meta = jnp.concatenate([my_start[None], row_starts[CHUNK - 1 :: CHUNK]]).astype(jnp.int32)
     ssm_y = ssm_forward(
-        x_ssm, b_in, c_in, chunk_cum, step_rows, state_in, skip_wide, ssm_meta, row_starts[:, None], start_row
+        conv_values, chunk_cum, step_rows, state_in, skip_wide, ssm_meta, row_starts[:, None], start_row
     )
     normed_ssm, gnorm_back = jax.vjp(gated_norm, ssm_y, gate_ssm, small_f32[NORM_SSM])
     ssm_low = normed_ssm.astype(jnp.bfloat16)
@@ -1438,7 +1531,7 @@
     grad_attended = matmul_right_t(grad_branch, weights[W_ATTN_OUT]).astype(jnp.bfloat16)
     grad_ssm_low = matmul_right_t(grad_branch, weights[W_SSM_OUT])
     grad_ssm_y, grad_gate_ssm_f32, grad_norm_ssm = gnorm_back(grad_ssm_low)
-    grad_state_local = weighted_state(c_in, grad_ssm_y, entry_rows)
+    grad_state_local = weighted_state(conv_values, PAIRS + 1, grad_ssm_y, entry_rows)
     pinned_by = ()
     if fast:
         late = pack_late(
@@ -1451,9 +1544,8 @@
         pinned_by = late_flow.values()
     grad_state_out = scan_states(carry_all, grad_state_local, span, fast, True)
     grad_x, grad_b, grad_c, grad_small = ssm_backward(
-        x_ssm, grad_ssm_y, b_in, c_in, chunk_cum, step_rows, state_in, grad_state_out, skip_wide, ssm_meta, start_row, pinned_by
-    )
-    grad_conv_values = jnp.concatenate([grad_x, grad_b, grad_c], axis=1)
+        conv_values, grad_ssm_y, chunk_cum, step_rows, state_in, grad_state_out, skip_wide, ssm_meta, start_row, pinned_by
+    )
     grad_direct = grad_small[:, 0:2].reshape(SSM_HEADS, rows_dev)
     grad_logs = grad_small[:, 2:4].reshape(SSM_HEADS, rows_dev)
     grad_decay_log = decay * jnp.sum(step_rows * grad_logs, axis=1)
@@ -1461,11 +1553,18 @@
     grad_step_bias = jnp.sum(grad_step_rows, axis=1)
     grad_step_raw_f32 = grad_step_rows.T
     grad_skip_gain = jnp.sum(grad_small[:, 4, : 2 * SSM_DIM].reshape(SSM_HEADS, SSM_DIM), axis=1)
-    grad_extended, grad_conv_weight, grad_conv_bias = conv_back(grad_conv_values)
-    rim_back = passed_along(grad_extended[: CONV - 1], span, -1)
-    grad_xbc_f32 = grad_extended[CONV - 1 :]
-    grad_xbc_f32 = grad_xbc_f32.at[rows_dev - (CONV - 1) :].add(rim_back)
-    grad_xbc = grad_xbc_f32.astype(jnp.bfloat16)
+    if fast:
+        late_flow.go()
+        pinned_by = late_flow.values()
+    grad_main, grad_tail, grad_edge, grad_taps = conv_backward(
+        grad_x, grad_b, grad_c, xbc, rim_rows, small_f32[CONV_WEIGHT], conv_bias, ssm_meta,
+        row_starts[:, None], pinned_by,
+    )
+    grad_conv_weight = grad_taps[:CONV]
+    grad_conv_bias = grad_taps[CONV]
+    rim_back = passed_along(grad_edge, span, -1)
+    grad_tail = grad_tail + jnp.pad(rim_back, ((8, 0), (0, 0)))
+    grad_xbc = lax.dynamic_update_slice(grad_main, grad_tail.astype(jnp.bfloat16), (rows_dev - 16, 0))
     grad_gate_ssm = grad_gate_ssm_f32.astype(jnp.bfloat16)
     grad_step_raw = grad_step_raw_f32.astype(jnp.bfloat16)
     grad_w_step = matmul_left_t(hidden, grad_step_raw)
@@ -1499,7 +1598,7 @@
         )
         late_flow.go()
         early_flow = Flow(reduce_stages(early, 0, 8))
-        pinned_by = late_flow.values() + early_flow.values()
+        pinned_by = early_flow.values()
     parts = []
     for group_at in range(HEADS_KV):
         parts.append(
@@ -1507,7 +1606,7 @@
         )
         if fast:
             early_flow.go()
-            pinned_by = early_flow.values() + [parts[-1][1]]
+            pinned_by = early_flow.values() + late_flow.values() + [parts[-1][1]]
     grad_kv = jnp.concatenate([part[0] for part in parts], axis=1)
     grad_q_turned = jnp.concatenate([part[1] for part in parts], axis=0)
     if rows_dev != KEYS:
@@ -1525,7 +1624,6 @@
             attended, grad_branch, early_flow.values(),
         )
         early_flow.go()
-        late_flow.go()
         corner_flow = Flow(corner_stages(corner))
         for flow in (early_flow, late_flow, corner_flow):
             while flow.sends:

time: 1050 us -> 1020 us (0.971)
  waiting for transfers between devices: 267 us -> 223 us
  starting transfers between devices: 272 us -> 298 us
  Pallas kernels: 181 us -> 205 us
  local copies, waits for them, and re-layouts: 107 us -> 84.7 us
    ppermute x36, waiting for transfers between devices: 131 us -> 88.6 us  [go(): lax.ppermute(value, axis, pairs)]
    pallas_call x0 -> x2, Pallas kernels: none -> 27.7 us  [the longest x1 15.5 us: conv_backward(): pl.pallas_call(pinned(kernel, 9, after), grid_spec=pltpu.PrefetchScalarGr...]
    ppermute x16, starting transfers between devices: 23.6 us -> 40.7 us  [gather_lines(): buffers += local + [lax.ppermute(piece, 'c', SWAP) for piece in local]]
    unnamed x415 -> x376, local copies, waits for them, and re-layouts: 36.9 us -> 28 us
  transfers between devices with their start and end apart: 105 -> 105, of which waited for: 32 -> 31; matrix products, arithmetic and copies ran while one was open for 20% -> 19% of each run, Pallas kernels for 11% -> 13%
where the time goes in v5:
time: 1020 us; the launch traced here: 1010 us
  starting transfers between devices  298 us (29%)
  waiting for transfers between devices  223 us (22%)
  Pallas kernels  205 us (20%)
  other arithmetic  117 us (11%)
  local copies, waits for them, and re-layouts  84.7 us (8%)
  matrix products  80.4 us (8%)
    ppermute x36, starting transfers between devices, go(): lax.ppermute(value, axis, pairs)  115 us
    ppermute x36, waiting for transfers between devices, go(): lax.ppermute(value, axis, pairs)  88.6 us
    ppermute x6, starting transfers between devices, scan_states(): lax.ppermute(packed.astype(jnp.bfloat16), name, SWAP).astype(jnp.float32)  48 us
    pallas_call x4, Pallas kernels, pack_lines(): pl.pallas_call(pinned(kernel, inputs, after), grid=(total,), in_specs=[le...  44.4 us
    pallas_call x2, Pallas kernels, unpack_lines(): pl.pallas_call(pinned(kernel, 2 + count_buffers, after), grid_spec=pltpu....  41.3 us
    dot_general x12, matrix products, matmul_right_t(): lax.dot_general(left, right, (((1,), (1,)), ((), ())), preferred_element_...  40.9 us
    ppermute x16, starting transfers between devices, gather_lines(): buffers += local + [lax.ppermute(piece, 'c', SWAP) for piece in local]  40.7 us
    pallas_call x1, Pallas kernels, ssm_backward(): pl.pallas_call(pinned(kernel, 11, after), grid_spec=pltpu.PrefetchScalarG...  40.5 us
  transfers between devices with their start and end apart: 105, of which 31 were waited for; matrix products, arithmetic and copies ran while one was open for 19% of the time, Pallas kernels for 13%

profile of v5, /device:TPU:0, one launch (start us, length us, event | category | flops | bytes accessed | tf_op | source)
XLA Modules:
  0.0 1014.0 jit_solution(8856719007160791896)
XLA Ops:
  1.9 7.7 collective-permute-start
  44.2 15.7 %collective-permute-done.32 = bf16[3088,128]{1,0:T(8,128)(2,1)} collective-permute-done((bf16[3088,128]{1,0:T(8,128)(2,1)S(1)}, bf16[3088,128]{1,0:T(8,128)(2,1)}, u32[]{:S(2)}, u32[]{:S(2)}) %collective-permute-start.32) | collective-permute-done | bytes 790560 | tf_op jit(solution)/shard_map/ppermute | solution.py:257
  76.2 12.3 %collective-permute-start.19 = (bf16[3088,128]{1,0:T(8,128)(2,1)}, bf16[3088,128]{1,0:T(8,128)(2,1)}, u32[]{:S(2)}, u32[]{:S(2)}) collective-permute-start(bf16[3088,128]{1,0:T(8,128)(2,1)} %get-tuple-element.150.refs_10_), channel_id=1, source_target_pairs={{0,1},{1,0},{2,3},{3,2},{4,5},{5,4},{6,7},{7,6},{8,9},{9,8},{10,11... | collective-permute-start | bytes 2371592 | tf_op jit(solution)/shard_map/ppermute | solution.py:268
  90.1 6.7 collective-permute-done.16.refs_11_
  96.7 19.6 %collective-permute-start.21 = (bf16[3088,128]{1,0:T(8,128)(2,1)}, bf16[3088,128]{1,0:T(8,128)(2,1)}, u32[]{:S(2)}, u32[]{:S(2)}) collective-permute-start(bf16[3088,128]{1,0:T(8,128)(2,1)} %collective-permute-done.17.refs_12_), channel_id=1, source_target_pairs={{0,1},{1,0},{2,3},{3,2},{4,5},{5,4},{6,7},{7,6},{8,9},{9,8},{10,11... | collective-permute-start | bytes 2371592 | tf_op jit(solution)/shard_map/ppermute | solution.py:268
  128.5 7.5 collective-permute-done.7.refs_5_
  142.5 5.9 collective-permute-start.34
  150.3 14.8 %unpack.2 = (bf16[1024,512]{1,0:T(8,128)(2,1)}, bf16[1024,128]{1,0:T(8,128)(2,1)S(1)}, bf16[1024,128]{1,0:T(8,128)(2,1)S(1)}, bf16[512,1024]{1,0:T(8,128)(2,1)},...) custom-call(s32[25,5]{1,0:T(8,128)S(1)} %copy-done.43, ...), custom_call_target="tpu_custom_call" | custom-call | bytes 26624000 | tf_op jit(solution)/shard_map/unpack/pallas_call | solution.py:409
  192.4 6.4 collective-permute-start.26
  201.0 12.2 %conv.1.refs_0_.refs_1_.x_ref.b_ref.c_ref.refs_3_.refs_4_ = f32[512,1792]{1,0:T(8,128)} custom-call(s32[5]{0:T(128)} %pad_add_fusion.1.meta_ref.refs_0_, f32[512,1792]{1,0:T(8,128)} %pad_maximum_fusion.x_ref.refs_4_, f32[8,1792]{1,0:T(8,128)} %copy-done.134, f32[4,1792]{1,0:T(4,128)} %reshape.384.weight_ref.refs_6_, f32[1,1792]{1,0:T(1,128)} %bitcast.292, ...), custom_call_target="tpu_custom_call" | custom-call | flops 1000000000 | bytes 7340032 | tf_op jit(solution)/shard_map/conv/pallas_call | solution.py:713
  213.2 9.2 state.2
  242.6 6.3 collective-permute-done.28
  266.6 8.5 ssm.1
  284.8 15.3 %collective-permute-done.47.refs_29_ = bf16[3088,128]{1,0:T(8,128)(2,1)} collective-permute-done((bf16[3088,128]{1,0:T(8,128)(2,1)}, bf16[3088,128]{1,0:T(8,128)(2,1)}, u32[]{:S(2)}, u32[]{:S(2)}) %collective-permute-start.47) | collective-permute-done | bytes 790560 | tf_op jit(solution)/shard_map/ppermute | solution.py:266
  302.1 5.9 collective-permute-start.51
  308.9 7.9 attend.1
  322.6 26.5 %unpack.3 = (bf16[1536,1024]{1,0:T(8,128)(2,1)}, bf16[1024,2048]{1,0:T(8,128)(2,1)}, bf16[1024,2048]{1,0:T(8,128)(2,1)}, bf16[2048,1024]{1,0:T(8,128)(2,1)}, bf16[16,128]{1,0:T(8,128)(2,1)S(1)}) custom-call(s32[31,5]{1,0:T(8,128)S(1)} %copy-done.42, s32[32]{0:T(128)S(1)} %fusion.68.refs_1_, bf16[3088,128]{1,0:T(8,128)(2,1)S(1)} %get-tuple-element.152.refs_2_, ...), custom_call_target="tpu_custom_call" | custom-call | bytes 33013760 | tf_op jit(solution)/shard_map/unpack/pallas_call | solution.py:409
  363.6 6.7 fusion.2
  387.1 7.2 fusion.23
  394.3 9.6 state.3.refs_7_
  404.0 6.5 pad_maximum_fusion.2
  410.5 20.5 %pack.4 = bf16[49344,128]{1,0:T(8,128)(2,1)} custom-call(bf16[512,1024]{1,0:T(8,128)(2,1)S(1)} %copy-done.33, bf16[512,2048]{1,0:T(8,128)(2,1)S(1)} %copy-done.46, bf16[512,2048]{1,0:T(8,128)(2,1)} %get-tuple-element.182.refs_2_, bf16[512,2048]{1,0:T(8,128)(2,1)} %get-tuple-element.183.refs_3_, bf16[512,1024]{1,0:T(8,128)(2,1)S(1)} %copy-done.31, ...), custom_call_target="tpu_custom_call" | custom-call | flops 6442450944 | bytes 16777216 | tf_op jit(solution)/shard_map/pack/pallas_call | solution.py:564
  431.1 5.9 constant_dynamic-slice_fusion.4.refs_3_
  437.0 7.0 collective-permute-start.55
  444.1 8.4 collective-permute-done.52
  454.6 10.8 %collective-permute-start.53 = (bf16[144,1536]{1,0:T(8,128)(2,1)}, bf16[144,1536]{1,0:T(8,128)(2,1)}, u32[]{:S(2)}, u32[]{:S(2)}) collective-permute-start(bf16[144,1536]{1,0:T(8,128)(2,1)} %pad_maximum_fusion.19), channel_id=1, source_target_pairs={{0,2},{2,0},{1,3},{3,1},{4,6},{6,4},{5,7},{7,5},{8,10},{10,8},{9,1... | collective-permute-start | bytes 1327112 | tf_op jit(solution)/shard_map/ppermute | solution.py:1083
  467.4 8.8 collective-permute-done.53
  480.7 32.1 %collective-permute-start.54 = (bf16[144,1536]{1,0:T(8,128)(2,1)S(1)}, bf16[144,1536]{1,0:T(8,128)(2,1)S(1)}, u32[]{:S(2)}, u32[]{:S(2)}) collective-permute-start(bf16[144,1536]{1,0:T(8,128)(2,1)S(1)} %pad_maximum_fusion.20), channel_id=1, source_target_pairs={{0,4},{4,0},{1,5},{5,1},{2,6},{6,2},{3,7},{7,3},{8,12},{12,8},{9,1... | collective-permute-start | bytes 1327112 | tf_op jit(solution)/shard_map/ppermute | solution.py:1083
  523.0 5.8 add_convert_fusion.1
  536.4 40.5 %ssm_back.1 = (f32[512,1536]{1,0:T(8,128)S(1)}, f32[512,128]{1,0:T(8,128)S(1)}, f32[512,128]{1,0:T(8,128)S(1)}, f32[12,8,512]{2,1,0:T(8,128)S(1)}) custom-call(s32[5]{0:T(128)S(1)} %copy-done.44, f32[512,1792]{1,0:T(8,128)} %conv.1.refs_0_.refs_1_.x_ref.b_ref.c_ref.refs_3_.refs_4_, f32[512,1536]{1,0:T(8,128)S(1)} %copy-done.1, ...), custom_call_target="tpu_custom_call" | custom-call | flops 3000000000 | bytes 9437184 | tf_op jit(solution)/shard_map/ssm_back/pallas_call | solution.py:1023
  592.0 15.5 %conv_back.1 = (bf16[512,1792]{1,0:T(8,128)(2,1)}, f32[16,1792]{1,0:T(8,128)}, f32[8,1792]{1,0:T(8,128)}, f32[8,1792]{1,0:T(8,128)}) custom-call(s32[5]{0:T(128)} %pad_add_fusion.1.meta_ref.refs_0_, f32[512,1536]{1,0:T(8,128)} %copy-done.22, f32[512,128]{1,0:T(8,128)} %copy-done.39, f32[512,128]{1,0:T(8,128)} %copy-done.40, ...), custom_call_target="tpu_custom_call" | custom-call | flops 2000000000 | bytes 9175040 | tf_op jit(solution)/shard_map/conv_back/pallas_call | solution.py:764
  608.3 6.1 collective-permute-start.58
  624.6 13.8 %pack.6 = bf16[49440,128]{1,0:T(8,128)(2,1)} custom-call(bf16[512,512]{1,0:T(8,128)(2,1)S(1)} %bitcast.251, bf16[512,1024]{1,0:T(8,128)(2,1)S(1)} %fusion.11.refs_1_.refs_0_, bf16[512,1024]{1,0:T(8,128)(2,1)S(1)} %fusion.77.refs_2_, bf16[512,1536]{1,0:T(8,128)(2,1)S(1)} %copy-done.10, ...), custom_call_target="tpu_custom_call", output_to_operand_aliasing={{}: (7, {})} | custom-call | flops 4026531840 | bytes 11010048 | tf_op jit(solution)/shard_map/pack/pallas_call | solution.py:564
  638.4 5.9 constant_dynamic-slice_fusion.3.refs_7_
  671.3 21.4 %collective-permute-start.66 = (bf16[3104,128]{1,0:T(8,128)(2,1)S(1)}, bf16[3104,128]{1,0:T(8,128)(2,1)S(1)}, u32[]{:S(2)}, u32[]{:S(2)}) collective-permute-start(bf16[3104,128]{1,0:T(8,128)(2,1)S(1)} %copy-done.3), channel_id=1, source_target_pairs={{0,16},{9,25},{2,18},{11,27},{4,20},{13,29},{6,22},{15,31}} | collective-permute-start | bytes 2383880 | tf_op jit(solution)/shard_map/ppermute | solution.py:607
  693.5 7.8 attend_back.2
  701.4 12.6 %collective-permute-start.100 = (f32[4]{0:T(128)S(1)}, f32[4]{0:T(128)S(1)}, u32[]{:S(2)}, u32[]{:S(2)}) collective-permute-start(f32[4]{0:T(128)S(1)} %pad_maximum_fusion.25), channel_id=1, source_target_pairs={{0,4},{4,0},{1,5},{5,1},{2,6},{6,2},{3,7},{7,3},{8,12},{12,8},{9,1... | collective-permute-start | bytes 56 | tf_op jit(solution)/shard_map/ppermute | solution.py:1311
  717.5 6.1 add_convert_fusion
  728.1 8.2 attend_back.3
  740.3 8.4 collective-permute-start.68
  756.5 11.7 %collective-permute-start.77 = (bf16[2,3104,128]{2,1,0:T(8,128)(2,1)}, bf16[2,3104,128]{2,1,0:T(8,128)(2,1)}, u32[]{:S(2)}, u32[]{:S(2)}) collective-permute-start(bf16[2,3104,128]{2,1,0:T(8,128)(2,1)} %pad_maximum_fusion.8.refs_8_), channel_id=1, source_target_pairs={{0,2},{2,0},{1,3},{3,1},{4,6},{6,4},{5,7},{7,5},{8,10},{10,8},{9,1... | collective-permute-start | bytes 4767752 | tf_op jit(solution)/shard_map/ppermute | solution.py:607
  768.3 11.5 %collective-permute-start.76 = (bf16[2,3104,128]{2,1,0:T(8,128)(2,1)}, bf16[2,3104,128]{2,1,0:T(8,128)(2,1)}, u32[]{:S(2)}, u32[]{:S(2)}) collective-permute-start(bf16[2,3104,128]{2,1,0:T(8,128)(2,1)} %pad_maximum_fusion.7.refs_7_), channel_id=1, source_target_pairs={{0,4},{4,0},{1,5},{5,1},{2,6},{6,2},{3,7},{7,3},{8,12},{12,8},{9,1... | collective-permute-start | bytes 4767752 | tf_op jit(solution)/shard_map/ppermute | solution.py:607
  797.1 28.9 %collective-permute-done.69 = bf16[2,2,512,128]{2,3,1,0:T(8,128)(2,1)} collective-permute-done((bf16[2,2,512,128]{2,3,1,0:T(8,128)(2,1)}, bf16[2,2,512,128]{2,3,1,0:T(8,128)(2,1)}, u32[]{:S(2)}, u32[]{:S(2)}) %collective-permute-start.69) | collective-permute-done | bytes 524320 | tf_op jit(solution)/shard_map/ppermute | solution.py:1301
  868.4 15.6 %collective-permute-done.94 = bf16[3104,128]{1,0:T(8,128)(2,1)S(1)} collective-permute-done((bf16[3104,128]{1,0:T(8,128)(2,1)S(1)}, bf16[3104,128]{1,0:T(8,128)(2,1)S(1)}, u32[]{:S(2)}, u32[]{:S(2)}) %collective-permute-start.94) | collective-permute-done | bytes 794656 | tf_op jit(solution)/shard_map/ppermute | solution.py:607
  916.3 6.1 collective-permute-done.85
  925.8 47.1 %collective-permute-done.96 = bf16[3104,128]{1,0:T(8,128)(2,1)S(1)} collective-permute-done((bf16[3104,128]{1,0:T(8,128)(2,1)S(1)}, bf16[3104,128]{1,0:T(8,128)(2,1)S(1)}, u32[]{:S(2)}, u32[]{:S(2)}) %collective-permute-start.96) | collective-permute-done | bytes 794656 | tf_op jit(solution)/shard_map/ppermute | solution.py:607
  987.5 7.8 collective-permute-start.98
  995.4 6.1 collective-permute-start.87
  (809 shorter events, 409.3 us)
Async XLA Ops:
  30.2 29.6 %collective-permute-start.32 = (bf16[3088,128]{1,0:T(8,128)(2,1)S(1)}, bf16[3088,128]{1,0:T(8,128)(2,1)}, u32[]{:S(2)}, u32[]{:S(2)}) collective-permute-start(bf16[3088,128]{1,0:T(8,128)(2,1)S(1)} %collective-permute-done.30), channel_id=1, source_target_pairs={{8,0},{17,9},{10,2},{19,11},{12,4},{21,13},{14,6},{23,15}} | collective-permute-start | bytes 2371592 | tf_op jit(solution)/shard_map/ppermute | solution.py:257
  34.3 26.3 %collective-permute-start.3 = (bf16[3088,128]{1,0:T(8,128)(2,1)S(1)}, bf16[3088,128]{1,0:T(8,128)(2,1)}, u32[]{:S(2)}, u32[]{:S(2)}) collective-permute-start(bf16[3088,128]{1,0:T(8,128)(2,1)S(1)} %collective-permute-done.1), channel_id=1, source_target_pairs={{8,16},{17,25},{10,18},{19,27},{12,20},{21,29},{14,22},{23,31}} | collective-permute-start | bytes 2371592 | tf_op jit(solution)/shard_map/ppermute | solution.py:252
  35.9 25.4 %collective-permute-start.15 = (bf16[3088,128]{1,0:T(8,128)(2,1)}, bf16[3088,128]{1,0:T(8,128)(2,1)}, u32[]{:S(2)}, u32[]{:S(2)}) collective-permute-start(bf16[3088,128]{1,0:T(8,128)(2,1)} %collective-permute-done.14), channel_id=1, source_target_pairs={{16,24},{18,26},{20,28},{22,30}} | collective-permute-start | bytes 2371592 | tf_op jit(solution)/shard_map/ppermute | solution.py:253
  43.5 24.2 %collective-permute-start.2 = (bf16[3088,128]{1,0:T(8,128)(2,1)S(1)}, bf16[3088,128]{1,0:T(8,128)(2,1)S(1)}, u32[]{:S(2)}, u32[]{:S(2)}) collective-permute-start(bf16[3088,128]{1,0:T(8,128)(2,1)S(1)} %get-tuple-element.140), channel_id=1, source_target_pairs={{9,1},{11,3},{13,5},{15,7}} | collective-permute-start | bytes 2371592 | tf_op jit(solution)/shard_map/ppermute | solution.py:251
  66.3 22.3 %collective-permute-start.17 = (bf16[3088,128]{1,0:T(8,128)(2,1)}, bf16[3088,128]{1,0:T(8,128)(2,1)}, u32[]{:S(2)}, u32[]{:S(2)}) collective-permute-start(bf16[3088,128]{1,0:T(8,128)(2,1)} %get-tuple-element.150.refs_10_), channel_id=1, source_target_pairs={{0,4},{4,0},{1,5},{5,1},{2,6},{6,2},{3,7},{7,3},{8,12},{12,8},{9,1... | collective-permute-start | bytes 2371592 | tf_op jit(solution)/shard_map/ppermute | solution.py:262
  71.9 24.8 %collective-permute-start.16 = (bf16[3088,128]{1,0:T(8,128)(2,1)}, bf16[3088,128]{1,0:T(8,128)(2,1)}, u32[]{:S(2)}, u32[]{:S(2)}) collective-permute-start(bf16[3088,128]{1,0:T(8,128)(2,1)} %get-tuple-element.150.refs_10_), channel_id=1, source_target_pairs={{0,2},{2,0},{1,3},{3,1},{4,6},{6,4},{5,7},{7,5},{8,10},{10,8},{9,1... | collective-permute-start | bytes 2371592 | tf_op jit(solution)/shard_map/ppermute | solution.py:261
  72.5 43.8 %collective-permute-start.6 = (bf16[3088,128]{1,0:T(8,128)(2,1)S(1)}, bf16[3088,128]{1,0:T(8,128)(2,1)S(1)}, u32[]{:S(2)}, u32[]{:S(2)}) collective-permute-start(bf16[3088,128]{1,0:T(8,128)(2,1)S(1)} %get-tuple-element.152.refs_2_), channel_id=1, source_target_pairs={{0,4},{4,0},{1,5},{5,1},{2,6},{6,2},{3,7},{7,3},{8,12},{12,8},{9,1... | collective-permute-start | bytes 2371592 | tf_op jit(solution)/shard_map/ppermute | solution.py:262
  76.2 51.6 %collective-permute-start.19 = (bf16[3088,128]{1,0:T(8,128)(2,1)}, bf16[3088,128]{1,0:T(8,128)(2,1)}, u32[]{:S(2)}, u32[]{:S(2)}) collective-permute-start(bf16[3088,128]{1,0:T(8,128)(2,1)} %get-tuple-element.150.refs_10_), channel_id=1, source_target_pairs={{0,1},{1,0},{2,3},{3,2},{4,5},{5,4},{6,7},{7,6},{8,9},{9,8},{10,11... | collective-permute-start | bytes 2371592 | tf_op jit(solution)/shard_map/ppermute | solution.py:268
  88.5 39.4 %collective-permute-start.8 = (bf16[3088,128]{1,0:T(8,128)(2,1)S(1)}, bf16[3088,128]{1,0:T(8,128)(2,1)S(1)}, u32[]{:S(2)}, u32[]{:S(2)}) collective-permute-start(bf16[3088,128]{1,0:T(8,128)(2,1)S(1)} %get-tuple-element.152.refs_2_), channel_id=1, source_target_pairs={{0,1},{1,0},{2,3},{3,2},{4,5},{5,4},{6,7},{7,6},{8,9},{9,8},{10,11... | collective-permute-start | bytes 2371592 | tf_op jit(solution)/shard_map/ppermute | solution.py:268
  88.6 39.8 %collective-permute-start.18 = (bf16[3088,128]{1,0:T(8,128)(2,1)}, bf16[3088,128]{1,0:T(8,128)(2,1)}, u32[]{:S(2)}, u32[]{:S(2)}) collective-permute-start(bf16[3088,128]{1,0:T(8,128)(2,1)} %collective-permute-done.17.refs_12_), channel_id=1, source_target_pairs={{0,2},{2,0},{1,3},{3,1},{4,6},{6,4},{5,7},{7,5},{8,10},{10,8},{9,1... | collective-permute-start | bytes 2371592 | tf_op jit(solution)/shard_map/ppermute | solution.py:266
  96.7 39.3 %collective-permute-start.21 = (bf16[3088,128]{1,0:T(8,128)(2,1)}, bf16[3088,128]{1,0:T(8,128)(2,1)}, u32[]{:S(2)}, u32[]{:S(2)}) collective-permute-start(bf16[3088,128]{1,0:T(8,128)(2,1)} %collective-permute-done.17.refs_12_), channel_id=1, source_target_pairs={{0,1},{1,0},{2,3},{3,2},{4,5},{5,4},{6,7},{7,6},{8,9},{9,8},{10,11... | collective-permute-start | bytes 2371592 | tf_op jit(solution)/shard_map/ppermute | solution.py:268
  137.9 141.2 %collective-permute-start.46 = (bf16[3088,128]{1,0:T(8,128)(2,1)}, bf16[3088,128]{1,0:T(8,128)(2,1)}, u32[]{:S(2)}, u32[]{:S(2)}) collective-permute-start(bf16[3088,128]{1,0:T(8,128)(2,1)} %get-tuple-element.149.refs_26_), channel_id=1, source_target_pairs={{0,4},{4,0},{1,5},{5,1},{2,6},{6,2},{3,7},{7,3},{8,12},{12,8},{9,1... | collective-permute-start | bytes 2371592 | tf_op jit(solution)/shard_map/ppermute | solution.py:262
  138.6 141.2 %collective-permute-start.45 = (bf16[3088,128]{1,0:T(8,128)(2,1)}, bf16[3088,128]{1,0:T(8,128)(2,1)}, u32[]{:S(2)}, u32[]{:S(2)}) collective-permute-start(bf16[3088,128]{1,0:T(8,128)(2,1)} %get-tuple-element.149.refs_26_), channel_id=1, source_target_pairs={{0,2},{2,0},{1,3},{3,1},{4,6},{6,4},{5,7},{7,5},{8,10},{10,8},{9,1... | collective-permute-start | bytes 2371592 | tf_op jit(solution)/shard_map/ppermute | solution.py:261
  142.5 137.2 %collective-permute-start.34 = (bf16[3088,128]{1,0:T(8,128)(2,1)}, bf16[3088,128]{1,0:T(8,128)(2,1)}, u32[]{:S(2)}, u32[]{:S(2)}) collective-permute-start(bf16[3088,128]{1,0:T(8,128)(2,1)} %get-tuple-element.151.refs_18_), channel_id=1, source_target_pairs={{0,2},{2,0},{1,3},{3,1},{4,6},{6,4},{5,7},{7,5},{8,10},{10,8},{9,1... | collective-permute-start | bytes 2371592 | tf_op jit(solution)/shard_map/ppermute | solution.py:261
  186.3 52.5 %collective-permute-start.23 = (bf16[2,512,128]{2,1,0:T(8,128)(2,1)}, bf16[2,512,128]{2,1,0:T(8,128)(2,1)}, u32[]{:S(2)}, u32[]{:S(2)}) collective-permute-start(bf16[2,512,128]{2,1,0:T(8,128)(2,1)} %maximum_bitcast_fusion.1), channel_id=1, source_target_pairs={{0,2},{2,0},{1,3},{3,1},{4,6},{6,4},{5,7},{7,5},{8,10},{10,8},{9,1... | collective-permute-start | bytes 786440 | tf_op jit(solution)/shard_map/ppermute | solution.py:1287
  258.8 23.0 %collective-permute-start.35 = (bf16[3088,128]{1,0:T(8,128)(2,1)}, bf16[3088,128]{1,0:T(8,128)(2,1)}, u32[]{:S(2)}, u32[]{:S(2)}) collective-permute-start(bf16[3088,128]{1,0:T(8,128)(2,1)} %get-tuple-element.151.refs_18_), channel_id=1, source_target_pairs={{0,4},{4,0},{1,5},{5,1},{2,6},{6,2},{3,7},{7,3},{8,12},{12,8},{9,1... | collective-permute-start | bytes 2371592 | tf_op jit(solution)/shard_map/ppermute | solution.py:262
  281.8 26.3 %collective-permute-start.50 = (bf16[3088,128]{1,0:T(8,128)(2,1)}, bf16[3088,128]{1,0:T(8,128)(2,1)S(1)}, u32[]{:S(2)}, u32[]{:S(2)}) collective-permute-start(bf16[3088,128]{1,0:T(8,128)(2,1)} %collective-permute-done.46.refs_28_), channel_id=1, source_target_pairs={{0,1},{1,0},{2,3},{3,2},{4,5},{5,4},{6,7},{7,6},{8,9},{9,8},{10,11... | collective-permute-start | bytes 2371592 | tf_op jit(solution)/shard_map/ppermute | solution.py:268
  284.2 37.2 %collective-permute-start.38 = (bf16[3088,128]{1,0:T(8,128)(2,1)}, bf16[3088,128]{1,0:T(8,128)(2,1)S(1)}, u32[]{:S(2)}, u32[]{:S(2)}) collective-permute-start(bf16[3088,128]{1,0:T(8,128)(2,1)} %collective-permute-done.34.refs_19_), channel_id=1, source_target_pairs={{0,1},{1,0},{2,3},{3,2},{4,5},{5,4},{6,7},{7,6},{8,9},{9,8},{10,11... | collective-permute-start | bytes 2371592 | tf_op jit(solution)/shard_map/ppermute | solution.py:268
  284.5 37.0 %collective-permute-start.49 = (bf16[3088,128]{1,0:T(8,128)(2,1)}, bf16[3088,128]{1,0:T(8,128)(2,1)S(1)}, u32[]{:S(2)}, u32[]{:S(2)}) collective-permute-start(bf16[3088,128]{1,0:T(8,128)(2,1)} %collective-permute-done.45.refs_27_), channel_id=1, source_target_pairs={{0,1},{1,0},{2,3},{3,2},{4,5},{5,4},{6,7},{7,6},{8,9},{9,8},{10,11... | collective-permute-start | bytes 2371592 | tf_op jit(solution)/shard_map/ppermute | solution.py:268
  437.0 85.9 %collective-permute-start.55 = (bf16[24688,128]{1,0:T(8,128)(2,1)}, bf16[24688,128]{1,0:T(8,128)(2,1)}, u32[]{:S(2)}, u32[]{:S(2)}) collective-permute-start(bf16[24688,128]{1,0:T(8,128)(2,1)} %constant_dynamic-slice_fusion.4.refs_3_), channel_id=1, source_target_pairs={{0,1},{1,0},{2,3},{3,2},{4,5},{5,4},{6,7},{7,6},{8,9},{9,8},{10,11... | collective-permute-start | bytes 18960392 | tf_op jit(solution)/shard_map/ppermute | solution.py:607
  480.7 42.1 %collective-permute-start.54 = (bf16[144,1536]{1,0:T(8,128)(2,1)S(1)}, bf16[144,1536]{1,0:T(8,128)(2,1)S(1)}, u32[]{:S(2)}, u32[]{:S(2)}) collective-permute-start(bf16[144,1536]{1,0:T(8,128)(2,1)S(1)} %pad_maximum_fusion.20), channel_id=1, source_target_pairs={{0,4},{4,0},{1,5},{5,1},{2,6},{6,2},{3,7},{7,3},{8,12},{12,8},{9,1... | collective-permute-start | bytes 1327112 | tf_op jit(solution)/shard_map/ppermute | solution.py:1083
  532.0 52.4 %collective-permute-start.57 = (bf16[2,3104,128]{2,1,0:T(8,128)(2,1)}, bf16[2,3104,128]{2,1,0:T(8,128)(2,1)}, u32[]{:S(2)}, u32[]{:S(2)}) collective-permute-start(bf16[2,3104,128]{2,1,0:T(8,128)(2,1)} %pad_maximum_fusion.6.refs_12_), channel_id=1, source_target_pairs={{0,2},{2,0},{1,3},{3,1},{4,6},{6,4},{5,7},{7,5},{8,10},{10,8},{9,1... | collective-permute-start | bytes 4767752 | tf_op jit(solution)/shard_map/ppermute | solution.py:607
  534.7 53.4 %collective-permute-start.56 = (bf16[2,3104,128]{2,1,0:T(8,128)(2,1)}, bf16[2,3104,128]{2,1,0:T(8,128)(2,1)}, u32[]{:S(2)}, u32[]{:S(2)}) collective-permute-start(bf16[2,3104,128]{2,1,0:T(8,128)(2,1)} %pad_maximum_fusion.5.refs_11_), channel_id=1, source_target_pairs={{0,4},{4,0},{1,5},{5,1},{2,6},{6,2},{3,7},{7,3},{8,12},{12,8},{9,1... | collective-permute-start | bytes 4767752 | tf_op jit(solution)/shard_map/ppermute | solution.py:607
  587.8 33.9 %collective-permute-start.60 = (bf16[3104,128]{1,0:T(8,128)(2,1)}, bf16[3104,128]{1,0:T(8,128)(2,1)}, u32[]{:S(2)}, u32[]{:S(2)}) collective-permute-start(bf16[3104,128]{1,0:T(8,128)(2,1)} %dynamic-slice_bitcast_fusion.10.refs_10_), channel_id=1, source_target_pairs={{0,4},{4,0},{1,5},{5,1},{2,6},{6,2},{3,7},{7,3},{8,12},{12,8},{9,1... | collective-permute-start | bytes 2383880 | tf_op jit(solution)/shard_map/ppermute | solution.py:607
  591.4 31.8 %collective-permute-start.59 = (bf16[3104,128]{1,0:T(8,128)(2,1)}, bf16[3104,128]{1,0:T(8,128)(2,1)}, u32[]{:S(2)}, u32[]{:S(2)}) collective-permute-start(bf16[3104,128]{1,0:T(8,128)(2,1)} %dynamic-slice_bitcast_fusion.13.refs_9_), channel_id=1, source_target_pairs={{0,2},{2,0},{1,3},{3,1},{4,6},{6,4},{5,7},{7,5},{8,10},{10,8},{9,1... | collective-permute-start | bytes 2383880 | tf_op jit(solution)/shard_map/ppermute | solution.py:607
  644.3 73.2 %collective-permute-start.61 = (bf16[24688,128]{1,0:T(8,128)(2,1)}, bf16[24688,128]{1,0:T(8,128)(2,1)}, u32[]{:S(2)}, u32[]{:S(2)}) collective-permute-start(bf16[24688,128]{1,0:T(8,128)(2,1)} %constant_dynamic-slice_fusion.3.refs_7_), channel_id=1, source_target_pairs={{0,1},{1,0},{2,3},{3,2},{4,5},{5,4},{6,7},{7,6},{8,9},{9,8},{10,11... | collective-permute-start | bytes 18960392 | tf_op jit(solution)/shard_map/ppermute | solution.py:607
  651.7 41.1 %collective-permute-start.63 = (bf16[3104,128]{1,0:T(8,128)(2,1)S(1)}, bf16[3104,128]{1,0:T(8,128)(2,1)}, u32[]{:S(2)}, u32[]{:S(2)}) collective-permute-start(bf16[3104,128]{1,0:T(8,128)(2,1)S(1)} %fusion.21.refs_11_.refs_12_.refs_13_), channel_id=1, source_target_pairs={{0,16},{9,25},{2,18},{11,27},{4,20},{13,29},{6,22},{15,31}} | collective-permute-start | bytes 2383880 | tf_op jit(solution)/shard_map/ppermute | solution.py:607
  669.7 31.7 %collective-permute-start.64 = (bf16[3104,128]{1,0:T(8,128)(2,1)S(1)}, bf16[3104,128]{1,0:T(8,128)(2,1)S(1)}, u32[]{:S(2)}, u32[]{:S(2)}) collective-permute-start(bf16[3104,128]{1,0:T(8,128)(2,1)S(1)} %fusion.21.refs_11_.refs_12_.refs_13_), channel_id=1, source_target_pairs={{24,16},{1,25},{26,18},{3,27},{28,20},{5,29},{30,22},{7,31}} | collective-permute-start | bytes 2383880 | tf_op jit(solution)/shard_map/ppermute | solution.py:607
  670.4 43.6 %collective-permute-start.65 = (bf16[3104,128]{1,0:T(8,128)(2,1)S(1)}, bf16[3104,128]{1,0:T(8,128)(2,1)S(1)}, u32[]{:S(2)}, u32[]{:S(2)}) collective-permute-start(bf16[3104,128]{1,0:T(8,128)(2,1)S(1)} %copy-done.3), channel_id=1, source_target_pairs={{8,16},{17,25},{10,18},{19,27},{12,20},{21,29},{14,22},{23,31}} | collective-permute-start | bytes 2383880 | tf_op jit(solution)/shard_map/ppermute | solution.py:607
  671.3 42.6 %collective-permute-start.66 = (bf16[3104,128]{1,0:T(8,128)(2,1)S(1)}, bf16[3104,128]{1,0:T(8,128)(2,1)S(1)}, u32[]{:S(2)}, u32[]{:S(2)}) collective-permute-start(bf16[3104,128]{1,0:T(8,128)(2,1)S(1)} %copy-done.3), channel_id=1, source_target_pairs={{0,16},{9,25},{2,18},{11,27},{4,20},{13,29},{6,22},{15,31}} | collective-permute-start | bytes 2383880 | tf_op jit(solution)/shard_map/ppermute | solution.py:607
  701.4 149.4 %collective-permute-start.100 = (f32[4]{0:T(128)S(1)}, f32[4]{0:T(128)S(1)}, u32[]{:S(2)}, u32[]{:S(2)}) collective-permute-start(f32[4]{0:T(128)S(1)} %pad_maximum_fusion.25), channel_id=1, source_target_pairs={{0,4},{4,0},{1,5},{5,1},{2,6},{6,2},{3,7},{7,3},{8,12},{12,8},{9,1... | collective-permute-start | bytes 56 | tf_op jit(solution)/shard_map/ppermute | solution.py:1311
  740.3 47.7 %collective-permute-start.68 = (bf16[2,2,2,512,128]{3,4,2,1,0:T(8,128)(2,1)}, bf16[2,2,2,512,128]{3,4,2,1,0:T(8,128)(2,1)}, u32[]{:S(2)}, u32[]{:S(2)}) collective-permute-start(bf16[2,2,2,512,128]{3,4,2,1,0:T(8,128)(2,1)} %bitcast.282), channel_id=1, source_target_pairs={{0,1},{1,0},{2,3},{3,2},{4,5},{5,4},{6,7},{7,6},{8,9},{9,8},{10,11... | collective-permute-start | bytes 3145736 | tf_op jit(solution)/shard_map/ppermute | solution.py:1301
  756.5 71.1 %collective-permute-start.77 = (bf16[2,3104,128]{2,1,0:T(8,128)(2,1)}, bf16[2,3104,128]{2,1,0:T(8,128)(2,1)}, u32[]{:S(2)}, u32[]{:S(2)}) collective-permute-start(bf16[2,3104,128]{2,1,0:T(8,128)(2,1)} %pad_maximum_fusion.8.refs_8_), channel_id=1, source_target_pairs={{0,2},{2,0},{1,3},{3,1},{4,6},{6,4},{5,7},{7,5},{8,10},{10,8},{9,1... | collective-permute-start | bytes 4767752 | tf_op jit(solution)/shard_map/ppermute | solution.py:607
  768.3 61.4 %collective-permute-start.76 = (bf16[2,3104,128]{2,1,0:T(8,128)(2,1)}, bf16[2,3104,128]{2,1,0:T(8,128)(2,1)}, u32[]{:S(2)}, u32[]{:S(2)}) collective-permute-start(bf16[2,3104,128]{2,1,0:T(8,128)(2,1)} %pad_maximum_fusion.7.refs_7_), channel_id=1, source_target_pairs={{0,4},{4,0},{1,5},{5,1},{2,6},{6,2},{3,7},{7,3},{8,12},{12,8},{9,1... | collective-permute-start | bytes 4767752 | tf_op jit(solution)/shard_map/ppermute | solution.py:607
  791.8 34.2 %collective-permute-start.69 = (bf16[2,2,512,128]{2,3,1,0:T(8,128)(2,1)}, bf16[2,2,512,128]{2,3,1,0:T(8,128)(2,1)}, u32[]{:S(2)}, u32[]{:S(2)}) collective-permute-start(bf16[2,2,512,128]{2,3,1,0:T(8,128)(2,1)} %dynamic-slice_bitcast_fusion.20), channel_id=1, source_target_pairs={{0,4},{4,0},{1,5},{5,1},{2,6},{6,2},{3,7},{7,3},{8,12},{12,8},{9,1... | collective-permute-start | bytes 1572872 | tf_op jit(solution)/shard_map/ppermute | solution.py:1301
  844.2 22.4 %collective-permute-start.78 = (bf16[3200,128]{1,0:T(8,128)(2,1)S(1)}, bf16[3200,128]{1,0:T(8,128)(2,1)S(1)}, u32[]{:S(2)}, u32[]{:S(2)}) collective-permute-start(bf16[3200,128]{1,0:T(8,128)(2,1)S(1)} %constant_dynamic-slice_fusion), channel_id=1, source_target_pairs={{0,1},{1,0},{2,3},{3,2},{4,5},{5,4},{6,7},{7,6},{8,9},{9,8},{10,11... | collective-permute-start | bytes 2457608 | tf_op jit(solution)/shard_map/ppermute | solution.py:607
  864.1 41.4 %collective-permute-start.104 = (f32[4]{0:T(128)S(1)}, f32[4]{0:T(128)S(1)}, u32[]{:S(2)}, u32[]{:S(2)}) collective-permute-start(f32[4]{0:T(128)S(1)} %add.756), channel_id=1, source_target_pairs={{0,16},{16,0},{8,24},{24,8},{1,17},{17,1},{9,25},{25,9},{2,18},{18... | collective-permute-start | bytes 56 | tf_op jit(solution)/shard_map/ppermute | solution.py:1313
  865.9 41.0 %collective-permute-start.90 = (bf16[3104,128]{1,0:T(8,128)(2,1)S(1)}, bf16[3104,128]{1,0:T(8,128)(2,1)S(1)}, u32[]{:S(2)}, u32[]{:S(2)}) collective-permute-start(bf16[3104,128]{1,0:T(8,128)(2,1)S(1)} %dynamic-slice_bitcast_fusion.3.refs_6_), channel_id=1, source_target_pairs={{0,2},{2,0},{1,3},{3,1},{4,6},{6,4},{5,7},{7,5},{8,10},{10,8},{9,1... | collective-permute-start | bytes 2383880 | tf_op jit(solution)/shard_map/ppermute | solution.py:607
  866.5 45.9 %collective-permute-start.73 = (f32[1024]{0:T(1024)S(1)}, f32[1024]{0:T(1024)S(1)}, u32[]{:S(2)}, u32[]{:S(2)}) collective-permute-start(f32[1024]{0:T(1024)S(1)} %add.715), channel_id=1, source_target_pairs={{0,1},{1,0},{2,3},{3,2},{4,5},{5,4},{6,7},{7,6},{8,9},{9,8},{10,11... | collective-permute-start | bytes 12296 | tf_op jit(solution)/shard_map/ppermute | solution.py:1311
  884.2 39.6 %collective-permute-start.95 = (bf16[3104,128]{1,0:T(8,128)(2,1)S(1)}, bf16[3104,128]{1,0:T(8,128)(2,1)S(1)}, u32[]{:S(2)}, u32[]{:S(2)}) collective-permute-start(bf16[3104,128]{1,0:T(8,128)(2,1)S(1)} %fusion.19), channel_id=1, source_target_pairs={{8,0},{17,9},{10,2},{19,11},{12,4},{21,13},{14,6},{23,15}} | collective-permute-start | bytes 2383880 | tf_op jit(solution)/shard_map/ppermute | solution.py:607
  912.4 60.5 %collective-permute-start.96 = (bf16[3104,128]{1,0:T(8,128)(2,1)S(1)}, bf16[3104,128]{1,0:T(8,128)(2,1)S(1)}, u32[]{:S(2)}, u32[]{:S(2)}) collective-permute-start(bf16[3104,128]{1,0:T(8,128)(2,1)S(1)} %fusion.19), channel_id=1, source_target_pairs={{16,0},{25,9},{18,2},{27,11},{20,4},{29,13},{22,6},{31,15}} | collective-permute-start | bytes 2383880 | tf_op jit(solution)/shard_map/ppermute | solution.py:607
  913.7 63.0 %collective-permute-start.97 = (bf16[3104,128]{1,0:T(8,128)(2,1)S(1)}, bf16[3104,128]{1,0:T(8,128)(2,1)S(1)}, u32[]{:S(2)}, u32[]{:S(2)}) collective-permute-start(bf16[3104,128]{1,0:T(8,128)(2,1)S(1)} %fusion.19), channel_id=1, source_target_pairs={{24,0},{1,9},{26,2},{3,11},{28,4},{5,13},{30,6},{7,15}} | collective-permute-start | bytes 2383880 | tf_op jit(solution)/shard_map/ppermute | solution.py:607
  915.0 62.9 %collective-permute-start.91 = (bf16[3104,128]{1,0:T(8,128)(2,1)S(1)}, bf16[3104,128]{1,0:T(8,128)(2,1)S(1)}, u32[]{:S(2)}, u32[]{:S(2)}) collective-permute-start(bf16[3104,128]{1,0:T(8,128)(2,1)S(1)} %fusion.20), channel_id=1, source_target_pairs={{8,0},{17,9},{10,2},{19,11},{12,4},{21,13},{14,6},{23,15}} | collective-permute-start | bytes 2383880 | tf_op jit(solution)/shard_map/ppermute | solution.py:607
  922.4 59.1 %collective-permute-start.92 = (bf16[3104,128]{1,0:T(8,128)(2,1)S(1)}, bf16[3104,128]{1,0:T(8,128)(2,1)S(1)}, u32[]{:S(2)}, u32[]{:S(2)}) collective-permute-start(bf16[3104,128]{1,0:T(8,128)(2,1)S(1)} %fusion.20), channel_id=1, source_target_pairs={{16,0},{25,9},{18,2},{27,11},{20,4},{29,13},{22,6},{31,15}} | collective-permute-start | bytes 2383880 | tf_op jit(solution)/shard_map/ppermute | solution.py:607
  923.7 62.8 %collective-permute-start.93 = (bf16[3104,128]{1,0:T(8,128)(2,1)S(1)}, bf16[3104,128]{1,0:T(8,128)(2,1)S(1)}, u32[]{:S(2)}, u32[]{:S(2)}) collective-permute-start(bf16[3104,128]{1,0:T(8,128)(2,1)S(1)} %fusion.20), channel_id=1, source_target_pairs={{24,0},{1,9},{26,2},{3,11},{28,4},{5,13},{30,6},{7,15}} | collective-permute-start | bytes 2383880 | tf_op jit(solution)/shard_map/ppermute | solution.py:607
  972.9 38.1 %collective-permute-start.99 = (bf16[3104,128]{1,0:T(8,128)(2,1)S(1)}, bf16[3104,128]{1,0:T(8,128)(2,1)S(1)}, u32[]{:S(2)}, u32[]{:S(2)}) collective-permute-start(bf16[3104,128]{1,0:T(8,128)(2,1)S(1)} %copy-done.38), channel_id=1, source_target_pairs={{0,1},{9,8},{16,17},{25,24},{2,3},{11,10},{18,19},{27,26},{4,5},{1... | collective-permute-start | bytes 2383880 | tf_op jit(solution)/shard_map/ppermute | solution.py:607
  976.7 28.5 %collective-permute-start.74 = (f32[1024]{0:T(1024)S(1)}, f32[1024]{0:T(1024)S(1)}, u32[]{:S(2)}, u32[]{:S(2)}) collective-permute-start(f32[1024]{0:T(1024)S(1)} %add.716), channel_id=1, source_target_pairs={{0,8},{8,0},{16,24},{24,16},{1,9},{9,1},{17,25},{25,17},{2,10},{10... | collective-permute-start | bytes 12296 | tf_op jit(solution)/shard_map/ppermute | solution.py:1313
  987.5 23.5 %collective-permute-start.98 = (bf16[3104,128]{1,0:T(8,128)(2,1)S(1)}, bf16[3104,128]{1,0:T(8,128)(2,1)S(1)}, u32[]{:S(2)}, u32[]{:S(2)}) collective-permute-start(bf16[3104,128]{1,0:T(8,128)(2,1)S(1)} %get-tuple-element.92), channel_id=1, source_target_pairs={{0,1},{9,8},{16,17},{25,24},{2,3},{11,10},{18,19},{27,26},{4,5},{1... | collective-permute-start | bytes 2383880 | tf_op jit(solution)/shard_map/ppermute | solution.py:607
  (241 other events, 2969.6 us)

commit v6 on v5

--- a/solution.py
+++ b/solution.py
@@ -237,44 +237,69 @@
     return [pl.BlockSpec(memory_space=pltpu.HBM)] * len(after)
 
 
+def fence(values, after):
+    def kernel(*refs):
+        del refs
+
+    return pl.pallas_call(
+        kernel,
+        in_specs=pins(values) + pins(after),
+        out_specs=pins(values),
+        out_shape=[jax.ShapeDtypeStruct(value.shape, value.dtype) for value in values],
+        input_output_aliases={k: k for k in range(len(values))},
+        name="fence",
+    )(*values, *after)
+
+
+def bracket(call, flows):
+    out = call([value for flow in flows for value in flow.values()])
+    for flow in flows:
+        flow.go()
+    return fence(out if isinstance(out, (list, tuple)) else [out], [v for flow in flows for v in flow.values()])
+
+
 def gather_lines(params):
     z, y, x, c = (lax.axis_index(name) for name in GRID)
     lines = jnp.pad(params.reshape(SHARD, LINE), ((0, SPAD - SHARD), (0, 0)))
     sibling = lax.ppermute(lines, ZC, [(2 * k + 1 - k % 2, 2 * k + k % 2) for k in range(4)])
-    batches = []
-    for batch in range(2):
-        buffers = []
-        for part in range(2):
-            here = jnp.where(c == part, lines, sibling)
-            if batch == 0:
-                one = lax.ppermute(here, ZC, zc_pairs((0, 1, 0), (1, 2, 1)))
-                side = lax.ppermute(here, ZC, zc_pairs((1, 0, 1)))
-                two = lax.ppermute(one, ZC, zc_pairs((1, 2, 0), (2, 3, 1)))
-                three = lax.ppermute(two, ZC, zc_pairs((2, 3, 0)))
-            else:
-                one = lax.ppermute(here, ZC, zc_pairs((2, 1, 0), (3, 2, 1)))
-                side = lax.ppermute(here, ZC, zc_pairs((2, 3, 0)))
-                two = lax.ppermute(one, ZC, zc_pairs((1, 0, 0), (2, 1, 1)))
-                three = lax.ppermute(two, ZC, zc_pairs((1, 0, 1)))
-            mine = z == 2 * batch + c
-            column = jnp.where(mine, here, one + side + two + three)
-            over_x = lax.ppermute(column, "x", SWAP)
-            over_y = lax.ppermute(column, "y", SWAP)
-            if part == 0:
-                corner = lax.ppermute(over_x, "y", SWAP)
-            else:
-                corner = lax.ppermute(over_y, "x", SWAP)
-            local = [column, over_x, over_y, corner]
-            buffers += local + [lax.ppermute(piece, "c", SWAP) for piece in local]
-        batches.append(buffers)
+    buffers = []
+    for part in range(2):
+        here = jnp.where(c == part, lines, sibling)
+        one = lax.ppermute(here, ZC, zc_pairs((0, 1, 0), (1, 2, 1)))
+        side = lax.ppermute(here, ZC, zc_pairs((1, 0, 1)))
+        two = lax.ppermute(one, ZC, zc_pairs((1, 2, 0), (2, 3, 1)))
+        three = lax.ppermute(two, ZC, zc_pairs((2, 3, 0)))
+        column = jnp.where(z == c, here, one + side + two + three)
+        over_x = lax.ppermute(column, "x", SWAP)
+        over_y = lax.ppermute(column, "y", SWAP)
+        corner = lax.ppermute(over_y if part else over_x, "x" if part else "y", SWAP)
+        local = [column, over_x, over_y, corner]
+        buffers += [piece[None] for piece in local]
+        buffers += [lax.ppermute(piece, "c", SWAP)[None] for piece in local]
+    early = [(k, 0) for k in range(16)]
+    here = jnp.where(c == 0, jnp.stack([lines, sibling]), jnp.stack([sibling, lines]))
+    one = lax.ppermute(here, ZC, zc_pairs((2, 1, 0), (3, 2, 1)))
+    side = lax.ppermute(here, ZC, zc_pairs((2, 3, 0)))
+    two = lax.ppermute(one, ZC, zc_pairs((1, 0, 0), (2, 1, 1)))
+    three = lax.ppermute(two, ZC, zc_pairs((1, 0, 1)))
+    column = jnp.where(z == 2 + c, here, one + side + two + three)
+    over_x = lax.ppermute(column, "x", SWAP)
+    over_y = lax.ppermute(column, "y", SWAP)
+    corners = [lax.ppermute(over_x[:1], "y", SWAP), lax.ppermute(over_y[1:], "x", SWAP)]
+    local = [column, over_x, over_y] + corners
+    buffers += local + [lax.ppermute(piece, "c", SWAP) for piece in local]
+    late = []
+    for part in range(2):
+        for first in (16, 21):
+            late += [(first, part), (first + 1, part), (first + 2, part), (first + 3 + part, 0)]
     shard = np.arange(32)
     sz, sy, sx, sc = shard // 8, shard // 4 % 2, shard // 2 % 2, shard % 2
     away = jnp.where(sz % 2 == c, 0, 4)
     where = sc * 8 + away + 2 * (sy ^ y) + (sx ^ x) + 16 * (sz // 2)
-    return batches, where.astype(jnp.int32)
-
-
-def unpack_lines(buffers, first, where, segments, after=()):
+    return buffers, (early, early + late), where.astype(jnp.int32)
+
+
+def unpack_lines(buffers, slots, where, segments, after=()):
     jobs, starts = [], []
     reach = 0
     for offset, rows, columns in segments:
@@ -320,27 +345,27 @@
         def fetch(job, slot):
             owner = table_ref[job, 0]
             begin = pl.multiple_of(table_ref[job, 1], 16)
-            for b in range(count_buffers):
-
-                @pl.when(where_ref[owner] == first + b)
+            for b, (source, part) in enumerate(slots):
+
+                @pl.when(where_ref[owner] == b)
                 def _():
                     pltpu.make_async_copy(
-                        sources[b].at[pl.ds(begin, window), :], raw.at[slot, 0], in_sem.at[slot, 0]
+                        sources[source].at[part, pl.ds(begin, window), :], raw.at[slot, 0], in_sem.at[slot, 0]
                     ).start()
 
             @pl.when(table_ref[job, 3] == 1)
             def _():
-                for b in range(count_buffers):
-
-                    @pl.when(where_ref[owner + 1] == first + b)
+                for b, (source, part) in enumerate(slots):
+
+                    @pl.when(where_ref[owner + 1] == b)
                     def _():
                         pltpu.make_async_copy(
-                            sources[b].at[pl.ds(0, window), :], raw.at[slot, 1], in_sem.at[slot, 1]
+                            sources[source].at[part, pl.ds(0, window), :], raw.at[slot, 1], in_sem.at[slot, 1]
                         ).start()
 
         def fetched(slot, half):
             return pltpu.make_async_copy(
-                sources[0].at[pl.ds(0, window), :], raw.at[slot, half], in_sem.at[slot, half]
+                sources[0].at[0, pl.ds(0, window), :], raw.at[slot, half], in_sem.at[slot, half]
             )
 
         @pl.when(step == 0)
@@ -601,7 +626,7 @@
         self.result = None
 
     def values(self):
-        return [value for value, _, _ in self.sends]
+        return [value for value, _, _ in self.sends] or [self.result]
 
     def go(self):
         arrived = [lax.ppermute(value, axis, pairs) for value, axis, pairs in self.sends]
@@ -637,8 +662,9 @@
         hops = [((1, 0, 0), (2, 1, 1)), ((2, 0, 0), (3, 1, 1)), ((3, 0, 0), (0, 1, 1))]
     else:
         hops = [((1, 2, 0), (2, 3, 1)), ((0, 2, 0), (1, 3, 1)), ((3, 2, 0), (0, 3, 1))]
-    got = yield [(column, ZC, zc_pairs(*hop)) for column in columns for hop in hops]
-    ends = [added(columns[0], *got[:3]), added(columns[1], *got[3:])]
+    columns = jnp.stack(columns)
+    got = yield [(columns, ZC, zc_pairs(*hop)) for hop in hops]
+    ends = added(columns, *got)
     mine = jnp.where(c == 0, ends[0], ends[1])
     other = jnp.where(c == 0, ends[1], ends[0])
     (handed,) = yield [(other, ZC, [(2 * k + k % 2, 2 * k + 1 - k % 2) for k in range(4)])]
@@ -1075,12 +1101,20 @@
     if not fast:
         ident = (jnp.ones_like(wide), jnp.zeros_like(state))
         return (carried_in if backward else prefix)((wide, state), span, chain_states, ident)[1]
-    total = (wide, state)
+    flow = Flow(scan_stages(carry, state, backward))
+    while flow.sends:
+        flow.go()
+    return flow.result
+
+
+def scan_stages(carry, state, backward):
+    total = (jnp.repeat(carry, SSM_DIM)[None, :], state)
     start = None
     for name in ("c", "x", "y"):
         place = lax.axis_index(name)
         packed = jnp.concatenate([total[1], jnp.broadcast_to(total[0], (16, INNER))], axis=0)
-        packed = lax.ppermute(packed.astype(jnp.bfloat16), name, SWAP).astype(jnp.float32)
+        (packed,) = yield [(packed.astype(jnp.bfloat16), name, SWAP)]
+        packed = packed.astype(jnp.float32)
         other = (packed[STATE : STATE + 1], packed[:STATE])
         leads = place == (0 if backward else 1)
         seen = (jnp.where(leads, other[0], 1.0), jnp.where(leads, other[1], 0.0))
@@ -1293,12 +1327,20 @@
 def scatter_span(value, span, fast):
     if not fast:
         return lax.psum_scatter(value, span, scatter_dimension=0).astype(jnp.float32)
+    flow = Flow(scatter_stages(value))
+    while flow.sends:
+        flow.go()
+    return flow.result
+
+
+def scatter_stages(value):
     _, y, x, c = (lax.axis_index(name) for name in GRID)
     value = value.reshape((2, 2, 2) + value.shape[1:])
     for name, place, axis in (("c", c, 2), ("y", y, 0), ("x", x, 0)):
+        send = lax.dynamic_index_in_dim(value, 1 - place, axis, keepdims=False)
+        (arrived,) = yield [(send, name, SWAP)]
         keep = lax.dynamic_index_in_dim(value, place, axis, keepdims=False)
-        send = lax.dynamic_index_in_dim(value, 1 - place, axis, keepdims=False)
-        value = keep.astype(jnp.float32) + lax.ppermute(send, name, SWAP).astype(jnp.float32)
+        value = keep.astype(jnp.float32) + arrived.astype(jnp.float32)
         if name != "x":
             value = value.astype(jnp.bfloat16)
     return value
@@ -1324,11 +1366,11 @@
 
 def early_weights(params):
     places = offsets_of()
-    (early, late), where = gather_lines(params)
+    buffers, (slots, all_slots), where = gather_lines(params)
     names = (W_QUERY, W_KEY, W_VALUE, W_ATTN_OUT, W_GATE_SSM, W_X_SSM, W_B_C)
     misc_at = places[W_STEP][0]
     first = unpack_lines(
-        early, 0, where, [flat_segment(name_key) for name_key in names] + [(0, 16, LINE), (misc_at, 288, LINE)]
+        buffers[:16], slots, where, [flat_segment(name_key) for name_key in names] + [(0, 16, LINE), (misc_at, 288, LINE)]
     )
     weights = dict(zip(names, first))
     weights[NORM_ATTN] = first[-2].reshape(-1)[:D]
@@ -1336,7 +1378,7 @@
     for name_key in (W_STEP,) + small_names[1:-1]:
         at, extent = places[name_key]
         weights[name_key] = misc[at - misc_at : at - misc_at + math.prod(extent)].reshape(extent)
-    return weights, (early + late, where)
+    return weights, (buffers, all_slots, where)
 
 
 def flat_segment(name_key):
@@ -1345,11 +1387,11 @@
 
 
 def late_weights(held, after):
-    buffers, where = held
+    buffers, slots, where = held
     names = (W_SSM_OUT, W_GATE, W_UP_PROJ, W_DOWN)
     norm_at = offsets_of()[NORM_FFN][0]
     second = unpack_lines(
-        buffers, 0, where, [flat_segment(name_key) for name_key in names] + [(norm_at, 16, LINE)], after
+        buffers, slots, where, [flat_segment(name_key) for name_key in names] + [(norm_at, 16, LINE)], after
     )
     weights = dict(zip(names, second))
     weights[NORM_FFN] = second[-1].reshape(-1)[norm_at % LINE : norm_at % LINE + D]
@@ -1515,8 +1557,6 @@
             jnp.sum(ffn_out * ffn_out),
         ]
     )
-    totals = sum_all(squares, group + span, fast)
-    stats = jnp.sqrt(totals / (all_rows * D))
     grad_out = cotangent.astype(jnp.float32)
     grad_activation = matmul_right_t(cotangent, weights[W_DOWN])
     grad_gate_f32, grad_upper_f32 = swiglu_back(grad_activation)
@@ -1532,19 +1572,29 @@
     grad_ssm_low = matmul_right_t(grad_branch, weights[W_SSM_OUT])
     grad_ssm_y, grad_gate_ssm_f32, grad_norm_ssm = gnorm_back(grad_ssm_low)
     grad_state_local = weighted_state(conv_values, PAIRS + 1, grad_ssm_y, entry_rows)
-    pinned_by = ()
     if fast:
-        late = pack_late(
-            (hidden_two, grad_gate), (hidden_two, grad_upper), (activation, cotangent),
-            ssm_low, grad_branch, grad_norm_ffn, [grad_state_local],
+        scan = Flow(scan_stages(carry_all, grad_state_local, True))
+        (late,) = bracket(
+            lambda after: pack_late(
+                (hidden_two, grad_gate), (hidden_two, grad_upper), (activation, cotangent),
+                ssm_low, grad_branch, grad_norm_ffn, after,
+            ),
+            [scan],
         )
         late_flow = Flow(reduce_stages(late, 1, 14))
-        early = pack_out(ssm_low, grad_branch, late_flow.values())
+        (early,) = bracket(lambda after: pack_out(ssm_low, grad_branch, after + late_flow.values()), [scan])
+        scan.go()
         late_flow.go()
-        pinned_by = late_flow.values()
-    grad_state_out = scan_states(carry_all, grad_state_local, span, fast, True)
-    grad_x, grad_b, grad_c, grad_small = ssm_backward(
-        conv_values, grad_ssm_y, chunk_cum, step_rows, state_in, grad_state_out, skip_wide, ssm_meta, start_row, pinned_by
+        grad_state_out = scan.result
+        around = lambda call: bracket(call, [late_flow])
+    else:
+        grad_state_out = scan_states(carry_all, grad_state_local, span, fast, True)
+        around = lambda call: call(())
+    grad_x, grad_b, grad_c, grad_small = around(
+        lambda after: ssm_backward(
+            conv_values, grad_ssm_y, chunk_cum, step_rows, state_in, grad_state_out, skip_wide, ssm_meta, start_row,
+            after,
+        )
     )
     grad_direct = grad_small[:, 0:2].reshape(SSM_HEADS, rows_dev)
     grad_logs = grad_small[:, 2:4].reshape(SSM_HEADS, rows_dev)
@@ -1553,12 +1603,11 @@
     grad_step_bias = jnp.sum(grad_step_rows, axis=1)
     grad_step_raw_f32 = grad_step_rows.T
     grad_skip_gain = jnp.sum(grad_small[:, 4, : 2 * SSM_DIM].reshape(SSM_HEADS, SSM_DIM), axis=1)
-    if fast:
-        late_flow.go()
-        pinned_by = late_flow.values()
-    grad_main, grad_tail, grad_edge, grad_taps = conv_backward(
-        grad_x, grad_b, grad_c, xbc, rim_rows, small_f32[CONV_WEIGHT], conv_bias, ssm_meta,
-        row_starts[:, None], pinned_by,
+    grad_main, grad_tail, grad_edge, grad_taps = around(
+        lambda after: conv_backward(
+            grad_x, grad_b, grad_c, xbc, rim_rows, small_f32[CONV_WEIGHT], conv_bias, ssm_meta,
+            row_starts[:, None], after,
+        )
     )
     grad_conv_weight = grad_taps[:CONV]
     grad_conv_bias = grad_taps[CONV]
@@ -1586,8 +1635,8 @@
     }
     g_low = grad_attended.reshape(rows_dev, HEADS_Q, HEAD_DIM).transpose(1, 0, 2)
     g_wide = jnp.pad(g_low, ((0, 0), (0, 0), (HEAD_DIM, 0)))
+    parts = []
     if fast:
-        late_flow.go()
         early = pack_ssm(
             early,
             [
@@ -1596,26 +1645,43 @@
             ],
             small, ssm_low, grad_branch, late_flow.values(),
         )
-        late_flow.go()
         early_flow = Flow(reduce_stages(early, 0, 8))
-        pinned_by = early_flow.values()
-    parts = []
+        around = lambda call: bracket(call, [early_flow])
     for group_at in range(HEADS_KV):
+        after_part = [part[1] for part in parts]
+        if fast and group_at == 0:
+            after_part = late_flow.values()
         parts.append(
-            attention_backward(q_wide, g_wide, key_blocks, logs, mixed, meta, start_row, group_at, pinned_by)
+            around(
+                lambda after: attention_backward(
+                    q_wide, g_wide, key_blocks, logs, mixed, meta, start_row, group_at, (*after, *after_part)
+                )
+            )
         )
-        if fast:
-            early_flow.go()
-            pinned_by = early_flow.values() + late_flow.values() + [parts[-1][1]]
     grad_kv = jnp.concatenate([part[0] for part in parts], axis=1)
     grad_q_turned = jnp.concatenate([part[1] for part in parts], axis=0)
     if rows_dev != KEYS:
         grad_kv = grad_kv.transpose(1, 0, 2, 3).reshape(HEADS_KV, -1, rows_dev, PAIR).transpose(1, 0, 2, 3)
-    grad_kv_mine = scatter_span(grad_kv, span, fast)
+    if fast:
+        late_flow.go()
+        scatter = Flow(scatter_stages(grad_kv))
+        (grad_q_turned,) = fence([grad_q_turned], scatter.values() + early_flow.values() + late_flow.values())
+    grad_q_rot = grad_q_turned.reshape(HEADS_Q * HEAD_DIM, rows_dev).T * score_scale
+    grad_query_low = rotate(grad_q_rot, cosine, -sine, HEADS_Q).astype(jnp.bfloat16)
+    if fast:
+        scatter.go()
+        (grad_query_low,) = fence([grad_query_low], scatter.values())
+    grad_hidden = grad_hidden_ssm + matmul_right_t(grad_query_low, weights[W_QUERY])
+    if fast:
+        scatter.go()
+        early_flow.go()
+        (grad_hidden,) = fence([grad_hidden], scatter.values() + early_flow.values())
+        scatter.go()
+        grad_kv_mine = scatter.result
+    else:
+        grad_kv_mine = scatter_span(grad_kv, span, fast)
     grad_keys_mine = grad_kv_mine[:, :, :HEAD_DIM].transpose(1, 0, 2).reshape(rows_dev, -1)
     grad_values_mine = grad_kv_mine[:, :, HEAD_DIM:].transpose(1, 0, 2).reshape(rows_dev, -1)
-    grad_q_rot = grad_q_turned.reshape(HEADS_Q * HEAD_DIM, rows_dev).T * score_scale
-    grad_query_low = rotate(grad_q_rot, cosine, -sine, HEADS_Q).astype(jnp.bfloat16)
     grad_key_low = rotate(grad_keys_mine, cosine, -sine, HEADS_KV).astype(jnp.bfloat16)
     grad_value_low = grad_values_mine.astype(jnp.bfloat16)
     if fast:
@@ -1623,24 +1689,25 @@
             [(hidden, grad_query_low), (hidden, grad_key_low), (hidden, grad_value_low)],
             attended, grad_branch, early_flow.values(),
         )
-        early_flow.go()
         corner_flow = Flow(corner_stages(corner))
         for flow in (early_flow, late_flow, corner_flow):
             while flow.sends:
                 flow.go()
     grad_hidden = (
-        grad_hidden_ssm
-        + matmul_right_t(grad_query_low, weights[W_QUERY])
+        grad_hidden
         + matmul_right_t(grad_key_low, weights[W_KEY])
         + matmul_right_t(grad_value_low, weights[W_VALUE])
     )
     grad_x_norm, grad_norm_attn = norm_one_back(grad_hidden)
     grad_tokens = grad_middle + grad_x_norm
     if fast:
-        norms = sum_all(grad_norm_attn, group + span, fast)
+        ends = sum_all(jnp.concatenate([grad_norm_attn, squares]), group + span, fast)
+        norms, totals = ends[:D], ends[D:]
+        stats = jnp.sqrt(totals / (all_rows * D))
         grad_shard = own_lines(early_flow.result, late_flow.result, corner_flow.result, norms)
         return (result.astype(jnp.bfloat16), grad_tokens, grad_shard, stats)
     small[NORM_ATTN] = grad_norm_attn
+    stats = jnp.sqrt(sum_all(squares, group + span, fast) / (all_rows * D))
     pairs = {
         W_QUERY: (hidden, grad_query_low),
         W_KEY: (hidden, grad_key_low),

time: 1020 us -> 946 us (0.927)
  starting transfers between devices: 298 us -> 215 us
    ppermute x13 -> x12, waiting for transfers between devices: 88.8 us -> 25.3 us  [the longest x1 13.7 us: gather_lines(): lax.ppermute(over_y[1:], 'x', SWAP)]
    ppermute x13 -> x12, starting transfers between devices: 61.7 us -> 16.1 us  [the longest x8 11.8 us: gather_lines(): buffers += [lax.ppermute(piece, 'c', SWAP)[None] for piece in local]]
    ppermute x16 -> x5, starting transfers between devices: 40.7 us -> 0.7 us  [gather_lines(): buffers += local + [lax.ppermute(piece, 'c', SWAP) for piece in local]]
    ppermute x4 -> x2, starting transfers between devices: 5.2 us -> 41.5 us  [sum_all(): value = value + lax.ppermute(value, 'z', pairs)]
    ppermute x36 -> x39, waiting for transfers between devices: 88.6 us -> 124 us  [go(): lax.ppermute(value, axis, pairs)]
    ppermute x4 -> x2, waiting for transfers between devices: 3.49 us -> 30.8 us  [sum_all(): value = value + lax.ppermute(value, 'z', pairs)]
    ppermute x4 -> x3, starting transfers between devices: 2.75 us -> 29.3 us  [gather_lines(): over_y = lax.ppermute(column, 'y', SWAP)]
    ppermute x36 -> x39, starting transfers between devices: 115 us -> 95.3 us  [go(): lax.ppermute(value, axis, pairs)]
  transfers between devices with their start and end apart: 105 -> 85, of which waited for: 31 -> 32; matrix products, arithmetic and copies ran while one was open for 19% -> 18% of each run, Pallas kernels for 13% -> 16%
where the time goes in v6:
time: 946 us; the launch traced here: 937 us
  waiting for transfers between devices  230 us (24%)
  starting transfers between devices  215 us (23%)
  Pallas kernels  204 us (22%)
  other arithmetic  122 us (13%)
  local copies, waits for them, and re-layouts  90.2 us (10%)
  matrix products  70.9 us (7%)
    ppermute x39, waiting for transfers between devices, go(): lax.ppermute(value, axis, pairs)  124 us
    ppermute x39, starting transfers between devices, go(): lax.ppermute(value, axis, pairs)  95.3 us
    pallas_call x4, Pallas kernels, pack_lines(): pl.pallas_call(pinned(kernel, inputs, after), grid=(total,), in_specs=[le...  42.8 us
    ppermute x2, starting transfers between devices, sum_all(): value = value + lax.ppermute(value, 'z', pairs)  41.5 us
    pallas_call x2, Pallas kernels, unpack_lines(): pl.pallas_call(pinned(kernel, 2 + count_buffers, after), grid_spec=pltpu....  41.1 us
    pallas_call x1, Pallas kernels, ssm_backward(): pl.pallas_call(pinned(kernel, 11, after), grid_spec=pltpu.PrefetchScalarG...  40.5 us
    dot_general x12, matrix products, matmul_right_t(): lax.dot_general(left, right, (((1,), (1,)), ((), ())), preferred_element_...  38.4 us
    unnamed x439, local copies, waits for them, and re-layouts  30.9 us
  transfers between devices with their start and end apart: 85, of which 32 were waited for; matrix products, arithmetic and copies ran while one was open for 18% of the time, Pallas kernels for 16%

profile of v6, /device:TPU:0, one launch (start us, length us, event | category | flops | bytes accessed | tf_op | source)
XLA Modules:
  0.0 937.3 jit_solution(10306034975705520499)
XLA Ops:
  6.6 4.6 collective-permute-start.12
  15.7 4.9 collective-permute-done.12
  23.8 5.3 collective-permute-done.1
  43.1 9.1 collective-permute-start.8
  52.2 15.9 %collective-permute-done.32 = bf16[2,3088,128]{2,1,0:T(8,128)(2,1)} collective-permute-done((bf16[2,3088,128]{2,1,0:T(8,128)(2,1)}, bf16[2,3088,128]{2,1,0:T(8,128)(2,1)}, u32[]{:S(2)}, u32[]{:S(2)}) %collective-permute-start.32) | collective-permute-done | bytes 1581088 | tf_op jit(solution)/shard_map/ppermute | solution.py:283
  88.7 13.8 %collective-permute-done.6 = bf16[3088,128]{1,0:T(8,128)(2,1)S(1)} collective-permute-done((bf16[3088,128]{1,0:T(8,128)(2,1)S(1)}, bf16[3088,128]{1,0:T(8,128)(2,1)S(1)}, u32[]{:S(2)}, u32[]{:S(2)}) %collective-permute-start.6) | collective-permute-done | bytes 790560 | tf_op jit(solution)/shard_map/ppermute | solution.py:274
  105.1 7.2 collective-permute-done.7
  117.1 26.2 %collective-permute-start.35 = (bf16[2,3088,128]{2,1,0:T(8,128)(2,1)}, bf16[2,3088,128]{2,1,0:T(8,128)(2,1)}, u32[]{:S(2)}, u32[]{:S(2)}) collective-permute-start(bf16[2,3088,128]{2,1,0:T(8,128)(2,1)} %add_select_fusion.refs_18_), channel_id=1, source_target_pairs={{0,4},{4,0},{1,5},{5,1},{2,6},{6,2},{3,7},{7,3},{8,12},{12,8},{9,1... | collective-permute-start | bytes 4743176 | tf_op jit(solution)/shard_map/ppermute | solution.py:287
  146.4 14.4 %unpack.2 = (bf16[1024,512]{1,0:T(8,128)(2,1)}, bf16[1024,128]{1,0:T(8,128)(2,1)S(1)}, bf16[1024,128]{1,0:T(8,128)(2,1)S(1)}, bf16[512,1024]{1,0:T(8,128)(2,1)},...) custom-call(s32[25,5]{1,0:T(8,128)S(1)} %copy-done.61, ...), custom_call_target="tpu_custom_call" | custom-call | bytes 26624000 | tf_op jit(solution)/shard_map/unpack/pallas_call | solution.py:434
  187.5 12.2 %conv.1.refs_0_.refs_1_.x_ref.b_ref.c_ref.refs_3_.refs_4_ = f32[512,1792]{1,0:T(8,128)} custom-call(s32[5]{0:T(128)} %pad_add_fusion.1.meta_ref.refs_0_, f32[512,1792]{1,0:T(8,128)} %pad_maximum_fusion.x_ref.refs_4_, f32[8,1792]{1,0:T(8,128)} %copy-done.167, f32[4,1792]{1,0:T(4,128)} %reshape.392.weight_ref.refs_6_, f32[1,1792]{1,0:T(1,128)} %bitcast.361, ...), custom_call_target="tpu_custom_call" | custom-call | flops 1000000000 | bytes 7340032 | tf_op jit(solution)/shard_map/conv/pallas_call | solution.py:739
  199.6 9.2 state.2
  231.1 6.4 collective-permute-done.28
  247.5 5.9 collective-permute-done.29
  254.6 8.5 ssm.1
  274.8 13.7 %collective-permute-done.37.refs_22_ = bf16[1,3088,128]{2,1,0:T(8,128)(2,1)} collective-permute-done((bf16[1,3088,128]{2,1,0:T(8,128)(2,1)S(1)}, bf16[1,3088,128]{2,1,0:T(8,128)(2,1)}, u32[]{:S(2)}, u32[]{:S(2)}) %collective-permute-start.37) | collective-permute-done | bytes 790560 | tf_op jit(solution)/shard_map/ppermute | solution.py:288
  290.9 8.4 attend.1
  301.0 26.7 %unpack.3 = (bf16[1536,1024]{1,0:T(8,128)(2,1)}, bf16[1024,2048]{1,0:T(8,128)(2,1)}, bf16[1024,2048]{1,0:T(8,128)(2,1)}, bf16[2048,1024]{1,0:T(8,128)(2,1)}, bf16[16,128]{1,0:T(8,128)(2,1)S(1)}) custom-call(s32[31,5]{1,0:T(8,128)S(1)} %copy-done.60, s32[32]{0:T(128)S(1)} %fusion.73.refs_1_, bf16[1,3088,128]{2,1,0:T(8,128)(2,1)S(1)} %bitcast.292, ...), custom_call_target="tpu_custom_call" | custom-call | bytes 33013760 | tf_op jit(solution)/shard_map/unpack/pallas_call | solution.py:434
  327.9 6.7 fusion.100
  342.9 6.7 fusion.2
  354.6 4.6 multiply_reduce_fusion.3
  367.0 7.2 fusion.23
  374.2 9.6 %state.3 = f32[128,1536]{1,0:T(8,128)} custom-call(f32[512,1792]{1,0:T(8,128)} %conv.1.refs_0_.refs_1_.x_ref.b_ref.c_ref.refs_3_.refs_4_, f32[512,1536]{1,0:T(8,128)} %get-tuple-element.125.refs_1_.refs_2_, f32[12,2,512]{2,1,0:T(2,128)} %reshape.377.refs_2_), custom_call_target="tpu_custom_call" | custom-call | flops 201326592 | bytes 3145728 | tf_op jit(solution)/shard_map/state/pallas_call | solution.py:839
  385.0 7.3 collective-permute-start.43
  392.3 6.5 pad_maximum_fusion.2
  398.9 20.6 %pack.4.refs_0_ = bf16[49344,128]{1,0:T(8,128)(2,1)} custom-call(bf16[512,1024]{1,0:T(8,128)(2,1)S(1)} %copy-done.49, bf16[512,2048]{1,0:T(8,128)(2,1)S(1)} %copy-done.64, bf16[512,2048]{1,0:T(8,128)(2,1)} %get-tuple-element.201.refs_2_, bf16[512,2048]{1,0:T(8,128)(2,1)} %get-tuple-element.202.refs_3_, bf16[512,1024]{1,0:T(8,128)(2,1)S(1)} %copy-done.47, ...), custom_call_target="tpu_custom_call" | custom-call | flops 6442450944 | bytes 16777216 | tf_op jit(solution)/shard_map/pack/pallas_call | solution.py:589
  421.3 6.0 constant_dynamic-slice_fusion.2.refs_4_
  427.4 9.4 %collective-permute-start.44 = (bf16[144,1536]{1,0:T(8,128)(2,1)S(1)}, bf16[144,1536]{1,0:T(8,128)(2,1)}, u32[]{:S(2)}, u32[]{:S(2)}) collective-permute-start(bf16[144,1536]{1,0:T(8,128)(2,1)S(1)} %copy-done.21), channel_id=1, source_target_pairs={{0,2},{2,0},{1,3},{3,1},{4,6},{6,4},{5,7},{7,5},{8,10},{10,8},{9,1... | collective-permute-start | bytes 1327112 | tf_op jit(solution)/shard_map/ppermute | solution.py:632
  439.8 7.9 collective-permute-done.44
  450.1 32.2 %collective-permute-start.45 = (bf16[144,1536]{1,0:T(8,128)(2,1)}, bf16[144,1536]{1,0:T(8,128)(2,1)}, u32[]{:S(2)}, u32[]{:S(2)}) collective-permute-start(bf16[144,1536]{1,0:T(8,128)(2,1)} %pad_maximum_fusion.23.refs_1_), channel_id=1, source_target_pairs={{0,4},{4,0},{1,5},{5,1},{2,6},{6,2},{3,7},{7,3},{8,12},{12,8},{9,1... | collective-permute-start | bytes 1327112 | tf_op jit(solution)/shard_map/ppermute | solution.py:632
  482.3 5.8 add_convert_fusion.1
  492.3 4.7 pack.5.refs_0_
  501.7 40.5 %ssm_back.1 = (f32[512,1536]{1,0:T(8,128)S(1)}, f32[512,128]{1,0:T(8,128)S(1)}, f32[512,128]{1,0:T(8,128)S(1)}, f32[12,8,512]{2,1,0:T(8,128)S(1)}) custom-call(s32[5]{0:T(128)S(1)} %copy-done.62, f32[512,1792]{1,0:T(8,128)} %conv.1.refs_0_.refs_1_.x_ref.b_ref.c_ref.refs_3_.refs_4_, f32[512,1536]{1,0:T(8,128)S(1)} %copy-done.4, ...), custom_call_target="tpu_custom_call" | custom-call | flops 3000000000 | bytes 9437184 | tf_op jit(solution)/shard_map/ssm_back/pallas_call | solution.py:1049
  554.5 15.4 %conv_back.1 = (bf16[512,1792]{1,0:T(8,128)(2,1)}, f32[16,1792]{1,0:T(8,128)}, f32[8,1792]{1,0:T(8,128)}, f32[8,1792]{1,0:T(8,128)}) custom-call(s32[5]{0:T(128)} %pad_add_fusion.1.meta_ref.refs_0_, f32[512,1536]{1,0:T(8,128)} %get-tuple-element.75.refs_1_, f32[512,128]{1,0:T(8,128)} %get-tuple-element.76.refs_2_, f32[512,128]{1,0:T(8,128)} %get-tuple-element.77.refs_3_, ...), custom_call_target="tpu_custom_call" | custom-call | flops 2000000000 | bytes 9175040 | tf_op jit(solution)/shard_map/conv_back/pallas_call | solution.py:790
  584.3 12.1 %pack.6 = bf16[49440,128]{1,0:T(8,128)(2,1)} custom-call(bf16[512,512]{1,0:T(8,128)(2,1)S(1)} %bitcast.305, bf16[512,1024]{1,0:T(8,128)(2,1)S(1)} %copy-done.3, bf16[512,1024]{1,0:T(8,128)(2,1)S(1)} %fusion.82.refs_2_, bf16[512,1536]{1,0:T(8,128)(2,1)S(1)} %copy-done.12, bf16[512,1536]{1,0:T(8,128)(2,1)S(1)} %slice.388.refs_4_, ...), custom_call_target="tpu_custom_call", output_to_operand_aliasing={{}: (7, {})} | custom-call | flops 4026531840 | bytes 11010048 | tf_op jit(solution)/shard_map/pack/pallas_call | solution.py:589
  596.4 5.9 constant_dynamic-slice_fusion.1.refs_7_
  609.1 5.5 fusion.102
  627.9 7.8 attend_back.2
  635.8 17.2 %collective-permute-done.56 = bf16[2,3104,128]{2,1,0:T(8,128)(2,1)S(1)} collective-permute-done((bf16[2,3104,128]{2,1,0:T(8,128)(2,1)S(1)}, bf16[2,3104,128]{2,1,0:T(8,128)(2,1)S(1)}, u32[]{:S(2)}, u32[]{:S(2)}) %collective-permute-start.56) | collective-permute-done | bytes 1589280 | tf_op jit(solution)/shard_map/ppermute | solution.py:632
  655.2 5.8 add_convert_fusion
  670.5 8.0 attend_back.3
  678.5 21.4 %collective-permute-done.53 = bf16[2,3104,128]{2,1,0:T(8,128)(2,1)} collective-permute-done((bf16[2,3104,128]{2,1,0:T(8,128)(2,1)}, bf16[2,3104,128]{2,1,0:T(8,128)(2,1)}, u32[]{:S(2)}, u32[]{:S(2)}) %collective-permute-start.53) | collective-permute-done | bytes 1589280 | tf_op jit(solution)/shard_map/ppermute | solution.py:632
  735.4 9.2 collective-permute-done.59
  746.3 5.6 add_add_fusion.4.refs_0_
  762.0 5.4 pack.7
  786.9 40.2 %collective-permute-start.66 = (f32[1028]{0:T(1024)S(1)}, f32[1028]{0:T(1024)S(1)}, u32[]{:S(2)}, u32[]{:S(2)}) collective-permute-start(f32[1028]{0:T(1024)S(1)} %add.679), channel_id=1, source_target_pairs={{0,8},{8,0},{16,24},{24,16},{1,9},{9,1},{17,25},{25,17},{2,10},{10... | collective-permute-start | bytes 12344 | tf_op jit(solution)/shard_map/ppermute | solution.py:1355
  827.1 30.8 %collective-permute-done.66 = f32[1028]{0:T(1024)S(1)} collective-permute-done((f32[1028]{0:T(1024)S(1)}, f32[1028]{0:T(1024)S(1)}, u32[]{:S(2)}, u32[]{:S(2)}) %collective-permute-start.66) | collective-permute-done | bytes 4144 | tf_op jit(solution)/shard_map/ppermute | solution.py:1355
  862.1 26.7 %collective-permute-done.81 = bf16[2,3104,128]{2,1,0:T(8,128)(2,1)S(1)} collective-permute-done((bf16[2,3104,128]{2,1,0:T(8,128)(2,1)S(1)}, bf16[2,3104,128]{2,1,0:T(8,128)(2,1)S(1)}, u32[]{:S(2)}, u32[]{:S(2)}) %collective-permute-start.81) | collective-permute-done | bytes 1589280 | tf_op jit(solution)/shard_map/ppermute | solution.py:632
  905.0 4.6 collective-permute-done.74
  (844 shorter events, 341.7 us)
Async XLA Ops:
  11.1 18.0 %collective-permute-start.1 = (bf16[3088,128]{1,0:T(8,128)(2,1)S(1)}, bf16[3088,128]{1,0:T(8,128)(2,1)S(1)}, u32[]{:S(2)}, u32[]{:S(2)}) collective-permute-start(bf16[3088,128]{1,0:T(8,128)(2,1)S(1)} %get-tuple-element.160), channel_id=1, source_target_pairs={{0,8},{9,17},{2,10},{11,19},{4,12},{13,21},{6,14},{15,23}} | collective-permute-start | bytes 2371592 | tf_op jit(solution)/shard_map/ppermute | solution.py:268
  13.9 20.6 %collective-permute-start.30 = (bf16[2,3088,128]{2,1,0:T(8,128)(2,1)}, bf16[2,3088,128]{2,1,0:T(8,128)(2,1)}, u32[]{:S(2)}, u32[]{:S(2)}) collective-permute-start(bf16[2,3088,128]{2,1,0:T(8,128)(2,1)} %maximum_select_fusion), channel_id=1, source_target_pairs={{16,8},{25,17},{18,10},{27,19},{20,12},{29,21},{22,14},{31,23}} | collective-permute-start | bytes 4743176 | tf_op jit(solution)/shard_map/ppermute | solution.py:281
  34.5 33.6 %collective-permute-start.32 = (bf16[2,3088,128]{2,1,0:T(8,128)(2,1)}, bf16[2,3088,128]{2,1,0:T(8,128)(2,1)}, u32[]{:S(2)}, u32[]{:S(2)}) collective-permute-start(bf16[2,3088,128]{2,1,0:T(8,128)(2,1)} %collective-permute-done.30), channel_id=1, source_target_pairs={{8,0},{17,9},{10,2},{19,11},{12,4},{21,13},{14,6},{23,15}} | collective-permute-start | bytes 4743176 | tf_op jit(solution)/shard_map/ppermute | solution.py:283
  38.0 31.6 %collective-permute-start.19 = (bf16[3088,128]{1,0:T(8,128)(2,1)S(1)}, bf16[3088,128]{1,0:T(8,128)(2,1)S(1)}, u32[]{:S(2)}, u32[]{:S(2)}) collective-permute-start(bf16[3088,128]{1,0:T(8,128)(2,1)S(1)} %add_select_fusion.1), channel_id=1, source_target_pairs={{0,1},{1,0},{2,3},{3,2},{4,5},{5,4},{6,7},{7,6},{8,9},{9,8},{10,11... | collective-permute-start | bytes 2371592 | tf_op jit(solution)/shard_map/ppermute | solution.py:278
  39.7 43.5 %collective-permute-start.17 = (bf16[3088,128]{1,0:T(8,128)(2,1)S(1)}, bf16[3088,128]{1,0:T(8,128)(2,1)}, u32[]{:S(2)}, u32[]{:S(2)}) collective-permute-start(bf16[3088,128]{1,0:T(8,128)(2,1)S(1)} %add_select_fusion.1), channel_id=1, source_target_pairs={{0,4},{4,0},{1,5},{5,1},{2,6},{6,2},{3,7},{7,3},{8,12},{12,8},{9,1... | collective-permute-start | bytes 2371592 | tf_op jit(solution)/shard_map/ppermute | solution.py:274
  41.2 43.6 %collective-permute-start.16 = (bf16[3088,128]{1,0:T(8,128)(2,1)S(1)}, bf16[3088,128]{1,0:T(8,128)(2,1)}, u32[]{:S(2)}, u32[]{:S(2)}) collective-permute-start(bf16[3088,128]{1,0:T(8,128)(2,1)S(1)} %add_select_fusion.1), channel_id=1, source_target_pairs={{0,2},{2,0},{1,3},{3,1},{4,6},{6,4},{5,7},{7,5},{8,10},{10,8},{9,1... | collective-permute-start | bytes 2371592 | tf_op jit(solution)/shard_map/ppermute | solution.py:273
  43.1 41.7 %collective-permute-start.8 = (bf16[3088,128]{1,0:T(8,128)(2,1)S(1)}, bf16[3088,128]{1,0:T(8,128)(2,1)S(1)}, u32[]{:S(2)}, u32[]{:S(2)}) collective-permute-start(bf16[3088,128]{1,0:T(8,128)(2,1)S(1)} %add_select_fusion.2), channel_id=1, source_target_pairs={{0,1},{1,0},{2,3},{3,2},{4,5},{5,4},{6,7},{7,6},{8,9},{9,8},{10,11... | collective-permute-start | bytes 2371592 | tf_op jit(solution)/shard_map/ppermute | solution.py:278
  70.5 41.8 %collective-permute-start.33 = (bf16[2,3088,128]{2,1,0:T(8,128)(2,1)}, bf16[2,3088,128]{2,1,0:T(8,128)(2,1)}, u32[]{:S(2)}, u32[]{:S(2)}) collective-permute-start(bf16[2,3088,128]{2,1,0:T(8,128)(2,1)} %collective-permute-done.32), channel_id=1, source_target_pairs={{9,1},{11,3},{13,5},{15,7}} | collective-permute-start | bytes 4743176 | tf_op jit(solution)/shard_map/ppermute | solution.py:284
  83.2 19.3 %collective-permute-start.6 = (bf16[3088,128]{1,0:T(8,128)(2,1)S(1)}, bf16[3088,128]{1,0:T(8,128)(2,1)S(1)}, u32[]{:S(2)}, u32[]{:S(2)}) collective-permute-start(bf16[3088,128]{1,0:T(8,128)(2,1)S(1)} %add_select_fusion.2), channel_id=1, source_target_pairs={{0,4},{4,0},{1,5},{5,1},{2,6},{6,2},{3,7},{7,3},{8,12},{12,8},{9,1... | collective-permute-start | bytes 2371592 | tf_op jit(solution)/shard_map/ppermute | solution.py:274
  84.8 17.7 %collective-permute-start.21 = (bf16[3088,128]{1,0:T(8,128)(2,1)}, bf16[3088,128]{1,0:T(8,128)(2,1)S(1)}, u32[]{:S(2)}, u32[]{:S(2)}) collective-permute-start(bf16[3088,128]{1,0:T(8,128)(2,1)} %collective-permute-done.17), channel_id=1, source_target_pairs={{0,1},{1,0},{2,3},{3,2},{4,5},{5,4},{6,7},{7,6},{8,9},{9,8},{10,11... | collective-permute-start | bytes 2371592 | tf_op jit(solution)/shard_map/ppermute | solution.py:278
  84.8 20.3 %collective-permute-start.18 = (bf16[3088,128]{1,0:T(8,128)(2,1)}, bf16[3088,128]{1,0:T(8,128)(2,1)S(1)}, u32[]{:S(2)}, u32[]{:S(2)}) collective-permute-start(bf16[3088,128]{1,0:T(8,128)(2,1)} %collective-permute-done.17), channel_id=1, source_target_pairs={{0,2},{2,0},{1,3},{3,1},{4,6},{6,4},{5,7},{7,5},{8,10},{10,8},{9,1... | collective-permute-start | bytes 2371592 | tf_op jit(solution)/shard_map/ppermute | solution.py:275
  85.4 26.8 %collective-permute-start.7 = (bf16[3088,128]{1,0:T(8,128)(2,1)S(1)}, bf16[3088,128]{1,0:T(8,128)(2,1)S(1)}, u32[]{:S(2)}, u32[]{:S(2)}) collective-permute-start(bf16[3088,128]{1,0:T(8,128)(2,1)S(1)} %collective-permute-done.5), channel_id=1, source_target_pairs={{0,4},{4,0},{1,5},{5,1},{2,6},{6,2},{3,7},{7,3},{8,12},{12,8},{9,1... | collective-permute-start | bytes 2371592 | tf_op jit(solution)/shard_map/ppermute | solution.py:275
  102.5 40.8 %collective-permute-start.9 = (bf16[3088,128]{1,0:T(8,128)(2,1)S(1)}, bf16[3088,128]{1,0:T(8,128)(2,1)S(1)}, u32[]{:S(2)}, u32[]{:S(2)}) collective-permute-start(bf16[3088,128]{1,0:T(8,128)(2,1)S(1)} %collective-permute-done.5), channel_id=1, source_target_pairs={{0,1},{1,0},{2,3},{3,2},{4,5},{5,4},{6,7},{7,6},{8,9},{9,8},{10,11... | collective-permute-start | bytes 2371592 | tf_op jit(solution)/shard_map/ppermute | solution.py:278
  112.3 33.0 %collective-permute-start.22 = (bf16[3088,128]{1,0:T(8,128)(2,1)S(1)}, bf16[3088,128]{1,0:T(8,128)(2,1)S(1)}, u32[]{:S(2)}, u32[]{:S(2)}) collective-permute-start(bf16[3088,128]{1,0:T(8,128)(2,1)S(1)} %collective-permute-done.18), channel_id=1, source_target_pairs={{0,1},{1,0},{2,3},{3,2},{4,5},{5,4},{6,7},{7,6},{8,9},{9,8},{10,11... | collective-permute-start | bytes 2371592 | tf_op jit(solution)/shard_map/ppermute | solution.py:278
  112.3 33.0 %collective-permute-start.11 = (bf16[3088,128]{1,0:T(8,128)(2,1)S(1)}, bf16[3088,128]{1,0:T(8,128)(2,1)S(1)}, u32[]{:S(2)}, u32[]{:S(2)}) collective-permute-start(bf16[3088,128]{1,0:T(8,128)(2,1)S(1)} %collective-permute-done.7), channel_id=1, source_target_pairs={{0,1},{1,0},{2,3},{3,2},{4,5},{5,4},{6,7},{7,6},{8,9},{9,8},{10,11... | collective-permute-start | bytes 2371592 | tf_op jit(solution)/shard_map/ppermute | solution.py:278
  117.0 182.5 %collective-permute-start.38 = (bf16[2,3088,128]{2,1,0:T(8,128)(2,1)}, bf16[2,3088,128]{2,1,0:T(8,128)(2,1)}, u32[]{:S(2)}, u32[]{:S(2)}) collective-permute-start(bf16[2,3088,128]{2,1,0:T(8,128)(2,1)} %add_select_fusion.refs_18_), channel_id=1, source_target_pairs={{0,1},{1,0},{2,3},{3,2},{4,5},{5,4},{6,7},{7,6},{8,9},{9,8},{10,11... | collective-permute-start | bytes 4743176 | tf_op jit(solution)/shard_map/ppermute | solution.py:290
  117.1 150.2 %collective-permute-start.35 = (bf16[2,3088,128]{2,1,0:T(8,128)(2,1)}, bf16[2,3088,128]{2,1,0:T(8,128)(2,1)}, u32[]{:S(2)}, u32[]{:S(2)}) collective-permute-start(bf16[2,3088,128]{2,1,0:T(8,128)(2,1)} %add_select_fusion.refs_18_), channel_id=1, source_target_pairs={{0,4},{4,0},{1,5},{5,1},{2,6},{6,2},{3,7},{7,3},{8,12},{12,8},{9,1... | collective-permute-start | bytes 4743176 | tf_op jit(solution)/shard_map/ppermute | solution.py:287
  143.3 127.2 %collective-permute-start.34 = (bf16[2,3088,128]{2,1,0:T(8,128)(2,1)}, bf16[2,3088,128]{2,1,0:T(8,128)(2,1)}, u32[]{:S(2)}, u32[]{:S(2)}) collective-permute-start(bf16[2,3088,128]{2,1,0:T(8,128)(2,1)} %add_select_fusion.refs_18_), channel_id=1, source_target_pairs={{0,2},{2,0},{1,3},{3,1},{4,6},{6,4},{5,7},{7,5},{8,10},{10,8},{9,1... | collective-permute-start | bytes 4743176 | tf_op jit(solution)/shard_map/ppermute | solution.py:286
  182.3 45.1 %collective-permute-start.23 = (bf16[2,512,128]{2,1,0:T(8,128)(2,1)}, bf16[2,512,128]{2,1,0:T(8,128)(2,1)}, u32[]{:S(2)}, u32[]{:S(2)}) collective-permute-start(bf16[2,512,128]{2,1,0:T(8,128)(2,1)} %maximum_bitcast_fusion.1), channel_id=1, source_target_pairs={{0,2},{2,0},{1,3},{3,1},{4,6},{6,4},{5,7},{7,5},{8,10},{10,8},{9,1... | collective-permute-start | bytes 786440 | tf_op jit(solution)/shard_map/ppermute | solution.py:1321
  247.4 26.5 %collective-permute-start.25 = (bf16[2,2,2,512,128]{4,3,2,1,0:T(8,128)(2,1)S(1)}, bf16[2,2,2,512,128]{4,3,2,1,0:T(8,128)(2,1)S(1)}, u32[]{:S(2)}, u32[]{:S(2)}) collective-permute-start(bf16[2,2,2,512,128]{4,3,2,1,0:T(8,128)(2,1)S(1)} %pad_maximum_fusion.11), channel_id=1, source_target_pairs={{0,1},{1,0},{2,3},{3,2},{4,5},{5,4},{6,7},{7,6},{8,9},{9,8},{10,11... | collective-permute-start | bytes 3145736 | tf_op jit(solution)/shard_map/ppermute | solution.py:1323
  269.1 19.3 %collective-permute-start.37 = (bf16[1,3088,128]{2,1,0:T(8,128)(2,1)S(1)}, bf16[1,3088,128]{2,1,0:T(8,128)(2,1)}, u32[]{:S(2)}, u32[]{:S(2)}) collective-permute-start(bf16[1,3088,128]{2,1,0:T(8,128)(2,1)S(1)} %slice.374), channel_id=1, source_target_pairs={{0,2},{2,0},{1,3},{3,1},{4,6},{6,4},{5,7},{7,5},{8,10},{10,8},{9,1... | collective-permute-start | bytes 2371592 | tf_op jit(solution)/shard_map/ppermute | solution.py:288
  271.6 19.2 %collective-permute-start.36 = (bf16[1,3088,128]{2,1,0:T(8,128)(2,1)S(1)}, bf16[1,3088,128]{2,1,0:T(8,128)(2,1)}, u32[]{:S(2)}, u32[]{:S(2)}) collective-permute-start(bf16[1,3088,128]{2,1,0:T(8,128)(2,1)S(1)} %slice.373), channel_id=1, source_target_pairs={{0,4},{4,0},{1,5},{5,1},{2,6},{6,2},{3,7},{7,3},{8,12},{12,8},{9,1... | collective-permute-start | bytes 2371592 | tf_op jit(solution)/shard_map/ppermute | solution.py:288
  273.8 25.6 %collective-permute-start.40 = (bf16[2,3088,128]{2,1,0:T(8,128)(2,1)}, bf16[2,3088,128]{2,1,0:T(8,128)(2,1)}, u32[]{:S(2)}, u32[]{:S(2)}) collective-permute-start(bf16[2,3088,128]{2,1,0:T(8,128)(2,1)} %collective-permute-done.35.refs_20_), channel_id=1, source_target_pairs={{0,1},{1,0},{2,3},{3,2},{4,5},{5,4},{6,7},{7,6},{8,9},{9,8},{10,11... | collective-permute-start | bytes 4743176 | tf_op jit(solution)/shard_map/ppermute | solution.py:290
  273.9 25.6 %collective-permute-start.39 = (bf16[2,3088,128]{2,1,0:T(8,128)(2,1)}, bf16[2,3088,128]{2,1,0:T(8,128)(2,1)}, u32[]{:S(2)}, u32[]{:S(2)}) collective-permute-start(bf16[2,3088,128]{2,1,0:T(8,128)(2,1)} %collective-permute-done.34.refs_19_), channel_id=1, source_target_pairs={{0,1},{1,0},{2,3},{3,2},{4,5},{5,4},{6,7},{7,6},{8,9},{9,8},{10,11... | collective-permute-start | bytes 4743176 | tf_op jit(solution)/shard_map/ppermute | solution.py:290
  385.0 34.5 %collective-permute-start.43 = (bf16[144,1536]{1,0:T(8,128)(2,1)S(1)}, bf16[144,1536]{1,0:T(8,128)(2,1)S(1)}, u32[]{:S(2)}, u32[]{:S(2)}) collective-permute-start(bf16[144,1536]{1,0:T(8,128)(2,1)S(1)} %pad_maximum_fusion.17.refs_7_), channel_id=1, source_target_pairs={{0,1},{1,0},{2,3},{3,2},{4,5},{5,4},{6,7},{7,6},{8,9},{9,8},{10,11... | collective-permute-start | bytes 1327112 | tf_op jit(solution)/shard_map/ppermute | solution.py:632
  427.4 55.0 %collective-permute-start.46 = (bf16[24688,128]{1,0:T(8,128)(2,1)}, bf16[24688,128]{1,0:T(8,128)(2,1)}, u32[]{:S(2)}, u32[]{:S(2)}) collective-permute-start(bf16[24688,128]{1,0:T(8,128)(2,1)} %constant_dynamic-slice_fusion.2.refs_4_), channel_id=1, source_target_pairs={{0,1},{1,0},{2,3},{3,2},{4,5},{5,4},{6,7},{7,6},{8,9},{9,8},{10,11... | collective-permute-start | bytes 18960392 | tf_op jit(solution)/shard_map/ppermute | solution.py:632
  427.4 20.3 %collective-permute-start.44 = (bf16[144,1536]{1,0:T(8,128)(2,1)S(1)}, bf16[144,1536]{1,0:T(8,128)(2,1)}, u32[]{:S(2)}, u32[]{:S(2)}) collective-permute-start(bf16[144,1536]{1,0:T(8,128)(2,1)S(1)} %copy-done.21), channel_id=1, source_target_pairs={{0,2},{2,0},{1,3},{3,1},{4,6},{6,4},{5,7},{7,5},{8,10},{10,8},{9,1... | collective-permute-start | bytes 1327112 | tf_op jit(solution)/shard_map/ppermute | solution.py:632
  450.1 47.0 %collective-permute-start.45 = (bf16[144,1536]{1,0:T(8,128)(2,1)}, bf16[144,1536]{1,0:T(8,128)(2,1)}, u32[]{:S(2)}, u32[]{:S(2)}) collective-permute-start(bf16[144,1536]{1,0:T(8,128)(2,1)} %pad_maximum_fusion.23.refs_1_), channel_id=1, source_target_pairs={{0,4},{4,0},{1,5},{5,1},{2,6},{6,2},{3,7},{7,3},{8,12},{12,8},{9,1... | collective-permute-start | bytes 1327112 | tf_op jit(solution)/shard_map/ppermute | solution.py:632
  491.7 50.6 %collective-permute-start.47 = (bf16[2,3104,128]{2,1,0:T(8,128)(2,1)}, bf16[2,3104,128]{2,1,0:T(8,128)(2,1)}, u32[]{:S(2)}, u32[]{:S(2)}) collective-permute-start(bf16[2,3104,128]{2,1,0:T(8,128)(2,1)} %pad_maximum_fusion.5.refs_11_), channel_id=1, source_target_pairs={{0,4},{4,0},{1,5},{5,1},{2,6},{6,2},{3,7},{7,3},{8,12},{12,8},{9,1... | collective-permute-start | bytes 4767752 | tf_op jit(solution)/shard_map/ppermute | solution.py:632
  499.9 47.4 %collective-permute-start.48 = (bf16[2,3104,128]{2,1,0:T(8,128)(2,1)S(1)}, bf16[2,3104,128]{2,1,0:T(8,128)(2,1)S(1)}, u32[]{:S(2)}, u32[]{:S(2)}) collective-permute-start(bf16[2,3104,128]{2,1,0:T(8,128)(2,1)S(1)} %pad_maximum_fusion.6.refs_12_), channel_id=1, source_target_pairs={{0,2},{2,0},{1,3},{3,1},{4,6},{6,4},{5,7},{7,5},{8,10},{10,8},{9,1... | collective-permute-start | bytes 4767752 | tf_op jit(solution)/shard_map/ppermute | solution.py:632
  545.6 25.7 %collective-permute-start.49 = (bf16[3104,128]{1,0:T(8,128)(2,1)S(1)}, bf16[3104,128]{1,0:T(8,128)(2,1)}, u32[]{:S(2)}, u32[]{:S(2)}) collective-permute-start(bf16[3104,128]{1,0:T(8,128)(2,1)S(1)} %dynamic-slice_bitcast_fusion.14.refs_4_.refs_9_), channel_id=1, source_target_pairs={{0,2},{2,0},{1,3},{3,1},{4,6},{6,4},{5,7},{7,5},{8,10},{10,8},{9,1... | collective-permute-start | bytes 2383880 | tf_op jit(solution)/shard_map/ppermute | solution.py:632
  551.2 21.7 %collective-permute-start.50 = (bf16[3104,128]{1,0:T(8,128)(2,1)}, bf16[3104,128]{1,0:T(8,128)(2,1)}, u32[]{:S(2)}, u32[]{:S(2)}) collective-permute-start(bf16[3104,128]{1,0:T(8,128)(2,1)} %dynamic-slice_bitcast_fusion.11.refs_5_.refs_10_), channel_id=1, source_target_pairs={{0,4},{4,0},{1,5},{5,1},{2,6},{6,2},{3,7},{7,3},{8,12},{12,8},{9,1... | collective-permute-start | bytes 2383880 | tf_op jit(solution)/shard_map/ppermute | solution.py:632
  602.4 52.8 %collective-permute-start.52 = (bf16[24688,128]{1,0:T(8,128)(2,1)}, bf16[24688,128]{1,0:T(8,128)(2,1)}, u32[]{:S(2)}, u32[]{:S(2)}) collective-permute-start(bf16[24688,128]{1,0:T(8,128)(2,1)} %constant_dynamic-slice_fusion.1.refs_7_), channel_id=1, source_target_pairs={{0,1},{1,0},{2,3},{3,2},{4,5},{5,4},{6,7},{7,6},{8,9},{9,8},{10,11... | collective-permute-start | bytes 18960392 | tf_op jit(solution)/shard_map/ppermute | solution.py:632
  616.4 36.6 %collective-permute-start.56 = (bf16[2,3104,128]{2,1,0:T(8,128)(2,1)S(1)}, bf16[2,3104,128]{2,1,0:T(8,128)(2,1)S(1)}, u32[]{:S(2)}, u32[]{:S(2)}) collective-permute-start(bf16[2,3104,128]{2,1,0:T(8,128)(2,1)S(1)} %copy-done.67), channel_id=1, source_target_pairs={{0,16},{9,25},{2,18},{11,27},{4,20},{13,29},{6,22},{15,31}} | collective-permute-start | bytes 4767752 | tf_op jit(solution)/shard_map/ppermute | solution.py:632
  620.9 32.0 %collective-permute-start.55 = (bf16[2,3104,128]{2,1,0:T(8,128)(2,1)S(1)}, bf16[2,3104,128]{2,1,0:T(8,128)(2,1)S(1)}, u32[]{:S(2)}, u32[]{:S(2)}) collective-permute-start(bf16[2,3104,128]{2,1,0:T(8,128)(2,1)S(1)} %copy-done.67), channel_id=1, source_target_pairs={{8,16},{17,25},{10,18},{19,27},{12,20},{21,29},{14,22},{23,31}} | collective-permute-start | bytes 4767752 | tf_op jit(solution)/shard_map/ppermute | solution.py:632
  622.1 30.9 %collective-permute-start.57 = (bf16[2,3104,128]{2,1,0:T(8,128)(2,1)S(1)}, bf16[2,3104,128]{2,1,0:T(8,128)(2,1)S(1)}, u32[]{:S(2)}, u32[]{:S(2)}) collective-permute-start(bf16[2,3104,128]{2,1,0:T(8,128)(2,1)S(1)} %copy-done.67), channel_id=1, source_target_pairs={{24,16},{1,25},{26,18},{3,27},{28,20},{5,29},{30,22},{7,31}} | collective-permute-start | bytes 4767752 | tf_op jit(solution)/shard_map/ppermute | solution.py:632
  664.2 35.7 %collective-permute-start.53 = (bf16[2,3104,128]{2,1,0:T(8,128)(2,1)}, bf16[2,3104,128]{2,1,0:T(8,128)(2,1)}, u32[]{:S(2)}, u32[]{:S(2)}) collective-permute-start(bf16[2,3104,128]{2,1,0:T(8,128)(2,1)} %pad_maximum_fusion.8.refs_2_.refs_7_), channel_id=1, source_target_pairs={{0,4},{4,0},{1,5},{5,1},{2,6},{6,2},{3,7},{7,3},{8,12},{12,8},{9,1... | collective-permute-start | bytes 4767752 | tf_op jit(solution)/shard_map/ppermute | solution.py:632
  665.6 38.9 %collective-permute-start.54 = (bf16[2,3104,128]{2,1,0:T(8,128)(2,1)}, bf16[2,3104,128]{2,1,0:T(8,128)(2,1)}, u32[]{:S(2)}, u32[]{:S(2)}) collective-permute-start(bf16[2,3104,128]{2,1,0:T(8,128)(2,1)} %pad_maximum_fusion.9.refs_3_.refs_8_), channel_id=1, source_target_pairs={{0,2},{2,0},{1,3},{3,1},{4,6},{6,4},{5,7},{7,5},{8,10},{10,8},{9,1... | collective-permute-start | bytes 4767752 | tf_op jit(solution)/shard_map/ppermute | solution.py:632
  703.0 24.0 %collective-permute-start.60 = (bf16[3104,128]{1,0:T(8,128)(2,1)}, bf16[3104,128]{1,0:T(8,128)(2,1)}, u32[]{:S(2)}, u32[]{:S(2)}) collective-permute-start(bf16[3104,128]{1,0:T(8,128)(2,1)} %dynamic-slice_bitcast_fusion.4.refs_2_), channel_id=1, source_target_pairs={{0,2},{2,0},{1,3},{3,1},{4,6},{6,4},{5,7},{7,5},{8,10},{10,8},{9,1... | collective-permute-start | bytes 2383880 | tf_op jit(solution)/shard_map/ppermute | solution.py:632
  707.3 24.5 %collective-permute-start.61 = (bf16[3104,128]{1,0:T(8,128)(2,1)}, bf16[3104,128]{1,0:T(8,128)(2,1)}, u32[]{:S(2)}, u32[]{:S(2)}) collective-permute-start(bf16[3104,128]{1,0:T(8,128)(2,1)} %dynamic-slice_bitcast_fusion.1.refs_3_), channel_id=1, source_target_pairs={{0,4},{4,0},{1,5},{5,1},{2,6},{6,2},{3,7},{7,3},{8,12},{12,8},{9,1... | collective-permute-start | bytes 2383880 | tf_op jit(solution)/shard_map/ppermute | solution.py:632
  769.5 89.7 %collective-permute-start.68 = (bf16[3200,128]{1,0:T(8,128)(2,1)}, bf16[3200,128]{1,0:T(8,128)(2,1)}, u32[]{:S(2)}, u32[]{:S(2)}) collective-permute-start(bf16[3200,128]{1,0:T(8,128)(2,1)} %constant_dynamic-slice_fusion), channel_id=1, source_target_pairs={{0,1},{1,0},{2,3},{3,2},{4,5},{5,4},{6,7},{7,6},{8,9},{9,8},{10,11... | collective-permute-start | bytes 2457608 | tf_op jit(solution)/shard_map/ppermute | solution.py:632
  783.0 105.9 %collective-permute-start.81 = (bf16[2,3104,128]{2,1,0:T(8,128)(2,1)S(1)}, bf16[2,3104,128]{2,1,0:T(8,128)(2,1)S(1)}, u32[]{:S(2)}, u32[]{:S(2)}) collective-permute-start(bf16[2,3104,128]{2,1,0:T(8,128)(2,1)S(1)} %copy-done.1), channel_id=1, source_target_pairs={{16,0},{25,9},{18,2},{27,11},{20,4},{29,13},{22,6},{31,15}} | collective-permute-start | bytes 4767752 | tf_op jit(solution)/shard_map/ppermute | solution.py:632
  784.2 104.8 %collective-permute-start.80 = (bf16[2,3104,128]{2,1,0:T(8,128)(2,1)S(1)}, bf16[2,3104,128]{2,1,0:T(8,128)(2,1)S(1)}, u32[]{:S(2)}, u32[]{:S(2)}) collective-permute-start(bf16[2,3104,128]{2,1,0:T(8,128)(2,1)S(1)} %copy-done.1), channel_id=1, source_target_pairs={{8,0},{17,9},{10,2},{19,11},{12,4},{21,13},{14,6},{23,15}} | collective-permute-start | bytes 4767752 | tf_op jit(solution)/shard_map/ppermute | solution.py:632
  785.5 103.5 %collective-permute-start.82 = (bf16[2,3104,128]{2,1,0:T(8,128)(2,1)S(1)}, bf16[2,3104,128]{2,1,0:T(8,128)(2,1)S(1)}, u32[]{:S(2)}, u32[]{:S(2)}) collective-permute-start(bf16[2,3104,128]{2,1,0:T(8,128)(2,1)S(1)} %copy-done.1), channel_id=1, source_target_pairs={{24,0},{1,9},{26,2},{3,11},{28,4},{5,13},{30,6},{7,15}} | collective-permute-start | bytes 4767752 | tf_op jit(solution)/shard_map/ppermute | solution.py:632
  786.9 71.0 %collective-permute-start.66 = (f32[1028]{0:T(1024)S(1)}, f32[1028]{0:T(1024)S(1)}, u32[]{:S(2)}, u32[]{:S(2)}) collective-permute-start(f32[1028]{0:T(1024)S(1)} %add.679), channel_id=1, source_target_pairs={{0,8},{8,0},{16,24},{24,16},{1,9},{9,1},{17,25},{25,17},{2,10},{10... | collective-permute-start | bytes 12344 | tf_op jit(solution)/shard_map/ppermute | solution.py:1355
  857.9 76.8 %collective-permute-start.84 = (bf16[3104,128]{1,0:T(8,128)(2,1)}, bf16[3104,128]{1,0:T(8,128)(2,1)S(1)}, u32[]{:S(2)}, u32[]{:S(2)}) collective-permute-start(bf16[3104,128]{1,0:T(8,128)(2,1)} %get-tuple-element.158.refs_4_), channel_id=1, source_target_pairs={{0,1},{9,8},{16,17},{25,24},{2,3},{11,10},{18,19},{27,26},{4,5},{1... | collective-permute-start | bytes 2383880 | tf_op jit(solution)/shard_map/ppermute | solution.py:632
  859.2 60.0 %collective-permute-start.67 = (f32[1028]{0:T(1024)S(1)}, f32[1028]{0:T(1024)S(1)}, u32[]{:S(2)}, u32[]{:S(2)}) collective-permute-start(f32[1028]{0:T(1024)S(1)} %add.680), channel_id=1, source_target_pairs={{0,16},{16,0},{8,24},{24,8},{1,17},{17,1},{9,25},{25,9},{2,18},{18... | collective-permute-start | bytes 12344 | tf_op jit(solution)/shard_map/ppermute | solution.py:1355
  909.6 25.1 %collective-permute-start.83 = (bf16[3104,128]{1,0:T(8,128)(2,1)S(1)}, bf16[3104,128]{1,0:T(8,128)(2,1)S(1)}, u32[]{:S(2)}, u32[]{:S(2)}) collective-permute-start(bf16[3104,128]{1,0:T(8,128)(2,1)S(1)} %get-tuple-element.156), channel_id=1, source_target_pairs={{0,1},{9,8},{16,17},{25,24},{2,3},{11,10},{18,19},{27,26},{4,5},{1... | collective-permute-start | bytes 2383880 | tf_op jit(solution)/shard_map/ppermute | solution.py:632
  (252 other events, 3190.2 us)

commit v7 on v6

--- a/solution.py
+++ b/solution.py
@@ -237,6 +237,26 @@
     return [pl.BlockSpec(memory_space=pltpu.HBM)] * len(after)
 
 
+class Flow:
+    def __init__(self, stages):
+        self.stages = stages
+        self.sends = next(stages)
+        self.result = None
+
+    def values(self):
+        return [value for value, _, _ in self.sends] or (list(self.result) if isinstance(self.result, list) else [self.result])
+
+    def go(self, after=()):
+        arrived = [lax.ppermute(value, axis, pairs) for value, axis, pairs in self.sends]
+        if after:
+            arrived = fence(arrived, after)
+        try:
+            self.sends = self.stages.send(arrived)
+        except StopIteration as stop:
+            self.sends, self.result = [], stop.value
+        return self
+
+
 def fence(values, after):
     def kernel(*refs):
         del refs
@@ -283,11 +303,6 @@
     two = lax.ppermute(one, ZC, zc_pairs((1, 0, 0), (2, 1, 1)))
     three = lax.ppermute(two, ZC, zc_pairs((1, 0, 1)))
     column = jnp.where(z == 2 + c, here, one + side + two + three)
-    over_x = lax.ppermute(column, "x", SWAP)
-    over_y = lax.ppermute(column, "y", SWAP)
-    corners = [lax.ppermute(over_x[:1], "y", SWAP), lax.ppermute(over_y[1:], "x", SWAP)]
-    local = [column, over_x, over_y] + corners
-    buffers += local + [lax.ppermute(piece, "c", SWAP) for piece in local]
     late = []
     for part in range(2):
         for first in (16, 21):
@@ -296,7 +311,14 @@
     sz, sy, sx, sc = shard // 8, shard // 4 % 2, shard // 2 % 2, shard % 2
     away = jnp.where(sz % 2 == c, 0, 4)
     where = sc * 8 + away + 2 * (sy ^ y) + (sx ^ x) + 16 * (sz // 2)
-    return buffers, (early, early + late), where.astype(jnp.int32)
+    return buffers, Flow(spread_stages(column)), (early, early + late), where.astype(jnp.int32)
+
+
+def spread_stages(column):
+    over_x, over_y = yield [(column, "x", SWAP), (column, "y", SWAP)]
+    corners = yield [(over_x[:1], "y", SWAP), (over_y[1:], "x", SWAP)]
+    local = [column, over_x, over_y] + list(corners)
+    return local + list((yield [(piece, "c", SWAP) for piece in local]))
 
 
 def unpack_lines(buffers, slots, where, segments, after=()):
@@ -619,24 +641,6 @@
     return total.astype(jnp.bfloat16)
 
 
-class Flow:
-    def __init__(self, stages):
-        self.stages = stages
-        self.sends = next(stages)
-        self.result = None
-
-    def values(self):
-        return [value for value, _, _ in self.sends] or [self.result]
-
-    def go(self):
-        arrived = [lax.ppermute(value, axis, pairs) for value, axis, pairs in self.sends]
-        try:
-            self.sends = self.stages.send(arrived)
-        except StopIteration as stop:
-            self.sends, self.result = [], stop.value
-        return self
-
-
 def reduce_stages(flat, batch, shift):
     z, y, x, c = (lax.axis_index(name) for name in GRID)
     length = PLANE + 32
@@ -662,9 +666,16 @@
         hops = [((1, 0, 0), (2, 1, 1)), ((2, 0, 0), (3, 1, 1)), ((3, 0, 0), (0, 1, 1))]
     else:
         hops = [((1, 2, 0), (2, 3, 1)), ((0, 2, 0), (1, 3, 1)), ((3, 2, 0), (0, 3, 1))]
-    columns = jnp.stack(columns)
-    got = yield [(columns, ZC, zc_pairs(*hop)) for hop in hops]
-    ends = added(columns, *got)
+    if batch == 0:
+        got = yield [(columns[0], ZC, zc_pairs(*hop)) for hop in hops]
+        end = added(columns[0], *got)
+        (column,) = fence(columns[1:], [end])
+        got = yield [(column, ZC, zc_pairs(*hop)) for hop in hops]
+        ends = [end, added(column, *got)]
+    else:
+        columns = jnp.stack(columns)
+        got = yield [(columns, ZC, zc_pairs(*hop)) for hop in hops]
+        ends = added(columns, *got)
     mine = jnp.where(c == 0, ends[0], ends[1])
     other = jnp.where(c == 0, ends[1], ends[0])
     (handed,) = yield [(other, ZC, [(2 * k + k % 2, 2 * k + 1 - k % 2) for k in range(4)])]
@@ -726,7 +737,7 @@
     return place, windows, total
 
 
-def conv_forward(xbc, rim, weight, bias, meta, start_column):
+def conv_forward(xbc, rim, weight, bias, meta, start_column, after=()):
     rows = xbc.shape[0]
 
     def kernel(meta_ref, x_ref, rim_ref, weight_ref, bias_ref, start_ref, out_ref, ext):
@@ -737,7 +748,7 @@
 
     lanes = lambda i, m: (0, i)
     return pl.pallas_call(
-        kernel,
+        pinned(kernel, 6, after),
         grid_spec=pltpu.PrefetchScalarGridSpec(
             num_scalar_prefetch=1,
             grid=(COLUMNS,),
@@ -747,14 +758,14 @@
                 pl.BlockSpec((CONV, LANES), lanes),
                 pl.BlockSpec((1, LANES), lanes),
                 pl.BlockSpec((rows, 1), lambda i, m: (0, 0)),
-            ],
+            ] + pins(after),
             out_specs=pl.BlockSpec((rows, LANES), lanes),
             scratch_shapes=[pltpu.VMEM((rows + 8, LANES), jnp.float32)],
         ),
         out_shape=jax.ShapeDtypeStruct((rows, CHANNELS), jnp.float32),
         cost_estimate=pl.CostEstimate(flops=10**9, bytes_accessed=rows * CHANNELS * 8, transcendentals=0),
         name="conv",
-    )(meta, xbc, rim, weight, bias, start_column)
+    )(meta, xbc, rim, weight, bias, start_column, *after)
 
 
 def conv_backward(dx, db, dc, xbc, rim, weight, bias, meta, start_column, after=()):
@@ -1317,11 +1328,20 @@
 def gather_span(value, span, fast):
     if not fast:
         return lax.all_gather(value, span)
+    flow = Flow(gather_stages(value))
+    while flow.sends:
+        flow.go()
+    return flow.result
+
+
+def gather_stages(value):
     _, y, x, c = (lax.axis_index(name) for name in GRID)
-    two = ordered(x, value, lax.ppermute(value, "x", SWAP), 0)
-    four = ordered(y, two, lax.ppermute(two, "y", SWAP), 0)
-    eight = ordered(c, four, lax.ppermute(four, "c", SWAP), 2)
-    return eight.reshape((8,) + value.shape)
+    (other,) = yield [(value, "x", SWAP)]
+    two = ordered(x, value, other, 0)
+    (other,) = yield [(two, "y", SWAP)]
+    four = ordered(y, two, other, 0)
+    (other,) = yield [(four, "c", SWAP)]
+    return ordered(c, four, other, 2).reshape((8,) + value.shape)
 
 
 def scatter_span(value, span, fast):
@@ -1346,13 +1366,13 @@
     return value
 
 
-def sum_all(value, axes, fast):
-    if not fast:
-        return lax.psum(value, axes)
+def sum_stages(value):
     for name in GRID[1:]:
-        value = value + lax.ppermute(value, name, SWAP)
+        (other,) = yield [(value, name, SWAP)]
+        value = value + other
     for pairs in ([(0, 1), (1, 0), (2, 3), (3, 2)], [(0, 2), (2, 0), (1, 3), (3, 1)]):
-        value = value + lax.ppermute(value, "z", pairs)
+        (other,) = yield [(value, "z", pairs)]
+        value = value + other
     return value
 
 
@@ -1366,7 +1386,8 @@
 
 def early_weights(params):
     places = offsets_of()
-    buffers, (slots, all_slots), where = gather_lines(params)
+    buffers, spread_flow, (slots, all_slots), where = gather_lines(params)
+    spread_flow.go()
     names = (W_QUERY, W_KEY, W_VALUE, W_ATTN_OUT, W_GATE_SSM, W_X_SSM, W_B_C)
     misc_at = places[W_STEP][0]
     first = unpack_lines(
@@ -1378,7 +1399,7 @@
     for name_key in (W_STEP,) + small_names[1:-1]:
         at, extent = places[name_key]
         weights[name_key] = misc[at - misc_at : at - misc_at + math.prod(extent)].reshape(extent)
-    return weights, (buffers, all_slots, where)
+    return weights, spread_flow, (buffers, all_slots, where)
 
 
 def flat_segment(name_key):
@@ -1439,18 +1460,19 @@
     )
 
 
-def pack_qkv(segments, attended, grad_branch, after):
+def pack_qkv(segments, attended, grad_branch, grad_norm_attn, after):
     places = offsets_of()
     out_row = 8 + places[W_ATTN_OUT][0] // LINE
     rows = (8 + SHARD) // 16 * 16 + 8 * PIECE
     closing = matmul_left_t(attended[:, :16], grad_branch).reshape(-1, LINE)
     closing = closing[: rows - out_row].astype(jnp.bfloat16)
+    opening = jnp.concatenate([jnp.zeros((8, LINE), jnp.float32), grad_norm_attn.reshape(-1, LINE)]).astype(jnp.bfloat16)
     return pack_lines(
-        None, rows, 16, segments, 0, 0, [(jnp.zeros((16, LINE), jnp.bfloat16), 0), (closing, out_row)], None, 0, after
-    )
-
-
-def own_lines(early, late, corner, grad_norm_attn):
+        None, rows, 16, segments, 0, 0, [(opening, 0), (closing, out_row)], None, 0, after
+    )
+
+
+def own_lines(early, late, corner):
     z, y, x, c = (lax.axis_index(name) for name in GRID)
     place = 4 * y + 2 * x + c
     shard = SHARD * place
@@ -1458,8 +1480,7 @@
     lines = jnp.where(z < 2, early, late)
     lines = jnp.where((z == 0) & (place < 2), corner[:WIN], lines)
     lines = lax.dynamic_slice(lines, (start, 0), (SHARD, LINE)).astype(jnp.float32)
-    norms = jnp.where((z == 0) & (place == 0), grad_norm_attn.reshape(-1, LINE), lines[: D // LINE])
-    return jnp.concatenate([norms, lines[D // LINE :]]).reshape(-1)
+    return lines.reshape(-1)
 
 
 def body(span, group, fast, tokens, params, cotangent, offsets):
@@ -1476,7 +1497,7 @@
     last_row = my_start + rows_dev - 1
     cosine, sine = rotary_tables(positions)
     if fast:
-        weights, held = early_weights(params)
+        weights, spread_flow, held = early_weights(params)
     else:
         weights = unpack(lax.all_gather(params, group + span, axis=0, tiled=True))
     small_f32 = {name_key: weights[name_key].astype(jnp.float32) for name_key in small_names[:-1]}
@@ -1491,20 +1512,8 @@
     k_heads = k_rot.reshape(rows_dev, HEADS_KV, HEAD_DIM)
     v_heads = value_low.reshape(rows_dev, HEADS_KV, HEAD_DIM)
     kv_mine = jnp.concatenate([k_heads, v_heads], axis=2).transpose(1, 0, 2)
-    key_blocks = gather_span(kv_mine.reshape(HEADS_KV, rows_dev, PAIR), span, fast)
-    if rows_dev != KEYS:
-        key_blocks = key_blocks.transpose(1, 0, 2, 3).reshape(HEADS_KV, -1, KEYS, PAIR).transpose(1, 0, 2, 3)
     row_starts = row_index - positions
-    meta = jnp.stack(
-        [first_start // KEYS, last_row // KEYS + 1, my_start, row_starts[rows_dev - 1]]
-    ).astype(jnp.int32)
-    q_low = (q_rot * jnp.bfloat16(score_scale)).reshape(rows_dev, HEADS_Q, HEAD_DIM).transpose(1, 0, 2)
-    q_wide = jnp.pad(q_low, ((0, 0), (0, 0), (0, HEAD_DIM)))
-    start_row = jnp.broadcast_to(row_starts[None, :], (8, rows_dev))
-    mixed, logs = attention_forward(q_wide, key_blocks, meta, start_row)
-    attended = mixed.astype(jnp.bfloat16).reshape(HEADS_Q * HEAD_DIM, rows_dev).T
-    attn_out = matmul(attended, weights[W_ATTN_OUT])
-    gate_ssm = matmul(hidden, weights[W_GATE_SSM])
+    kv_local = kv_mine.reshape(HEADS_KV, rows_dev, PAIR)
     xbc = jnp.concatenate(
         [matmul(hidden, weights[W_X_SSM]), matmul(hidden, weights[W_B_C])], axis=1
     )
@@ -1512,7 +1521,14 @@
     rim_rows = passed_along(xbc[rows_dev - 8 :], span, 1)
     ssm_meta = jnp.concatenate([my_start[None], row_starts[CHUNK - 1 :: CHUNK]]).astype(jnp.int32)
     conv_bias = small_f32[CONV_BIAS][None, :]
-    conv_values = conv_forward(xbc, rim_rows, small_f32[CONV_WEIGHT], conv_bias, ssm_meta, row_starts[:, None])
+    convolve = lambda after: conv_forward(
+        xbc, rim_rows, small_f32[CONV_WEIGHT], conv_bias, ssm_meta, row_starts[:, None], after
+    )
+    if fast:
+        keys_flow = Flow(gather_stages(kv_local))
+        (conv_values,) = bracket(convolve, [keys_flow, spread_flow])
+    else:
+        conv_values = convolve(())
     step_in = step_raw.T + small_f32[STEP_BIAS][:, None]
     step_rows = jax.nn.softplus(step_in)
     decay = -jnp.exp(small_f32[DECAY_LOG])
@@ -1528,8 +1544,40 @@
     in_last = row_index >= row_starts[rows_dev - 1]
     tail_rows = jnp.exp(jnp.where(in_last[None, :], cumul[:, -1:] - cumul, masked_score))
     carry_all = entry_rows[:, -1]
-    local_state = weighted_state(conv_values, PAIRS, conv_values, tail_rows * step_rows)
-    state_in = scan_states(carry_all, local_state, span, fast, False)
+    summarize = lambda after: weighted_state(conv_values, PAIRS, conv_values, tail_rows * step_rows, after)
+    meta = jnp.stack(
+        [first_start // KEYS, last_row // KEYS + 1, my_start, row_starts[rows_dev - 1]]
+    ).astype(jnp.int32)
+    q_low = (q_rot * jnp.bfloat16(score_scale)).reshape(rows_dev, HEADS_Q, HEAD_DIM).transpose(1, 0, 2)
+    q_wide = jnp.pad(q_low, ((0, 0), (0, 0), (0, HEAD_DIM)))
+    start_row = jnp.broadcast_to(row_starts[None, :], (8, rows_dev))
+    if fast:
+        (local_state,) = bracket(lambda after: summarize((*after, *spread_flow.values())), [keys_flow])
+        scan = Flow(scan_stages(carry_all, local_state, False))
+        (gate_in,) = fence([hidden], scan.values() + keys_flow.values())
+        gate_ssm = matmul(gate_in, weights[W_GATE_SSM])
+        scan.go()
+        keys_flow.go()
+        key_blocks = keys_flow.result
+        (gate_ssm,) = fence([gate_ssm], scan.values() + keys_flow.values())
+        scan.go()
+        mixed, logs = bracket(
+            lambda after: attention_forward(
+                q_wide, key_blocks, meta, start_row, (*after, gate_ssm, *spread_flow.values())
+            ),
+            [scan],
+        )
+        spread_flow.go()
+        state_in = scan.result
+    else:
+        gate_ssm = matmul(hidden, weights[W_GATE_SSM])
+        key_blocks = lax.all_gather(kv_local, span)
+        if rows_dev != KEYS:
+            key_blocks = key_blocks.transpose(1, 0, 2, 3).reshape(HEADS_KV, -1, KEYS, PAIR).transpose(1, 0, 2, 3)
+        state_in = scan_states(carry_all, summarize(()), span, fast, False)
+        mixed, logs = attention_forward(q_wide, key_blocks, meta, start_row)
+    attended = mixed.astype(jnp.bfloat16).reshape(HEADS_Q * HEAD_DIM, rows_dev).T
+    attn_out = matmul(attended, weights[W_ATTN_OUT])
     skip_wide = jnp.repeat(small_f32[SKIP_GAIN], SSM_DIM)[None, :]
     ssm_y = ssm_forward(
         conv_values, chunk_cum, step_rows, state_in, skip_wide, ssm_meta, row_starts[:, None], start_row
@@ -1537,7 +1585,8 @@
     normed_ssm, gnorm_back = jax.vjp(gated_norm, ssm_y, gate_ssm, small_f32[NORM_SSM])
     ssm_low = normed_ssm.astype(jnp.bfloat16)
     if fast:
-        weights.update(late_weights(held, [mixed]))
+        held = (held[0] + spread_flow.result,) + held[1:]
+        weights.update(late_weights(held, [ssm_y]))
     small_f32[NORM_FFN] = weights[NORM_FFN].astype(jnp.float32)
     ssm_out = matmul(ssm_low, weights[W_SSM_OUT])
     middle = x_rows + attn_out + ssm_out
@@ -1574,19 +1623,20 @@
     grad_state_local = weighted_state(conv_values, PAIRS + 1, grad_ssm_y, entry_rows)
     if fast:
         scan = Flow(scan_stages(carry_all, grad_state_local, True))
+        stats_flow = Flow(sum_stages(squares))
         (late,) = bracket(
             lambda after: pack_late(
                 (hidden_two, grad_gate), (hidden_two, grad_upper), (activation, cotangent),
                 ssm_low, grad_branch, grad_norm_ffn, after,
             ),
-            [scan],
+            [scan, stats_flow],
         )
         late_flow = Flow(reduce_stages(late, 1, 14))
-        (early,) = bracket(lambda after: pack_out(ssm_low, grad_branch, after + late_flow.values()), [scan])
+        (early,) = bracket(lambda after: pack_out(ssm_low, grad_branch, after + late_flow.values()), [scan, stats_flow])
         scan.go()
         late_flow.go()
         grad_state_out = scan.result
-        around = lambda call: bracket(call, [late_flow])
+        around = lambda call: bracket(call, [late_flow, stats_flow])
     else:
         grad_state_out = scan_states(carry_all, grad_state_local, span, fast, True)
         around = lambda call: call(())
@@ -1633,20 +1683,24 @@
         NORM_SSM: grad_norm_ssm,
         NORM_FFN: grad_norm_ffn,
     }
-    g_low = grad_attended.reshape(rows_dev, HEADS_Q, HEAD_DIM).transpose(1, 0, 2)
-    g_wide = jnp.pad(g_low, ((0, 0), (0, 0), (HEAD_DIM, 0)))
     parts = []
     if fast:
-        early = pack_ssm(
+        (early,) = bracket(lambda after: pack_ssm(
             early,
             [
                 (attended, grad_branch), (hidden, grad_gate_ssm),
                 (hidden, grad_xbc[:, :ssm_inner]), (hidden, grad_xbc[:, ssm_inner:]),
             ],
-            small, ssm_low, grad_branch, late_flow.values(),
-        )
+            small, ssm_low, grad_branch, (*after, *late_flow.values()),
+        ), [stats_flow])
         early_flow = Flow(reduce_stages(early, 0, 8))
+        (grad_attended,) = fence([grad_attended], early_flow.values() + late_flow.values())
         around = lambda call: bracket(call, [early_flow])
+    g_low = grad_attended.reshape(rows_dev, HEADS_Q, HEAD_DIM).transpose(1, 0, 2)
+    g_wide = jnp.pad(g_low, ((0, 0), (0, 0), (HEAD_DIM, 0)))
+    if fast:
+        early_flow.go()
+        (g_wide,) = fence([g_wide], early_flow.values())
     for group_at in range(HEADS_KV):
         after_part = [part[1] for part in parts]
         if fast and group_at == 0:
@@ -1663,19 +1717,19 @@
     if rows_dev != KEYS:
         grad_kv = grad_kv.transpose(1, 0, 2, 3).reshape(HEADS_KV, -1, rows_dev, PAIR).transpose(1, 0, 2, 3)
     if fast:
-        late_flow.go()
+        late_flow.go([parts[-1][1]])
         scatter = Flow(scatter_stages(grad_kv))
         (grad_q_turned,) = fence([grad_q_turned], scatter.values() + early_flow.values() + late_flow.values())
     grad_q_rot = grad_q_turned.reshape(HEADS_Q * HEAD_DIM, rows_dev).T * score_scale
     grad_query_low = rotate(grad_q_rot, cosine, -sine, HEADS_Q).astype(jnp.bfloat16)
     if fast:
         scatter.go()
-        (grad_query_low,) = fence([grad_query_low], scatter.values())
+        early_flow.go()
+        (grad_query_low,) = fence([grad_query_low], scatter.values() + early_flow.values())
     grad_hidden = grad_hidden_ssm + matmul_right_t(grad_query_low, weights[W_QUERY])
     if fast:
         scatter.go()
-        early_flow.go()
-        (grad_hidden,) = fence([grad_hidden], scatter.values() + early_flow.values())
+        (grad_hidden,) = fence([grad_hidden], scatter.values())
         scatter.go()
         grad_kv_mine = scatter.result
     else:
@@ -1684,15 +1738,6 @@
     grad_values_mine = grad_kv_mine[:, :, HEAD_DIM:].transpose(1, 0, 2).reshape(rows_dev, -1)
     grad_key_low = rotate(grad_keys_mine, cosine, -sine, HEADS_KV).astype(jnp.bfloat16)
     grad_value_low = grad_values_mine.astype(jnp.bfloat16)
-    if fast:
-        corner = pack_qkv(
-            [(hidden, grad_query_low), (hidden, grad_key_low), (hidden, grad_value_low)],
-            attended, grad_branch, early_flow.values(),
-        )
-        corner_flow = Flow(corner_stages(corner))
-        for flow in (early_flow, late_flow, corner_flow):
-            while flow.sends:
-                flow.go()
     grad_hidden = (
         grad_hidden
         + matmul_right_t(grad_key_low, weights[W_KEY])
@@ -1701,13 +1746,25 @@
     grad_x_norm, grad_norm_attn = norm_one_back(grad_hidden)
     grad_tokens = grad_middle + grad_x_norm
     if fast:
-        ends = sum_all(jnp.concatenate([grad_norm_attn, squares]), group + span, fast)
-        norms, totals = ends[:D], ends[D:]
-        stats = jnp.sqrt(totals / (all_rows * D))
-        grad_shard = own_lines(early_flow.result, late_flow.result, corner_flow.result, norms)
+        corner = pack_qkv(
+            [(hidden, grad_query_low), (hidden, grad_key_low), (hidden, grad_value_low)],
+            attended, grad_branch, grad_norm_attn, early_flow.values(),
+        )
+        corner_flow = Flow(corner_stages(corner))
+        for _ in range(3):
+            corner_flow.go()
+        early_flow.go()
+        ((pieces, _, _), *_) = corner_flow.sends
+        (pieces,) = fence([pieces], early_flow.values())
+        corner_flow.sends = [(pieces, axis, pairs) for _, axis, pairs in corner_flow.sends]
+        for flow in (early_flow, late_flow, corner_flow):
+            while flow.sends:
+                flow.go()
+        stats = jnp.sqrt(stats_flow.result / (all_rows * D))
+        grad_shard = own_lines(early_flow.result, late_flow.result, corner_flow.result)
         return (result.astype(jnp.bfloat16), grad_tokens, grad_shard, stats)
     small[NORM_ATTN] = grad_norm_attn
-    stats = jnp.sqrt(sum_all(squares, group + span, fast) / (all_rows * D))
+    stats = jnp.sqrt(lax.psum(squares, group + span) / (all_rows * D))
     pairs = {
         W_QUERY: (hidden, grad_query_low),
         W_KEY: (hidden, grad_key_low),

time: 946 us -> 921 us (0.974)
  waiting for transfers between devices: 230 us -> 169 us
  other arithmetic: 122 us -> 148 us
  starting transfers between devices: 215 us -> 197 us
  local copies, waits for them, and re-layouts: 90.2 us -> 104 us
    ppermute x39 -> x59, starting transfers between devices: 95.3 us -> 155 us  [go(): lax.ppermute(value, axis, pairs)]
    ppermute x15 -> x0, waiting for transfers between devices: 52.5 us -> none  [the longest x2 30.8 us: sum_all(): value = value + lax.ppermute(value, 'z', pairs)]
    ppermute x15 -> x0, starting transfers between devices: 48.9 us -> none  [the longest x2 41.5 us: sum_all(): value = value + lax.ppermute(value, 'z', pairs)]
    ppermute x3 -> x2, starting transfers between devices: 29.3 us -> 3.1 us  [gather_lines(): over_y = lax.ppermute(column, 'y', SWAP)]
    unnamed x439 -> x432, local copies, waits for them, and re-layouts: 30.9 us -> 44.7 us
    convert_element_type x12 -> x14, other arithmetic: 22.2 us -> 32.4 us  [added(): return total.astype(jnp.bfloat16)]
    ppermute x39 -> x59, waiting for transfers between devices: 124 us -> 119 us  [go(): lax.ppermute(value, axis, pairs)]
  transfers between devices with their start and end apart: 85 -> 88, of which waited for: 32 -> 27; matrix products, arithmetic and copies ran while one was open for 18% -> 24% of each run, Pallas kernels for 16% -> 18%
where the time goes in v7:
time: 921 us; the launch traced here: 912 us
  Pallas kernels  210 us (23%)
  starting transfers between devices  197 us (21%)
  waiting for transfers between devices  169 us (18%)
  other arithmetic  148 us (16%)
  local copies, waits for them, and re-layouts  104 us (11%)
  matrix products  77.2 us (8%)
    ppermute x59, starting transfers between devices, go(): lax.ppermute(value, axis, pairs)  155 us
    ppermute x59, waiting for transfers between devices, go(): lax.ppermute(value, axis, pairs)  119 us
    dot_general x12, matrix products, matmul_right_t(): lax.dot_general(left, right, (((1,), (1,)), ((), ())), preferred_element_...  47.1 us
    unnamed x432, local copies, waits for them, and re-layouts  44.7 us
    pallas_call x4, Pallas kernels, pack_lines(): pl.pallas_call(pinned(kernel, inputs, after), grid=(total,), in_specs=[le...  42.8 us
    pallas_call x2, Pallas kernels, unpack_lines(): pl.pallas_call(pinned(kernel, 2 + count_buffers, after), grid_spec=pltpu....  41.2 us
    pallas_call x1, Pallas kernels, ssm_backward(): pl.pallas_call(pinned(kernel, 11, after), grid_spec=pltpu.PrefetchScalarG...  40.3 us
    convert_element_type x14, other arithmetic, added(): return total.astype(jnp.bfloat16)  32.4 us
  transfers between devices with their start and end apart: 88, of which 27 were waited for; matrix products, arithmetic and copies ran while one was open for 24% of the time, Pallas kernels for 18%

profile of v7, /device:TPU:0, one launch (start us, length us, event | category | flops | bytes accessed | tf_op | source)
XLA Modules:
  0.0 912.1 jit_solution(8795439313640196427)
XLA Ops:
  15.7 4.9 collective-permute-done.12
  23.7 5.4 collective-permute-done.1
  44.9 9.4 %collective-permute-start.8 = (bf16[3088,128]{1,0:T(8,128)(2,1)S(1)}, bf16[3088,128]{1,0:T(8,128)(2,1)S(1)}, u32[]{:S(2)}, u32[]{:S(2)}) collective-permute-start(bf16[3088,128]{1,0:T(8,128)(2,1)S(1)} %add_select_fusion.2), channel_id=1, source_target_pairs={{0,1},{1,0},{2,3},{3,2},{4,5},{5,4},{6,7},{7,6},{8,9},{9,8},{10,11... | collective-permute-start | bytes 2371592 | tf_op jit(solution)/shard_map/ppermute | solution.py:298
  54.3 13.8 %collective-permute-done.29 = bf16[2,3088,128]{2,1,0:T(8,128)(2,1)} collective-permute-done((bf16[2,3088,128]{2,1,0:T(8,128)(2,1)}, bf16[2,3088,128]{2,1,0:T(8,128)(2,1)}, u32[]{:S(2)}, u32[]{:S(2)}) %collective-permute-start.29) | collective-permute-done | bytes 1581088 | tf_op jit(solution)/shard_map/ppermute | solution.py:303
  89.7 12.4 %collective-permute-done.6 = bf16[3088,128]{1,0:T(8,128)(2,1)S(1)} collective-permute-done((bf16[3088,128]{1,0:T(8,128)(2,1)S(1)}, bf16[3088,128]{1,0:T(8,128)(2,1)S(1)}, u32[]{:S(2)}, u32[]{:S(2)}) %collective-permute-start.6) | collective-permute-done | bytes 790560 | tf_op jit(solution)/shard_map/ppermute | solution.py:294
  104.7 7.2 collective-permute-done.7
  120.0 14.5 %unpack.2 = (bf16[1024,512]{1,0:T(8,128)(2,1)}, bf16[1024,128]{1,0:T(8,128)(2,1)S(1)}, bf16[1024,128]{1,0:T(8,128)(2,1)S(1)}, bf16[512,1024]{1,0:T(8,128)(2,1)},...) custom-call(s32[25,5]{1,0:T(8,128)S(1)} %copy-done.71, ...), custom_call_target="tpu_custom_call" | custom-call | bytes 26624000 | tf_op jit(solution)/shard_map/unpack/pallas_call | solution.py:456
  164.7 10.4 %collective-permute-done.24 = bf16[2,2,512,128]{3,2,1,0:T(8,128)(2,1)S(1)} collective-permute-done((bf16[2,2,512,128]{3,2,1,0:T(8,128)(2,1)S(1)}, bf16[2,2,512,128]{3,2,1,0:T(8,128)(2,1)S(1)}, u32[]{:S(2)}, u32[]{:S(2)}) %collective-permute-start.24) | collective-permute-done | bytes 524320 | tf_op jit(solution)/shard_map/ppermute | solution.py:250
  201.9 12.2 %conv.1.refs_0_ = f32[512,1792]{1,0:T(8,128)} custom-call(s32[5]{0:T(128)} %pad_add_fusion.1.refs_0_.meta_ref, f32[512,1792]{1,0:T(8,128)} %pad_maximum_fusion.refs_1_.refs_4_, f32[8,1792]{1,0:T(8,128)} %collective-permute-done.26.refs_2_.refs_5_, f32[4,1792]{1,0:T(4,128)} %reshape.394.refs_3_.refs_6_, f32[1,1792]{1,0:T(1,128)} %bitcast.348, ...), custom_call_target="tpu_custom_call" | custom-call | flops 1000000000 | bytes 7340032 | tf_op jit(solution)/shard_map/conv/pallas_call | solution.py:750
  215.8 9.2 %state.2.refs_0_ = f32[128,1536]{1,0:T(8,128)} custom-call(f32[512,1792]{1,0:T(8,128)} %fence.20.refs_0_.refs_1_.x_ref.b_ref.c_ref.refs_3_.refs_4_, f32[512,1792]{1,0:T(8,128)} %fence.20.refs_0_.refs_1_.x_ref.b_ref.c_ref.refs_3_.refs_4_, f32[12,2,512]{2,1,0:T(2,128)} %reshape.373.refs_2_, bf16[2,2,512,128]{3,2,1,0:T(8,128)(2,1)} %copy-done.123, ...), custom_call_target="tpu_custom_call" | custom-call | flops 201326592 | bytes 3145728 | tf_op jit(solution)/shard_map/state/pallas_call | solution.py:850
  239.4 7.1 collective-permute-done.36
  252.5 14.8 %attend.1 = (f32[8,64,512]{2,1,0:T(8,128)S(1)}, f32[8,8,512]{2,1,0:T(8,128)S(1)}) custom-call(s32[4]{0:T(128)S(1)} %pad_add_fusion.refs_0_, bf16[8,512,128]{2,1,0:T(8,128)(2,1)S(1)} %copy-done.56, bf16[8,2,512,128]{3,2,1,0:T(8,128)(2,1)} %bitcast.307, s32[8,512]{1,0:T(8,128)S(1)} %broadcast_in_dim.213.refs_3_.row_ref.refs_10_.refs_6_, ...), custom_call_target="tpu_custom_call" | custom-call | flops 20000000000 | bytes 8388608 | tf_op jit(solution)/shard_map/attend/pallas_call | solution.py:1202
  277.5 8.5 ssm.1.refs_28_
  290.7 26.8 %unpack.3 = (bf16[1536,1024]{1,0:T(8,128)(2,1)}, bf16[1024,2048]{1,0:T(8,128)(2,1)}, bf16[1024,2048]{1,0:T(8,128)(2,1)}, bf16[2048,1024]{1,0:T(8,128)(2,1)}, bf16[16,128]{1,0:T(8,128)(2,1)S(1)}) custom-call(s32[31,5]{1,0:T(8,128)S(1)} %copy-done.70, s32[32]{0:T(128)S(1)} %fusion.71.refs_1_, bf16[1,3088,128]{2,1,0:T(8,128)(2,1)S(1)} %bitcast.282, ...), custom_call_target="tpu_custom_call" | custom-call | bytes 33013760 | tf_op jit(solution)/shard_map/unpack/pallas_call | solution.py:456
  333.3 6.7 fusion.2
  340.1 6.9 fusion.100
  349.4 4.6 multiply_reduce_fusion.6
  363.8 14.9 %collective-permute-start.46 = (f32[4]{0:T(128)S(1)}, f32[4]{0:T(128)S(1)}, u32[]{:S(2)}, u32[]{:S(2)}) collective-permute-start(f32[4]{0:T(128)S(1)} %pad_maximum_fusion.27.refs_8_), channel_id=1, source_target_pairs={{0,4},{4,0},{1,5},{5,1},{2,6},{6,2},{3,7},{7,3},{8,12},{12,8},{9,1... | collective-permute-start | bytes 56 | tf_op jit(solution)/shard_map/ppermute | solution.py:250
  378.9 6.3 fusion.23
  385.2 9.7 %state.3 = f32[128,1536]{1,0:T(8,128)} custom-call(f32[512,1792]{1,0:T(8,128)} %fence.20.refs_0_.refs_1_.x_ref.b_ref.c_ref.refs_3_.refs_4_, f32[512,1536]{1,0:T(8,128)} %get-tuple-element.139.refs_1_.refs_2_, f32[12,2,512]{2,1,0:T(2,128)} %reshape.378.refs_2_), custom_call_target="tpu_custom_call" | custom-call | flops 201326592 | bytes 3145728 | tf_op jit(solution)/shard_map/state/pallas_call | solution.py:850
  396.4 6.0 pad_maximum_fusion.2
  402.4 20.6 %pack.4.refs_0_ = bf16[49344,128]{1,0:T(8,128)(2,1)} custom-call(bf16[512,1024]{1,0:T(8,128)(2,1)S(1)} %copy-done.61, bf16[512,2048]{1,0:T(8,128)(2,1)S(1)} %copy-done.79, bf16[512,2048]{1,0:T(8,128)(2,1)} %get-tuple-element.212.refs_2_, bf16[512,2048]{1,0:T(8,128)(2,1)} %get-tuple-element.213.refs_3_, bf16[512,1024]{1,0:T(8,128)(2,1)S(1)} %copy-done.59, ...), custom_call_target="tpu_custom_call" | custom-call | flops 6442450944 | bytes 16777216 | tf_op jit(solution)/shard_map/pack/pallas_call | solution.py:611
  428.1 6.3 constant_dynamic-slice_fusion.2.refs_5_
  434.8 22.0 %collective-permute-start.44 = (bf16[144,1536]{1,0:T(8,128)(2,1)S(1)}, bf16[144,1536]{1,0:T(8,128)(2,1)}, u32[]{:S(2)}, u32[]{:S(2)}) collective-permute-start(bf16[144,1536]{1,0:T(8,128)(2,1)S(1)} %copy-done.33), channel_id=1, source_target_pairs={{0,2},{2,0},{1,3},{3,1},{4,6},{6,4},{5,7},{7,5},{8,10},{10,8},{9,1... | collective-permute-start | bytes 1327112 | tf_op jit(solution)/shard_map/ppermute | solution.py:250
  460.0 7.3 collective-permute-done.48
  471.1 27.1 %collective-permute-start.54 = (f32[4]{0:T(128)S(1)}, f32[4]{0:T(128)S(1)}, u32[]{:S(2)}, u32[]{:S(2)}) collective-permute-start(f32[4]{0:T(128)S(1)} %add.642.refs_6_.refs_11_), channel_id=1, source_target_pairs={{0,8},{8,0},{16,24},{24,16},{1,9},{9,1},{17,25},{25,17},{2,10},{10... | collective-permute-start | bytes 56 | tf_op jit(solution)/shard_map/ppermute | solution.py:250
  510.3 6.0 add_convert_fusion.1
  520.5 4.7 pack.5.refs_0_
  530.1 40.3 %ssm_back.1 = (f32[512,1536]{1,0:T(8,128)S(1)}, f32[512,128]{1,0:T(8,128)S(1)}, f32[512,128]{1,0:T(8,128)S(1)}, f32[12,8,512]{2,1,0:T(8,128)S(1)}) custom-call(s32[5]{0:T(128)S(1)} %copy-done.72, f32[512,1792]{1,0:T(8,128)} %fence.20.refs_0_.refs_1_.x_ref.b_ref.c_ref.refs_3_.refs_4_, f32[512,1536]{1,0:T(8,128)S(1)} %copy-done.8, ...), custom_call_target="tpu_custom_call" | custom-call | flops 3000000000 | bytes 9437184 | tf_op jit(solution)/shard_map/ssm_back/pallas_call | solution.py:1060
  582.1 15.4 %conv_back.1 = (bf16[512,1792]{1,0:T(8,128)(2,1)}, f32[16,1792]{1,0:T(8,128)}, f32[8,1792]{1,0:T(8,128)}, f32[8,1792]{1,0:T(8,128)}) custom-call(s32[5]{0:T(128)} %pad_add_fusion.1.refs_0_.meta_ref, f32[512,1536]{1,0:T(8,128)} %get-tuple-element.82.refs_1_, f32[512,128]{1,0:T(8,128)} %get-tuple-element.83.refs_2_, f32[512,128]{1,0:T(8,128)} %get-tuple-element.84.refs_3_, ...), custom_call_target="tpu_custom_call" | custom-call | flops 2000000000 | bytes 9175040 | tf_op jit(solution)/shard_map/conv_back/pallas_call | solution.py:801
  611.4 12.1 %pack.6.refs_0_ = bf16[49440,128]{1,0:T(8,128)(2,1)} custom-call(bf16[512,512]{1,0:T(8,128)(2,1)S(1)} %bitcast.295, bf16[512,1024]{1,0:T(8,128)(2,1)S(1)} %copy-done.2, bf16[512,1024]{1,0:T(8,128)(2,1)S(1)} %copy-done.7, bf16[512,1536]{1,0:T(8,128)(2,1)S(1)} %copy-done.20, bf16[512,1536]{1,0:T(8,128)(2,1)S(1)} %slice.362.refs_4_, ...), custom_call_target="tpu_custom_call", output_to_operand_aliasing={{}: (7, {})} | custom-call | flops 4026531840 | bytes 11010048 | tf_op jit(solution)/shard_map/pack/pallas_call | solution.py:611
  623.5 5.9 constant_dynamic-slice_fusion.1.refs_1_
  634.3 5.1 fusion.101
  641.2 5.5 collective-permute-start.62
  659.8 6.0 add_convert_fusion
  673.7 7.8 attend_back.2
  681.5 24.2 %collective-permute-done.58 = bf16[2,3104,128]{2,1,0:T(8,128)(2,1)} collective-permute-done((bf16[2,3104,128]{2,1,0:T(8,128)(2,1)}, bf16[2,3104,128]{2,1,0:T(8,128)(2,1)}, u32[]{:S(2)}, u32[]{:S(2)}) %collective-permute-start.58) | collective-permute-done | bytes 1589280 | tf_op jit(solution)/shard_map/ppermute | solution.py:250
  718.6 8.5 attend_back.3
  741.4 6.1 collective-permute-start.64
  768.8 11.4 %collective-permute-start.69 = (bf16[2,2,512,128]{3,2,1,0:T(8,128)(2,1)}, bf16[2,2,512,128]{3,2,1,0:T(8,128)(2,1)}, u32[]{:S(2)}, u32[]{:S(2)}) collective-permute-start(bf16[2,2,512,128]{3,2,1,0:T(8,128)(2,1)} %dynamic-slice_bitcast_fusion.21.refs_1_), channel_id=1, source_target_pairs={{0,4},{4,0},{1,5},{5,1},{2,6},{6,2},{3,7},{7,3},{8,12},{12,8},{9,1... | collective-permute-start | bytes 1572872 | tf_op jit(solution)/shard_map/ppermute | solution.py:250
  783.1 10.0 %collective-permute-done.69 = bf16[2,2,512,128]{3,2,1,0:T(8,128)(2,1)} collective-permute-done((bf16[2,2,512,128]{3,2,1,0:T(8,128)(2,1)}, bf16[2,2,512,128]{3,2,1,0:T(8,128)(2,1)}, u32[]{:S(2)}, u32[]{:S(2)}) %collective-permute-start.69) | collective-permute-done | bytes 524320 | tf_op jit(solution)/shard_map/ppermute | solution.py:250
  794.5 6.0 collective-permute-start.70
  800.5 5.6 add_add_fusion.4.refs_0_
  810.3 5.4 fusion.12
  815.7 5.4 pack.7
  829.8 15.5 %collective-permute-done.78 = bf16[3104,128]{1,0:T(8,128)(2,1)S(1)} collective-permute-done((bf16[3104,128]{1,0:T(8,128)(2,1)S(1)}, bf16[3104,128]{1,0:T(8,128)(2,1)S(1)}, u32[]{:S(2)}, u32[]{:S(2)}) %collective-permute-start.78) | collective-permute-done | bytes 794656 | tf_op jit(solution)/shard_map/ppermute | solution.py:250
  845.3 19.1 %collective-permute-done.77 = bf16[3104,128]{1,0:T(8,128)(2,1)S(1)} collective-permute-done((bf16[3104,128]{1,0:T(8,128)(2,1)S(1)}, bf16[3104,128]{1,0:T(8,128)(2,1)S(1)}, u32[]{:S(2)}, u32[]{:S(2)}) %collective-permute-start.77) | collective-permute-done | bytes 794656 | tf_op jit(solution)/shard_map/ppermute | solution.py:250
  903.0 4.8 fusion.14
  (852 shorter events, 381.1 us)
Async XLA Ops:
  13.9 21.6 %collective-permute-start.27 = (bf16[2,3088,128]{2,1,0:T(8,128)(2,1)}, bf16[2,3088,128]{2,1,0:T(8,128)(2,1)}, u32[]{:S(2)}, u32[]{:S(2)}) collective-permute-start(bf16[2,3088,128]{2,1,0:T(8,128)(2,1)} %maximum_select_fusion), channel_id=1, source_target_pairs={{16,8},{25,17},{18,10},{27,19},{20,12},{29,21},{22,14},{31,23}} | collective-permute-start | bytes 4743176 | tf_op jit(solution)/shard_map/ppermute | solution.py:301
  35.5 32.6 %collective-permute-start.29 = (bf16[2,3088,128]{2,1,0:T(8,128)(2,1)}, bf16[2,3088,128]{2,1,0:T(8,128)(2,1)}, u32[]{:S(2)}, u32[]{:S(2)}) collective-permute-start(bf16[2,3088,128]{2,1,0:T(8,128)(2,1)} %collective-permute-done.27), channel_id=1, source_target_pairs={{8,0},{17,9},{10,2},{19,11},{12,4},{21,13},{14,6},{23,15}} | collective-permute-start | bytes 4743176 | tf_op jit(solution)/shard_map/ppermute | solution.py:303
  39.8 29.8 %collective-permute-start.19 = (bf16[3088,128]{1,0:T(8,128)(2,1)}, bf16[3088,128]{1,0:T(8,128)(2,1)}, u32[]{:S(2)}, u32[]{:S(2)}) collective-permute-start(bf16[3088,128]{1,0:T(8,128)(2,1)} %add_select_fusion.1), channel_id=1, source_target_pairs={{0,1},{1,0},{2,3},{3,2},{4,5},{5,4},{6,7},{7,6},{8,9},{9,8},{10,11... | collective-permute-start | bytes 2371592 | tf_op jit(solution)/shard_map/ppermute | solution.py:298
  40.4 42.4 %collective-permute-start.17 = (bf16[3088,128]{1,0:T(8,128)(2,1)}, bf16[3088,128]{1,0:T(8,128)(2,1)}, u32[]{:S(2)}, u32[]{:S(2)}) collective-permute-start(bf16[3088,128]{1,0:T(8,128)(2,1)} %add_select_fusion.1), channel_id=1, source_target_pairs={{0,4},{4,0},{1,5},{5,1},{2,6},{6,2},{3,7},{7,3},{8,12},{12,8},{9,1... | collective-permute-start | bytes 2371592 | tf_op jit(solution)/shard_map/ppermute | solution.py:294
  41.9 42.4 %collective-permute-start.16 = (bf16[3088,128]{1,0:T(8,128)(2,1)}, bf16[3088,128]{1,0:T(8,128)(2,1)}, u32[]{:S(2)}, u32[]{:S(2)}) collective-permute-start(bf16[3088,128]{1,0:T(8,128)(2,1)} %add_select_fusion.1), channel_id=1, source_target_pairs={{0,2},{2,0},{1,3},{3,1},{4,6},{6,4},{5,7},{7,5},{8,10},{10,8},{9,1... | collective-permute-start | bytes 2371592 | tf_op jit(solution)/shard_map/ppermute | solution.py:293
  44.9 39.5 %collective-permute-start.8 = (bf16[3088,128]{1,0:T(8,128)(2,1)S(1)}, bf16[3088,128]{1,0:T(8,128)(2,1)S(1)}, u32[]{:S(2)}, u32[]{:S(2)}) collective-permute-start(bf16[3088,128]{1,0:T(8,128)(2,1)S(1)} %add_select_fusion.2), channel_id=1, source_target_pairs={{0,1},{1,0},{2,3},{3,2},{4,5},{5,4},{6,7},{7,6},{8,9},{9,8},{10,11... | collective-permute-start | bytes 2371592 | tf_op jit(solution)/shard_map/ppermute | solution.py:298
  69.6 42.3 %collective-permute-start.30 = (bf16[2,3088,128]{2,1,0:T(8,128)(2,1)}, bf16[2,3088,128]{2,1,0:T(8,128)(2,1)}, u32[]{:S(2)}, u32[]{:S(2)}) collective-permute-start(bf16[2,3088,128]{2,1,0:T(8,128)(2,1)} %collective-permute-done.29), channel_id=1, source_target_pairs={{9,1},{11,3},{13,5},{15,7}} | collective-permute-start | bytes 4743176 | tf_op jit(solution)/shard_map/ppermute | solution.py:304
  82.8 19.3 %collective-permute-start.6 = (bf16[3088,128]{1,0:T(8,128)(2,1)S(1)}, bf16[3088,128]{1,0:T(8,128)(2,1)S(1)}, u32[]{:S(2)}, u32[]{:S(2)}) collective-permute-start(bf16[3088,128]{1,0:T(8,128)(2,1)S(1)} %add_select_fusion.2), channel_id=1, source_target_pairs={{0,4},{4,0},{1,5},{5,1},{2,6},{6,2},{3,7},{7,3},{8,12},{12,8},{9,1... | collective-permute-start | bytes 2371592 | tf_op jit(solution)/shard_map/ppermute | solution.py:294
  84.4 20.3 %collective-permute-start.18 = (bf16[3088,128]{1,0:T(8,128)(2,1)}, bf16[3088,128]{1,0:T(8,128)(2,1)S(1)}, u32[]{:S(2)}, u32[]{:S(2)}) collective-permute-start(bf16[3088,128]{1,0:T(8,128)(2,1)} %collective-permute-done.17), channel_id=1, source_target_pairs={{0,2},{2,0},{1,3},{3,1},{4,6},{6,4},{5,7},{7,5},{8,10},{10,8},{9,1... | collective-permute-start | bytes 2371592 | tf_op jit(solution)/shard_map/ppermute | solution.py:295
  85.0 26.8 %collective-permute-start.7 = (bf16[3088,128]{1,0:T(8,128)(2,1)S(1)}, bf16[3088,128]{1,0:T(8,128)(2,1)S(1)}, u32[]{:S(2)}, u32[]{:S(2)}) collective-permute-start(bf16[3088,128]{1,0:T(8,128)(2,1)S(1)} %collective-permute-done.5), channel_id=1, source_target_pairs={{0,4},{4,0},{1,5},{5,1},{2,6},{6,2},{3,7},{7,3},{8,12},{12,8},{9,1... | collective-permute-start | bytes 2371592 | tf_op jit(solution)/shard_map/ppermute | solution.py:295
  116.6 171.2 %collective-permute-start.38 = (bf16[2,3088,128]{2,1,0:T(8,128)(2,1)}, bf16[2,3088,128]{2,1,0:T(8,128)(2,1)}, u32[]{:S(2)}, u32[]{:S(2)}) collective-permute-start(bf16[2,3088,128]{2,1,0:T(8,128)(2,1)} %add_select_fusion.refs_2_.refs_4_.refs_6_.refs_18_), channel_id=1, source_target_pairs={{0,1},{1,0},{2,3},{3,2},{4,5},{5,4},{6,7},{7,6},{8,9},{9,8},{10,11... | collective-permute-start | bytes 4743176 | tf_op jit(solution)/shard_map/ppermute | solution.py:250
  116.8 59.7 %collective-permute-start.32 = (bf16[2,3088,128]{2,1,0:T(8,128)(2,1)}, bf16[2,3088,128]{2,1,0:T(8,128)(2,1)}, u32[]{:S(2)}, u32[]{:S(2)}) collective-permute-start(bf16[2,3088,128]{2,1,0:T(8,128)(2,1)} %add_select_fusion.refs_2_.refs_4_.refs_6_.refs_18_), channel_id=1, source_target_pairs={{0,4},{4,0},{1,5},{5,1},{2,6},{6,2},{3,7},{7,3},{8,12},{12,8},{9,1... | collective-permute-start | bytes 4743176 | tf_op jit(solution)/shard_map/ppermute | solution.py:250
  118.3 60.9 %collective-permute-start.31 = (bf16[2,3088,128]{2,1,0:T(8,128)(2,1)}, bf16[2,3088,128]{2,1,0:T(8,128)(2,1)}, u32[]{:S(2)}, u32[]{:S(2)}) collective-permute-start(bf16[2,3088,128]{2,1,0:T(8,128)(2,1)} %add_select_fusion.refs_2_.refs_4_.refs_6_.refs_18_), channel_id=1, source_target_pairs={{0,2},{2,0},{1,3},{3,1},{4,6},{6,4},{5,7},{7,5},{8,10},{10,8},{9,1... | collective-permute-start | bytes 4743176 | tf_op jit(solution)/shard_map/ppermute | solution.py:250
  176.4 50.7 %collective-permute-start.25 = (bf16[2,2,2,512,128]{4,3,2,1,0:T(8,128)(2,1)}, bf16[2,2,2,512,128]{4,3,2,1,0:T(8,128)(2,1)}, u32[]{:S(2)}, u32[]{:S(2)}) collective-permute-start(bf16[2,2,2,512,128]{4,3,2,1,0:T(8,128)(2,1)} %pad_maximum_fusion.10.refs_1_.refs_2_), channel_id=1, source_target_pairs={{0,1},{1,0},{2,3},{3,2},{4,5},{5,4},{6,7},{7,6},{8,9},{9,8},{10,11... | collective-permute-start | bytes 3145736 | tf_op jit(solution)/shard_map/ppermute | solution.py:250
  178.7 35.4 %collective-permute-start.34 = (bf16[1,3088,128]{2,1,0:T(8,128)(2,1)}, bf16[1,3088,128]{2,1,0:T(8,128)(2,1)S(1)}, u32[]{:S(2)}, u32[]{:S(2)}) collective-permute-start(bf16[1,3088,128]{2,1,0:T(8,128)(2,1)} %slice.336.refs_8_), channel_id=1, source_target_pairs={{0,2},{2,0},{1,3},{3,1},{4,6},{6,4},{5,7},{7,5},{8,10},{10,8},{9,1... | collective-permute-start | bytes 2371592 | tf_op jit(solution)/shard_map/ppermute | solution.py:250
  181.3 32.8 %collective-permute-start.33 = (bf16[1,3088,128]{2,1,0:T(8,128)(2,1)}, bf16[1,3088,128]{2,1,0:T(8,128)(2,1)S(1)}, u32[]{:S(2)}, u32[]{:S(2)}) collective-permute-start(bf16[1,3088,128]{2,1,0:T(8,128)(2,1)} %slice.335.refs_7_), channel_id=1, source_target_pairs={{0,4},{4,0},{1,5},{5,1},{2,6},{6,2},{3,7},{7,3},{8,12},{12,8},{9,1... | collective-permute-start | bytes 2371592 | tf_op jit(solution)/shard_map/ppermute | solution.py:250
  200.6 87.2 %collective-permute-start.40 = (bf16[2,3088,128]{2,1,0:T(8,128)(2,1)}, bf16[2,3088,128]{2,1,0:T(8,128)(2,1)}, u32[]{:S(2)}, u32[]{:S(2)}) collective-permute-start(bf16[2,3088,128]{2,1,0:T(8,128)(2,1)} %collective-permute-done.32.refs_4_.refs_6_.refs_8_.refs_20_), channel_id=1, source_target_pairs={{0,1},{1,0},{2,3},{3,2},{4,5},{5,4},{6,7},{7,6},{8,9},{9,8},{10,11... | collective-permute-start | bytes 4743176 | tf_op jit(solution)/shard_map/ppermute | solution.py:250
  214.0 73.8 %collective-permute-start.39 = (bf16[2,3088,128]{2,1,0:T(8,128)(2,1)}, bf16[2,3088,128]{2,1,0:T(8,128)(2,1)}, u32[]{:S(2)}, u32[]{:S(2)}) collective-permute-start(bf16[2,3088,128]{2,1,0:T(8,128)(2,1)} %collective-permute-done.31.refs_3_.refs_5_.refs_7_.refs_19_), channel_id=1, source_target_pairs={{0,1},{1,0},{2,3},{3,2},{4,5},{5,4},{6,7},{7,6},{8,9},{9,8},{10,11... | collective-permute-start | bytes 4743176 | tf_op jit(solution)/shard_map/ppermute | solution.py:250
  231.3 56.5 %collective-permute-start.42 = (bf16[1,3088,128]{2,1,0:T(8,128)(2,1)S(1)}, bf16[1,3088,128]{2,1,0:T(8,128)(2,1)}, u32[]{:S(2)}, u32[]{:S(2)}) collective-permute-start(bf16[1,3088,128]{2,1,0:T(8,128)(2,1)S(1)} %copy-done.16), channel_id=1, source_target_pairs={{0,1},{1,0},{2,3},{3,2},{4,5},{5,4},{6,7},{7,6},{8,9},{9,8},{10,11... | collective-permute-start | bytes 2371592 | tf_op jit(solution)/shard_map/ppermute | solution.py:250
  268.3 19.5 %collective-permute-start.41 = (bf16[1,3088,128]{2,1,0:T(8,128)(2,1)S(1)}, bf16[1,3088,128]{2,1,0:T(8,128)(2,1)}, u32[]{:S(2)}, u32[]{:S(2)}) collective-permute-start(bf16[1,3088,128]{2,1,0:T(8,128)(2,1)S(1)} %copy-done.18), channel_id=1, source_target_pairs={{0,1},{1,0},{2,3},{3,2},{4,5},{5,4},{6,7},{7,6},{8,9},{9,8},{10,11... | collective-permute-start | bytes 2371592 | tf_op jit(solution)/shard_map/ppermute | solution.py:250
  363.8 59.2 %collective-permute-start.46 = (f32[4]{0:T(128)S(1)}, f32[4]{0:T(128)S(1)}, u32[]{:S(2)}, u32[]{:S(2)}) collective-permute-start(f32[4]{0:T(128)S(1)} %pad_maximum_fusion.27.refs_8_), channel_id=1, source_target_pairs={{0,4},{4,0},{1,5},{5,1},{2,6},{6,2},{3,7},{7,3},{8,12},{12,8},{9,1... | collective-permute-start | bytes 56 | tf_op jit(solution)/shard_map/ppermute | solution.py:250
  396.2 30.0 %collective-permute-start.43 = (bf16[144,1536]{1,0:T(8,128)(2,1)S(1)}, bf16[144,1536]{1,0:T(8,128)(2,1)S(1)}, u32[]{:S(2)}, u32[]{:S(2)}) collective-permute-start(bf16[144,1536]{1,0:T(8,128)(2,1)S(1)} %pad_maximum_fusion.16.refs_7_), channel_id=1, source_target_pairs={{0,1},{1,0},{2,3},{3,2},{4,5},{5,4},{6,7},{7,6},{8,9},{9,8},{10,11... | collective-permute-start | bytes 1327112 | tf_op jit(solution)/shard_map/ppermute | solution.py:250
  434.4 75.9 %collective-permute-start.47 = (bf16[24688,128]{1,0:T(8,128)(2,1)}, bf16[24688,128]{1,0:T(8,128)(2,1)}, u32[]{:S(2)}, u32[]{:S(2)}) collective-permute-start(bf16[24688,128]{1,0:T(8,128)(2,1)} %constant_dynamic-slice_fusion.2.refs_5_), channel_id=1, source_target_pairs={{0,1},{1,0},{2,3},{3,2},{4,5},{5,4},{6,7},{7,6},{8,9},{9,8},{10,11... | collective-permute-start | bytes 18960392 | tf_op jit(solution)/shard_map/ppermute | solution.py:250
  434.8 71.2 %collective-permute-start.44 = (bf16[144,1536]{1,0:T(8,128)(2,1)S(1)}, bf16[144,1536]{1,0:T(8,128)(2,1)}, u32[]{:S(2)}, u32[]{:S(2)}) collective-permute-start(bf16[144,1536]{1,0:T(8,128)(2,1)S(1)} %copy-done.33), channel_id=1, source_target_pairs={{0,2},{2,0},{1,3},{3,1},{4,6},{6,4},{5,7},{7,5},{8,10},{10,8},{9,1... | collective-permute-start | bytes 1327112 | tf_op jit(solution)/shard_map/ppermute | solution.py:250
  471.1 30.5 %collective-permute-start.54 = (f32[4]{0:T(128)S(1)}, f32[4]{0:T(128)S(1)}, u32[]{:S(2)}, u32[]{:S(2)}) collective-permute-start(f32[4]{0:T(128)S(1)} %add.642.refs_6_.refs_11_), channel_id=1, source_target_pairs={{0,8},{8,0},{16,24},{24,16},{1,9},{9,1},{17,25},{25,17},{2,10},{10... | collective-permute-start | bytes 56 | tf_op jit(solution)/shard_map/ppermute | solution.py:250
  519.8 50.6 %collective-permute-start.49 = (bf16[2,3104,128]{2,1,0:T(8,128)(2,1)}, bf16[2,3104,128]{2,1,0:T(8,128)(2,1)}, u32[]{:S(2)}, u32[]{:S(2)}) collective-permute-start(bf16[2,3104,128]{2,1,0:T(8,128)(2,1)} %pad_maximum_fusion.5.refs_11_), channel_id=1, source_target_pairs={{0,4},{4,0},{1,5},{5,1},{2,6},{6,2},{3,7},{7,3},{8,12},{12,8},{9,1... | collective-permute-start | bytes 4767752 | tf_op jit(solution)/shard_map/ppermute | solution.py:250
  528.2 47.3 %collective-permute-start.50 = (bf16[2,3104,128]{2,1,0:T(8,128)(2,1)S(1)}, bf16[2,3104,128]{2,1,0:T(8,128)(2,1)S(1)}, u32[]{:S(2)}, u32[]{:S(2)}) collective-permute-start(bf16[2,3104,128]{2,1,0:T(8,128)(2,1)S(1)} %pad_maximum_fusion.6.refs_12_), channel_id=1, source_target_pairs={{0,2},{2,0},{1,3},{3,1},{4,6},{6,4},{5,7},{7,5},{8,10},{10,8},{9,1... | collective-permute-start | bytes 4767752 | tf_op jit(solution)/shard_map/ppermute | solution.py:250
  573.8 24.6 %collective-permute-start.52 = (bf16[3104,128]{1,0:T(8,128)(2,1)S(1)}, bf16[3104,128]{1,0:T(8,128)(2,1)}, u32[]{:S(2)}, u32[]{:S(2)}) collective-permute-start(bf16[3104,128]{1,0:T(8,128)(2,1)S(1)} %dynamic-slice_bitcast_fusion.14.refs_4_.refs_9_), channel_id=1, source_target_pairs={{0,2},{2,0},{1,3},{3,1},{4,6},{6,4},{5,7},{7,5},{8,10},{10,8},{9,1... | collective-permute-start | bytes 2383880 | tf_op jit(solution)/shard_map/ppermute | solution.py:250
  579.3 20.6 %collective-permute-start.53 = (bf16[3104,128]{1,0:T(8,128)(2,1)}, bf16[3104,128]{1,0:T(8,128)(2,1)}, u32[]{:S(2)}, u32[]{:S(2)}) collective-permute-start(bf16[3104,128]{1,0:T(8,128)(2,1)} %dynamic-slice_bitcast_fusion.11.refs_5_.refs_10_), channel_id=1, source_target_pairs={{0,4},{4,0},{1,5},{5,1},{2,6},{6,2},{3,7},{7,3},{8,12},{12,8},{9,1... | collective-permute-start | bytes 2383880 | tf_op jit(solution)/shard_map/ppermute | solution.py:250
  629.5 30.3 %collective-permute-start.57 = (bf16[24688,128]{1,0:T(8,128)(2,1)}, bf16[24688,128]{1,0:T(8,128)(2,1)}, u32[]{:S(2)}, u32[]{:S(2)}) collective-permute-start(bf16[24688,128]{1,0:T(8,128)(2,1)} %constant_dynamic-slice_fusion.1.refs_1_), channel_id=1, source_target_pairs={{0,1},{1,0},{2,3},{3,2},{4,5},{5,4},{6,7},{7,6},{8,9},{9,8},{10,11... | collective-permute-start | bytes 18960392 | tf_op jit(solution)/shard_map/ppermute | solution.py:250
  641.2 90.4 %collective-permute-start.62 = (bf16[2,3104,128]{2,1,0:T(8,128)(2,1)}, bf16[2,3104,128]{2,1,0:T(8,128)(2,1)}, u32[]{:S(2)}, u32[]{:S(2)}) collective-permute-start(bf16[2,3104,128]{2,1,0:T(8,128)(2,1)} %pad_maximum_fusion.7.refs_4_.refs_5_.refs_6_.refs_9_.refs_10_.refs_11_.refs_2_.refs_3_), channel_id=1, source_target_pairs={{0,16},{9,25},{2,18},{11,27},{4,20},{13,29},{6,22},{15,31}} | collective-permute-start | bytes 4767752 | tf_op jit(solution)/shard_map/ppermute | solution.py:250
  646.6 86.2 %collective-permute-start.61 = (bf16[2,3104,128]{2,1,0:T(8,128)(2,1)}, bf16[2,3104,128]{2,1,0:T(8,128)(2,1)}, u32[]{:S(2)}, u32[]{:S(2)}) collective-permute-start(bf16[2,3104,128]{2,1,0:T(8,128)(2,1)} %pad_maximum_fusion.7.refs_4_.refs_5_.refs_6_.refs_9_.refs_10_.refs_11_.refs_2_.refs_3_), channel_id=1, source_target_pairs={{8,16},{17,25},{10,18},{19,27},{12,20},{21,29},{14,22},{23,31}} | collective-permute-start | bytes 4767752 | tf_op jit(solution)/shard_map/ppermute | solution.py:250
  648.4 85.9 %collective-permute-start.63 = (bf16[2,3104,128]{2,1,0:T(8,128)(2,1)}, bf16[2,3104,128]{2,1,0:T(8,128)(2,1)}, u32[]{:S(2)}, u32[]{:S(2)}) collective-permute-start(bf16[2,3104,128]{2,1,0:T(8,128)(2,1)} %pad_maximum_fusion.7.refs_4_.refs_5_.refs_6_.refs_9_.refs_10_.refs_11_.refs_2_.refs_3_), channel_id=1, source_target_pairs={{24,16},{1,25},{26,18},{3,27},{28,20},{5,29},{30,22},{7,31}} | collective-permute-start | bytes 4767752 | tf_op jit(solution)/shard_map/ppermute | solution.py:250
  669.1 36.6 %collective-permute-start.58 = (bf16[2,3104,128]{2,1,0:T(8,128)(2,1)}, bf16[2,3104,128]{2,1,0:T(8,128)(2,1)}, u32[]{:S(2)}, u32[]{:S(2)}) collective-permute-start(bf16[2,3104,128]{2,1,0:T(8,128)(2,1)} %pad_maximum_fusion.8.refs_1_.refs_7_), channel_id=1, source_target_pairs={{0,4},{4,0},{1,5},{5,1},{2,6},{6,2},{3,7},{7,3},{8,12},{12,8},{9,1... | collective-permute-start | bytes 4767752 | tf_op jit(solution)/shard_map/ppermute | solution.py:250
  670.9 39.7 %collective-permute-start.59 = (bf16[2,3104,128]{2,1,0:T(8,128)(2,1)}, bf16[2,3104,128]{2,1,0:T(8,128)(2,1)}, u32[]{:S(2)}, u32[]{:S(2)}) collective-permute-start(bf16[2,3104,128]{2,1,0:T(8,128)(2,1)} %pad_maximum_fusion.9.refs_2_.refs_8_), channel_id=1, source_target_pairs={{0,2},{2,0},{1,3},{3,1},{4,6},{6,4},{5,7},{7,5},{8,10},{10,8},{9,1... | collective-permute-start | bytes 4767752 | tf_op jit(solution)/shard_map/ppermute | solution.py:250
  708.7 20.1 %collective-permute-start.60 = (bf16[3104,128]{1,0:T(8,128)(2,1)}, bf16[3104,128]{1,0:T(8,128)(2,1)}, u32[]{:S(2)}, u32[]{:S(2)}) collective-permute-start(bf16[3104,128]{1,0:T(8,128)(2,1)} %dynamic-slice_bitcast_fusion.4.refs_2_.refs_7_), channel_id=1, source_target_pairs={{0,2},{2,0},{1,3},{3,1},{4,6},{6,4},{5,7},{7,5},{8,10},{10,8},{9,1... | collective-permute-start | bytes 2383880 | tf_op jit(solution)/shard_map/ppermute | solution.py:250
  713.7 43.4 %collective-permute-start.65 = (bf16[3104,128]{1,0:T(8,128)(2,1)S(1)}, bf16[3104,128]{1,0:T(8,128)(2,1)}, u32[]{:S(2)}, u32[]{:S(2)}) collective-permute-start(bf16[3104,128]{1,0:T(8,128)(2,1)S(1)} %dynamic-slice_bitcast_fusion.1.refs_3_.refs_8_), channel_id=1, source_target_pairs={{0,4},{4,0},{1,5},{5,1},{2,6},{6,2},{3,7},{7,3},{8,12},{12,8},{9,1... | collective-permute-start | bytes 2383880 | tf_op jit(solution)/shard_map/ppermute | solution.py:250
  730.2 50.0 %collective-permute-start.68 = (bf16[3104,128]{1,0:T(8,128)(2,1)S(1)}, bf16[3104,128]{1,0:T(8,128)(2,1)}, u32[]{:S(2)}, u32[]{:S(2)}) collective-permute-start(bf16[3104,128]{1,0:T(8,128)(2,1)S(1)} %fusion.20.refs_2_.refs_3_.refs_4_), channel_id=1, source_target_pairs={{24,0},{1,9},{26,2},{3,11},{28,4},{5,13},{30,6},{7,15}} | collective-permute-start | bytes 2383880 | tf_op jit(solution)/shard_map/ppermute | solution.py:250
  731.5 48.6 %collective-permute-start.67 = (bf16[3104,128]{1,0:T(8,128)(2,1)}, bf16[3104,128]{1,0:T(8,128)(2,1)}, u32[]{:S(2)}, u32[]{:S(2)}) collective-permute-start(bf16[3104,128]{1,0:T(8,128)(2,1)} %copy-done.80), channel_id=1, source_target_pairs={{16,0},{25,9},{18,2},{27,11},{20,4},{29,13},{22,6},{31,15}} | collective-permute-start | bytes 2383880 | tf_op jit(solution)/shard_map/ppermute | solution.py:250
  732.8 47.3 %collective-permute-start.66 = (bf16[3104,128]{1,0:T(8,128)(2,1)}, bf16[3104,128]{1,0:T(8,128)(2,1)}, u32[]{:S(2)}, u32[]{:S(2)}) collective-permute-start(bf16[3104,128]{1,0:T(8,128)(2,1)} %copy-done.80), channel_id=1, source_target_pairs={{8,0},{17,9},{10,2},{19,11},{12,4},{21,13},{14,6},{23,15}} | collective-permute-start | bytes 2383880 | tf_op jit(solution)/shard_map/ppermute | solution.py:250
  741.4 24.5 %collective-permute-start.64 = (bf16[2,2,2,512,128]{4,3,2,1,0:T(8,128)(2,1)}, bf16[2,2,2,512,128]{4,3,2,1,0:T(8,128)(2,1)}, u32[]{:S(2)}, u32[]{:S(2)}) collective-permute-start(bf16[2,2,2,512,128]{4,3,2,1,0:T(8,128)(2,1)} %dynamic-slice_bitcast_fusion.refs_1_), channel_id=1, source_target_pairs={{0,1},{1,0},{2,3},{3,2},{4,5},{5,4},{6,7},{7,6},{8,9},{9,8},{10,11... | collective-permute-start | bytes 3145736 | tf_op jit(solution)/shard_map/ppermute | solution.py:250
  768.8 24.3 %collective-permute-start.69 = (bf16[2,2,512,128]{3,2,1,0:T(8,128)(2,1)}, bf16[2,2,512,128]{3,2,1,0:T(8,128)(2,1)}, u32[]{:S(2)}, u32[]{:S(2)}) collective-permute-start(bf16[2,2,512,128]{3,2,1,0:T(8,128)(2,1)} %dynamic-slice_bitcast_fusion.21.refs_1_), channel_id=1, source_target_pairs={{0,4},{4,0},{1,5},{5,1},{2,6},{6,2},{3,7},{7,3},{8,12},{12,8},{9,1... | collective-permute-start | bytes 1572872 | tf_op jit(solution)/shard_map/ppermute | solution.py:250
  822.5 22.8 %collective-permute-start.78 = (bf16[3104,128]{1,0:T(8,128)(2,1)S(1)}, bf16[3104,128]{1,0:T(8,128)(2,1)S(1)}, u32[]{:S(2)}, u32[]{:S(2)}) collective-permute-start(bf16[3104,128]{1,0:T(8,128)(2,1)S(1)} %copy-done.3), channel_id=1, source_target_pairs={{24,0},{1,9},{26,2},{3,11},{28,4},{5,13},{30,6},{7,15}} | collective-permute-start | bytes 2383880 | tf_op jit(solution)/shard_map/ppermute | solution.py:250
  823.9 40.5 %collective-permute-start.77 = (bf16[3104,128]{1,0:T(8,128)(2,1)S(1)}, bf16[3104,128]{1,0:T(8,128)(2,1)S(1)}, u32[]{:S(2)}, u32[]{:S(2)}) collective-permute-start(bf16[3104,128]{1,0:T(8,128)(2,1)S(1)} %copy-done.3), channel_id=1, source_target_pairs={{16,0},{25,9},{18,2},{27,11},{20,4},{29,13},{22,6},{31,15}} | collective-permute-start | bytes 2383880 | tf_op jit(solution)/shard_map/ppermute | solution.py:250
  825.2 39.2 %collective-permute-start.76 = (bf16[3104,128]{1,0:T(8,128)(2,1)S(1)}, bf16[3104,128]{1,0:T(8,128)(2,1)S(1)}, u32[]{:S(2)}, u32[]{:S(2)}) collective-permute-start(bf16[3104,128]{1,0:T(8,128)(2,1)S(1)} %copy-done.3), channel_id=1, source_target_pairs={{8,0},{17,9},{10,2},{19,11},{12,4},{21,13},{14,6},{23,15}} | collective-permute-start | bytes 2383880 | tf_op jit(solution)/shard_map/ppermute | solution.py:250
  828.0 39.7 %collective-permute-start.72 = (bf16[2,400,128]{2,1,0:T(8,128)(2,1)S(1)}, bf16[2,400,128]{2,1,0:T(8,128)(2,1)S(1)}, u32[]{:S(2)}, u32[]{:S(2)}) collective-permute-start(bf16[2,400,128]{2,1,0:T(8,128)(2,1)S(1)} %dynamic-slice_bitcast_fusion.24), channel_id=1, source_target_pairs={{0,2},{2,0},{1,3},{3,1},{4,6},{6,4},{5,7},{7,5},{8,10},{10,8},{9,1... | collective-permute-start | bytes 614408 | tf_op jit(solution)/shard_map/ppermute | solution.py:250
  881.7 27.8 %collective-permute-start.87 = (bf16[3104,128]{1,0:T(8,128)(2,1)}, bf16[3104,128]{1,0:T(8,128)(2,1)S(1)}, u32[]{:S(2)}, u32[]{:S(2)}) collective-permute-start(bf16[3104,128]{1,0:T(8,128)(2,1)} %get-tuple-element.170.refs_5_), channel_id=1, source_target_pairs={{0,1},{9,8},{16,17},{25,24},{2,3},{11,10},{18,19},{27,26},{4,5},{1... | collective-permute-start | bytes 2383880 | tf_op jit(solution)/shard_map/ppermute | solution.py:250
  883.1 26.4 %collective-permute-start.86 = (bf16[3104,128]{1,0:T(8,128)(2,1)}, bf16[3104,128]{1,0:T(8,128)(2,1)S(1)}, u32[]{:S(2)}, u32[]{:S(2)}) collective-permute-start(bf16[3104,128]{1,0:T(8,128)(2,1)} %get-tuple-element.128.refs_1_), channel_id=1, source_target_pairs={{0,1},{9,8},{16,17},{25,24},{2,3},{11,10},{18,19},{27,26},{4,5},{1... | collective-permute-start | bytes 2383880 | tf_op jit(solution)/shard_map/ppermute | solution.py:250
  (251 other events, 2556.5 us)

commit v8 on v7

--- a/solution.py
+++ b/solution.py
@@ -273,9 +273,10 @@
 
 def bracket(call, flows):
     out = call([value for flow in flows for value in flow.values()])
+    out = list(out) if isinstance(out, (list, tuple)) else [out]
     for flow in flows:
-        flow.go()
-    return fence(out if isinstance(out, (list, tuple)) else [out], [v for flow in flows for v in flow.values()])
+        flow.go(out[-1:])
+    return fence(out, [v for flow in flows for v in flow.values()])
 
 
 def gather_lines(params):
@@ -305,8 +306,8 @@
     column = jnp.where(z == 2 + c, here, one + side + two + three)
     late = []
     for part in range(2):
-        for first in (16, 21):
-            late += [(first, part), (first + 1, part), (first + 2, part), (first + 3 + part, 0)]
+        for first in (16, 20):
+            late += [(first + k, part) for k in range(4)]
     shard = np.arange(32)
     sz, sy, sx, sc = shard // 8, shard // 4 % 2, shard // 2 % 2, shard % 2
     away = jnp.where(sz % 2 == c, 0, 4)
@@ -317,7 +318,7 @@
 def spread_stages(column):
     over_x, over_y = yield [(column, "x", SWAP), (column, "y", SWAP)]
     corners = yield [(over_x[:1], "y", SWAP), (over_y[1:], "x", SWAP)]
-    local = [column, over_x, over_y] + list(corners)
+    local = [column, over_x, over_y, jnp.concatenate(corners)]
     return local + list((yield [(piece, "c", SWAP) for piece in local]))
 
 
@@ -416,7 +417,7 @@
             @pl.when((step >= begin) & (step < begin + blocks))
             def _():
                 block = step - begin
-                side = lax.rem(block, 2)
+                side = lax.rem(block, DEPTH)
 
                 def written(k, s):
                     return pltpu.make_async_copy(
@@ -425,9 +426,9 @@
                         out_sem.at[s],
                     )
 
-                @pl.when(block >= 2)
+                @pl.when(block >= DEPTH)
                 def _():
-                    written(block - 2, side).wait()
+                    written(block - DEPTH, side).wait()
 
                 def tile(j):
                     picked = flat[pl.ds(base_row + j, tall, stride=per_row), :]
@@ -449,9 +450,8 @@
 
                 @pl.when(block == blocks - 1)
                 def _():
-                    if blocks > 1:
-                        written(block - 1, 1 - side).wait()
-                    written(block, side).wait()
+                    for back in reversed(range(min(DEPTH, blocks))):
+                        written(block - back, lax.rem(block - back, DEPTH)).wait()
 
     return pl.pallas_call(
         pinned(kernel, 2 + count_buffers, after),
@@ -460,12 +460,12 @@
             grid=(total,),
             in_specs=[pl.BlockSpec(memory_space=pl.ANY)] * count_buffers + pins(after),
             out_specs=[pl.BlockSpec(memory_space=pl.ANY)] * len(segments),
-            scratch_shapes=[pltpu.VMEM((2,) + size, jnp.bfloat16) for size in sizes]
+            scratch_shapes=[pltpu.VMEM((DEPTH,) + size, jnp.bfloat16) for size in sizes]
             + [
                 pltpu.VMEM((DEPTH, 2, window, LINE), jnp.bfloat16),
                 pltpu.VMEM((room, LINE), jnp.float32),
                 pltpu.SemaphoreType.DMA((DEPTH, 2)),
-                pltpu.SemaphoreType.DMA((2,)),
+                pltpu.SemaphoreType.DMA((DEPTH,)),
             ],
         ),
         out_shape=[jax.ShapeDtypeStruct((rows, columns), jnp.bfloat16) for _, rows, columns in segments],
@@ -1526,6 +1526,7 @@
     )
     if fast:
         keys_flow = Flow(gather_stages(kv_local))
+        keys_flow.go()
         (conv_values,) = bracket(convolve, [keys_flow, spread_flow])
     else:
         conv_values = convolve(())
@@ -1554,12 +1555,11 @@
     if fast:
         (local_state,) = bracket(lambda after: summarize((*after, *spread_flow.values())), [keys_flow])
         scan = Flow(scan_stages(carry_all, local_state, False))
-        (gate_in,) = fence([hidden], scan.values() + keys_flow.values())
+        key_blocks = keys_flow.result
+        (gate_in,) = fence([hidden], scan.values())
         gate_ssm = matmul(gate_in, weights[W_GATE_SSM])
         scan.go()
-        keys_flow.go()
-        key_blocks = keys_flow.result
-        (gate_ssm,) = fence([gate_ssm], scan.values() + keys_flow.values())
+        (gate_ssm,) = fence([gate_ssm], scan.values())
         scan.go()
         mixed, logs = bracket(
             lambda after: attention_forward(
@@ -1623,20 +1623,19 @@
     grad_state_local = weighted_state(conv_values, PAIRS + 1, grad_ssm_y, entry_rows)
     if fast:
         scan = Flow(scan_stages(carry_all, grad_state_local, True))
-        stats_flow = Flow(sum_stages(squares))
         (late,) = bracket(
             lambda after: pack_late(
                 (hidden_two, grad_gate), (hidden_two, grad_upper), (activation, cotangent),
                 ssm_low, grad_branch, grad_norm_ffn, after,
             ),
-            [scan, stats_flow],
+            [scan],
         )
         late_flow = Flow(reduce_stages(late, 1, 14))
-        (early,) = bracket(lambda after: pack_out(ssm_low, grad_branch, after + late_flow.values()), [scan, stats_flow])
+        (early,) = bracket(lambda after: pack_out(ssm_low, grad_branch, after + late_flow.values()), [scan])
         scan.go()
         late_flow.go()
         grad_state_out = scan.result
-        around = lambda call: bracket(call, [late_flow, stats_flow])
+        around = lambda call: bracket(call, [late_flow])
     else:
         grad_state_out = scan_states(carry_all, grad_state_local, span, fast, True)
         around = lambda call: call(())
@@ -1685,14 +1684,14 @@
     }
     parts = []
     if fast:
-        (early,) = bracket(lambda after: pack_ssm(
+        early = pack_ssm(
             early,
             [
                 (attended, grad_branch), (hidden, grad_gate_ssm),
                 (hidden, grad_xbc[:, :ssm_inner]), (hidden, grad_xbc[:, ssm_inner:]),
             ],
-            small, ssm_low, grad_branch, (*after, *late_flow.values()),
-        ), [stats_flow])
+            small, ssm_low, grad_branch, late_flow.values(),
+        )
         early_flow = Flow(reduce_stages(early, 0, 8))
         (grad_attended,) = fence([grad_attended], early_flow.values() + late_flow.values())
         around = lambda call: bracket(call, [early_flow])
@@ -1720,8 +1719,12 @@
         late_flow.go([parts[-1][1]])
         scatter = Flow(scatter_stages(grad_kv))
         (grad_q_turned,) = fence([grad_q_turned], scatter.values() + early_flow.values() + late_flow.values())
-    grad_q_rot = grad_q_turned.reshape(HEADS_Q * HEAD_DIM, rows_dev).T * score_scale
-    grad_query_low = rotate(grad_q_rot, cosine, -sine, HEADS_Q).astype(jnp.bfloat16)
+    halves = grad_q_turned.reshape(HEADS_Q, 2, HEAD_DIM // 2, rows_dev) * score_scale
+    cos_t, sin_t = cosine.T[None], sine.T[None]
+    turned_back = jnp.stack(
+        [halves[:, 0] * cos_t + halves[:, 1] * sin_t, halves[:, 1] * cos_t - halves[:, 0] * sin_t], axis=1
+    ).astype(jnp.bfloat16)
+    grad_query_low = turned_back.reshape(HEADS_Q * HEAD_DIM, rows_dev).T
     if fast:
         scatter.go()
         early_flow.go()
@@ -1751,13 +1754,16 @@
             attended, grad_branch, grad_norm_attn, early_flow.values(),
         )
         corner_flow = Flow(corner_stages(corner))
+        (squares,) = fence([squares], corner_flow.values())
+        stats_flow = Flow(sum_stages(squares))
         for _ in range(3):
             corner_flow.go()
+            stats_flow.go()
         early_flow.go()
         ((pieces, _, _), *_) = corner_flow.sends
         (pieces,) = fence([pieces], early_flow.values())
         corner_flow.sends = [(pieces, axis, pairs) for _, axis, pairs in corner_flow.sends]
-        for flow in (early_flow, late_flow, corner_flow):
+        for flow in (stats_flow, early_flow, late_flow, corner_flow):
             while flow.sends:
                 flow.go()
         stats = jnp.sqrt(stats_flow.result / (all_rows * D))

time: 921 us -> 965 us (1.048)
  waiting for transfers between devices: 169 us -> 217 us
    ppermute x59 -> x58, waiting for transfers between devices: 119 us -> 164 us  [go(): lax.ppermute(value, axis, pairs)]
    unnamed x432 -> x429, local copies, waits for them, and re-layouts: 44.7 us -> 51.9 us
    ppermute x59 -> x58, starting transfers between devices: 155 us -> 149 us  [go(): lax.ppermute(value, axis, pairs)]
  transfers between devices with their start and end apart: 88 -> 87, of which waited for: 27 -> 33; matrix products, arithmetic and copies ran while one was open for 24% -> 20% of each run, Pallas kernels for 18% -> 16%
where the time goes in v8:
time: 965 us; the launch traced here: 956 us
  waiting for transfers between devices  217 us (22%)
  Pallas kernels  211 us (22%)
  starting transfers between devices  191 us (20%)
  other arithmetic  145 us (15%)
  local copies, waits for them, and re-layouts  110 us (11%)
  matrix products  77.8 us (8%)
    ppermute x58, waiting for transfers between devices, go(): lax.ppermute(value, axis, pairs)  164 us
    ppermute x58, starting transfers between devices, go(): lax.ppermute(value, axis, pairs)  149 us
    unnamed x429, local copies, waits for them, and re-layouts  51.9 us
    dot_general x12, matrix products, matmul_right_t(): lax.dot_general(left, right, (((1,), (1,)), ((), ())), preferred_element_...  46.4 us
    pallas_call x4, Pallas kernels, pack_lines(): pl.pallas_call(pinned(kernel, inputs, after), grid=(total,), in_specs=[le...  42.8 us
    pallas_call x2, Pallas kernels, unpack_lines(): pl.pallas_call(pinned(kernel, 2 + count_buffers, after), grid_spec=pltpu....  41.1 us
    pallas_call x1, Pallas kernels, ssm_backward(): pl.pallas_call(pinned(kernel, 11, after), grid_spec=pltpu.PrefetchScalarG...  40.8 us
    convert_element_type x14, other arithmetic, added(): return total.astype(jnp.bfloat16)  32 us
  transfers between devices with their start and end apart: 87, of which 33 were waited for; matrix products, arithmetic and copies ran while one was open for 20% of the time, Pallas kernels for 16%

profile of v8, /device:TPU:0, one launch (start us, length us, event | category | flops | bytes accessed | tf_op | source)
XLA Modules:
  0.0 956.0 jit_solution(2443807898591623637)
XLA Ops:
  15.7 4.9 collective-permute-done.12
  23.7 5.4 collective-permute-done.1
  44.2 9.0 collective-permute-start.8
  53.2 14.9 %collective-permute-done.28 = bf16[2,3088,128]{2,1,0:T(8,128)(2,1)} collective-permute-done((bf16[2,3088,128]{2,1,0:T(8,128)(2,1)}, bf16[2,3088,128]{2,1,0:T(8,128)(2,1)}, u32[]{:S(2)}, u32[]{:S(2)}) %collective-permute-start.28) | collective-permute-done | bytes 1581088 | tf_op jit(solution)/shard_map/ppermute | solution.py:304
  88.6 13.8 %collective-permute-done.6 = bf16[3088,128]{1,0:T(8,128)(2,1)S(1)} collective-permute-done((bf16[3088,128]{1,0:T(8,128)(2,1)S(1)}, bf16[3088,128]{1,0:T(8,128)(2,1)S(1)}, u32[]{:S(2)}, u32[]{:S(2)}) %collective-permute-start.6) | collective-permute-done | bytes 790560 | tf_op jit(solution)/shard_map/ppermute | solution.py:295
  105.0 7.2 collective-permute-done.7
  120.4 14.4 %unpack.2 = (bf16[1024,512]{1,0:T(8,128)(2,1)}, bf16[1024,128]{1,0:T(8,128)(2,1)S(1)}, bf16[1024,128]{1,0:T(8,128)(2,1)S(1)}, bf16[512,1024]{1,0:T(8,128)(2,1)},...) custom-call(s32[25,5]{1,0:T(8,128)S(1)} %copy-done.64, ...), custom_call_target="tpu_custom_call" | custom-call | bytes 26624000 | tf_op jit(solution)/shard_map/unpack/pallas_call | solution.py:456
  185.3 12.5 %conv.1.refs_1_.refs_2_.refs_0_ = f32[512,1792]{1,0:T(8,128)} custom-call(s32[5]{0:T(128)} %pad_add_fusion.1.refs_0_.meta_ref, f32[512,1792]{1,0:T(8,128)} %pad_maximum_fusion.refs_1_.refs_4_, f32[8,1792]{1,0:T(8,128)} %collective-permute-done.25.refs_2_.refs_5_, f32[4,1792]{1,0:T(4,128)} %reshape.444.refs_3_.refs_6_, f32[1,1792]{1,0:T(1,128)} %bitcast.352, ...), custom_call_target="tpu_custom_call" | custom-call | flops 1000000000 | bytes 7340032 | tf_op jit(solution)/shard_map/conv/pallas_call | solution.py:750
  202.8 5.0 collective-permute-done.33.refs_0_
  212.0 9.2 state.2.refs_1_.refs_0_
  239.3 8.6 collective-permute-done.36
  253.3 14.8 %attend.1 = (f32[8,64,512]{2,1,0:T(8,128)S(1)}, f32[8,8,512]{2,1,0:T(8,128)S(1)}) custom-call(s32[4]{0:T(128)S(1)} %pad_add_fusion.refs_0_, bf16[8,512,128]{2,1,0:T(8,128)(2,1)S(1)} %pad.23.refs_1_, bf16[8,2,512,128]{3,2,1,0:T(8,128)(2,1)} %bitcast.304, s32[8,512]{1,0:T(8,128)S(1)} %broadcast_in_dim.215.refs_3_.row_ref.refs_10_.refs_6_, ...), custom_call_target="tpu_custom_call" | custom-call | flops 20000000000 | bytes 8388608 | tf_op jit(solution)/shard_map/attend/pallas_call | solution.py:1202
  276.6 8.9 ssm.1.refs_26_
  289.9 26.7 %unpack.3 = (bf16[1536,1024]{1,0:T(8,128)(2,1)}, bf16[1024,2048]{1,0:T(8,128)(2,1)}, bf16[1024,2048]{1,0:T(8,128)(2,1)}, bf16[2048,1024]{1,0:T(8,128)(2,1)}, bf16[16,128]{1,0:T(8,128)(2,1)S(1)}) custom-call(s32[31,5]{1,0:T(8,128)S(1)} %copy-done.63, s32[32]{0:T(128)S(1)} %fusion.71.refs_1_, bf16[1,3088,128]{2,1,0:T(8,128)(2,1)S(1)} %bitcast.281, ...), custom_call_target="tpu_custom_call" | custom-call | bytes 33013760 | tf_op jit(solution)/shard_map/unpack/pallas_call | solution.py:456
  332.5 6.7 fusion.2
  339.2 6.9 fusion.99
  360.9 6.5 fusion.23
  367.4 9.3 state.3
  378.0 4.9 collective-permute-start.42
  383.0 6.0 pad_maximum_fusion.2
  389.0 20.6 %pack.4.refs_1_.refs_0_ = bf16[49344,128]{1,0:T(8,128)(2,1)} custom-call(bf16[512,1024]{1,0:T(8,128)(2,1)S(1)} %copy-done.53, bf16[512,2048]{1,0:T(8,128)(2,1)S(1)} %copy-done.69, bf16[512,2048]{1,0:T(8,128)(2,1)} %get-tuple-element.230.refs_2_, bf16[512,2048]{1,0:T(8,128)(2,1)} %get-tuple-element.231.refs_3_, bf16[512,1024]{1,0:T(8,128)(2,1)S(1)} %copy-done.51, ...), custom_call_target="tpu_custom_call" | custom-call | flops 6442450944 | bytes 16777216 | tf_op jit(solution)/shard_map/pack/pallas_call | solution.py:611
  413.2 6.0 constant_dynamic-slice_fusion.2.refs_4_
  419.3 7.9 collective-permute-start.43
  432.5 5.5 collective-permute-done.43.refs_0_
  442.1 5.8 add_convert_fusion.1
  451.2 29.3 %collective-permute-start.46 = (bf16[2,3104,128]{2,1,0:T(8,128)(2,1)}, bf16[2,3104,128]{2,1,0:T(8,128)(2,1)}, u32[]{:S(2)}, u32[]{:S(2)}) collective-permute-start(bf16[2,3104,128]{2,1,0:T(8,128)(2,1)} %pad_maximum_fusion.5.refs_11_), channel_id=1, source_target_pairs={{0,4},{4,0},{1,5},{5,1},{2,6},{6,2},{3,7},{7,3},{8,12},{12,8},{9,1... | collective-permute-start | bytes 4767752 | tf_op jit(solution)/shard_map/ppermute | solution.py:250
  486.7 38.3 %collective-permute-done.44 = bf16[144,1536]{1,0:T(8,128)(2,1)} collective-permute-done((bf16[144,1536]{1,0:T(8,128)(2,1)}, bf16[144,1536]{1,0:T(8,128)(2,1)}, u32[]{:S(2)}, u32[]{:S(2)}) %collective-permute-start.44) | collective-permute-done | bytes 442400 | tf_op jit(solution)/shard_map/ppermute | solution.py:250
  528.5 40.8 %ssm_back.1 = (f32[512,1536]{1,0:T(8,128)S(1)}, f32[512,128]{1,0:T(8,128)S(1)}, f32[512,128]{1,0:T(8,128)S(1)}, f32[12,8,512]{2,1,0:T(8,128)S(1)}) custom-call(s32[5]{0:T(128)S(1)} %copy-done.65, f32[512,1792]{1,0:T(8,128)} %fence.32.refs_0_.refs_1_.x_ref.b_ref.c_ref.refs_3_.refs_4_, f32[512,1536]{1,0:T(8,128)S(1)} %copy-done.8, ...), custom_call_target="tpu_custom_call" | custom-call | flops 3000000000 | bytes 9437184 | tf_op jit(solution)/shard_map/ssm_back/pallas_call | solution.py:1060
  586.3 15.4 %conv_back.1 = (bf16[512,1792]{1,0:T(8,128)(2,1)}, f32[16,1792]{1,0:T(8,128)}, f32[8,1792]{1,0:T(8,128)}, f32[8,1792]{1,0:T(8,128)}) custom-call(s32[5]{0:T(128)} %pad_add_fusion.1.refs_0_.meta_ref, f32[512,1536]{1,0:T(8,128)} %get-tuple-element.96.refs_1_, f32[512,128]{1,0:T(8,128)} %get-tuple-element.97.refs_2_, f32[512,128]{1,0:T(8,128)} %get-tuple-element.98.refs_3_, ...), custom_call_target="tpu_custom_call" | custom-call | flops 2000000000 | bytes 9175040 | tf_op jit(solution)/shard_map/conv_back/pallas_call | solution.py:801
  615.4 12.1 %pack.6 = bf16[49440,128]{1,0:T(8,128)(2,1)} custom-call(bf16[512,512]{1,0:T(8,128)(2,1)S(1)} %bitcast.294, bf16[512,1024]{1,0:T(8,128)(2,1)S(1)} %copy-done.2, bf16[512,1024]{1,0:T(8,128)(2,1)S(1)} %copy-done.7, bf16[512,1536]{1,0:T(8,128)(2,1)S(1)} %copy-done.18, bf16[512,1536]{1,0:T(8,128)(2,1)S(1)} %slice.366.refs_4_, ...), custom_call_target="tpu_custom_call", output_to_operand_aliasing={{}: (7, {})} | custom-call | flops 4026531840 | bytes 11010048 | tf_op jit(solution)/shard_map/pack/pallas_call | solution.py:611
  627.5 5.9 constant_dynamic-slice_fusion.1.refs_1_
  638.3 5.1 fusion.100
  645.3 26.7 %collective-permute-start.57 = (bf16[2,3104,128]{2,1,0:T(8,128)(2,1)}, bf16[2,3104,128]{2,1,0:T(8,128)(2,1)}, u32[]{:S(2)}, u32[]{:S(2)}) collective-permute-start(bf16[2,3104,128]{2,1,0:T(8,128)(2,1)} %pad_maximum_fusion.7.refs_4_.refs_5_.refs_6_.refs_8_.refs_9_.refs_10_.refs_2_.refs_3_.refs_11_), channel_id=1, source_target_pairs={{0,16},{9,25},{2,18},{11,27},{4,20},{13,29},{6,22},{15,31}} | collective-permute-start | bytes 4767752 | tf_op jit(solution)/shard_map/ppermute | solution.py:250
  685.3 5.8 add_convert_fusion
  699.6 7.8 attend_back.2
  709.2 22.7 %collective-permute-done.52.refs_0_ = bf16[2,3104,128]{2,1,0:T(8,128)(2,1)} collective-permute-done((bf16[2,3104,128]{2,1,0:T(8,128)(2,1)}, bf16[2,3104,128]{2,1,0:T(8,128)(2,1)}, u32[]{:S(2)}, u32[]{:S(2)}) %collective-permute-start.52) | collective-permute-done | bytes 1589280 | tf_op jit(solution)/shard_map/ppermute | solution.py:250
  746.4 8.0 attend_back.3
  785.2 9.5 collective-permute-start.63
  794.8 8.2 collective-permute-done.61
  808.4 6.8 collective-permute-start.64
  815.2 5.6 add_add_fusion.4.refs_0_
  827.2 4.8 fusion.12
  832.0 5.4 pack.7
  852.5 15.3 %collective-permute-done.72 = bf16[3104,128]{1,0:T(8,128)(2,1)S(1)} collective-permute-done((bf16[3104,128]{1,0:T(8,128)(2,1)S(1)}, bf16[3104,128]{1,0:T(8,128)(2,1)S(1)}, u32[]{:S(2)}, u32[]{:S(2)}) %collective-permute-start.72) | collective-permute-done | bytes 794656 | tf_op jit(solution)/shard_map/ppermute | solution.py:250
  867.8 16.6 %collective-permute-done.71 = bf16[3104,128]{1,0:T(8,128)(2,1)S(1)} collective-permute-done((bf16[3104,128]{1,0:T(8,128)(2,1)S(1)}, bf16[3104,128]{1,0:T(8,128)(2,1)S(1)}, u32[]{:S(2)}, u32[]{:S(2)}) %collective-permute-start.71) | collective-permute-done | bytes 794656 | tf_op jit(solution)/shard_map/ppermute | solution.py:250
  888.3 7.3 collective-permute-start.68
  908.9 5.9 collective-permute-done.75
  920.5 4.8 fusion.14
  (857 shorter events, 401.1 us)
Async XLA Ops:
  13.9 20.5 %collective-permute-start.26 = (bf16[2,3088,128]{2,1,0:T(8,128)(2,1)}, bf16[2,3088,128]{2,1,0:T(8,128)(2,1)}, u32[]{:S(2)}, u32[]{:S(2)}) collective-permute-start(bf16[2,3088,128]{2,1,0:T(8,128)(2,1)} %maximum_select_fusion), channel_id=1, source_target_pairs={{16,8},{25,17},{18,10},{27,19},{20,12},{29,21},{22,14},{31,23}} | collective-permute-start | bytes 4743176 | tf_op jit(solution)/shard_map/ppermute | solution.py:302
  34.4 33.7 %collective-permute-start.28 = (bf16[2,3088,128]{2,1,0:T(8,128)(2,1)}, bf16[2,3088,128]{2,1,0:T(8,128)(2,1)}, u32[]{:S(2)}, u32[]{:S(2)}) collective-permute-start(bf16[2,3088,128]{2,1,0:T(8,128)(2,1)} %collective-permute-done.26), channel_id=1, source_target_pairs={{8,0},{17,9},{10,2},{19,11},{12,4},{21,13},{14,6},{23,15}} | collective-permute-start | bytes 4743176 | tf_op jit(solution)/shard_map/ppermute | solution.py:304
  37.9 31.7 %collective-permute-start.19 = (bf16[3088,128]{1,0:T(8,128)(2,1)S(1)}, bf16[3088,128]{1,0:T(8,128)(2,1)S(1)}, u32[]{:S(2)}, u32[]{:S(2)}) collective-permute-start(bf16[3088,128]{1,0:T(8,128)(2,1)S(1)} %add_select_fusion.1), channel_id=1, source_target_pairs={{0,1},{1,0},{2,3},{3,2},{4,5},{5,4},{6,7},{7,6},{8,9},{9,8},{10,11... | collective-permute-start | bytes 2371592 | tf_op jit(solution)/shard_map/ppermute | solution.py:299
  39.7 43.5 %collective-permute-start.17 = (bf16[3088,128]{1,0:T(8,128)(2,1)S(1)}, bf16[3088,128]{1,0:T(8,128)(2,1)}, u32[]{:S(2)}, u32[]{:S(2)}) collective-permute-start(bf16[3088,128]{1,0:T(8,128)(2,1)S(1)} %add_select_fusion.1), channel_id=1, source_target_pairs={{0,4},{4,0},{1,5},{5,1},{2,6},{6,2},{3,7},{7,3},{8,12},{12,8},{9,1... | collective-permute-start | bytes 2371592 | tf_op jit(solution)/shard_map/ppermute | solution.py:295
  41.2 43.6 %collective-permute-start.16 = (bf16[3088,128]{1,0:T(8,128)(2,1)S(1)}, bf16[3088,128]{1,0:T(8,128)(2,1)}, u32[]{:S(2)}, u32[]{:S(2)}) collective-permute-start(bf16[3088,128]{1,0:T(8,128)(2,1)S(1)} %add_select_fusion.1), channel_id=1, source_target_pairs={{0,2},{2,0},{1,3},{3,1},{4,6},{6,4},{5,7},{7,5},{8,10},{10,8},{9,1... | collective-permute-start | bytes 2371592 | tf_op jit(solution)/shard_map/ppermute | solution.py:294
  44.2 40.6 %collective-permute-start.8 = (bf16[3088,128]{1,0:T(8,128)(2,1)S(1)}, bf16[3088,128]{1,0:T(8,128)(2,1)S(1)}, u32[]{:S(2)}, u32[]{:S(2)}) collective-permute-start(bf16[3088,128]{1,0:T(8,128)(2,1)S(1)} %add_select_fusion.2), channel_id=1, source_target_pairs={{0,1},{1,0},{2,3},{3,2},{4,5},{5,4},{6,7},{7,6},{8,9},{9,8},{10,11... | collective-permute-start | bytes 2371592 | tf_op jit(solution)/shard_map/ppermute | solution.py:299
  70.5 41.7 %collective-permute-start.29 = (bf16[2,3088,128]{2,1,0:T(8,128)(2,1)}, bf16[2,3088,128]{2,1,0:T(8,128)(2,1)}, u32[]{:S(2)}, u32[]{:S(2)}) collective-permute-start(bf16[2,3088,128]{2,1,0:T(8,128)(2,1)} %collective-permute-done.28), channel_id=1, source_target_pairs={{9,1},{11,3},{13,5},{15,7}} | collective-permute-start | bytes 4743176 | tf_op jit(solution)/shard_map/ppermute | solution.py:305
  83.2 19.3 %collective-permute-start.6 = (bf16[3088,128]{1,0:T(8,128)(2,1)S(1)}, bf16[3088,128]{1,0:T(8,128)(2,1)S(1)}, u32[]{:S(2)}, u32[]{:S(2)}) collective-permute-start(bf16[3088,128]{1,0:T(8,128)(2,1)S(1)} %add_select_fusion.2), channel_id=1, source_target_pairs={{0,4},{4,0},{1,5},{5,1},{2,6},{6,2},{3,7},{7,3},{8,12},{12,8},{9,1... | collective-permute-start | bytes 2371592 | tf_op jit(solution)/shard_map/ppermute | solution.py:295
  84.8 20.3 %collective-permute-start.18 = (bf16[3088,128]{1,0:T(8,128)(2,1)}, bf16[3088,128]{1,0:T(8,128)(2,1)S(1)}, u32[]{:S(2)}, u32[]{:S(2)}) collective-permute-start(bf16[3088,128]{1,0:T(8,128)(2,1)} %collective-permute-done.17), channel_id=1, source_target_pairs={{0,2},{2,0},{1,3},{3,1},{4,6},{6,4},{5,7},{7,5},{8,10},{10,8},{9,1... | collective-permute-start | bytes 2371592 | tf_op jit(solution)/shard_map/ppermute | solution.py:296
  85.4 26.8 %collective-permute-start.7 = (bf16[3088,128]{1,0:T(8,128)(2,1)S(1)}, bf16[3088,128]{1,0:T(8,128)(2,1)S(1)}, u32[]{:S(2)}, u32[]{:S(2)}) collective-permute-start(bf16[3088,128]{1,0:T(8,128)(2,1)S(1)} %collective-permute-done.5), channel_id=1, source_target_pairs={{0,4},{4,0},{1,5},{5,1},{2,6},{6,2},{3,7},{7,3},{8,12},{12,8},{9,1... | collective-permute-start | bytes 2371592 | tf_op jit(solution)/shard_map/ppermute | solution.py:296
  117.0 170.3 %collective-permute-start.38 = (bf16[2,3088,128]{2,1,0:T(8,128)(2,1)}, bf16[2,3088,128]{2,1,0:T(8,128)(2,1)}, u32[]{:S(2)}, u32[]{:S(2)}) collective-permute-start(bf16[2,3088,128]{2,1,0:T(8,128)(2,1)} %add_select_fusion.refs_2_.refs_4_.refs_6_.refs_18_), channel_id=1, source_target_pairs={{0,1},{1,0},{2,3},{3,2},{4,5},{5,4},{6,7},{7,6},{8,9},{9,8},{10,11... | collective-permute-start | bytes 4743176 | tf_op jit(solution)/shard_map/ppermute | solution.py:250
  117.1 59.6 %collective-permute-start.31 = (bf16[2,3088,128]{2,1,0:T(8,128)(2,1)}, bf16[2,3088,128]{2,1,0:T(8,128)(2,1)}, u32[]{:S(2)}, u32[]{:S(2)}) collective-permute-start(bf16[2,3088,128]{2,1,0:T(8,128)(2,1)} %add_select_fusion.refs_2_.refs_4_.refs_6_.refs_18_), channel_id=1, source_target_pairs={{0,4},{4,0},{1,5},{5,1},{2,6},{6,2},{3,7},{7,3},{8,12},{12,8},{9,1... | collective-permute-start | bytes 4743176 | tf_op jit(solution)/shard_map/ppermute | solution.py:250
  118.7 60.7 %collective-permute-start.30 = (bf16[2,3088,128]{2,1,0:T(8,128)(2,1)}, bf16[2,3088,128]{2,1,0:T(8,128)(2,1)}, u32[]{:S(2)}, u32[]{:S(2)}) collective-permute-start(bf16[2,3088,128]{2,1,0:T(8,128)(2,1)} %add_select_fusion.refs_2_.refs_4_.refs_6_.refs_18_), channel_id=1, source_target_pairs={{0,2},{2,0},{1,3},{3,1},{4,6},{6,4},{5,7},{7,5},{8,10},{10,8},{9,1... | collective-permute-start | bytes 4743176 | tf_op jit(solution)/shard_map/ppermute | solution.py:250
  155.4 18.8 %collective-permute-start.23 = (bf16[2,512,128]{2,1,0:T(8,128)(2,1)}, bf16[2,512,128]{2,1,0:T(8,128)(2,1)}, u32[]{:S(2)}, u32[]{:S(2)}) collective-permute-start(bf16[2,512,128]{2,1,0:T(8,128)(2,1)} %maximum_bitcast_fusion), channel_id=1, source_target_pairs={{0,2},{2,0},{1,3},{3,1},{4,6},{6,4},{5,7},{7,5},{8,10},{10,8},{9,1... | collective-permute-start | bytes 786440 | tf_op jit(solution)/shard_map/ppermute | solution.py:250
  176.4 21.4 %collective-permute-start.24 = (bf16[2,2,512,128]{3,2,1,0:T(8,128)(2,1)}, bf16[2,2,512,128]{3,2,1,0:T(8,128)(2,1)}, u32[]{:S(2)}, u32[]{:S(2)}) collective-permute-start(bf16[2,2,512,128]{3,2,1,0:T(8,128)(2,1)} %pad_maximum_fusion.17.refs_6_), channel_id=1, source_target_pairs={{0,4},{4,0},{1,5},{5,1},{2,6},{6,2},{3,7},{7,3},{8,12},{12,8},{9,1... | collective-permute-start | bytes 1572872 | tf_op jit(solution)/shard_map/ppermute | solution.py:250
  178.9 23.9 %collective-permute-start.34 = (bf16[1,3088,128]{2,1,0:T(8,128)(2,1)}, bf16[1,3088,128]{2,1,0:T(8,128)(2,1)}, u32[]{:S(2)}, u32[]{:S(2)}) collective-permute-start(bf16[1,3088,128]{2,1,0:T(8,128)(2,1)} %slice.338.refs_8_), channel_id=1, source_target_pairs={{0,2},{2,0},{1,3},{3,1},{4,6},{6,4},{5,7},{7,5},{8,10},{10,8},{9,1... | collective-permute-start | bytes 2371592 | tf_op jit(solution)/shard_map/ppermute | solution.py:250
  181.5 26.3 %collective-permute-start.33 = (bf16[1,3088,128]{2,1,0:T(8,128)(2,1)}, bf16[1,3088,128]{2,1,0:T(8,128)(2,1)}, u32[]{:S(2)}, u32[]{:S(2)}) collective-permute-start(bf16[1,3088,128]{2,1,0:T(8,128)(2,1)} %slice.337.refs_7_), channel_id=1, source_target_pairs={{0,4},{4,0},{1,5},{5,1},{2,6},{6,2},{3,7},{7,3},{8,12},{12,8},{9,1... | collective-permute-start | bytes 2371592 | tf_op jit(solution)/shard_map/ppermute | solution.py:250
  200.9 20.3 %collective-permute-start.32 = (bf16[2,2,2,512,128]{4,3,2,1,0:T(8,128)(2,1)}, bf16[2,2,2,512,128]{4,3,2,1,0:T(8,128)(2,1)}, u32[]{:S(2)}, u32[]{:S(2)}) collective-permute-start(bf16[2,2,2,512,128]{4,3,2,1,0:T(8,128)(2,1)} %pad_maximum_fusion.10.refs_1_.refs_3_), channel_id=1, source_target_pairs={{0,1},{1,0},{2,3},{3,2},{4,5},{5,4},{6,7},{7,6},{8,9},{9,8},{10,11... | collective-permute-start | bytes 3145736 | tf_op jit(solution)/shard_map/ppermute | solution.py:250
  231.1 56.2 %collective-permute-start.40 = (bf16[2,3088,128]{2,1,0:T(8,128)(2,1)}, bf16[2,3088,128]{2,1,0:T(8,128)(2,1)}, u32[]{:S(2)}, u32[]{:S(2)}) collective-permute-start(bf16[2,3088,128]{2,1,0:T(8,128)(2,1)} %collective-permute-done.31.refs_4_.refs_6_.refs_8_.refs_20_), channel_id=1, source_target_pairs={{0,1},{1,0},{2,3},{3,2},{4,5},{5,4},{6,7},{7,6},{8,9},{9,8},{10,11... | collective-permute-start | bytes 4743176 | tf_op jit(solution)/shard_map/ppermute | solution.py:250
  231.6 55.7 %collective-permute-start.39 = (bf16[2,3088,128]{2,1,0:T(8,128)(2,1)}, bf16[2,3088,128]{2,1,0:T(8,128)(2,1)}, u32[]{:S(2)}, u32[]{:S(2)}) collective-permute-start(bf16[2,3088,128]{2,1,0:T(8,128)(2,1)} %collective-permute-done.30.refs_3_.refs_5_.refs_7_.refs_19_), channel_id=1, source_target_pairs={{0,1},{1,0},{2,3},{3,2},{4,5},{5,4},{6,7},{7,6},{8,9},{9,8},{10,11... | collective-permute-start | bytes 4743176 | tf_op jit(solution)/shard_map/ppermute | solution.py:250
  231.6 55.7 %collective-permute-start.41 = (bf16[2,3088,128]{2,1,0:T(8,128)(2,1)}, bf16[2,3088,128]{2,1,0:T(8,128)(2,1)}, u32[]{:S(2)}, u32[]{:S(2)}) collective-permute-start(bf16[2,3088,128]{2,1,0:T(8,128)(2,1)} %constant_dynamic-update-slice_fusion.refs_5_.refs_7_.refs_9_.refs_21_), channel_id=1, source_target_pairs={{0,1},{1,0},{2,3},{3,2},{4,5},{5,4},{6,7},{7,6},{8,9},{9,8},{10,11... | collective-permute-start | bytes 4743176 | tf_op jit(solution)/shard_map/ppermute | solution.py:250
  378.0 31.6 %collective-permute-start.42 = (bf16[144,1536]{1,0:T(8,128)(2,1)S(1)}, bf16[144,1536]{1,0:T(8,128)(2,1)S(1)}, u32[]{:S(2)}, u32[]{:S(2)}) collective-permute-start(bf16[144,1536]{1,0:T(8,128)(2,1)S(1)} %pad_maximum_fusion.15.refs_7_), channel_id=1, source_target_pairs={{0,1},{1,0},{2,3},{3,2},{4,5},{5,4},{6,7},{7,6},{8,9},{9,8},{10,11... | collective-permute-start | bytes 1327112 | tf_op jit(solution)/shard_map/ppermute | solution.py:250
  419.2 22.9 %collective-permute-start.45 = (bf16[24688,128]{1,0:T(8,128)(2,1)}, bf16[24688,128]{1,0:T(8,128)(2,1)}, u32[]{:S(2)}, u32[]{:S(2)}) collective-permute-start(bf16[24688,128]{1,0:T(8,128)(2,1)} %constant_dynamic-slice_fusion.2.refs_4_), channel_id=1, source_target_pairs={{0,1},{1,0},{2,3},{3,2},{4,5},{5,4},{6,7},{7,6},{8,9},{9,8},{10,11... | collective-permute-start | bytes 18960392 | tf_op jit(solution)/shard_map/ppermute | solution.py:250
  419.3 18.7 %collective-permute-start.43 = (bf16[144,1536]{1,0:T(8,128)(2,1)S(1)}, bf16[144,1536]{1,0:T(8,128)(2,1)}, u32[]{:S(2)}, u32[]{:S(2)}) collective-permute-start(bf16[144,1536]{1,0:T(8,128)(2,1)S(1)} %copy-done.32), channel_id=1, source_target_pairs={{0,2},{2,0},{1,3},{3,1},{4,6},{6,4},{5,7},{7,5},{8,10},{10,8},{9,1... | collective-permute-start | bytes 1327112 | tf_op jit(solution)/shard_map/ppermute | solution.py:250
  451.2 121.8 %collective-permute-start.46 = (bf16[2,3104,128]{2,1,0:T(8,128)(2,1)}, bf16[2,3104,128]{2,1,0:T(8,128)(2,1)}, u32[]{:S(2)}, u32[]{:S(2)}) collective-permute-start(bf16[2,3104,128]{2,1,0:T(8,128)(2,1)} %pad_maximum_fusion.5.refs_11_), channel_id=1, source_target_pairs={{0,4},{4,0},{1,5},{5,1},{2,6},{6,2},{3,7},{7,3},{8,12},{12,8},{9,1... | collective-permute-start | bytes 4767752 | tf_op jit(solution)/shard_map/ppermute | solution.py:250
  481.8 91.2 %collective-permute-start.47 = (bf16[2,3104,128]{2,1,0:T(8,128)(2,1)}, bf16[2,3104,128]{2,1,0:T(8,128)(2,1)}, u32[]{:S(2)}, u32[]{:S(2)}) collective-permute-start(bf16[2,3104,128]{2,1,0:T(8,128)(2,1)} %pad_maximum_fusion.6.refs_12_), channel_id=1, source_target_pairs={{0,2},{2,0},{1,3},{3,1},{4,6},{6,4},{5,7},{7,5},{8,10},{10,8},{9,1... | collective-permute-start | bytes 4767752 | tf_op jit(solution)/shard_map/ppermute | solution.py:250
  485.1 40.0 %collective-permute-start.44 = (bf16[144,1536]{1,0:T(8,128)(2,1)}, bf16[144,1536]{1,0:T(8,128)(2,1)}, u32[]{:S(2)}, u32[]{:S(2)}) collective-permute-start(bf16[144,1536]{1,0:T(8,128)(2,1)} %pad_maximum_fusion.22.refs_1_), channel_id=1, source_target_pairs={{0,4},{4,0},{1,5},{5,1},{2,6},{6,2},{3,7},{7,3},{8,12},{12,8},{9,1... | collective-permute-start | bytes 1327112 | tf_op jit(solution)/shard_map/ppermute | solution.py:250
  581.8 20.6 %collective-permute-start.48 = (bf16[3104,128]{1,0:T(8,128)(2,1)}, bf16[3104,128]{1,0:T(8,128)(2,1)}, u32[]{:S(2)}, u32[]{:S(2)}) collective-permute-start(bf16[3104,128]{1,0:T(8,128)(2,1)} %dynamic-slice_bitcast_fusion.14.refs_4_.refs_9_), channel_id=1, source_target_pairs={{0,2},{2,0},{1,3},{3,1},{4,6},{6,4},{5,7},{7,5},{8,10},{10,8},{9,1... | collective-permute-start | bytes 2383880 | tf_op jit(solution)/shard_map/ppermute | solution.py:250
  583.3 19.1 %collective-permute-start.49 = (bf16[3104,128]{1,0:T(8,128)(2,1)}, bf16[3104,128]{1,0:T(8,128)(2,1)}, u32[]{:S(2)}, u32[]{:S(2)}) collective-permute-start(bf16[3104,128]{1,0:T(8,128)(2,1)} %dynamic-slice_bitcast_fusion.11.refs_5_.refs_10_), channel_id=1, source_target_pairs={{0,4},{4,0},{1,5},{5,1},{2,6},{6,2},{3,7},{7,3},{8,12},{12,8},{9,1... | collective-permute-start | bytes 2383880 | tf_op jit(solution)/shard_map/ppermute | solution.py:250
  633.4 51.8 %collective-permute-start.51 = (bf16[24688,128]{1,0:T(8,128)(2,1)}, bf16[24688,128]{1,0:T(8,128)(2,1)}, u32[]{:S(2)}, u32[]{:S(2)}) collective-permute-start(bf16[24688,128]{1,0:T(8,128)(2,1)} %constant_dynamic-slice_fusion.1.refs_1_), channel_id=1, source_target_pairs={{0,1},{1,0},{2,3},{3,2},{4,5},{5,4},{6,7},{7,6},{8,9},{9,8},{10,11... | collective-permute-start | bytes 18960392 | tf_op jit(solution)/shard_map/ppermute | solution.py:250
  645.3 119.5 %collective-permute-start.57 = (bf16[2,3104,128]{2,1,0:T(8,128)(2,1)}, bf16[2,3104,128]{2,1,0:T(8,128)(2,1)}, u32[]{:S(2)}, u32[]{:S(2)}) collective-permute-start(bf16[2,3104,128]{2,1,0:T(8,128)(2,1)} %pad_maximum_fusion.7.refs_4_.refs_5_.refs_6_.refs_8_.refs_9_.refs_10_.refs_2_.refs_3_.refs_11_), channel_id=1, source_target_pairs={{0,16},{9,25},{2,18},{11,27},{4,20},{13,29},{6,22},{15,31}} | collective-permute-start | bytes 4767752 | tf_op jit(solution)/shard_map/ppermute | solution.py:250
  672.0 94.2 %collective-permute-start.56 = (bf16[2,3104,128]{2,1,0:T(8,128)(2,1)}, bf16[2,3104,128]{2,1,0:T(8,128)(2,1)}, u32[]{:S(2)}, u32[]{:S(2)}) collective-permute-start(bf16[2,3104,128]{2,1,0:T(8,128)(2,1)} %pad_maximum_fusion.7.refs_4_.refs_5_.refs_6_.refs_8_.refs_9_.refs_10_.refs_2_.refs_3_.refs_11_), channel_id=1, source_target_pairs={{8,16},{17,25},{10,18},{19,27},{12,20},{21,29},{14,22},{23,31}} | collective-permute-start | bytes 4767752 | tf_op jit(solution)/shard_map/ppermute | solution.py:250
  673.8 92.5 %collective-permute-start.58 = (bf16[2,3104,128]{2,1,0:T(8,128)(2,1)}, bf16[2,3104,128]{2,1,0:T(8,128)(2,1)}, u32[]{:S(2)}, u32[]{:S(2)}) collective-permute-start(bf16[2,3104,128]{2,1,0:T(8,128)(2,1)} %pad_maximum_fusion.7.refs_4_.refs_5_.refs_6_.refs_8_.refs_9_.refs_10_.refs_2_.refs_3_.refs_11_), channel_id=1, source_target_pairs={{24,16},{1,25},{26,18},{3,27},{28,20},{5,29},{30,22},{7,31}} | collective-permute-start | bytes 4767752 | tf_op jit(solution)/shard_map/ppermute | solution.py:250
  694.3 37.6 %collective-permute-start.52 = (bf16[2,3104,128]{2,1,0:T(8,128)(2,1)}, bf16[2,3104,128]{2,1,0:T(8,128)(2,1)}, u32[]{:S(2)}, u32[]{:S(2)}) collective-permute-start(bf16[2,3104,128]{2,1,0:T(8,128)(2,1)} %pad_maximum_fusion.8.refs_1_.refs_7_), channel_id=1, source_target_pairs={{0,4},{4,0},{1,5},{5,1},{2,6},{6,2},{3,7},{7,3},{8,12},{12,8},{9,1... | collective-permute-start | bytes 4767752 | tf_op jit(solution)/shard_map/ppermute | solution.py:250
  696.8 37.4 %collective-permute-start.53 = (bf16[2,3104,128]{2,1,0:T(8,128)(2,1)}, bf16[2,3104,128]{2,1,0:T(8,128)(2,1)}, u32[]{:S(2)}, u32[]{:S(2)}) collective-permute-start(bf16[2,3104,128]{2,1,0:T(8,128)(2,1)} %pad_maximum_fusion.9.refs_2_.refs_8_), channel_id=1, source_target_pairs={{0,2},{2,0},{1,3},{3,1},{4,6},{6,4},{5,7},{7,5},{8,10},{10,8},{9,1... | collective-permute-start | bytes 4767752 | tf_op jit(solution)/shard_map/ppermute | solution.py:250
  740.3 19.5 %collective-permute-start.54 = (bf16[3104,128]{1,0:T(8,128)(2,1)}, bf16[3104,128]{1,0:T(8,128)(2,1)}, u32[]{:S(2)}, u32[]{:S(2)}) collective-permute-start(bf16[3104,128]{1,0:T(8,128)(2,1)} %dynamic-slice_bitcast_fusion.4.refs_2_.refs_7_), channel_id=1, source_target_pairs={{0,2},{2,0},{1,3},{3,1},{4,6},{6,4},{5,7},{7,5},{8,10},{10,8},{9,1... | collective-permute-start | bytes 2383880 | tf_op jit(solution)/shard_map/ppermute | solution.py:250
  741.3 19.2 %collective-permute-start.55 = (bf16[3104,128]{1,0:T(8,128)(2,1)S(1)}, bf16[3104,128]{1,0:T(8,128)(2,1)}, u32[]{:S(2)}, u32[]{:S(2)}) collective-permute-start(bf16[3104,128]{1,0:T(8,128)(2,1)S(1)} %dynamic-slice_bitcast_fusion.1.refs_3_.refs_8_), channel_id=1, source_target_pairs={{0,4},{4,0},{1,5},{5,1},{2,6},{6,2},{3,7},{7,3},{8,12},{12,8},{9,1... | collective-permute-start | bytes 2383880 | tf_op jit(solution)/shard_map/ppermute | solution.py:250
  762.1 32.7 %collective-permute-start.62 = (bf16[3104,128]{1,0:T(8,128)(2,1)S(1)}, bf16[3104,128]{1,0:T(8,128)(2,1)}, u32[]{:S(2)}, u32[]{:S(2)}) collective-permute-start(bf16[3104,128]{1,0:T(8,128)(2,1)S(1)} %fusion.20.refs_2_.refs_3_.refs_4_), channel_id=1, source_target_pairs={{24,0},{1,9},{26,2},{3,11},{28,4},{5,13},{30,6},{7,15}} | collective-permute-start | bytes 2383880 | tf_op jit(solution)/shard_map/ppermute | solution.py:250
  763.4 39.6 %collective-permute-start.61 = (bf16[3104,128]{1,0:T(8,128)(2,1)S(1)}, bf16[3104,128]{1,0:T(8,128)(2,1)}, u32[]{:S(2)}, u32[]{:S(2)}) collective-permute-start(bf16[3104,128]{1,0:T(8,128)(2,1)S(1)} %fusion.20.refs_2_.refs_3_.refs_4_), channel_id=1, source_target_pairs={{16,0},{25,9},{18,2},{27,11},{20,4},{29,13},{22,6},{31,15}} | collective-permute-start | bytes 2383880 | tf_op jit(solution)/shard_map/ppermute | solution.py:250
  764.7 38.3 %collective-permute-start.60 = (bf16[3104,128]{1,0:T(8,128)(2,1)}, bf16[3104,128]{1,0:T(8,128)(2,1)}, u32[]{:S(2)}, u32[]{:S(2)}) collective-permute-start(bf16[3104,128]{1,0:T(8,128)(2,1)} %copy-done.70), channel_id=1, source_target_pairs={{8,0},{17,9},{10,2},{19,11},{12,4},{21,13},{14,6},{23,15}} | collective-permute-start | bytes 2383880 | tf_op jit(solution)/shard_map/ppermute | solution.py:250
  785.2 21.9 %collective-permute-start.63 = (bf16[2,2,512,128]{3,2,1,0:T(8,128)(2,1)}, bf16[2,2,512,128]{3,2,1,0:T(8,128)(2,1)}, u32[]{:S(2)}, u32[]{:S(2)}) collective-permute-start(bf16[2,2,512,128]{3,2,1,0:T(8,128)(2,1)} %dynamic-slice_bitcast_fusion.21.refs_1_), channel_id=1, source_target_pairs={{0,4},{4,0},{1,5},{5,1},{2,6},{6,2},{3,7},{7,3},{8,12},{12,8},{9,1... | collective-permute-start | bytes 1572872 | tf_op jit(solution)/shard_map/ppermute | solution.py:250
  842.0 110.0 %collective-permute-start.81 = (bf16[3104,128]{1,0:T(8,128)(2,1)}, bf16[3104,128]{1,0:T(8,128)(2,1)}, u32[]{:S(2)}, u32[]{:S(2)}) collective-permute-start(bf16[3104,128]{1,0:T(8,128)(2,1)} %get-tuple-element.186.refs_5_), channel_id=1, source_target_pairs={{0,1},{9,8},{16,17},{25,24},{2,3},{11,10},{18,19},{27,26},{4,5},{1... | collective-permute-start | bytes 2383880 | tf_op jit(solution)/shard_map/ppermute | solution.py:250
  845.3 22.5 %collective-permute-start.72 = (bf16[3104,128]{1,0:T(8,128)(2,1)S(1)}, bf16[3104,128]{1,0:T(8,128)(2,1)S(1)}, u32[]{:S(2)}, u32[]{:S(2)}) collective-permute-start(bf16[3104,128]{1,0:T(8,128)(2,1)S(1)} %copy-done.3), channel_id=1, source_target_pairs={{24,0},{1,9},{26,2},{3,11},{28,4},{5,13},{30,6},{7,15}} | collective-permute-start | bytes 2383880 | tf_op jit(solution)/shard_map/ppermute | solution.py:250
  846.6 37.7 %collective-permute-start.71 = (bf16[3104,128]{1,0:T(8,128)(2,1)S(1)}, bf16[3104,128]{1,0:T(8,128)(2,1)S(1)}, u32[]{:S(2)}, u32[]{:S(2)}) collective-permute-start(bf16[3104,128]{1,0:T(8,128)(2,1)S(1)} %copy-done.3), channel_id=1, source_target_pairs={{16,0},{25,9},{18,2},{27,11},{20,4},{29,13},{22,6},{31,15}} | collective-permute-start | bytes 2383880 | tf_op jit(solution)/shard_map/ppermute | solution.py:250
  847.9 36.5 %collective-permute-start.70 = (bf16[3104,128]{1,0:T(8,128)(2,1)S(1)}, bf16[3104,128]{1,0:T(8,128)(2,1)S(1)}, u32[]{:S(2)}, u32[]{:S(2)}) collective-permute-start(bf16[3104,128]{1,0:T(8,128)(2,1)S(1)} %copy-done.3), channel_id=1, source_target_pairs={{8,0},{17,9},{10,2},{19,11},{12,4},{21,13},{14,6},{23,15}} | collective-permute-start | bytes 2383880 | tf_op jit(solution)/shard_map/ppermute | solution.py:250
  850.7 44.9 %collective-permute-start.66 = (bf16[2,400,128]{2,1,0:T(8,128)(2,1)S(1)}, bf16[2,400,128]{2,1,0:T(8,128)(2,1)S(1)}, u32[]{:S(2)}, u32[]{:S(2)}) collective-permute-start(bf16[2,400,128]{2,1,0:T(8,128)(2,1)S(1)} %dynamic-slice_bitcast_fusion.24), channel_id=1, source_target_pairs={{0,2},{2,0},{1,3},{3,1},{4,6},{6,4},{5,7},{7,5},{8,10},{10,8},{9,1... | collective-permute-start | bytes 614408 | tf_op jit(solution)/shard_map/ppermute | solution.py:250
  886.1 66.0 %collective-permute-start.80 = (bf16[3104,128]{1,0:T(8,128)(2,1)}, bf16[3104,128]{1,0:T(8,128)(2,1)}, u32[]{:S(2)}, u32[]{:S(2)}) collective-permute-start(bf16[3104,128]{1,0:T(8,128)(2,1)} %get-tuple-element.146.refs_1_), channel_id=1, source_target_pairs={{0,1},{9,8},{16,17},{25,24},{2,3},{11,10},{18,19},{27,26},{4,5},{1... | collective-permute-start | bytes 2383880 | tf_op jit(solution)/shard_map/ppermute | solution.py:250
  919.2 18.5 %collective-permute-start.76 = (bf16[400,128]{1,0:T(8,128)(2,1)S(1)}, bf16[400,128]{1,0:T(8,128)(2,1)S(1)}, u32[]{:S(2)}, u32[]{:S(2)}) collective-permute-start(bf16[400,128]{1,0:T(8,128)(2,1)S(1)} %get-tuple-element.209), channel_id=1, source_target_pairs={{4,0},{5,1},{6,2},{7,3},{12,8},{13,9},{14,10},{15,11},{20,16},{21,... | collective-permute-start | bytes 307208 | tf_op jit(solution)/shard_map/ppermute | solution.py:250
  (249 other events, 3098.9 us)

commit v9 on v8

--- a/solution.py
+++ b/solution.py
@@ -188,23 +188,17 @@
     freqs = jnp.exp(
         -jnp.arange(half_dim, dtype=jnp.float32) * (2.0 * math.log(rope_base) / HEAD_DIM)
     )
-    angles = positions.astype(jnp.float32)[:, None] * freqs[None, :]
+    angles = freqs[:, None] * positions.astype(jnp.float32)[None, :]
     return (jnp.cos(angles), jnp.sin(angles))
 
 
 def rotate(values, cosine, sine, heads):
-    row_count = values.shape[0]
-    half_dim = HEAD_DIM // 2
-    split_heads = values.reshape(row_count, heads, HEAD_DIM)
-    first_half = split_heads[..., :half_dim]
-    second_half = split_heads[..., half_dim:]
-    cos_b = cosine[:, None, :]
-    sin_b = sine[:, None, :]
-    turned = jnp.concatenate(
-        [first_half * cos_b - second_half * sin_b, second_half * cos_b + first_half * sin_b],
-        axis=-1,
-    )
-    return turned.reshape(row_count, heads * HEAD_DIM)
+    halves = values.reshape(heads, 2, HEAD_DIM // 2, -1)
+    first_half, second_half = halves[:, 0], halves[:, 1]
+    turned = jnp.stack(
+        [first_half * cosine - second_half * sine, second_half * cosine + first_half * sine], axis=1
+    )
+    return turned.reshape(heads, HEAD_DIM, -1)
 
 
 def add_rows(target, addend, first_row):
@@ -246,6 +240,10 @@
     def values(self):
         return [value for value, _, _ in self.sends] or (list(self.result) if isinstance(self.result, list) else [self.result])
 
+    def hold(self, after):
+        held = fence(self.values(), after)
+        self.sends = [(value, axis, pairs) for value, (_, axis, pairs) in zip(held, self.sends)]
+
     def go(self, after=()):
         arrived = [lax.ppermute(value, axis, pairs) for value, axis, pairs in self.sends]
         if after:
@@ -275,7 +273,7 @@
     out = call([value for flow in flows for value in flow.values()])
     out = list(out) if isinstance(out, (list, tuple)) else [out]
     for flow in flows:
-        flow.go(out[-1:])
+        flow.go()
     return fence(out, [v for flow in flows for v in flow.values()])
 
 
@@ -306,8 +304,8 @@
     column = jnp.where(z == 2 + c, here, one + side + two + three)
     late = []
     for part in range(2):
-        for first in (16, 20):
-            late += [(first + k, part) for k in range(4)]
+        for first in (16, 21):
+            late += [(first, part), (first + 1, part), (first + 2, part), (first + 3 + part, 0)]
     shard = np.arange(32)
     sz, sy, sx, sc = shard // 8, shard // 4 % 2, shard // 2 % 2, shard % 2
     away = jnp.where(sz % 2 == c, 0, 4)
@@ -318,7 +316,7 @@
 def spread_stages(column):
     over_x, over_y = yield [(column, "x", SWAP), (column, "y", SWAP)]
     corners = yield [(over_x[:1], "y", SWAP), (over_y[1:], "x", SWAP)]
-    local = [column, over_x, over_y, jnp.concatenate(corners)]
+    local = [column, over_x, over_y] + list(corners)
     return local + list((yield [(piece, "c", SWAP) for piece in local]))
 
 
@@ -725,25 +723,36 @@
 COLUMNS = CHANNELS // LANES
 
 
-def conv_parts(ext, weight_ref, bias_ref, start_ref, first, rows):
-    place = first + lax.broadcasted_iota(jnp.int32, (rows, 1), 0) - start_ref[...]
+def conv_masks(masks, start_ref, first, rows):
+    place = first + lax.broadcasted_iota(jnp.int32, (rows, LANES), 0) - start_ref[...]
+    for reach in range(1, CONV):
+        masks[reach - 1] = jnp.where(place >= reach, 1.0, 0.0)
+
+
+def conv_parts(ext, weight_ref, bias_ref, masks, rows):
     windows = []
     total = bias_ref[...]
     for tap in range(CONV):
         reach = CONV - 1 - tap
-        window = jnp.where(place >= reach, ext[8 - reach : 8 - reach + rows, :], 0.0)
+        window = ext[8 - reach : 8 - reach + rows, :]
+        if reach:
+            window = window * masks[reach - 1]
         windows.append(window)
         total = total + window * weight_ref[tap : tap + 1, :]
-    return place, windows, total
+    return windows, total
 
 
 def conv_forward(xbc, rim, weight, bias, meta, start_column, after=()):
     rows = xbc.shape[0]
 
-    def kernel(meta_ref, x_ref, rim_ref, weight_ref, bias_ref, start_ref, out_ref, ext):
+    def kernel(meta_ref, x_ref, rim_ref, weight_ref, bias_ref, start_ref, out_ref, ext, masks):
+        @pl.when(pl.program_id(0) == 0)
+        def _():
+            conv_masks(masks, start_ref, meta_ref[0], rows)
+
         ext[0:8, :] = rim_ref[...]
         ext[8:, :] = x_ref[...]
-        _, _, total = conv_parts(ext, weight_ref, bias_ref, start_ref, meta_ref[0], rows)
+        _, total = conv_parts(ext, weight_ref, bias_ref, masks, rows)
         out_ref[...] = total * jax.nn.sigmoid(total)
 
     lanes = lambda i, m: (0, i)
@@ -760,7 +769,10 @@
                 pl.BlockSpec((rows, 1), lambda i, m: (0, 0)),
             ] + pins(after),
             out_specs=pl.BlockSpec((rows, LANES), lanes),
-            scratch_shapes=[pltpu.VMEM((rows + 8, LANES), jnp.float32)],
+            scratch_shapes=[
+                pltpu.VMEM((rows + 8, LANES), jnp.float32),
+                pltpu.VMEM((CONV - 1, rows, LANES), jnp.float32),
+            ],
         ),
         out_shape=jax.ShapeDtypeStruct((rows, CHANNELS), jnp.float32),
         cost_estimate=pl.CostEstimate(flops=10**9, bytes_accessed=rows * CHANNELS * 8, transcendentals=0),
@@ -772,16 +784,20 @@
     rows = xbc.shape[0]
 
     def kernel(meta_ref, dx_ref, db_ref, dc_ref, x_ref, rim_ref, weight_ref, bias_ref, start_ref,
-               low_ref, tail_ref, edge_ref, small_ref, ext, upper):
+               low_ref, tail_ref, edge_ref, small_ref, ext, upper, masks):
+        @pl.when(pl.program_id(0) == 0)
+        def _():
+            conv_masks(masks, start_ref, meta_ref[0], rows)
+            upper[0:8, :] = jnp.zeros((8, LANES), jnp.float32)
+            upper[8 + rows :, :] = jnp.zeros((8, LANES), jnp.float32)
+
         ext[0:8, :] = rim_ref[...]
         ext[8:, :] = x_ref[...]
         at = pl.program_id(0)
         arrived = jnp.where(at < PAIRS, dx_ref[...], jnp.where(at == PAIRS, db_ref[...], dc_ref[...]))
-        place, windows, total = conv_parts(ext, weight_ref, bias_ref, start_ref, meta_ref[0], rows)
+        windows, total = conv_parts(ext, weight_ref, bias_ref, masks, rows)
         gate = jax.nn.sigmoid(total)
         change = arrived * gate * (1.0 + total * (1.0 - gate))
-        upper[0:8, :] = jnp.zeros((8, LANES), jnp.float32)
-        upper[8 + rows :, :] = jnp.zeros((8, LANES), jnp.float32)
         main = jnp.zeros((rows, LANES), jnp.float32)
         edge = jnp.zeros((8, LANES), jnp.float32)
         small_ref[...] = jnp.zeros((8, LANES), jnp.float32)
@@ -789,7 +805,8 @@
         for tap in range(CONV):
             reach = CONV - 1 - tap
             small_ref[tap : tap + 1, :] = jnp.sum(change * windows[tap], axis=0, keepdims=True)
-            upper[8 : 8 + rows, :] = jnp.where(place >= reach, change, 0.0) * weight_ref[tap : tap + 1, :]
+            masked = change * masks[reach - 1] if reach else change
+            upper[8 : 8 + rows, :] = masked * weight_ref[tap : tap + 1, :]
             main = main + upper[8 + reach : 8 + reach + rows, :]
             edge = edge + upper[reach : reach + 8, :]
         low_ref[...] = main.astype(jnp.bfloat16)
@@ -822,6 +839,7 @@
             scratch_shapes=[
                 pltpu.VMEM((rows + 8, LANES), jnp.float32),
                 pltpu.VMEM((rows + 16, LANES), jnp.float32),
+                pltpu.VMEM((CONV - 1, rows, LANES), jnp.float32),
             ],
         ),
         out_shape=[
@@ -841,11 +859,14 @@
     def kernel(left_ref, value_ref, weight_ref, out_ref, turned):
         @pl.when(pl.program_id(0) == 0)
         def _():
-            turned[...] = left_ref[...].T.astype(jnp.bfloat16)
-
-        wide = spread(weight_ref[0, 0:1, :], weight_ref[0, 1:2, :])
-        scaled = (value_ref[...] * wide).astype(jnp.bfloat16)
-        out_ref[...] = jnp.dot(turned[...], scaled, preferred_element_type=jnp.float32)
+            turned[...] = left_ref[...].T
+
+        scaled = [(turned[...] * weight_ref[0, e : e + 1, :]).astype(jnp.bfloat16) for e in range(2)]
+        both = jnp.dot(
+            jnp.concatenate(scaled, axis=0), value_ref[...].astype(jnp.bfloat16), preferred_element_type=jnp.float32
+        )
+        low_lane = lax.broadcasted_iota(jnp.int32, (STATE, 2 * SSM_DIM), 1) < SSM_DIM
+        out_ref[...] = jnp.where(low_lane, both[:STATE], both[STATE:])
 
     return pl.pallas_call(
         pinned(kernel, 3, after),
@@ -857,7 +878,7 @@
         ] + pins(after),
         out_specs=pl.BlockSpec((STATE, 2 * SSM_DIM), lambda i: (0, i)),
         out_shape=jax.ShapeDtypeStruct((STATE, INNER), jnp.float32),
-        scratch_shapes=[pltpu.VMEM((STATE, rows), jnp.bfloat16)],
+        scratch_shapes=[pltpu.VMEM((STATE, rows), jnp.float32)],
         cost_estimate=pl.CostEstimate(flops=2 * rows * STATE * INNER, bytes_accessed=rows * INNER * 4, transcendentals=0),
         name="state",
     )(left, values, weight_rows.reshape(PAIRS, 2, rows), *after)
@@ -1014,18 +1035,25 @@
             scaled = x_now * steps
             dy_low = low(dy_now)
             flow_low, state_low = low(flow[...]), low(states[k])
-            mixed, within = [], []
+            both = low(
+                jnp.concatenate([jnp.where(low_lane, scaled, 0.0), jnp.where(low_lane, 0.0, scaled)], axis=0)
+            )
+            reached = dot(both, dy_low, NT)
+            mixes, weighed = [], []
             for e in range(2):
                 across = jnp.broadcast_to(cums[e], (CHUNK, CHUNK))
                 decays = jnp.exp(across - across.T + hide[k])
-                own = low(jnp.where(low_lane == (e == 0), scaled, 0.0))
-                reach = decays * dot(own, dy_low, NT)
+                reach = decays * reached[e * CHUNK : (e + 1) * CHUNK]
                 inner_grad[k] += reach
-                sums = dot(low(inner[k] * reach), until)
-                within.append(jnp.sum(sums * before, axis=0, keepdims=True))
-                mixed.append(dot(low(inner[k] * decays), dy_low))
+                weighed.append(low(inner[k] * reach))
+                mixes.append(low(inner[k] * decays))
+            sums = dot(jnp.concatenate(weighed, axis=0), until)
+            within = [
+                jnp.sum(sums[e * CHUNK : (e + 1) * CHUNK] * before, axis=0, keepdims=True) for e in range(2)
+            ]
+            mixed = dot(jnp.concatenate(mixes, axis=0), dy_low)
             back = tail * dot(b_low, flow_low)
-            dxs = jnp.where(low_lane, mixed[0], mixed[1]) + back
+            dxs = jnp.where(low_lane, mixed[:CHUNK], mixed[CHUNK:]) + back
             db_ref[here, :] += dot(low(scaled * tail), flow_low, NT)
             entered = low(dy_now * entry)
             dc_ref[here, :] += dot(entered, state_low, NT)
@@ -1118,15 +1146,27 @@
     return flow.result
 
 
-def scan_stages(carry, state, backward):
+def scan_stages(carry, state, backward, extra=None):
     total = (jnp.repeat(carry, SSM_DIM)[None, :], state)
     start = None
     for name in ("c", "x", "y"):
         place = lax.axis_index(name)
-        packed = jnp.concatenate([total[1], jnp.broadcast_to(total[0], (16, INNER))], axis=0)
+        rows = [total[1], total[0]]
+        if extra is None:
+            rows.append(jnp.zeros((15, INNER), jnp.float32))
+        else:
+            rest = extra
+            for _ in range(3):
+                term = lax.reduce_precision(rest, 8, 7)
+                rows.append(jnp.pad(term, (0, INNER - term.shape[0]))[None, :])
+                rest = rest - term
+            rows.append(jnp.zeros((12, INNER), jnp.float32))
+        packed = jnp.concatenate(rows, axis=0)
         (packed,) = yield [(packed.astype(jnp.bfloat16), name, SWAP)]
         packed = packed.astype(jnp.float32)
         other = (packed[STATE : STATE + 1], packed[:STATE])
+        if extra is not None:
+            extra = extra + jnp.sum(packed[STATE + 1 : STATE + 4, : extra.shape[0]], axis=0)
         leads = place == (0 if backward else 1)
         seen = (jnp.where(leads, other[0], 1.0), jnp.where(leads, other[1], 0.0))
         start = seen if start is None else chain_states(seen, start)
@@ -1134,7 +1174,7 @@
             forward = chain_states(other, total)
             reverse = chain_states(total, other)
             total = jax.tree.map(lambda p, q: jnp.where(leads, p, q), forward, reverse)
-    return start[1]
+    return start[1] if extra is None else [start[1], extra]
 
 
 KEYS = 512
@@ -1142,7 +1182,7 @@
 
 
 def attention_forward(q_wide, kv, meta, starts, after=()):
-    rows = q_wide.shape[1]
+    rows = q_wide.shape[2]
     blocks = kv.shape[0]
     ratio = HEADS_Q // HEADS_KV
     wide = min(512, rows)
@@ -1162,7 +1202,7 @@
             for h in range(ratio):
                 for r in range(0, rows, wide):
                     here = slice(r, r + wide)
-                    scores = lax.dot_general(pair, q_ref[h, here, :], NT, preferred_element_type=jnp.float32)
+                    scores = jnp.dot(pair, q_ref[h, :, here], preferred_element_type=jnp.float32)
                     if partial:
                         keys = b * KEYS + lax.broadcasted_iota(jnp.int32, scores.shape, 0)
                         mine = meta_ref[2] + r + lax.broadcasted_iota(jnp.int32, scores.shape, 1)
@@ -1205,7 +1245,7 @@
             num_scalar_prefetch=1,
             grid=(HEADS_KV, blocks),
             in_specs=[
-                pl.BlockSpec((ratio, rows, PAIR), heads),
+                pl.BlockSpec((ratio, PAIR, rows), heads),
                 pl.BlockSpec((1, 1, KEYS, PAIR), lambda g, b, m: (b, g, 0, 0)),
                 pl.BlockSpec((8, rows), lambda g, b, m: (0, 0)),
             ] + pins(after),
@@ -1229,7 +1269,7 @@
 
 
 def attention_backward(q_wide, g_wide, kv, logs, mixed, meta, starts, group, after=()):
-    rows = q_wide.shape[1]
+    rows = q_wide.shape[2]
     blocks = kv.shape[0]
     ratio = HEADS_Q // HEADS_KV
     wide = min(512, rows)
@@ -1241,7 +1281,7 @@
         def _():
             dq_ref[...] = jnp.zeros(dq_ref.shape, jnp.float32)
             for h in range(ratio):
-                both = g_ref[h].astype(jnp.float32).T[HEAD_DIM:, :] * o_ref[h]
+                both = g_ref[h, HEAD_DIM:, :].astype(jnp.float32) * o_ref[h]
                 delta[h] = jnp.broadcast_to(jnp.sum(both, axis=0, keepdims=True), (8, rows))
 
         def block(partial):
@@ -1250,20 +1290,20 @@
             for h in range(ratio):
                 for r in range(0, rows, wide):
                     here = slice(r, r + wide)
-                    q_now = q_ref[h, here, :]
-                    g_now = g_ref[h, here, :]
-                    scores = lax.dot_general(pair, q_now, NT, preferred_element_type=jnp.float32)
+                    q_now = q_ref[h, :, here]
+                    g_now = g_ref[h, :, here]
+                    scores = jnp.dot(pair, q_now, preferred_element_type=jnp.float32)
                     probs = jnp.exp(scores - log_ref[h, 0:1, here])
                     if partial:
                         keys = b * KEYS + lax.broadcasted_iota(jnp.int32, scores.shape, 0)
                         mine = meta_ref[2] + r + lax.broadcasted_iota(jnp.int32, scores.shape, 1)
                         visible = (keys >= start_ref[0:1, here]) & (keys <= mine)
                         probs = jnp.where(visible, probs, 0.0)
-                    grads = lax.dot_general(pair, g_now, NT, preferred_element_type=jnp.float32)
+                    grads = jnp.dot(pair, g_now, preferred_element_type=jnp.float32)
                     low_grads = (probs * (grads - delta[h, 0:1, here])).astype(jnp.bfloat16)
-                    change = jnp.dot(
-                        probs.astype(jnp.bfloat16), g_now, preferred_element_type=jnp.float32
-                    ) + jnp.dot(low_grads, q_now, preferred_element_type=jnp.float32)
+                    change = lax.dot_general(
+                        probs.astype(jnp.bfloat16), g_now, NT, preferred_element_type=jnp.float32
+                    ) + lax.dot_general(low_grads, q_now, NT, preferred_element_type=jnp.float32)
                     if h == 0 and r == 0:
                         sums[...] = change
                     else:
@@ -1293,8 +1333,8 @@
             num_scalar_prefetch=1,
             grid=(blocks,),
             in_specs=[
-                pl.BlockSpec((ratio, rows, PAIR), heads),
-                pl.BlockSpec((ratio, rows, PAIR), heads),
+                pl.BlockSpec((ratio, PAIR, rows), heads),
+                pl.BlockSpec((ratio, PAIR, rows), heads),
                 pl.BlockSpec((1, 1, KEYS, PAIR), lambda b, m: (b, group, 0, 0)),
                 pl.BlockSpec((ratio, 8, rows), heads),
                 pl.BlockSpec((ratio, HEAD_DIM, rows), heads),
@@ -1319,31 +1359,6 @@
     )(meta, q_wide, g_wide, kv, logs, mixed, starts, *after)
 
 
-def ordered(place, own, other, axis):
-    first = jnp.where(place == 0, own, other)
-    second = jnp.where(place == 0, other, own)
-    return jnp.stack([first, second], axis=axis)
-
-
-def gather_span(value, span, fast):
-    if not fast:
-        return lax.all_gather(value, span)
-    flow = Flow(gather_stages(value))
-    while flow.sends:
-        flow.go()
-    return flow.result
-
-
-def gather_stages(value):
-    _, y, x, c = (lax.axis_index(name) for name in GRID)
-    (other,) = yield [(value, "x", SWAP)]
-    two = ordered(x, value, other, 0)
-    (other,) = yield [(two, "y", SWAP)]
-    four = ordered(y, two, other, 0)
-    (other,) = yield [(four, "c", SWAP)]
-    return ordered(c, four, other, 2).reshape((8,) + value.shape)
-
-
 def scatter_span(value, span, fast):
     if not fast:
         return lax.psum_scatter(value, span, scatter_dimension=0).astype(jnp.float32)
@@ -1366,10 +1381,7 @@
     return value
 
 
-def sum_stages(value):
-    for name in GRID[1:]:
-        (other,) = yield [(value, name, SWAP)]
-        value = value + other
+def plane_stages(value):
     for pairs in ([(0, 1), (1, 0), (2, 3), (3, 2)], [(0, 2), (2, 0), (1, 3), (3, 1)]):
         (other,) = yield [(value, "z", pairs)]
         value = value + other
@@ -1504,14 +1516,13 @@
     x_rows = tokens.astype(jnp.float32)
     normed_one, norm_one_back = jax.vjp(rms_norm, x_rows, small_f32[NORM_ATTN])
     hidden = normed_one.astype(jnp.bfloat16)
-    query = matmul(hidden, weights[W_QUERY])
-    key_raw = matmul(hidden, weights[W_KEY])
-    value_low = matmul(hidden, weights[W_VALUE]).astype(jnp.bfloat16)
-    q_rot = rotate(query, cosine, sine, HEADS_Q).astype(jnp.bfloat16)
-    k_rot = rotate(key_raw, cosine, sine, HEADS_KV).astype(jnp.bfloat16)
-    k_heads = k_rot.reshape(rows_dev, HEADS_KV, HEAD_DIM)
-    v_heads = value_low.reshape(rows_dev, HEADS_KV, HEAD_DIM)
-    kv_mine = jnp.concatenate([k_heads, v_heads], axis=2).transpose(1, 0, 2)
+    across = lambda weight: lax.dot_general(
+        weight, hidden, (((0,), (1,)), ((), ())), preferred_element_type=jnp.float32
+    )
+    q_rot = rotate(across(weights[W_QUERY]), cosine, sine, HEADS_Q).astype(jnp.bfloat16)
+    k_rot = rotate(across(weights[W_KEY]), cosine, sine, HEADS_KV).astype(jnp.bfloat16)
+    value_low = across(weights[W_VALUE]).astype(jnp.bfloat16).reshape(HEADS_KV, HEAD_DIM, rows_dev)
+    kv_mine = jnp.concatenate([k_rot, value_low], axis=1).transpose(0, 2, 1)
     row_starts = row_index - positions
     kv_local = kv_mine.reshape(HEADS_KV, rows_dev, PAIR)
     xbc = jnp.concatenate(
@@ -1525,9 +1536,8 @@
         xbc, rim_rows, small_f32[CONV_WEIGHT], conv_bias, ssm_meta, row_starts[:, None], after
     )
     if fast:
-        keys_flow = Flow(gather_stages(kv_local))
-        keys_flow.go()
-        (conv_values,) = bracket(convolve, [keys_flow, spread_flow])
+        key_blocks = lax.all_gather(kv_local, span)
+        (conv_values,) = bracket(convolve, [spread_flow])
     else:
         conv_values = convolve(())
     step_in = step_raw.T + small_f32[STEP_BIAS][:, None]
@@ -1549,13 +1559,11 @@
     meta = jnp.stack(
         [first_start // KEYS, last_row // KEYS + 1, my_start, row_starts[rows_dev - 1]]
     ).astype(jnp.int32)
-    q_low = (q_rot * jnp.bfloat16(score_scale)).reshape(rows_dev, HEADS_Q, HEAD_DIM).transpose(1, 0, 2)
-    q_wide = jnp.pad(q_low, ((0, 0), (0, 0), (0, HEAD_DIM)))
+    q_wide = jnp.pad(q_rot * jnp.bfloat16(score_scale), ((0, 0), (0, HEAD_DIM), (0, 0)))
     start_row = jnp.broadcast_to(row_starts[None, :], (8, rows_dev))
     if fast:
-        (local_state,) = bracket(lambda after: summarize((*after, *spread_flow.values())), [keys_flow])
+        local_state = summarize(())
         scan = Flow(scan_stages(carry_all, local_state, False))
-        key_blocks = keys_flow.result
         (gate_in,) = fence([hidden], scan.values())
         gate_ssm = matmul(gate_in, weights[W_GATE_SSM])
         scan.go()
@@ -1617,12 +1625,12 @@
     grad_middle_norm, grad_norm_ffn = norm_two_back(grad_hidden_two)
     grad_middle = grad_out + grad_middle_norm
     grad_branch = grad_middle.astype(jnp.bfloat16)
-    grad_attended = matmul_right_t(grad_branch, weights[W_ATTN_OUT]).astype(jnp.bfloat16)
+    grad_attended = matmul_right_t(weights[W_ATTN_OUT], grad_branch).astype(jnp.bfloat16)
     grad_ssm_low = matmul_right_t(grad_branch, weights[W_SSM_OUT])
     grad_ssm_y, grad_gate_ssm_f32, grad_norm_ssm = gnorm_back(grad_ssm_low)
     grad_state_local = weighted_state(conv_values, PAIRS + 1, grad_ssm_y, entry_rows)
     if fast:
-        scan = Flow(scan_stages(carry_all, grad_state_local, True))
+        scan = Flow(scan_stages(carry_all, grad_state_local, True, squares)).go()
         (late,) = bracket(
             lambda after: pack_late(
                 (hidden_two, grad_gate), (hidden_two, grad_upper), (activation, cotangent),
@@ -1631,10 +1639,14 @@
             [scan],
         )
         late_flow = Flow(reduce_stages(late, 1, 14))
-        (early,) = bracket(lambda after: pack_out(ssm_low, grad_branch, after + late_flow.values()), [scan])
+        (grad_branch_low,) = fence([grad_branch], scan.values() + late_flow.values())
+        early = pack_out(ssm_low, grad_branch_low, ())
         scan.go()
+        grad_state_out, squares = scan.result
+        (early,) = fence([early], [grad_state_out])
         late_flow.go()
-        grad_state_out = scan.result
+        (early,) = fence([early], late_flow.values())
+        stats_flow = Flow(plane_stages(squares))
         around = lambda call: bracket(call, [late_flow])
     else:
         grad_state_out = scan_states(carry_all, grad_state_local, span, fast, True)
@@ -1652,6 +1664,8 @@
     grad_step_bias = jnp.sum(grad_step_rows, axis=1)
     grad_step_raw_f32 = grad_step_rows.T
     grad_skip_gain = jnp.sum(grad_small[:, 4, : 2 * SSM_DIM].reshape(SSM_HEADS, SSM_DIM), axis=1)
+    if fast:
+        around = lambda call: bracket(call, [late_flow, stats_flow])
     grad_main, grad_tail, grad_edge, grad_taps = around(
         lambda after: conv_backward(
             grad_x, grad_b, grad_c, xbc, rim_rows, small_f32[CONV_WEIGHT], conv_bias, ssm_meta,
@@ -1684,19 +1698,18 @@
     }
     parts = []
     if fast:
-        early = pack_ssm(
+        (early,) = bracket(lambda after: pack_ssm(
             early,
             [
                 (attended, grad_branch), (hidden, grad_gate_ssm),
                 (hidden, grad_xbc[:, :ssm_inner]), (hidden, grad_xbc[:, ssm_inner:]),
             ],
-            small, ssm_low, grad_branch, late_flow.values(),
-        )
+            small, ssm_low, grad_branch, (*after, *late_flow.values()),
+        ), [stats_flow])
         early_flow = Flow(reduce_stages(early, 0, 8))
         (grad_attended,) = fence([grad_attended], early_flow.values() + late_flow.values())
         around = lambda call: bracket(call, [early_flow])
-    g_low = grad_attended.reshape(rows_dev, HEADS_Q, HEAD_DIM).transpose(1, 0, 2)
-    g_wide = jnp.pad(g_low, ((0, 0), (0, 0), (HEAD_DIM, 0)))
+    g_wide = jnp.pad(grad_attended.reshape(HEADS_Q, HEAD_DIM, rows_dev), ((0, 0), (HEAD_DIM, 0), (0, 0)))
     if fast:
         early_flow.go()
         (g_wide,) = fence([g_wide], early_flow.values())
@@ -1719,11 +1732,7 @@
         late_flow.go([parts[-1][1]])
         scatter = Flow(scatter_stages(grad_kv))
         (grad_q_turned,) = fence([grad_q_turned], scatter.values() + early_flow.values() + late_flow.values())
-    halves = grad_q_turned.reshape(HEADS_Q, 2, HEAD_DIM // 2, rows_dev) * score_scale
-    cos_t, sin_t = cosine.T[None], sine.T[None]
-    turned_back = jnp.stack(
-        [halves[:, 0] * cos_t + halves[:, 1] * sin_t, halves[:, 1] * cos_t - halves[:, 0] * sin_t], axis=1
-    ).astype(jnp.bfloat16)
+    turned_back = rotate(grad_q_turned * score_scale, cosine, -sine, HEADS_Q).astype(jnp.bfloat16)
     grad_query_low = turned_back.reshape(HEADS_Q * HEAD_DIM, rows_dev).T
     if fast:
         scatter.go()
@@ -1737,10 +1746,10 @@
         grad_kv_mine = scatter.result
     else:
         grad_kv_mine = scatter_span(grad_kv, span, fast)
-    grad_keys_mine = grad_kv_mine[:, :, :HEAD_DIM].transpose(1, 0, 2).reshape(rows_dev, -1)
-    grad_values_mine = grad_kv_mine[:, :, HEAD_DIM:].transpose(1, 0, 2).reshape(rows_dev, -1)
-    grad_key_low = rotate(grad_keys_mine, cosine, -sine, HEADS_KV).astype(jnp.bfloat16)
-    grad_value_low = grad_values_mine.astype(jnp.bfloat16)
+    grad_kv_mine = grad_kv_mine.transpose(0, 2, 1)
+    grad_key_low = rotate(grad_kv_mine[:, :HEAD_DIM], cosine, -sine, HEADS_KV).astype(jnp.bfloat16)
+    grad_key_low = grad_key_low.reshape(HEADS_KV * HEAD_DIM, rows_dev).T
+    grad_value_low = grad_kv_mine[:, HEAD_DIM:].astype(jnp.bfloat16).reshape(HEADS_KV * HEAD_DIM, rows_dev).T
     grad_hidden = (
         grad_hidden
         + matmul_right_t(grad_key_low, weights[W_KEY])
@@ -1754,16 +1763,13 @@
             attended, grad_branch, grad_norm_attn, early_flow.values(),
         )
         corner_flow = Flow(corner_stages(corner))
-        (squares,) = fence([squares], corner_flow.values())
-        stats_flow = Flow(sum_stages(squares))
         for _ in range(3):
             corner_flow.go()
-            stats_flow.go()
         early_flow.go()
         ((pieces, _, _), *_) = corner_flow.sends
         (pieces,) = fence([pieces], early_flow.values())
         corner_flow.sends = [(pieces, axis, pairs) for _, axis, pairs in corner_flow.sends]
-        for flow in (stats_flow, early_flow, late_flow, corner_flow):
+        for flow in (early_flow, late_flow, corner_flow):
             while flow.sends:
                 flow.go()
         stats = jnp.sqrt(stats_flow.result / (all_rows * D))

time: 965 us -> 917 us (0.950)
  waiting for transfers between devices: 217 us -> 149 us
  between operations: 5.33 us -> 18.5 us
    ppermute x58 -> x53, waiting for transfers between devices: 164 us -> 105 us  [go(): lax.ppermute(value, axis, pairs)]
    concatenate x2 -> x4, local copies, waits for them, and re-layouts: 2.19 us -> 16.4 us  [scan_stages(): packed = jnp.concatenate(rows, axis=0)]
    ppermute x2, waiting for transfers between devices: 13.8 us -> 0.01 us  [gather_lines(): over_y = lax.ppermute(column, 'y', SWAP)]
    another operation x26 -> x24, other arithmetic: 25.6 us -> 15.7 us
    unnamed x429 -> x403, local copies, waits for them, and re-layouts: 51.9 us -> 42.5 us
    ppermute x58 -> x53, starting transfers between devices: 149 us -> 146 us  [go(): lax.ppermute(value, axis, pairs)]
    dot_general x12 -> x9, matrix products: 28.3 us -> 29.5 us  [matmul(): return jnp.dot(left, right, preferred_element_type=jnp.float32)]
  transfers between devices with their start and end apart: 87 -> 83, of which waited for: 33 -> 27; matrix products, arithmetic and copies ran while one was open for 20% -> 20% of each run, Pallas kernels for 16% -> 16%
where the time goes in v9:
time: 917 us; the launch traced here: 902 us
  Pallas kernels  207 us (23%)
  starting transfers between devices  189 us (21%)
  waiting for transfers between devices  149 us (16%)
  other arithmetic  138 us (15%)
  local copies, waits for them, and re-layouts  119 us (13%)
  matrix products  81 us (9%)
  between operations  18.5 us (2%)
    ppermute x53, starting transfers between devices, go(): lax.ppermute(value, axis, pairs)  146 us
    ppermute x53, waiting for transfers between devices, go(): lax.ppermute(value, axis, pairs)  105 us
    pallas_call x2, Pallas kernels, unpack_lines(): pl.pallas_call(pinned(kernel, 2 + count_buffers, after), grid_spec=pltpu....  48.5 us
    dot_general x12, matrix products, matmul_right_t(): lax.dot_general(left, right, (((1,), (1,)), ((), ())), preferred_element_...  46.8 us
    pallas_call x4, Pallas kernels, pack_lines(): pl.pallas_call(pinned(kernel, inputs, after), grid=(total,), in_specs=[le...  42.8 us
    unnamed x403, local copies, waits for them, and re-layouts  42.5 us
    pallas_call x1, Pallas kernels, ssm_backward(): pl.pallas_call(pinned(kernel, 11, after), grid_spec=pltpu.PrefetchScalarG...  33.2 us
    convert_element_type x14, other arithmetic, added(): return total.astype(jnp.bfloat16)  32.9 us
  transfers between devices with their start and end apart: 83, of which 27 were waited for; matrix products, arithmetic and copies ran while one was open for 20% of the time, Pallas kernels for 16%

profile of v9, /device:TPU:0, one launch (start us, length us, event | category | flops | bytes accessed | tf_op | source)
XLA Modules:
  0.0 901.7 jit_solution(14322223243299762396)
XLA Ops:
  29.5 6.1 collective-permute-done.12
  48.3 9.4 %collective-permute-start.8 = (bf16[3088,128]{1,0:T(8,128)(2,1)S(1)}, bf16[3088,128]{1,0:T(8,128)(2,1)}, u32[]{:S(2)}, u32[]{:S(2)}) collective-permute-start(bf16[3088,128]{1,0:T(8,128)(2,1)S(1)} %add_select_fusion.2), channel_id=1, source_target_pairs={{0,1},{1,0},{2,3},{3,2},{4,5},{5,4},{6,7},{7,6},{8,9},{9,8},{10,11... | collective-permute-start | bytes 2371592 | tf_op jit(solution)/shard_map/ppermute | solution.py:297
  62.2 12.5 %collective-permute-done.26 = bf16[2,3088,128]{2,1,0:T(8,128)(2,1)} collective-permute-done((bf16[2,3088,128]{2,1,0:T(8,128)(2,1)}, bf16[2,3088,128]{2,1,0:T(8,128)(2,1)}, u32[]{:S(2)}, u32[]{:S(2)}) %collective-permute-start.26) | collective-permute-done | bytes 1581088 | tf_op jit(solution)/shard_map/ppermute | solution.py:302
  92.9 16.0 %collective-permute-done.7 = bf16[3088,128]{1,0:T(8,128)(2,1)} collective-permute-done((bf16[3088,128]{1,0:T(8,128)(2,1)S(1)}, bf16[3088,128]{1,0:T(8,128)(2,1)}, u32[]{:S(2)}, u32[]{:S(2)}) %collective-permute-start.7) | collective-permute-done | bytes 790560 | tf_op jit(solution)/shard_map/ppermute | solution.py:294
  110.2 5.4 add_select_fusion.refs_1_.refs_6_.refs_18_
  120.1 14.4 %unpack.2 = (bf16[1024,512]{1,0:T(8,128)(2,1)}, bf16[1024,128]{1,0:T(8,128)(2,1)S(1)}, bf16[1024,128]{1,0:T(8,128)(2,1)S(1)}, bf16[512,1024]{1,0:T(8,128)(2,1)},...) custom-call(s32[25,5]{1,0:T(8,128)S(1)} %copy-done.57, ...), custom_call_target="tpu_custom_call" | custom-call | bytes 26624000 | tf_op jit(solution)/shard_map/unpack/pallas_call | solution.py:454
  166.4 11.3 %conv.1.refs_0_ = f32[512,1792]{1,0:T(8,128)} custom-call(s32[5]{0:T(128)} %pad_add_fusion.1.refs_0_.meta_ref, f32[512,1792]{1,0:T(8,128)} %pad_maximum_fusion.refs_1_.refs_4_, f32[8,1792]{1,0:T(8,128)} %collective-permute-done.23.refs_2_.refs_5_, f32[4,1792]{1,0:T(4,128)} %reshape.411.refs_3_.refs_6_, f32[1,1792]{1,0:T(1,128)} %bitcast.328, ...), custom_call_target="tpu_custom_call" | custom-call | flops 1000000000 | bytes 7340032 | tf_op jit(solution)/shard_map/conv/pallas_call | solution.py:759
  179.4 8.8 state.2
  199.9 5.3 fusion.102.refs_0_
  205.2 7.6 collective-permute-done.33
  218.4 14.6 %attend.1 = (f32[8,64,512]{2,1,0:T(8,128)S(1)}, f32[8,8,512]{2,1,0:T(8,128)S(1)}) custom-call(s32[4]{0:T(128)S(1)} %pad_add_fusion.refs_0_, bf16[8,128,512]{2,1,0:T(8,128)(2,1)S(1)} %pad.60.refs_1_, bf16[8,2,512,128]{3,2,1,0:T(8,128)(2,1)} %bitcast.333, s32[8,512]{1,0:T(8,128)S(1)} %broadcast_in_dim.221.refs_3_.row_ref.refs_10_.refs_6_, ...), custom_call_target="tpu_custom_call" | custom-call | flops 20000000000 | bytes 8388608 | tf_op jit(solution)/shard_map/attend/pallas_call | solution.py:1242
  234.6 5.8 collective-permute-start.39
  246.8 8.5 ssm.1.refs_28_
  257.9 34.1 %unpack.3 = (bf16[1536,1024]{1,0:T(8,128)(2,1)}, bf16[1024,2048]{1,0:T(8,128)(2,1)}, bf16[1024,2048]{1,0:T(8,128)(2,1)}, bf16[2048,1024]{1,0:T(8,128)(2,1)}, bf16[16,128]{1,0:T(8,128)(2,1)S(1)}) custom-call(s32[31,5]{1,0:T(8,128)S(1)} %copy-done.56, s32[32]{0:T(128)S(1)} %fusion.78.refs_1_, bf16[1,3088,128]{2,1,0:T(8,128)(2,1)S(1)} %bitcast.267, ...), custom_call_target="tpu_custom_call" | custom-call | bytes 33013760 | tf_op jit(solution)/shard_map/unpack/pallas_call | solution.py:454
  307.4 6.7 fusion.2
  314.2 6.9 fusion.106
  337.8 8.7 state.3
  354.0 5.4 concatenate.72
  368.9 6.4 pad_maximum_fusion.1
  380.4 5.4 concatenate.73.refs_7_
  385.9 8.1 collective-permute-start.41
  399.8 20.6 %pack.4.refs_0_ = bf16[49344,128]{1,0:T(8,128)(2,1)} custom-call(bf16[512,1024]{1,0:T(8,128)(2,1)S(1)} %copy-done.41, bf16[512,2048]{1,0:T(8,128)(2,1)S(1)} %copy-done.64, bf16[512,2048]{1,0:T(8,128)(2,1)} %get-tuple-element.214.refs_2_, bf16[512,2048]{1,0:T(8,128)(2,1)} %get-tuple-element.215.refs_3_, bf16[512,1024]{1,0:T(8,128)(2,1)S(1)} %copy-done.39, ...), custom_call_target="tpu_custom_call" | custom-call | flops 6442450944 | bytes 16777216 | tf_op jit(solution)/shard_map/pack/pallas_call | solution.py:609
  425.2 5.5 concatenate.74.refs_1_
  430.7 5.9 constant_dynamic-slice_fusion.2.refs_2_
  439.8 28.6 %collective-permute-start.42 = (bf16[144,1536]{1,0:T(8,128)(2,1)}, bf16[144,1536]{1,0:T(8,128)(2,1)}, u32[]{:S(2)}, u32[]{:S(2)}) collective-permute-start(bf16[144,1536]{1,0:T(8,128)(2,1)} %concatenate.74.refs_1_), channel_id=1, source_target_pairs={{0,4},{4,0},{1,5},{5,1},{2,6},{6,2},{3,7},{7,3},{8,12},{12,8},{9,1... | collective-permute-start | bytes 1327112 | tf_op jit(solution)/shard_map/ppermute | solution.py:248
  480.5 5.8 add_convert_fusion.1
  489.8 5.1 collective-permute-start.48
  496.5 22.0 %collective-permute-start.50 = (f32[4]{0:T(128)S(1)}, f32[4]{0:T(128)S(1)}, u32[]{:S(2)}, u32[]{:S(2)}) collective-permute-start(f32[4]{0:T(128)S(1)} %add.669.refs_7_.refs_8_), channel_id=1, source_target_pairs={{0,16},{16,0},{8,24},{24,8},{1,17},{17,1},{9,25},{25,9},{2,18},{18... | collective-permute-start | bytes 56 | tf_op jit(solution)/shard_map/ppermute | solution.py:248
  527.6 33.2 %ssm_back.1 = (f32[512,1536]{1,0:T(8,128)S(1)}, f32[512,128]{1,0:T(8,128)S(1)}, f32[512,128]{1,0:T(8,128)S(1)}, f32[12,8,512]{2,1,0:T(8,128)S(1)}) custom-call(s32[5]{0:T(128)S(1)} %copy-done.58, f32[512,1792]{1,0:T(8,128)} %fence.21.refs_0_.refs_1_.x_ref.b_ref.c_ref.refs_3_.refs_4_, f32[512,1536]{1,0:T(8,128)S(1)} %copy-done.6, ...), custom_call_target="tpu_custom_call" | custom-call | flops 3000000000 | bytes 9437184 | tf_op jit(solution)/shard_map/ssm_back/pallas_call | solution.py:1088
  576.4 14.7 %conv_back.1 = (bf16[512,1792]{1,0:T(8,128)(2,1)}, f32[16,1792]{1,0:T(8,128)}, f32[8,1792]{1,0:T(8,128)}, f32[8,1792]{1,0:T(8,128)}) custom-call(s32[5]{0:T(128)} %pad_add_fusion.1.refs_0_.meta_ref, f32[512,1536]{1,0:T(8,128)} %get-tuple-element.82.refs_1_, f32[512,128]{1,0:T(8,128)} %get-tuple-element.83.refs_2_, f32[512,128]{1,0:T(8,128)} %get-tuple-element.84.refs_3_, ...), custom_call_target="tpu_custom_call" | custom-call | flops 2000000000 | bytes 9175040 | tf_op jit(solution)/shard_map/conv_back/pallas_call | solution.py:818
  604.0 12.1 %pack.6.refs_0_ = bf16[49440,128]{1,0:T(8,128)(2,1)} custom-call(bf16[512,512]{1,0:T(8,128)(2,1)S(1)} %bitcast.274, bf16[512,1024]{1,0:T(8,128)(2,1)S(1)} %copy-done.2, bf16[512,1024]{1,0:T(8,128)(2,1)S(1)} %fusion.89.refs_2_, bf16[512,1536]{1,0:T(8,128)(2,1)S(1)} %copy-done.12, ...), custom_call_target="tpu_custom_call", output_to_operand_aliasing={{}: (7, {})} | custom-call | flops 4026531840 | bytes 11010048 | tf_op jit(solution)/shard_map/pack/pallas_call | solution.py:609
  616.1 5.9 constant_dynamic-slice_fusion.1.refs_1_
  626.5 5.1 fusion.107
  645.6 5.0 fusion.87
  650.6 5.8 add_convert_fusion
  664.9 7.6 attend_back.2
  672.5 24.0 %collective-permute-done.52 = bf16[2,3104,128]{2,1,0:T(8,128)(2,1)} collective-permute-done((bf16[2,3104,128]{2,1,0:T(8,128)(2,1)}, bf16[2,3104,128]{2,1,0:T(8,128)(2,1)}, u32[]{:S(2)}, u32[]{:S(2)}) %collective-permute-start.52) | collective-permute-done | bytes 1589280 | tf_op jit(solution)/shard_map/ppermute | solution.py:248
  708.7 8.2 attend_back.3
  748.6 11.5 %collective-permute-start.63 = (bf16[2,2,512,128]{3,2,1,0:T(8,128)(2,1)S(1)}, bf16[2,2,512,128]{3,2,1,0:T(8,128)(2,1)}, u32[]{:S(2)}, u32[]{:S(2)}) collective-permute-start(bf16[2,2,512,128]{3,2,1,0:T(8,128)(2,1)S(1)} %dynamic-slice_bitcast_fusion.21.refs_1_), channel_id=1, source_target_pairs={{0,4},{4,0},{1,5},{5,1},{2,6},{6,2},{3,7},{7,3},{8,12},{12,8},{9,1... | collective-permute-start | bytes 1572872 | tf_op jit(solution)/shard_map/ppermute | solution.py:248
  760.1 6.3 collective-permute-done.61
  773.6 6.0 collective-permute-start.64
  779.5 5.6 add_add_fusion.4.refs_0_
  789.2 5.4 fusion.12
  794.5 5.4 pack.7
  811.5 12.8 %collective-permute-done.72 = bf16[3104,128]{1,0:T(8,128)(2,1)S(1)} collective-permute-done((bf16[3104,128]{1,0:T(8,128)(2,1)S(1)}, bf16[3104,128]{1,0:T(8,128)(2,1)S(1)}, u32[]{:S(2)}, u32[]{:S(2)}) %collective-permute-start.72) | collective-permute-done | bytes 794656 | tf_op jit(solution)/shard_map/ppermute | solution.py:248
  824.3 19.1 %collective-permute-done.71 = bf16[3104,128]{1,0:T(8,128)(2,1)S(1)} collective-permute-done((bf16[3104,128]{1,0:T(8,128)(2,1)S(1)}, bf16[3104,128]{1,0:T(8,128)(2,1)S(1)}, u32[]{:S(2)}, u32[]{:S(2)}) %collective-permute-start.71) | collective-permute-done | bytes 794656 | tf_op jit(solution)/shard_map/ppermute | solution.py:248
  851.1 5.3 collective-permute-start.67
  885.9 4.8 fusion.14
  (821 shorter events, 378.5 us)
Async XLA Ops:
  7.2 211.2 %all-gather.3.cloned.1.call-start = ((), (), s32[]{:S(2)}) async-start(), calls=%async_computation | async-start | bytes 2359296 | tf_op jit(solution)/shard_map/all_gather | solution.py:1539
  20.4 21.4 %collective-permute-start.24 = (bf16[2,3088,128]{2,1,0:T(8,128)(2,1)}, bf16[2,3088,128]{2,1,0:T(8,128)(2,1)}, u32[]{:S(2)}, u32[]{:S(2)}) collective-permute-start(bf16[2,3088,128]{2,1,0:T(8,128)(2,1)} %maximum_select_fusion), channel_id=1, source_target_pairs={{16,8},{25,17},{18,10},{27,19},{20,12},{29,21},{22,14},{31,23}} | collective-permute-start | bytes 4743176 | tf_op jit(solution)/shard_map/ppermute | solution.py:300
  40.3 20.3 %collective-permute-start.25 = (bf16[2,3088,128]{2,1,0:T(8,128)(2,1)}, bf16[2,3088,128]{2,1,0:T(8,128)(2,1)S(1)}, u32[]{:S(2)}, u32[]{:S(2)}) collective-permute-start(bf16[2,3088,128]{2,1,0:T(8,128)(2,1)} %maximum_select_fusion), channel_id=1, source_target_pairs={{16,24},{18,26},{20,28},{22,30}} | collective-permute-start | bytes 4743176 | tf_op jit(solution)/shard_map/ppermute | solution.py:301
  41.8 32.8 %collective-permute-start.26 = (bf16[2,3088,128]{2,1,0:T(8,128)(2,1)}, bf16[2,3088,128]{2,1,0:T(8,128)(2,1)}, u32[]{:S(2)}, u32[]{:S(2)}) collective-permute-start(bf16[2,3088,128]{2,1,0:T(8,128)(2,1)} %collective-permute-done.24), channel_id=1, source_target_pairs={{8,0},{17,9},{10,2},{19,11},{12,4},{21,13},{14,6},{23,15}} | collective-permute-start | bytes 4743176 | tf_op jit(solution)/shard_map/ppermute | solution.py:302
  45.3 30.9 %collective-permute-start.5 = (bf16[3088,128]{1,0:T(8,128)(2,1)S(1)}, bf16[3088,128]{1,0:T(8,128)(2,1)S(1)}, u32[]{:S(2)}, u32[]{:S(2)}) collective-permute-start(bf16[3088,128]{1,0:T(8,128)(2,1)S(1)} %add_select_fusion.2), channel_id=1, source_target_pairs={{0,2},{2,0},{1,3},{3,1},{4,6},{6,4},{5,7},{7,5},{8,10},{10,8},{9,1... | collective-permute-start | bytes 2371592 | tf_op jit(solution)/shard_map/ppermute | solution.py:292
  46.8 41.8 %collective-permute-start.6 = (bf16[3088,128]{1,0:T(8,128)(2,1)S(1)}, bf16[3088,128]{1,0:T(8,128)(2,1)S(1)}, u32[]{:S(2)}, u32[]{:S(2)}) collective-permute-start(bf16[3088,128]{1,0:T(8,128)(2,1)S(1)} %add_select_fusion.2), channel_id=1, source_target_pairs={{0,4},{4,0},{1,5},{5,1},{2,6},{6,2},{3,7},{7,3},{8,12},{12,8},{9,1... | collective-permute-start | bytes 2371592 | tf_op jit(solution)/shard_map/ppermute | solution.py:293
  48.3 40.4 %collective-permute-start.8 = (bf16[3088,128]{1,0:T(8,128)(2,1)S(1)}, bf16[3088,128]{1,0:T(8,128)(2,1)}, u32[]{:S(2)}, u32[]{:S(2)}) collective-permute-start(bf16[3088,128]{1,0:T(8,128)(2,1)S(1)} %add_select_fusion.2), channel_id=1, source_target_pairs={{0,1},{1,0},{2,3},{3,2},{4,5},{5,4},{6,7},{7,6},{8,9},{9,8},{10,11... | collective-permute-start | bytes 2371592 | tf_op jit(solution)/shard_map/ppermute | solution.py:297
  60.6 28.7 %collective-permute-start.16 = (bf16[3088,128]{1,0:T(8,128)(2,1)}, bf16[3088,128]{1,0:T(8,128)(2,1)}, u32[]{:S(2)}, u32[]{:S(2)}) collective-permute-start(bf16[3088,128]{1,0:T(8,128)(2,1)} %add_select_fusion.1), channel_id=1, source_target_pairs={{0,2},{2,0},{1,3},{3,1},{4,6},{6,4},{5,7},{7,5},{8,10},{10,8},{9,1... | collective-permute-start | bytes 2371592 | tf_op jit(solution)/shard_map/ppermute | solution.py:292
  76.2 33.5 %collective-permute-start.27 = (bf16[2,3088,128]{2,1,0:T(8,128)(2,1)}, bf16[2,3088,128]{2,1,0:T(8,128)(2,1)}, u32[]{:S(2)}, u32[]{:S(2)}) collective-permute-start(bf16[2,3088,128]{2,1,0:T(8,128)(2,1)} %collective-permute-done.26), channel_id=1, source_target_pairs={{9,1},{11,3},{13,5},{15,7}} | collective-permute-start | bytes 4743176 | tf_op jit(solution)/shard_map/ppermute | solution.py:303
  88.8 20.1 %collective-permute-start.7 = (bf16[3088,128]{1,0:T(8,128)(2,1)S(1)}, bf16[3088,128]{1,0:T(8,128)(2,1)}, u32[]{:S(2)}, u32[]{:S(2)}) collective-permute-start(bf16[3088,128]{1,0:T(8,128)(2,1)S(1)} %collective-permute-done.5), channel_id=1, source_target_pairs={{0,4},{4,0},{1,5},{5,1},{2,6},{6,2},{3,7},{7,3},{8,12},{12,8},{9,1... | collective-permute-start | bytes 2371592 | tf_op jit(solution)/shard_map/ppermute | solution.py:294
  89.3 19.6 %collective-permute-start.9 = (bf16[3088,128]{1,0:T(8,128)(2,1)S(1)}, bf16[3088,128]{1,0:T(8,128)(2,1)}, u32[]{:S(2)}, u32[]{:S(2)}) collective-permute-start(bf16[3088,128]{1,0:T(8,128)(2,1)S(1)} %collective-permute-done.5), channel_id=1, source_target_pairs={{0,1},{1,0},{2,3},{3,2},{4,5},{5,4},{6,7},{7,6},{8,9},{9,8},{10,11... | collective-permute-start | bytes 2371592 | tf_op jit(solution)/shard_map/ppermute | solution.py:297
  89.5 20.2 %collective-permute-start.18 = (bf16[3088,128]{1,0:T(8,128)(2,1)}, bf16[3088,128]{1,0:T(8,128)(2,1)}, u32[]{:S(2)}, u32[]{:S(2)}) collective-permute-start(bf16[3088,128]{1,0:T(8,128)(2,1)} %collective-permute-done.17), channel_id=1, source_target_pairs={{0,2},{2,0},{1,3},{3,1},{4,6},{6,4},{5,7},{7,5},{8,10},{10,8},{9,1... | collective-permute-start | bytes 2371592 | tf_op jit(solution)/shard_map/ppermute | solution.py:294
  92.8 25.9 %collective-permute-start.21 = (bf16[3088,128]{1,0:T(8,128)(2,1)}, bf16[3088,128]{1,0:T(8,128)(2,1)S(1)}, u32[]{:S(2)}, u32[]{:S(2)}) collective-permute-start(bf16[3088,128]{1,0:T(8,128)(2,1)} %collective-permute-done.17), channel_id=1, source_target_pairs={{0,1},{1,0},{2,3},{3,2},{4,5},{5,4},{6,7},{7,6},{8,9},{9,8},{10,11... | collective-permute-start | bytes 2371592 | tf_op jit(solution)/shard_map/ppermute | solution.py:297
  115.6 39.5 %collective-permute-start.28 = (bf16[2,3088,128]{2,1,0:T(8,128)(2,1)}, bf16[2,3088,128]{2,1,0:T(8,128)(2,1)}, u32[]{:S(2)}, u32[]{:S(2)}) collective-permute-start(bf16[2,3088,128]{2,1,0:T(8,128)(2,1)} %add_select_fusion.refs_1_.refs_6_.refs_18_), channel_id=1, source_target_pairs={{0,2},{2,0},{1,3},{3,1},{4,6},{6,4},{5,7},{7,5},{8,10},{10,8},{9,1... | collective-permute-start | bytes 4743176 | tf_op jit(solution)/shard_map/ppermute | solution.py:248
  117.2 40.4 %collective-permute-start.29 = (bf16[2,3088,128]{2,1,0:T(8,128)(2,1)}, bf16[2,3088,128]{2,1,0:T(8,128)(2,1)}, u32[]{:S(2)}, u32[]{:S(2)}) collective-permute-start(bf16[2,3088,128]{2,1,0:T(8,128)(2,1)} %add_select_fusion.refs_1_.refs_6_.refs_18_), channel_id=1, source_target_pairs={{0,4},{4,0},{1,5},{5,1},{2,6},{6,2},{3,7},{7,3},{8,12},{12,8},{9,1... | collective-permute-start | bytes 4743176 | tf_op jit(solution)/shard_map/ppermute | solution.py:248
  118.7 138.3 %collective-permute-start.35 = (bf16[2,3088,128]{2,1,0:T(8,128)(2,1)}, bf16[2,3088,128]{2,1,0:T(8,128)(2,1)}, u32[]{:S(2)}, u32[]{:S(2)}) collective-permute-start(bf16[2,3088,128]{2,1,0:T(8,128)(2,1)} %add_select_fusion.refs_1_.refs_6_.refs_18_), channel_id=1, source_target_pairs={{0,1},{1,0},{2,3},{3,2},{4,5},{5,4},{6,7},{7,6},{8,9},{9,8},{10,11... | collective-permute-start | bytes 4743176 | tf_op jit(solution)/shard_map/ppermute | solution.py:248
  157.4 20.4 %collective-permute-start.30 = (bf16[1,3088,128]{2,1,0:T(8,128)(2,1)}, bf16[1,3088,128]{2,1,0:T(8,128)(2,1)}, u32[]{:S(2)}, u32[]{:S(2)}) collective-permute-start(bf16[1,3088,128]{2,1,0:T(8,128)(2,1)} %slice.343.refs_6_), channel_id=1, source_target_pairs={{0,4},{4,0},{1,5},{5,1},{2,6},{6,2},{3,7},{7,3},{8,12},{12,8},{9,1... | collective-permute-start | bytes 2371592 | tf_op jit(solution)/shard_map/ppermute | solution.py:248
  159.6 19.8 %collective-permute-start.31 = (bf16[1,3088,128]{2,1,0:T(8,128)(2,1)}, bf16[1,3088,128]{2,1,0:T(8,128)(2,1)}, u32[]{:S(2)}, u32[]{:S(2)}) collective-permute-start(bf16[1,3088,128]{2,1,0:T(8,128)(2,1)} %slice.344.refs_7_), channel_id=1, source_target_pairs={{0,2},{2,0},{1,3},{3,1},{4,6},{6,4},{5,7},{7,5},{8,10},{10,8},{9,1... | collective-permute-start | bytes 2371592 | tf_op jit(solution)/shard_map/ppermute | solution.py:248
  194.5 62.6 %collective-permute-start.36 = (bf16[2,3088,128]{2,1,0:T(8,128)(2,1)}, bf16[2,3088,128]{2,1,0:T(8,128)(2,1)}, u32[]{:S(2)}, u32[]{:S(2)}) collective-permute-start(bf16[2,3088,128]{2,1,0:T(8,128)(2,1)} %collective-permute-done.28.refs_2_.refs_7_.refs_19_), channel_id=1, source_target_pairs={{0,1},{1,0},{2,3},{3,2},{4,5},{5,4},{6,7},{7,6},{8,9},{9,8},{10,11... | collective-permute-start | bytes 4743176 | tf_op jit(solution)/shard_map/ppermute | solution.py:248
  194.9 62.1 %collective-permute-start.37 = (bf16[2,3088,128]{2,1,0:T(8,128)(2,1)}, bf16[2,3088,128]{2,1,0:T(8,128)(2,1)}, u32[]{:S(2)}, u32[]{:S(2)}) collective-permute-start(bf16[2,3088,128]{2,1,0:T(8,128)(2,1)} %collective-permute-done.29.refs_3_.refs_8_.refs_20_), channel_id=1, source_target_pairs={{0,1},{1,0},{2,3},{3,2},{4,5},{5,4},{6,7},{7,6},{8,9},{9,8},{10,11... | collective-permute-start | bytes 4743176 | tf_op jit(solution)/shard_map/ppermute | solution.py:248
  195.0 62.1 %collective-permute-start.38 = (bf16[1,3088,128]{2,1,0:T(8,128)(2,1)}, bf16[1,3088,128]{2,1,0:T(8,128)(2,1)}, u32[]{:S(2)}, u32[]{:S(2)}) collective-permute-start(bf16[1,3088,128]{2,1,0:T(8,128)(2,1)} %collective-permute-done.30.refs_4_.refs_9_.refs_21_), channel_id=1, source_target_pairs={{0,1},{1,0},{2,3},{3,2},{4,5},{5,4},{6,7},{7,6},{8,9},{9,8},{10,11... | collective-permute-start | bytes 2371592 | tf_op jit(solution)/shard_map/ppermute | solution.py:248
  234.6 23.0 %collective-permute-start.39 = (bf16[1,3088,128]{2,1,0:T(8,128)(2,1)}, bf16[1,3088,128]{2,1,0:T(8,128)(2,1)}, u32[]{:S(2)}, u32[]{:S(2)}) collective-permute-start(bf16[1,3088,128]{2,1,0:T(8,128)(2,1)} %collective-permute-done.31.refs_5_.refs_10_.refs_22_), channel_id=1, source_target_pairs={{0,1},{1,0},{2,3},{3,2},{4,5},{5,4},{6,7},{7,6},{8,9},{9,8},{10,11... | collective-permute-start | bytes 2371592 | tf_op jit(solution)/shard_map/ppermute | solution.py:248
  385.9 34.5 %collective-permute-start.41 = (bf16[144,1536]{1,0:T(8,128)(2,1)}, bf16[144,1536]{1,0:T(8,128)(2,1)S(1)}, u32[]{:S(2)}, u32[]{:S(2)}) collective-permute-start(bf16[144,1536]{1,0:T(8,128)(2,1)} %concatenate.73.refs_7_), channel_id=1, source_target_pairs={{0,2},{2,0},{1,3},{3,1},{4,6},{6,4},{5,7},{7,5},{8,10},{10,8},{9,1... | collective-permute-start | bytes 1327112 | tf_op jit(solution)/shard_map/ppermute | solution.py:248
  436.6 43.9 %collective-permute-start.43 = (bf16[24688,128]{1,0:T(8,128)(2,1)}, bf16[24688,128]{1,0:T(8,128)(2,1)}, u32[]{:S(2)}, u32[]{:S(2)}) collective-permute-start(bf16[24688,128]{1,0:T(8,128)(2,1)} %constant_dynamic-slice_fusion.2.refs_2_), channel_id=1, source_target_pairs={{0,1},{1,0},{2,3},{3,2},{4,5},{5,4},{6,7},{7,6},{8,9},{9,8},{10,11... | collective-permute-start | bytes 18960392 | tf_op jit(solution)/shard_map/ppermute | solution.py:248
  439.8 39.5 %collective-permute-start.42 = (bf16[144,1536]{1,0:T(8,128)(2,1)}, bf16[144,1536]{1,0:T(8,128)(2,1)}, u32[]{:S(2)}, u32[]{:S(2)}) collective-permute-start(bf16[144,1536]{1,0:T(8,128)(2,1)} %concatenate.74.refs_1_), channel_id=1, source_target_pairs={{0,4},{4,0},{1,5},{5,1},{2,6},{6,2},{3,7},{7,3},{8,12},{12,8},{9,1... | collective-permute-start | bytes 1327112 | tf_op jit(solution)/shard_map/ppermute | solution.py:248
  489.8 74.8 %collective-permute-start.45 = (bf16[2,3104,128]{2,1,0:T(8,128)(2,1)}, bf16[2,3104,128]{2,1,0:T(8,128)(2,1)}, u32[]{:S(2)}, u32[]{:S(2)}) collective-permute-start(bf16[2,3104,128]{2,1,0:T(8,128)(2,1)} %pad_maximum_fusion.5.refs_12_.refs_2_), channel_id=1, source_target_pairs={{0,2},{2,0},{1,3},{3,1},{4,6},{6,4},{5,7},{7,5},{8,10},{10,8},{9,1... | collective-permute-start | bytes 4767752 | tf_op jit(solution)/shard_map/ppermute | solution.py:248
  496.5 26.4 %collective-permute-start.50 = (f32[4]{0:T(128)S(1)}, f32[4]{0:T(128)S(1)}, u32[]{:S(2)}, u32[]{:S(2)}) collective-permute-start(f32[4]{0:T(128)S(1)} %add.669.refs_7_.refs_8_), channel_id=1, source_target_pairs={{0,16},{16,0},{8,24},{24,8},{1,17},{17,1},{9,25},{25,9},{2,18},{18... | collective-permute-start | bytes 56 | tf_op jit(solution)/shard_map/ppermute | solution.py:248
  526.1 42.5 %collective-permute-start.44 = (bf16[2,3104,128]{2,1,0:T(8,128)(2,1)}, bf16[2,3104,128]{2,1,0:T(8,128)(2,1)}, u32[]{:S(2)}, u32[]{:S(2)}) collective-permute-start(bf16[2,3104,128]{2,1,0:T(8,128)(2,1)} %pad_maximum_fusion.4.refs_11_.refs_1_), channel_id=1, source_target_pairs={{0,4},{4,0},{1,5},{5,1},{2,6},{6,2},{3,7},{7,3},{8,12},{12,8},{9,1... | collective-permute-start | bytes 4767752 | tf_op jit(solution)/shard_map/ppermute | solution.py:248
  568.0 23.9 %collective-permute-start.47 = (bf16[3104,128]{1,0:T(8,128)(2,1)S(1)}, bf16[3104,128]{1,0:T(8,128)(2,1)}, u32[]{:S(2)}, u32[]{:S(2)}) collective-permute-start(bf16[3104,128]{1,0:T(8,128)(2,1)S(1)} %dynamic-slice_bitcast_fusion.11.refs_5_.refs_10_), channel_id=1, source_target_pairs={{0,4},{4,0},{1,5},{5,1},{2,6},{6,2},{3,7},{7,3},{8,12},{12,8},{9,1... | collective-permute-start | bytes 2383880 | tf_op jit(solution)/shard_map/ppermute | solution.py:248
  571.6 21.9 %collective-permute-start.46 = (bf16[3104,128]{1,0:T(8,128)(2,1)}, bf16[3104,128]{1,0:T(8,128)(2,1)}, u32[]{:S(2)}, u32[]{:S(2)}) collective-permute-start(bf16[3104,128]{1,0:T(8,128)(2,1)} %dynamic-slice_bitcast_fusion.14.refs_4_.refs_9_), channel_id=1, source_target_pairs={{0,2},{2,0},{1,3},{3,1},{4,6},{6,4},{5,7},{7,5},{8,10},{10,8},{9,1... | collective-permute-start | bytes 2383880 | tf_op jit(solution)/shard_map/ppermute | solution.py:248
  622.0 28.5 %collective-permute-start.51 = (bf16[24688,128]{1,0:T(8,128)(2,1)}, bf16[24688,128]{1,0:T(8,128)(2,1)}, u32[]{:S(2)}, u32[]{:S(2)}) collective-permute-start(bf16[24688,128]{1,0:T(8,128)(2,1)} %constant_dynamic-slice_fusion.1.refs_1_), channel_id=1, source_target_pairs={{0,1},{1,0},{2,3},{3,2},{4,5},{5,4},{6,7},{7,6},{8,9},{9,8},{10,11... | collective-permute-start | bytes 18960392 | tf_op jit(solution)/shard_map/ppermute | solution.py:248
  633.4 96.5 %collective-permute-start.55 = (bf16[2,3104,128]{2,1,0:T(8,128)(2,1)}, bf16[2,3104,128]{2,1,0:T(8,128)(2,1)}, u32[]{:S(2)}, u32[]{:S(2)}) collective-permute-start(bf16[2,3104,128]{2,1,0:T(8,128)(2,1)} %pad_maximum_fusion.6.refs_4_.refs_5_.refs_6_.refs_9_.refs_10_.refs_11_.refs_2_.refs_3_), channel_id=1, source_target_pairs={{8,16},{17,25},{10,18},{19,27},{12,20},{21,29},{14,22},{23,31}} | collective-permute-start | bytes 4767752 | tf_op jit(solution)/shard_map/ppermute | solution.py:248
  635.4 95.8 %collective-permute-start.56 = (bf16[2,3104,128]{2,1,0:T(8,128)(2,1)}, bf16[2,3104,128]{2,1,0:T(8,128)(2,1)}, u32[]{:S(2)}, u32[]{:S(2)}) collective-permute-start(bf16[2,3104,128]{2,1,0:T(8,128)(2,1)} %pad_maximum_fusion.6.refs_4_.refs_5_.refs_6_.refs_9_.refs_10_.refs_11_.refs_2_.refs_3_), channel_id=1, source_target_pairs={{0,16},{9,25},{2,18},{11,27},{4,20},{13,29},{6,22},{15,31}} | collective-permute-start | bytes 4767752 | tf_op jit(solution)/shard_map/ppermute | solution.py:248
  638.5 94.1 %collective-permute-start.57 = (bf16[2,3104,128]{2,1,0:T(8,128)(2,1)}, bf16[2,3104,128]{2,1,0:T(8,128)(2,1)}, u32[]{:S(2)}, u32[]{:S(2)}) collective-permute-start(bf16[2,3104,128]{2,1,0:T(8,128)(2,1)} %pad_maximum_fusion.6.refs_4_.refs_5_.refs_6_.refs_9_.refs_10_.refs_11_.refs_2_.refs_3_), channel_id=1, source_target_pairs={{24,16},{1,25},{26,18},{3,27},{28,20},{5,29},{30,22},{7,31}} | collective-permute-start | bytes 4767752 | tf_op jit(solution)/shard_map/ppermute | solution.py:248
  659.5 37.0 %collective-permute-start.52 = (bf16[2,3104,128]{2,1,0:T(8,128)(2,1)}, bf16[2,3104,128]{2,1,0:T(8,128)(2,1)}, u32[]{:S(2)}, u32[]{:S(2)}) collective-permute-start(bf16[2,3104,128]{2,1,0:T(8,128)(2,1)} %pad_maximum_fusion.7.refs_1_.refs_7_), channel_id=1, source_target_pairs={{0,4},{4,0},{1,5},{5,1},{2,6},{6,2},{3,7},{7,3},{8,12},{12,8},{9,1... | collective-permute-start | bytes 4767752 | tf_op jit(solution)/shard_map/ppermute | solution.py:248
  662.2 37.4 %collective-permute-start.53 = (bf16[2,3104,128]{2,1,0:T(8,128)(2,1)}, bf16[2,3104,128]{2,1,0:T(8,128)(2,1)}, u32[]{:S(2)}, u32[]{:S(2)}) collective-permute-start(bf16[2,3104,128]{2,1,0:T(8,128)(2,1)} %pad_maximum_fusion.8.refs_2_.refs_8_), channel_id=1, source_target_pairs={{0,2},{2,0},{1,3},{3,1},{4,6},{6,4},{5,7},{7,5},{8,10},{10,8},{9,1... | collective-permute-start | bytes 4767752 | tf_op jit(solution)/shard_map/ppermute | solution.py:248
  702.7 19.7 %collective-permute-start.54 = (bf16[3104,128]{1,0:T(8,128)(2,1)}, bf16[3104,128]{1,0:T(8,128)(2,1)}, u32[]{:S(2)}, u32[]{:S(2)}) collective-permute-start(bf16[3104,128]{1,0:T(8,128)(2,1)} %dynamic-slice_bitcast_fusion.4.refs_2_.refs_7_), channel_id=1, source_target_pairs={{0,2},{2,0},{1,3},{3,1},{4,6},{6,4},{5,7},{7,5},{8,10},{10,8},{9,1... | collective-permute-start | bytes 2383880 | tf_op jit(solution)/shard_map/ppermute | solution.py:248
  705.0 35.1 %collective-permute-start.59 = (bf16[3104,128]{1,0:T(8,128)(2,1)S(1)}, bf16[3104,128]{1,0:T(8,128)(2,1)}, u32[]{:S(2)}, u32[]{:S(2)}) collective-permute-start(bf16[3104,128]{1,0:T(8,128)(2,1)S(1)} %dynamic-slice_bitcast_fusion.1.refs_3_.refs_8_), channel_id=1, source_target_pairs={{0,4},{4,0},{1,5},{5,1},{2,6},{6,2},{3,7},{7,3},{8,12},{12,8},{9,1... | collective-permute-start | bytes 2383880 | tf_op jit(solution)/shard_map/ppermute | solution.py:248
  724.6 35.5 %collective-permute-start.62 = (bf16[3104,128]{1,0:T(8,128)(2,1)}, bf16[3104,128]{1,0:T(8,128)(2,1)}, u32[]{:S(2)}, u32[]{:S(2)}) collective-permute-start(bf16[3104,128]{1,0:T(8,128)(2,1)} %fusion.20.refs_2_.refs_3_.refs_4_), channel_id=1, source_target_pairs={{24,0},{1,9},{26,2},{3,11},{28,4},{5,13},{30,6},{7,15}} | collective-permute-start | bytes 2383880 | tf_op jit(solution)/shard_map/ppermute | solution.py:248
  729.9 36.5 %collective-permute-start.61 = (bf16[3104,128]{1,0:T(8,128)(2,1)}, bf16[3104,128]{1,0:T(8,128)(2,1)}, u32[]{:S(2)}, u32[]{:S(2)}) collective-permute-start(bf16[3104,128]{1,0:T(8,128)(2,1)} %fusion.20.refs_2_.refs_3_.refs_4_), channel_id=1, source_target_pairs={{16,0},{25,9},{18,2},{27,11},{20,4},{29,13},{22,6},{31,15}} | collective-permute-start | bytes 2383880 | tf_op jit(solution)/shard_map/ppermute | solution.py:248
  731.2 35.2 %collective-permute-start.60 = (bf16[3104,128]{1,0:T(8,128)(2,1)}, bf16[3104,128]{1,0:T(8,128)(2,1)}, u32[]{:S(2)}, u32[]{:S(2)}) collective-permute-start(bf16[3104,128]{1,0:T(8,128)(2,1)} %fusion.20.refs_2_.refs_3_.refs_4_), channel_id=1, source_target_pairs={{8,0},{17,9},{10,2},{19,11},{12,4},{21,13},{14,6},{23,15}} | collective-permute-start | bytes 2383880 | tf_op jit(solution)/shard_map/ppermute | solution.py:248
  748.6 23.7 %collective-permute-start.63 = (bf16[2,2,512,128]{3,2,1,0:T(8,128)(2,1)S(1)}, bf16[2,2,512,128]{3,2,1,0:T(8,128)(2,1)}, u32[]{:S(2)}, u32[]{:S(2)}) collective-permute-start(bf16[2,2,512,128]{3,2,1,0:T(8,128)(2,1)S(1)} %dynamic-slice_bitcast_fusion.21.refs_1_), channel_id=1, source_target_pairs={{0,4},{4,0},{1,5},{5,1},{2,6},{6,2},{3,7},{7,3},{8,12},{12,8},{9,1... | collective-permute-start | bytes 1572872 | tf_op jit(solution)/shard_map/ppermute | solution.py:248
  801.3 23.1 %collective-permute-start.72 = (bf16[3104,128]{1,0:T(8,128)(2,1)S(1)}, bf16[3104,128]{1,0:T(8,128)(2,1)S(1)}, u32[]{:S(2)}, u32[]{:S(2)}) collective-permute-start(bf16[3104,128]{1,0:T(8,128)(2,1)S(1)} %copy-done.3), channel_id=1, source_target_pairs={{24,0},{1,9},{26,2},{3,11},{28,4},{5,13},{30,6},{7,15}} | collective-permute-start | bytes 2383880 | tf_op jit(solution)/shard_map/ppermute | solution.py:248
  802.7 40.7 %collective-permute-start.71 = (bf16[3104,128]{1,0:T(8,128)(2,1)S(1)}, bf16[3104,128]{1,0:T(8,128)(2,1)S(1)}, u32[]{:S(2)}, u32[]{:S(2)}) collective-permute-start(bf16[3104,128]{1,0:T(8,128)(2,1)S(1)} %copy-done.3), channel_id=1, source_target_pairs={{16,0},{25,9},{18,2},{27,11},{20,4},{29,13},{22,6},{31,15}} | collective-permute-start | bytes 2383880 | tf_op jit(solution)/shard_map/ppermute | solution.py:248
  804.0 39.4 %collective-permute-start.70 = (bf16[3104,128]{1,0:T(8,128)(2,1)S(1)}, bf16[3104,128]{1,0:T(8,128)(2,1)S(1)}, u32[]{:S(2)}, u32[]{:S(2)}) collective-permute-start(bf16[3104,128]{1,0:T(8,128)(2,1)S(1)} %copy-done.3), channel_id=1, source_target_pairs={{8,0},{17,9},{10,2},{19,11},{12,4},{21,13},{14,6},{23,15}} | collective-permute-start | bytes 2383880 | tf_op jit(solution)/shard_map/ppermute | solution.py:248
  806.8 40.2 %collective-permute-start.68 = (bf16[2,400,128]{2,1,0:T(8,128)(2,1)S(1)}, bf16[2,400,128]{2,1,0:T(8,128)(2,1)S(1)}, u32[]{:S(2)}, u32[]{:S(2)}) collective-permute-start(bf16[2,400,128]{2,1,0:T(8,128)(2,1)S(1)} %dynamic-slice_bitcast_fusion.23), channel_id=1, source_target_pairs={{0,4},{4,0},{1,5},{5,1},{2,6},{6,2},{3,7},{7,3},{8,12},{12,8},{9,1... | collective-permute-start | bytes 614408 | tf_op jit(solution)/shard_map/ppermute | solution.py:248
  864.1 28.0 %collective-permute-start.81 = (bf16[3104,128]{1,0:T(8,128)(2,1)}, bf16[3104,128]{1,0:T(8,128)(2,1)S(1)}, u32[]{:S(2)}, u32[]{:S(2)}) collective-permute-start(bf16[3104,128]{1,0:T(8,128)(2,1)} %get-tuple-element.168.refs_5_), channel_id=1, source_target_pairs={{0,1},{9,8},{16,17},{25,24},{2,3},{11,10},{18,19},{27,26},{4,5},{1... | collective-permute-start | bytes 2383880 | tf_op jit(solution)/shard_map/ppermute | solution.py:248
  865.4 26.7 %collective-permute-start.80 = (bf16[3104,128]{1,0:T(8,128)(2,1)}, bf16[3104,128]{1,0:T(8,128)(2,1)S(1)}, u32[]{:S(2)}, u32[]{:S(2)}) collective-permute-start(bf16[3104,128]{1,0:T(8,128)(2,1)} %get-tuple-element.124.refs_1_), channel_id=1, source_target_pairs={{0,1},{9,8},{16,17},{25,24},{2,3},{11,10},{18,19},{27,26},{4,5},{1... | collective-permute-start | bytes 2383880 | tf_op jit(solution)/shard_map/ppermute | solution.py:248
  (234 other events, 2480.7 us)
Sparse Core Ops, SparseCore 0:
  166.5 51.7 all-gather.2

commit v10 on v9

--- a/solution.py
+++ b/solution.py
@@ -1151,18 +1151,16 @@
     start = None
     for name in ("c", "x", "y"):
         place = lax.axis_index(name)
-        rows = [total[1], total[0]]
-        if extra is None:
-            rows.append(jnp.zeros((15, INNER), jnp.float32))
-        else:
-            rest = extra
-            for _ in range(3):
+        at = lax.broadcasted_iota(jnp.int32, (16, INNER), 0)
+        block = jnp.where(at == 0, total[0], 0.0)
+        if extra is not None:
+            rest = jnp.pad(extra, (0, INNER - extra.shape[0]))[None, :]
+            for place_at in range(1, 4):
                 term = lax.reduce_precision(rest, 8, 7)
-                rows.append(jnp.pad(term, (0, INNER - term.shape[0]))[None, :])
+                block = jnp.where(at == place_at, term, block)
                 rest = rest - term
-            rows.append(jnp.zeros((12, INNER), jnp.float32))
-        packed = jnp.concatenate(rows, axis=0)
-        (packed,) = yield [(packed.astype(jnp.bfloat16), name, SWAP)]
+        packed = jnp.concatenate([total[1].astype(jnp.bfloat16), block.astype(jnp.bfloat16)], axis=0)
+        (packed,) = yield [(packed, name, SWAP)]
         packed = packed.astype(jnp.float32)
         other = (packed[STATE : STATE + 1], packed[:STATE])
         if extra is not None:
@@ -1537,7 +1535,7 @@
     )
     if fast:
         key_blocks = lax.all_gather(kv_local, span)
-        (conv_values,) = bracket(convolve, [spread_flow])
+        conv_values = convolve(())
     else:
         conv_values = convolve(())
     step_in = step_raw.T + small_f32[STEP_BIAS][:, None]
@@ -1562,7 +1560,7 @@
     q_wide = jnp.pad(q_rot * jnp.bfloat16(score_scale), ((0, 0), (0, HEAD_DIM), (0, 0)))
     start_row = jnp.broadcast_to(row_starts[None, :], (8, rows_dev))
     if fast:
-        local_state = summarize(())
+        (local_state,) = bracket(summarize, [spread_flow])
         scan = Flow(scan_stages(carry_all, local_state, False))
         (gate_in,) = fence([hidden], scan.values())
         gate_ssm = matmul(gate_in, weights[W_GATE_SSM])

time: 917 us -> 882 us (0.962)
  local copies, waits for them, and re-layouts: 119 us -> 86.3 us
    concatenate x4 -> x0, local copies, waits for them, and re-layouts: 16.4 us -> none  [scan_stages(): packed = jnp.concatenate(rows, axis=0)]
    unnamed x403 -> x371, local copies, waits for them, and re-layouts: 42.5 us -> 32.6 us
    another operation x21 -> x8, other arithmetic: 15.6 us -> 6.16 us
  transfers between devices with their start and end apart: 83 -> 83, of which waited for: 27 -> 25; matrix products, arithmetic and copies ran while one was open for 20% -> 20% of each run, Pallas kernels for 16% -> 17%
where the time goes in v10:
time: 882 us; the launch traced here: 869 us
  Pallas kernels  207 us (23%)
  starting transfers between devices  185 us (21%)
  waiting for transfers between devices  151 us (17%)
  other arithmetic  143 us (16%)
  local copies, waits for them, and re-layouts  86.3 us (10%)
  matrix products  79 us (9%)
  between operations  18.6 us (2%)
    ppermute x53, starting transfers between devices, go(): lax.ppermute(value, axis, pairs)  141 us
    ppermute x53, waiting for transfers between devices, go(): lax.ppermute(value, axis, pairs)  108 us
    pallas_call x2, Pallas kernels, unpack_lines(): pl.pallas_call(pinned(kernel, 2 + count_buffers, after), grid_spec=pltpu....  48.5 us
    dot_general x12, matrix products, matmul_right_t(): lax.dot_general(left, right, (((1,), (1,)), ((), ())), preferred_element_...  46.9 us
    pallas_call x4, Pallas kernels, pack_lines(): pl.pallas_call(pinned(kernel, inputs, after), grid=(total,), in_specs=[le...  42.8 us
    pallas_call x1, Pallas kernels, ssm_backward(): pl.pallas_call(pinned(kernel, 11, after), grid_spec=pltpu.PrefetchScalarG...  33.2 us
    convert_element_type x14, other arithmetic, added(): return total.astype(jnp.bfloat16)  32.9 us
    unnamed x371, local copies, waits for them, and re-layouts  32.6 us
  transfers between devices with their start and end apart: 83, of which 25 were waited for; matrix products, arithmetic and copies ran while one was open for 20% of the time, Pallas kernels for 17%

profile of v10, /device:TPU:0, one launch (start us, length us, event | category | flops | bytes accessed | tf_op | source)
XLA Modules:
  0.0 868.6 jit_solution(75545789061379987)
XLA Ops:
  13.1 5.4 collective-permute-start.1
  19.9 7.3 collective-permute-done.1
  50.1 9.1 %collective-permute-start.8 = (bf16[3088,128]{1,0:T(8,128)(2,1)S(1)}, bf16[3088,128]{1,0:T(8,128)(2,1)}, u32[]{:S(2)}, u32[]{:S(2)}) collective-permute-start(bf16[3088,128]{1,0:T(8,128)(2,1)S(1)} %add_select_fusion.2), channel_id=1, source_target_pairs={{0,1},{1,0},{2,3},{3,2},{4,5},{5,4},{6,7},{7,6},{8,9},{9,8},{10,11... | collective-permute-start | bytes 2371592 | tf_op jit(solution)/shard_map/ppermute | solution.py:297
  63.6 12.5 %collective-permute-done.26 = bf16[2,3088,128]{2,1,0:T(8,128)(2,1)} collective-permute-done((bf16[2,3088,128]{2,1,0:T(8,128)(2,1)}, bf16[2,3088,128]{2,1,0:T(8,128)(2,1)}, u32[]{:S(2)}, u32[]{:S(2)}) %collective-permute-start.26) | collective-permute-done | bytes 1581088 | tf_op jit(solution)/shard_map/ppermute | solution.py:302
  94.1 15.4 %collective-permute-done.7 = bf16[3088,128]{1,0:T(8,128)(2,1)} collective-permute-done((bf16[3088,128]{1,0:T(8,128)(2,1)S(1)}, bf16[3088,128]{1,0:T(8,128)(2,1)}, u32[]{:S(2)}, u32[]{:S(2)}) %collective-permute-start.7) | collective-permute-done | bytes 790560 | tf_op jit(solution)/shard_map/ppermute | solution.py:294
  110.7 5.3 add_select_fusion.refs_1_.refs_6_.refs_18_
  120.5 14.4 %unpack.2 = (bf16[1024,512]{1,0:T(8,128)(2,1)}, bf16[1024,128]{1,0:T(8,128)(2,1)S(1)}, bf16[1024,128]{1,0:T(8,128)(2,1)S(1)}, bf16[512,1024]{1,0:T(8,128)(2,1)},...) custom-call(s32[25,5]{1,0:T(8,128)S(1)} %copy-done.55, ...), custom_call_target="tpu_custom_call" | custom-call | bytes 26624000 | tf_op jit(solution)/shard_map/unpack/pallas_call | solution.py:454
  163.8 11.3 %conv.1.refs_0_.refs_1_.x_ref.b_ref.c_ref.refs_3_.refs_4_ = f32[512,1792]{1,0:T(8,128)} custom-call(s32[5]{0:T(128)} %pad_add_fusion.1.refs_0_.meta_ref, f32[512,1792]{1,0:T(8,128)} %pad_maximum_fusion.refs_1_.refs_4_, f32[8,1792]{1,0:T(8,128)} %collective-permute-done.23.refs_2_.refs_5_, f32[4,1792]{1,0:T(4,128)} %reshape.435.refs_3_.refs_6_, ...), custom_call_target="tpu_custom_call" | custom-call | flops 1000000000 | bytes 7340032 | tf_op jit(solution)/shard_map/conv/pallas_call | solution.py:759
  175.1 8.8 %state.2.refs_0_ = f32[128,1536]{1,0:T(8,128)} custom-call(f32[512,1792]{1,0:T(8,128)} %conv.1.refs_0_.refs_1_.x_ref.b_ref.c_ref.refs_3_.refs_4_, f32[512,1792]{1,0:T(8,128)} %conv.1.refs_0_.refs_1_.x_ref.b_ref.c_ref.refs_3_.refs_4_, f32[12,2,512]{2,1,0:T(2,128)} %reshape.412.refs_2_, bf16[1,3088,128]{2,1,0:T(8,128)(2,1)} %slice.346.refs_3_, ...), custom_call_target="tpu_custom_call" | custom-call | flops 201326592 | bytes 3145728 | tf_op jit(solution)/shard_map/state/pallas_call | solution.py:871
  198.2 12.3 %collective-permute-done.33 = bf16[144,1536]{1,0:T(8,128)(2,1)} collective-permute-done((bf16[144,1536]{1,0:T(8,128)(2,1)S(1)}, bf16[144,1536]{1,0:T(8,128)(2,1)}, u32[]{:S(2)}, u32[]{:S(2)}) %collective-permute-start.33) | collective-permute-done | bytes 442400 | tf_op jit(solution)/shard_map/ppermute | solution.py:248
  214.6 14.6 %attend.1 = (f32[8,64,512]{2,1,0:T(8,128)S(1)}, f32[8,8,512]{2,1,0:T(8,128)S(1)}) custom-call(s32[4]{0:T(128)S(1)} %pad_add_fusion.refs_0_, bf16[8,128,512]{2,1,0:T(8,128)(2,1)S(1)} %pad.33.refs_1_, bf16[8,2,512,128]{3,2,1,0:T(8,128)(2,1)} %bitcast.333, s32[8,512]{1,0:T(8,128)S(1)} %broadcast_in_dim.286.refs_3_.row_ref.refs_10_.refs_6_, ...), custom_call_target="tpu_custom_call" | custom-call | flops 20000000000 | bytes 8388608 | tf_op jit(solution)/shard_map/attend/pallas_call | solution.py:1240
  230.8 5.3 collective-permute-start.39
  242.4 8.5 ssm.1.refs_28_
  253.4 34.1 %unpack.3 = (bf16[1536,1024]{1,0:T(8,128)(2,1)}, bf16[1024,2048]{1,0:T(8,128)(2,1)}, bf16[1024,2048]{1,0:T(8,128)(2,1)}, bf16[2048,1024]{1,0:T(8,128)(2,1)}, bf16[16,128]{1,0:T(8,128)(2,1)S(1)}) custom-call(s32[31,5]{1,0:T(8,128)S(1)} %copy-done.54, s32[32]{0:T(128)S(1)} %fusion.78.refs_1_, bf16[1,3088,128]{2,1,0:T(8,128)(2,1)S(1)} %bitcast.267, ...), custom_call_target="tpu_custom_call" | custom-call | bytes 33013760 | tf_op jit(solution)/shard_map/unpack/pallas_call | solution.py:454
  303.0 6.7 fusion.2
  309.7 6.9 fusion.104
  319.0 4.7 multiply_reduce_fusion.3
  336.5 8.8 %state.3 = f32[128,1536]{1,0:T(8,128)} custom-call(f32[512,1792]{1,0:T(8,128)} %conv.1.refs_0_.refs_1_.x_ref.b_ref.c_ref.refs_3_.refs_4_, f32[512,1536]{1,0:T(8,128)} %get-tuple-element.139.refs_1_.refs_2_, f32[12,2,512]{2,1,0:T(2,128)} %reshape.417.refs_2_), custom_call_target="tpu_custom_call" | custom-call | flops 201326592 | bytes 3145728 | tf_op jit(solution)/shard_map/state/pallas_call | solution.py:871
  356.8 6.4 pad_maximum_fusion.1
  367.9 7.6 collective-permute-start.41
  375.5 20.5 %pack.4.refs_0_ = bf16[49344,128]{1,0:T(8,128)(2,1)} custom-call(bf16[512,1024]{1,0:T(8,128)(2,1)S(1)} %copy-done.41, bf16[512,2048]{1,0:T(8,128)(2,1)S(1)} %copy-done.62, bf16[512,2048]{1,0:T(8,128)(2,1)} %get-tuple-element.211.refs_2_, bf16[512,2048]{1,0:T(8,128)(2,1)} %get-tuple-element.212.refs_3_, bf16[512,1024]{1,0:T(8,128)(2,1)S(1)} %copy-done.39, ...), custom_call_target="tpu_custom_call" | custom-call | flops 6442450944 | bytes 16777216 | tf_op jit(solution)/shard_map/pack/pallas_call | solution.py:609
  400.7 5.9 constant_dynamic-slice_fusion.2.refs_2_
  409.8 27.6 %collective-permute-start.42 = (bf16[144,1536]{1,0:T(8,128)(2,1)}, bf16[144,1536]{1,0:T(8,128)(2,1)}, u32[]{:S(2)}, u32[]{:S(2)}) collective-permute-start(bf16[144,1536]{1,0:T(8,128)(2,1)} %pad_maximum_fusion.19.refs_1_), channel_id=1, source_target_pairs={{0,4},{4,0},{1,5},{5,1},{2,6},{6,2},{3,7},{7,3},{8,12},{12,8},{9,1... | collective-permute-start | bytes 1327112 | tf_op jit(solution)/shard_map/ppermute | solution.py:248
  440.5 4.8 pack.5.refs_0_
  449.5 5.8 add_convert_fusion.1
  459.0 7.5 collective-permute-start.48
  468.0 17.3 %collective-permute-start.50 = (f32[4]{0:T(128)S(1)}, f32[4]{0:T(128)S(1)}, u32[]{:S(2)}, u32[]{:S(2)}) collective-permute-start(f32[4]{0:T(128)S(1)} %add.657.refs_7_.refs_8_), channel_id=1, source_target_pairs={{0,16},{16,0},{8,24},{24,8},{1,17},{17,1},{9,25},{25,9},{2,18},{18... | collective-permute-start | bytes 56 | tf_op jit(solution)/shard_map/ppermute | solution.py:248
  494.3 33.2 %ssm_back.1 = (f32[512,1536]{1,0:T(8,128)S(1)}, f32[512,128]{1,0:T(8,128)S(1)}, f32[512,128]{1,0:T(8,128)S(1)}, f32[12,8,512]{2,1,0:T(8,128)S(1)}) custom-call(s32[5]{0:T(128)S(1)} %copy-done.56, f32[512,1792]{1,0:T(8,128)} %conv.1.refs_0_.refs_1_.x_ref.b_ref.c_ref.refs_3_.refs_4_, f32[512,1536]{1,0:T(8,128)S(1)} %copy-done.6, ...), custom_call_target="tpu_custom_call" | custom-call | flops 3000000000 | bytes 9437184 | tf_op jit(solution)/shard_map/ssm_back/pallas_call | solution.py:1088
  543.1 14.7 %conv_back.1 = (bf16[512,1792]{1,0:T(8,128)(2,1)}, f32[16,1792]{1,0:T(8,128)}, f32[8,1792]{1,0:T(8,128)}, f32[8,1792]{1,0:T(8,128)}) custom-call(s32[5]{0:T(128)} %pad_add_fusion.1.refs_0_.meta_ref, f32[512,1536]{1,0:T(8,128)} %get-tuple-element.82.refs_1_, f32[512,128]{1,0:T(8,128)} %get-tuple-element.83.refs_2_, f32[512,128]{1,0:T(8,128)} %get-tuple-element.84.refs_3_, ...), custom_call_target="tpu_custom_call" | custom-call | flops 2000000000 | bytes 9175040 | tf_op jit(solution)/shard_map/conv_back/pallas_call | solution.py:818
  570.6 12.1 %pack.6.refs_0_ = bf16[49440,128]{1,0:T(8,128)(2,1)} custom-call(bf16[512,512]{1,0:T(8,128)(2,1)S(1)} %bitcast.274, bf16[512,1024]{1,0:T(8,128)(2,1)S(1)} %copy-done.2, bf16[512,1024]{1,0:T(8,128)(2,1)S(1)} %fusion.87.refs_2_, bf16[512,1536]{1,0:T(8,128)(2,1)S(1)} %copy-done.12, ...), custom_call_target="tpu_custom_call", output_to_operand_aliasing={{}: (7, {})} | custom-call | flops 4026531840 | bytes 11010048 | tf_op jit(solution)/shard_map/pack/pallas_call | solution.py:609
  582.8 6.0 constant_dynamic-slice_fusion.1.refs_1_
  593.3 5.1 fusion.105
  612.2 5.1 fusion.85
  617.4 5.8 add_convert_fusion
  631.9 7.6 attend_back.2
  639.5 24.0 %collective-permute-done.52 = bf16[2,3104,128]{2,1,0:T(8,128)(2,1)} collective-permute-done((bf16[2,3104,128]{2,1,0:T(8,128)(2,1)}, bf16[2,3104,128]{2,1,0:T(8,128)(2,1)}, u32[]{:S(2)}, u32[]{:S(2)}) %collective-permute-start.52) | collective-permute-done | bytes 1589280 | tf_op jit(solution)/shard_map/ppermute | solution.py:248
  675.5 8.2 attend_back.3
  715.6 11.4 %collective-permute-start.63 = (bf16[2,2,512,128]{3,2,1,0:T(8,128)(2,1)S(1)}, bf16[2,2,512,128]{3,2,1,0:T(8,128)(2,1)}, u32[]{:S(2)}, u32[]{:S(2)}) collective-permute-start(bf16[2,2,512,128]{3,2,1,0:T(8,128)(2,1)S(1)} %dynamic-slice_bitcast_fusion.21.refs_1_), channel_id=1, source_target_pairs={{0,4},{4,0},{1,5},{5,1},{2,6},{6,2},{3,7},{7,3},{8,12},{12,8},{9,1... | collective-permute-start | bytes 1572872 | tf_op jit(solution)/shard_map/ppermute | solution.py:248
  727.0 6.2 collective-permute-done.61
  740.4 5.9 collective-permute-start.64
  746.4 5.6 add_add_fusion.4.refs_0_
  756.0 5.4 fusion.12
  761.4 5.4 pack.7
  773.6 4.8 collective-permute-start.68
  778.4 12.9 %collective-permute-done.72 = bf16[3104,128]{1,0:T(8,128)(2,1)S(1)} collective-permute-done((bf16[3104,128]{1,0:T(8,128)(2,1)S(1)}, bf16[3104,128]{1,0:T(8,128)(2,1)S(1)}, u32[]{:S(2)}, u32[]{:S(2)}) %collective-permute-start.72) | collective-permute-done | bytes 794656 | tf_op jit(solution)/shard_map/ppermute | solution.py:248
  791.3 19.1 %collective-permute-done.71 = bf16[3104,128]{1,0:T(8,128)(2,1)S(1)} collective-permute-done((bf16[3104,128]{1,0:T(8,128)(2,1)S(1)}, bf16[3104,128]{1,0:T(8,128)(2,1)S(1)}, u32[]{:S(2)}, u32[]{:S(2)}) %collective-permute-start.71) | collective-permute-done | bytes 794656 | tf_op jit(solution)/shard_map/ppermute | solution.py:248
  818.0 5.3 collective-permute-start.67
  852.7 4.8 fusion.14
  (776 shorter events, 346.9 us)
Async XLA Ops:
  7.2 207.3 %all-gather.3.cloned.1.call-start = ((), (), s32[]{:S(2)}) async-start(), calls=%async_computation | async-start | bytes 2359296 | tf_op jit(solution)/shard_map/all_gather | solution.py:1537
  42.0 20.0 %collective-permute-start.25 = (bf16[2,3088,128]{2,1,0:T(8,128)(2,1)}, bf16[2,3088,128]{2,1,0:T(8,128)(2,1)S(1)}, u32[]{:S(2)}, u32[]{:S(2)}) collective-permute-start(bf16[2,3088,128]{2,1,0:T(8,128)(2,1)} %maximum_select_fusion), channel_id=1, source_target_pairs={{16,24},{18,26},{20,28},{22,30}} | collective-permute-start | bytes 4743176 | tf_op jit(solution)/shard_map/ppermute | solution.py:301
  43.5 32.6 %collective-permute-start.26 = (bf16[2,3088,128]{2,1,0:T(8,128)(2,1)}, bf16[2,3088,128]{2,1,0:T(8,128)(2,1)}, u32[]{:S(2)}, u32[]{:S(2)}) collective-permute-start(bf16[2,3088,128]{2,1,0:T(8,128)(2,1)} %collective-permute-done.24), channel_id=1, source_target_pairs={{8,0},{17,9},{10,2},{19,11},{12,4},{21,13},{14,6},{23,15}} | collective-permute-start | bytes 4743176 | tf_op jit(solution)/shard_map/ppermute | solution.py:302
  47.0 30.7 %collective-permute-start.5 = (bf16[3088,128]{1,0:T(8,128)(2,1)S(1)}, bf16[3088,128]{1,0:T(8,128)(2,1)S(1)}, u32[]{:S(2)}, u32[]{:S(2)}) collective-permute-start(bf16[3088,128]{1,0:T(8,128)(2,1)S(1)} %add_select_fusion.2), channel_id=1, source_target_pairs={{0,2},{2,0},{1,3},{3,1},{4,6},{6,4},{5,7},{7,5},{8,10},{10,8},{9,1... | collective-permute-start | bytes 2371592 | tf_op jit(solution)/shard_map/ppermute | solution.py:292
  48.5 40.6 %collective-permute-start.6 = (bf16[3088,128]{1,0:T(8,128)(2,1)S(1)}, bf16[3088,128]{1,0:T(8,128)(2,1)S(1)}, u32[]{:S(2)}, u32[]{:S(2)}) collective-permute-start(bf16[3088,128]{1,0:T(8,128)(2,1)S(1)} %add_select_fusion.2), channel_id=1, source_target_pairs={{0,4},{4,0},{1,5},{5,1},{2,6},{6,2},{3,7},{7,3},{8,12},{12,8},{9,1... | collective-permute-start | bytes 2371592 | tf_op jit(solution)/shard_map/ppermute | solution.py:293
  50.1 39.2 %collective-permute-start.8 = (bf16[3088,128]{1,0:T(8,128)(2,1)S(1)}, bf16[3088,128]{1,0:T(8,128)(2,1)}, u32[]{:S(2)}, u32[]{:S(2)}) collective-permute-start(bf16[3088,128]{1,0:T(8,128)(2,1)S(1)} %add_select_fusion.2), channel_id=1, source_target_pairs={{0,1},{1,0},{2,3},{3,2},{4,5},{5,4},{6,7},{7,6},{8,9},{9,8},{10,11... | collective-permute-start | bytes 2371592 | tf_op jit(solution)/shard_map/ppermute | solution.py:297
  62.0 27.8 %collective-permute-start.16 = (bf16[3088,128]{1,0:T(8,128)(2,1)}, bf16[3088,128]{1,0:T(8,128)(2,1)}, u32[]{:S(2)}, u32[]{:S(2)}) collective-permute-start(bf16[3088,128]{1,0:T(8,128)(2,1)} %add_select_fusion.1), channel_id=1, source_target_pairs={{0,2},{2,0},{1,3},{3,1},{4,6},{6,4},{5,7},{7,5},{8,10},{10,8},{9,1... | collective-permute-start | bytes 2371592 | tf_op jit(solution)/shard_map/ppermute | solution.py:292
  77.6 32.6 %collective-permute-start.27 = (bf16[2,3088,128]{2,1,0:T(8,128)(2,1)}, bf16[2,3088,128]{2,1,0:T(8,128)(2,1)}, u32[]{:S(2)}, u32[]{:S(2)}) collective-permute-start(bf16[2,3088,128]{2,1,0:T(8,128)(2,1)} %collective-permute-done.26), channel_id=1, source_target_pairs={{9,1},{11,3},{13,5},{15,7}} | collective-permute-start | bytes 4743176 | tf_op jit(solution)/shard_map/ppermute | solution.py:303
  89.3 20.1 %collective-permute-start.7 = (bf16[3088,128]{1,0:T(8,128)(2,1)S(1)}, bf16[3088,128]{1,0:T(8,128)(2,1)}, u32[]{:S(2)}, u32[]{:S(2)}) collective-permute-start(bf16[3088,128]{1,0:T(8,128)(2,1)S(1)} %collective-permute-done.5), channel_id=1, source_target_pairs={{0,4},{4,0},{1,5},{5,1},{2,6},{6,2},{3,7},{7,3},{8,12},{12,8},{9,1... | collective-permute-start | bytes 2371592 | tf_op jit(solution)/shard_map/ppermute | solution.py:294
  89.8 19.6 %collective-permute-start.9 = (bf16[3088,128]{1,0:T(8,128)(2,1)S(1)}, bf16[3088,128]{1,0:T(8,128)(2,1)}, u32[]{:S(2)}, u32[]{:S(2)}) collective-permute-start(bf16[3088,128]{1,0:T(8,128)(2,1)S(1)} %collective-permute-done.5), channel_id=1, source_target_pairs={{0,1},{1,0},{2,3},{3,2},{4,5},{5,4},{6,7},{7,6},{8,9},{9,8},{10,11... | collective-permute-start | bytes 2371592 | tf_op jit(solution)/shard_map/ppermute | solution.py:297
  90.0 20.2 %collective-permute-start.18 = (bf16[3088,128]{1,0:T(8,128)(2,1)}, bf16[3088,128]{1,0:T(8,128)(2,1)}, u32[]{:S(2)}, u32[]{:S(2)}) collective-permute-start(bf16[3088,128]{1,0:T(8,128)(2,1)} %collective-permute-done.17), channel_id=1, source_target_pairs={{0,2},{2,0},{1,3},{3,1},{4,6},{6,4},{5,7},{7,5},{8,10},{10,8},{9,1... | collective-permute-start | bytes 2371592 | tf_op jit(solution)/shard_map/ppermute | solution.py:294
  94.0 25.1 %collective-permute-start.21 = (bf16[3088,128]{1,0:T(8,128)(2,1)}, bf16[3088,128]{1,0:T(8,128)(2,1)S(1)}, u32[]{:S(2)}, u32[]{:S(2)}) collective-permute-start(bf16[3088,128]{1,0:T(8,128)(2,1)} %collective-permute-done.17), channel_id=1, source_target_pairs={{0,1},{1,0},{2,3},{3,2},{4,5},{5,4},{6,7},{7,6},{8,9},{9,8},{10,11... | collective-permute-start | bytes 2371592 | tf_op jit(solution)/shard_map/ppermute | solution.py:297
  116.0 37.5 %collective-permute-start.28 = (bf16[2,3088,128]{2,1,0:T(8,128)(2,1)}, bf16[2,3088,128]{2,1,0:T(8,128)(2,1)}, u32[]{:S(2)}, u32[]{:S(2)}) collective-permute-start(bf16[2,3088,128]{2,1,0:T(8,128)(2,1)} %add_select_fusion.refs_1_.refs_6_.refs_18_), channel_id=1, source_target_pairs={{0,2},{2,0},{1,3},{3,1},{4,6},{6,4},{5,7},{7,5},{8,10},{10,8},{9,1... | collective-permute-start | bytes 4743176 | tf_op jit(solution)/shard_map/ppermute | solution.py:248
  117.6 38.9 %collective-permute-start.29 = (bf16[2,3088,128]{2,1,0:T(8,128)(2,1)}, bf16[2,3088,128]{2,1,0:T(8,128)(2,1)}, u32[]{:S(2)}, u32[]{:S(2)}) collective-permute-start(bf16[2,3088,128]{2,1,0:T(8,128)(2,1)} %add_select_fusion.refs_1_.refs_6_.refs_18_), channel_id=1, source_target_pairs={{0,4},{4,0},{1,5},{5,1},{2,6},{6,2},{3,7},{7,3},{8,12},{12,8},{9,1... | collective-permute-start | bytes 4743176 | tf_op jit(solution)/shard_map/ppermute | solution.py:248
  119.1 133.6 %collective-permute-start.35 = (bf16[2,3088,128]{2,1,0:T(8,128)(2,1)}, bf16[2,3088,128]{2,1,0:T(8,128)(2,1)}, u32[]{:S(2)}, u32[]{:S(2)}) collective-permute-start(bf16[2,3088,128]{2,1,0:T(8,128)(2,1)} %add_select_fusion.refs_1_.refs_6_.refs_18_), channel_id=1, source_target_pairs={{0,1},{1,0},{2,3},{3,2},{4,5},{5,4},{6,7},{7,6},{8,9},{9,8},{10,11... | collective-permute-start | bytes 4743176 | tf_op jit(solution)/shard_map/ppermute | solution.py:248
  145.3 18.5 %collective-permute-start.23 = (f32[8,1792]{1,0:T(8,128)}, f32[8,1792]{1,0:T(8,128)}, u32[]{:S(2)}, u32[]{:S(2)}) collective-permute-start(f32[8,1792]{1,0:T(8,128)} %fusion.53), channel_id=1, source_target_pairs={{0,1},{1,2},{2,3},{3,4},{4,5},{5,6},{6,7},{8,9},{9,10},{10,11},{11... | collective-permute-start | bytes 172040 | tf_op jit(solution)/shard_map/ppermute | solution.py:63
  155.5 28.4 %collective-permute-start.30 = (bf16[1,3088,128]{2,1,0:T(8,128)(2,1)}, bf16[1,3088,128]{2,1,0:T(8,128)(2,1)}, u32[]{:S(2)}, u32[]{:S(2)}) collective-permute-start(bf16[1,3088,128]{2,1,0:T(8,128)(2,1)} %slice.346.refs_3_), channel_id=1, source_target_pairs={{0,4},{4,0},{1,5},{5,1},{2,6},{6,2},{3,7},{7,3},{8,12},{12,8},{9,1... | collective-permute-start | bytes 2371592 | tf_op jit(solution)/shard_map/ppermute | solution.py:248
  158.5 25.4 %collective-permute-start.31 = (bf16[1,3088,128]{2,1,0:T(8,128)(2,1)}, bf16[1,3088,128]{2,1,0:T(8,128)(2,1)}, u32[]{:S(2)}, u32[]{:S(2)}) collective-permute-start(bf16[1,3088,128]{2,1,0:T(8,128)(2,1)} %slice.347.refs_4_), channel_id=1, source_target_pairs={{0,2},{2,0},{1,3},{3,1},{4,6},{6,4},{5,7},{7,5},{8,10},{10,8},{9,1... | collective-permute-start | bytes 2371592 | tf_op jit(solution)/shard_map/ppermute | solution.py:248
  190.1 62.5 %collective-permute-start.36 = (bf16[2,3088,128]{2,1,0:T(8,128)(2,1)}, bf16[2,3088,128]{2,1,0:T(8,128)(2,1)}, u32[]{:S(2)}, u32[]{:S(2)}) collective-permute-start(bf16[2,3088,128]{2,1,0:T(8,128)(2,1)} %collective-permute-done.28.refs_2_.refs_7_.refs_19_), channel_id=1, source_target_pairs={{0,1},{1,0},{2,3},{3,2},{4,5},{5,4},{6,7},{7,6},{8,9},{9,8},{10,11... | collective-permute-start | bytes 4743176 | tf_op jit(solution)/shard_map/ppermute | solution.py:248
  190.5 62.1 %collective-permute-start.37 = (bf16[2,3088,128]{2,1,0:T(8,128)(2,1)}, bf16[2,3088,128]{2,1,0:T(8,128)(2,1)}, u32[]{:S(2)}, u32[]{:S(2)}) collective-permute-start(bf16[2,3088,128]{2,1,0:T(8,128)(2,1)} %collective-permute-done.29.refs_3_.refs_8_.refs_20_), channel_id=1, source_target_pairs={{0,1},{1,0},{2,3},{3,2},{4,5},{5,4},{6,7},{7,6},{8,9},{9,8},{10,11... | collective-permute-start | bytes 4743176 | tf_op jit(solution)/shard_map/ppermute | solution.py:248
  190.6 62.0 %collective-permute-start.38 = (bf16[1,3088,128]{2,1,0:T(8,128)(2,1)}, bf16[1,3088,128]{2,1,0:T(8,128)(2,1)}, u32[]{:S(2)}, u32[]{:S(2)}) collective-permute-start(bf16[1,3088,128]{2,1,0:T(8,128)(2,1)} %collective-permute-done.30.refs_4_.refs_9_.refs_21_), channel_id=1, source_target_pairs={{0,1},{1,0},{2,3},{3,2},{4,5},{5,4},{6,7},{7,6},{8,9},{9,8},{10,11... | collective-permute-start | bytes 2371592 | tf_op jit(solution)/shard_map/ppermute | solution.py:248
  230.8 22.4 %collective-permute-start.39 = (bf16[1,3088,128]{2,1,0:T(8,128)(2,1)}, bf16[1,3088,128]{2,1,0:T(8,128)(2,1)}, u32[]{:S(2)}, u32[]{:S(2)}) collective-permute-start(bf16[1,3088,128]{2,1,0:T(8,128)(2,1)} %collective-permute-done.31.refs_5_.refs_10_.refs_22_), channel_id=1, source_target_pairs={{0,1},{1,0},{2,3},{3,2},{4,5},{5,4},{6,7},{7,6},{8,9},{9,8},{10,11... | collective-permute-start | bytes 2371592 | tf_op jit(solution)/shard_map/ppermute | solution.py:248
  367.9 28.1 %collective-permute-start.41 = (bf16[144,1536]{1,0:T(8,128)(2,1)S(1)}, bf16[144,1536]{1,0:T(8,128)(2,1)S(1)}, u32[]{:S(2)}, u32[]{:S(2)}) collective-permute-start(bf16[144,1536]{1,0:T(8,128)(2,1)S(1)} %pad_maximum_fusion.18.refs_7_), channel_id=1, source_target_pairs={{0,2},{2,0},{1,3},{3,1},{4,6},{6,4},{5,7},{7,5},{8,10},{10,8},{9,1... | collective-permute-start | bytes 1327112 | tf_op jit(solution)/shard_map/ppermute | solution.py:248
  406.6 42.9 %collective-permute-start.43 = (bf16[24688,128]{1,0:T(8,128)(2,1)}, bf16[24688,128]{1,0:T(8,128)(2,1)}, u32[]{:S(2)}, u32[]{:S(2)}) collective-permute-start(bf16[24688,128]{1,0:T(8,128)(2,1)} %constant_dynamic-slice_fusion.2.refs_2_), channel_id=1, source_target_pairs={{0,1},{1,0},{2,3},{3,2},{4,5},{5,4},{6,7},{7,6},{8,9},{9,8},{10,11... | collective-permute-start | bytes 18960392 | tf_op jit(solution)/shard_map/ppermute | solution.py:248
  409.8 38.6 %collective-permute-start.42 = (bf16[144,1536]{1,0:T(8,128)(2,1)}, bf16[144,1536]{1,0:T(8,128)(2,1)}, u32[]{:S(2)}, u32[]{:S(2)}) collective-permute-start(bf16[144,1536]{1,0:T(8,128)(2,1)} %pad_maximum_fusion.19.refs_1_), channel_id=1, source_target_pairs={{0,4},{4,0},{1,5},{5,1},{2,6},{6,2},{3,7},{7,3},{8,12},{12,8},{9,1... | collective-permute-start | bytes 1327112 | tf_op jit(solution)/shard_map/ppermute | solution.py:248
  458.9 72.4 %collective-permute-start.45 = (bf16[2,3104,128]{2,1,0:T(8,128)(2,1)}, bf16[2,3104,128]{2,1,0:T(8,128)(2,1)}, u32[]{:S(2)}, u32[]{:S(2)}) collective-permute-start(bf16[2,3104,128]{2,1,0:T(8,128)(2,1)} %pad_maximum_fusion.5.refs_12_.refs_2_), channel_id=1, source_target_pairs={{0,2},{2,0},{1,3},{3,1},{4,6},{6,4},{5,7},{7,5},{8,10},{10,8},{9,1... | collective-permute-start | bytes 4767752 | tf_op jit(solution)/shard_map/ppermute | solution.py:248
  468.0 21.6 %collective-permute-start.50 = (f32[4]{0:T(128)S(1)}, f32[4]{0:T(128)S(1)}, u32[]{:S(2)}, u32[]{:S(2)}) collective-permute-start(f32[4]{0:T(128)S(1)} %add.657.refs_7_.refs_8_), channel_id=1, source_target_pairs={{0,16},{16,0},{8,24},{24,8},{1,17},{17,1},{9,25},{25,9},{2,18},{18... | collective-permute-start | bytes 56 | tf_op jit(solution)/shard_map/ppermute | solution.py:248
  492.8 42.5 %collective-permute-start.44 = (bf16[2,3104,128]{2,1,0:T(8,128)(2,1)}, bf16[2,3104,128]{2,1,0:T(8,128)(2,1)}, u32[]{:S(2)}, u32[]{:S(2)}) collective-permute-start(bf16[2,3104,128]{2,1,0:T(8,128)(2,1)} %pad_maximum_fusion.4.refs_11_.refs_1_), channel_id=1, source_target_pairs={{0,4},{4,0},{1,5},{5,1},{2,6},{6,2},{3,7},{7,3},{8,12},{12,8},{9,1... | collective-permute-start | bytes 4767752 | tf_op jit(solution)/shard_map/ppermute | solution.py:248
  534.7 23.9 %collective-permute-start.47 = (bf16[3104,128]{1,0:T(8,128)(2,1)S(1)}, bf16[3104,128]{1,0:T(8,128)(2,1)}, u32[]{:S(2)}, u32[]{:S(2)}) collective-permute-start(bf16[3104,128]{1,0:T(8,128)(2,1)S(1)} %dynamic-slice_bitcast_fusion.11.refs_5_.refs_10_), channel_id=1, source_target_pairs={{0,4},{4,0},{1,5},{5,1},{2,6},{6,2},{3,7},{7,3},{8,12},{12,8},{9,1... | collective-permute-start | bytes 2383880 | tf_op jit(solution)/shard_map/ppermute | solution.py:248
  538.3 21.9 %collective-permute-start.46 = (bf16[3104,128]{1,0:T(8,128)(2,1)}, bf16[3104,128]{1,0:T(8,128)(2,1)}, u32[]{:S(2)}, u32[]{:S(2)}) collective-permute-start(bf16[3104,128]{1,0:T(8,128)(2,1)} %dynamic-slice_bitcast_fusion.14.refs_4_.refs_9_), channel_id=1, source_target_pairs={{0,2},{2,0},{1,3},{3,1},{4,6},{6,4},{5,7},{7,5},{8,10},{10,8},{9,1... | collective-permute-start | bytes 2383880 | tf_op jit(solution)/shard_map/ppermute | solution.py:248
  588.8 28.6 %collective-permute-start.51 = (bf16[24688,128]{1,0:T(8,128)(2,1)}, bf16[24688,128]{1,0:T(8,128)(2,1)}, u32[]{:S(2)}, u32[]{:S(2)}) collective-permute-start(bf16[24688,128]{1,0:T(8,128)(2,1)} %constant_dynamic-slice_fusion.1.refs_1_), channel_id=1, source_target_pairs={{0,1},{1,0},{2,3},{3,2},{4,5},{5,4},{6,7},{7,6},{8,9},{9,8},{10,11... | collective-permute-start | bytes 18960392 | tf_op jit(solution)/shard_map/ppermute | solution.py:248
  600.1 96.6 %collective-permute-start.55 = (bf16[2,3104,128]{2,1,0:T(8,128)(2,1)}, bf16[2,3104,128]{2,1,0:T(8,128)(2,1)}, u32[]{:S(2)}, u32[]{:S(2)}) collective-permute-start(bf16[2,3104,128]{2,1,0:T(8,128)(2,1)} %pad_maximum_fusion.6.refs_4_.refs_5_.refs_6_.refs_9_.refs_10_.refs_11_.refs_2_.refs_3_), channel_id=1, source_target_pairs={{8,16},{17,25},{10,18},{19,27},{12,20},{21,29},{14,22},{23,31}} | collective-permute-start | bytes 4767752 | tf_op jit(solution)/shard_map/ppermute | solution.py:248
  602.1 96.0 %collective-permute-start.56 = (bf16[2,3104,128]{2,1,0:T(8,128)(2,1)}, bf16[2,3104,128]{2,1,0:T(8,128)(2,1)}, u32[]{:S(2)}, u32[]{:S(2)}) collective-permute-start(bf16[2,3104,128]{2,1,0:T(8,128)(2,1)} %pad_maximum_fusion.6.refs_4_.refs_5_.refs_6_.refs_9_.refs_10_.refs_11_.refs_2_.refs_3_), channel_id=1, source_target_pairs={{0,16},{9,25},{2,18},{11,27},{4,20},{13,29},{6,22},{15,31}} | collective-permute-start | bytes 4767752 | tf_op jit(solution)/shard_map/ppermute | solution.py:248
  605.2 94.3 %collective-permute-start.57 = (bf16[2,3104,128]{2,1,0:T(8,128)(2,1)}, bf16[2,3104,128]{2,1,0:T(8,128)(2,1)}, u32[]{:S(2)}, u32[]{:S(2)}) collective-permute-start(bf16[2,3104,128]{2,1,0:T(8,128)(2,1)} %pad_maximum_fusion.6.refs_4_.refs_5_.refs_6_.refs_9_.refs_10_.refs_11_.refs_2_.refs_3_), channel_id=1, source_target_pairs={{24,16},{1,25},{26,18},{3,27},{28,20},{5,29},{30,22},{7,31}} | collective-permute-start | bytes 4767752 | tf_op jit(solution)/shard_map/ppermute | solution.py:248
  626.4 37.0 %collective-permute-start.52 = (bf16[2,3104,128]{2,1,0:T(8,128)(2,1)}, bf16[2,3104,128]{2,1,0:T(8,128)(2,1)}, u32[]{:S(2)}, u32[]{:S(2)}) collective-permute-start(bf16[2,3104,128]{2,1,0:T(8,128)(2,1)} %pad_maximum_fusion.7.refs_1_.refs_7_), channel_id=1, source_target_pairs={{0,4},{4,0},{1,5},{5,1},{2,6},{6,2},{3,7},{7,3},{8,12},{12,8},{9,1... | collective-permute-start | bytes 4767752 | tf_op jit(solution)/shard_map/ppermute | solution.py:248
  629.1 37.3 %collective-permute-start.53 = (bf16[2,3104,128]{2,1,0:T(8,128)(2,1)}, bf16[2,3104,128]{2,1,0:T(8,128)(2,1)}, u32[]{:S(2)}, u32[]{:S(2)}) collective-permute-start(bf16[2,3104,128]{2,1,0:T(8,128)(2,1)} %pad_maximum_fusion.8.refs_2_.refs_8_), channel_id=1, source_target_pairs={{0,2},{2,0},{1,3},{3,1},{4,6},{6,4},{5,7},{7,5},{8,10},{10,8},{9,1... | collective-permute-start | bytes 4767752 | tf_op jit(solution)/shard_map/ppermute | solution.py:248
  669.5 19.8 %collective-permute-start.54 = (bf16[3104,128]{1,0:T(8,128)(2,1)}, bf16[3104,128]{1,0:T(8,128)(2,1)}, u32[]{:S(2)}, u32[]{:S(2)}) collective-permute-start(bf16[3104,128]{1,0:T(8,128)(2,1)} %dynamic-slice_bitcast_fusion.4.refs_2_.refs_7_), channel_id=1, source_target_pairs={{0,2},{2,0},{1,3},{3,1},{4,6},{6,4},{5,7},{7,5},{8,10},{10,8},{9,1... | collective-permute-start | bytes 2383880 | tf_op jit(solution)/shard_map/ppermute | solution.py:248
  671.8 35.2 %collective-permute-start.59 = (bf16[3104,128]{1,0:T(8,128)(2,1)S(1)}, bf16[3104,128]{1,0:T(8,128)(2,1)}, u32[]{:S(2)}, u32[]{:S(2)}) collective-permute-start(bf16[3104,128]{1,0:T(8,128)(2,1)S(1)} %dynamic-slice_bitcast_fusion.1.refs_3_.refs_8_), channel_id=1, source_target_pairs={{0,4},{4,0},{1,5},{5,1},{2,6},{6,2},{3,7},{7,3},{8,12},{12,8},{9,1... | collective-permute-start | bytes 2383880 | tf_op jit(solution)/shard_map/ppermute | solution.py:248
  691.5 35.5 %collective-permute-start.62 = (bf16[3104,128]{1,0:T(8,128)(2,1)}, bf16[3104,128]{1,0:T(8,128)(2,1)}, u32[]{:S(2)}, u32[]{:S(2)}) collective-permute-start(bf16[3104,128]{1,0:T(8,128)(2,1)} %fusion.20.refs_2_.refs_3_.refs_4_), channel_id=1, source_target_pairs={{24,0},{1,9},{26,2},{3,11},{28,4},{5,13},{30,6},{7,15}} | collective-permute-start | bytes 2383880 | tf_op jit(solution)/shard_map/ppermute | solution.py:248
  696.7 36.5 %collective-permute-start.61 = (bf16[3104,128]{1,0:T(8,128)(2,1)}, bf16[3104,128]{1,0:T(8,128)(2,1)}, u32[]{:S(2)}, u32[]{:S(2)}) collective-permute-start(bf16[3104,128]{1,0:T(8,128)(2,1)} %fusion.20.refs_2_.refs_3_.refs_4_), channel_id=1, source_target_pairs={{16,0},{25,9},{18,2},{27,11},{20,4},{29,13},{22,6},{31,15}} | collective-permute-start | bytes 2383880 | tf_op jit(solution)/shard_map/ppermute | solution.py:248
  698.0 35.2 %collective-permute-start.60 = (bf16[3104,128]{1,0:T(8,128)(2,1)}, bf16[3104,128]{1,0:T(8,128)(2,1)}, u32[]{:S(2)}, u32[]{:S(2)}) collective-permute-start(bf16[3104,128]{1,0:T(8,128)(2,1)} %fusion.20.refs_2_.refs_3_.refs_4_), channel_id=1, source_target_pairs={{8,0},{17,9},{10,2},{19,11},{12,4},{21,13},{14,6},{23,15}} | collective-permute-start | bytes 2383880 | tf_op jit(solution)/shard_map/ppermute | solution.py:248
  715.6 23.6 %collective-permute-start.63 = (bf16[2,2,512,128]{3,2,1,0:T(8,128)(2,1)S(1)}, bf16[2,2,512,128]{3,2,1,0:T(8,128)(2,1)}, u32[]{:S(2)}, u32[]{:S(2)}) collective-permute-start(bf16[2,2,512,128]{3,2,1,0:T(8,128)(2,1)S(1)} %dynamic-slice_bitcast_fusion.21.refs_1_), channel_id=1, source_target_pairs={{0,4},{4,0},{1,5},{5,1},{2,6},{6,2},{3,7},{7,3},{8,12},{12,8},{9,1... | collective-permute-start | bytes 1572872 | tf_op jit(solution)/shard_map/ppermute | solution.py:248
  768.1 23.1 %collective-permute-start.72 = (bf16[3104,128]{1,0:T(8,128)(2,1)S(1)}, bf16[3104,128]{1,0:T(8,128)(2,1)S(1)}, u32[]{:S(2)}, u32[]{:S(2)}) collective-permute-start(bf16[3104,128]{1,0:T(8,128)(2,1)S(1)} %copy-done.3), channel_id=1, source_target_pairs={{24,0},{1,9},{26,2},{3,11},{28,4},{5,13},{30,6},{7,15}} | collective-permute-start | bytes 2383880 | tf_op jit(solution)/shard_map/ppermute | solution.py:248
  769.6 40.8 %collective-permute-start.71 = (bf16[3104,128]{1,0:T(8,128)(2,1)S(1)}, bf16[3104,128]{1,0:T(8,128)(2,1)S(1)}, u32[]{:S(2)}, u32[]{:S(2)}) collective-permute-start(bf16[3104,128]{1,0:T(8,128)(2,1)S(1)} %copy-done.3), channel_id=1, source_target_pairs={{16,0},{25,9},{18,2},{27,11},{20,4},{29,13},{22,6},{31,15}} | collective-permute-start | bytes 2383880 | tf_op jit(solution)/shard_map/ppermute | solution.py:248
  770.9 39.5 %collective-permute-start.70 = (bf16[3104,128]{1,0:T(8,128)(2,1)S(1)}, bf16[3104,128]{1,0:T(8,128)(2,1)S(1)}, u32[]{:S(2)}, u32[]{:S(2)}) collective-permute-start(bf16[3104,128]{1,0:T(8,128)(2,1)S(1)} %copy-done.3), channel_id=1, source_target_pairs={{8,0},{17,9},{10,2},{19,11},{12,4},{21,13},{14,6},{23,15}} | collective-permute-start | bytes 2383880 | tf_op jit(solution)/shard_map/ppermute | solution.py:248
  773.6 40.3 %collective-permute-start.68 = (bf16[2,400,128]{2,1,0:T(8,128)(2,1)S(1)}, bf16[2,400,128]{2,1,0:T(8,128)(2,1)S(1)}, u32[]{:S(2)}, u32[]{:S(2)}) collective-permute-start(bf16[2,400,128]{2,1,0:T(8,128)(2,1)S(1)} %dynamic-slice_bitcast_fusion.23), channel_id=1, source_target_pairs={{0,4},{4,0},{1,5},{5,1},{2,6},{6,2},{3,7},{7,3},{8,12},{12,8},{9,1... | collective-permute-start | bytes 614408 | tf_op jit(solution)/shard_map/ppermute | solution.py:248
  830.9 28.0 %collective-permute-start.81 = (bf16[3104,128]{1,0:T(8,128)(2,1)}, bf16[3104,128]{1,0:T(8,128)(2,1)S(1)}, u32[]{:S(2)}, u32[]{:S(2)}) collective-permute-start(bf16[3104,128]{1,0:T(8,128)(2,1)} %get-tuple-element.164.refs_5_), channel_id=1, source_target_pairs={{0,1},{9,8},{16,17},{25,24},{2,3},{11,10},{18,19},{27,26},{4,5},{1... | collective-permute-start | bytes 2383880 | tf_op jit(solution)/shard_map/ppermute | solution.py:248
  832.3 26.7 %collective-permute-start.80 = (bf16[3104,128]{1,0:T(8,128)(2,1)}, bf16[3104,128]{1,0:T(8,128)(2,1)S(1)}, u32[]{:S(2)}, u32[]{:S(2)}) collective-permute-start(bf16[3104,128]{1,0:T(8,128)(2,1)} %get-tuple-element.128.refs_1_), channel_id=1, source_target_pairs={{0,1},{9,8},{16,17},{25,24},{2,3},{11,10},{18,19},{27,26},{4,5},{1... | collective-permute-start | bytes 2383880 | tf_op jit(solution)/shard_map/ppermute | solution.py:248
  (218 other events, 2423.4 us)
Sparse Core Ops, SparseCore 0:
  161.9 51.9 all-gather.2

commit v11 on v10

--- a/solution.py
+++ b/solution.py
@@ -1527,7 +1527,11 @@
         [matmul(hidden, weights[W_X_SSM]), matmul(hidden, weights[W_B_C])], axis=1
     )
     step_raw = matmul(hidden, weights[W_STEP])
-    rim_rows = passed_along(xbc[rows_dev - 8 :], span, 1)
+    q_wide = jnp.pad(q_rot * jnp.bfloat16(score_scale), ((0, 0), (0, HEAD_DIM), (0, 0)))
+    rim_source = xbc[rows_dev - 8 :]
+    if fast:
+        (rim_source,) = fence([rim_source], [q_wide])
+    rim_rows = passed_along(rim_source, span, 1)
     ssm_meta = jnp.concatenate([my_start[None], row_starts[CHUNK - 1 :: CHUNK]]).astype(jnp.int32)
     conv_bias = small_f32[CONV_BIAS][None, :]
     convolve = lambda after: conv_forward(
@@ -1557,7 +1561,6 @@
     meta = jnp.stack(
         [first_start // KEYS, last_row // KEYS + 1, my_start, row_starts[rows_dev - 1]]
     ).astype(jnp.int32)
-    q_wide = jnp.pad(q_rot * jnp.bfloat16(score_scale), ((0, 0), (0, HEAD_DIM), (0, 0)))
     start_row = jnp.broadcast_to(row_starts[None, :], (8, rows_dev))
     if fast:
         (local_state,) = bracket(summarize, [spread_flow])
@@ -1644,7 +1647,6 @@
         (early,) = fence([early], [grad_state_out])
         late_flow.go()
         (early,) = fence([early], late_flow.values())
-        stats_flow = Flow(plane_stages(squares))
         around = lambda call: bracket(call, [late_flow])
     else:
         grad_state_out = scan_states(carry_all, grad_state_local, span, fast, True)
@@ -1662,8 +1664,6 @@
     grad_step_bias = jnp.sum(grad_step_rows, axis=1)
     grad_step_raw_f32 = grad_step_rows.T
     grad_skip_gain = jnp.sum(grad_small[:, 4, : 2 * SSM_DIM].reshape(SSM_HEADS, SSM_DIM), axis=1)
-    if fast:
-        around = lambda call: bracket(call, [late_flow, stats_flow])
     grad_main, grad_tail, grad_edge, grad_taps = around(
         lambda after: conv_backward(
             grad_x, grad_b, grad_c, xbc, rim_rows, small_f32[CONV_WEIGHT], conv_bias, ssm_meta,
@@ -1696,14 +1696,14 @@
     }
     parts = []
     if fast:
-        (early,) = bracket(lambda after: pack_ssm(
+        early = pack_ssm(
             early,
             [
                 (attended, grad_branch), (hidden, grad_gate_ssm),
                 (hidden, grad_xbc[:, :ssm_inner]), (hidden, grad_xbc[:, ssm_inner:]),
             ],
-            small, ssm_low, grad_branch, (*after, *late_flow.values()),
-        ), [stats_flow])
+            small, ssm_low, grad_branch, late_flow.values(),
+        )
         early_flow = Flow(reduce_stages(early, 0, 8))
         (grad_attended,) = fence([grad_attended], early_flow.values() + late_flow.values())
         around = lambda call: bracket(call, [early_flow])
@@ -1767,7 +1767,9 @@
         ((pieces, _, _), *_) = corner_flow.sends
         (pieces,) = fence([pieces], early_flow.values())
         corner_flow.sends = [(pieces, axis, pairs) for _, axis, pairs in corner_flow.sends]
-        for flow in (early_flow, late_flow, corner_flow):
+        stats_flow = Flow(plane_stages(squares))
+        stats_flow.hold([pieces])
+        for flow in (early_flow, late_flow, corner_flow, stats_flow):
             while flow.sends:
                 flow.go()
         stats = jnp.sqrt(stats_flow.result / (all_rows * D))

time: 882 us -> 870 us (0.986)
    unnamed x371 -> x378, local copies, waits for them, and re-layouts: 32.6 us -> 31.9 us
  transfers between devices with their start and end apart: 83 -> 83, of which waited for: 25 -> 25; matrix products, arithmetic and copies ran while one was open for 20% -> 22% of each run, Pallas kernels for 17% -> 17%
where the time goes in v11:
time: 870 us; the launch traced here: 863 us
  Pallas kernels  199 us (23%)
  starting transfers between devices  182 us (21%)
  waiting for transfers between devices  158 us (18%)
  other arithmetic  140 us (16%)
  local copies, waits for them, and re-layouts  86.5 us (10%)
  matrix products  78.6 us (9%)
  between operations  18.5 us (2%)
    ppermute x53, starting transfers between devices, go(): lax.ppermute(value, axis, pairs)  138 us
    ppermute x53, waiting for transfers between devices, go(): lax.ppermute(value, axis, pairs)  110 us
    dot_general x12, matrix products, matmul_right_t(): lax.dot_general(left, right, (((1,), (1,)), ((), ())), preferred_element_...  46.3 us
    pallas_call x4, Pallas kernels, pack_lines(): pl.pallas_call(pinned(kernel, inputs, after), grid=(total,), in_specs=[le...  42.8 us
    pallas_call x2, Pallas kernels, unpack_lines(): pl.pallas_call(pinned(kernel, 2 + count_buffers, after), grid_spec=pltpu....  40.6 us
    pallas_call x1, Pallas kernels, ssm_backward(): pl.pallas_call(pinned(kernel, 11, after), grid_spec=pltpu.PrefetchScalarG...  33.4 us
    convert_element_type x14, other arithmetic, added(): return total.astype(jnp.bfloat16)  32.2 us
    unnamed x378, local copies, waits for them, and re-layouts  31.9 us
  transfers between devices with their start and end apart: 83, of which 25 were waited for; matrix products, arithmetic and copies ran while one was open for 22% of the time, Pallas kernels for 17%

profile of v11, /device:TPU:0, one launch (start us, length us, event | category | flops | bytes accessed | tf_op | source)
XLA Modules:
  0.0 862.6 jit_solution(16249653584311843047)
XLA Ops:
  13.1 5.4 collective-permute-start.1
  19.9 7.3 collective-permute-done.1
  50.3 9.1 %collective-permute-start.8 = (bf16[3088,128]{1,0:T(8,128)(2,1)S(1)}, bf16[3088,128]{1,0:T(8,128)(2,1)}, u32[]{:S(2)}, u32[]{:S(2)}) collective-permute-start(bf16[3088,128]{1,0:T(8,128)(2,1)S(1)} %add_select_fusion.2), channel_id=1, source_target_pairs={{0,1},{1,0},{2,3},{3,2},{4,5},{5,4},{6,7},{7,6},{8,9},{9,8},{10,11... | collective-permute-start | bytes 2371592 | tf_op jit(solution)/shard_map/ppermute | solution.py:297
  63.8 12.3 %collective-permute-done.26 = bf16[2,3088,128]{2,1,0:T(8,128)(2,1)} collective-permute-done((bf16[2,3088,128]{2,1,0:T(8,128)(2,1)}, bf16[2,3088,128]{2,1,0:T(8,128)(2,1)}, u32[]{:S(2)}, u32[]{:S(2)}) %collective-permute-start.26) | collective-permute-done | bytes 1581088 | tf_op jit(solution)/shard_map/ppermute | solution.py:302
  94.2 15.4 %collective-permute-done.7 = bf16[3088,128]{1,0:T(8,128)(2,1)} collective-permute-done((bf16[3088,128]{1,0:T(8,128)(2,1)S(1)}, bf16[3088,128]{1,0:T(8,128)(2,1)}, u32[]{:S(2)}, u32[]{:S(2)}) %collective-permute-start.7) | collective-permute-done | bytes 790560 | tf_op jit(solution)/shard_map/ppermute | solution.py:294
  110.9 5.2 add_select_fusion.refs_1_.refs_6_.refs_18_
  120.7 14.4 %unpack.2 = (bf16[1024,512]{1,0:T(8,128)(2,1)}, bf16[1024,128]{1,0:T(8,128)(2,1)S(1)}, bf16[1024,128]{1,0:T(8,128)(2,1)S(1)}, bf16[512,1024]{1,0:T(8,128)(2,1)},...) custom-call(s32[25,5]{1,0:T(8,128)S(1)} %copy-done.52, ...), custom_call_target="tpu_custom_call" | custom-call | bytes 26624000 | tf_op jit(solution)/shard_map/unpack/pallas_call | solution.py:454
  163.6 11.5 %conv.1.refs_0_.refs_1_.x_ref.b_ref.c_ref.refs_3_.refs_4_ = f32[512,1792]{1,0:T(8,128)} custom-call(s32[5]{0:T(128)} %pad_add_fusion.1.refs_0_.meta_ref, f32[512,1792]{1,0:T(8,128)} %pad_maximum_fusion.refs_1_.refs_4_, f32[8,1792]{1,0:T(8,128)} %collective-permute-done.23.refs_2_.refs_5_, f32[4,1792]{1,0:T(4,128)} %reshape.435.refs_3_.refs_6_, ...), custom_call_target="tpu_custom_call" | custom-call | flops 1000000000 | bytes 7340032 | tf_op jit(solution)/shard_map/conv/pallas_call | solution.py:759
  175.1 8.8 %state.2.refs_0_ = f32[128,1536]{1,0:T(8,128)} custom-call(f32[512,1792]{1,0:T(8,128)} %conv.1.refs_0_.refs_1_.x_ref.b_ref.c_ref.refs_3_.refs_4_, f32[512,1792]{1,0:T(8,128)} %conv.1.refs_0_.refs_1_.x_ref.b_ref.c_ref.refs_3_.refs_4_, f32[12,2,512]{2,1,0:T(2,128)} %reshape.412.refs_2_, bf16[1,3088,128]{2,1,0:T(8,128)(2,1)} %copy-done.116, ...), custom_call_target="tpu_custom_call" | custom-call | flops 201326592 | bytes 3145728 | tf_op jit(solution)/shard_map/state/pallas_call | solution.py:871
  195.8 9.0 %collective-permute-done.33 = bf16[144,1536]{1,0:T(8,128)(2,1)S(1)} collective-permute-done((bf16[144,1536]{1,0:T(8,128)(2,1)S(1)}, bf16[144,1536]{1,0:T(8,128)(2,1)S(1)}, u32[]{:S(2)}, u32[]{:S(2)}) %collective-permute-start.33) | collective-permute-done | bytes 442400 | tf_op jit(solution)/shard_map/ppermute | solution.py:248
  209.3 5.1 all-gather.3.cloned.1.call-done
  214.4 14.6 %attend.1 = (f32[8,64,512]{2,1,0:T(8,128)S(1)}, f32[8,8,512]{2,1,0:T(8,128)S(1)}) custom-call(s32[4]{0:T(128)S(1)} %pad_add_fusion.refs_0_, bf16[8,128,512]{2,1,0:T(8,128)(2,1)S(1)} %copy-done.19, bf16[8,2,512,128]{3,2,1,0:T(8,128)(2,1)} %bitcast.332, s32[8,512]{1,0:T(8,128)S(1)} %broadcast_in_dim.286.refs_3_.row_ref.refs_10_.refs_6_, ...), custom_call_target="tpu_custom_call" | custom-call | flops 20000000000 | bytes 8388608 | tf_op jit(solution)/shard_map/attend/pallas_call | solution.py:1240
  230.6 5.9 collective-permute-start.39
  242.8 8.5 ssm.1.refs_28_
  253.9 26.1 %unpack.3 = (bf16[1536,1024]{1,0:T(8,128)(2,1)}, bf16[1024,2048]{1,0:T(8,128)(2,1)}, bf16[1024,2048]{1,0:T(8,128)(2,1)}, bf16[2048,1024]{1,0:T(8,128)(2,1)}, bf16[16,128]{1,0:T(8,128)(2,1)S(1)}) custom-call(s32[31,5]{1,0:T(8,128)S(1)} %copy-done.51, s32[32]{0:T(128)S(1)} %fusion.78.refs_1_, bf16[1,3088,128]{2,1,0:T(8,128)(2,1)S(1)} %bitcast.267, ...), custom_call_target="tpu_custom_call" | custom-call | bytes 33013760 | tf_op jit(solution)/shard_map/unpack/pallas_call | solution.py:454
  295.5 6.7 fusion.2
  302.2 6.9 fusion.104
  328.9 8.8 %state.3 = f32[128,1536]{1,0:T(8,128)} custom-call(f32[512,1792]{1,0:T(8,128)} %conv.1.refs_0_.refs_1_.x_ref.b_ref.c_ref.refs_3_.refs_4_, f32[512,1536]{1,0:T(8,128)} %get-tuple-element.137.refs_1_.refs_2_, f32[12,2,512]{2,1,0:T(2,128)} %reshape.417.refs_2_), custom_call_target="tpu_custom_call" | custom-call | flops 201326592 | bytes 3145728 | tf_op jit(solution)/shard_map/state/pallas_call | solution.py:871
  349.0 6.4 pad_maximum_fusion.1
  360.0 10.1 %collective-permute-start.41 = (bf16[144,1536]{1,0:T(8,128)(2,1)S(1)}, bf16[144,1536]{1,0:T(8,128)(2,1)S(1)}, u32[]{:S(2)}, u32[]{:S(2)}) collective-permute-start(bf16[144,1536]{1,0:T(8,128)(2,1)S(1)} %pad_maximum_fusion.18.refs_7_), channel_id=1, source_target_pairs={{0,2},{2,0},{1,3},{3,1},{4,6},{6,4},{5,7},{7,5},{8,10},{10,8},{9,1... | collective-permute-start | bytes 1327112 | tf_op jit(solution)/shard_map/ppermute | solution.py:248
  370.1 20.5 %pack.4.refs_0_ = bf16[49344,128]{1,0:T(8,128)(2,1)} custom-call(bf16[512,1024]{1,0:T(8,128)(2,1)S(1)} %copy-done.38, bf16[512,2048]{1,0:T(8,128)(2,1)S(1)} %copy-done.57, bf16[512,2048]{1,0:T(8,128)(2,1)} %get-tuple-element.209.refs_2_, bf16[512,2048]{1,0:T(8,128)(2,1)} %get-tuple-element.210.refs_3_, bf16[512,1024]{1,0:T(8,128)(2,1)S(1)} %copy-done.36, ...), custom_call_target="tpu_custom_call" | custom-call | flops 6442450944 | bytes 16777216 | tf_op jit(solution)/shard_map/pack/pallas_call | solution.py:609
  395.5 6.0 constant_dynamic-slice_fusion.2.refs_2_
  405.0 26.4 %collective-permute-start.42 = (bf16[144,1536]{1,0:T(8,128)(2,1)}, bf16[144,1536]{1,0:T(8,128)(2,1)}, u32[]{:S(2)}, u32[]{:S(2)}) collective-permute-start(bf16[144,1536]{1,0:T(8,128)(2,1)} %pad_maximum_fusion.19.refs_1_), channel_id=1, source_target_pairs={{0,4},{4,0},{1,5},{5,1},{2,6},{6,2},{3,7},{7,3},{8,12},{12,8},{9,1... | collective-permute-start | bytes 1327112 | tf_op jit(solution)/shard_map/ppermute | solution.py:248
  432.4 5.8 add_convert_fusion.1
  453.4 5.9 collective-permute-start.44
  459.3 33.4 %ssm_back.1 = (f32[512,1536]{1,0:T(8,128)S(1)}, f32[512,128]{1,0:T(8,128)S(1)}, f32[512,128]{1,0:T(8,128)S(1)}, f32[12,8,512]{2,1,0:T(8,128)S(1)}) custom-call(s32[5]{0:T(128)S(1)} %copy-done.53, f32[512,1792]{1,0:T(8,128)} %conv.1.refs_0_.refs_1_.x_ref.b_ref.c_ref.refs_3_.refs_4_, f32[512,1536]{1,0:T(8,128)S(1)} %copy-done.6, ...), custom_call_target="tpu_custom_call" | custom-call | flops 3000000000 | bytes 9437184 | tf_op jit(solution)/shard_map/ssm_back/pallas_call | solution.py:1088
  508.5 14.7 %conv_back.1 = (bf16[512,1792]{1,0:T(8,128)(2,1)}, f32[16,1792]{1,0:T(8,128)}, f32[8,1792]{1,0:T(8,128)}, f32[8,1792]{1,0:T(8,128)}) custom-call(s32[5]{0:T(128)} %pad_add_fusion.1.refs_0_.meta_ref, f32[512,1536]{1,0:T(8,128)} %get-tuple-element.82.refs_1_, f32[512,128]{1,0:T(8,128)} %get-tuple-element.83.refs_2_, f32[512,128]{1,0:T(8,128)} %get-tuple-element.84.refs_3_, ...), custom_call_target="tpu_custom_call" | custom-call | flops 2000000000 | bytes 9175040 | tf_op jit(solution)/shard_map/conv_back/pallas_call | solution.py:818
  536.1 12.2 %pack.6 = bf16[49440,128]{1,0:T(8,128)(2,1)} custom-call(bf16[512,512]{1,0:T(8,128)(2,1)S(1)} %bitcast.274, bf16[512,1024]{1,0:T(8,128)(2,1)S(1)} %copy-done.2, bf16[512,1024]{1,0:T(8,128)(2,1)S(1)} %fusion.87.refs_2_, bf16[512,1536]{1,0:T(8,128)(2,1)S(1)} %copy-done.12, bf16[512,1536]{1,0:T(8,128)(2,1)S(1)} %slice.372.refs_4_, ...), custom_call_target="tpu_custom_call", output_to_operand_aliasing={{}: (7, {})} | custom-call | flops 4026531840 | bytes 11010048 | tf_op jit(solution)/shard_map/pack/pallas_call | solution.py:609
  548.3 6.0 constant_dynamic-slice_fusion.1.refs_1_
  559.2 5.1 fusion.105
  568.1 14.5 %collective-permute-start.54 = (bf16[2,3104,128]{2,1,0:T(8,128)(2,1)}, bf16[2,3104,128]{2,1,0:T(8,128)(2,1)}, u32[]{:S(2)}, u32[]{:S(2)}) collective-permute-start(bf16[2,3104,128]{2,1,0:T(8,128)(2,1)} %pad_maximum_fusion.6.refs_4_.refs_5_.refs_6_.refs_8_.refs_9_.refs_10_.refs_2_.refs_3_.refs_11_), channel_id=1, source_target_pairs={{0,16},{9,25},{2,18},{11,27},{4,20},{13,29},{6,22},{15,31}} | collective-permute-start | bytes 4767752 | tf_op jit(solution)/shard_map/ppermute | solution.py:248
  589.5 5.1 fusion.85
  594.6 5.8 add_convert_fusion
  608.8 7.6 attend_back.2
  616.4 25.0 %collective-permute-done.50 = bf16[2,3104,128]{2,1,0:T(8,128)(2,1)} collective-permute-done((bf16[2,3104,128]{2,1,0:T(8,128)(2,1)}, bf16[2,3104,128]{2,1,0:T(8,128)(2,1)}, u32[]{:S(2)}, u32[]{:S(2)}) %collective-permute-start.50) | collective-permute-done | bytes 1589280 | tf_op jit(solution)/shard_map/ppermute | solution.py:248
  651.8 7.8 attend_back.3
  661.4 7.3 collective-permute-done.52
  696.1 7.7 collective-permute-start.61
  703.8 8.9 %collective-permute-done.59 = bf16[3104,128]{1,0:T(8,128)(2,1)} collective-permute-done((bf16[3104,128]{1,0:T(8,128)(2,1)}, bf16[3104,128]{1,0:T(8,128)(2,1)}, u32[]{:S(2)}, u32[]{:S(2)}) %collective-permute-start.59) | collective-permute-done | bytes 794656 | tf_op jit(solution)/shard_map/ppermute | solution.py:248
  717.4 5.8 collective-permute-start.62
  723.2 5.6 add_add_fusion.4.refs_0_
  737.7 5.4 pack.7
  758.2 13.1 %collective-permute-done.70 = bf16[3104,128]{1,0:T(8,128)(2,1)S(1)} collective-permute-done((bf16[3104,128]{1,0:T(8,128)(2,1)S(1)}, bf16[3104,128]{1,0:T(8,128)(2,1)S(1)}, u32[]{:S(2)}, u32[]{:S(2)}) %collective-permute-start.70) | collective-permute-done | bytes 794656 | tf_op jit(solution)/shard_map/ppermute | solution.py:248
  771.3 16.7 %collective-permute-done.69 = bf16[3104,128]{1,0:T(8,128)(2,1)S(1)} collective-permute-done((bf16[3104,128]{1,0:T(8,128)(2,1)S(1)}, bf16[3104,128]{1,0:T(8,128)(2,1)S(1)}, u32[]{:S(2)}, u32[]{:S(2)}) %collective-permute-start.69) | collective-permute-done | bytes 794656 | tf_op jit(solution)/shard_map/ppermute | solution.py:248
  797.9 5.2 collective-permute-start.65
  810.4 5.9 collective-permute-done.73
  822.0 4.8 fusion.14
  831.3 4.8 collective-permute-start.81
  (784 shorter events, 353.6 us)
Async XLA Ops:
  7.2 207.2 %all-gather.3.cloned.1.call-start = ((), (), s32[]{:S(2)}) async-start(), calls=%async_computation | async-start | bytes 2359296 | tf_op jit(solution)/shard_map/all_gather | solution.py:1541
  18.5 17.1 %collective-permute-start.12 = (bf16[3088,128]{1,0:T(8,128)(2,1)S(1)}, bf16[3088,128]{1,0:T(8,128)(2,1)S(1)}, u32[]{:S(2)}, u32[]{:S(2)}) collective-permute-start(bf16[3088,128]{1,0:T(8,128)(2,1)S(1)} %get-tuple-element.163), channel_id=1, source_target_pairs={{0,8},{9,17},{2,10},{11,19},{4,12},{13,21},{6,14},{15,23}} | collective-permute-start | bytes 2371592 | tf_op jit(solution)/shard_map/ppermute | solution.py:287
  42.3 19.9 %collective-permute-start.25 = (bf16[2,3088,128]{2,1,0:T(8,128)(2,1)}, bf16[2,3088,128]{2,1,0:T(8,128)(2,1)S(1)}, u32[]{:S(2)}, u32[]{:S(2)}) collective-permute-start(bf16[2,3088,128]{2,1,0:T(8,128)(2,1)} %maximum_select_fusion), channel_id=1, source_target_pairs={{16,24},{18,26},{20,28},{22,30}} | collective-permute-start | bytes 4743176 | tf_op jit(solution)/shard_map/ppermute | solution.py:301
  43.8 32.3 %collective-permute-start.26 = (bf16[2,3088,128]{2,1,0:T(8,128)(2,1)}, bf16[2,3088,128]{2,1,0:T(8,128)(2,1)}, u32[]{:S(2)}, u32[]{:S(2)}) collective-permute-start(bf16[2,3088,128]{2,1,0:T(8,128)(2,1)} %collective-permute-done.24), channel_id=1, source_target_pairs={{8,0},{17,9},{10,2},{19,11},{12,4},{21,13},{14,6},{23,15}} | collective-permute-start | bytes 4743176 | tf_op jit(solution)/shard_map/ppermute | solution.py:302
  47.2 30.4 %collective-permute-start.5 = (bf16[3088,128]{1,0:T(8,128)(2,1)S(1)}, bf16[3088,128]{1,0:T(8,128)(2,1)S(1)}, u32[]{:S(2)}, u32[]{:S(2)}) collective-permute-start(bf16[3088,128]{1,0:T(8,128)(2,1)S(1)} %add_select_fusion.2), channel_id=1, source_target_pairs={{0,2},{2,0},{1,3},{3,1},{4,6},{6,4},{5,7},{7,5},{8,10},{10,8},{9,1... | collective-permute-start | bytes 2371592 | tf_op jit(solution)/shard_map/ppermute | solution.py:292
  48.8 40.6 %collective-permute-start.6 = (bf16[3088,128]{1,0:T(8,128)(2,1)S(1)}, bf16[3088,128]{1,0:T(8,128)(2,1)S(1)}, u32[]{:S(2)}, u32[]{:S(2)}) collective-permute-start(bf16[3088,128]{1,0:T(8,128)(2,1)S(1)} %add_select_fusion.2), channel_id=1, source_target_pairs={{0,4},{4,0},{1,5},{5,1},{2,6},{6,2},{3,7},{7,3},{8,12},{12,8},{9,1... | collective-permute-start | bytes 2371592 | tf_op jit(solution)/shard_map/ppermute | solution.py:293
  50.3 39.2 %collective-permute-start.8 = (bf16[3088,128]{1,0:T(8,128)(2,1)S(1)}, bf16[3088,128]{1,0:T(8,128)(2,1)}, u32[]{:S(2)}, u32[]{:S(2)}) collective-permute-start(bf16[3088,128]{1,0:T(8,128)(2,1)S(1)} %add_select_fusion.2), channel_id=1, source_target_pairs={{0,1},{1,0},{2,3},{3,2},{4,5},{5,4},{6,7},{7,6},{8,9},{9,8},{10,11... | collective-permute-start | bytes 2371592 | tf_op jit(solution)/shard_map/ppermute | solution.py:297
  62.2 27.8 %collective-permute-start.16 = (bf16[3088,128]{1,0:T(8,128)(2,1)}, bf16[3088,128]{1,0:T(8,128)(2,1)}, u32[]{:S(2)}, u32[]{:S(2)}) collective-permute-start(bf16[3088,128]{1,0:T(8,128)(2,1)} %add_select_fusion.1), channel_id=1, source_target_pairs={{0,2},{2,0},{1,3},{3,1},{4,6},{6,4},{5,7},{7,5},{8,10},{10,8},{9,1... | collective-permute-start | bytes 2371592 | tf_op jit(solution)/shard_map/ppermute | solution.py:292
  77.6 32.8 %collective-permute-start.27 = (bf16[2,3088,128]{2,1,0:T(8,128)(2,1)}, bf16[2,3088,128]{2,1,0:T(8,128)(2,1)}, u32[]{:S(2)}, u32[]{:S(2)}) collective-permute-start(bf16[2,3088,128]{2,1,0:T(8,128)(2,1)} %collective-permute-done.26), channel_id=1, source_target_pairs={{9,1},{11,3},{13,5},{15,7}} | collective-permute-start | bytes 4743176 | tf_op jit(solution)/shard_map/ppermute | solution.py:303
  89.5 20.1 %collective-permute-start.7 = (bf16[3088,128]{1,0:T(8,128)(2,1)S(1)}, bf16[3088,128]{1,0:T(8,128)(2,1)}, u32[]{:S(2)}, u32[]{:S(2)}) collective-permute-start(bf16[3088,128]{1,0:T(8,128)(2,1)S(1)} %collective-permute-done.5), channel_id=1, source_target_pairs={{0,4},{4,0},{1,5},{5,1},{2,6},{6,2},{3,7},{7,3},{8,12},{12,8},{9,1... | collective-permute-start | bytes 2371592 | tf_op jit(solution)/shard_map/ppermute | solution.py:294
  90.0 19.6 %collective-permute-start.9 = (bf16[3088,128]{1,0:T(8,128)(2,1)S(1)}, bf16[3088,128]{1,0:T(8,128)(2,1)}, u32[]{:S(2)}, u32[]{:S(2)}) collective-permute-start(bf16[3088,128]{1,0:T(8,128)(2,1)S(1)} %collective-permute-done.5), channel_id=1, source_target_pairs={{0,1},{1,0},{2,3},{3,2},{4,5},{5,4},{6,7},{7,6},{8,9},{9,8},{10,11... | collective-permute-start | bytes 2371592 | tf_op jit(solution)/shard_map/ppermute | solution.py:297
  90.2 20.2 %collective-permute-start.18 = (bf16[3088,128]{1,0:T(8,128)(2,1)}, bf16[3088,128]{1,0:T(8,128)(2,1)}, u32[]{:S(2)}, u32[]{:S(2)}) collective-permute-start(bf16[3088,128]{1,0:T(8,128)(2,1)} %collective-permute-done.17), channel_id=1, source_target_pairs={{0,2},{2,0},{1,3},{3,1},{4,6},{6,4},{5,7},{7,5},{8,10},{10,8},{9,1... | collective-permute-start | bytes 2371592 | tf_op jit(solution)/shard_map/ppermute | solution.py:294
  94.2 25.1 %collective-permute-start.21 = (bf16[3088,128]{1,0:T(8,128)(2,1)}, bf16[3088,128]{1,0:T(8,128)(2,1)S(1)}, u32[]{:S(2)}, u32[]{:S(2)}) collective-permute-start(bf16[3088,128]{1,0:T(8,128)(2,1)} %collective-permute-done.17), channel_id=1, source_target_pairs={{0,1},{1,0},{2,3},{3,2},{4,5},{5,4},{6,7},{7,6},{8,9},{9,8},{10,11... | collective-permute-start | bytes 2371592 | tf_op jit(solution)/shard_map/ppermute | solution.py:297
  116.2 40.6 %collective-permute-start.28 = (bf16[2,3088,128]{2,1,0:T(8,128)(2,1)}, bf16[2,3088,128]{2,1,0:T(8,128)(2,1)}, u32[]{:S(2)}, u32[]{:S(2)}) collective-permute-start(bf16[2,3088,128]{2,1,0:T(8,128)(2,1)} %add_select_fusion.refs_1_.refs_6_.refs_18_), channel_id=1, source_target_pairs={{0,2},{2,0},{1,3},{3,1},{4,6},{6,4},{5,7},{7,5},{8,10},{10,8},{9,1... | collective-permute-start | bytes 4743176 | tf_op jit(solution)/shard_map/ppermute | solution.py:248
  117.8 40.5 %collective-permute-start.29 = (bf16[2,3088,128]{2,1,0:T(8,128)(2,1)}, bf16[2,3088,128]{2,1,0:T(8,128)(2,1)}, u32[]{:S(2)}, u32[]{:S(2)}) collective-permute-start(bf16[2,3088,128]{2,1,0:T(8,128)(2,1)} %add_select_fusion.refs_1_.refs_6_.refs_18_), channel_id=1, source_target_pairs={{0,4},{4,0},{1,5},{5,1},{2,6},{6,2},{3,7},{7,3},{8,12},{12,8},{9,1... | collective-permute-start | bytes 4743176 | tf_op jit(solution)/shard_map/ppermute | solution.py:248
  119.3 133.8 %collective-permute-start.35 = (bf16[2,3088,128]{2,1,0:T(8,128)(2,1)}, bf16[2,3088,128]{2,1,0:T(8,128)(2,1)}, u32[]{:S(2)}, u32[]{:S(2)}) collective-permute-start(bf16[2,3088,128]{2,1,0:T(8,128)(2,1)} %add_select_fusion.refs_1_.refs_6_.refs_18_), channel_id=1, source_target_pairs={{0,1},{1,0},{2,3},{3,2},{4,5},{5,4},{6,7},{7,6},{8,9},{9,8},{10,11... | collective-permute-start | bytes 4743176 | tf_op jit(solution)/shard_map/ppermute | solution.py:248
  158.0 25.8 %collective-permute-start.30 = (bf16[1,3088,128]{2,1,0:T(8,128)(2,1)S(1)}, bf16[1,3088,128]{2,1,0:T(8,128)(2,1)}, u32[]{:S(2)}, u32[]{:S(2)}) collective-permute-start(bf16[1,3088,128]{2,1,0:T(8,128)(2,1)S(1)} %slice.346.refs_3_), channel_id=1, source_target_pairs={{0,4},{4,0},{1,5},{5,1},{2,6},{6,2},{3,7},{7,3},{8,12},{12,8},{9,1... | collective-permute-start | bytes 2371592 | tf_op jit(solution)/shard_map/ppermute | solution.py:248
  160.4 23.5 %collective-permute-start.31 = (bf16[1,3088,128]{2,1,0:T(8,128)(2,1)}, bf16[1,3088,128]{2,1,0:T(8,128)(2,1)}, u32[]{:S(2)}, u32[]{:S(2)}) collective-permute-start(bf16[1,3088,128]{2,1,0:T(8,128)(2,1)} %slice.347.refs_4_), channel_id=1, source_target_pairs={{0,2},{2,0},{1,3},{3,1},{4,6},{6,4},{5,7},{7,5},{8,10},{10,8},{9,1... | collective-permute-start | bytes 2371592 | tf_op jit(solution)/shard_map/ppermute | solution.py:248
  187.5 65.6 %collective-permute-start.36 = (bf16[2,3088,128]{2,1,0:T(8,128)(2,1)}, bf16[2,3088,128]{2,1,0:T(8,128)(2,1)}, u32[]{:S(2)}, u32[]{:S(2)}) collective-permute-start(bf16[2,3088,128]{2,1,0:T(8,128)(2,1)} %collective-permute-done.28.refs_2_.refs_7_.refs_19_), channel_id=1, source_target_pairs={{0,1},{1,0},{2,3},{3,2},{4,5},{5,4},{6,7},{7,6},{8,9},{9,8},{10,11... | collective-permute-start | bytes 4743176 | tf_op jit(solution)/shard_map/ppermute | solution.py:248
  187.6 65.6 %collective-permute-start.37 = (bf16[2,3088,128]{2,1,0:T(8,128)(2,1)}, bf16[2,3088,128]{2,1,0:T(8,128)(2,1)}, u32[]{:S(2)}, u32[]{:S(2)}) collective-permute-start(bf16[2,3088,128]{2,1,0:T(8,128)(2,1)} %collective-permute-done.29.refs_3_.refs_8_.refs_20_), channel_id=1, source_target_pairs={{0,1},{1,0},{2,3},{3,2},{4,5},{5,4},{6,7},{7,6},{8,9},{9,8},{10,11... | collective-permute-start | bytes 4743176 | tf_op jit(solution)/shard_map/ppermute | solution.py:248
  188.0 65.1 %collective-permute-start.38 = (bf16[1,3088,128]{2,1,0:T(8,128)(2,1)}, bf16[1,3088,128]{2,1,0:T(8,128)(2,1)}, u32[]{:S(2)}, u32[]{:S(2)}) collective-permute-start(bf16[1,3088,128]{2,1,0:T(8,128)(2,1)} %collective-permute-done.30.refs_4_.refs_9_.refs_21_), channel_id=1, source_target_pairs={{0,1},{1,0},{2,3},{3,2},{4,5},{5,4},{6,7},{7,6},{8,9},{9,8},{10,11... | collective-permute-start | bytes 2371592 | tf_op jit(solution)/shard_map/ppermute | solution.py:248
  207.8 22.8 %collective-permute-start.34 = (bf16[144,1536]{1,0:T(8,128)(2,1)S(1)}, bf16[144,1536]{1,0:T(8,128)(2,1)}, u32[]{:S(2)}, u32[]{:S(2)}) collective-permute-start(bf16[144,1536]{1,0:T(8,128)(2,1)S(1)} %pad_maximum_fusion.16.refs_4_), channel_id=1, source_target_pairs={{0,4},{4,0},{1,5},{5,1},{2,6},{6,2},{3,7},{7,3},{8,12},{12,8},{9,1... | collective-permute-start | bytes 1327112 | tf_op jit(solution)/shard_map/ppermute | solution.py:248
  230.6 23.0 %collective-permute-start.39 = (bf16[1,3088,128]{2,1,0:T(8,128)(2,1)}, bf16[1,3088,128]{2,1,0:T(8,128)(2,1)}, u32[]{:S(2)}, u32[]{:S(2)}) collective-permute-start(bf16[1,3088,128]{2,1,0:T(8,128)(2,1)} %collective-permute-done.31.refs_5_.refs_10_.refs_22_), channel_id=1, source_target_pairs={{0,1},{1,0},{2,3},{3,2},{4,5},{5,4},{6,7},{7,6},{8,9},{9,8},{10,11... | collective-permute-start | bytes 2371592 | tf_op jit(solution)/shard_map/ppermute | solution.py:248
  360.0 30.6 %collective-permute-start.41 = (bf16[144,1536]{1,0:T(8,128)(2,1)S(1)}, bf16[144,1536]{1,0:T(8,128)(2,1)S(1)}, u32[]{:S(2)}, u32[]{:S(2)}) collective-permute-start(bf16[144,1536]{1,0:T(8,128)(2,1)S(1)} %pad_maximum_fusion.18.refs_7_), channel_id=1, source_target_pairs={{0,2},{2,0},{1,3},{3,1},{4,6},{6,4},{5,7},{7,5},{8,10},{10,8},{9,1... | collective-permute-start | bytes 1327112 | tf_op jit(solution)/shard_map/ppermute | solution.py:248
  401.5 30.9 %collective-permute-start.43 = (bf16[24688,128]{1,0:T(8,128)(2,1)}, bf16[24688,128]{1,0:T(8,128)(2,1)}, u32[]{:S(2)}, u32[]{:S(2)}) collective-permute-start(bf16[24688,128]{1,0:T(8,128)(2,1)} %constant_dynamic-slice_fusion.2.refs_2_), channel_id=1, source_target_pairs={{0,1},{1,0},{2,3},{3,2},{4,5},{5,4},{6,7},{7,6},{8,9},{9,8},{10,11... | collective-permute-start | bytes 18960392 | tf_op jit(solution)/shard_map/ppermute | solution.py:248
  405.0 42.4 %collective-permute-start.42 = (bf16[144,1536]{1,0:T(8,128)(2,1)}, bf16[144,1536]{1,0:T(8,128)(2,1)}, u32[]{:S(2)}, u32[]{:S(2)}) collective-permute-start(bf16[144,1536]{1,0:T(8,128)(2,1)} %pad_maximum_fusion.19.refs_1_), channel_id=1, source_target_pairs={{0,4},{4,0},{1,5},{5,1},{2,6},{6,2},{3,7},{7,3},{8,12},{12,8},{9,1... | collective-permute-start | bytes 1327112 | tf_op jit(solution)/shard_map/ppermute | solution.py:248
  441.7 54.7 %collective-permute-start.45 = (bf16[2,3104,128]{2,1,0:T(8,128)(2,1)}, bf16[2,3104,128]{2,1,0:T(8,128)(2,1)}, u32[]{:S(2)}, u32[]{:S(2)}) collective-permute-start(bf16[2,3104,128]{2,1,0:T(8,128)(2,1)} %pad_maximum_fusion.5.refs_12_.refs_2_), channel_id=1, source_target_pairs={{0,2},{2,0},{1,3},{3,1},{4,6},{6,4},{5,7},{7,5},{8,10},{10,8},{9,1... | collective-permute-start | bytes 4767752 | tf_op jit(solution)/shard_map/ppermute | solution.py:248
  453.4 46.6 %collective-permute-start.44 = (bf16[2,3104,128]{2,1,0:T(8,128)(2,1)}, bf16[2,3104,128]{2,1,0:T(8,128)(2,1)}, u32[]{:S(2)}, u32[]{:S(2)}) collective-permute-start(bf16[2,3104,128]{2,1,0:T(8,128)(2,1)} %pad_maximum_fusion.4.refs_11_.refs_1_), channel_id=1, source_target_pairs={{0,4},{4,0},{1,5},{5,1},{2,6},{6,2},{3,7},{7,3},{8,12},{12,8},{9,1... | collective-permute-start | bytes 4767752 | tf_op jit(solution)/shard_map/ppermute | solution.py:248
  499.8 24.2 %collective-permute-start.47 = (bf16[3104,128]{1,0:T(8,128)(2,1)S(1)}, bf16[3104,128]{1,0:T(8,128)(2,1)}, u32[]{:S(2)}, u32[]{:S(2)}) collective-permute-start(bf16[3104,128]{1,0:T(8,128)(2,1)S(1)} %dynamic-slice_bitcast_fusion.11.refs_5_.refs_10_), channel_id=1, source_target_pairs={{0,4},{4,0},{1,5},{5,1},{2,6},{6,2},{3,7},{7,3},{8,12},{12,8},{9,1... | collective-permute-start | bytes 2383880 | tf_op jit(solution)/shard_map/ppermute | solution.py:248
  503.5 22.1 %collective-permute-start.46 = (bf16[3104,128]{1,0:T(8,128)(2,1)}, bf16[3104,128]{1,0:T(8,128)(2,1)}, u32[]{:S(2)}, u32[]{:S(2)}) collective-permute-start(bf16[3104,128]{1,0:T(8,128)(2,1)} %dynamic-slice_bitcast_fusion.14.refs_4_.refs_9_), channel_id=1, source_target_pairs={{0,2},{2,0},{1,3},{3,1},{4,6},{6,4},{5,7},{7,5},{8,10},{10,8},{9,1... | collective-permute-start | bytes 2383880 | tf_op jit(solution)/shard_map/ppermute | solution.py:248
  554.2 40.4 %collective-permute-start.49 = (bf16[24688,128]{1,0:T(8,128)(2,1)}, bf16[24688,128]{1,0:T(8,128)(2,1)}, u32[]{:S(2)}, u32[]{:S(2)}) collective-permute-start(bf16[24688,128]{1,0:T(8,128)(2,1)} %constant_dynamic-slice_fusion.1.refs_1_), channel_id=1, source_target_pairs={{0,1},{1,0},{2,3},{3,2},{4,5},{5,4},{6,7},{7,6},{8,9},{9,8},{10,11... | collective-permute-start | bytes 18960392 | tf_op jit(solution)/shard_map/ppermute | solution.py:248
  566.1 110.2 %collective-permute-start.53 = (bf16[2,3104,128]{2,1,0:T(8,128)(2,1)}, bf16[2,3104,128]{2,1,0:T(8,128)(2,1)}, u32[]{:S(2)}, u32[]{:S(2)}) collective-permute-start(bf16[2,3104,128]{2,1,0:T(8,128)(2,1)} %pad_maximum_fusion.6.refs_4_.refs_5_.refs_6_.refs_8_.refs_9_.refs_10_.refs_2_.refs_3_.refs_11_), channel_id=1, source_target_pairs={{8,16},{17,25},{10,18},{19,27},{12,20},{21,29},{14,22},{23,31}} | collective-permute-start | bytes 4767752 | tf_op jit(solution)/shard_map/ppermute | solution.py:248
  568.1 109.5 %collective-permute-start.54 = (bf16[2,3104,128]{2,1,0:T(8,128)(2,1)}, bf16[2,3104,128]{2,1,0:T(8,128)(2,1)}, u32[]{:S(2)}, u32[]{:S(2)}) collective-permute-start(bf16[2,3104,128]{2,1,0:T(8,128)(2,1)} %pad_maximum_fusion.6.refs_4_.refs_5_.refs_6_.refs_8_.refs_9_.refs_10_.refs_2_.refs_3_.refs_11_), channel_id=1, source_target_pairs={{0,16},{9,25},{2,18},{11,27},{4,20},{13,29},{6,22},{15,31}} | collective-permute-start | bytes 4767752 | tf_op jit(solution)/shard_map/ppermute | solution.py:248
  582.6 96.5 %collective-permute-start.55 = (bf16[2,3104,128]{2,1,0:T(8,128)(2,1)}, bf16[2,3104,128]{2,1,0:T(8,128)(2,1)}, u32[]{:S(2)}, u32[]{:S(2)}) collective-permute-start(bf16[2,3104,128]{2,1,0:T(8,128)(2,1)} %pad_maximum_fusion.6.refs_4_.refs_5_.refs_6_.refs_8_.refs_9_.refs_10_.refs_2_.refs_3_.refs_11_), channel_id=1, source_target_pairs={{24,16},{1,25},{26,18},{3,27},{28,20},{5,29},{30,22},{7,31}} | collective-permute-start | bytes 4767752 | tf_op jit(solution)/shard_map/ppermute | solution.py:248
  603.7 37.7 %collective-permute-start.50 = (bf16[2,3104,128]{2,1,0:T(8,128)(2,1)}, bf16[2,3104,128]{2,1,0:T(8,128)(2,1)}, u32[]{:S(2)}, u32[]{:S(2)}) collective-permute-start(bf16[2,3104,128]{2,1,0:T(8,128)(2,1)} %pad_maximum_fusion.7.refs_1_.refs_7_), channel_id=1, source_target_pairs={{0,4},{4,0},{1,5},{5,1},{2,6},{6,2},{3,7},{7,3},{8,12},{12,8},{9,1... | collective-permute-start | bytes 4767752 | tf_op jit(solution)/shard_map/ppermute | solution.py:248
  606.0 38.3 %collective-permute-start.51 = (bf16[2,3104,128]{2,1,0:T(8,128)(2,1)}, bf16[2,3104,128]{2,1,0:T(8,128)(2,1)}, u32[]{:S(2)}, u32[]{:S(2)}) collective-permute-start(bf16[2,3104,128]{2,1,0:T(8,128)(2,1)} %pad_maximum_fusion.8.refs_2_.refs_8_), channel_id=1, source_target_pairs={{0,2},{2,0},{1,3},{3,1},{4,6},{6,4},{5,7},{7,5},{8,10},{10,8},{9,1... | collective-permute-start | bytes 4767752 | tf_op jit(solution)/shard_map/ppermute | solution.py:248
  648.3 20.4 %collective-permute-start.52 = (bf16[3104,128]{1,0:T(8,128)(2,1)}, bf16[3104,128]{1,0:T(8,128)(2,1)}, u32[]{:S(2)}, u32[]{:S(2)}) collective-permute-start(bf16[3104,128]{1,0:T(8,128)(2,1)} %dynamic-slice_bitcast_fusion.4.refs_2_.refs_7_), channel_id=1, source_target_pairs={{0,2},{2,0},{1,3},{3,1},{4,6},{6,4},{5,7},{7,5},{8,10},{10,8},{9,1... | collective-permute-start | bytes 2383880 | tf_op jit(solution)/shard_map/ppermute | solution.py:248
  650.2 37.4 %collective-permute-start.57 = (bf16[3104,128]{1,0:T(8,128)(2,1)}, bf16[3104,128]{1,0:T(8,128)(2,1)}, u32[]{:S(2)}, u32[]{:S(2)}) collective-permute-start(bf16[3104,128]{1,0:T(8,128)(2,1)} %dynamic-slice_bitcast_fusion.1.refs_3_.refs_8_), channel_id=1, source_target_pairs={{0,4},{4,0},{1,5},{5,1},{2,6},{6,2},{3,7},{7,3},{8,12},{12,8},{9,1... | collective-permute-start | bytes 2383880 | tf_op jit(solution)/shard_map/ppermute | solution.py:248
  671.0 32.8 %collective-permute-start.60 = (bf16[3104,128]{1,0:T(8,128)(2,1)}, bf16[3104,128]{1,0:T(8,128)(2,1)}, u32[]{:S(2)}, u32[]{:S(2)}) collective-permute-start(bf16[3104,128]{1,0:T(8,128)(2,1)} %fusion.20.refs_2_.refs_3_.refs_4_), channel_id=1, source_target_pairs={{24,0},{1,9},{26,2},{3,11},{28,4},{5,13},{30,6},{7,15}} | collective-permute-start | bytes 2383880 | tf_op jit(solution)/shard_map/ppermute | solution.py:248
  676.3 36.4 %collective-permute-start.59 = (bf16[3104,128]{1,0:T(8,128)(2,1)}, bf16[3104,128]{1,0:T(8,128)(2,1)}, u32[]{:S(2)}, u32[]{:S(2)}) collective-permute-start(bf16[3104,128]{1,0:T(8,128)(2,1)} %fusion.20.refs_2_.refs_3_.refs_4_), channel_id=1, source_target_pairs={{16,0},{25,9},{18,2},{27,11},{20,4},{29,13},{22,6},{31,15}} | collective-permute-start | bytes 2383880 | tf_op jit(solution)/shard_map/ppermute | solution.py:248
  677.6 35.1 %collective-permute-start.58 = (bf16[3104,128]{1,0:T(8,128)(2,1)}, bf16[3104,128]{1,0:T(8,128)(2,1)}, u32[]{:S(2)}, u32[]{:S(2)}) collective-permute-start(bf16[3104,128]{1,0:T(8,128)(2,1)} %fusion.20.refs_2_.refs_3_.refs_4_), channel_id=1, source_target_pairs={{8,0},{17,9},{10,2},{19,11},{12,4},{21,13},{14,6},{23,15}} | collective-permute-start | bytes 2383880 | tf_op jit(solution)/shard_map/ppermute | solution.py:248
  696.1 19.9 %collective-permute-start.61 = (bf16[2,2,512,128]{3,2,1,0:T(8,128)(2,1)S(1)}, bf16[2,2,512,128]{3,2,1,0:T(8,128)(2,1)}, u32[]{:S(2)}, u32[]{:S(2)}) collective-permute-start(bf16[2,2,512,128]{3,2,1,0:T(8,128)(2,1)S(1)} %dynamic-slice_bitcast_fusion.21.refs_1_), channel_id=1, source_target_pairs={{0,4},{4,0},{1,5},{5,1},{2,6},{6,2},{3,7},{7,3},{8,12},{12,8},{9,1... | collective-permute-start | bytes 1572872 | tf_op jit(solution)/shard_map/ppermute | solution.py:248
  745.7 106.1 %collective-permute-start.79 = (bf16[3104,128]{1,0:T(8,128)(2,1)}, bf16[3104,128]{1,0:T(8,128)(2,1)}, u32[]{:S(2)}, u32[]{:S(2)}) collective-permute-start(bf16[3104,128]{1,0:T(8,128)(2,1)} %get-tuple-element.162.refs_5_), channel_id=1, source_target_pairs={{0,1},{9,8},{16,17},{25,24},{2,3},{11,10},{18,19},{27,26},{4,5},{1... | collective-permute-start | bytes 2383880 | tf_op jit(solution)/shard_map/ppermute | solution.py:248
  749.1 22.2 %collective-permute-start.70 = (bf16[3104,128]{1,0:T(8,128)(2,1)S(1)}, bf16[3104,128]{1,0:T(8,128)(2,1)S(1)}, u32[]{:S(2)}, u32[]{:S(2)}) collective-permute-start(bf16[3104,128]{1,0:T(8,128)(2,1)S(1)} %copy-done.3), channel_id=1, source_target_pairs={{24,0},{1,9},{26,2},{3,11},{28,4},{5,13},{30,6},{7,15}} | collective-permute-start | bytes 2383880 | tf_op jit(solution)/shard_map/ppermute | solution.py:248
  750.3 37.6 %collective-permute-start.69 = (bf16[3104,128]{1,0:T(8,128)(2,1)S(1)}, bf16[3104,128]{1,0:T(8,128)(2,1)S(1)}, u32[]{:S(2)}, u32[]{:S(2)}) collective-permute-start(bf16[3104,128]{1,0:T(8,128)(2,1)S(1)} %copy-done.3), channel_id=1, source_target_pairs={{16,0},{25,9},{18,2},{27,11},{20,4},{29,13},{22,6},{31,15}} | collective-permute-start | bytes 2383880 | tf_op jit(solution)/shard_map/ppermute | solution.py:248
  751.6 36.3 %collective-permute-start.68 = (bf16[3104,128]{1,0:T(8,128)(2,1)S(1)}, bf16[3104,128]{1,0:T(8,128)(2,1)S(1)}, u32[]{:S(2)}, u32[]{:S(2)}) collective-permute-start(bf16[3104,128]{1,0:T(8,128)(2,1)S(1)} %copy-done.3), channel_id=1, source_target_pairs={{8,0},{17,9},{10,2},{19,11},{12,4},{21,13},{14,6},{23,15}} | collective-permute-start | bytes 2383880 | tf_op jit(solution)/shard_map/ppermute | solution.py:248
  754.4 39.3 %collective-permute-start.66 = (bf16[2,400,128]{2,1,0:T(8,128)(2,1)S(1)}, bf16[2,400,128]{2,1,0:T(8,128)(2,1)S(1)}, u32[]{:S(2)}, u32[]{:S(2)}) collective-permute-start(bf16[2,400,128]{2,1,0:T(8,128)(2,1)S(1)} %dynamic-slice_bitcast_fusion.23), channel_id=1, source_target_pairs={{0,4},{4,0},{1,5},{5,1},{2,6},{6,2},{3,7},{7,3},{8,12},{12,8},{9,1... | collective-permute-start | bytes 614408 | tf_op jit(solution)/shard_map/ppermute | solution.py:248
  789.7 62.1 %collective-permute-start.78 = (bf16[3104,128]{1,0:T(8,128)(2,1)}, bf16[3104,128]{1,0:T(8,128)(2,1)}, u32[]{:S(2)}, u32[]{:S(2)}) collective-permute-start(bf16[3104,128]{1,0:T(8,128)(2,1)} %get-tuple-element.126.refs_1_), channel_id=1, source_target_pairs={{0,1},{9,8},{16,17},{25,24},{2,3},{11,10},{18,19},{27,26},{4,5},{1... | collective-permute-start | bytes 2383880 | tf_op jit(solution)/shard_map/ppermute | solution.py:248
  (221 other events, 2162.3 us)
Sparse Core Ops, SparseCore 0:
  161.7 52.5 all-gather.2

commit v12 on v11

--- a/solution.py
+++ b/solution.py
@@ -1647,7 +1647,13 @@
         (early,) = fence([early], [grad_state_out])
         late_flow.go()
         (early,) = fence([early], late_flow.values())
-        around = lambda call: bracket(call, [late_flow])
+        stats_flow = Flow(plane_stages(squares))
+
+        def around(call):
+            out = bracket(lambda after: call((*after, *stats_flow.values())), [late_flow])
+            stats_flow.go(out[:1])
+            return out
+
     else:
         grad_state_out = scan_states(carry_all, grad_state_local, span, fast, True)
         around = lambda call: call(())
@@ -1767,9 +1773,7 @@
         ((pieces, _, _), *_) = corner_flow.sends
         (pieces,) = fence([pieces], early_flow.values())
         corner_flow.sends = [(pieces, axis, pairs) for _, axis, pairs in corner_flow.sends]
-        stats_flow = Flow(plane_stages(squares))
-        stats_flow.hold([pieces])
-        for flow in (early_flow, late_flow, corner_flow, stats_flow):
+        for flow in (early_flow, late_flow, corner_flow):
             while flow.sends:
                 flow.go()
         stats = jnp.sqrt(stats_flow.result / (all_rows * D))

time: 870 us -> 860 us (0.989)
  waiting for transfers between devices: 158 us -> 145 us
  starting transfers between devices: 182 us -> 193 us
    ppermute x53, starting transfers between devices: 138 us -> 159 us  [go(): lax.ppermute(value, axis, pairs)]
    ppermute x53, waiting for transfers between devices: 110 us -> 93.4 us  [go(): lax.ppermute(value, axis, pairs)]
    ppermute x1, waiting for transfers between devices: 12.3 us -> 22.6 us  [gather_lines(): two = lax.ppermute(one, ZC, zc_pairs((1, 0, 0), (2, 1, 1)))]
    ppermute x8, starting transfers between devices: 10.4 us -> 1.22 us  [gather_lines(): buffers += [lax.ppermute(piece, 'c', SWAP)[None] for piece in local]]
    unnamed x378 -> x375, local copies, waits for them, and re-layouts: 31.9 us -> 34.6 us
  transfers between devices with their start and end apart: 83 -> 83, of which waited for: 25 -> 22; matrix products, arithmetic and copies ran while one was open for 22% -> 21% of each run, Pallas kernels for 17% -> 17%
where the time goes in v12:
time: 860 us; the launch traced here: 852 us
  Pallas kernels  200 us (23%)
  starting transfers between devices  193 us (22%)
  waiting for transfers between devices  145 us (17%)
  other arithmetic  134 us (16%)
  local copies, waits for them, and re-layouts  80.8 us (9%)
  matrix products  80.8 us (9%)
  between operations  18.6 us (2%)
    ppermute x53, starting transfers between devices, go(): lax.ppermute(value, axis, pairs)  159 us
    ppermute x53, waiting for transfers between devices, go(): lax.ppermute(value, axis, pairs)  93.4 us
    dot_general x12, matrix products, matmul_right_t(): lax.dot_general(left, right, (((1,), (1,)), ((), ())), preferred_element_...  47.2 us
    pallas_call x4, Pallas kernels, pack_lines(): pl.pallas_call(pinned(kernel, inputs, after), grid=(total,), in_specs=[le...  42.8 us
    pallas_call x2, Pallas kernels, unpack_lines(): pl.pallas_call(pinned(kernel, 2 + count_buffers, after), grid_spec=pltpu....  41.4 us
    unnamed x375, local copies, waits for them, and re-layouts  34.6 us
    pallas_call x1, Pallas kernels, ssm_backward(): pl.pallas_call(pinned(kernel, 11, after), grid_spec=pltpu.PrefetchScalarG...  33.2 us
    convert_element_type x14, other arithmetic, added(): return total.astype(jnp.bfloat16)  32 us
  transfers between devices with their start and end apart: 83, of which 22 were waited for; matrix products, arithmetic and copies ran while one was open for 21% of the time, Pallas kernels for 17%

profile of v12, /device:TPU:0, one launch (start us, length us, event | category | flops | bytes accessed | tf_op | source)
XLA Modules:
  0.0 851.9 jit_solution(3715609640668991018)
XLA Ops:
  13.1 5.5 collective-permute-start.12
  19.9 7.2 collective-permute-done.12
  53.6 22.6 %collective-permute-done.26 = bf16[2,3088,128]{2,1,0:T(8,128)(2,1)} collective-permute-done((bf16[2,3088,128]{2,1,0:T(8,128)(2,1)}, bf16[2,3088,128]{2,1,0:T(8,128)(2,1)}, u32[]{:S(2)}, u32[]{:S(2)}) %collective-permute-start.26) | collective-permute-done | bytes 1581088 | tf_op jit(solution)/shard_map/ppermute | solution.py:302
  94.5 14.2 %collective-permute-done.18 = bf16[3088,128]{1,0:T(8,128)(2,1)} collective-permute-done((bf16[3088,128]{1,0:T(8,128)(2,1)}, bf16[3088,128]{1,0:T(8,128)(2,1)}, u32[]{:S(2)}, u32[]{:S(2)}) %collective-permute-start.18) | collective-permute-done | bytes 790560 | tf_op jit(solution)/shard_map/ppermute | solution.py:294
  110.3 5.4 add_select_fusion.refs_1_.refs_6_.refs_18_
  119.7 14.9 %unpack.2 = (bf16[1024,512]{1,0:T(8,128)(2,1)}, bf16[1024,128]{1,0:T(8,128)(2,1)S(1)}, bf16[1024,128]{1,0:T(8,128)(2,1)S(1)}, bf16[512,1024]{1,0:T(8,128)(2,1)},...) custom-call(s32[25,5]{1,0:T(8,128)S(1)} %copy-done.62, ...), custom_call_target="tpu_custom_call" | custom-call | bytes 26624000 | tf_op jit(solution)/shard_map/unpack/pallas_call | solution.py:454
  166.5 11.3 %conv.1.refs_0_.refs_1_.x_ref.b_ref.c_ref.refs_3_.refs_4_ = f32[512,1792]{1,0:T(8,128)} custom-call(s32[5]{0:T(128)} %pad_add_fusion.1.refs_0_.meta_ref, f32[512,1792]{1,0:T(8,128)} %pad_maximum_fusion.refs_1_.refs_4_, f32[8,1792]{1,0:T(8,128)} %copy-done.139, f32[4,1792]{1,0:T(4,128)} %reshape.435.refs_3_.refs_6_, f32[1,1792]{1,0:T(1,128)} %bitcast.330, ...), custom_call_target="tpu_custom_call" | custom-call | flops 1000000000 | bytes 7340032 | tf_op jit(solution)/shard_map/conv/pallas_call | solution.py:759
  177.9 8.9 %state.2.refs_0_ = f32[128,1536]{1,0:T(8,128)} custom-call(f32[512,1792]{1,0:T(8,128)} %conv.1.refs_0_.refs_1_.x_ref.b_ref.c_ref.refs_3_.refs_4_, f32[512,1792]{1,0:T(8,128)} %conv.1.refs_0_.refs_1_.x_ref.b_ref.c_ref.refs_3_.refs_4_, f32[12,2,512]{2,1,0:T(2,128)} %reshape.412.refs_2_, bf16[1,3088,128]{2,1,0:T(8,128)(2,1)} %copy-done.116, ...), custom_call_target="tpu_custom_call" | custom-call | flops 201326592 | bytes 3145728 | tf_op jit(solution)/shard_map/state/pallas_call | solution.py:871
  188.0 15.1 %collective-permute-start.32 = (bf16[144,1536]{1,0:T(8,128)(2,1)S(1)}, bf16[144,1536]{1,0:T(8,128)(2,1)}, u32[]{:S(2)}, u32[]{:S(2)}) collective-permute-start(bf16[144,1536]{1,0:T(8,128)(2,1)S(1)} %pad_maximum_fusion.14.refs_1_), channel_id=1, source_target_pairs={{0,1},{1,0},{2,3},{3,2},{4,5},{5,4},{6,7},{7,6},{8,9},{9,8},{10,11... | collective-permute-start | bytes 1327112 | tf_op jit(solution)/shard_map/ppermute | solution.py:248
  214.8 7.1 collective-permute-done.33
  228.0 14.6 %attend.1 = (f32[8,64,512]{2,1,0:T(8,128)S(1)}, f32[8,8,512]{2,1,0:T(8,128)S(1)}) custom-call(s32[4]{0:T(128)S(1)} %pad_add_fusion.refs_0_, bf16[8,128,512]{2,1,0:T(8,128)(2,1)S(1)} %copy-done.24, bf16[8,2,512,128]{3,2,1,0:T(8,128)(2,1)} %bitcast.335, s32[8,512]{1,0:T(8,128)S(1)} %broadcast_in_dim.286.refs_3_.row_ref.refs_10_.refs_6_, ...), custom_call_target="tpu_custom_call" | custom-call | flops 20000000000 | bytes 8388608 | tf_op jit(solution)/shard_map/attend/pallas_call | solution.py:1240
  244.2 4.7 collective-permute-start.39
  254.7 8.5 %ssm.1.refs_28_ = f32[512,1536]{1,0:T(8,128)S(1)} custom-call(s32[5]{0:T(128)S(1)} %copy-done.63, f32[512,1792]{1,0:T(8,128)S(1)} %copy-done, f32[512,1792]{1,0:T(8,128)S(1)} %copy-done, f32[512,1792]{1,0:T(8,128)S(1)} %copy-done, f32[12,2,512]{2,1,0:T(2,128)S(1)} %reshape_reshape.4.cum_ref.refs_5_, f32[12,2,512]{2,1,0:T(2,128)S(1)} %reshape.415.step_ref.refs_6_, ...), custom_call_target="tpu_custom_call" | custom-call | flops 1000000000 | bytes 6291456 | tf_op jit(solution)/shard_map/ssm/pallas_call | solution.py:949
  268.5 26.5 %unpack.3 = (bf16[1536,1024]{1,0:T(8,128)(2,1)}, bf16[1024,2048]{1,0:T(8,128)(2,1)}, bf16[1024,2048]{1,0:T(8,128)(2,1)}, bf16[2048,1024]{1,0:T(8,128)(2,1)}, bf16[16,128]{1,0:T(8,128)(2,1)S(1)}) custom-call(s32[31,5]{1,0:T(8,128)S(1)} %copy-done.61, s32[32]{0:T(128)S(1)} %fusion.78.refs_1_, bf16[1,3088,128]{2,1,0:T(8,128)(2,1)S(1)} %bitcast.267, ...), custom_call_target="tpu_custom_call" | custom-call | bytes 33013760 | tf_op jit(solution)/shard_map/unpack/pallas_call | solution.py:454
  310.4 6.9 fusion.2
  317.4 6.8 fusion.104
  326.6 4.6 multiply_reduce_fusion.3
  337.6 6.4 fusion.23
  344.1 9.1 %state.3 = f32[128,1536]{1,0:T(8,128)} custom-call(f32[512,1792]{1,0:T(8,128)} %conv.1.refs_0_.refs_1_.x_ref.b_ref.c_ref.refs_3_.refs_4_, f32[512,1536]{1,0:T(8,128)} %get-tuple-element.137.refs_1_.refs_2_, f32[12,2,512]{2,1,0:T(2,128)} %reshape.417.refs_2_), custom_call_target="tpu_custom_call" | custom-call | flops 201326592 | bytes 3145728 | tf_op jit(solution)/shard_map/state/pallas_call | solution.py:871
  365.9 8.0 collective-permute-start.41
  373.9 20.5 %pack.4.refs_0_ = bf16[49344,128]{1,0:T(8,128)(2,1)} custom-call(bf16[512,1024]{1,0:T(8,128)(2,1)S(1)} %copy-done.47, bf16[512,2048]{1,0:T(8,128)(2,1)S(1)} %copy-done.67, bf16[512,2048]{1,0:T(8,128)(2,1)} %get-tuple-element.209.refs_2_, bf16[512,2048]{1,0:T(8,128)(2,1)} %get-tuple-element.210.refs_3_, bf16[512,1024]{1,0:T(8,128)(2,1)S(1)} %copy-done.45, ...), custom_call_target="tpu_custom_call" | custom-call | flops 6442450944 | bytes 16777216 | tf_op jit(solution)/shard_map/pack/pallas_call | solution.py:609
  399.0 6.1 constant_dynamic-slice_fusion.2.refs_2_
  407.8 27.0 %collective-permute-start.42 = (bf16[144,1536]{1,0:T(8,128)(2,1)}, bf16[144,1536]{1,0:T(8,128)(2,1)}, u32[]{:S(2)}, u32[]{:S(2)}) collective-permute-start(bf16[144,1536]{1,0:T(8,128)(2,1)} %pad_maximum_fusion.19.refs_1_), channel_id=1, source_target_pairs={{0,4},{4,0},{1,5},{5,1},{2,6},{6,2},{3,7},{7,3},{8,12},{12,8},{9,1... | collective-permute-start | bytes 1327112 | tf_op jit(solution)/shard_map/ppermute | solution.py:248
  437.5 5.8 add_convert_fusion.1
  446.9 5.0 collective-permute-start.44
  451.8 4.7 pack.5.refs_0_
  457.7 9.7 %collective-permute-start.46 = (f32[4]{0:T(128)S(1)}, f32[4]{0:T(128)S(1)}, u32[]{:S(2)}, u32[]{:S(2)}) collective-permute-start(f32[4]{0:T(128)S(1)} %add.637.refs_13_), channel_id=1, source_target_pairs={{0,8},{8,0},{16,24},{24,16},{1,9},{9,1},{17,25},{25,17},{2,10},{10... | collective-permute-start | bytes 56 | tf_op jit(solution)/shard_map/ppermute | solution.py:248
  471.9 33.2 %ssm_back.1 = (f32[512,1536]{1,0:T(8,128)S(1)}, f32[512,128]{1,0:T(8,128)S(1)}, f32[512,128]{1,0:T(8,128)S(1)}, f32[12,8,512]{2,1,0:T(8,128)S(1)}) custom-call(s32[5]{0:T(128)S(1)} %copy-done.63, f32[512,1792]{1,0:T(8,128)} %conv.1.refs_0_.refs_1_.x_ref.b_ref.c_ref.refs_3_.refs_4_, f32[512,1536]{1,0:T(8,128)S(1)} %copy-done.9, ...), custom_call_target="tpu_custom_call" | custom-call | flops 3000000000 | bytes 9437184 | tf_op jit(solution)/shard_map/ssm_back/pallas_call | solution.py:1088
  518.3 12.8 %collective-permute-start.81 = (f32[4]{0:T(128)S(1)}, f32[4]{0:T(128)S(1)}, u32[]{:S(2)}, u32[]{:S(2)}) collective-permute-start(f32[4]{0:T(128)S(1)} %add.653.refs_11_), channel_id=1, source_target_pairs={{0,16},{16,0},{8,24},{24,8},{1,17},{17,1},{9,25},{25,9},{2,18},{18... | collective-permute-start | bytes 56 | tf_op jit(solution)/shard_map/ppermute | solution.py:248
  532.5 14.7 %conv_back.1 = (bf16[512,1792]{1,0:T(8,128)(2,1)}, f32[16,1792]{1,0:T(8,128)}, f32[8,1792]{1,0:T(8,128)}, f32[8,1792]{1,0:T(8,128)}) custom-call(s32[5]{0:T(128)} %pad_add_fusion.1.refs_0_.meta_ref, f32[512,1536]{1,0:T(8,128)} %get-tuple-element.82.refs_1_, f32[512,128]{1,0:T(8,128)} %get-tuple-element.83.refs_2_, f32[512,128]{1,0:T(8,128)} %get-tuple-element.84.refs_3_, ...), custom_call_target="tpu_custom_call" | custom-call | flops 2000000000 | bytes 9175040 | tf_op jit(solution)/shard_map/conv_back/pallas_call | solution.py:818
  560.1 12.1 %pack.6 = bf16[49440,128]{1,0:T(8,128)(2,1)} custom-call(bf16[512,512]{1,0:T(8,128)(2,1)S(1)} %bitcast.278, bf16[512,1024]{1,0:T(8,128)(2,1)S(1)} %copy-done.2, bf16[512,1024]{1,0:T(8,128)(2,1)S(1)} %copy-done.7, bf16[512,1536]{1,0:T(8,128)(2,1)S(1)} %copy-done.17, bf16[512,1536]{1,0:T(8,128)(2,1)S(1)} %slice.373.refs_4_, ...), custom_call_target="tpu_custom_call", output_to_operand_aliasing={{}: (7, {})} | custom-call | flops 4026531840 | bytes 11010048 | tf_op jit(solution)/shard_map/pack/pallas_call | solution.py:609
  572.3 6.0 constant_dynamic-slice_fusion.1.refs_1_
  584.2 5.1 fusion.105
  593.0 5.1 collective-permute-start.55
  605.3 5.0 fusion.85
  610.4 5.8 add_convert_fusion
  624.9 7.6 attend_back.2
  632.5 23.9 %collective-permute-done.51 = bf16[2,3104,128]{2,1,0:T(8,128)(2,1)} collective-permute-done((bf16[2,3104,128]{2,1,0:T(8,128)(2,1)}, bf16[2,3104,128]{2,1,0:T(8,128)(2,1)}, u32[]{:S(2)}, u32[]{:S(2)}) %collective-permute-start.51) | collective-permute-done | bytes 1589280 | tf_op jit(solution)/shard_map/ppermute | solution.py:248
  667.5 8.0 attend_back.3
  706.5 11.6 %collective-permute-start.62 = (bf16[2,2,512,128]{3,2,1,0:T(8,128)(2,1)S(1)}, bf16[2,2,512,128]{3,2,1,0:T(8,128)(2,1)}, u32[]{:S(2)}, u32[]{:S(2)}) collective-permute-start(bf16[2,2,512,128]{3,2,1,0:T(8,128)(2,1)S(1)} %dynamic-slice_bitcast_fusion.21.refs_1_), channel_id=1, source_target_pairs={{0,4},{4,0},{1,5},{5,1},{2,6},{6,2},{3,7},{7,3},{8,12},{12,8},{9,1... | collective-permute-start | bytes 1572872 | tf_op jit(solution)/shard_map/ppermute | solution.py:248
  724.3 6.1 collective-permute-done.62
  731.6 6.0 collective-permute-start.63
  737.6 5.6 add_add_fusion.4.refs_0_
  747.2 4.8 fusion.12
  752.0 5.4 pack.7
  766.1 10.8 %collective-permute-done.69 = bf16[3104,128]{1,0:T(8,128)(2,1)S(1)} collective-permute-done((bf16[3104,128]{1,0:T(8,128)(2,1)S(1)}, bf16[3104,128]{1,0:T(8,128)(2,1)S(1)}, u32[]{:S(2)}, u32[]{:S(2)}) %collective-permute-start.69) | collective-permute-done | bytes 794656 | tf_op jit(solution)/shard_map/ppermute | solution.py:248
  776.9 22.8 %collective-permute-done.70 = bf16[3104,128]{1,0:T(8,128)(2,1)S(1)} collective-permute-done((bf16[3104,128]{1,0:T(8,128)(2,1)S(1)}, bf16[3104,128]{1,0:T(8,128)(2,1)S(1)}, u32[]{:S(2)}, u32[]{:S(2)}) %collective-permute-start.70) | collective-permute-done | bytes 794656 | tf_op jit(solution)/shard_map/ppermute | solution.py:248
  836.0 4.8 fusion.14
  (782 shorter events, 329.1 us)
Async XLA Ops:
  7.2 220.7 %all-gather.3.cloned.1.call-start = ((), (), s32[]{:S(2)}) async-start(), calls=%async_computation | async-start | bytes 2359296 | tf_op jit(solution)/shard_map/all_gather | solution.py:1541
  43.7 32.5 %collective-permute-start.26 = (bf16[2,3088,128]{2,1,0:T(8,128)(2,1)}, bf16[2,3088,128]{2,1,0:T(8,128)(2,1)}, u32[]{:S(2)}, u32[]{:S(2)}) collective-permute-start(bf16[2,3088,128]{2,1,0:T(8,128)(2,1)} %collective-permute-done.24), channel_id=1, source_target_pairs={{8,0},{17,9},{10,2},{19,11},{12,4},{21,13},{14,6},{23,15}} | collective-permute-start | bytes 4743176 | tf_op jit(solution)/shard_map/ppermute | solution.py:302
  48.0 28.2 %collective-permute-start.17 = (bf16[3088,128]{1,0:T(8,128)(2,1)}, bf16[3088,128]{1,0:T(8,128)(2,1)}, u32[]{:S(2)}, u32[]{:S(2)}) collective-permute-start(bf16[3088,128]{1,0:T(8,128)(2,1)} %add_select_fusion.1), channel_id=1, source_target_pairs={{0,4},{4,0},{1,5},{5,1},{2,6},{6,2},{3,7},{7,3},{8,12},{12,8},{9,1... | collective-permute-start | bytes 2371592 | tf_op jit(solution)/shard_map/ppermute | solution.py:293
  49.5 38.8 %collective-permute-start.16 = (bf16[3088,128]{1,0:T(8,128)(2,1)}, bf16[3088,128]{1,0:T(8,128)(2,1)}, u32[]{:S(2)}, u32[]{:S(2)}) collective-permute-start(bf16[3088,128]{1,0:T(8,128)(2,1)} %add_select_fusion.1), channel_id=1, source_target_pairs={{0,2},{2,0},{1,3},{3,1},{4,6},{6,4},{5,7},{7,5},{8,10},{10,8},{9,1... | collective-permute-start | bytes 2371592 | tf_op jit(solution)/shard_map/ppermute | solution.py:292
  52.4 35.8 %collective-permute-start.5 = (bf16[3088,128]{1,0:T(8,128)(2,1)S(1)}, bf16[3088,128]{1,0:T(8,128)(2,1)S(1)}, u32[]{:S(2)}, u32[]{:S(2)}) collective-permute-start(bf16[3088,128]{1,0:T(8,128)(2,1)S(1)} %add_select_fusion.2), channel_id=1, source_target_pairs={{0,2},{2,0},{1,3},{3,1},{4,6},{6,4},{5,7},{7,5},{8,10},{10,8},{9,1... | collective-permute-start | bytes 2371592 | tf_op jit(solution)/shard_map/ppermute | solution.py:292
  53.1 36.9 %collective-permute-start.6 = (bf16[3088,128]{1,0:T(8,128)(2,1)S(1)}, bf16[3088,128]{1,0:T(8,128)(2,1)S(1)}, u32[]{:S(2)}, u32[]{:S(2)}) collective-permute-start(bf16[3088,128]{1,0:T(8,128)(2,1)S(1)} %add_select_fusion.2), channel_id=1, source_target_pairs={{0,4},{4,0},{1,5},{5,1},{2,6},{6,2},{3,7},{7,3},{8,12},{12,8},{9,1... | collective-permute-start | bytes 2371592 | tf_op jit(solution)/shard_map/ppermute | solution.py:293
  76.1 34.1 %collective-permute-start.27 = (bf16[2,3088,128]{2,1,0:T(8,128)(2,1)}, bf16[2,3088,128]{2,1,0:T(8,128)(2,1)}, u32[]{:S(2)}, u32[]{:S(2)}) collective-permute-start(bf16[2,3088,128]{2,1,0:T(8,128)(2,1)} %collective-permute-done.26), channel_id=1, source_target_pairs={{9,1},{11,3},{13,5},{15,7}} | collective-permute-start | bytes 4743176 | tf_op jit(solution)/shard_map/ppermute | solution.py:303
  88.3 20.4 %collective-permute-start.18 = (bf16[3088,128]{1,0:T(8,128)(2,1)}, bf16[3088,128]{1,0:T(8,128)(2,1)}, u32[]{:S(2)}, u32[]{:S(2)}) collective-permute-start(bf16[3088,128]{1,0:T(8,128)(2,1)} %collective-permute-done.17), channel_id=1, source_target_pairs={{0,2},{2,0},{1,3},{3,1},{4,6},{6,4},{5,7},{7,5},{8,10},{10,8},{9,1... | collective-permute-start | bytes 2371592 | tf_op jit(solution)/shard_map/ppermute | solution.py:294
  89.9 19.8 %collective-permute-start.7 = (bf16[3088,128]{1,0:T(8,128)(2,1)S(1)}, bf16[3088,128]{1,0:T(8,128)(2,1)}, u32[]{:S(2)}, u32[]{:S(2)}) collective-permute-start(bf16[3088,128]{1,0:T(8,128)(2,1)S(1)} %collective-permute-done.5), channel_id=1, source_target_pairs={{0,4},{4,0},{1,5},{5,1},{2,6},{6,2},{3,7},{7,3},{8,12},{12,8},{9,1... | collective-permute-start | bytes 2371592 | tf_op jit(solution)/shard_map/ppermute | solution.py:294
  91.4 18.3 %collective-permute-start.21 = (bf16[3088,128]{1,0:T(8,128)(2,1)}, bf16[3088,128]{1,0:T(8,128)(2,1)}, u32[]{:S(2)}, u32[]{:S(2)}) collective-permute-start(bf16[3088,128]{1,0:T(8,128)(2,1)} %collective-permute-done.17), channel_id=1, source_target_pairs={{0,1},{1,0},{2,3},{3,2},{4,5},{5,4},{6,7},{7,6},{8,9},{9,8},{10,11... | collective-permute-start | bytes 2371592 | tf_op jit(solution)/shard_map/ppermute | solution.py:297
  94.0 21.7 %collective-permute-start.9 = (bf16[3088,128]{1,0:T(8,128)(2,1)S(1)}, bf16[3088,128]{1,0:T(8,128)(2,1)S(1)}, u32[]{:S(2)}, u32[]{:S(2)}) collective-permute-start(bf16[3088,128]{1,0:T(8,128)(2,1)S(1)} %collective-permute-done.5), channel_id=1, source_target_pairs={{0,1},{1,0},{2,3},{3,2},{4,5},{5,4},{6,7},{7,6},{8,9},{9,8},{10,11... | collective-permute-start | bytes 2371592 | tf_op jit(solution)/shard_map/ppermute | solution.py:297
  115.7 40.3 %collective-permute-start.28 = (bf16[2,3088,128]{2,1,0:T(8,128)(2,1)}, bf16[2,3088,128]{2,1,0:T(8,128)(2,1)}, u32[]{:S(2)}, u32[]{:S(2)}) collective-permute-start(bf16[2,3088,128]{2,1,0:T(8,128)(2,1)} %add_select_fusion.refs_1_.refs_6_.refs_18_), channel_id=1, source_target_pairs={{0,2},{2,0},{1,3},{3,1},{4,6},{6,4},{5,7},{7,5},{8,10},{10,8},{9,1... | collective-permute-start | bytes 4743176 | tf_op jit(solution)/shard_map/ppermute | solution.py:248
  116.7 41.0 %collective-permute-start.29 = (bf16[2,3088,128]{2,1,0:T(8,128)(2,1)}, bf16[2,3088,128]{2,1,0:T(8,128)(2,1)}, u32[]{:S(2)}, u32[]{:S(2)}) collective-permute-start(bf16[2,3088,128]{2,1,0:T(8,128)(2,1)} %add_select_fusion.refs_1_.refs_6_.refs_18_), channel_id=1, source_target_pairs={{0,4},{4,0},{1,5},{5,1},{2,6},{6,2},{3,7},{7,3},{8,12},{12,8},{9,1... | collective-permute-start | bytes 4743176 | tf_op jit(solution)/shard_map/ppermute | solution.py:248
  118.2 147.1 %collective-permute-start.35 = (bf16[2,3088,128]{2,1,0:T(8,128)(2,1)}, bf16[2,3088,128]{2,1,0:T(8,128)(2,1)}, u32[]{:S(2)}, u32[]{:S(2)}) collective-permute-start(bf16[2,3088,128]{2,1,0:T(8,128)(2,1)} %add_select_fusion.refs_1_.refs_6_.refs_18_), channel_id=1, source_target_pairs={{0,1},{1,0},{2,3},{3,2},{4,5},{5,4},{6,7},{7,6},{8,9},{9,8},{10,11... | collective-permute-start | bytes 4743176 | tf_op jit(solution)/shard_map/ppermute | solution.py:248
  157.2 29.5 %collective-permute-start.30 = (bf16[1,3088,128]{2,1,0:T(8,128)(2,1)S(1)}, bf16[1,3088,128]{2,1,0:T(8,128)(2,1)}, u32[]{:S(2)}, u32[]{:S(2)}) collective-permute-start(bf16[1,3088,128]{2,1,0:T(8,128)(2,1)S(1)} %slice.346.refs_3_), channel_id=1, source_target_pairs={{0,4},{4,0},{1,5},{5,1},{2,6},{6,2},{3,7},{7,3},{8,12},{12,8},{9,1... | collective-permute-start | bytes 2371592 | tf_op jit(solution)/shard_map/ppermute | solution.py:248
  159.8 27.0 %collective-permute-start.31 = (bf16[1,3088,128]{2,1,0:T(8,128)(2,1)}, bf16[1,3088,128]{2,1,0:T(8,128)(2,1)}, u32[]{:S(2)}, u32[]{:S(2)}) collective-permute-start(bf16[1,3088,128]{2,1,0:T(8,128)(2,1)} %slice.347.refs_4_), channel_id=1, source_target_pairs={{0,2},{2,0},{1,3},{3,1},{4,6},{6,4},{5,7},{7,5},{8,10},{10,8},{9,1... | collective-permute-start | bytes 2371592 | tf_op jit(solution)/shard_map/ppermute | solution.py:248
  188.0 18.4 %collective-permute-start.32 = (bf16[144,1536]{1,0:T(8,128)(2,1)S(1)}, bf16[144,1536]{1,0:T(8,128)(2,1)}, u32[]{:S(2)}, u32[]{:S(2)}) collective-permute-start(bf16[144,1536]{1,0:T(8,128)(2,1)S(1)} %pad_maximum_fusion.14.refs_1_), channel_id=1, source_target_pairs={{0,1},{1,0},{2,3},{3,2},{4,5},{5,4},{6,7},{7,6},{8,9},{9,8},{10,11... | collective-permute-start | bytes 1327112 | tf_op jit(solution)/shard_map/ppermute | solution.py:248
  205.6 59.7 %collective-permute-start.36 = (bf16[2,3088,128]{2,1,0:T(8,128)(2,1)}, bf16[2,3088,128]{2,1,0:T(8,128)(2,1)}, u32[]{:S(2)}, u32[]{:S(2)}) collective-permute-start(bf16[2,3088,128]{2,1,0:T(8,128)(2,1)} %collective-permute-done.28.refs_2_.refs_7_.refs_19_), channel_id=1, source_target_pairs={{0,1},{1,0},{2,3},{3,2},{4,5},{5,4},{6,7},{7,6},{8,9},{9,8},{10,11... | collective-permute-start | bytes 4743176 | tf_op jit(solution)/shard_map/ppermute | solution.py:248
  205.9 59.5 %collective-permute-start.37 = (bf16[2,3088,128]{2,1,0:T(8,128)(2,1)}, bf16[2,3088,128]{2,1,0:T(8,128)(2,1)}, u32[]{:S(2)}, u32[]{:S(2)}) collective-permute-start(bf16[2,3088,128]{2,1,0:T(8,128)(2,1)} %collective-permute-done.29.refs_3_.refs_8_.refs_20_), channel_id=1, source_target_pairs={{0,1},{1,0},{2,3},{3,2},{4,5},{5,4},{6,7},{7,6},{8,9},{9,8},{10,11... | collective-permute-start | bytes 4743176 | tf_op jit(solution)/shard_map/ppermute | solution.py:248
  206.1 59.2 %collective-permute-start.38 = (bf16[1,3088,128]{2,1,0:T(8,128)(2,1)}, bf16[1,3088,128]{2,1,0:T(8,128)(2,1)}, u32[]{:S(2)}, u32[]{:S(2)}) collective-permute-start(bf16[1,3088,128]{2,1,0:T(8,128)(2,1)} %collective-permute-done.30.refs_4_.refs_9_.refs_21_), channel_id=1, source_target_pairs={{0,1},{1,0},{2,3},{3,2},{4,5},{5,4},{6,7},{7,6},{8,9},{9,8},{10,11... | collective-permute-start | bytes 2371592 | tf_op jit(solution)/shard_map/ppermute | solution.py:248
  224.8 19.4 %collective-permute-start.34 = (bf16[144,1536]{1,0:T(8,128)(2,1)S(1)}, bf16[144,1536]{1,0:T(8,128)(2,1)}, u32[]{:S(2)}, u32[]{:S(2)}) collective-permute-start(bf16[144,1536]{1,0:T(8,128)(2,1)S(1)} %pad_maximum_fusion.16.refs_4_), channel_id=1, source_target_pairs={{0,4},{4,0},{1,5},{5,1},{2,6},{6,2},{3,7},{7,3},{8,12},{12,8},{9,1... | collective-permute-start | bytes 1327112 | tf_op jit(solution)/shard_map/ppermute | solution.py:248
  244.2 21.1 %collective-permute-start.39 = (bf16[1,3088,128]{2,1,0:T(8,128)(2,1)}, bf16[1,3088,128]{2,1,0:T(8,128)(2,1)}, u32[]{:S(2)}, u32[]{:S(2)}) collective-permute-start(bf16[1,3088,128]{2,1,0:T(8,128)(2,1)} %collective-permute-done.31.refs_5_.refs_10_.refs_22_), channel_id=1, source_target_pairs={{0,1},{1,0},{2,3},{3,2},{4,5},{5,4},{6,7},{7,6},{8,9},{9,8},{10,11... | collective-permute-start | bytes 2371592 | tf_op jit(solution)/shard_map/ppermute | solution.py:248
  365.9 28.5 %collective-permute-start.41 = (bf16[144,1536]{1,0:T(8,128)(2,1)S(1)}, bf16[144,1536]{1,0:T(8,128)(2,1)S(1)}, u32[]{:S(2)}, u32[]{:S(2)}) collective-permute-start(bf16[144,1536]{1,0:T(8,128)(2,1)S(1)} %pad_maximum_fusion.18.refs_7_), channel_id=1, source_target_pairs={{0,2},{2,0},{1,3},{3,1},{4,6},{6,4},{5,7},{7,5},{8,10},{10,8},{9,1... | collective-permute-start | bytes 1327112 | tf_op jit(solution)/shard_map/ppermute | solution.py:248
  405.0 32.5 %collective-permute-start.43 = (bf16[24688,128]{1,0:T(8,128)(2,1)}, bf16[24688,128]{1,0:T(8,128)(2,1)}, u32[]{:S(2)}, u32[]{:S(2)}) collective-permute-start(bf16[24688,128]{1,0:T(8,128)(2,1)} %constant_dynamic-slice_fusion.2.refs_2_), channel_id=1, source_target_pairs={{0,1},{1,0},{2,3},{3,2},{4,5},{5,4},{6,7},{7,6},{8,9},{9,8},{10,11... | collective-permute-start | bytes 18960392 | tf_op jit(solution)/shard_map/ppermute | solution.py:248
  407.8 48.8 %collective-permute-start.42 = (bf16[144,1536]{1,0:T(8,128)(2,1)}, bf16[144,1536]{1,0:T(8,128)(2,1)}, u32[]{:S(2)}, u32[]{:S(2)}) collective-permute-start(bf16[144,1536]{1,0:T(8,128)(2,1)} %pad_maximum_fusion.19.refs_1_), channel_id=1, source_target_pairs={{0,4},{4,0},{1,5},{5,1},{2,6},{6,2},{3,7},{7,3},{8,12},{12,8},{9,1... | collective-permute-start | bytes 1327112 | tf_op jit(solution)/shard_map/ppermute | solution.py:248
  446.9 62.0 %collective-permute-start.44 = (bf16[2,3104,128]{2,1,0:T(8,128)(2,1)}, bf16[2,3104,128]{2,1,0:T(8,128)(2,1)}, u32[]{:S(2)}, u32[]{:S(2)}) collective-permute-start(bf16[2,3104,128]{2,1,0:T(8,128)(2,1)} %pad_maximum_fusion.4.refs_11_.refs_1_), channel_id=1, source_target_pairs={{0,4},{4,0},{1,5},{5,1},{2,6},{6,2},{3,7},{7,3},{8,12},{12,8},{9,1... | collective-permute-start | bytes 4767752 | tf_op jit(solution)/shard_map/ppermute | solution.py:248
  457.7 59.4 %collective-permute-start.46 = (f32[4]{0:T(128)S(1)}, f32[4]{0:T(128)S(1)}, u32[]{:S(2)}, u32[]{:S(2)}) collective-permute-start(f32[4]{0:T(128)S(1)} %add.637.refs_13_), channel_id=1, source_target_pairs={{0,8},{8,0},{16,24},{24,16},{1,9},{9,1},{17,25},{25,17},{2,10},{10... | collective-permute-start | bytes 56 | tf_op jit(solution)/shard_map/ppermute | solution.py:248
  471.4 42.4 %collective-permute-start.45 = (bf16[2,3104,128]{2,1,0:T(8,128)(2,1)}, bf16[2,3104,128]{2,1,0:T(8,128)(2,1)}, u32[]{:S(2)}, u32[]{:S(2)}) collective-permute-start(bf16[2,3104,128]{2,1,0:T(8,128)(2,1)} %pad_maximum_fusion.5.refs_12_.refs_2_), channel_id=1, source_target_pairs={{0,2},{2,0},{1,3},{3,1},{4,6},{6,4},{5,7},{7,5},{8,10},{10,8},{9,1... | collective-permute-start | bytes 4767752 | tf_op jit(solution)/shard_map/ppermute | solution.py:248
  512.3 35.8 %collective-permute-start.47 = (bf16[3104,128]{1,0:T(8,128)(2,1)}, bf16[3104,128]{1,0:T(8,128)(2,1)}, u32[]{:S(2)}, u32[]{:S(2)}) collective-permute-start(bf16[3104,128]{1,0:T(8,128)(2,1)} %dynamic-slice_bitcast_fusion.14.refs_4_.refs_9_), channel_id=1, source_target_pairs={{0,2},{2,0},{1,3},{3,1},{4,6},{6,4},{5,7},{7,5},{8,10},{10,8},{9,1... | collective-permute-start | bytes 2383880 | tf_op jit(solution)/shard_map/ppermute | solution.py:248
  517.1 32.6 %collective-permute-start.48 = (bf16[3104,128]{1,0:T(8,128)(2,1)}, bf16[3104,128]{1,0:T(8,128)(2,1)}, u32[]{:S(2)}, u32[]{:S(2)}) collective-permute-start(bf16[3104,128]{1,0:T(8,128)(2,1)} %dynamic-slice_bitcast_fusion.11.refs_5_.refs_10_), channel_id=1, source_target_pairs={{0,4},{4,0},{1,5},{5,1},{2,6},{6,2},{3,7},{7,3},{8,12},{12,8},{9,1... | collective-permute-start | bytes 2383880 | tf_op jit(solution)/shard_map/ppermute | solution.py:248
  518.3 36.8 %collective-permute-start.81 = (f32[4]{0:T(128)S(1)}, f32[4]{0:T(128)S(1)}, u32[]{:S(2)}, u32[]{:S(2)}) collective-permute-start(f32[4]{0:T(128)S(1)} %add.653.refs_11_), channel_id=1, source_target_pairs={{0,16},{16,0},{8,24},{24,8},{1,17},{17,1},{9,25},{25,9},{2,18},{18... | collective-permute-start | bytes 56 | tf_op jit(solution)/shard_map/ppermute | solution.py:248
  578.2 32.1 %collective-permute-start.50 = (bf16[24688,128]{1,0:T(8,128)(2,1)}, bf16[24688,128]{1,0:T(8,128)(2,1)}, u32[]{:S(2)}, u32[]{:S(2)}) collective-permute-start(bf16[24688,128]{1,0:T(8,128)(2,1)} %constant_dynamic-slice_fusion.1.refs_1_), channel_id=1, source_target_pairs={{0,1},{1,0},{2,3},{3,2},{4,5},{5,4},{6,7},{7,6},{8,9},{9,8},{10,11... | collective-permute-start | bytes 18960392 | tf_op jit(solution)/shard_map/ppermute | solution.py:248
  591.1 95.9 %collective-permute-start.54 = (bf16[2,3104,128]{2,1,0:T(8,128)(2,1)}, bf16[2,3104,128]{2,1,0:T(8,128)(2,1)}, u32[]{:S(2)}, u32[]{:S(2)}) collective-permute-start(bf16[2,3104,128]{2,1,0:T(8,128)(2,1)} %pad_maximum_fusion.6.refs_4_.refs_5_.refs_6_.refs_8_.refs_9_.refs_10_.refs_2_.refs_3_.refs_11_), channel_id=1, source_target_pairs={{8,16},{17,25},{10,18},{19,27},{12,20},{21,29},{14,22},{23,31}} | collective-permute-start | bytes 4767752 | tf_op jit(solution)/shard_map/ppermute | solution.py:248
  593.0 95.3 %collective-permute-start.55 = (bf16[2,3104,128]{2,1,0:T(8,128)(2,1)}, bf16[2,3104,128]{2,1,0:T(8,128)(2,1)}, u32[]{:S(2)}, u32[]{:S(2)}) collective-permute-start(bf16[2,3104,128]{2,1,0:T(8,128)(2,1)} %pad_maximum_fusion.6.refs_4_.refs_5_.refs_6_.refs_8_.refs_9_.refs_10_.refs_2_.refs_3_.refs_11_), channel_id=1, source_target_pairs={{0,16},{9,25},{2,18},{11,27},{4,20},{13,29},{6,22},{15,31}} | collective-permute-start | bytes 4767752 | tf_op jit(solution)/shard_map/ppermute | solution.py:248
  598.2 91.7 %collective-permute-start.56 = (bf16[2,3104,128]{2,1,0:T(8,128)(2,1)}, bf16[2,3104,128]{2,1,0:T(8,128)(2,1)}, u32[]{:S(2)}, u32[]{:S(2)}) collective-permute-start(bf16[2,3104,128]{2,1,0:T(8,128)(2,1)} %pad_maximum_fusion.6.refs_4_.refs_5_.refs_6_.refs_8_.refs_9_.refs_10_.refs_2_.refs_3_.refs_11_), channel_id=1, source_target_pairs={{24,16},{1,25},{26,18},{3,27},{28,20},{5,29},{30,22},{7,31}} | collective-permute-start | bytes 4767752 | tf_op jit(solution)/shard_map/ppermute | solution.py:248
  619.4 37.1 %collective-permute-start.51 = (bf16[2,3104,128]{2,1,0:T(8,128)(2,1)}, bf16[2,3104,128]{2,1,0:T(8,128)(2,1)}, u32[]{:S(2)}, u32[]{:S(2)}) collective-permute-start(bf16[2,3104,128]{2,1,0:T(8,128)(2,1)} %pad_maximum_fusion.7.refs_1_.refs_7_), channel_id=1, source_target_pairs={{0,4},{4,0},{1,5},{5,1},{2,6},{6,2},{3,7},{7,3},{8,12},{12,8},{9,1... | collective-permute-start | bytes 4767752 | tf_op jit(solution)/shard_map/ppermute | solution.py:248
  622.2 39.8 %collective-permute-start.52 = (bf16[2,3104,128]{2,1,0:T(8,128)(2,1)}, bf16[2,3104,128]{2,1,0:T(8,128)(2,1)}, u32[]{:S(2)}, u32[]{:S(2)}) collective-permute-start(bf16[2,3104,128]{2,1,0:T(8,128)(2,1)} %pad_maximum_fusion.8.refs_2_.refs_8_), channel_id=1, source_target_pairs={{0,2},{2,0},{1,3},{3,1},{4,6},{6,4},{5,7},{7,5},{8,10},{10,8},{9,1... | collective-permute-start | bytes 4767752 | tf_op jit(solution)/shard_map/ppermute | solution.py:248
  659.5 20.0 %collective-permute-start.53 = (bf16[3104,128]{1,0:T(8,128)(2,1)}, bf16[3104,128]{1,0:T(8,128)(2,1)}, u32[]{:S(2)}, u32[]{:S(2)}) collective-permute-start(bf16[3104,128]{1,0:T(8,128)(2,1)} %dynamic-slice_bitcast_fusion.4.refs_2_.refs_7_), channel_id=1, source_target_pairs={{0,2},{2,0},{1,3},{3,1},{4,6},{6,4},{5,7},{7,5},{8,10},{10,8},{9,1... | collective-permute-start | bytes 2383880 | tf_op jit(solution)/shard_map/ppermute | solution.py:248
  665.9 32.1 %collective-permute-start.58 = (bf16[3104,128]{1,0:T(8,128)(2,1)}, bf16[3104,128]{1,0:T(8,128)(2,1)}, u32[]{:S(2)}, u32[]{:S(2)}) collective-permute-start(bf16[3104,128]{1,0:T(8,128)(2,1)} %dynamic-slice_bitcast_fusion.1.refs_3_.refs_8_), channel_id=1, source_target_pairs={{0,4},{4,0},{1,5},{5,1},{2,6},{6,2},{3,7},{7,3},{8,12},{12,8},{9,1... | collective-permute-start | bytes 2383880 | tf_op jit(solution)/shard_map/ppermute | solution.py:248
  681.7 36.4 %collective-permute-start.59 = (bf16[3104,128]{1,0:T(8,128)(2,1)}, bf16[3104,128]{1,0:T(8,128)(2,1)}, u32[]{:S(2)}, u32[]{:S(2)}) collective-permute-start(bf16[3104,128]{1,0:T(8,128)(2,1)} %fusion.20.refs_2_.refs_3_.refs_4_), channel_id=1, source_target_pairs={{8,0},{17,9},{10,2},{19,11},{12,4},{21,13},{14,6},{23,15}} | collective-permute-start | bytes 2383880 | tf_op jit(solution)/shard_map/ppermute | solution.py:248
  687.0 34.1 %collective-permute-start.60 = (bf16[3104,128]{1,0:T(8,128)(2,1)}, bf16[3104,128]{1,0:T(8,128)(2,1)}, u32[]{:S(2)}, u32[]{:S(2)}) collective-permute-start(bf16[3104,128]{1,0:T(8,128)(2,1)} %fusion.20.refs_2_.refs_3_.refs_4_), channel_id=1, source_target_pairs={{16,0},{25,9},{18,2},{27,11},{20,4},{29,13},{22,6},{31,15}} | collective-permute-start | bytes 2383880 | tf_op jit(solution)/shard_map/ppermute | solution.py:248
  688.3 32.8 %collective-permute-start.61 = (bf16[3104,128]{1,0:T(8,128)(2,1)}, bf16[3104,128]{1,0:T(8,128)(2,1)}, u32[]{:S(2)}, u32[]{:S(2)}) collective-permute-start(bf16[3104,128]{1,0:T(8,128)(2,1)} %fusion.20.refs_2_.refs_3_.refs_4_), channel_id=1, source_target_pairs={{24,0},{1,9},{26,2},{3,11},{28,4},{5,13},{30,6},{7,15}} | collective-permute-start | bytes 2383880 | tf_op jit(solution)/shard_map/ppermute | solution.py:248
  706.5 23.8 %collective-permute-start.62 = (bf16[2,2,512,128]{3,2,1,0:T(8,128)(2,1)S(1)}, bf16[2,2,512,128]{3,2,1,0:T(8,128)(2,1)}, u32[]{:S(2)}, u32[]{:S(2)}) collective-permute-start(bf16[2,2,512,128]{3,2,1,0:T(8,128)(2,1)S(1)} %dynamic-slice_bitcast_fusion.21.refs_1_), channel_id=1, source_target_pairs={{0,4},{4,0},{1,5},{5,1},{2,6},{6,2},{3,7},{7,3},{8,12},{12,8},{9,1... | collective-permute-start | bytes 1572872 | tf_op jit(solution)/shard_map/ppermute | solution.py:248
  760.2 39.5 %collective-permute-start.70 = (bf16[3104,128]{1,0:T(8,128)(2,1)S(1)}, bf16[3104,128]{1,0:T(8,128)(2,1)S(1)}, u32[]{:S(2)}, u32[]{:S(2)}) collective-permute-start(bf16[3104,128]{1,0:T(8,128)(2,1)S(1)} %copy-done.3), channel_id=1, source_target_pairs={{16,0},{25,9},{18,2},{27,11},{20,4},{29,13},{22,6},{31,15}} | collective-permute-start | bytes 2383880 | tf_op jit(solution)/shard_map/ppermute | solution.py:248
  761.5 38.2 %collective-permute-start.71 = (bf16[3104,128]{1,0:T(8,128)(2,1)S(1)}, bf16[3104,128]{1,0:T(8,128)(2,1)S(1)}, u32[]{:S(2)}, u32[]{:S(2)}) collective-permute-start(bf16[3104,128]{1,0:T(8,128)(2,1)S(1)} %copy-done.3), channel_id=1, source_target_pairs={{24,0},{1,9},{26,2},{3,11},{28,4},{5,13},{30,6},{7,15}} | collective-permute-start | bytes 2383880 | tf_op jit(solution)/shard_map/ppermute | solution.py:248
  764.3 40.2 %collective-permute-start.65 = (bf16[2,400,128]{2,1,0:T(8,128)(2,1)S(1)}, bf16[2,400,128]{2,1,0:T(8,128)(2,1)S(1)}, u32[]{:S(2)}, u32[]{:S(2)}) collective-permute-start(bf16[2,400,128]{2,1,0:T(8,128)(2,1)S(1)} %dynamic-slice_bitcast_fusion.24), channel_id=1, source_target_pairs={{0,2},{2,0},{1,3},{3,1},{4,6},{6,4},{5,7},{7,5},{8,10},{10,8},{9,1... | collective-permute-start | bytes 614408 | tf_op jit(solution)/shard_map/ppermute | solution.py:248
  818.5 23.8 %collective-permute-start.80 = (bf16[3104,128]{1,0:T(8,128)(2,1)}, bf16[3104,128]{1,0:T(8,128)(2,1)S(1)}, u32[]{:S(2)}, u32[]{:S(2)}) collective-permute-start(bf16[3104,128]{1,0:T(8,128)(2,1)} %get-tuple-element.162.refs_5_), channel_id=1, source_target_pairs={{0,1},{9,8},{16,17},{25,24},{2,3},{11,10},{18,19},{27,26},{4,5},{1... | collective-permute-start | bytes 2383880 | tf_op jit(solution)/shard_map/ppermute | solution.py:248
  819.8 22.4 %collective-permute-start.79 = (bf16[3104,128]{1,0:T(8,128)(2,1)}, bf16[3104,128]{1,0:T(8,128)(2,1)S(1)}, u32[]{:S(2)}, u32[]{:S(2)}) collective-permute-start(bf16[3104,128]{1,0:T(8,128)(2,1)} %get-tuple-element.126.refs_1_), channel_id=1, source_target_pairs={{0,1},{9,8},{16,17},{25,24},{2,3},{11,10},{18,19},{27,26},{4,5},{1... | collective-permute-start | bytes 2383880 | tf_op jit(solution)/shard_map/ppermute | solution.py:248
  (220 other events, 2352.8 us)
Sparse Core Ops, SparseCore 0:
  147.7 44.0 all-gather.2

commit v13 on v12

--- a/solution.py
+++ b/solution.py
@@ -1769,7 +1769,7 @@
         corner_flow = Flow(corner_stages(corner))
         for _ in range(3):
             corner_flow.go()
-        early_flow.go()
+        early_flow.go(corner_flow.values()[:1])
         ((pieces, _, _), *_) = corner_flow.sends
         (pieces,) = fence([pieces], early_flow.values())
         corner_flow.sends = [(pieces, axis, pairs) for _, axis, pairs in corner_flow.sends]

time: 860 us -> 857 us (level)
  waiting for transfers between devices: 145 us -> 133 us
    ppermute x53, waiting for transfers between devices: 93.4 us -> 81.7 us  [go(): lax.ppermute(value, axis, pairs)]
    unnamed x375 -> x383, local copies, waits for them, and re-layouts: 34.6 us -> 36.3 us
  transfers between devices with their start and end apart: 83 -> 83, of which waited for: 22 -> 23; matrix products, arithmetic and copies ran while one was open for 21% -> 21% of each run, Pallas kernels for 17% -> 17%
where the time goes in v13:
time: 857 us; the launch traced here: 849 us
  Pallas kernels  200 us (23%)
  starting transfers between devices  196 us (23%)
  other arithmetic  138 us (16%)
  waiting for transfers between devices  133 us (16%)
  local copies, waits for them, and re-layouts  82.6 us (10%)
  matrix products  80.9 us (9%)
  between operations  18.5 us (2%)
    ppermute x53, starting transfers between devices, go(): lax.ppermute(value, axis, pairs)  163 us
    ppermute x53, waiting for transfers between devices, go(): lax.ppermute(value, axis, pairs)  81.7 us
    dot_general x12, matrix products, matmul_right_t(): lax.dot_general(left, right, (((1,), (1,)), ((), ())), preferred_element_...  47.3 us
    pallas_call x4, Pallas kernels, pack_lines(): pl.pallas_call(pinned(kernel, inputs, after), grid=(total,), in_specs=[le...  42.8 us
    pallas_call x2, Pallas kernels, unpack_lines(): pl.pallas_call(pinned(kernel, 2 + count_buffers, after), grid_spec=pltpu....  41.4 us
    unnamed x383, local copies, waits for them, and re-layouts  36.3 us
    convert_element_type x14, other arithmetic, added(): return total.astype(jnp.bfloat16)  33.9 us
    pallas_call x1, Pallas kernels, ssm_backward(): pl.pallas_call(pinned(kernel, 11, after), grid_spec=pltpu.PrefetchScalarG...  33.2 us
  transfers between devices with their start and end apart: 83, of which 23 were waited for; matrix products, arithmetic and copies ran while one was open for 21% of the time, Pallas kernels for 17%

profile of v13, /device:TPU:0, one launch (start us, length us, event | category | flops | bytes accessed | tf_op | source)
XLA Modules:
  0.0 848.9 jit_solution(2991594662309973983)
XLA Ops:
  13.1 5.5 collective-permute-start.12
  19.9 7.3 collective-permute-done.12
  53.8 22.3 %collective-permute-done.26 = bf16[2,3088,128]{2,1,0:T(8,128)(2,1)} collective-permute-done((bf16[2,3088,128]{2,1,0:T(8,128)(2,1)}, bf16[2,3088,128]{2,1,0:T(8,128)(2,1)}, u32[]{:S(2)}, u32[]{:S(2)}) %collective-permute-start.26) | collective-permute-done | bytes 1581088 | tf_op jit(solution)/shard_map/ppermute | solution.py:302
  94.6 14.2 %collective-permute-done.18 = bf16[3088,128]{1,0:T(8,128)(2,1)} collective-permute-done((bf16[3088,128]{1,0:T(8,128)(2,1)}, bf16[3088,128]{1,0:T(8,128)(2,1)}, u32[]{:S(2)}, u32[]{:S(2)}) %collective-permute-start.18) | collective-permute-done | bytes 790560 | tf_op jit(solution)/shard_map/ppermute | solution.py:294
  110.4 5.4 add_select_fusion.refs_1_.refs_6_.refs_18_
  119.8 14.9 %unpack.2 = (bf16[1024,512]{1,0:T(8,128)(2,1)}, bf16[1024,128]{1,0:T(8,128)(2,1)S(1)}, bf16[1024,128]{1,0:T(8,128)(2,1)S(1)}, bf16[512,1024]{1,0:T(8,128)(2,1)},...) custom-call(s32[25,5]{1,0:T(8,128)S(1)} %copy-done.62, ...), custom_call_target="tpu_custom_call" | custom-call | bytes 26624000 | tf_op jit(solution)/shard_map/unpack/pallas_call | solution.py:454
  166.6 11.3 %conv.1.refs_0_.refs_1_.x_ref.b_ref.c_ref.refs_3_.refs_4_ = f32[512,1792]{1,0:T(8,128)} custom-call(s32[5]{0:T(128)} %pad_add_fusion.1.refs_0_.meta_ref, f32[512,1792]{1,0:T(8,128)} %pad_maximum_fusion.refs_1_.refs_4_, f32[8,1792]{1,0:T(8,128)} %copy-done.143, f32[4,1792]{1,0:T(4,128)} %reshape.435.refs_3_.refs_6_, f32[1,1792]{1,0:T(1,128)} %bitcast.330, ...), custom_call_target="tpu_custom_call" | custom-call | flops 1000000000 | bytes 7340032 | tf_op jit(solution)/shard_map/conv/pallas_call | solution.py:759
  177.9 8.8 %state.2.refs_0_ = f32[128,1536]{1,0:T(8,128)} custom-call(f32[512,1792]{1,0:T(8,128)} %conv.1.refs_0_.refs_1_.x_ref.b_ref.c_ref.refs_3_.refs_4_, f32[512,1792]{1,0:T(8,128)} %conv.1.refs_0_.refs_1_.x_ref.b_ref.c_ref.refs_3_.refs_4_, f32[12,2,512]{2,1,0:T(2,128)} %reshape.412.refs_2_, bf16[1,3088,128]{2,1,0:T(8,128)(2,1)} %copy-done.118, ...), custom_call_target="tpu_custom_call" | custom-call | flops 201326592 | bytes 3145728 | tf_op jit(solution)/shard_map/state/pallas_call | solution.py:871
  188.1 15.2 %collective-permute-start.32 = (bf16[144,1536]{1,0:T(8,128)(2,1)S(1)}, bf16[144,1536]{1,0:T(8,128)(2,1)}, u32[]{:S(2)}, u32[]{:S(2)}) collective-permute-start(bf16[144,1536]{1,0:T(8,128)(2,1)S(1)} %pad_maximum_fusion.14.refs_1_), channel_id=1, source_target_pairs={{0,1},{1,0},{2,3},{3,2},{4,5},{5,4},{6,7},{7,6},{8,9},{9,8},{10,11... | collective-permute-start | bytes 1327112 | tf_op jit(solution)/shard_map/ppermute | solution.py:248
  214.8 7.1 collective-permute-done.33
  228.0 14.6 %attend.1 = (f32[8,64,512]{2,1,0:T(8,128)S(1)}, f32[8,8,512]{2,1,0:T(8,128)S(1)}) custom-call(s32[4]{0:T(128)S(1)} %pad_add_fusion.refs_0_, bf16[8,128,512]{2,1,0:T(8,128)(2,1)S(1)} %copy-done.24, bf16[8,2,512,128]{3,2,1,0:T(8,128)(2,1)} %bitcast.335, s32[8,512]{1,0:T(8,128)S(1)} %broadcast_in_dim.286.refs_3_.row_ref.refs_10_.refs_6_, ...), custom_call_target="tpu_custom_call" | custom-call | flops 20000000000 | bytes 8388608 | tf_op jit(solution)/shard_map/attend/pallas_call | solution.py:1240
  244.2 4.7 collective-permute-start.39
  254.6 8.5 %ssm.1.refs_28_ = f32[512,1536]{1,0:T(8,128)S(1)} custom-call(s32[5]{0:T(128)S(1)} %copy-done.63, f32[512,1792]{1,0:T(8,128)S(1)} %copy-done, f32[512,1792]{1,0:T(8,128)S(1)} %copy-done, f32[512,1792]{1,0:T(8,128)S(1)} %copy-done, f32[12,2,512]{2,1,0:T(2,128)S(1)} %reshape_reshape.4.cum_ref.refs_5_, f32[12,2,512]{2,1,0:T(2,128)S(1)} %reshape.415.step_ref.refs_6_, ...), custom_call_target="tpu_custom_call" | custom-call | flops 1000000000 | bytes 6291456 | tf_op jit(solution)/shard_map/ssm/pallas_call | solution.py:949
  268.4 26.5 %unpack.3 = (bf16[1536,1024]{1,0:T(8,128)(2,1)}, bf16[1024,2048]{1,0:T(8,128)(2,1)}, bf16[1024,2048]{1,0:T(8,128)(2,1)}, bf16[2048,1024]{1,0:T(8,128)(2,1)}, bf16[16,128]{1,0:T(8,128)(2,1)S(1)}) custom-call(s32[31,5]{1,0:T(8,128)S(1)} %copy-done.61, s32[32]{0:T(128)S(1)} %fusion.78.refs_1_, bf16[1,3088,128]{2,1,0:T(8,128)(2,1)S(1)} %bitcast.267, ...), custom_call_target="tpu_custom_call" | custom-call | bytes 33013760 | tf_op jit(solution)/shard_map/unpack/pallas_call | solution.py:454
  310.4 6.9 fusion.2
  317.3 6.8 fusion.104
  326.6 4.6 multiply_reduce_fusion.3
  337.6 6.3 fusion.23
  344.0 9.1 %state.3 = f32[128,1536]{1,0:T(8,128)} custom-call(f32[512,1792]{1,0:T(8,128)} %conv.1.refs_0_.refs_1_.x_ref.b_ref.c_ref.refs_3_.refs_4_, f32[512,1536]{1,0:T(8,128)} %get-tuple-element.143.refs_1_.refs_2_, f32[12,2,512]{2,1,0:T(2,128)} %reshape.417.refs_2_), custom_call_target="tpu_custom_call" | custom-call | flops 201326592 | bytes 3145728 | tf_op jit(solution)/shard_map/state/pallas_call | solution.py:871
  357.5 4.5 pad_maximum_fusion.1
  365.7 8.0 collective-permute-start.41
  373.7 20.5 %pack.4.refs_0_ = bf16[49344,128]{1,0:T(8,128)(2,1)} custom-call(bf16[512,1024]{1,0:T(8,128)(2,1)S(1)} %copy-done.47, bf16[512,2048]{1,0:T(8,128)(2,1)S(1)} %copy-done.67, bf16[512,2048]{1,0:T(8,128)(2,1)} %get-tuple-element.215.refs_2_, bf16[512,2048]{1,0:T(8,128)(2,1)} %get-tuple-element.216.refs_3_, bf16[512,1024]{1,0:T(8,128)(2,1)S(1)} %copy-done.45, ...), custom_call_target="tpu_custom_call" | custom-call | flops 6442450944 | bytes 16777216 | tf_op jit(solution)/shard_map/pack/pallas_call | solution.py:609
  398.7 6.0 constant_dynamic-slice_fusion.2.refs_2_
  407.4 27.0 %collective-permute-start.42 = (bf16[144,1536]{1,0:T(8,128)(2,1)}, bf16[144,1536]{1,0:T(8,128)(2,1)}, u32[]{:S(2)}, u32[]{:S(2)}) collective-permute-start(bf16[144,1536]{1,0:T(8,128)(2,1)} %pad_maximum_fusion.19.refs_1_), channel_id=1, source_target_pairs={{0,4},{4,0},{1,5},{5,1},{2,6},{6,2},{3,7},{7,3},{8,12},{12,8},{9,1... | collective-permute-start | bytes 1327112 | tf_op jit(solution)/shard_map/ppermute | solution.py:248
  437.2 5.8 add_convert_fusion.1
  446.6 4.9 collective-permute-start.44
  451.5 4.7 pack.5.refs_0_
  457.4 9.7 %collective-permute-start.46 = (f32[4]{0:T(128)S(1)}, f32[4]{0:T(128)S(1)}, u32[]{:S(2)}, u32[]{:S(2)}) collective-permute-start(f32[4]{0:T(128)S(1)} %add.637.refs_13_), channel_id=1, source_target_pairs={{0,8},{8,0},{16,24},{24,16},{1,9},{9,1},{17,25},{25,17},{2,10},{10... | collective-permute-start | bytes 56 | tf_op jit(solution)/shard_map/ppermute | solution.py:248
  471.5 33.2 %ssm_back.1 = (f32[512,1536]{1,0:T(8,128)S(1)}, f32[512,128]{1,0:T(8,128)S(1)}, f32[512,128]{1,0:T(8,128)S(1)}, f32[12,8,512]{2,1,0:T(8,128)S(1)}) custom-call(s32[5]{0:T(128)S(1)} %copy-done.63, f32[512,1792]{1,0:T(8,128)} %conv.1.refs_0_.refs_1_.x_ref.b_ref.c_ref.refs_3_.refs_4_, f32[512,1536]{1,0:T(8,128)S(1)} %copy-done.9, ...), custom_call_target="tpu_custom_call" | custom-call | flops 3000000000 | bytes 9437184 | tf_op jit(solution)/shard_map/ssm_back/pallas_call | solution.py:1088
  517.9 12.9 %collective-permute-start.81 = (f32[4]{0:T(128)S(1)}, f32[4]{0:T(128)S(1)}, u32[]{:S(2)}, u32[]{:S(2)}) collective-permute-start(f32[4]{0:T(128)S(1)} %add.653.refs_11_), channel_id=1, source_target_pairs={{0,16},{16,0},{8,24},{24,8},{1,17},{17,1},{9,25},{25,9},{2,18},{18... | collective-permute-start | bytes 56 | tf_op jit(solution)/shard_map/ppermute | solution.py:248
  532.2 14.7 %conv_back.1 = (bf16[512,1792]{1,0:T(8,128)(2,1)}, f32[16,1792]{1,0:T(8,128)}, f32[8,1792]{1,0:T(8,128)}, f32[8,1792]{1,0:T(8,128)}) custom-call(s32[5]{0:T(128)} %pad_add_fusion.1.refs_0_.meta_ref, f32[512,1536]{1,0:T(8,128)} %get-tuple-element.85.refs_1_, f32[512,128]{1,0:T(8,128)} %get-tuple-element.86.refs_2_, f32[512,128]{1,0:T(8,128)} %get-tuple-element.87.refs_3_, ...), custom_call_target="tpu_custom_call" | custom-call | flops 2000000000 | bytes 9175040 | tf_op jit(solution)/shard_map/conv_back/pallas_call | solution.py:818
  559.8 12.1 %pack.6 = bf16[49440,128]{1,0:T(8,128)(2,1)} custom-call(bf16[512,512]{1,0:T(8,128)(2,1)S(1)} %bitcast.278, bf16[512,1024]{1,0:T(8,128)(2,1)S(1)} %copy-done.2, bf16[512,1024]{1,0:T(8,128)(2,1)S(1)} %copy-done.7, bf16[512,1536]{1,0:T(8,128)(2,1)S(1)} %copy-done.17, bf16[512,1536]{1,0:T(8,128)(2,1)S(1)} %slice.373.refs_4_, ...), custom_call_target="tpu_custom_call", output_to_operand_aliasing={{}: (7, {})} | custom-call | flops 4026531840 | bytes 11010048 | tf_op jit(solution)/shard_map/pack/pallas_call | solution.py:609
  572.0 6.0 constant_dynamic-slice_fusion.1.refs_1_
  583.9 5.1 fusion.105
  592.7 5.1 collective-permute-start.55
  605.0 5.0 fusion.85
  610.0 5.8 add_convert_fusion
  624.7 7.6 attend_back.2
  632.3 24.0 %collective-permute-done.51 = bf16[2,3104,128]{2,1,0:T(8,128)(2,1)} collective-permute-done((bf16[2,3104,128]{2,1,0:T(8,128)(2,1)}, bf16[2,3104,128]{2,1,0:T(8,128)(2,1)}, u32[]{:S(2)}, u32[]{:S(2)}) %collective-permute-start.51) | collective-permute-done | bytes 1589280 | tf_op jit(solution)/shard_map/ppermute | solution.py:248
  667.2 8.0 attend_back.3
  706.4 11.6 %collective-permute-start.62 = (bf16[2,2,512,128]{3,2,1,0:T(8,128)(2,1)S(1)}, bf16[2,2,512,128]{3,2,1,0:T(8,128)(2,1)}, u32[]{:S(2)}, u32[]{:S(2)}) collective-permute-start(bf16[2,2,512,128]{3,2,1,0:T(8,128)(2,1)S(1)} %dynamic-slice_bitcast_fusion.21.refs_1_), channel_id=1, source_target_pairs={{0,4},{4,0},{1,5},{5,1},{2,6},{6,2},{3,7},{7,3},{8,12},{12,8},{9,1... | collective-permute-start | bytes 1572872 | tf_op jit(solution)/shard_map/ppermute | solution.py:248
  724.1 6.1 collective-permute-done.62
  731.4 6.0 collective-permute-start.63
  737.4 5.6 add_add_fusion.4.refs_0_
  747.1 4.8 fusion.12
  751.9 5.4 pack.7
  785.5 19.7 %collective-permute-done.70.refs_1_ = bf16[3104,128]{1,0:T(8,128)(2,1)S(1)} collective-permute-done((bf16[3104,128]{1,0:T(8,128)(2,1)S(1)}, bf16[3104,128]{1,0:T(8,128)(2,1)S(1)}, u32[]{:S(2)}, u32[]{:S(2)}) %collective-permute-start.70) | collective-permute-done | bytes 794656 | tf_op jit(solution)/shard_map/ppermute | solution.py:248
  833.0 4.8 fusion.14
  (791 shorter events, 335.7 us)
Async XLA Ops:
  7.2 220.7 %all-gather.3.cloned.1.call-start = ((), (), s32[]{:S(2)}) async-start(), calls=%async_computation | async-start | bytes 2359296 | tf_op jit(solution)/shard_map/all_gather | solution.py:1541
  18.6 17.1 %collective-permute-start.1 = (bf16[3088,128]{1,0:T(8,128)(2,1)S(1)}, bf16[3088,128]{1,0:T(8,128)(2,1)S(1)}, u32[]{:S(2)}, u32[]{:S(2)}) collective-permute-start(bf16[3088,128]{1,0:T(8,128)(2,1)S(1)} %get-tuple-element.170), channel_id=1, source_target_pairs={{0,8},{9,17},{2,10},{11,19},{4,12},{13,21},{6,14},{15,23}} | collective-permute-start | bytes 2371592 | tf_op jit(solution)/shard_map/ppermute | solution.py:287
  43.9 32.2 %collective-permute-start.26 = (bf16[2,3088,128]{2,1,0:T(8,128)(2,1)}, bf16[2,3088,128]{2,1,0:T(8,128)(2,1)}, u32[]{:S(2)}, u32[]{:S(2)}) collective-permute-start(bf16[2,3088,128]{2,1,0:T(8,128)(2,1)} %collective-permute-done.24), channel_id=1, source_target_pairs={{8,0},{17,9},{10,2},{19,11},{12,4},{21,13},{14,6},{23,15}} | collective-permute-start | bytes 4743176 | tf_op jit(solution)/shard_map/ppermute | solution.py:302
  48.2 27.9 %collective-permute-start.17 = (bf16[3088,128]{1,0:T(8,128)(2,1)}, bf16[3088,128]{1,0:T(8,128)(2,1)}, u32[]{:S(2)}, u32[]{:S(2)}) collective-permute-start(bf16[3088,128]{1,0:T(8,128)(2,1)} %add_select_fusion.1), channel_id=1, source_target_pairs={{0,4},{4,0},{1,5},{5,1},{2,6},{6,2},{3,7},{7,3},{8,12},{12,8},{9,1... | collective-permute-start | bytes 2371592 | tf_op jit(solution)/shard_map/ppermute | solution.py:293
  49.7 38.7 %collective-permute-start.16 = (bf16[3088,128]{1,0:T(8,128)(2,1)}, bf16[3088,128]{1,0:T(8,128)(2,1)}, u32[]{:S(2)}, u32[]{:S(2)}) collective-permute-start(bf16[3088,128]{1,0:T(8,128)(2,1)} %add_select_fusion.1), channel_id=1, source_target_pairs={{0,2},{2,0},{1,3},{3,1},{4,6},{6,4},{5,7},{7,5},{8,10},{10,8},{9,1... | collective-permute-start | bytes 2371592 | tf_op jit(solution)/shard_map/ppermute | solution.py:292
  52.7 35.7 %collective-permute-start.5 = (bf16[3088,128]{1,0:T(8,128)(2,1)S(1)}, bf16[3088,128]{1,0:T(8,128)(2,1)S(1)}, u32[]{:S(2)}, u32[]{:S(2)}) collective-permute-start(bf16[3088,128]{1,0:T(8,128)(2,1)S(1)} %add_select_fusion.2), channel_id=1, source_target_pairs={{0,2},{2,0},{1,3},{3,1},{4,6},{6,4},{5,7},{7,5},{8,10},{10,8},{9,1... | collective-permute-start | bytes 2371592 | tf_op jit(solution)/shard_map/ppermute | solution.py:292
  53.3 36.8 %collective-permute-start.6 = (bf16[3088,128]{1,0:T(8,128)(2,1)S(1)}, bf16[3088,128]{1,0:T(8,128)(2,1)S(1)}, u32[]{:S(2)}, u32[]{:S(2)}) collective-permute-start(bf16[3088,128]{1,0:T(8,128)(2,1)S(1)} %add_select_fusion.2), channel_id=1, source_target_pairs={{0,4},{4,0},{1,5},{5,1},{2,6},{6,2},{3,7},{7,3},{8,12},{12,8},{9,1... | collective-permute-start | bytes 2371592 | tf_op jit(solution)/shard_map/ppermute | solution.py:293
  76.1 34.2 %collective-permute-start.27 = (bf16[2,3088,128]{2,1,0:T(8,128)(2,1)}, bf16[2,3088,128]{2,1,0:T(8,128)(2,1)}, u32[]{:S(2)}, u32[]{:S(2)}) collective-permute-start(bf16[2,3088,128]{2,1,0:T(8,128)(2,1)} %collective-permute-done.26), channel_id=1, source_target_pairs={{9,1},{11,3},{13,5},{15,7}} | collective-permute-start | bytes 4743176 | tf_op jit(solution)/shard_map/ppermute | solution.py:303
  88.5 20.4 %collective-permute-start.18 = (bf16[3088,128]{1,0:T(8,128)(2,1)}, bf16[3088,128]{1,0:T(8,128)(2,1)}, u32[]{:S(2)}, u32[]{:S(2)}) collective-permute-start(bf16[3088,128]{1,0:T(8,128)(2,1)} %collective-permute-done.17), channel_id=1, source_target_pairs={{0,2},{2,0},{1,3},{3,1},{4,6},{6,4},{5,7},{7,5},{8,10},{10,8},{9,1... | collective-permute-start | bytes 2371592 | tf_op jit(solution)/shard_map/ppermute | solution.py:294
  90.0 19.8 %collective-permute-start.7 = (bf16[3088,128]{1,0:T(8,128)(2,1)S(1)}, bf16[3088,128]{1,0:T(8,128)(2,1)}, u32[]{:S(2)}, u32[]{:S(2)}) collective-permute-start(bf16[3088,128]{1,0:T(8,128)(2,1)S(1)} %collective-permute-done.5), channel_id=1, source_target_pairs={{0,4},{4,0},{1,5},{5,1},{2,6},{6,2},{3,7},{7,3},{8,12},{12,8},{9,1... | collective-permute-start | bytes 2371592 | tf_op jit(solution)/shard_map/ppermute | solution.py:294
  91.6 18.3 %collective-permute-start.21 = (bf16[3088,128]{1,0:T(8,128)(2,1)}, bf16[3088,128]{1,0:T(8,128)(2,1)}, u32[]{:S(2)}, u32[]{:S(2)}) collective-permute-start(bf16[3088,128]{1,0:T(8,128)(2,1)} %collective-permute-done.17), channel_id=1, source_target_pairs={{0,1},{1,0},{2,3},{3,2},{4,5},{5,4},{6,7},{7,6},{8,9},{9,8},{10,11... | collective-permute-start | bytes 2371592 | tf_op jit(solution)/shard_map/ppermute | solution.py:297
  94.1 21.8 %collective-permute-start.9 = (bf16[3088,128]{1,0:T(8,128)(2,1)S(1)}, bf16[3088,128]{1,0:T(8,128)(2,1)S(1)}, u32[]{:S(2)}, u32[]{:S(2)}) collective-permute-start(bf16[3088,128]{1,0:T(8,128)(2,1)S(1)} %collective-permute-done.5), channel_id=1, source_target_pairs={{0,1},{1,0},{2,3},{3,2},{4,5},{5,4},{6,7},{7,6},{8,9},{9,8},{10,11... | collective-permute-start | bytes 2371592 | tf_op jit(solution)/shard_map/ppermute | solution.py:297
  115.8 40.3 %collective-permute-start.28 = (bf16[2,3088,128]{2,1,0:T(8,128)(2,1)}, bf16[2,3088,128]{2,1,0:T(8,128)(2,1)}, u32[]{:S(2)}, u32[]{:S(2)}) collective-permute-start(bf16[2,3088,128]{2,1,0:T(8,128)(2,1)} %add_select_fusion.refs_1_.refs_6_.refs_18_), channel_id=1, source_target_pairs={{0,2},{2,0},{1,3},{3,1},{4,6},{6,4},{5,7},{7,5},{8,10},{10,8},{9,1... | collective-permute-start | bytes 4743176 | tf_op jit(solution)/shard_map/ppermute | solution.py:248
  116.8 40.9 %collective-permute-start.29 = (bf16[2,3088,128]{2,1,0:T(8,128)(2,1)}, bf16[2,3088,128]{2,1,0:T(8,128)(2,1)}, u32[]{:S(2)}, u32[]{:S(2)}) collective-permute-start(bf16[2,3088,128]{2,1,0:T(8,128)(2,1)} %add_select_fusion.refs_1_.refs_6_.refs_18_), channel_id=1, source_target_pairs={{0,4},{4,0},{1,5},{5,1},{2,6},{6,2},{3,7},{7,3},{8,12},{12,8},{9,1... | collective-permute-start | bytes 4743176 | tf_op jit(solution)/shard_map/ppermute | solution.py:248
  118.3 146.9 %collective-permute-start.35 = (bf16[2,3088,128]{2,1,0:T(8,128)(2,1)}, bf16[2,3088,128]{2,1,0:T(8,128)(2,1)}, u32[]{:S(2)}, u32[]{:S(2)}) collective-permute-start(bf16[2,3088,128]{2,1,0:T(8,128)(2,1)} %add_select_fusion.refs_1_.refs_6_.refs_18_), channel_id=1, source_target_pairs={{0,1},{1,0},{2,3},{3,2},{4,5},{5,4},{6,7},{7,6},{8,9},{9,8},{10,11... | collective-permute-start | bytes 4743176 | tf_op jit(solution)/shard_map/ppermute | solution.py:248
  157.3 29.4 %collective-permute-start.30 = (bf16[1,3088,128]{2,1,0:T(8,128)(2,1)S(1)}, bf16[1,3088,128]{2,1,0:T(8,128)(2,1)}, u32[]{:S(2)}, u32[]{:S(2)}) collective-permute-start(bf16[1,3088,128]{2,1,0:T(8,128)(2,1)S(1)} %slice.346.refs_3_), channel_id=1, source_target_pairs={{0,4},{4,0},{1,5},{5,1},{2,6},{6,2},{3,7},{7,3},{8,12},{12,8},{9,1... | collective-permute-start | bytes 2371592 | tf_op jit(solution)/shard_map/ppermute | solution.py:248
  159.8 26.9 %collective-permute-start.31 = (bf16[1,3088,128]{2,1,0:T(8,128)(2,1)}, bf16[1,3088,128]{2,1,0:T(8,128)(2,1)}, u32[]{:S(2)}, u32[]{:S(2)}) collective-permute-start(bf16[1,3088,128]{2,1,0:T(8,128)(2,1)} %slice.347.refs_4_), channel_id=1, source_target_pairs={{0,2},{2,0},{1,3},{3,1},{4,6},{6,4},{5,7},{7,5},{8,10},{10,8},{9,1... | collective-permute-start | bytes 2371592 | tf_op jit(solution)/shard_map/ppermute | solution.py:248
  188.1 18.4 %collective-permute-start.32 = (bf16[144,1536]{1,0:T(8,128)(2,1)S(1)}, bf16[144,1536]{1,0:T(8,128)(2,1)}, u32[]{:S(2)}, u32[]{:S(2)}) collective-permute-start(bf16[144,1536]{1,0:T(8,128)(2,1)S(1)} %pad_maximum_fusion.14.refs_1_), channel_id=1, source_target_pairs={{0,1},{1,0},{2,3},{3,2},{4,5},{5,4},{6,7},{7,6},{8,9},{9,8},{10,11... | collective-permute-start | bytes 1327112 | tf_op jit(solution)/shard_map/ppermute | solution.py:248
  205.7 59.6 %collective-permute-start.36 = (bf16[2,3088,128]{2,1,0:T(8,128)(2,1)}, bf16[2,3088,128]{2,1,0:T(8,128)(2,1)}, u32[]{:S(2)}, u32[]{:S(2)}) collective-permute-start(bf16[2,3088,128]{2,1,0:T(8,128)(2,1)} %collective-permute-done.28.refs_2_.refs_7_.refs_19_), channel_id=1, source_target_pairs={{0,1},{1,0},{2,3},{3,2},{4,5},{5,4},{6,7},{7,6},{8,9},{9,8},{10,11... | collective-permute-start | bytes 4743176 | tf_op jit(solution)/shard_map/ppermute | solution.py:248
  205.9 59.4 %collective-permute-start.37 = (bf16[2,3088,128]{2,1,0:T(8,128)(2,1)}, bf16[2,3088,128]{2,1,0:T(8,128)(2,1)}, u32[]{:S(2)}, u32[]{:S(2)}) collective-permute-start(bf16[2,3088,128]{2,1,0:T(8,128)(2,1)} %collective-permute-done.29.refs_3_.refs_8_.refs_20_), channel_id=1, source_target_pairs={{0,1},{1,0},{2,3},{3,2},{4,5},{5,4},{6,7},{7,6},{8,9},{9,8},{10,11... | collective-permute-start | bytes 4743176 | tf_op jit(solution)/shard_map/ppermute | solution.py:248
  206.2 59.1 %collective-permute-start.38 = (bf16[1,3088,128]{2,1,0:T(8,128)(2,1)}, bf16[1,3088,128]{2,1,0:T(8,128)(2,1)}, u32[]{:S(2)}, u32[]{:S(2)}) collective-permute-start(bf16[1,3088,128]{2,1,0:T(8,128)(2,1)} %collective-permute-done.30.refs_4_.refs_9_.refs_21_), channel_id=1, source_target_pairs={{0,1},{1,0},{2,3},{3,2},{4,5},{5,4},{6,7},{7,6},{8,9},{9,8},{10,11... | collective-permute-start | bytes 2371592 | tf_op jit(solution)/shard_map/ppermute | solution.py:248
  224.9 19.4 %collective-permute-start.34 = (bf16[144,1536]{1,0:T(8,128)(2,1)S(1)}, bf16[144,1536]{1,0:T(8,128)(2,1)}, u32[]{:S(2)}, u32[]{:S(2)}) collective-permute-start(bf16[144,1536]{1,0:T(8,128)(2,1)S(1)} %pad_maximum_fusion.16.refs_4_), channel_id=1, source_target_pairs={{0,4},{4,0},{1,5},{5,1},{2,6},{6,2},{3,7},{7,3},{8,12},{12,8},{9,1... | collective-permute-start | bytes 1327112 | tf_op jit(solution)/shard_map/ppermute | solution.py:248
  244.2 21.1 %collective-permute-start.39 = (bf16[1,3088,128]{2,1,0:T(8,128)(2,1)}, bf16[1,3088,128]{2,1,0:T(8,128)(2,1)}, u32[]{:S(2)}, u32[]{:S(2)}) collective-permute-start(bf16[1,3088,128]{2,1,0:T(8,128)(2,1)} %collective-permute-done.31.refs_5_.refs_10_.refs_22_), channel_id=1, source_target_pairs={{0,1},{1,0},{2,3},{3,2},{4,5},{5,4},{6,7},{7,6},{8,9},{9,8},{10,11... | collective-permute-start | bytes 2371592 | tf_op jit(solution)/shard_map/ppermute | solution.py:248
  365.7 28.5 %collective-permute-start.41 = (bf16[144,1536]{1,0:T(8,128)(2,1)S(1)}, bf16[144,1536]{1,0:T(8,128)(2,1)S(1)}, u32[]{:S(2)}, u32[]{:S(2)}) collective-permute-start(bf16[144,1536]{1,0:T(8,128)(2,1)S(1)} %pad_maximum_fusion.18.refs_7_), channel_id=1, source_target_pairs={{0,2},{2,0},{1,3},{3,1},{4,6},{6,4},{5,7},{7,5},{8,10},{10,8},{9,1... | collective-permute-start | bytes 1327112 | tf_op jit(solution)/shard_map/ppermute | solution.py:248
  404.7 32.5 %collective-permute-start.43 = (bf16[24688,128]{1,0:T(8,128)(2,1)}, bf16[24688,128]{1,0:T(8,128)(2,1)}, u32[]{:S(2)}, u32[]{:S(2)}) collective-permute-start(bf16[24688,128]{1,0:T(8,128)(2,1)} %constant_dynamic-slice_fusion.2.refs_2_), channel_id=1, source_target_pairs={{0,1},{1,0},{2,3},{3,2},{4,5},{5,4},{6,7},{7,6},{8,9},{9,8},{10,11... | collective-permute-start | bytes 18960392 | tf_op jit(solution)/shard_map/ppermute | solution.py:248
  407.4 48.8 %collective-permute-start.42 = (bf16[144,1536]{1,0:T(8,128)(2,1)}, bf16[144,1536]{1,0:T(8,128)(2,1)}, u32[]{:S(2)}, u32[]{:S(2)}) collective-permute-start(bf16[144,1536]{1,0:T(8,128)(2,1)} %pad_maximum_fusion.19.refs_1_), channel_id=1, source_target_pairs={{0,4},{4,0},{1,5},{5,1},{2,6},{6,2},{3,7},{7,3},{8,12},{12,8},{9,1... | collective-permute-start | bytes 1327112 | tf_op jit(solution)/shard_map/ppermute | solution.py:248
  446.6 61.9 %collective-permute-start.44 = (bf16[2,3104,128]{2,1,0:T(8,128)(2,1)}, bf16[2,3104,128]{2,1,0:T(8,128)(2,1)}, u32[]{:S(2)}, u32[]{:S(2)}) collective-permute-start(bf16[2,3104,128]{2,1,0:T(8,128)(2,1)} %pad_maximum_fusion.4.refs_11_.refs_1_), channel_id=1, source_target_pairs={{0,4},{4,0},{1,5},{5,1},{2,6},{6,2},{3,7},{7,3},{8,12},{12,8},{9,1... | collective-permute-start | bytes 4767752 | tf_op jit(solution)/shard_map/ppermute | solution.py:248
  457.4 59.3 %collective-permute-start.46 = (f32[4]{0:T(128)S(1)}, f32[4]{0:T(128)S(1)}, u32[]{:S(2)}, u32[]{:S(2)}) collective-permute-start(f32[4]{0:T(128)S(1)} %add.637.refs_13_), channel_id=1, source_target_pairs={{0,8},{8,0},{16,24},{24,16},{1,9},{9,1},{17,25},{25,17},{2,10},{10... | collective-permute-start | bytes 56 | tf_op jit(solution)/shard_map/ppermute | solution.py:248
  471.0 42.4 %collective-permute-start.45 = (bf16[2,3104,128]{2,1,0:T(8,128)(2,1)}, bf16[2,3104,128]{2,1,0:T(8,128)(2,1)}, u32[]{:S(2)}, u32[]{:S(2)}) collective-permute-start(bf16[2,3104,128]{2,1,0:T(8,128)(2,1)} %pad_maximum_fusion.5.refs_12_.refs_2_), channel_id=1, source_target_pairs={{0,2},{2,0},{1,3},{3,1},{4,6},{6,4},{5,7},{7,5},{8,10},{10,8},{9,1... | collective-permute-start | bytes 4767752 | tf_op jit(solution)/shard_map/ppermute | solution.py:248
  511.9 35.9 %collective-permute-start.47 = (bf16[3104,128]{1,0:T(8,128)(2,1)}, bf16[3104,128]{1,0:T(8,128)(2,1)}, u32[]{:S(2)}, u32[]{:S(2)}) collective-permute-start(bf16[3104,128]{1,0:T(8,128)(2,1)} %dynamic-slice_bitcast_fusion.14.refs_4_.refs_9_), channel_id=1, source_target_pairs={{0,2},{2,0},{1,3},{3,1},{4,6},{6,4},{5,7},{7,5},{8,10},{10,8},{9,1... | collective-permute-start | bytes 2383880 | tf_op jit(solution)/shard_map/ppermute | solution.py:248
  516.6 32.7 %collective-permute-start.48 = (bf16[3104,128]{1,0:T(8,128)(2,1)}, bf16[3104,128]{1,0:T(8,128)(2,1)}, u32[]{:S(2)}, u32[]{:S(2)}) collective-permute-start(bf16[3104,128]{1,0:T(8,128)(2,1)} %dynamic-slice_bitcast_fusion.11.refs_5_.refs_10_), channel_id=1, source_target_pairs={{0,4},{4,0},{1,5},{5,1},{2,6},{6,2},{3,7},{7,3},{8,12},{12,8},{9,1... | collective-permute-start | bytes 2383880 | tf_op jit(solution)/shard_map/ppermute | solution.py:248
  517.9 37.0 %collective-permute-start.81 = (f32[4]{0:T(128)S(1)}, f32[4]{0:T(128)S(1)}, u32[]{:S(2)}, u32[]{:S(2)}) collective-permute-start(f32[4]{0:T(128)S(1)} %add.653.refs_11_), channel_id=1, source_target_pairs={{0,16},{16,0},{8,24},{24,8},{1,17},{17,1},{9,25},{25,9},{2,18},{18... | collective-permute-start | bytes 56 | tf_op jit(solution)/shard_map/ppermute | solution.py:248
  577.9 32.1 %collective-permute-start.50 = (bf16[24688,128]{1,0:T(8,128)(2,1)}, bf16[24688,128]{1,0:T(8,128)(2,1)}, u32[]{:S(2)}, u32[]{:S(2)}) collective-permute-start(bf16[24688,128]{1,0:T(8,128)(2,1)} %constant_dynamic-slice_fusion.1.refs_1_), channel_id=1, source_target_pairs={{0,1},{1,0},{2,3},{3,2},{4,5},{5,4},{6,7},{7,6},{8,9},{9,8},{10,11... | collective-permute-start | bytes 18960392 | tf_op jit(solution)/shard_map/ppermute | solution.py:248
  590.8 96.1 %collective-permute-start.54 = (bf16[2,3104,128]{2,1,0:T(8,128)(2,1)}, bf16[2,3104,128]{2,1,0:T(8,128)(2,1)}, u32[]{:S(2)}, u32[]{:S(2)}) collective-permute-start(bf16[2,3104,128]{2,1,0:T(8,128)(2,1)} %pad_maximum_fusion.6.refs_4_.refs_5_.refs_6_.refs_8_.refs_9_.refs_10_.refs_2_.refs_3_.refs_11_), channel_id=1, source_target_pairs={{8,16},{17,25},{10,18},{19,27},{12,20},{21,29},{14,22},{23,31}} | collective-permute-start | bytes 4767752 | tf_op jit(solution)/shard_map/ppermute | solution.py:248
  592.7 95.4 %collective-permute-start.55 = (bf16[2,3104,128]{2,1,0:T(8,128)(2,1)}, bf16[2,3104,128]{2,1,0:T(8,128)(2,1)}, u32[]{:S(2)}, u32[]{:S(2)}) collective-permute-start(bf16[2,3104,128]{2,1,0:T(8,128)(2,1)} %pad_maximum_fusion.6.refs_4_.refs_5_.refs_6_.refs_8_.refs_9_.refs_10_.refs_2_.refs_3_.refs_11_), channel_id=1, source_target_pairs={{0,16},{9,25},{2,18},{11,27},{4,20},{13,29},{6,22},{15,31}} | collective-permute-start | bytes 4767752 | tf_op jit(solution)/shard_map/ppermute | solution.py:248
  597.8 91.8 %collective-permute-start.56 = (bf16[2,3104,128]{2,1,0:T(8,128)(2,1)}, bf16[2,3104,128]{2,1,0:T(8,128)(2,1)}, u32[]{:S(2)}, u32[]{:S(2)}) collective-permute-start(bf16[2,3104,128]{2,1,0:T(8,128)(2,1)} %pad_maximum_fusion.6.refs_4_.refs_5_.refs_6_.refs_8_.refs_9_.refs_10_.refs_2_.refs_3_.refs_11_), channel_id=1, source_target_pairs={{24,16},{1,25},{26,18},{3,27},{28,20},{5,29},{30,22},{7,31}} | collective-permute-start | bytes 4767752 | tf_op jit(solution)/shard_map/ppermute | solution.py:248
  619.1 37.1 %collective-permute-start.51 = (bf16[2,3104,128]{2,1,0:T(8,128)(2,1)}, bf16[2,3104,128]{2,1,0:T(8,128)(2,1)}, u32[]{:S(2)}, u32[]{:S(2)}) collective-permute-start(bf16[2,3104,128]{2,1,0:T(8,128)(2,1)} %pad_maximum_fusion.7.refs_1_.refs_7_), channel_id=1, source_target_pairs={{0,4},{4,0},{1,5},{5,1},{2,6},{6,2},{3,7},{7,3},{8,12},{12,8},{9,1... | collective-permute-start | bytes 4767752 | tf_op jit(solution)/shard_map/ppermute | solution.py:248
  621.9 39.8 %collective-permute-start.52 = (bf16[2,3104,128]{2,1,0:T(8,128)(2,1)}, bf16[2,3104,128]{2,1,0:T(8,128)(2,1)}, u32[]{:S(2)}, u32[]{:S(2)}) collective-permute-start(bf16[2,3104,128]{2,1,0:T(8,128)(2,1)} %pad_maximum_fusion.8.refs_2_.refs_8_), channel_id=1, source_target_pairs={{0,2},{2,0},{1,3},{3,1},{4,6},{6,4},{5,7},{7,5},{8,10},{10,8},{9,1... | collective-permute-start | bytes 4767752 | tf_op jit(solution)/shard_map/ppermute | solution.py:248
  659.3 19.9 %collective-permute-start.53 = (bf16[3104,128]{1,0:T(8,128)(2,1)}, bf16[3104,128]{1,0:T(8,128)(2,1)}, u32[]{:S(2)}, u32[]{:S(2)}) collective-permute-start(bf16[3104,128]{1,0:T(8,128)(2,1)} %dynamic-slice_bitcast_fusion.4.refs_2_.refs_7_), channel_id=1, source_target_pairs={{0,2},{2,0},{1,3},{3,1},{4,6},{6,4},{5,7},{7,5},{8,10},{10,8},{9,1... | collective-permute-start | bytes 2383880 | tf_op jit(solution)/shard_map/ppermute | solution.py:248
  665.6 32.2 %collective-permute-start.58 = (bf16[3104,128]{1,0:T(8,128)(2,1)}, bf16[3104,128]{1,0:T(8,128)(2,1)}, u32[]{:S(2)}, u32[]{:S(2)}) collective-permute-start(bf16[3104,128]{1,0:T(8,128)(2,1)} %dynamic-slice_bitcast_fusion.1.refs_3_.refs_8_), channel_id=1, source_target_pairs={{0,4},{4,0},{1,5},{5,1},{2,6},{6,2},{3,7},{7,3},{8,12},{12,8},{9,1... | collective-permute-start | bytes 2383880 | tf_op jit(solution)/shard_map/ppermute | solution.py:248
  681.5 36.5 %collective-permute-start.59 = (bf16[3104,128]{1,0:T(8,128)(2,1)}, bf16[3104,128]{1,0:T(8,128)(2,1)}, u32[]{:S(2)}, u32[]{:S(2)}) collective-permute-start(bf16[3104,128]{1,0:T(8,128)(2,1)} %fusion.20.refs_2_.refs_3_.refs_4_), channel_id=1, source_target_pairs={{8,0},{17,9},{10,2},{19,11},{12,4},{21,13},{14,6},{23,15}} | collective-permute-start | bytes 2383880 | tf_op jit(solution)/shard_map/ppermute | solution.py:248
  686.8 34.0 %collective-permute-start.60 = (bf16[3104,128]{1,0:T(8,128)(2,1)}, bf16[3104,128]{1,0:T(8,128)(2,1)}, u32[]{:S(2)}, u32[]{:S(2)}) collective-permute-start(bf16[3104,128]{1,0:T(8,128)(2,1)} %fusion.20.refs_2_.refs_3_.refs_4_), channel_id=1, source_target_pairs={{16,0},{25,9},{18,2},{27,11},{20,4},{29,13},{22,6},{31,15}} | collective-permute-start | bytes 2383880 | tf_op jit(solution)/shard_map/ppermute | solution.py:248
  688.1 32.7 %collective-permute-start.61 = (bf16[3104,128]{1,0:T(8,128)(2,1)}, bf16[3104,128]{1,0:T(8,128)(2,1)}, u32[]{:S(2)}, u32[]{:S(2)}) collective-permute-start(bf16[3104,128]{1,0:T(8,128)(2,1)} %fusion.20.refs_2_.refs_3_.refs_4_), channel_id=1, source_target_pairs={{24,0},{1,9},{26,2},{3,11},{28,4},{5,13},{30,6},{7,15}} | collective-permute-start | bytes 2383880 | tf_op jit(solution)/shard_map/ppermute | solution.py:248
  706.4 23.8 %collective-permute-start.62 = (bf16[2,2,512,128]{3,2,1,0:T(8,128)(2,1)S(1)}, bf16[2,2,512,128]{3,2,1,0:T(8,128)(2,1)}, u32[]{:S(2)}, u32[]{:S(2)}) collective-permute-start(bf16[2,2,512,128]{3,2,1,0:T(8,128)(2,1)S(1)} %dynamic-slice_bitcast_fusion.21.refs_1_), channel_id=1, source_target_pairs={{0,4},{4,0},{1,5},{5,1},{2,6},{6,2},{3,7},{7,3},{8,12},{12,8},{9,1... | collective-permute-start | bytes 1572872 | tf_op jit(solution)/shard_map/ppermute | solution.py:248
  765.0 20.5 %collective-permute-start.69 = (bf16[3104,128]{1,0:T(8,128)(2,1)S(1)}, bf16[3104,128]{1,0:T(8,128)(2,1)S(1)}, u32[]{:S(2)}, u32[]{:S(2)}) collective-permute-start(bf16[3104,128]{1,0:T(8,128)(2,1)S(1)} %copy-done.3), channel_id=1, source_target_pairs={{8,0},{17,9},{10,2},{19,11},{12,4},{21,13},{14,6},{23,15}} | collective-permute-start | bytes 2383880 | tf_op jit(solution)/shard_map/ppermute | solution.py:248
  766.2 38.9 %collective-permute-start.70 = (bf16[3104,128]{1,0:T(8,128)(2,1)S(1)}, bf16[3104,128]{1,0:T(8,128)(2,1)S(1)}, u32[]{:S(2)}, u32[]{:S(2)}) collective-permute-start(bf16[3104,128]{1,0:T(8,128)(2,1)S(1)} %copy-done.3), channel_id=1, source_target_pairs={{16,0},{25,9},{18,2},{27,11},{20,4},{29,13},{22,6},{31,15}} | collective-permute-start | bytes 2383880 | tf_op jit(solution)/shard_map/ppermute | solution.py:248
  767.5 37.6 %collective-permute-start.71 = (bf16[3104,128]{1,0:T(8,128)(2,1)S(1)}, bf16[3104,128]{1,0:T(8,128)(2,1)}, u32[]{:S(2)}, u32[]{:S(2)}) collective-permute-start(bf16[3104,128]{1,0:T(8,128)(2,1)S(1)} %copy-done.3), channel_id=1, source_target_pairs={{24,0},{1,9},{26,2},{3,11},{28,4},{5,13},{30,6},{7,15}} | collective-permute-start | bytes 2383880 | tf_op jit(solution)/shard_map/ppermute | solution.py:248
  814.2 25.1 %collective-permute-start.80 = (bf16[3104,128]{1,0:T(8,128)(2,1)}, bf16[3104,128]{1,0:T(8,128)(2,1)S(1)}, u32[]{:S(2)}, u32[]{:S(2)}) collective-permute-start(bf16[3104,128]{1,0:T(8,128)(2,1)} %get-tuple-element.168.refs_5_), channel_id=1, source_target_pairs={{0,1},{9,8},{16,17},{25,24},{2,3},{11,10},{18,19},{27,26},{4,5},{1... | collective-permute-start | bytes 2383880 | tf_op jit(solution)/shard_map/ppermute | solution.py:248
  (224 other events, 2359.6 us)
Sparse Core Ops, SparseCore 0:
  147.8 44.0 all-gather.2

commit v14 on v13

--- a/solution.py
+++ b/solution.py
@@ -474,7 +474,7 @@
 
 
 def pack_lines(target, target_rows, first_row, segments, lane, phase, extras, carry, tail_rows, after=()):
-    tall = 256
+    tall = 512
     lefts, rights, plan = [], [], []
     left_of, right_of = {}, {}
     row = first_row

time: 857 us -> 852 us (level)
  no operation moved by 1% of the time
where the time goes in v14:
time: 852 us; the launch traced here: 844 us
  starting transfers between devices  196 us (23%)
  Pallas kernels  195 us (23%)
  other arithmetic  138 us (16%)
  waiting for transfers between devices  133 us (16%)
  local copies, waits for them, and re-layouts  82.9 us (10%)
  matrix products  80.9 us (9%)
  between operations  18.5 us (2%)
    ppermute x53, starting transfers between devices, go(): lax.ppermute(value, axis, pairs)  163 us
    ppermute x53, waiting for transfers between devices, go(): lax.ppermute(value, axis, pairs)  81.7 us
    dot_general x12, matrix products, matmul_right_t(): lax.dot_general(left, right, (((1,), (1,)), ((), ())), preferred_element_...  47.3 us
    pallas_call x2, Pallas kernels, unpack_lines(): pl.pallas_call(pinned(kernel, 2 + count_buffers, after), grid_spec=pltpu....  41.4 us
    pallas_call x4, Pallas kernels, pack_lines(): pl.pallas_call(pinned(kernel, inputs, after), grid=(total,), in_specs=[le...  38.2 us
    unnamed x383, local copies, waits for them, and re-layouts  36.3 us
    convert_element_type x14, other arithmetic, added(): return total.astype(jnp.bfloat16)  34.3 us
    pallas_call x1, Pallas kernels, ssm_backward(): pl.pallas_call(pinned(kernel, 11, after), grid_spec=pltpu.PrefetchScalarG...  33 us
  transfers between devices with their start and end apart: 83, of which 23 were waited for; matrix products, arithmetic and copies ran while one was open for 21% of the time, Pallas kernels for 17%

profile of v14, /device:TPU:0, one launch (start us, length us, event | category | flops | bytes accessed | tf_op | source)
XLA Modules:
  0.0 844.2 jit_solution(10294313568601517760)
XLA Ops:
  13.1 5.5 collective-permute-start.12
  19.9 7.3 collective-permute-done.12
  53.8 22.3 %collective-permute-done.26 = bf16[2,3088,128]{2,1,0:T(8,128)(2,1)} collective-permute-done((bf16[2,3088,128]{2,1,0:T(8,128)(2,1)}, bf16[2,3088,128]{2,1,0:T(8,128)(2,1)}, u32[]{:S(2)}, u32[]{:S(2)}) %collective-permute-start.26) | collective-permute-done | bytes 1581088 | tf_op jit(solution)/shard_map/ppermute | solution.py:302
  94.6 14.2 %collective-permute-done.18 = bf16[3088,128]{1,0:T(8,128)(2,1)} collective-permute-done((bf16[3088,128]{1,0:T(8,128)(2,1)}, bf16[3088,128]{1,0:T(8,128)(2,1)}, u32[]{:S(2)}, u32[]{:S(2)}) %collective-permute-start.18) | collective-permute-done | bytes 790560 | tf_op jit(solution)/shard_map/ppermute | solution.py:294
  110.4 5.4 add_select_fusion.refs_1_.refs_6_.refs_18_
  119.8 14.9 %unpack.2 = (bf16[1024,512]{1,0:T(8,128)(2,1)}, bf16[1024,128]{1,0:T(8,128)(2,1)S(1)}, bf16[1024,128]{1,0:T(8,128)(2,1)S(1)}, bf16[512,1024]{1,0:T(8,128)(2,1)},...) custom-call(s32[25,5]{1,0:T(8,128)S(1)} %copy-done.62, ...), custom_call_target="tpu_custom_call" | custom-call | bytes 26624000 | tf_op jit(solution)/shard_map/unpack/pallas_call | solution.py:454
  166.6 11.3 %conv.1.refs_0_.refs_1_.x_ref.b_ref.c_ref.refs_3_.refs_4_ = f32[512,1792]{1,0:T(8,128)} custom-call(s32[5]{0:T(128)} %pad_add_fusion.1.refs_0_.meta_ref, f32[512,1792]{1,0:T(8,128)} %pad_maximum_fusion.refs_1_.refs_4_, f32[8,1792]{1,0:T(8,128)} %copy-done.143, f32[4,1792]{1,0:T(4,128)} %reshape.435.refs_3_.refs_6_, f32[1,1792]{1,0:T(1,128)} %bitcast.330, ...), custom_call_target="tpu_custom_call" | custom-call | flops 1000000000 | bytes 7340032 | tf_op jit(solution)/shard_map/conv/pallas_call | solution.py:759
  177.9 8.8 %state.2.refs_0_ = f32[128,1536]{1,0:T(8,128)} custom-call(f32[512,1792]{1,0:T(8,128)} %conv.1.refs_0_.refs_1_.x_ref.b_ref.c_ref.refs_3_.refs_4_, f32[512,1792]{1,0:T(8,128)} %conv.1.refs_0_.refs_1_.x_ref.b_ref.c_ref.refs_3_.refs_4_, f32[12,2,512]{2,1,0:T(2,128)} %reshape.412.refs_2_, bf16[1,3088,128]{2,1,0:T(8,128)(2,1)} %copy-done.118, ...), custom_call_target="tpu_custom_call" | custom-call | flops 201326592 | bytes 3145728 | tf_op jit(solution)/shard_map/state/pallas_call | solution.py:871
  188.1 15.2 %collective-permute-start.32 = (bf16[144,1536]{1,0:T(8,128)(2,1)S(1)}, bf16[144,1536]{1,0:T(8,128)(2,1)}, u32[]{:S(2)}, u32[]{:S(2)}) collective-permute-start(bf16[144,1536]{1,0:T(8,128)(2,1)S(1)} %pad_maximum_fusion.14.refs_1_), channel_id=1, source_target_pairs={{0,1},{1,0},{2,3},{3,2},{4,5},{5,4},{6,7},{7,6},{8,9},{9,8},{10,11... | collective-permute-start | bytes 1327112 | tf_op jit(solution)/shard_map/ppermute | solution.py:248
  214.8 7.1 collective-permute-done.33
  228.0 14.6 %attend.1 = (f32[8,64,512]{2,1,0:T(8,128)S(1)}, f32[8,8,512]{2,1,0:T(8,128)S(1)}) custom-call(s32[4]{0:T(128)S(1)} %pad_add_fusion.refs_0_, bf16[8,128,512]{2,1,0:T(8,128)(2,1)S(1)} %copy-done.24, bf16[8,2,512,128]{3,2,1,0:T(8,128)(2,1)} %bitcast.335, s32[8,512]{1,0:T(8,128)S(1)} %broadcast_in_dim.286.refs_3_.row_ref.refs_10_.refs_6_, ...), custom_call_target="tpu_custom_call" | custom-call | flops 20000000000 | bytes 8388608 | tf_op jit(solution)/shard_map/attend/pallas_call | solution.py:1240
  244.2 4.7 collective-permute-start.39
  254.6 8.5 %ssm.1.refs_28_ = f32[512,1536]{1,0:T(8,128)S(1)} custom-call(s32[5]{0:T(128)S(1)} %copy-done.63, f32[512,1792]{1,0:T(8,128)S(1)} %copy-done, f32[512,1792]{1,0:T(8,128)S(1)} %copy-done, f32[512,1792]{1,0:T(8,128)S(1)} %copy-done, f32[12,2,512]{2,1,0:T(2,128)S(1)} %reshape_reshape.4.cum_ref.refs_5_, f32[12,2,512]{2,1,0:T(2,128)S(1)} %reshape.415.step_ref.refs_6_, ...), custom_call_target="tpu_custom_call" | custom-call | flops 1000000000 | bytes 6291456 | tf_op jit(solution)/shard_map/ssm/pallas_call | solution.py:949
  268.4 26.5 %unpack.3 = (bf16[1536,1024]{1,0:T(8,128)(2,1)}, bf16[1024,2048]{1,0:T(8,128)(2,1)}, bf16[1024,2048]{1,0:T(8,128)(2,1)}, bf16[2048,1024]{1,0:T(8,128)(2,1)}, bf16[16,128]{1,0:T(8,128)(2,1)S(1)}) custom-call(s32[31,5]{1,0:T(8,128)S(1)} %copy-done.61, s32[32]{0:T(128)S(1)} %fusion.78.refs_1_, bf16[1,3088,128]{2,1,0:T(8,128)(2,1)S(1)} %bitcast.267, ...), custom_call_target="tpu_custom_call" | custom-call | bytes 33013760 | tf_op jit(solution)/shard_map/unpack/pallas_call | solution.py:454
  301.4 4.4 fusion.103
  306.0 4.3 fusion.102
  310.4 6.9 fusion.2
  317.3 6.8 fusion.104
  326.6 4.6 multiply_reduce_fusion.3
  337.6 6.3 fusion.23
  344.0 9.1 %state.3 = f32[128,1536]{1,0:T(8,128)} custom-call(f32[512,1792]{1,0:T(8,128)} %conv.1.refs_0_.refs_1_.x_ref.b_ref.c_ref.refs_3_.refs_4_, f32[512,1536]{1,0:T(8,128)} %get-tuple-element.143.refs_1_.refs_2_, f32[12,2,512]{2,1,0:T(2,128)} %reshape.417.refs_2_), custom_call_target="tpu_custom_call" | custom-call | flops 201326592 | bytes 3145728 | tf_op jit(solution)/shard_map/state/pallas_call | solution.py:871
  357.5 4.5 pad_maximum_fusion.1
  365.7 8.0 collective-permute-start.41
  373.7 19.8 %pack.4.refs_0_ = bf16[49344,128]{1,0:T(8,128)(2,1)} custom-call(bf16[512,1024]{1,0:T(8,128)(2,1)S(1)} %copy-done.47, bf16[512,2048]{1,0:T(8,128)(2,1)S(1)} %copy-done.67, bf16[512,2048]{1,0:T(8,128)(2,1)} %get-tuple-element.215.refs_2_, bf16[512,2048]{1,0:T(8,128)(2,1)} %get-tuple-element.216.refs_3_, bf16[512,1024]{1,0:T(8,128)(2,1)S(1)} %copy-done.45, ...), custom_call_target="tpu_custom_call" | custom-call | flops 6442450944 | bytes 16777216 | tf_op jit(solution)/shard_map/pack/pallas_call | solution.py:609
  398.0 6.0 constant_dynamic-slice_fusion.2.refs_2_
  406.8 27.0 %collective-permute-start.42 = (bf16[144,1536]{1,0:T(8,128)(2,1)}, bf16[144,1536]{1,0:T(8,128)(2,1)}, u32[]{:S(2)}, u32[]{:S(2)}) collective-permute-start(bf16[144,1536]{1,0:T(8,128)(2,1)} %pad_maximum_fusion.19.refs_1_), channel_id=1, source_target_pairs={{0,4},{4,0},{1,5},{5,1},{2,6},{6,2},{3,7},{7,3},{8,12},{12,8},{9,1... | collective-permute-start | bytes 1327112 | tf_op jit(solution)/shard_map/ppermute | solution.py:248
  436.5 5.8 add_convert_fusion.1
  445.9 4.9 collective-permute-start.44
  456.2 9.7 %collective-permute-start.46 = (f32[4]{0:T(128)S(1)}, f32[4]{0:T(128)S(1)}, u32[]{:S(2)}, u32[]{:S(2)}) collective-permute-start(f32[4]{0:T(128)S(1)} %add.637.refs_13_), channel_id=1, source_target_pairs={{0,8},{8,0},{16,24},{24,16},{1,9},{9,1},{17,25},{25,17},{2,10},{10... | collective-permute-start | bytes 56 | tf_op jit(solution)/shard_map/ppermute | solution.py:248
  470.3 33.0 %ssm_back.1 = (f32[512,1536]{1,0:T(8,128)S(1)}, f32[512,128]{1,0:T(8,128)S(1)}, f32[512,128]{1,0:T(8,128)S(1)}, f32[12,8,512]{2,1,0:T(8,128)S(1)}) custom-call(s32[5]{0:T(128)S(1)} %copy-done.63, f32[512,1792]{1,0:T(8,128)} %conv.1.refs_0_.refs_1_.x_ref.b_ref.c_ref.refs_3_.refs_4_, f32[512,1536]{1,0:T(8,128)S(1)} %copy-done.9, ...), custom_call_target="tpu_custom_call" | custom-call | flops 3000000000 | bytes 9437184 | tf_op jit(solution)/shard_map/ssm_back/pallas_call | solution.py:1088
  516.4 12.9 %collective-permute-start.81 = (f32[4]{0:T(128)S(1)}, f32[4]{0:T(128)S(1)}, u32[]{:S(2)}, u32[]{:S(2)}) collective-permute-start(f32[4]{0:T(128)S(1)} %add.653.refs_11_), channel_id=1, source_target_pairs={{0,16},{16,0},{8,24},{24,8},{1,17},{17,1},{9,25},{25,9},{2,18},{18... | collective-permute-start | bytes 56 | tf_op jit(solution)/shard_map/ppermute | solution.py:248
  530.7 14.7 %conv_back.1 = (bf16[512,1792]{1,0:T(8,128)(2,1)}, f32[16,1792]{1,0:T(8,128)}, f32[8,1792]{1,0:T(8,128)}, f32[8,1792]{1,0:T(8,128)}) custom-call(s32[5]{0:T(128)} %pad_add_fusion.1.refs_0_.meta_ref, f32[512,1536]{1,0:T(8,128)} %get-tuple-element.85.refs_1_, f32[512,128]{1,0:T(8,128)} %get-tuple-element.86.refs_2_, f32[512,128]{1,0:T(8,128)} %get-tuple-element.87.refs_3_, ...), custom_call_target="tpu_custom_call" | custom-call | flops 2000000000 | bytes 9175040 | tf_op jit(solution)/shard_map/conv_back/pallas_call | solution.py:818
  558.4 10.5 %pack.6 = bf16[49440,128]{1,0:T(8,128)(2,1)} custom-call(bf16[512,512]{1,0:T(8,128)(2,1)S(1)} %bitcast.278, bf16[512,1024]{1,0:T(8,128)(2,1)S(1)} %copy-done.2, bf16[512,1024]{1,0:T(8,128)(2,1)S(1)} %copy-done.7, bf16[512,1536]{1,0:T(8,128)(2,1)S(1)} %copy-done.17, bf16[512,1536]{1,0:T(8,128)(2,1)S(1)} %slice.373.refs_4_, ...), custom_call_target="tpu_custom_call", output_to_operand_aliasing={{}: (7, {})} | custom-call | flops 4026531840 | bytes 11010048 | tf_op jit(solution)/shard_map/pack/pallas_call | solution.py:609
  568.9 6.0 constant_dynamic-slice_fusion.1.refs_1_
  580.8 5.1 fusion.105
  589.6 5.1 collective-permute-start.55
  601.5 5.0 fusion.85
  606.6 6.2 add_convert_fusion
  621.6 7.6 attend_back.2
  629.2 23.9 %collective-permute-done.51 = bf16[2,3104,128]{2,1,0:T(8,128)(2,1)} collective-permute-done((bf16[2,3104,128]{2,1,0:T(8,128)(2,1)}, bf16[2,3104,128]{2,1,0:T(8,128)(2,1)}, u32[]{:S(2)}, u32[]{:S(2)}) %collective-permute-start.51) | collective-permute-done | bytes 1589280 | tf_op jit(solution)/shard_map/ppermute | solution.py:248
  664.2 8.0 attend_back.3
  703.3 11.6 %collective-permute-start.62 = (bf16[2,2,512,128]{3,2,1,0:T(8,128)(2,1)S(1)}, bf16[2,2,512,128]{3,2,1,0:T(8,128)(2,1)}, u32[]{:S(2)}, u32[]{:S(2)}) collective-permute-start(bf16[2,2,512,128]{3,2,1,0:T(8,128)(2,1)S(1)} %dynamic-slice_bitcast_fusion.21.refs_1_), channel_id=1, source_target_pairs={{0,4},{4,0},{1,5},{5,1},{2,6},{6,2},{3,7},{7,3},{8,12},{12,8},{9,1... | collective-permute-start | bytes 1572872 | tf_op jit(solution)/shard_map/ppermute | solution.py:248
  721.0 6.1 collective-permute-done.62
  728.4 5.9 collective-permute-start.63
  734.3 5.6 add_add_fusion.4.refs_0_
  744.0 4.8 fusion.12
  780.7 19.7 %collective-permute-done.70.refs_1_ = bf16[3104,128]{1,0:T(8,128)(2,1)S(1)} collective-permute-done((bf16[3104,128]{1,0:T(8,128)(2,1)S(1)}, bf16[3104,128]{1,0:T(8,128)(2,1)S(1)}, u32[]{:S(2)}, u32[]{:S(2)}) %collective-permute-start.70) | collective-permute-done | bytes 794656 | tf_op jit(solution)/shard_map/ppermute | solution.py:248
  828.3 4.8 fusion.14
  (791 shorter events, 334.6 us)
Async XLA Ops:
  7.2 220.7 %all-gather.3.cloned.1.call-start = ((), (), s32[]{:S(2)}) async-start(), calls=%async_computation | async-start | bytes 2359296 | tf_op jit(solution)/shard_map/all_gather | solution.py:1541
  18.6 17.1 %collective-permute-start.1 = (bf16[3088,128]{1,0:T(8,128)(2,1)S(1)}, bf16[3088,128]{1,0:T(8,128)(2,1)S(1)}, u32[]{:S(2)}, u32[]{:S(2)}) collective-permute-start(bf16[3088,128]{1,0:T(8,128)(2,1)S(1)} %get-tuple-element.170), channel_id=1, source_target_pairs={{0,8},{9,17},{2,10},{11,19},{4,12},{13,21},{6,14},{15,23}} | collective-permute-start | bytes 2371592 | tf_op jit(solution)/shard_map/ppermute | solution.py:287
  43.9 32.2 %collective-permute-start.26 = (bf16[2,3088,128]{2,1,0:T(8,128)(2,1)}, bf16[2,3088,128]{2,1,0:T(8,128)(2,1)}, u32[]{:S(2)}, u32[]{:S(2)}) collective-permute-start(bf16[2,3088,128]{2,1,0:T(8,128)(2,1)} %collective-permute-done.24), channel_id=1, source_target_pairs={{8,0},{17,9},{10,2},{19,11},{12,4},{21,13},{14,6},{23,15}} | collective-permute-start | bytes 4743176 | tf_op jit(solution)/shard_map/ppermute | solution.py:302
  48.2 27.9 %collective-permute-start.17 = (bf16[3088,128]{1,0:T(8,128)(2,1)}, bf16[3088,128]{1,0:T(8,128)(2,1)}, u32[]{:S(2)}, u32[]{:S(2)}) collective-permute-start(bf16[3088,128]{1,0:T(8,128)(2,1)} %add_select_fusion.1), channel_id=1, source_target_pairs={{0,4},{4,0},{1,5},{5,1},{2,6},{6,2},{3,7},{7,3},{8,12},{12,8},{9,1... | collective-permute-start | bytes 2371592 | tf_op jit(solution)/shard_map/ppermute | solution.py:293
  49.7 38.7 %collective-permute-start.16 = (bf16[3088,128]{1,0:T(8,128)(2,1)}, bf16[3088,128]{1,0:T(8,128)(2,1)}, u32[]{:S(2)}, u32[]{:S(2)}) collective-permute-start(bf16[3088,128]{1,0:T(8,128)(2,1)} %add_select_fusion.1), channel_id=1, source_target_pairs={{0,2},{2,0},{1,3},{3,1},{4,6},{6,4},{5,7},{7,5},{8,10},{10,8},{9,1... | collective-permute-start | bytes 2371592 | tf_op jit(solution)/shard_map/ppermute | solution.py:292
  52.7 35.7 %collective-permute-start.5 = (bf16[3088,128]{1,0:T(8,128)(2,1)S(1)}, bf16[3088,128]{1,0:T(8,128)(2,1)S(1)}, u32[]{:S(2)}, u32[]{:S(2)}) collective-permute-start(bf16[3088,128]{1,0:T(8,128)(2,1)S(1)} %add_select_fusion.2), channel_id=1, source_target_pairs={{0,2},{2,0},{1,3},{3,1},{4,6},{6,4},{5,7},{7,5},{8,10},{10,8},{9,1... | collective-permute-start | bytes 2371592 | tf_op jit(solution)/shard_map/ppermute | solution.py:292
  53.3 36.8 %collective-permute-start.6 = (bf16[3088,128]{1,0:T(8,128)(2,1)S(1)}, bf16[3088,128]{1,0:T(8,128)(2,1)S(1)}, u32[]{:S(2)}, u32[]{:S(2)}) collective-permute-start(bf16[3088,128]{1,0:T(8,128)(2,1)S(1)} %add_select_fusion.2), channel_id=1, source_target_pairs={{0,4},{4,0},{1,5},{5,1},{2,6},{6,2},{3,7},{7,3},{8,12},{12,8},{9,1... | collective-permute-start | bytes 2371592 | tf_op jit(solution)/shard_map/ppermute | solution.py:293
  76.1 34.2 %collective-permute-start.27 = (bf16[2,3088,128]{2,1,0:T(8,128)(2,1)}, bf16[2,3088,128]{2,1,0:T(8,128)(2,1)}, u32[]{:S(2)}, u32[]{:S(2)}) collective-permute-start(bf16[2,3088,128]{2,1,0:T(8,128)(2,1)} %collective-permute-done.26), channel_id=1, source_target_pairs={{9,1},{11,3},{13,5},{15,7}} | collective-permute-start | bytes 4743176 | tf_op jit(solution)/shard_map/ppermute | solution.py:303
  88.5 20.4 %collective-permute-start.18 = (bf16[3088,128]{1,0:T(8,128)(2,1)}, bf16[3088,128]{1,0:T(8,128)(2,1)}, u32[]{:S(2)}, u32[]{:S(2)}) collective-permute-start(bf16[3088,128]{1,0:T(8,128)(2,1)} %collective-permute-done.17), channel_id=1, source_target_pairs={{0,2},{2,0},{1,3},{3,1},{4,6},{6,4},{5,7},{7,5},{8,10},{10,8},{9,1... | collective-permute-start | bytes 2371592 | tf_op jit(solution)/shard_map/ppermute | solution.py:294
  90.0 19.8 %collective-permute-start.7 = (bf16[3088,128]{1,0:T(8,128)(2,1)S(1)}, bf16[3088,128]{1,0:T(8,128)(2,1)}, u32[]{:S(2)}, u32[]{:S(2)}) collective-permute-start(bf16[3088,128]{1,0:T(8,128)(2,1)S(1)} %collective-permute-done.5), channel_id=1, source_target_pairs={{0,4},{4,0},{1,5},{5,1},{2,6},{6,2},{3,7},{7,3},{8,12},{12,8},{9,1... | collective-permute-start | bytes 2371592 | tf_op jit(solution)/shard_map/ppermute | solution.py:294
  91.6 18.3 %collective-permute-start.21 = (bf16[3088,128]{1,0:T(8,128)(2,1)}, bf16[3088,128]{1,0:T(8,128)(2,1)}, u32[]{:S(2)}, u32[]{:S(2)}) collective-permute-start(bf16[3088,128]{1,0:T(8,128)(2,1)} %collective-permute-done.17), channel_id=1, source_target_pairs={{0,1},{1,0},{2,3},{3,2},{4,5},{5,4},{6,7},{7,6},{8,9},{9,8},{10,11... | collective-permute-start | bytes 2371592 | tf_op jit(solution)/shard_map/ppermute | solution.py:297
  94.1 21.8 %collective-permute-start.9 = (bf16[3088,128]{1,0:T(8,128)(2,1)S(1)}, bf16[3088,128]{1,0:T(8,128)(2,1)S(1)}, u32[]{:S(2)}, u32[]{:S(2)}) collective-permute-start(bf16[3088,128]{1,0:T(8,128)(2,1)S(1)} %collective-permute-done.5), channel_id=1, source_target_pairs={{0,1},{1,0},{2,3},{3,2},{4,5},{5,4},{6,7},{7,6},{8,9},{9,8},{10,11... | collective-permute-start | bytes 2371592 | tf_op jit(solution)/shard_map/ppermute | solution.py:297
  115.8 40.3 %collective-permute-start.28 = (bf16[2,3088,128]{2,1,0:T(8,128)(2,1)}, bf16[2,3088,128]{2,1,0:T(8,128)(2,1)}, u32[]{:S(2)}, u32[]{:S(2)}) collective-permute-start(bf16[2,3088,128]{2,1,0:T(8,128)(2,1)} %add_select_fusion.refs_1_.refs_6_.refs_18_), channel_id=1, source_target_pairs={{0,2},{2,0},{1,3},{3,1},{4,6},{6,4},{5,7},{7,5},{8,10},{10,8},{9,1... | collective-permute-start | bytes 4743176 | tf_op jit(solution)/shard_map/ppermute | solution.py:248
  116.8 40.9 %collective-permute-start.29 = (bf16[2,3088,128]{2,1,0:T(8,128)(2,1)}, bf16[2,3088,128]{2,1,0:T(8,128)(2,1)}, u32[]{:S(2)}, u32[]{:S(2)}) collective-permute-start(bf16[2,3088,128]{2,1,0:T(8,128)(2,1)} %add_select_fusion.refs_1_.refs_6_.refs_18_), channel_id=1, source_target_pairs={{0,4},{4,0},{1,5},{5,1},{2,6},{6,2},{3,7},{7,3},{8,12},{12,8},{9,1... | collective-permute-start | bytes 4743176 | tf_op jit(solution)/shard_map/ppermute | solution.py:248
  118.3 146.9 %collective-permute-start.35 = (bf16[2,3088,128]{2,1,0:T(8,128)(2,1)}, bf16[2,3088,128]{2,1,0:T(8,128)(2,1)}, u32[]{:S(2)}, u32[]{:S(2)}) collective-permute-start(bf16[2,3088,128]{2,1,0:T(8,128)(2,1)} %add_select_fusion.refs_1_.refs_6_.refs_18_), channel_id=1, source_target_pairs={{0,1},{1,0},{2,3},{3,2},{4,5},{5,4},{6,7},{7,6},{8,9},{9,8},{10,11... | collective-permute-start | bytes 4743176 | tf_op jit(solution)/shard_map/ppermute | solution.py:248
  157.3 29.4 %collective-permute-start.30 = (bf16[1,3088,128]{2,1,0:T(8,128)(2,1)S(1)}, bf16[1,3088,128]{2,1,0:T(8,128)(2,1)}, u32[]{:S(2)}, u32[]{:S(2)}) collective-permute-start(bf16[1,3088,128]{2,1,0:T(8,128)(2,1)S(1)} %slice.346.refs_3_), channel_id=1, source_target_pairs={{0,4},{4,0},{1,5},{5,1},{2,6},{6,2},{3,7},{7,3},{8,12},{12,8},{9,1... | collective-permute-start | bytes 2371592 | tf_op jit(solution)/shard_map/ppermute | solution.py:248
  159.8 26.9 %collective-permute-start.31 = (bf16[1,3088,128]{2,1,0:T(8,128)(2,1)}, bf16[1,3088,128]{2,1,0:T(8,128)(2,1)}, u32[]{:S(2)}, u32[]{:S(2)}) collective-permute-start(bf16[1,3088,128]{2,1,0:T(8,128)(2,1)} %slice.347.refs_4_), channel_id=1, source_target_pairs={{0,2},{2,0},{1,3},{3,1},{4,6},{6,4},{5,7},{7,5},{8,10},{10,8},{9,1... | collective-permute-start | bytes 2371592 | tf_op jit(solution)/shard_map/ppermute | solution.py:248
  188.1 18.4 %collective-permute-start.32 = (bf16[144,1536]{1,0:T(8,128)(2,1)S(1)}, bf16[144,1536]{1,0:T(8,128)(2,1)}, u32[]{:S(2)}, u32[]{:S(2)}) collective-permute-start(bf16[144,1536]{1,0:T(8,128)(2,1)S(1)} %pad_maximum_fusion.14.refs_1_), channel_id=1, source_target_pairs={{0,1},{1,0},{2,3},{3,2},{4,5},{5,4},{6,7},{7,6},{8,9},{9,8},{10,11... | collective-permute-start | bytes 1327112 | tf_op jit(solution)/shard_map/ppermute | solution.py:248
  205.7 59.6 %collective-permute-start.36 = (bf16[2,3088,128]{2,1,0:T(8,128)(2,1)}, bf16[2,3088,128]{2,1,0:T(8,128)(2,1)}, u32[]{:S(2)}, u32[]{:S(2)}) collective-permute-start(bf16[2,3088,128]{2,1,0:T(8,128)(2,1)} %collective-permute-done.28.refs_2_.refs_7_.refs_19_), channel_id=1, source_target_pairs={{0,1},{1,0},{2,3},{3,2},{4,5},{5,4},{6,7},{7,6},{8,9},{9,8},{10,11... | collective-permute-start | bytes 4743176 | tf_op jit(solution)/shard_map/ppermute | solution.py:248
  205.9 59.4 %collective-permute-start.37 = (bf16[2,3088,128]{2,1,0:T(8,128)(2,1)}, bf16[2,3088,128]{2,1,0:T(8,128)(2,1)}, u32[]{:S(2)}, u32[]{:S(2)}) collective-permute-start(bf16[2,3088,128]{2,1,0:T(8,128)(2,1)} %collective-permute-done.29.refs_3_.refs_8_.refs_20_), channel_id=1, source_target_pairs={{0,1},{1,0},{2,3},{3,2},{4,5},{5,4},{6,7},{7,6},{8,9},{9,8},{10,11... | collective-permute-start | bytes 4743176 | tf_op jit(solution)/shard_map/ppermute | solution.py:248
  206.2 59.1 %collective-permute-start.38 = (bf16[1,3088,128]{2,1,0:T(8,128)(2,1)}, bf16[1,3088,128]{2,1,0:T(8,128)(2,1)}, u32[]{:S(2)}, u32[]{:S(2)}) collective-permute-start(bf16[1,3088,128]{2,1,0:T(8,128)(2,1)} %collective-permute-done.30.refs_4_.refs_9_.refs_21_), channel_id=1, source_target_pairs={{0,1},{1,0},{2,3},{3,2},{4,5},{5,4},{6,7},{7,6},{8,9},{9,8},{10,11... | collective-permute-start | bytes 2371592 | tf_op jit(solution)/shard_map/ppermute | solution.py:248
  224.9 19.4 %collective-permute-start.34 = (bf16[144,1536]{1,0:T(8,128)(2,1)S(1)}, bf16[144,1536]{1,0:T(8,128)(2,1)}, u32[]{:S(2)}, u32[]{:S(2)}) collective-permute-start(bf16[144,1536]{1,0:T(8,128)(2,1)S(1)} %pad_maximum_fusion.16.refs_4_), channel_id=1, source_target_pairs={{0,4},{4,0},{1,5},{5,1},{2,6},{6,2},{3,7},{7,3},{8,12},{12,8},{9,1... | collective-permute-start | bytes 1327112 | tf_op jit(solution)/shard_map/ppermute | solution.py:248
  244.2 21.1 %collective-permute-start.39 = (bf16[1,3088,128]{2,1,0:T(8,128)(2,1)}, bf16[1,3088,128]{2,1,0:T(8,128)(2,1)}, u32[]{:S(2)}, u32[]{:S(2)}) collective-permute-start(bf16[1,3088,128]{2,1,0:T(8,128)(2,1)} %collective-permute-done.31.refs_5_.refs_10_.refs_22_), channel_id=1, source_target_pairs={{0,1},{1,0},{2,3},{3,2},{4,5},{5,4},{6,7},{7,6},{8,9},{9,8},{10,11... | collective-permute-start | bytes 2371592 | tf_op jit(solution)/shard_map/ppermute | solution.py:248
  365.7 27.8 %collective-permute-start.41 = (bf16[144,1536]{1,0:T(8,128)(2,1)S(1)}, bf16[144,1536]{1,0:T(8,128)(2,1)S(1)}, u32[]{:S(2)}, u32[]{:S(2)}) collective-permute-start(bf16[144,1536]{1,0:T(8,128)(2,1)S(1)} %pad_maximum_fusion.18.refs_7_), channel_id=1, source_target_pairs={{0,2},{2,0},{1,3},{3,1},{4,6},{6,4},{5,7},{7,5},{8,10},{10,8},{9,1... | collective-permute-start | bytes 1327112 | tf_op jit(solution)/shard_map/ppermute | solution.py:248
  404.0 32.5 %collective-permute-start.43 = (bf16[24688,128]{1,0:T(8,128)(2,1)}, bf16[24688,128]{1,0:T(8,128)(2,1)}, u32[]{:S(2)}, u32[]{:S(2)}) collective-permute-start(bf16[24688,128]{1,0:T(8,128)(2,1)} %constant_dynamic-slice_fusion.2.refs_2_), channel_id=1, source_target_pairs={{0,1},{1,0},{2,3},{3,2},{4,5},{5,4},{6,7},{7,6},{8,9},{9,8},{10,11... | collective-permute-start | bytes 18960392 | tf_op jit(solution)/shard_map/ppermute | solution.py:248
  406.8 48.3 %collective-permute-start.42 = (bf16[144,1536]{1,0:T(8,128)(2,1)}, bf16[144,1536]{1,0:T(8,128)(2,1)}, u32[]{:S(2)}, u32[]{:S(2)}) collective-permute-start(bf16[144,1536]{1,0:T(8,128)(2,1)} %pad_maximum_fusion.19.refs_1_), channel_id=1, source_target_pairs={{0,4},{4,0},{1,5},{5,1},{2,6},{6,2},{3,7},{7,3},{8,12},{12,8},{9,1... | collective-permute-start | bytes 1327112 | tf_op jit(solution)/shard_map/ppermute | solution.py:248
  445.9 61.1 %collective-permute-start.44 = (bf16[2,3104,128]{2,1,0:T(8,128)(2,1)}, bf16[2,3104,128]{2,1,0:T(8,128)(2,1)}, u32[]{:S(2)}, u32[]{:S(2)}) collective-permute-start(bf16[2,3104,128]{2,1,0:T(8,128)(2,1)} %pad_maximum_fusion.4.refs_11_.refs_1_), channel_id=1, source_target_pairs={{0,4},{4,0},{1,5},{5,1},{2,6},{6,2},{3,7},{7,3},{8,12},{12,8},{9,1... | collective-permute-start | bytes 4767752 | tf_op jit(solution)/shard_map/ppermute | solution.py:248
  456.2 59.1 %collective-permute-start.46 = (f32[4]{0:T(128)S(1)}, f32[4]{0:T(128)S(1)}, u32[]{:S(2)}, u32[]{:S(2)}) collective-permute-start(f32[4]{0:T(128)S(1)} %add.637.refs_13_), channel_id=1, source_target_pairs={{0,8},{8,0},{16,24},{24,16},{1,9},{9,1},{17,25},{25,17},{2,10},{10... | collective-permute-start | bytes 56 | tf_op jit(solution)/shard_map/ppermute | solution.py:248
  469.8 42.2 %collective-permute-start.45 = (bf16[2,3104,128]{2,1,0:T(8,128)(2,1)}, bf16[2,3104,128]{2,1,0:T(8,128)(2,1)}, u32[]{:S(2)}, u32[]{:S(2)}) collective-permute-start(bf16[2,3104,128]{2,1,0:T(8,128)(2,1)} %pad_maximum_fusion.5.refs_12_.refs_2_), channel_id=1, source_target_pairs={{0,2},{2,0},{1,3},{3,1},{4,6},{6,4},{5,7},{7,5},{8,10},{10,8},{9,1... | collective-permute-start | bytes 4767752 | tf_op jit(solution)/shard_map/ppermute | solution.py:248
  510.4 35.9 %collective-permute-start.47 = (bf16[3104,128]{1,0:T(8,128)(2,1)}, bf16[3104,128]{1,0:T(8,128)(2,1)}, u32[]{:S(2)}, u32[]{:S(2)}) collective-permute-start(bf16[3104,128]{1,0:T(8,128)(2,1)} %dynamic-slice_bitcast_fusion.14.refs_4_.refs_9_), channel_id=1, source_target_pairs={{0,2},{2,0},{1,3},{3,1},{4,6},{6,4},{5,7},{7,5},{8,10},{10,8},{9,1... | collective-permute-start | bytes 2383880 | tf_op jit(solution)/shard_map/ppermute | solution.py:248
  515.2 32.7 %collective-permute-start.48 = (bf16[3104,128]{1,0:T(8,128)(2,1)}, bf16[3104,128]{1,0:T(8,128)(2,1)}, u32[]{:S(2)}, u32[]{:S(2)}) collective-permute-start(bf16[3104,128]{1,0:T(8,128)(2,1)} %dynamic-slice_bitcast_fusion.11.refs_5_.refs_10_), channel_id=1, source_target_pairs={{0,4},{4,0},{1,5},{5,1},{2,6},{6,2},{3,7},{7,3},{8,12},{12,8},{9,1... | collective-permute-start | bytes 2383880 | tf_op jit(solution)/shard_map/ppermute | solution.py:248
  516.4 37.2 %collective-permute-start.81 = (f32[4]{0:T(128)S(1)}, f32[4]{0:T(128)S(1)}, u32[]{:S(2)}, u32[]{:S(2)}) collective-permute-start(f32[4]{0:T(128)S(1)} %add.653.refs_11_), channel_id=1, source_target_pairs={{0,16},{16,0},{8,24},{24,8},{1,17},{17,1},{9,25},{25,9},{2,18},{18... | collective-permute-start | bytes 56 | tf_op jit(solution)/shard_map/ppermute | solution.py:248
  574.8 31.7 %collective-permute-start.50 = (bf16[24688,128]{1,0:T(8,128)(2,1)}, bf16[24688,128]{1,0:T(8,128)(2,1)}, u32[]{:S(2)}, u32[]{:S(2)}) collective-permute-start(bf16[24688,128]{1,0:T(8,128)(2,1)} %constant_dynamic-slice_fusion.1.refs_1_), channel_id=1, source_target_pairs={{0,1},{1,0},{2,3},{3,2},{4,5},{5,4},{6,7},{7,6},{8,9},{9,8},{10,11... | collective-permute-start | bytes 18960392 | tf_op jit(solution)/shard_map/ppermute | solution.py:248
  587.7 96.1 %collective-permute-start.54 = (bf16[2,3104,128]{2,1,0:T(8,128)(2,1)}, bf16[2,3104,128]{2,1,0:T(8,128)(2,1)}, u32[]{:S(2)}, u32[]{:S(2)}) collective-permute-start(bf16[2,3104,128]{2,1,0:T(8,128)(2,1)} %pad_maximum_fusion.6.refs_4_.refs_5_.refs_6_.refs_8_.refs_9_.refs_10_.refs_2_.refs_3_.refs_11_), channel_id=1, source_target_pairs={{8,16},{17,25},{10,18},{19,27},{12,20},{21,29},{14,22},{23,31}} | collective-permute-start | bytes 4767752 | tf_op jit(solution)/shard_map/ppermute | solution.py:248
  589.6 95.5 %collective-permute-start.55 = (bf16[2,3104,128]{2,1,0:T(8,128)(2,1)}, bf16[2,3104,128]{2,1,0:T(8,128)(2,1)}, u32[]{:S(2)}, u32[]{:S(2)}) collective-permute-start(bf16[2,3104,128]{2,1,0:T(8,128)(2,1)} %pad_maximum_fusion.6.refs_4_.refs_5_.refs_6_.refs_8_.refs_9_.refs_10_.refs_2_.refs_3_.refs_11_), channel_id=1, source_target_pairs={{0,16},{9,25},{2,18},{11,27},{4,20},{13,29},{6,22},{15,31}} | collective-permute-start | bytes 4767752 | tf_op jit(solution)/shard_map/ppermute | solution.py:248
  594.8 91.8 %collective-permute-start.56 = (bf16[2,3104,128]{2,1,0:T(8,128)(2,1)}, bf16[2,3104,128]{2,1,0:T(8,128)(2,1)}, u32[]{:S(2)}, u32[]{:S(2)}) collective-permute-start(bf16[2,3104,128]{2,1,0:T(8,128)(2,1)} %pad_maximum_fusion.6.refs_4_.refs_5_.refs_6_.refs_8_.refs_9_.refs_10_.refs_2_.refs_3_.refs_11_), channel_id=1, source_target_pairs={{24,16},{1,25},{26,18},{3,27},{28,20},{5,29},{30,22},{7,31}} | collective-permute-start | bytes 4767752 | tf_op jit(solution)/shard_map/ppermute | solution.py:248
  616.1 37.1 %collective-permute-start.51 = (bf16[2,3104,128]{2,1,0:T(8,128)(2,1)}, bf16[2,3104,128]{2,1,0:T(8,128)(2,1)}, u32[]{:S(2)}, u32[]{:S(2)}) collective-permute-start(bf16[2,3104,128]{2,1,0:T(8,128)(2,1)} %pad_maximum_fusion.7.refs_1_.refs_7_), channel_id=1, source_target_pairs={{0,4},{4,0},{1,5},{5,1},{2,6},{6,2},{3,7},{7,3},{8,12},{12,8},{9,1... | collective-permute-start | bytes 4767752 | tf_op jit(solution)/shard_map/ppermute | solution.py:248
  618.9 39.8 %collective-permute-start.52 = (bf16[2,3104,128]{2,1,0:T(8,128)(2,1)}, bf16[2,3104,128]{2,1,0:T(8,128)(2,1)}, u32[]{:S(2)}, u32[]{:S(2)}) collective-permute-start(bf16[2,3104,128]{2,1,0:T(8,128)(2,1)} %pad_maximum_fusion.8.refs_2_.refs_8_), channel_id=1, source_target_pairs={{0,2},{2,0},{1,3},{3,1},{4,6},{6,4},{5,7},{7,5},{8,10},{10,8},{9,1... | collective-permute-start | bytes 4767752 | tf_op jit(solution)/shard_map/ppermute | solution.py:248
  656.2 19.9 %collective-permute-start.53 = (bf16[3104,128]{1,0:T(8,128)(2,1)}, bf16[3104,128]{1,0:T(8,128)(2,1)}, u32[]{:S(2)}, u32[]{:S(2)}) collective-permute-start(bf16[3104,128]{1,0:T(8,128)(2,1)} %dynamic-slice_bitcast_fusion.4.refs_2_.refs_7_), channel_id=1, source_target_pairs={{0,2},{2,0},{1,3},{3,1},{4,6},{6,4},{5,7},{7,5},{8,10},{10,8},{9,1... | collective-permute-start | bytes 2383880 | tf_op jit(solution)/shard_map/ppermute | solution.py:248
  662.6 32.2 %collective-permute-start.58 = (bf16[3104,128]{1,0:T(8,128)(2,1)}, bf16[3104,128]{1,0:T(8,128)(2,1)}, u32[]{:S(2)}, u32[]{:S(2)}) collective-permute-start(bf16[3104,128]{1,0:T(8,128)(2,1)} %dynamic-slice_bitcast_fusion.1.refs_3_.refs_8_), channel_id=1, source_target_pairs={{0,4},{4,0},{1,5},{5,1},{2,6},{6,2},{3,7},{7,3},{8,12},{12,8},{9,1... | collective-permute-start | bytes 2383880 | tf_op jit(solution)/shard_map/ppermute | solution.py:248
  678.4 36.5 %collective-permute-start.59 = (bf16[3104,128]{1,0:T(8,128)(2,1)}, bf16[3104,128]{1,0:T(8,128)(2,1)}, u32[]{:S(2)}, u32[]{:S(2)}) collective-permute-start(bf16[3104,128]{1,0:T(8,128)(2,1)} %fusion.20.refs_2_.refs_3_.refs_4_), channel_id=1, source_target_pairs={{8,0},{17,9},{10,2},{19,11},{12,4},{21,13},{14,6},{23,15}} | collective-permute-start | bytes 2383880 | tf_op jit(solution)/shard_map/ppermute | solution.py:248
  683.8 34.1 %collective-permute-start.60 = (bf16[3104,128]{1,0:T(8,128)(2,1)}, bf16[3104,128]{1,0:T(8,128)(2,1)}, u32[]{:S(2)}, u32[]{:S(2)}) collective-permute-start(bf16[3104,128]{1,0:T(8,128)(2,1)} %fusion.20.refs_2_.refs_3_.refs_4_), channel_id=1, source_target_pairs={{16,0},{25,9},{18,2},{27,11},{20,4},{29,13},{22,6},{31,15}} | collective-permute-start | bytes 2383880 | tf_op jit(solution)/shard_map/ppermute | solution.py:248
  685.1 32.8 %collective-permute-start.61 = (bf16[3104,128]{1,0:T(8,128)(2,1)}, bf16[3104,128]{1,0:T(8,128)(2,1)}, u32[]{:S(2)}, u32[]{:S(2)}) collective-permute-start(bf16[3104,128]{1,0:T(8,128)(2,1)} %fusion.20.refs_2_.refs_3_.refs_4_), channel_id=1, source_target_pairs={{24,0},{1,9},{26,2},{3,11},{28,4},{5,13},{30,6},{7,15}} | collective-permute-start | bytes 2383880 | tf_op jit(solution)/shard_map/ppermute | solution.py:248
  703.3 23.8 %collective-permute-start.62 = (bf16[2,2,512,128]{3,2,1,0:T(8,128)(2,1)S(1)}, bf16[2,2,512,128]{3,2,1,0:T(8,128)(2,1)}, u32[]{:S(2)}, u32[]{:S(2)}) collective-permute-start(bf16[2,2,512,128]{3,2,1,0:T(8,128)(2,1)S(1)} %dynamic-slice_bitcast_fusion.21.refs_1_), channel_id=1, source_target_pairs={{0,4},{4,0},{1,5},{5,1},{2,6},{6,2},{3,7},{7,3},{8,12},{12,8},{9,1... | collective-permute-start | bytes 1572872 | tf_op jit(solution)/shard_map/ppermute | solution.py:248
  760.2 20.5 %collective-permute-start.69 = (bf16[3104,128]{1,0:T(8,128)(2,1)S(1)}, bf16[3104,128]{1,0:T(8,128)(2,1)S(1)}, u32[]{:S(2)}, u32[]{:S(2)}) collective-permute-start(bf16[3104,128]{1,0:T(8,128)(2,1)S(1)} %copy-done.3), channel_id=1, source_target_pairs={{8,0},{17,9},{10,2},{19,11},{12,4},{21,13},{14,6},{23,15}} | collective-permute-start | bytes 2383880 | tf_op jit(solution)/shard_map/ppermute | solution.py:248
  761.5 38.9 %collective-permute-start.70 = (bf16[3104,128]{1,0:T(8,128)(2,1)S(1)}, bf16[3104,128]{1,0:T(8,128)(2,1)S(1)}, u32[]{:S(2)}, u32[]{:S(2)}) collective-permute-start(bf16[3104,128]{1,0:T(8,128)(2,1)S(1)} %copy-done.3), channel_id=1, source_target_pairs={{16,0},{25,9},{18,2},{27,11},{20,4},{29,13},{22,6},{31,15}} | collective-permute-start | bytes 2383880 | tf_op jit(solution)/shard_map/ppermute | solution.py:248
  762.8 37.6 %collective-permute-start.71 = (bf16[3104,128]{1,0:T(8,128)(2,1)S(1)}, bf16[3104,128]{1,0:T(8,128)(2,1)}, u32[]{:S(2)}, u32[]{:S(2)}) collective-permute-start(bf16[3104,128]{1,0:T(8,128)(2,1)S(1)} %copy-done.3), channel_id=1, source_target_pairs={{24,0},{1,9},{26,2},{3,11},{28,4},{5,13},{30,6},{7,15}} | collective-permute-start | bytes 2383880 | tf_op jit(solution)/shard_map/ppermute | solution.py:248
  809.4 25.1 %collective-permute-start.80 = (bf16[3104,128]{1,0:T(8,128)(2,1)}, bf16[3104,128]{1,0:T(8,128)(2,1)S(1)}, u32[]{:S(2)}, u32[]{:S(2)}) collective-permute-start(bf16[3104,128]{1,0:T(8,128)(2,1)} %get-tuple-element.168.refs_5_), channel_id=1, source_target_pairs={{0,1},{9,8},{16,17},{25,24},{2,3},{11,10},{18,19},{27,26},{4,5},{1... | collective-permute-start | bytes 2383880 | tf_op jit(solution)/shard_map/ppermute | solution.py:248
  (224 other events, 2356.9 us)
Sparse Core Ops, SparseCore 0:
  147.8 44.0 all-gather.2

commit v15 on v14

--- a/solution.py
+++ b/solution.py
@@ -1488,8 +1488,9 @@
     shard = SHARD * place
     start = jnp.where(z < 2, (8 + shard) % 16, (14 + shard) % 16)
     lines = jnp.where(z < 2, early, late)
-    lines = jnp.where((z == 0) & (place < 2), corner[:WIN], lines)
-    lines = lax.dynamic_slice(lines, (start, 0), (SHARD, LINE)).astype(jnp.float32)
+    lines = lax.dynamic_slice(lines, (start, 0), (SHARD, LINE))
+    edge = lax.dynamic_slice(corner, (start, 0), (SHARD, LINE))
+    lines = jnp.where((z == 0) & (place < 2), edge, lines).astype(jnp.float32)
     return lines.reshape(-1)
 
 

time: 852 us -> 852 us (level)
  no operation moved by 1% of the time
where the time goes in v15:
time: 852 us; the launch traced here: 844 us
  starting transfers between devices  196 us (23%)
  Pallas kernels  195 us (23%)
  other arithmetic  138 us (16%)
  waiting for transfers between devices  132 us (15%)
  local copies, waits for them, and re-layouts  82.7 us (10%)
  matrix products  80.9 us (9%)
  between operations  18.5 us (2%)
    ppermute x53, starting transfers between devices, go(): lax.ppermute(value, axis, pairs)  163 us
    ppermute x53, waiting for transfers between devices, go(): lax.ppermute(value, axis, pairs)  81.6 us
    dot_general x12, matrix products, matmul_right_t(): lax.dot_general(left, right, (((1,), (1,)), ((), ())), preferred_element_...  47.3 us
    pallas_call x2, Pallas kernels, unpack_lines(): pl.pallas_call(pinned(kernel, 2 + count_buffers, after), grid_spec=pltpu....  41.4 us
    pallas_call x4, Pallas kernels, pack_lines(): pl.pallas_call(pinned(kernel, inputs, after), grid=(total,), in_specs=[le...  38.2 us
    unnamed x383, local copies, waits for them, and re-layouts  36.2 us
    convert_element_type x14, other arithmetic, added(): return total.astype(jnp.bfloat16)  34.3 us
    pallas_call x1, Pallas kernels, ssm_backward(): pl.pallas_call(pinned(kernel, 11, after), grid_spec=pltpu.PrefetchScalarG...  33 us
  transfers between devices with their start and end apart: 83, of which 23 were waited for; matrix products, arithmetic and copies ran while one was open for 21% of the time, Pallas kernels for 17%

profile of v15, /device:TPU:0, one launch (start us, length us, event | category | flops | bytes accessed | tf_op | source)
XLA Modules:
  0.0 844.0 jit_solution(4475005038749230905)
XLA Ops:
  13.1 5.5 collective-permute-start.12
  19.9 7.3 collective-permute-done.12
  53.8 22.3 %collective-permute-done.26 = bf16[2,3088,128]{2,1,0:T(8,128)(2,1)} collective-permute-done((bf16[2,3088,128]{2,1,0:T(8,128)(2,1)}, bf16[2,3088,128]{2,1,0:T(8,128)(2,1)}, u32[]{:S(2)}, u32[]{:S(2)}) %collective-permute-start.26) | collective-permute-done | bytes 1581088 | tf_op jit(solution)/shard_map/ppermute | solution.py:302
  94.6 14.2 %collective-permute-done.18 = bf16[3088,128]{1,0:T(8,128)(2,1)} collective-permute-done((bf16[3088,128]{1,0:T(8,128)(2,1)}, bf16[3088,128]{1,0:T(8,128)(2,1)}, u32[]{:S(2)}, u32[]{:S(2)}) %collective-permute-start.18) | collective-permute-done | bytes 790560 | tf_op jit(solution)/shard_map/ppermute | solution.py:294
  110.4 5.4 add_select_fusion.refs_1_.refs_6_.refs_18_
  119.8 14.9 %unpack.2 = (bf16[1024,512]{1,0:T(8,128)(2,1)}, bf16[1024,128]{1,0:T(8,128)(2,1)S(1)}, bf16[1024,128]{1,0:T(8,128)(2,1)S(1)}, bf16[512,1024]{1,0:T(8,128)(2,1)},...) custom-call(s32[25,5]{1,0:T(8,128)S(1)} %copy-done.62, ...), custom_call_target="tpu_custom_call" | custom-call | bytes 26624000 | tf_op jit(solution)/shard_map/unpack/pallas_call | solution.py:454
  166.6 11.3 %conv.1.refs_0_.refs_1_.x_ref.b_ref.c_ref.refs_3_.refs_4_ = f32[512,1792]{1,0:T(8,128)} custom-call(s32[5]{0:T(128)} %pad_add_fusion.1.refs_0_.meta_ref, f32[512,1792]{1,0:T(8,128)} %pad_maximum_fusion.refs_1_.refs_4_, f32[8,1792]{1,0:T(8,128)} %copy-done.143, f32[4,1792]{1,0:T(4,128)} %reshape.435.refs_3_.refs_6_, f32[1,1792]{1,0:T(1,128)} %bitcast.330, ...), custom_call_target="tpu_custom_call" | custom-call | flops 1000000000 | bytes 7340032 | tf_op jit(solution)/shard_map/conv/pallas_call | solution.py:759
  177.9 8.8 %state.2.refs_0_ = f32[128,1536]{1,0:T(8,128)} custom-call(f32[512,1792]{1,0:T(8,128)} %conv.1.refs_0_.refs_1_.x_ref.b_ref.c_ref.refs_3_.refs_4_, f32[512,1792]{1,0:T(8,128)} %conv.1.refs_0_.refs_1_.x_ref.b_ref.c_ref.refs_3_.refs_4_, f32[12,2,512]{2,1,0:T(2,128)} %reshape.412.refs_2_, bf16[1,3088,128]{2,1,0:T(8,128)(2,1)} %copy-done.118, ...), custom_call_target="tpu_custom_call" | custom-call | flops 201326592 | bytes 3145728 | tf_op jit(solution)/shard_map/state/pallas_call | solution.py:871
  188.1 15.2 %collective-permute-start.32 = (bf16[144,1536]{1,0:T(8,128)(2,1)S(1)}, bf16[144,1536]{1,0:T(8,128)(2,1)}, u32[]{:S(2)}, u32[]{:S(2)}) collective-permute-start(bf16[144,1536]{1,0:T(8,128)(2,1)S(1)} %pad_maximum_fusion.14.refs_1_), channel_id=1, source_target_pairs={{0,1},{1,0},{2,3},{3,2},{4,5},{5,4},{6,7},{7,6},{8,9},{9,8},{10,11... | collective-permute-start | bytes 1327112 | tf_op jit(solution)/shard_map/ppermute | solution.py:248
  214.8 7.1 collective-permute-done.33
  228.0 14.6 %attend.1 = (f32[8,64,512]{2,1,0:T(8,128)S(1)}, f32[8,8,512]{2,1,0:T(8,128)S(1)}) custom-call(s32[4]{0:T(128)S(1)} %pad_add_fusion.refs_0_, bf16[8,128,512]{2,1,0:T(8,128)(2,1)S(1)} %copy-done.24, bf16[8,2,512,128]{3,2,1,0:T(8,128)(2,1)} %bitcast.335, s32[8,512]{1,0:T(8,128)S(1)} %broadcast_in_dim.286.refs_3_.row_ref.refs_10_.refs_6_, ...), custom_call_target="tpu_custom_call" | custom-call | flops 20000000000 | bytes 8388608 | tf_op jit(solution)/shard_map/attend/pallas_call | solution.py:1240
  244.2 4.7 collective-permute-start.39
  254.6 8.5 %ssm.1.refs_28_ = f32[512,1536]{1,0:T(8,128)S(1)} custom-call(s32[5]{0:T(128)S(1)} %copy-done.63, f32[512,1792]{1,0:T(8,128)S(1)} %copy-done, f32[512,1792]{1,0:T(8,128)S(1)} %copy-done, f32[512,1792]{1,0:T(8,128)S(1)} %copy-done, f32[12,2,512]{2,1,0:T(2,128)S(1)} %reshape_reshape.4.cum_ref.refs_5_, f32[12,2,512]{2,1,0:T(2,128)S(1)} %reshape.415.step_ref.refs_6_, ...), custom_call_target="tpu_custom_call" | custom-call | flops 1000000000 | bytes 6291456 | tf_op jit(solution)/shard_map/ssm/pallas_call | solution.py:949
  268.4 26.5 %unpack.3 = (bf16[1536,1024]{1,0:T(8,128)(2,1)}, bf16[1024,2048]{1,0:T(8,128)(2,1)}, bf16[1024,2048]{1,0:T(8,128)(2,1)}, bf16[2048,1024]{1,0:T(8,128)(2,1)}, bf16[16,128]{1,0:T(8,128)(2,1)S(1)}) custom-call(s32[31,5]{1,0:T(8,128)S(1)} %copy-done.61, s32[32]{0:T(128)S(1)} %fusion.79.refs_1_, bf16[1,3088,128]{2,1,0:T(8,128)(2,1)S(1)} %bitcast.267, ...), custom_call_target="tpu_custom_call" | custom-call | bytes 33013760 | tf_op jit(solution)/shard_map/unpack/pallas_call | solution.py:454
  301.4 4.4 fusion.104
  306.0 4.3 fusion.103
  310.4 6.9 fusion.2
  317.3 6.8 fusion.105
  326.6 4.6 multiply_reduce_fusion.3
  337.6 6.3 fusion.23
  344.0 9.1 %state.3 = f32[128,1536]{1,0:T(8,128)} custom-call(f32[512,1792]{1,0:T(8,128)} %conv.1.refs_0_.refs_1_.x_ref.b_ref.c_ref.refs_3_.refs_4_, f32[512,1536]{1,0:T(8,128)} %get-tuple-element.143.refs_1_.refs_2_, f32[12,2,512]{2,1,0:T(2,128)} %reshape.417.refs_2_), custom_call_target="tpu_custom_call" | custom-call | flops 201326592 | bytes 3145728 | tf_op jit(solution)/shard_map/state/pallas_call | solution.py:871
  357.5 4.5 pad_maximum_fusion.1
  365.7 8.0 collective-permute-start.41
  373.7 19.8 %pack.4.refs_0_ = bf16[49344,128]{1,0:T(8,128)(2,1)} custom-call(bf16[512,1024]{1,0:T(8,128)(2,1)S(1)} %copy-done.47, bf16[512,2048]{1,0:T(8,128)(2,1)S(1)} %copy-done.67, bf16[512,2048]{1,0:T(8,128)(2,1)} %get-tuple-element.215.refs_2_, bf16[512,2048]{1,0:T(8,128)(2,1)} %get-tuple-element.216.refs_3_, bf16[512,1024]{1,0:T(8,128)(2,1)S(1)} %copy-done.45, ...), custom_call_target="tpu_custom_call" | custom-call | flops 6442450944 | bytes 16777216 | tf_op jit(solution)/shard_map/pack/pallas_call | solution.py:609
  398.0 6.0 constant_dynamic-slice_fusion.2.refs_2_
  406.8 27.0 %collective-permute-start.42 = (bf16[144,1536]{1,0:T(8,128)(2,1)}, bf16[144,1536]{1,0:T(8,128)(2,1)}, u32[]{:S(2)}, u32[]{:S(2)}) collective-permute-start(bf16[144,1536]{1,0:T(8,128)(2,1)} %pad_maximum_fusion.19.refs_1_), channel_id=1, source_target_pairs={{0,4},{4,0},{1,5},{5,1},{2,6},{6,2},{3,7},{7,3},{8,12},{12,8},{9,1... | collective-permute-start | bytes 1327112 | tf_op jit(solution)/shard_map/ppermute | solution.py:248
  436.5 5.8 add_convert_fusion.1
  445.9 4.9 collective-permute-start.44
  456.2 9.7 %collective-permute-start.46 = (f32[4]{0:T(128)S(1)}, f32[4]{0:T(128)S(1)}, u32[]{:S(2)}, u32[]{:S(2)}) collective-permute-start(f32[4]{0:T(128)S(1)} %add.640.refs_13_), channel_id=1, source_target_pairs={{0,8},{8,0},{16,24},{24,16},{1,9},{9,1},{17,25},{25,17},{2,10},{10... | collective-permute-start | bytes 56 | tf_op jit(solution)/shard_map/ppermute | solution.py:248
  470.3 33.0 %ssm_back.1 = (f32[512,1536]{1,0:T(8,128)S(1)}, f32[512,128]{1,0:T(8,128)S(1)}, f32[512,128]{1,0:T(8,128)S(1)}, f32[12,8,512]{2,1,0:T(8,128)S(1)}) custom-call(s32[5]{0:T(128)S(1)} %copy-done.63, f32[512,1792]{1,0:T(8,128)} %conv.1.refs_0_.refs_1_.x_ref.b_ref.c_ref.refs_3_.refs_4_, f32[512,1536]{1,0:T(8,128)S(1)} %copy-done.9, ...), custom_call_target="tpu_custom_call" | custom-call | flops 3000000000 | bytes 9437184 | tf_op jit(solution)/shard_map/ssm_back/pallas_call | solution.py:1088
  516.4 12.9 %collective-permute-start.81 = (f32[4]{0:T(128)S(1)}, f32[4]{0:T(128)S(1)}, u32[]{:S(2)}, u32[]{:S(2)}) collective-permute-start(f32[4]{0:T(128)S(1)} %add.656.refs_11_), channel_id=1, source_target_pairs={{0,16},{16,0},{8,24},{24,8},{1,17},{17,1},{9,25},{25,9},{2,18},{18... | collective-permute-start | bytes 56 | tf_op jit(solution)/shard_map/ppermute | solution.py:248
  530.7 14.7 %conv_back.1 = (bf16[512,1792]{1,0:T(8,128)(2,1)}, f32[16,1792]{1,0:T(8,128)}, f32[8,1792]{1,0:T(8,128)}, f32[8,1792]{1,0:T(8,128)}) custom-call(s32[5]{0:T(128)} %pad_add_fusion.1.refs_0_.meta_ref, f32[512,1536]{1,0:T(8,128)} %get-tuple-element.85.refs_1_, f32[512,128]{1,0:T(8,128)} %get-tuple-element.86.refs_2_, f32[512,128]{1,0:T(8,128)} %get-tuple-element.87.refs_3_, ...), custom_call_target="tpu_custom_call" | custom-call | flops 2000000000 | bytes 9175040 | tf_op jit(solution)/shard_map/conv_back/pallas_call | solution.py:818
  558.4 10.5 %pack.6 = bf16[49440,128]{1,0:T(8,128)(2,1)} custom-call(bf16[512,512]{1,0:T(8,128)(2,1)S(1)} %bitcast.278, bf16[512,1024]{1,0:T(8,128)(2,1)S(1)} %copy-done.2, bf16[512,1024]{1,0:T(8,128)(2,1)S(1)} %copy-done.7, bf16[512,1536]{1,0:T(8,128)(2,1)S(1)} %copy-done.17, bf16[512,1536]{1,0:T(8,128)(2,1)S(1)} %slice.369.refs_4_, ...), custom_call_target="tpu_custom_call", output_to_operand_aliasing={{}: (7, {})} | custom-call | flops 4026531840 | bytes 11010048 | tf_op jit(solution)/shard_map/pack/pallas_call | solution.py:609
  568.9 6.0 constant_dynamic-slice_fusion.1.refs_1_
  580.8 5.1 fusion.106
  589.6 5.1 collective-permute-start.55
  601.5 5.0 fusion.86
  606.6 6.2 add_convert_fusion
  621.6 7.6 attend_back.2
  629.2 23.9 %collective-permute-done.51 = bf16[2,3104,128]{2,1,0:T(8,128)(2,1)} collective-permute-done((bf16[2,3104,128]{2,1,0:T(8,128)(2,1)}, bf16[2,3104,128]{2,1,0:T(8,128)(2,1)}, u32[]{:S(2)}, u32[]{:S(2)}) %collective-permute-start.51) | collective-permute-done | bytes 1589280 | tf_op jit(solution)/shard_map/ppermute | solution.py:248
  664.2 8.0 attend_back.3
  703.3 11.6 %collective-permute-start.62 = (bf16[2,2,512,128]{3,2,1,0:T(8,128)(2,1)S(1)}, bf16[2,2,512,128]{3,2,1,0:T(8,128)(2,1)}, u32[]{:S(2)}, u32[]{:S(2)}) collective-permute-start(bf16[2,2,512,128]{3,2,1,0:T(8,128)(2,1)S(1)} %dynamic-slice_bitcast_fusion.21.refs_1_), channel_id=1, source_target_pairs={{0,4},{4,0},{1,5},{5,1},{2,6},{6,2},{3,7},{7,3},{8,12},{12,8},{9,1... | collective-permute-start | bytes 1572872 | tf_op jit(solution)/shard_map/ppermute | solution.py:248
  721.0 6.1 collective-permute-done.62
  728.4 5.9 collective-permute-start.63
  734.3 5.6 add_add_fusion.4.refs_0_
  744.0 4.8 fusion.12
  780.7 19.7 %collective-permute-done.70.refs_1_ = bf16[3104,128]{1,0:T(8,128)(2,1)S(1)} collective-permute-done((bf16[3104,128]{1,0:T(8,128)(2,1)S(1)}, bf16[3104,128]{1,0:T(8,128)(2,1)S(1)}, u32[]{:S(2)}, u32[]{:S(2)}) %collective-permute-start.70) | collective-permute-done | bytes 794656 | tf_op jit(solution)/shard_map/ppermute | solution.py:248
  828.3 4.9 fusion.14
  (790 shorter events, 334.4 us)
Async XLA Ops:
  7.2 220.7 %all-gather.3.cloned.1.call-start = ((), (), s32[]{:S(2)}) async-start(), calls=%async_computation | async-start | bytes 2359296 | tf_op jit(solution)/shard_map/all_gather | solution.py:1542
  18.6 17.1 %collective-permute-start.1 = (bf16[3088,128]{1,0:T(8,128)(2,1)S(1)}, bf16[3088,128]{1,0:T(8,128)(2,1)S(1)}, u32[]{:S(2)}, u32[]{:S(2)}) collective-permute-start(bf16[3088,128]{1,0:T(8,128)(2,1)S(1)} %get-tuple-element.170), channel_id=1, source_target_pairs={{0,8},{9,17},{2,10},{11,19},{4,12},{13,21},{6,14},{15,23}} | collective-permute-start | bytes 2371592 | tf_op jit(solution)/shard_map/ppermute | solution.py:287
  43.9 32.2 %collective-permute-start.26 = (bf16[2,3088,128]{2,1,0:T(8,128)(2,1)}, bf16[2,3088,128]{2,1,0:T(8,128)(2,1)}, u32[]{:S(2)}, u32[]{:S(2)}) collective-permute-start(bf16[2,3088,128]{2,1,0:T(8,128)(2,1)} %collective-permute-done.24), channel_id=1, source_target_pairs={{8,0},{17,9},{10,2},{19,11},{12,4},{21,13},{14,6},{23,15}} | collective-permute-start | bytes 4743176 | tf_op jit(solution)/shard_map/ppermute | solution.py:302
  48.2 27.9 %collective-permute-start.17 = (bf16[3088,128]{1,0:T(8,128)(2,1)}, bf16[3088,128]{1,0:T(8,128)(2,1)}, u32[]{:S(2)}, u32[]{:S(2)}) collective-permute-start(bf16[3088,128]{1,0:T(8,128)(2,1)} %add_select_fusion.1), channel_id=1, source_target_pairs={{0,4},{4,0},{1,5},{5,1},{2,6},{6,2},{3,7},{7,3},{8,12},{12,8},{9,1... | collective-permute-start | bytes 2371592 | tf_op jit(solution)/shard_map/ppermute | solution.py:293
  49.7 38.7 %collective-permute-start.16 = (bf16[3088,128]{1,0:T(8,128)(2,1)}, bf16[3088,128]{1,0:T(8,128)(2,1)}, u32[]{:S(2)}, u32[]{:S(2)}) collective-permute-start(bf16[3088,128]{1,0:T(8,128)(2,1)} %add_select_fusion.1), channel_id=1, source_target_pairs={{0,2},{2,0},{1,3},{3,1},{4,6},{6,4},{5,7},{7,5},{8,10},{10,8},{9,1... | collective-permute-start | bytes 2371592 | tf_op jit(solution)/shard_map/ppermute | solution.py:292
  52.7 35.7 %collective-permute-start.5 = (bf16[3088,128]{1,0:T(8,128)(2,1)S(1)}, bf16[3088,128]{1,0:T(8,128)(2,1)S(1)}, u32[]{:S(2)}, u32[]{:S(2)}) collective-permute-start(bf16[3088,128]{1,0:T(8,128)(2,1)S(1)} %add_select_fusion.2), channel_id=1, source_target_pairs={{0,2},{2,0},{1,3},{3,1},{4,6},{6,4},{5,7},{7,5},{8,10},{10,8},{9,1... | collective-permute-start | bytes 2371592 | tf_op jit(solution)/shard_map/ppermute | solution.py:292
  53.3 36.8 %collective-permute-start.6 = (bf16[3088,128]{1,0:T(8,128)(2,1)S(1)}, bf16[3088,128]{1,0:T(8,128)(2,1)S(1)}, u32[]{:S(2)}, u32[]{:S(2)}) collective-permute-start(bf16[3088,128]{1,0:T(8,128)(2,1)S(1)} %add_select_fusion.2), channel_id=1, source_target_pairs={{0,4},{4,0},{1,5},{5,1},{2,6},{6,2},{3,7},{7,3},{8,12},{12,8},{9,1... | collective-permute-start | bytes 2371592 | tf_op jit(solution)/shard_map/ppermute | solution.py:293
  76.1 34.2 %collective-permute-start.27 = (bf16[2,3088,128]{2,1,0:T(8,128)(2,1)}, bf16[2,3088,128]{2,1,0:T(8,128)(2,1)}, u32[]{:S(2)}, u32[]{:S(2)}) collective-permute-start(bf16[2,3088,128]{2,1,0:T(8,128)(2,1)} %collective-permute-done.26), channel_id=1, source_target_pairs={{9,1},{11,3},{13,5},{15,7}} | collective-permute-start | bytes 4743176 | tf_op jit(solution)/shard_map/ppermute | solution.py:303
  88.5 20.4 %collective-permute-start.18 = (bf16[3088,128]{1,0:T(8,128)(2,1)}, bf16[3088,128]{1,0:T(8,128)(2,1)}, u32[]{:S(2)}, u32[]{:S(2)}) collective-permute-start(bf16[3088,128]{1,0:T(8,128)(2,1)} %collective-permute-done.17), channel_id=1, source_target_pairs={{0,2},{2,0},{1,3},{3,1},{4,6},{6,4},{5,7},{7,5},{8,10},{10,8},{9,1... | collective-permute-start | bytes 2371592 | tf_op jit(solution)/shard_map/ppermute | solution.py:294
  90.0 19.8 %collective-permute-start.7 = (bf16[3088,128]{1,0:T(8,128)(2,1)S(1)}, bf16[3088,128]{1,0:T(8,128)(2,1)}, u32[]{:S(2)}, u32[]{:S(2)}) collective-permute-start(bf16[3088,128]{1,0:T(8,128)(2,1)S(1)} %collective-permute-done.5), channel_id=1, source_target_pairs={{0,4},{4,0},{1,5},{5,1},{2,6},{6,2},{3,7},{7,3},{8,12},{12,8},{9,1... | collective-permute-start | bytes 2371592 | tf_op jit(solution)/shard_map/ppermute | solution.py:294
  91.6 18.3 %collective-permute-start.21 = (bf16[3088,128]{1,0:T(8,128)(2,1)}, bf16[3088,128]{1,0:T(8,128)(2,1)}, u32[]{:S(2)}, u32[]{:S(2)}) collective-permute-start(bf16[3088,128]{1,0:T(8,128)(2,1)} %collective-permute-done.17), channel_id=1, source_target_pairs={{0,1},{1,0},{2,3},{3,2},{4,5},{5,4},{6,7},{7,6},{8,9},{9,8},{10,11... | collective-permute-start | bytes 2371592 | tf_op jit(solution)/shard_map/ppermute | solution.py:297
  94.1 21.8 %collective-permute-start.9 = (bf16[3088,128]{1,0:T(8,128)(2,1)S(1)}, bf16[3088,128]{1,0:T(8,128)(2,1)S(1)}, u32[]{:S(2)}, u32[]{:S(2)}) collective-permute-start(bf16[3088,128]{1,0:T(8,128)(2,1)S(1)} %collective-permute-done.5), channel_id=1, source_target_pairs={{0,1},{1,0},{2,3},{3,2},{4,5},{5,4},{6,7},{7,6},{8,9},{9,8},{10,11... | collective-permute-start | bytes 2371592 | tf_op jit(solution)/shard_map/ppermute | solution.py:297
  115.8 40.3 %collective-permute-start.28 = (bf16[2,3088,128]{2,1,0:T(8,128)(2,1)}, bf16[2,3088,128]{2,1,0:T(8,128)(2,1)}, u32[]{:S(2)}, u32[]{:S(2)}) collective-permute-start(bf16[2,3088,128]{2,1,0:T(8,128)(2,1)} %add_select_fusion.refs_1_.refs_6_.refs_18_), channel_id=1, source_target_pairs={{0,2},{2,0},{1,3},{3,1},{4,6},{6,4},{5,7},{7,5},{8,10},{10,8},{9,1... | collective-permute-start | bytes 4743176 | tf_op jit(solution)/shard_map/ppermute | solution.py:248
  116.8 40.9 %collective-permute-start.29 = (bf16[2,3088,128]{2,1,0:T(8,128)(2,1)}, bf16[2,3088,128]{2,1,0:T(8,128)(2,1)}, u32[]{:S(2)}, u32[]{:S(2)}) collective-permute-start(bf16[2,3088,128]{2,1,0:T(8,128)(2,1)} %add_select_fusion.refs_1_.refs_6_.refs_18_), channel_id=1, source_target_pairs={{0,4},{4,0},{1,5},{5,1},{2,6},{6,2},{3,7},{7,3},{8,12},{12,8},{9,1... | collective-permute-start | bytes 4743176 | tf_op jit(solution)/shard_map/ppermute | solution.py:248
  118.3 146.9 %collective-permute-start.35 = (bf16[2,3088,128]{2,1,0:T(8,128)(2,1)}, bf16[2,3088,128]{2,1,0:T(8,128)(2,1)}, u32[]{:S(2)}, u32[]{:S(2)}) collective-permute-start(bf16[2,3088,128]{2,1,0:T(8,128)(2,1)} %add_select_fusion.refs_1_.refs_6_.refs_18_), channel_id=1, source_target_pairs={{0,1},{1,0},{2,3},{3,2},{4,5},{5,4},{6,7},{7,6},{8,9},{9,8},{10,11... | collective-permute-start | bytes 4743176 | tf_op jit(solution)/shard_map/ppermute | solution.py:248
  157.3 29.4 %collective-permute-start.30 = (bf16[1,3088,128]{2,1,0:T(8,128)(2,1)S(1)}, bf16[1,3088,128]{2,1,0:T(8,128)(2,1)}, u32[]{:S(2)}, u32[]{:S(2)}) collective-permute-start(bf16[1,3088,128]{2,1,0:T(8,128)(2,1)S(1)} %slice.342.refs_3_), channel_id=1, source_target_pairs={{0,4},{4,0},{1,5},{5,1},{2,6},{6,2},{3,7},{7,3},{8,12},{12,8},{9,1... | collective-permute-start | bytes 2371592 | tf_op jit(solution)/shard_map/ppermute | solution.py:248
  159.8 26.9 %collective-permute-start.31 = (bf16[1,3088,128]{2,1,0:T(8,128)(2,1)}, bf16[1,3088,128]{2,1,0:T(8,128)(2,1)}, u32[]{:S(2)}, u32[]{:S(2)}) collective-permute-start(bf16[1,3088,128]{2,1,0:T(8,128)(2,1)} %slice.343.refs_4_), channel_id=1, source_target_pairs={{0,2},{2,0},{1,3},{3,1},{4,6},{6,4},{5,7},{7,5},{8,10},{10,8},{9,1... | collective-permute-start | bytes 2371592 | tf_op jit(solution)/shard_map/ppermute | solution.py:248
  188.1 18.4 %collective-permute-start.32 = (bf16[144,1536]{1,0:T(8,128)(2,1)S(1)}, bf16[144,1536]{1,0:T(8,128)(2,1)}, u32[]{:S(2)}, u32[]{:S(2)}) collective-permute-start(bf16[144,1536]{1,0:T(8,128)(2,1)S(1)} %pad_maximum_fusion.14.refs_1_), channel_id=1, source_target_pairs={{0,1},{1,0},{2,3},{3,2},{4,5},{5,4},{6,7},{7,6},{8,9},{9,8},{10,11... | collective-permute-start | bytes 1327112 | tf_op jit(solution)/shard_map/ppermute | solution.py:248
  205.7 59.6 %collective-permute-start.36 = (bf16[2,3088,128]{2,1,0:T(8,128)(2,1)}, bf16[2,3088,128]{2,1,0:T(8,128)(2,1)}, u32[]{:S(2)}, u32[]{:S(2)}) collective-permute-start(bf16[2,3088,128]{2,1,0:T(8,128)(2,1)} %collective-permute-done.28.refs_2_.refs_7_.refs_19_), channel_id=1, source_target_pairs={{0,1},{1,0},{2,3},{3,2},{4,5},{5,4},{6,7},{7,6},{8,9},{9,8},{10,11... | collective-permute-start | bytes 4743176 | tf_op jit(solution)/shard_map/ppermute | solution.py:248
  205.9 59.4 %collective-permute-start.37 = (bf16[2,3088,128]{2,1,0:T(8,128)(2,1)}, bf16[2,3088,128]{2,1,0:T(8,128)(2,1)}, u32[]{:S(2)}, u32[]{:S(2)}) collective-permute-start(bf16[2,3088,128]{2,1,0:T(8,128)(2,1)} %collective-permute-done.29.refs_3_.refs_8_.refs_20_), channel_id=1, source_target_pairs={{0,1},{1,0},{2,3},{3,2},{4,5},{5,4},{6,7},{7,6},{8,9},{9,8},{10,11... | collective-permute-start | bytes 4743176 | tf_op jit(solution)/shard_map/ppermute | solution.py:248
  206.2 59.1 %collective-permute-start.38 = (bf16[1,3088,128]{2,1,0:T(8,128)(2,1)}, bf16[1,3088,128]{2,1,0:T(8,128)(2,1)}, u32[]{:S(2)}, u32[]{:S(2)}) collective-permute-start(bf16[1,3088,128]{2,1,0:T(8,128)(2,1)} %collective-permute-done.30.refs_4_.refs_9_.refs_21_), channel_id=1, source_target_pairs={{0,1},{1,0},{2,3},{3,2},{4,5},{5,4},{6,7},{7,6},{8,9},{9,8},{10,11... | collective-permute-start | bytes 2371592 | tf_op jit(solution)/shard_map/ppermute | solution.py:248
  224.9 19.4 %collective-permute-start.34 = (bf16[144,1536]{1,0:T(8,128)(2,1)S(1)}, bf16[144,1536]{1,0:T(8,128)(2,1)}, u32[]{:S(2)}, u32[]{:S(2)}) collective-permute-start(bf16[144,1536]{1,0:T(8,128)(2,1)S(1)} %pad_maximum_fusion.16.refs_4_), channel_id=1, source_target_pairs={{0,4},{4,0},{1,5},{5,1},{2,6},{6,2},{3,7},{7,3},{8,12},{12,8},{9,1... | collective-permute-start | bytes 1327112 | tf_op jit(solution)/shard_map/ppermute | solution.py:248
  244.2 21.1 %collective-permute-start.39 = (bf16[1,3088,128]{2,1,0:T(8,128)(2,1)}, bf16[1,3088,128]{2,1,0:T(8,128)(2,1)}, u32[]{:S(2)}, u32[]{:S(2)}) collective-permute-start(bf16[1,3088,128]{2,1,0:T(8,128)(2,1)} %collective-permute-done.31.refs_5_.refs_10_.refs_22_), channel_id=1, source_target_pairs={{0,1},{1,0},{2,3},{3,2},{4,5},{5,4},{6,7},{7,6},{8,9},{9,8},{10,11... | collective-permute-start | bytes 2371592 | tf_op jit(solution)/shard_map/ppermute | solution.py:248
  365.7 27.8 %collective-permute-start.41 = (bf16[144,1536]{1,0:T(8,128)(2,1)S(1)}, bf16[144,1536]{1,0:T(8,128)(2,1)S(1)}, u32[]{:S(2)}, u32[]{:S(2)}) collective-permute-start(bf16[144,1536]{1,0:T(8,128)(2,1)S(1)} %pad_maximum_fusion.18.refs_7_), channel_id=1, source_target_pairs={{0,2},{2,0},{1,3},{3,1},{4,6},{6,4},{5,7},{7,5},{8,10},{10,8},{9,1... | collective-permute-start | bytes 1327112 | tf_op jit(solution)/shard_map/ppermute | solution.py:248
  404.0 32.5 %collective-permute-start.43 = (bf16[24688,128]{1,0:T(8,128)(2,1)}, bf16[24688,128]{1,0:T(8,128)(2,1)}, u32[]{:S(2)}, u32[]{:S(2)}) collective-permute-start(bf16[24688,128]{1,0:T(8,128)(2,1)} %constant_dynamic-slice_fusion.2.refs_2_), channel_id=1, source_target_pairs={{0,1},{1,0},{2,3},{3,2},{4,5},{5,4},{6,7},{7,6},{8,9},{9,8},{10,11... | collective-permute-start | bytes 18960392 | tf_op jit(solution)/shard_map/ppermute | solution.py:248
  406.8 48.3 %collective-permute-start.42 = (bf16[144,1536]{1,0:T(8,128)(2,1)}, bf16[144,1536]{1,0:T(8,128)(2,1)}, u32[]{:S(2)}, u32[]{:S(2)}) collective-permute-start(bf16[144,1536]{1,0:T(8,128)(2,1)} %pad_maximum_fusion.19.refs_1_), channel_id=1, source_target_pairs={{0,4},{4,0},{1,5},{5,1},{2,6},{6,2},{3,7},{7,3},{8,12},{12,8},{9,1... | collective-permute-start | bytes 1327112 | tf_op jit(solution)/shard_map/ppermute | solution.py:248
  445.9 61.1 %collective-permute-start.44 = (bf16[2,3104,128]{2,1,0:T(8,128)(2,1)}, bf16[2,3104,128]{2,1,0:T(8,128)(2,1)}, u32[]{:S(2)}, u32[]{:S(2)}) collective-permute-start(bf16[2,3104,128]{2,1,0:T(8,128)(2,1)} %pad_maximum_fusion.4.refs_11_.refs_1_), channel_id=1, source_target_pairs={{0,4},{4,0},{1,5},{5,1},{2,6},{6,2},{3,7},{7,3},{8,12},{12,8},{9,1... | collective-permute-start | bytes 4767752 | tf_op jit(solution)/shard_map/ppermute | solution.py:248
  456.2 59.1 %collective-permute-start.46 = (f32[4]{0:T(128)S(1)}, f32[4]{0:T(128)S(1)}, u32[]{:S(2)}, u32[]{:S(2)}) collective-permute-start(f32[4]{0:T(128)S(1)} %add.640.refs_13_), channel_id=1, source_target_pairs={{0,8},{8,0},{16,24},{24,16},{1,9},{9,1},{17,25},{25,17},{2,10},{10... | collective-permute-start | bytes 56 | tf_op jit(solution)/shard_map/ppermute | solution.py:248
  469.8 42.2 %collective-permute-start.45 = (bf16[2,3104,128]{2,1,0:T(8,128)(2,1)}, bf16[2,3104,128]{2,1,0:T(8,128)(2,1)}, u32[]{:S(2)}, u32[]{:S(2)}) collective-permute-start(bf16[2,3104,128]{2,1,0:T(8,128)(2,1)} %pad_maximum_fusion.5.refs_12_.refs_2_), channel_id=1, source_target_pairs={{0,2},{2,0},{1,3},{3,1},{4,6},{6,4},{5,7},{7,5},{8,10},{10,8},{9,1... | collective-permute-start | bytes 4767752 | tf_op jit(solution)/shard_map/ppermute | solution.py:248
  510.4 35.9 %collective-permute-start.47 = (bf16[3104,128]{1,0:T(8,128)(2,1)}, bf16[3104,128]{1,0:T(8,128)(2,1)}, u32[]{:S(2)}, u32[]{:S(2)}) collective-permute-start(bf16[3104,128]{1,0:T(8,128)(2,1)} %dynamic-slice_bitcast_fusion.14.refs_4_.refs_9_), channel_id=1, source_target_pairs={{0,2},{2,0},{1,3},{3,1},{4,6},{6,4},{5,7},{7,5},{8,10},{10,8},{9,1... | collective-permute-start | bytes 2383880 | tf_op jit(solution)/shard_map/ppermute | solution.py:248
  515.2 32.7 %collective-permute-start.48 = (bf16[3104,128]{1,0:T(8,128)(2,1)}, bf16[3104,128]{1,0:T(8,128)(2,1)}, u32[]{:S(2)}, u32[]{:S(2)}) collective-permute-start(bf16[3104,128]{1,0:T(8,128)(2,1)} %dynamic-slice_bitcast_fusion.11.refs_5_.refs_10_), channel_id=1, source_target_pairs={{0,4},{4,0},{1,5},{5,1},{2,6},{6,2},{3,7},{7,3},{8,12},{12,8},{9,1... | collective-permute-start | bytes 2383880 | tf_op jit(solution)/shard_map/ppermute | solution.py:248
  516.4 37.2 %collective-permute-start.81 = (f32[4]{0:T(128)S(1)}, f32[4]{0:T(128)S(1)}, u32[]{:S(2)}, u32[]{:S(2)}) collective-permute-start(f32[4]{0:T(128)S(1)} %add.656.refs_11_), channel_id=1, source_target_pairs={{0,16},{16,0},{8,24},{24,8},{1,17},{17,1},{9,25},{25,9},{2,18},{18... | collective-permute-start | bytes 56 | tf_op jit(solution)/shard_map/ppermute | solution.py:248
  574.8 31.7 %collective-permute-start.50 = (bf16[24688,128]{1,0:T(8,128)(2,1)}, bf16[24688,128]{1,0:T(8,128)(2,1)}, u32[]{:S(2)}, u32[]{:S(2)}) collective-permute-start(bf16[24688,128]{1,0:T(8,128)(2,1)} %constant_dynamic-slice_fusion.1.refs_1_), channel_id=1, source_target_pairs={{0,1},{1,0},{2,3},{3,2},{4,5},{5,4},{6,7},{7,6},{8,9},{9,8},{10,11... | collective-permute-start | bytes 18960392 | tf_op jit(solution)/shard_map/ppermute | solution.py:248
  587.7 96.1 %collective-permute-start.54 = (bf16[2,3104,128]{2,1,0:T(8,128)(2,1)}, bf16[2,3104,128]{2,1,0:T(8,128)(2,1)}, u32[]{:S(2)}, u32[]{:S(2)}) collective-permute-start(bf16[2,3104,128]{2,1,0:T(8,128)(2,1)} %pad_maximum_fusion.6.refs_4_.refs_5_.refs_6_.refs_8_.refs_9_.refs_10_.refs_2_.refs_3_.refs_11_), channel_id=1, source_target_pairs={{8,16},{17,25},{10,18},{19,27},{12,20},{21,29},{14,22},{23,31}} | collective-permute-start | bytes 4767752 | tf_op jit(solution)/shard_map/ppermute | solution.py:248
  589.6 95.5 %collective-permute-start.55 = (bf16[2,3104,128]{2,1,0:T(8,128)(2,1)}, bf16[2,3104,128]{2,1,0:T(8,128)(2,1)}, u32[]{:S(2)}, u32[]{:S(2)}) collective-permute-start(bf16[2,3104,128]{2,1,0:T(8,128)(2,1)} %pad_maximum_fusion.6.refs_4_.refs_5_.refs_6_.refs_8_.refs_9_.refs_10_.refs_2_.refs_3_.refs_11_), channel_id=1, source_target_pairs={{0,16},{9,25},{2,18},{11,27},{4,20},{13,29},{6,22},{15,31}} | collective-permute-start | bytes 4767752 | tf_op jit(solution)/shard_map/ppermute | solution.py:248
  594.8 91.8 %collective-permute-start.56 = (bf16[2,3104,128]{2,1,0:T(8,128)(2,1)}, bf16[2,3104,128]{2,1,0:T(8,128)(2,1)}, u32[]{:S(2)}, u32[]{:S(2)}) collective-permute-start(bf16[2,3104,128]{2,1,0:T(8,128)(2,1)} %pad_maximum_fusion.6.refs_4_.refs_5_.refs_6_.refs_8_.refs_9_.refs_10_.refs_2_.refs_3_.refs_11_), channel_id=1, source_target_pairs={{24,16},{1,25},{26,18},{3,27},{28,20},{5,29},{30,22},{7,31}} | collective-permute-start | bytes 4767752 | tf_op jit(solution)/shard_map/ppermute | solution.py:248
  616.1 37.1 %collective-permute-start.51 = (bf16[2,3104,128]{2,1,0:T(8,128)(2,1)}, bf16[2,3104,128]{2,1,0:T(8,128)(2,1)}, u32[]{:S(2)}, u32[]{:S(2)}) collective-permute-start(bf16[2,3104,128]{2,1,0:T(8,128)(2,1)} %pad_maximum_fusion.7.refs_1_.refs_7_), channel_id=1, source_target_pairs={{0,4},{4,0},{1,5},{5,1},{2,6},{6,2},{3,7},{7,3},{8,12},{12,8},{9,1... | collective-permute-start | bytes 4767752 | tf_op jit(solution)/shard_map/ppermute | solution.py:248
  618.9 39.8 %collective-permute-start.52 = (bf16[2,3104,128]{2,1,0:T(8,128)(2,1)}, bf16[2,3104,128]{2,1,0:T(8,128)(2,1)}, u32[]{:S(2)}, u32[]{:S(2)}) collective-permute-start(bf16[2,3104,128]{2,1,0:T(8,128)(2,1)} %pad_maximum_fusion.8.refs_2_.refs_8_), channel_id=1, source_target_pairs={{0,2},{2,0},{1,3},{3,1},{4,6},{6,4},{5,7},{7,5},{8,10},{10,8},{9,1... | collective-permute-start | bytes 4767752 | tf_op jit(solution)/shard_map/ppermute | solution.py:248
  656.2 19.9 %collective-permute-start.53 = (bf16[3104,128]{1,0:T(8,128)(2,1)}, bf16[3104,128]{1,0:T(8,128)(2,1)}, u32[]{:S(2)}, u32[]{:S(2)}) collective-permute-start(bf16[3104,128]{1,0:T(8,128)(2,1)} %dynamic-slice_bitcast_fusion.4.refs_2_.refs_7_), channel_id=1, source_target_pairs={{0,2},{2,0},{1,3},{3,1},{4,6},{6,4},{5,7},{7,5},{8,10},{10,8},{9,1... | collective-permute-start | bytes 2383880 | tf_op jit(solution)/shard_map/ppermute | solution.py:248
  662.6 32.2 %collective-permute-start.58 = (bf16[3104,128]{1,0:T(8,128)(2,1)}, bf16[3104,128]{1,0:T(8,128)(2,1)}, u32[]{:S(2)}, u32[]{:S(2)}) collective-permute-start(bf16[3104,128]{1,0:T(8,128)(2,1)} %dynamic-slice_bitcast_fusion.1.refs_3_.refs_8_), channel_id=1, source_target_pairs={{0,4},{4,0},{1,5},{5,1},{2,6},{6,2},{3,7},{7,3},{8,12},{12,8},{9,1... | collective-permute-start | bytes 2383880 | tf_op jit(solution)/shard_map/ppermute | solution.py:248
  678.4 36.5 %collective-permute-start.59 = (bf16[3104,128]{1,0:T(8,128)(2,1)}, bf16[3104,128]{1,0:T(8,128)(2,1)}, u32[]{:S(2)}, u32[]{:S(2)}) collective-permute-start(bf16[3104,128]{1,0:T(8,128)(2,1)} %fusion.20.refs_2_.refs_3_.refs_4_), channel_id=1, source_target_pairs={{8,0},{17,9},{10,2},{19,11},{12,4},{21,13},{14,6},{23,15}} | collective-permute-start | bytes 2383880 | tf_op jit(solution)/shard_map/ppermute | solution.py:248
  683.8 34.1 %collective-permute-start.60 = (bf16[3104,128]{1,0:T(8,128)(2,1)}, bf16[3104,128]{1,0:T(8,128)(2,1)}, u32[]{:S(2)}, u32[]{:S(2)}) collective-permute-start(bf16[3104,128]{1,0:T(8,128)(2,1)} %fusion.20.refs_2_.refs_3_.refs_4_), channel_id=1, source_target_pairs={{16,0},{25,9},{18,2},{27,11},{20,4},{29,13},{22,6},{31,15}} | collective-permute-start | bytes 2383880 | tf_op jit(solution)/shard_map/ppermute | solution.py:248
  685.1 32.8 %collective-permute-start.61 = (bf16[3104,128]{1,0:T(8,128)(2,1)}, bf16[3104,128]{1,0:T(8,128)(2,1)}, u32[]{:S(2)}, u32[]{:S(2)}) collective-permute-start(bf16[3104,128]{1,0:T(8,128)(2,1)} %fusion.20.refs_2_.refs_3_.refs_4_), channel_id=1, source_target_pairs={{24,0},{1,9},{26,2},{3,11},{28,4},{5,13},{30,6},{7,15}} | collective-permute-start | bytes 2383880 | tf_op jit(solution)/shard_map/ppermute | solution.py:248
  703.3 23.8 %collective-permute-start.62 = (bf16[2,2,512,128]{3,2,1,0:T(8,128)(2,1)S(1)}, bf16[2,2,512,128]{3,2,1,0:T(8,128)(2,1)}, u32[]{:S(2)}, u32[]{:S(2)}) collective-permute-start(bf16[2,2,512,128]{3,2,1,0:T(8,128)(2,1)S(1)} %dynamic-slice_bitcast_fusion.21.refs_1_), channel_id=1, source_target_pairs={{0,4},{4,0},{1,5},{5,1},{2,6},{6,2},{3,7},{7,3},{8,12},{12,8},{9,1... | collective-permute-start | bytes 1572872 | tf_op jit(solution)/shard_map/ppermute | solution.py:248
  760.2 20.5 %collective-permute-start.69 = (bf16[3104,128]{1,0:T(8,128)(2,1)S(1)}, bf16[3104,128]{1,0:T(8,128)(2,1)S(1)}, u32[]{:S(2)}, u32[]{:S(2)}) collective-permute-start(bf16[3104,128]{1,0:T(8,128)(2,1)S(1)} %copy-done.3), channel_id=1, source_target_pairs={{8,0},{17,9},{10,2},{19,11},{12,4},{21,13},{14,6},{23,15}} | collective-permute-start | bytes 2383880 | tf_op jit(solution)/shard_map/ppermute | solution.py:248
  761.5 38.9 %collective-permute-start.70 = (bf16[3104,128]{1,0:T(8,128)(2,1)S(1)}, bf16[3104,128]{1,0:T(8,128)(2,1)S(1)}, u32[]{:S(2)}, u32[]{:S(2)}) collective-permute-start(bf16[3104,128]{1,0:T(8,128)(2,1)S(1)} %copy-done.3), channel_id=1, source_target_pairs={{16,0},{25,9},{18,2},{27,11},{20,4},{29,13},{22,6},{31,15}} | collective-permute-start | bytes 2383880 | tf_op jit(solution)/shard_map/ppermute | solution.py:248
  762.8 37.6 %collective-permute-start.71 = (bf16[3104,128]{1,0:T(8,128)(2,1)S(1)}, bf16[3104,128]{1,0:T(8,128)(2,1)}, u32[]{:S(2)}, u32[]{:S(2)}) collective-permute-start(bf16[3104,128]{1,0:T(8,128)(2,1)S(1)} %copy-done.3), channel_id=1, source_target_pairs={{24,0},{1,9},{26,2},{3,11},{28,4},{5,13},{30,6},{7,15}} | collective-permute-start | bytes 2383880 | tf_op jit(solution)/shard_map/ppermute | solution.py:248
  809.4 25.0 %collective-permute-start.80 = (bf16[3104,128]{1,0:T(8,128)(2,1)}, bf16[3104,128]{1,0:T(8,128)(2,1)S(1)}, u32[]{:S(2)}, u32[]{:S(2)}) collective-permute-start(bf16[3104,128]{1,0:T(8,128)(2,1)} %get-tuple-element.168.refs_5_), channel_id=1, source_target_pairs={{0,1},{9,8},{16,17},{25,24},{2,3},{11,10},{18,19},{27,26},{4,5},{1... | collective-permute-start | bytes 2383880 | tf_op jit(solution)/shard_map/ppermute | solution.py:248
  (224 other events, 2361.3 us)
Sparse Core Ops, SparseCore 0:
  147.8 44.0 all-gather.2
